TPU v7x, 32 devices: a whole 2x2x4 slice. The times are simulated.
32 devices in a mesh: blk: 4 (over y, x), box: 8 (over z, core).
Axes of the slice: x: 2, y: 2, z: 4, core: 2. Of those that a mesh axis runs over, the one named last changes fastest.
Arguments:
- excitation: bfloat16 [4, 16, 1024, 512], P('blk', 'box'), may hold values from -6 to 6
- leaf_basis: bfloat16 [4, 16, 384, 1024], P('blk', 'box'), may hold values from -0.1875 to 0.1875
- transfer: bfloat16 [4, 5, 16, 384, 768], P('blk', None, 'box'), may hold values from -0.21875 to 0.21875
- transfer_index: int32 [4, 5, 16], P('blk', None, 'box'), may hold values from 0 to 1
- out_basis: bfloat16 [4, 16, 1024, 384], P('blk', 'box'), may hold values from -0.21875 to 0.21875
Outputs:
- field: bfloat16 [16, 1024, 512], P('box', 'blk')
All inputs are finite; a program needn't handle non-finite values.
Results may differ from a plain program's by a relative error of at most 0.018.
Values may be sent and summed in bfloat16 or wider, within the bound.
No kernel may reach another device: no remote copies, remote signals or barrier semaphores. Data moves between devices by JAX's collectives and lax.ppermute only.
A program may use at most 64 MiB of HBM per device.

v0:
```python
import jax
import jax.numpy as jnp
from jax import lax
from jax.sharding import PartitionSpec as P


def partner(value, axis, distance):
    mask = 2**distance
    pairs = [(source, source ^ mask) for source in range(lax.axis_size(axis))]
    return lax.ppermute(value, axis, pairs)


def on_device(excitation, leaf_basis, transfer, transfer_index, out_basis):
    excite = excitation[0]
    leaves = leaf_basis[0]
    blocks = transfer[0]
    index = transfer_index[0]
    basis = out_basis[0]
    rank = leaves.shape[1]
    levels = blocks.shape[0]
    coeff = jnp.einsum("brp,bpc->brc", leaves, excite, preferred_element_type=jnp.float32).astype(
        jnp.bfloat16
    )
    nbits = lax.axis_size("box").bit_length() - 1
    position = lax.axis_index("box")

    def chosen(level, slot_here):
        return lax.dynamic_index_in_dim(blocks[level], index[level, slot_here], 0, keepdims=False)

    def combine(matrix, first, second):
        mixed = jnp.dot(matrix[:, :rank], first, preferred_element_type=jnp.float32)
        mixed = mixed + jnp.dot(matrix[:, rank:], second, preferred_element_type=jnp.float32)
        return mixed.astype(jnp.bfloat16)

    coeff = jnp.stack(
        [combine(chosen(0, 0), coeff[0], coeff[1]), combine(chosen(0, 1), coeff[0], coeff[1])]
    )
    for level in range(1, levels):
        bit = (level - 1) % nbits
        lower = position // 2**bit % 2 == 0
        results = []
        for slot_here in range(2):
            own = coeff[slot_here]
            other = partner(own, "box", bit)
            first = jnp.where(lower, own, other)
            second = jnp.where(lower, other, own)
            results.append(combine(chosen(level, slot_here), first, second))
        coeff = jnp.stack(results)
    shares = lax.psum_scatter(
        jnp.einsum("bqr,brc->qbc", basis, coeff, preferred_element_type=jnp.float32).astype(
            jnp.bfloat16
        ),
        "blk",
        scatter_dimension=0,
        tiled=True,
    ).astype(jnp.float32)
    return jnp.transpose(shares, (1, 0, 2)).astype(jnp.bfloat16)


def solution(mesh):
    in_specs = (
        P("blk", "box", None, None),
        P("blk", "box", None, None),
        P("blk", None, "box", None, None),
        P("blk", None, "box"),
        P("blk", "box", None, None),
    )
    out_specs = P("box", "blk", None)
    return jax.shard_map(
        on_device, mesh=mesh, in_specs=in_specs, out_specs=out_specs, check_vma=False
    )
```

profile of v0, /device:TPU:0, one launch (start us, length us, event | category | flops | bytes accessed | tf_op | source)
XLA Modules:
  0.0 146.2 jit_solution(3534916857661857861)
XLA Ops:
  6.5 1.7 %fusion.88 = (s32[1,1]{0,1:T(1,128)}, s32[1,1]{0,1:T(1,128)}, s32[1,1]{0,1:T(1,128)}, s32[1,1]{0,1:T(1,128)}, s32[1,1]{0,1:T(1,128)}, /*index=5*/s32[1,1]{0,1:T(...) fusion(s32[5,2]{0,1:T(2,128)} %bitcast.60), kind=kLoop, calls=%fused_computation.107 | loop fusion | bytes 80 | tf_op jit(solution)/shard_map/slice | solution.py:28
  10.8 4.9 %fusion.87 = (bf16[1,1,2,384,768]{4,3,2,1,0:T(8,128)(2,1)}, bf16[1,1,2,384,768]{4,3,2,1,0:T(8,128)(2,1)}, bf16[1,1,2,384,768]{4,3,2,1,0:T(8,128)(2,1)}, bf16[1,1...) fusion(bf16[1,5,2,384,768]{4,3,2,1,0:T(8,128)(2,1)} %param.7), kind=kLoop, calls=%fused_computation.106 | loop fusion | bytes 11796480 | tf_op jit(solution)/shard_map/slice | solution.py:28
  17.0 2.5 %fusion.4 = bf16[2,384,512]{2,1,0:T(8,128)(2,1)S(1)} fusion(bf16[1,2,1024,512]{3,2,1,0:T(8,128)(2,1)S(1)} %copy-done, bf16[1,2,384,1024]{3,2,1,0:T(8,128)(2,1)} %param.6), kind=kOutput, calls=%fused_computation.5 | convolution fusion | flops 805699584 | bytes 4456448 | tf_op jit(solution)/shard_map/brp,bpc->brc/dot_general | solution.py:21
  19.5 0.1 dynamic-slice_bitcast_fusion.5
  19.6 0.4 fusion.65
  20.0 1.1 fusion.9
  21.1 0.5 collective-permute-start
  21.6 0.4 fusion.64
  21.9 1.1 fusion.14
  23.0 0.1 collective-permute-start.4
  38.1 1.4 dynamic-slice_bitcast_fusion.9
  39.5 0.2 copy-done.2
  39.7 0.1 dynamic-slice_bitcast_fusion.7
  39.8 1.0 copy-done.1
  40.8 0.1 dynamic-slice_bitcast_fusion.8
  40.9 0.1 dynamic-slice_bitcast_fusion.6
  41.0 1.4 fusion.45
  42.4 1.4 fusion.10
  43.8 3.1 %collective-permute-start.1 = (bf16[384,512]{1,0:T(8,128)(2,1)S(1)}, bf16[384,512]{1,0:T(8,128)(2,1)S(1)}, u32[]{:S(2)}, u32[]{:S(2)}) collective-permute-start(bf16[384,512]{1,0:T(8,128)(2,1)S(1)} %fusion.10), channel_id=1, source_target_pairs={{0,2},{1,3},{2,0},{3,1},{4,6},{5,7},{6,4},{7,5},{8,10},{9,11},{10,... | collective-permute-start | bytes 1179656 | tf_op jit(solution)/shard_map/ppermute | solution.py:10
  46.9 1.4 fusion.33
  48.2 1.4 fusion.15
  49.6 0.1 collective-permute-start.5
  49.7 7.1 %collective-permute-done.1 = bf16[384,512]{1,0:T(8,128)(2,1)S(1)} collective-permute-done((bf16[384,512]{1,0:T(8,128)(2,1)S(1)}, bf16[384,512]{1,0:T(8,128)(2,1)S(1)}, u32[]{:S(2)}, u32[]{:S(2)}) %collective-permute-start.1) | collective-permute-done | bytes 393248 | tf_op jit(solution)/shard_map/ppermute | solution.py:10
  56.8 0.4 fusion.42
  57.1 0.4 fusion.11
  57.5 3.1 %collective-permute-start.2 = (bf16[384,512]{1,0:T(8,128)(2,1)S(1)}, bf16[384,512]{1,0:T(8,128)(2,1)S(1)}, u32[]{:S(2)}, u32[]{:S(2)}) collective-permute-start(bf16[384,512]{1,0:T(8,128)(2,1)S(1)} %fusion.11), channel_id=1, source_target_pairs={{0,4},{1,5},{2,6},{3,7},{4,0},{5,1},{6,2},{7,3},{8,12},{9,13},{10,... | collective-permute-start | bytes 1179656 | tf_op jit(solution)/shard_map/ppermute | solution.py:10
  60.7 10.8 %collective-permute-done.5 = bf16[384,512]{1,0:T(8,128)(2,1)S(1)} collective-permute-done((bf16[384,512]{1,0:T(8,128)(2,1)S(1)}, bf16[384,512]{1,0:T(8,128)(2,1)S(1)}, u32[]{:S(2)}, u32[]{:S(2)}) %collective-permute-start.5) | collective-permute-done | bytes 393248 | tf_op jit(solution)/shard_map/ppermute | solution.py:10
  71.4 0.4 fusion.30
  71.8 0.4 fusion.16
  72.2 0.1 collective-permute-start.6
  72.3 14.5 %collective-permute-done.2 = bf16[384,512]{1,0:T(8,128)(2,1)S(1)} collective-permute-done((bf16[384,512]{1,0:T(8,128)(2,1)S(1)}, bf16[384,512]{1,0:T(8,128)(2,1)S(1)}, u32[]{:S(2)}, u32[]{:S(2)}) %collective-permute-start.2) | collective-permute-done | bytes 393248 | tf_op jit(solution)/shard_map/ppermute | solution.py:10
  86.8 0.4 fusion.39
  87.1 0.4 fusion.12
  87.5 0.1 collective-permute-start.3
  87.6 6.1 %collective-permute-done.6 = bf16[384,512]{1,0:T(8,128)(2,1)S(1)} collective-permute-done((bf16[384,512]{1,0:T(8,128)(2,1)S(1)}, bf16[384,512]{1,0:T(8,128)(2,1)S(1)}, u32[]{:S(2)}, u32[]{:S(2)}) %collective-permute-start.6) | collective-permute-done | bytes 393248 | tf_op jit(solution)/shard_map/ppermute | solution.py:10
  93.7 0.4 fusion.27
  94.1 0.4 fusion.17
  94.5 0.1 collective-permute-start.7
  94.5 0.4 fusion.36
  94.9 0.4 fusion.20
  95.3 0.9 collective-permute-done.7
  96.2 0.4 fusion.24
  96.6 0.4 fusion.19
  97.0 1.0 copy-done.4
  98.0 2.8 %convert_bitcast_fusion = bf16[1024,2,512]{0,2,1:T(8,128)(2,1)} fusion(bf16[1,2,1024,384]{3,2,1,0:T(8,128)(2,1)S(1)} %copy-done.4, bf16[1,384,512]{2,1,0:T(8,128)(2,1)S(1)} %fusion.19, bf16[1,384,512]{2,1,0:T(8,128)(2,1)S(1)} %fusion.20), kind=kOutput, calls=%fused_computation.2 | convolution fusion | flops 806748160 | bytes 4456448 | tf_op jit(solution)/shard_map/bqr,brc->qbc/dot_general | solution.py:50
  100.8 0.0 reduce-scatter.2.cloned.1.call-update
  100.8 36.4 %reduce-scatter.2.cloned.1.call-done = bf16[256,2,512]{0,2,1:T(8,128)(2,1)} async-done(((bf16[1024,2,512]{0,2,1:T(8,128)(2,1)}), bf16[256,2,512]{0,2,1:T(8,128)(2,1)}) %reduce-scatter.2.cloned.1.call-update) | async-done | bytes 524304 | tf_op jit(solution)/shard_map/reduce_scatter | solution.py:49
  137.3 2.0 %copy.7 = bf16[2,256,512]{2,1,0:T(8,128)(2,1)} copy(bf16[2,256,512]{1,2,0:T(8,128)(2,1)} %bitcast.59) | data formatting | bytes 1048576 | tf_op jit(solution)/shard_map/convert_element_type | solution.py:57
  (11 shorter events, 0.0 us)
Async XLA Ops:
  6.5 10.5 %copy-start = (bf16[1,2,1024,512]{3,2,1,0:T(8,128)(2,1)S(1)}, bf16[1,2,1024,512]{3,2,1,0:T(8,128)(2,1)}, u32[]{:S(2)}) copy-start(bf16[1,2,1024,512]{3,2,1,0:T(8,128)(2,1)} %param.5) | copy-start | bytes 6291460
  6.5 130.7 %reduce-scatter.2.cloned.1.call-start = ((), (), s32[]{:S(2)}) async-start(), calls=%async_computation.1 | async-start | bytes 2621440 | tf_op jit(solution)/shard_map/reduce_scatter | solution.py:49
  17.0 2.5 %copy-start.3 = (bf16[1,1,2,384,768]{4,3,2,1,0:T(8,128)(2,1)S(1)}, bf16[1,1,2,384,768]{4,3,2,1,0:T(8,128)(2,1)}, u32[]{:S(2)}) copy-start(bf16[1,1,2,384,768]{4,3,2,1,0:T(8,128)(2,1)} %get-tuple-element.8) | copy-start | bytes 3538948
  21.1 19.9 %collective-permute-start = (bf16[384,512]{1,0:T(8,128)(2,1)}, bf16[384,512]{1,0:T(8,128)(2,1)}, u32[]{:S(2)}, u32[]{:S(2)}) collective-permute-start(bf16[384,512]{1,0:T(8,128)(2,1)} %fusion.9), channel_id=1, source_target_pairs={{0,1},{1,0},{2,3},{3,2},{4,5},{5,4},{6,7},{7,6},{8,9},{9,8},{10,11... | collective-permute-start | bytes 1179656 | tf_op jit(solution)/shard_map/ppermute | solution.py:10
  23.0 23.8 %collective-permute-start.4 = (bf16[384,512]{1,0:T(8,128)(2,1)}, bf16[384,512]{1,0:T(8,128)(2,1)}, u32[]{:S(2)}, u32[]{:S(2)}) collective-permute-start(bf16[384,512]{1,0:T(8,128)(2,1)} %fusion.14), channel_id=1, source_target_pairs={{0,1},{1,0},{2,3},{3,2},{4,5},{5,4},{6,7},{7,6},{8,9},{9,8},{10,11... | collective-permute-start | bytes 1179656 | tf_op jit(solution)/shard_map/ppermute | solution.py:10
  38.1 1.6 %copy-start.2 = (bf16[1,1,2,384,768]{4,3,2,1,0:T(8,128)(2,1)S(1)}, bf16[1,1,2,384,768]{4,3,2,1,0:T(8,128)(2,1)}, u32[]{:S(2)}) copy-start(bf16[1,1,2,384,768]{4,3,2,1,0:T(8,128)(2,1)} %get-tuple-element.6) | copy-start | bytes 3538948
  39.5 1.3 copy-start.1
  43.8 13.0 %collective-permute-start.1 = (bf16[384,512]{1,0:T(8,128)(2,1)S(1)}, bf16[384,512]{1,0:T(8,128)(2,1)S(1)}, u32[]{:S(2)}, u32[]{:S(2)}) collective-permute-start(bf16[384,512]{1,0:T(8,128)(2,1)S(1)} %fusion.10), channel_id=1, source_target_pairs={{0,2},{1,3},{2,0},{3,1},{4,6},{5,7},{6,4},{7,5},{8,10},{9,11},{10,... | collective-permute-start | bytes 1179656 | tf_op jit(solution)/shard_map/ppermute | solution.py:10
  49.6 21.8 %collective-permute-start.5 = (bf16[384,512]{1,0:T(8,128)(2,1)S(1)}, bf16[384,512]{1,0:T(8,128)(2,1)S(1)}, u32[]{:S(2)}, u32[]{:S(2)}) collective-permute-start(bf16[384,512]{1,0:T(8,128)(2,1)S(1)} %fusion.15), channel_id=1, source_target_pairs={{0,2},{1,3},{2,0},{3,1},{4,6},{5,7},{6,4},{7,5},{8,10},{9,11},{10,... | collective-permute-start | bytes 1179656 | tf_op jit(solution)/shard_map/ppermute | solution.py:10
  57.5 29.2 %collective-permute-start.2 = (bf16[384,512]{1,0:T(8,128)(2,1)S(1)}, bf16[384,512]{1,0:T(8,128)(2,1)S(1)}, u32[]{:S(2)}, u32[]{:S(2)}) collective-permute-start(bf16[384,512]{1,0:T(8,128)(2,1)S(1)} %fusion.11), channel_id=1, source_target_pairs={{0,4},{1,5},{2,6},{3,7},{4,0},{5,1},{6,2},{7,3},{8,12},{9,13},{10,... | collective-permute-start | bytes 1179656 | tf_op jit(solution)/shard_map/ppermute | solution.py:10
  72.2 21.5 %collective-permute-start.6 = (bf16[384,512]{1,0:T(8,128)(2,1)S(1)}, bf16[384,512]{1,0:T(8,128)(2,1)S(1)}, u32[]{:S(2)}, u32[]{:S(2)}) collective-permute-start(bf16[384,512]{1,0:T(8,128)(2,1)S(1)} %fusion.16), channel_id=1, source_target_pairs={{0,4},{1,5},{2,6},{3,7},{4,0},{5,1},{6,2},{7,3},{8,12},{9,13},{10,... | collective-permute-start | bytes 1179656 | tf_op jit(solution)/shard_map/ppermute | solution.py:10
  87.5 7.0 %collective-permute-start.3 = (bf16[384,512]{1,0:T(8,128)(2,1)S(1)}, bf16[384,512]{1,0:T(8,128)(2,1)S(1)}, u32[]{:S(2)}, u32[]{:S(2)}) collective-permute-start(bf16[384,512]{1,0:T(8,128)(2,1)S(1)} %fusion.12), channel_id=1, source_target_pairs={{0,1},{1,0},{2,3},{3,2},{4,5},{5,4},{6,7},{7,6},{8,9},{9,8},{10,11... | collective-permute-start | bytes 1179656 | tf_op jit(solution)/shard_map/ppermute | solution.py:10
  94.5 1.8 %collective-permute-start.7 = (bf16[384,512]{1,0:T(8,128)(2,1)S(1)}, bf16[384,512]{1,0:T(8,128)(2,1)S(1)}, u32[]{:S(2)}, u32[]{:S(2)}) collective-permute-start(bf16[384,512]{1,0:T(8,128)(2,1)S(1)} %fusion.17), channel_id=1, source_target_pairs={{0,1},{1,0},{2,3},{3,2},{4,5},{5,4},{6,7},{7,6},{8,9},{9,8},{10,11... | collective-permute-start | bytes 1179656 | tf_op jit(solution)/shard_map/ppermute | solution.py:10
  96.6 1.4 copy-start.4
Sparse Core Ops, SparseCore 0:
  100.9 36.2 reduce-scatter.1
where the time goes:
time: 147 us; the launch traced here: 146 us
  waiting for transfers between devices  75.9 us (52%)
  between operations  32.5 us (22%)
  matrix products  18.1 us (12%)
  local copies, waits for them, and re-layouts  12.7 us (9%)
  starting transfers between devices  7.05 us (5%)
    ppermute x8, waiting for transfers between devices, partner(): return lax.ppermute(value, axis, pairs)  39.4 us
    reduce_scatter x1, waiting for transfers between devices, on_device(): lax.psum_scatter(jnp.einsum('bqr,brc->qbc', basis, coeff, preferred_eleme...  36.4 us
    dot_general x10, matrix products, combine(): jnp.dot(matrix[:, rank:], second, preferred_element_type=jnp.float32)  7.16 us
    ppermute x8, starting transfers between devices, partner(): return lax.ppermute(value, axis, pairs)  7.04 us
    dot_general x10, matrix products, combine(): mixed = jnp.dot(matrix[:, :rank], first, preferred_element_type=jnp.float32)  5.69 us
    slice x1, local copies, waits for them, and re-layouts, chosen(): blocks[level]  4.89 us
  transfers between devices with their start and end apart: 9, of which 6 were waited for; matrix products, arithmetic and copies ran while one was open for 8% of the time, Pallas kernels for 0%

commit v1 on v0

v1 whole, which is shorter than its diff:
```python
import jax
import jax.numpy as jnp
from jax import lax
from jax.sharding import PartitionSpec as P

COLUMN_CHUNKS = 2


def partner(value, axis, mask):
    pairs = [(source, source ^ mask) for source in range(lax.axis_size(axis))]
    return lax.ppermute(value, axis, pairs)


def dot(a, b):
    return jnp.dot(a, b, preferred_element_type=jnp.float32)


def on_device(excitation, leaf_basis, transfer, transfer_index, out_basis):
    boxes = leaf_basis.shape[1]
    rank = leaf_basis.shape[2]
    levels = transfer.shape[1]
    columns = excitation.shape[3]
    width = columns // COLUMN_CHUNKS
    n_blk = lax.axis_size("blk")
    rows = out_basis.shape[2] // n_blk
    nbits = lax.axis_size("box").bit_length() - 1
    position = lax.axis_index("box")
    block = lax.axis_index("blk")

    def half(level, slot, upper):
        index = transfer_index[0, level, slot]
        lo = jnp.where(index == 1, transfer[0, level, 1, :, :rank], transfer[0, level, 0, :, :rank])
        hi = jnp.where(index == 1, transfer[0, level, 1, :, rank:], transfer[0, level, 0, :, rank:])
        return jnp.where(upper, hi, lo), jnp.where(upper, lo, hi)

    chunks = [(c, s) for c in range(COLUMN_CHUNKS) for s in range(boxes)]
    leaf = {
        (c, s): dot(leaf_basis[0, s], excitation[0, s, :, c * width : (c + 1) * width]).astype(jnp.bfloat16)
        for c, s in chunks
    }
    coeff = {}
    for c, s in chunks:
        lo, hi = half(0, s, False)
        coeff[c, s] = (dot(lo, leaf[c, 0]) + dot(hi, leaf[c, 1])).astype(jnp.bfloat16)
    for level in range(1, levels):
        bit = (level - 1) % nbits
        upper = (position >> bit) & 1 == 1
        pairs = [half(level, s, upper) for s in range(boxes)]
        after = {}
        for c, s in chunks:
            own, other = pairs[s]
            mine = coeff[c, s]
            theirs = partner(mine, "box", 2**bit)
            after[c, s] = (dot(own, mine) + dot(other, theirs)).astype(jnp.bfloat16)
        coeff = after
    parts = [
        [lax.dynamic_slice_in_dim(out_basis[0, s], (block ^ d) * rows, rows, 0) for d in range(n_blk)]
        for s in range(boxes)
    ]
    total = {}
    for c, s in chunks:
        total[c, s] = dot(parts[s][0], coeff[c, s])
        for d in range(n_blk - 1, 0, -1):
            piece = dot(parts[s][d], coeff[c, s]).astype(jnp.bfloat16)
            total[c, s] = total[c, s] + partner(piece, "blk", d).astype(jnp.float32)
        total[c, s] = total[c, s].astype(jnp.bfloat16)
    return jnp.stack(
        [jnp.concatenate([total[c, s] for c in range(COLUMN_CHUNKS)], axis=1) for s in range(boxes)]
    )


def solution(mesh):
    in_specs = (
        P("blk", "box", None, None),
        P("blk", "box", None, None),
        P("blk", None, "box", None, None),
        P("blk", None, "box"),
        P("blk", "box", None, None),
    )
    out_specs = P("box", "blk", None)
    return jax.shard_map(
        on_device, mesh=mesh, in_specs=in_specs, out_specs=out_specs, check_vma=False
    )
```

time: 147 us -> 130 us (0.88)
  waiting for transfers between devices: 75.9 us -> 43.2 us
  between operations: 32.5 us -> 6.67 us
  starting transfers between devices: 7.05 us -> 30.6 us
  matrix products: 18.1 us -> 39.1 us
  local copies, waits for them, and re-layouts: 12.7 us -> 5.16 us
  other arithmetic: 0 us -> 5.06 us
    reduce_scatter x1 -> x0, waiting for transfers between devices: 36.4 us -> none  [on_device(): lax.psum_scatter(jnp.einsum('bqr,brc->qbc', basis, coeff, preferred_eleme...]
    ppermute x8 -> x28, starting transfers between devices: 7.04 us -> 30.6 us  [partner(): return lax.ppermute(value, axis, pairs)]
    dot_general x22 -> x60, matrix products: 18.1 us -> 39.1 us  [dot(): return jnp.dot(a, b, preferred_element_type=jnp.float32)]
    select_n x0 -> x3, other arithmetic: none -> 4.97 us  [the longest x2 3.09 us: half(): jnp.where(index == 1, transfer[0, level, 1, :, :rank], transfer[0, level,...]
    ppermute x8 -> x28, waiting for transfers between devices: 39.4 us -> 43.2 us  [partner(): return lax.ppermute(value, axis, pairs)]
    slice x2, local copies, waits for them, and re-layouts: 6.61 us -> 4.13 us  [the longest x1 2.42 us: on_device(): out_basis[0, s]]
    unnamed x10 -> x12, local copies, waits for them, and re-layouts: 2.26 us -> 0.02 us
    convert_element_type x1 -> x0, local copies, waits for them, and re-layouts: 2.04 us -> none  [on_device(): return jnp.transpose(shares, (1, 0, 2)).astype(jnp.bfloat16)]
  transfers between devices with their start and end apart: 9 -> 28, of which waited for: 6 -> 9; matrix products, arithmetic and copies ran while one was open for 8% -> 30% of each run, Pallas kernels for 0% -> 0%
where the time goes in v1:
time: 130 us
  waiting for transfers between devices  43.2 us (33%)
  matrix products  39.1 us (30%)
  starting transfers between devices  30.6 us (24%)
  between operations  6.67 us (5%)
  local copies, waits for them, and re-layouts  5.16 us (4%)
  other arithmetic  5.06 us (4%)
    ppermute x28, waiting for transfers between devices, partner(): return lax.ppermute(value, axis, pairs)  43.2 us
    dot_general x60, matrix products, dot(): return jnp.dot(a, b, preferred_element_type=jnp.float32)  39.1 us
    ppermute x28, starting transfers between devices, partner(): return lax.ppermute(value, axis, pairs)  30.6 us
    select_n x2, other arithmetic, half(): jnp.where(index == 1, transfer[0, level, 1, :, :rank], transfer[0, level,...  3.09 us
  transfers between devices with their start and end apart: 28, of which 9 were waited for; matrix products, arithmetic and copies ran while one was open for 30% of the time, Pallas kernels for 0%

profile of v1, /device:TPU:0, one launch (start us, length us, event | category | flops | bytes accessed | tf_op | source)
XLA Modules:
  0.0 129.7 jit_solution(3230628015688534736)
XLA Ops:
  0.0 1.8 %convolution_convert_fusion = bf16[384,256]{1,0:T(8,128)(2,1)S(1)} fusion(bf16[1,2,384,1024]{3,2,1,0:T(8,128)(2,1)} %param.6, bf16[1,2,1024,512]{3,2,1,0:T(8,128)(2,1)} %param.5), kind=kOutput, calls=%fused_computation.20 | convolution fusion | flops 201424896 | bytes 1507328 | tf_op jit(solution)/shard_map/dot_general | solution.py:15
  1.8 1.7 %convolution_convert_fusion.1 = bf16[384,256]{1,0:T(8,128)(2,1)S(1)} fusion(bf16[1,2,384,1024]{3,2,1,0:T(8,128)(2,1)} %param.6, bf16[1,2,1024,512]{3,2,1,0:T(8,128)(2,1)} %param.5), kind=kOutput, calls=%fused_computation.21 | convolution fusion | flops 201424896 | bytes 1507328 | tf_op jit(solution)/shard_map/dot_general | solution.py:15
  3.5 1.7 %fusion.157 = (s32[1,1,1]{1,2,0:T(1,128)}, s32[1,1,1]{1,2,0:T(1,128)}, s32[1,1,1]{1,2,0:T(1,128)}, s32[1,1,1]{1,2,0:T(1,128)}, s32[1,1,1]{1,2,0:T(1,128)}, /*ind...) fusion(s32[1,5,2]{1,2,0:T(2,128)} %param.8), kind=kLoop, calls=%fused_computation.228 | loop fusion | bytes 80 | tf_op jit(solution)/shard_map/slice | solution.py:31
  5.7 1.3 %fusion.76 = f32[384,256]{1,0:T(8,128)S(1)} fusion(bf16[384,256]{1,0:T(8,128)(2,1)S(1)} %convolution_convert_fusion.1, pred[]{:T(512)} %bitcast.9, bf16[1,5,2,384,768]{4,3,2,1,0:T(8,128)(2,1)} %param.7), kind=kOutput, calls=%fused_computation.113 | convolution fusion | flops 75644928 | bytes 1180160 | tf_op jit(solution)/shard_map/dot_general | solution.py:15
  7.0 2.0 %fusion.5 = bf16[384,256]{1,0:T(8,128)(2,1)} fusion(f32[384,256]{1,0:T(8,128)S(1)} %fusion.76, bf16[384,256]{1,0:T(8,128)(2,1)S(1)} %convolution_convert_fusion, pred[]{:T(512)} %bitcast.9, bf16[1,5,2,384,768]{4,3,2,1,0:T(8,128)(2,1)} %param.7), kind=kOutput, calls=%fused_computation.29 | convolution fusion | flops 75841536 | bytes 1376768 | tf_op jit(solution)/shard_map/dot_general | solution.py:15
  10.2 1.3 %fusion.46 = f32[384,256]{1,0:T(8,128)S(1)} fusion(bf16[384,256]{1,0:T(8,128)(2,1)S(1)} %convolution_convert_fusion.1, pred[]{:T(512)} %bitcast.35, bf16[1,5,2,384,768]{4,3,2,1,0:T(8,128)(2,1)} %param.7), kind=kOutput, calls=%fused_computation.83 | convolution fusion | flops 75644928 | bytes 1180160 | tf_op jit(solution)/shard_map/dot_general | solution.py:15
  11.5 2.0 %fusion.15 = bf16[384,256]{1,0:T(8,128)(2,1)} fusion(f32[384,256]{1,0:T(8,128)S(1)} %fusion.46, bf16[384,256]{1,0:T(8,128)(2,1)S(1)} %convolution_convert_fusion, pred[]{:T(512)} %bitcast.35, bf16[1,5,2,384,768]{4,3,2,1,0:T(8,128)(2,1)} %param.7), kind=kOutput, calls=%fused_computation.39 | convolution fusion | flops 75841536 | bytes 1376768 | tf_op jit(solution)/shard_map/dot_general | solution.py:15
  14.3 1.3 %fusion.78 = f32[384,256]{1,0:T(8,128)S(1)} fusion(bf16[384,256]{1,0:T(8,128)(2,1)S(1)} %convolution_convert_fusion.3, pred[]{:T(512)} %bitcast.9, bf16[1,5,2,384,768]{4,3,2,1,0:T(8,128)(2,1)} %param.7), kind=kOutput, calls=%fused_computation.115 | convolution fusion | flops 75644928 | bytes 1180160 | tf_op jit(solution)/shard_map/dot_general | solution.py:15
  15.6 2.0 %fusion = bf16[384,256]{1,0:T(8,128)(2,1)} fusion(f32[384,256]{1,0:T(8,128)S(1)} %fusion.78, bf16[384,256]{1,0:T(8,128)(2,1)S(1)} %convolution_convert_fusion.2, pred[]{:T(512)} %bitcast.9, bf16[1,5,2,384,768]{4,3,2,1,0:T(8,128)(2,1)} %param.7), kind=kOutput, calls=%fused_computation.24 | convolution fusion | flops 75841536 | bytes 1376768 | tf_op jit(solution)/shard_map/dot_general | solution.py:15
  18.1 1.3 %fusion.48 = f32[384,256]{1,0:T(8,128)S(1)} fusion(bf16[384,256]{1,0:T(8,128)(2,1)S(1)} %convolution_convert_fusion.3, pred[]{:T(512)} %bitcast.35, bf16[1,5,2,384,768]{4,3,2,1,0:T(8,128)(2,1)} %param.7), kind=kOutput, calls=%fused_computation.85 | convolution fusion | flops 75644928 | bytes 1180160 | tf_op jit(solution)/shard_map/dot_general | solution.py:15
  19.4 2.0 %fusion.10 = bf16[384,256]{1,0:T(8,128)(2,1)} fusion(f32[384,256]{1,0:T(8,128)S(1)} %fusion.48, bf16[384,256]{1,0:T(8,128)(2,1)S(1)} %convolution_convert_fusion.2, pred[]{:T(512)} %bitcast.35, bf16[1,5,2,384,768]{4,3,2,1,0:T(8,128)(2,1)} %param.7), kind=kOutput, calls=%fused_computation.34 | convolution fusion | flops 75841536 | bytes 1376768 | tf_op jit(solution)/shard_map/dot_general | solution.py:15
  24.5 1.8 %broadcast_select_fusion.26 = (bf16[1,1,1,384,384]{4,3,2,1,0:T(8,128)(2,1)S(1)}, bf16[1,1,1,384,384]{4,3,2,1,0:T(8,128)(2,1)S(1)}, bf16[1,1,1,384,384]{4,3,2,1,0...) fusion(pred[]{:T(512)} %bitcast.1, ...), kind=kLoop, calls=%fused_computation.159 | loop fusion | flops 1032192 | bytes 4423685 | tf_op jit(solution)/shard_map/jit(_where)/select_n | solution.py:32
  26.3 2.0 %fusion.80 = f32[384,256]{1,0:T(8,128)} fusion(bf16[384,256]{1,0:T(8,128)(2,1)} %fusion.5, bf16[1,1,1,384,384]{4,3,2,1,0:T(8,128)(2,1)S(1)} %get-tuple-element.8, bf16[1,1,1,384,384]{4,3,2,1,0:T(8,128)(2,1)S(1)} %get-tuple-element.6, pred[]{:T(512)S(6)} %eq.84), kind=kOutput, calls=%fused_computation.117 | convolution fusion | flops 75644928 | bytes 1179649 | tf_op jit(solution)/shard_map/dot_general | solution.py:15
  28.3 1.9 %fusion.82 = f32[384,256]{1,0:T(8,128)} fusion(bf16[384,256]{1,0:T(8,128)(2,1)} %fusion, bf16[1,1,1,384,384]{4,3,2,1,0:T(8,128)(2,1)S(1)} %get-tuple-element.8, bf16[1,1,1,384,384]{4,3,2,1,0:T(8,128)(2,1)S(1)} %get-tuple-element.6, pred[]{:T(512)S(6)} %eq.84), kind=kOutput, calls=%fused_computation.119 | convolution fusion | flops 75644928 | bytes 1179649 | tf_op jit(solution)/shard_map/dot_general | solution.py:15
  30.2 1.2 fusion.50
  31.4 1.9 %fusion.52 = f32[384,256]{1,0:T(8,128)} fusion(bf16[384,256]{1,0:T(8,128)(2,1)} %fusion.10, bf16[1,1,1,384,384]{4,3,2,1,0:T(8,128)(2,1)S(1)} %get-tuple-element.9, bf16[1,1,1,384,384]{4,3,2,1,0:T(8,128)(2,1)S(1)} %get-tuple-element.7, pred[]{:T(512)S(6)} %eq.84), kind=kOutput, calls=%fused_computation.89 | convolution fusion | flops 75644928 | bytes 1179649 | tf_op jit(solution)/shard_map/dot_general | solution.py:15
  35.2 2.4 %fusion.156 = (bf16[1,1,1024,384]{3,2,1,0:T(8,128)(2,1)}, bf16[1,1,1024,384]{3,2,1,0:T(8,128)(2,1)S(1)}) fusion(bf16[1,2,1024,384]{3,2,1,0:T(8,128)(2,1)} %param.9), kind=kLoop, calls=%fused_computation.227 | loop fusion | bytes 3145728 | tf_op jit(solution)/shard_map/slice | solution.py:57
  37.6 1.9 %broadcast_select_fusion.27 = (bf16[1,1,1,384,384]{4,3,2,1,0:T(8,128)(2,1)S(1)}, bf16[1,1,1,384,384]{4,3,2,1,0:T(8,128)(2,1)S(1)}, bf16[1,1,1,384,384]{4,3,2,1,0...) fusion(pred[]{:T(512)} %bitcast.1, ...), kind=kLoop, calls=%fused_computation.160 | loop fusion | flops 1032192 | bytes 4423685 | tf_op jit(solution)/shard_map/jit(_where)/select_n | solution.py:33
  39.5 1.3 %broadcast_select_fusion.8 = (bf16[1,1,1,384,384]{4,3,2,1,0:T(8,128)(2,1)S(1)}, bf16[1,1,1,384,384]{4,3,2,1,0:T(8,128)(2,1)S(1)}) fusion(pred[]{:T(512)} %bitcast.27, bf16[1,5,2,384,768]{4,3,2,1,0:T(8,128)(2,1)} %param.7), kind=kLoop, calls=%fused_computation.141 | loop fusion | flops 294912 | bytes 1769473 | tf_op jit(solution)/shard_map/jit(_where)/select_n | solution.py:32
  40.8 1.2 fusion.11
  42.0 3.1 %collective-permute-start.15 = (bf16[384,256]{1,0:T(8,128)(2,1)S(1)}, bf16[384,256]{1,0:T(8,128)(2,1)S(1)}, u32[]{:S(2)}, u32[]{:S(2)}) collective-permute-start(bf16[384,256]{1,0:T(8,128)(2,1)S(1)} %fusion.11), channel_id=1, source_target_pairs={{0,2},{1,3},{2,0},{3,1},{4,6},{5,7},{6,4},{7,5},{8,10},{9,11},{10,... | collective-permute-start | bytes 589832 | tf_op jit(solution)/shard_map/ppermute | solution.py:11
  45.1 1.2 fusion.1
  46.4 1.2 fusion.6
  47.5 2.1 %collective-permute-start.8 = (bf16[384,256]{1,0:T(8,128)(2,1)S(1)}, bf16[384,256]{1,0:T(8,128)(2,1)S(1)}, u32[]{:S(2)}, u32[]{:S(2)}) collective-permute-start(bf16[384,256]{1,0:T(8,128)(2,1)S(1)} %fusion.6), channel_id=1, source_target_pairs={{0,2},{1,3},{2,0},{3,1},{4,6},{5,7},{6,4},{7,5},{8,10},{9,11},{10,... | collective-permute-start | bytes 589832 | tf_op jit(solution)/shard_map/ppermute | solution.py:11
  51.3 3.1 %collective-permute-start.16 = (bf16[384,256]{1,0:T(8,128)(2,1)S(1)}, bf16[384,256]{1,0:T(8,128)(2,1)S(1)}, u32[]{:S(2)}, u32[]{:S(2)}) collective-permute-start(bf16[384,256]{1,0:T(8,128)(2,1)S(1)} %fusion.12), channel_id=1, source_target_pairs={{0,4},{1,5},{2,6},{3,7},{4,0},{5,1},{6,2},{7,3},{8,12},{9,13},{10,... | collective-permute-start | bytes 589832 | tf_op jit(solution)/shard_map/ppermute | solution.py:11
  54.4 12.6 %collective-permute-done.22 = bf16[384,256]{1,0:T(8,128)(2,1)S(1)} collective-permute-done((bf16[384,256]{1,0:T(8,128)(2,1)S(1)}, bf16[384,256]{1,0:T(8,128)(2,1)S(1)}, u32[]{:S(2)}, u32[]{:S(2)}) %collective-permute-start.22) | collective-permute-done | bytes 196640 | tf_op jit(solution)/shard_map/ppermute | solution.py:11
  67.3 1.9 %collective-permute-start.23 = (bf16[384,256]{1,0:T(8,128)(2,1)S(1)}, bf16[384,256]{1,0:T(8,128)(2,1)S(1)}, u32[]{:S(2)}, u32[]{:S(2)}) collective-permute-start(bf16[384,256]{1,0:T(8,128)(2,1)S(1)} %fusion.17), channel_id=1, source_target_pairs={{0,4},{1,5},{2,6},{3,7},{4,0},{5,1},{6,2},{7,3},{8,12},{9,13},{10,... | collective-permute-start | bytes 589832 | tf_op jit(solution)/shard_map/ppermute | solution.py:11
  69.4 1.1 collective-permute-start.2
  71.4 1.9 %collective-permute-start.9 = (bf16[384,256]{1,0:T(8,128)(2,1)S(1)}, bf16[384,256]{1,0:T(8,128)(2,1)S(1)}, u32[]{:S(2)}, u32[]{:S(2)}) collective-permute-start(bf16[384,256]{1,0:T(8,128)(2,1)S(1)} %fusion.7), channel_id=1, source_target_pairs={{0,4},{1,5},{2,6},{3,7},{4,0},{5,1},{6,2},{7,3},{8,12},{9,13},{10,... | collective-permute-start | bytes 589832 | tf_op jit(solution)/shard_map/ppermute | solution.py:11
  74.2 18.1 %collective-permute-done.2 = bf16[384,256]{1,0:T(8,128)(2,1)S(1)} collective-permute-done((bf16[384,256]{1,0:T(8,128)(2,1)S(1)}, bf16[384,256]{1,0:T(8,128)(2,1)S(1)}, u32[]{:S(2)}, u32[]{:S(2)}) %collective-permute-start.2) | collective-permute-done | bytes 196640 | tf_op jit(solution)/shard_map/ppermute | solution.py:11
  92.7 2.9 %collective-permute-done.9 = bf16[384,256]{1,0:T(8,128)(2,1)S(1)} collective-permute-done((bf16[384,256]{1,0:T(8,128)(2,1)S(1)}, bf16[384,256]{1,0:T(8,128)(2,1)S(1)}, u32[]{:S(2)}, u32[]{:S(2)}) %collective-permute-start.9) | collective-permute-done | bytes 196640 | tf_op jit(solution)/shard_map/ppermute | solution.py:11
  96.7 0.6 collective-permute-start.24
  102.2 2.3 %collective-permute-start.18 = (bf16[256,256]{0,1:T(8,128)(2,1)S(1)}, bf16[256,256]{0,1:T(8,128)(2,1)S(1)}, u32[]{:S(2)}, u32[]{:S(2)}) collective-permute-start(bf16[256,256]{0,1:T(8,128)(2,1)S(1)} %convolution_convert_fusion.9), channel_id=1, source_target_pairs={{0,24},{8,16},{16,8},{24,0},{1,25},{9,17},{17,9},{25,1},{2,26},{10... | collective-permute-start | bytes 393224 | tf_op jit(solution)/shard_map/ppermute | solution.py:11
  104.6 0.5 collective-permute-start.19
  105.1 0.7 collective-permute-start.20
  105.8 2.3 %collective-permute-start.4 = (bf16[256,256]{0,1:T(8,128)(2,1)S(1)}, bf16[256,256]{0,1:T(8,128)(2,1)S(1)}, u32[]{:S(2)}, u32[]{:S(2)}) collective-permute-start(bf16[256,256]{0,1:T(8,128)(2,1)S(1)} %convolution_convert_fusion.15), channel_id=1, source_target_pairs={{0,24},{8,16},{16,8},{24,0},{1,25},{9,17},{17,9},{25,1},{2,26},{10... | collective-permute-start | bytes 393224 | tf_op jit(solution)/shard_map/ppermute | solution.py:11
  108.1 0.5 collective-permute-start.5
  109.1 1.8 %collective-permute-start.6 = (bf16[256,256]{0,1:T(8,128)(2,1)S(1)}, bf16[256,256]{0,1:T(8,128)(2,1)S(1)}, u32[]{:S(2)}, u32[]{:S(2)}) collective-permute-start(bf16[256,256]{0,1:T(8,128)(2,1)S(1)} %convolution_convert_fusion.13), channel_id=1, source_target_pairs={{0,8},{8,0},{16,24},{24,16},{1,9},{9,1},{17,25},{25,17},{2,10},{10... | collective-permute-start | bytes 393224 | tf_op jit(solution)/shard_map/ppermute | solution.py:11
  110.9 1.7 %collective-permute-done.19 = bf16[256,256]{0,1:T(8,128)(2,1)S(1)} collective-permute-done((bf16[256,256]{0,1:T(8,128)(2,1)S(1)}, bf16[256,256]{0,1:T(8,128)(2,1)S(1)}, u32[]{:S(2)}, u32[]{:S(2)}) %collective-permute-start.19) | collective-permute-done | bytes 131104 | tf_op jit(solution)/shard_map/ppermute | solution.py:11
  112.6 2.2 %collective-permute-start.11 = (bf16[256,256]{0,1:T(8,128)(2,1)S(1)}, bf16[256,256]{0,1:T(8,128)(2,1)S(1)}, u32[]{:S(2)}, u32[]{:S(2)}) collective-permute-start(bf16[256,256]{0,1:T(8,128)(2,1)S(1)} %convolution_convert_fusion.12), channel_id=1, source_target_pairs={{0,24},{8,16},{16,8},{24,0},{1,25},{9,17},{17,9},{25,1},{2,26},{10... | collective-permute-start | bytes 393224 | tf_op jit(solution)/shard_map/ppermute | solution.py:11
  115.6 0.9 collective-permute-start.13
  116.5 1.7 %collective-permute-done.5 = bf16[256,256]{0,1:T(8,128)(2,1)S(1)} collective-permute-done((bf16[256,256]{0,1:T(8,128)(2,1)S(1)}, bf16[256,256]{0,1:T(8,128)(2,1)S(1)}, u32[]{:S(2)}, u32[]{:S(2)}) %collective-permute-start.5) | collective-permute-done | bytes 131104 | tf_op jit(solution)/shard_map/ppermute | solution.py:11
  118.2 2.2 %collective-permute-start.25 = (bf16[256,256]{0,1:T(8,128)(2,1)S(1)}, bf16[256,256]{0,1:T(8,128)(2,1)S(1)}, u32[]{:S(2)}, u32[]{:S(2)}) collective-permute-start(bf16[256,256]{0,1:T(8,128)(2,1)S(1)} %convolution_convert_fusion.6), channel_id=1, source_target_pairs={{0,24},{8,16},{16,8},{24,0},{1,25},{9,17},{17,9},{25,1},{2,26},{10... | collective-permute-start | bytes 393224 | tf_op jit(solution)/shard_map/ppermute | solution.py:11
  121.2 1.0 collective-permute-start.27
  122.1 2.6 %collective-permute-done.12 = bf16[256,256]{0,1:T(8,128)(2,1)S(1)} collective-permute-done((bf16[256,256]{0,1:T(8,128)(2,1)S(1)}, bf16[256,256]{0,1:T(8,128)(2,1)S(1)}, u32[]{:S(2)}, u32[]{:S(2)}) %collective-permute-start.12) | collective-permute-done | bytes 131104 | tf_op jit(solution)/shard_map/ppermute | solution.py:11
  125.0 1.5 %collective-permute-done.25 = bf16[256,256]{0,1:T(8,128)(2,1)S(1)} collective-permute-done((bf16[256,256]{0,1:T(8,128)(2,1)S(1)}, bf16[256,256]{0,1:T(8,128)(2,1)S(1)}, u32[]{:S(2)}, u32[]{:S(2)}) %collective-permute-start.25) | collective-permute-done | bytes 131104 | tf_op jit(solution)/shard_map/ppermute | solution.py:11
  126.5 1.8 %collective-permute-done.26 = bf16[256,256]{0,1:T(8,128)(2,1)S(1)} collective-permute-done((bf16[256,256]{0,1:T(8,128)(2,1)S(1)}, bf16[256,256]{0,1:T(8,128)(2,1)S(1)}, u32[]{:S(2)}, u32[]{:S(2)}) %collective-permute-start.26) | collective-permute-done | bytes 131104 | tf_op jit(solution)/shard_map/ppermute | solution.py:11
  128.6 1.0 copy.18
  (89 shorter events, 14.6 us)
Async XLA Ops:
  0.0 13.5 %copy-start.5 = (bf16[1,2,384,1024]{3,2,1,0:T(8,128)(2,1)S(1)}, bf16[1,2,384,1024]{3,2,1,0:T(8,128)(2,1)}, u32[]{:S(2)}) copy-start(bf16[1,2,384,1024]{3,2,1,0:T(8,128)(2,1)} %param.6) | copy-start | bytes 4718596
  0.0 13.5 %copy-start.4 = (bf16[1,2,1024,512]{3,2,1,0:T(8,128)(2,1)S(1)}, bf16[1,2,1024,512]{3,2,1,0:T(8,128)(2,1)}, u32[]{:S(2)}) copy-start(bf16[1,2,1024,512]{3,2,1,0:T(8,128)(2,1)} %param.5) | copy-start | bytes 6291460
  9.0 37.3 %collective-permute-start.7 = (bf16[384,256]{1,0:T(8,128)(2,1)}, bf16[384,256]{1,0:T(8,128)(2,1)}, u32[]{:S(2)}, u32[]{:S(2)}) collective-permute-start(bf16[384,256]{1,0:T(8,128)(2,1)} %fusion.5), channel_id=1, source_target_pairs={{0,1},{1,0},{2,3},{3,2},{4,5},{5,4},{6,7},{7,6},{8,9},{9,8},{10,11... | collective-permute-start | bytes 589832 | tf_op jit(solution)/shard_map/ppermute | solution.py:11
  13.5 36.7 %collective-permute-start.21 = (bf16[384,256]{1,0:T(8,128)(2,1)}, bf16[384,256]{1,0:T(8,128)(2,1)S(1)}, u32[]{:S(2)}, u32[]{:S(2)}) collective-permute-start(bf16[384,256]{1,0:T(8,128)(2,1)} %fusion.15), channel_id=1, source_target_pairs={{0,1},{1,0},{2,3},{3,2},{4,5},{5,4},{6,7},{7,6},{8,9},{9,8},{10,11... | collective-permute-start | bytes 589832 | tf_op jit(solution)/shard_map/ppermute | solution.py:11
  17.6 27.5 %collective-permute-start = (bf16[384,256]{1,0:T(8,128)(2,1)}, bf16[384,256]{1,0:T(8,128)(2,1)}, u32[]{:S(2)}, u32[]{:S(2)}) collective-permute-start(bf16[384,256]{1,0:T(8,128)(2,1)} %fusion), channel_id=1, source_target_pairs={{0,1},{1,0},{2,3},{3,2},{4,5},{5,4},{6,7},{7,6},{8,9},{9,8},{10,11... | collective-permute-start | bytes 589832 | tf_op jit(solution)/shard_map/ppermute | solution.py:11
  21.4 19.4 %collective-permute-start.14 = (bf16[384,256]{1,0:T(8,128)(2,1)}, bf16[384,256]{1,0:T(8,128)(2,1)}, u32[]{:S(2)}, u32[]{:S(2)}) collective-permute-start(bf16[384,256]{1,0:T(8,128)(2,1)} %fusion.10), channel_id=1, source_target_pairs={{0,1},{1,0},{2,3},{3,2},{4,5},{5,4},{6,7},{7,6},{8,9},{9,8},{10,11... | collective-permute-start | bytes 589832 | tf_op jit(solution)/shard_map/ppermute | solution.py:11
  37.6 3.2 %copy-start.3 = (f32[384,256]{1,0:T(8,128)S(1)}, f32[384,256]{1,0:T(8,128)}, u32[]{:S(2)}) copy-start(f32[384,256]{1,0:T(8,128)} %fusion.52) | copy-start | bytes 1179652
  37.6 7.5 %copy-start.2 = (f32[384,256]{1,0:T(8,128)S(1)}, f32[384,256]{1,0:T(8,128)}, u32[]{:S(2)}) copy-start(f32[384,256]{1,0:T(8,128)} %fusion.82) | copy-start | bytes 1179652
  37.6 8.8 %copy-start.1 = (f32[384,256]{1,0:T(8,128)S(1)}, f32[384,256]{1,0:T(8,128)}, u32[]{:S(2)}) copy-start(f32[384,256]{1,0:T(8,128)} %fusion.80) | copy-start | bytes 1179652
  42.0 9.1 %collective-permute-start.15 = (bf16[384,256]{1,0:T(8,128)(2,1)S(1)}, bf16[384,256]{1,0:T(8,128)(2,1)S(1)}, u32[]{:S(2)}, u32[]{:S(2)}) collective-permute-start(bf16[384,256]{1,0:T(8,128)(2,1)S(1)} %fusion.11), channel_id=1, source_target_pairs={{0,2},{1,3},{2,0},{3,1},{4,6},{5,7},{6,4},{7,5},{8,10},{9,11},{10,... | collective-permute-start | bytes 589832 | tf_op jit(solution)/shard_map/ppermute | solution.py:11
  46.3 22.9 %collective-permute-start.1 = (bf16[384,256]{1,0:T(8,128)(2,1)S(1)}, bf16[384,256]{1,0:T(8,128)(2,1)S(1)}, u32[]{:S(2)}, u32[]{:S(2)}) collective-permute-start(bf16[384,256]{1,0:T(8,128)(2,1)S(1)} %fusion.1), channel_id=1, source_target_pairs={{0,2},{1,3},{2,0},{3,1},{4,6},{5,7},{6,4},{7,5},{8,10},{9,11},{10,... | collective-permute-start | bytes 589832 | tf_op jit(solution)/shard_map/ppermute | solution.py:11
  47.5 23.6 %collective-permute-start.8 = (bf16[384,256]{1,0:T(8,128)(2,1)S(1)}, bf16[384,256]{1,0:T(8,128)(2,1)S(1)}, u32[]{:S(2)}, u32[]{:S(2)}) collective-permute-start(bf16[384,256]{1,0:T(8,128)(2,1)S(1)} %fusion.6), channel_id=1, source_target_pairs={{0,2},{1,3},{2,0},{3,1},{4,6},{5,7},{6,4},{7,5},{8,10},{9,11},{10,... | collective-permute-start | bytes 589832 | tf_op jit(solution)/shard_map/ppermute | solution.py:11
  50.4 16.6 %collective-permute-start.22 = (bf16[384,256]{1,0:T(8,128)(2,1)S(1)}, bf16[384,256]{1,0:T(8,128)(2,1)S(1)}, u32[]{:S(2)}, u32[]{:S(2)}) collective-permute-start(bf16[384,256]{1,0:T(8,128)(2,1)S(1)} %fusion.16), channel_id=1, source_target_pairs={{0,2},{1,3},{2,0},{3,1},{4,6},{5,7},{6,4},{7,5},{8,10},{9,11},{10,... | collective-permute-start | bytes 589832 | tf_op jit(solution)/shard_map/ppermute | solution.py:11
  51.3 22.5 %collective-permute-start.16 = (bf16[384,256]{1,0:T(8,128)(2,1)S(1)}, bf16[384,256]{1,0:T(8,128)(2,1)S(1)}, u32[]{:S(2)}, u32[]{:S(2)}) collective-permute-start(bf16[384,256]{1,0:T(8,128)(2,1)S(1)} %fusion.12), channel_id=1, source_target_pairs={{0,4},{1,5},{2,6},{3,7},{4,0},{5,1},{6,2},{7,3},{8,12},{9,13},{10,... | collective-permute-start | bytes 589832 | tf_op jit(solution)/shard_map/ppermute | solution.py:11
  67.3 29.2 %collective-permute-start.23 = (bf16[384,256]{1,0:T(8,128)(2,1)S(1)}, bf16[384,256]{1,0:T(8,128)(2,1)S(1)}, u32[]{:S(2)}, u32[]{:S(2)}) collective-permute-start(bf16[384,256]{1,0:T(8,128)(2,1)S(1)} %fusion.17), channel_id=1, source_target_pairs={{0,4},{1,5},{2,6},{3,7},{4,0},{5,1},{6,2},{7,3},{8,12},{9,13},{10,... | collective-permute-start | bytes 589832 | tf_op jit(solution)/shard_map/ppermute | solution.py:11
  69.4 22.9 %collective-permute-start.2 = (bf16[384,256]{1,0:T(8,128)(2,1)S(1)}, bf16[384,256]{1,0:T(8,128)(2,1)S(1)}, u32[]{:S(2)}, u32[]{:S(2)}) collective-permute-start(bf16[384,256]{1,0:T(8,128)(2,1)S(1)} %fusion.2), channel_id=1, source_target_pairs={{0,4},{1,5},{2,6},{3,7},{4,0},{5,1},{6,2},{7,3},{8,12},{9,13},{10,... | collective-permute-start | bytes 589832 | tf_op jit(solution)/shard_map/ppermute | solution.py:11
  71.4 24.2 %collective-permute-start.9 = (bf16[384,256]{1,0:T(8,128)(2,1)S(1)}, bf16[384,256]{1,0:T(8,128)(2,1)S(1)}, u32[]{:S(2)}, u32[]{:S(2)}) collective-permute-start(bf16[384,256]{1,0:T(8,128)(2,1)S(1)} %fusion.7), channel_id=1, source_target_pairs={{0,4},{1,5},{2,6},{3,7},{4,0},{5,1},{6,2},{7,3},{8,12},{9,13},{10,... | collective-permute-start | bytes 589832 | tf_op jit(solution)/shard_map/ppermute | solution.py:11
  74.1 23.7 %collective-permute-start.17 = (bf16[384,256]{1,0:T(8,128)(2,1)S(1)}, bf16[384,256]{1,0:T(8,128)(2,1)S(1)}, u32[]{:S(2)}, u32[]{:S(2)}) collective-permute-start(bf16[384,256]{1,0:T(8,128)(2,1)S(1)} %fusion.13), channel_id=1, source_target_pairs={{0,1},{1,0},{2,3},{3,2},{4,5},{5,4},{6,7},{7,6},{8,9},{9,8},{10,11... | collective-permute-start | bytes 589832 | tf_op jit(solution)/shard_map/ppermute | solution.py:11
  92.6 6.4 %copy-start = (bf16[1,1,1024,384]{3,2,1,0:T(8,128)(2,1)S(1)}, bf16[1,1,1024,384]{3,2,1,0:T(8,128)(2,1)}, u32[]{:S(2)}) copy-start(bf16[1,1,1024,384]{3,2,1,0:T(8,128)(2,1)} %get-tuple-element.21) | copy-start | bytes 2359300
  92.6 6.1 %collective-permute-start.3 = (bf16[384,256]{1,0:T(8,128)(2,1)S(1)}, bf16[384,256]{1,0:T(8,128)(2,1)S(1)}, u32[]{:S(2)}, u32[]{:S(2)}) collective-permute-start(bf16[384,256]{1,0:T(8,128)(2,1)S(1)} %fusion.3), channel_id=1, source_target_pairs={{0,1},{1,0},{2,3},{3,2},{4,5},{5,4},{6,7},{7,6},{8,9},{9,8},{10,11... | collective-permute-start | bytes 589832 | tf_op jit(solution)/shard_map/ppermute | solution.py:11
  95.8 4.4 %collective-permute-start.10 = (bf16[384,256]{1,0:T(8,128)(2,1)S(1)}, bf16[384,256]{1,0:T(8,128)(2,1)S(1)}, u32[]{:S(2)}, u32[]{:S(2)}) collective-permute-start(bf16[384,256]{1,0:T(8,128)(2,1)S(1)} %fusion.8), channel_id=1, source_target_pairs={{0,1},{1,0},{2,3},{3,2},{4,5},{5,4},{6,7},{7,6},{8,9},{9,8},{10,11... | collective-permute-start | bytes 589832 | tf_op jit(solution)/shard_map/ppermute | solution.py:11
  96.7 4.7 %collective-permute-start.24 = (bf16[384,256]{1,0:T(8,128)(2,1)S(1)}, bf16[384,256]{1,0:T(8,128)(2,1)S(1)}, u32[]{:S(2)}, u32[]{:S(2)}) collective-permute-start(bf16[384,256]{1,0:T(8,128)(2,1)S(1)} %fusion.18), channel_id=1, source_target_pairs={{0,1},{1,0},{2,3},{3,2},{4,5},{5,4},{6,7},{7,6},{8,9},{9,8},{10,11... | collective-permute-start | bytes 589832 | tf_op jit(solution)/shard_map/ppermute | solution.py:11
  102.2 6.9 %collective-permute-start.18 = (bf16[256,256]{0,1:T(8,128)(2,1)S(1)}, bf16[256,256]{0,1:T(8,128)(2,1)S(1)}, u32[]{:S(2)}, u32[]{:S(2)}) collective-permute-start(bf16[256,256]{0,1:T(8,128)(2,1)S(1)} %convolution_convert_fusion.9), channel_id=1, source_target_pairs={{0,24},{8,16},{16,8},{24,0},{1,25},{9,17},{17,9},{25,1},{2,26},{10... | collective-permute-start | bytes 393224 | tf_op jit(solution)/shard_map/ppermute | solution.py:11
  104.6 8.0 %collective-permute-start.19 = (bf16[256,256]{0,1:T(8,128)(2,1)S(1)}, bf16[256,256]{0,1:T(8,128)(2,1)S(1)}, u32[]{:S(2)}, u32[]{:S(2)}) collective-permute-start(bf16[256,256]{0,1:T(8,128)(2,1)S(1)} %convolution_convert_fusion.8), channel_id=1, source_target_pairs={{0,16},{8,24},{16,0},{24,8},{1,17},{9,25},{17,1},{25,9},{2,18},{10... | collective-permute-start | bytes 393224 | tf_op jit(solution)/shard_map/ppermute | solution.py:11
  105.1 9.7 %collective-permute-start.20 = (bf16[256,256]{0,1:T(8,128)(2,1)S(1)}, bf16[256,256]{0,1:T(8,128)(2,1)S(1)}, u32[]{:S(2)}, u32[]{:S(2)}) collective-permute-start(bf16[256,256]{0,1:T(8,128)(2,1)S(1)} %convolution_convert_fusion.7), channel_id=1, source_target_pairs={{0,8},{8,0},{16,24},{24,16},{1,9},{9,1},{17,25},{25,17},{2,10},{10... | collective-permute-start | bytes 393224 | tf_op jit(solution)/shard_map/ppermute | solution.py:11
  105.8 9.8 %collective-permute-start.4 = (bf16[256,256]{0,1:T(8,128)(2,1)S(1)}, bf16[256,256]{0,1:T(8,128)(2,1)S(1)}, u32[]{:S(2)}, u32[]{:S(2)}) collective-permute-start(bf16[256,256]{0,1:T(8,128)(2,1)S(1)} %convolution_convert_fusion.15), channel_id=1, source_target_pairs={{0,24},{8,16},{16,8},{24,0},{1,25},{9,17},{17,9},{25,1},{2,26},{10... | collective-permute-start | bytes 393224 | tf_op jit(solution)/shard_map/ppermute | solution.py:11
  108.1 10.1 %collective-permute-start.5 = (bf16[256,256]{0,1:T(8,128)(2,1)S(1)}, bf16[256,256]{0,1:T(8,128)(2,1)S(1)}, u32[]{:S(2)}, u32[]{:S(2)}) collective-permute-start(bf16[256,256]{0,1:T(8,128)(2,1)S(1)} %convolution_convert_fusion.14), channel_id=1, source_target_pairs={{0,16},{8,24},{16,0},{24,8},{1,17},{9,25},{17,1},{25,9},{2,18},{10... | collective-permute-start | bytes 393224 | tf_op jit(solution)/shard_map/ppermute | solution.py:11
  109.1 11.3 %collective-permute-start.6 = (bf16[256,256]{0,1:T(8,128)(2,1)S(1)}, bf16[256,256]{0,1:T(8,128)(2,1)S(1)}, u32[]{:S(2)}, u32[]{:S(2)}) collective-permute-start(bf16[256,256]{0,1:T(8,128)(2,1)S(1)} %convolution_convert_fusion.13), channel_id=1, source_target_pairs={{0,8},{8,0},{16,24},{24,16},{1,9},{9,1},{17,25},{25,17},{2,10},{10... | collective-permute-start | bytes 393224 | tf_op jit(solution)/shard_map/ppermute | solution.py:11
  112.6 8.6 %collective-permute-start.11 = (bf16[256,256]{0,1:T(8,128)(2,1)S(1)}, bf16[256,256]{0,1:T(8,128)(2,1)S(1)}, u32[]{:S(2)}, u32[]{:S(2)}) collective-permute-start(bf16[256,256]{0,1:T(8,128)(2,1)S(1)} %convolution_convert_fusion.12), channel_id=1, source_target_pairs={{0,24},{8,16},{16,8},{24,0},{1,25},{9,17},{17,9},{25,1},{2,26},{10... | collective-permute-start | bytes 393224 | tf_op jit(solution)/shard_map/ppermute | solution.py:11
  114.8 10.0 %collective-permute-start.12 = (bf16[256,256]{0,1:T(8,128)(2,1)S(1)}, bf16[256,256]{0,1:T(8,128)(2,1)S(1)}, u32[]{:S(2)}, u32[]{:S(2)}) collective-permute-start(bf16[256,256]{0,1:T(8,128)(2,1)S(1)} %convolution_convert_fusion.11), channel_id=1, source_target_pairs={{0,16},{8,24},{16,0},{24,8},{1,17},{9,25},{17,1},{25,9},{2,18},{10... | collective-permute-start | bytes 393224 | tf_op jit(solution)/shard_map/ppermute | solution.py:11
  115.6 9.2 %collective-permute-start.13 = (bf16[256,256]{0,1:T(8,128)(2,1)S(1)}, bf16[256,256]{0,1:T(8,128)(2,1)S(1)}, u32[]{:S(2)}, u32[]{:S(2)}) collective-permute-start(bf16[256,256]{0,1:T(8,128)(2,1)S(1)} %convolution_convert_fusion.10), channel_id=1, source_target_pairs={{0,8},{8,0},{16,24},{24,16},{1,9},{9,1},{17,25},{25,17},{2,10},{10... | collective-permute-start | bytes 393224 | tf_op jit(solution)/shard_map/ppermute | solution.py:11
  118.2 8.3 %collective-permute-start.25 = (bf16[256,256]{0,1:T(8,128)(2,1)S(1)}, bf16[256,256]{0,1:T(8,128)(2,1)S(1)}, u32[]{:S(2)}, u32[]{:S(2)}) collective-permute-start(bf16[256,256]{0,1:T(8,128)(2,1)S(1)} %convolution_convert_fusion.6), channel_id=1, source_target_pairs={{0,24},{8,16},{16,8},{24,0},{1,25},{9,17},{17,9},{25,1},{2,26},{10... | collective-permute-start | bytes 393224 | tf_op jit(solution)/shard_map/ppermute | solution.py:11
  120.4 7.9 %collective-permute-start.26 = (bf16[256,256]{0,1:T(8,128)(2,1)S(1)}, bf16[256,256]{0,1:T(8,128)(2,1)S(1)}, u32[]{:S(2)}, u32[]{:S(2)}) collective-permute-start(bf16[256,256]{0,1:T(8,128)(2,1)S(1)} %convolution_convert_fusion.5), channel_id=1, source_target_pairs={{0,16},{8,24},{16,0},{24,8},{1,17},{9,25},{17,1},{25,9},{2,18},{10... | collective-permute-start | bytes 393224 | tf_op jit(solution)/shard_map/ppermute | solution.py:11
  121.2 7.1 %collective-permute-start.27 = (bf16[256,256]{0,1:T(8,128)(2,1)S(1)}, bf16[256,256]{0,1:T(8,128)(2,1)S(1)}, u32[]{:S(2)}, u32[]{:S(2)}) collective-permute-start(bf16[256,256]{0,1:T(8,128)(2,1)S(1)} %convolution_convert_fusion.4), channel_id=1, source_target_pairs={{0,8},{8,0},{16,24},{24,16},{1,9},{9,1},{17,25},{25,17},{2,10},{10... | collective-permute-start | bytes 393224 | tf_op jit(solution)/shard_map/ppermute | solution.py:11

commit v2 on v0

v2 whole, which is shorter than its diff:
```python
import functools

import jax
import jax.numpy as jnp
from jax import lax
from jax.experimental import pallas as pl
from jax.experimental.pallas import tpu as pltpu
from jax.sharding import PartitionSpec as P

HALVES = 2
BF16 = jnp.bfloat16
ANY = pl.BlockSpec(memory_space=pl.ANY)
VMEM = pl.BlockSpec(memory_space=pltpu.VMEM)


def dot(a, b):
    return jnp.dot(a, b, preferred_element_type=jnp.float32)


def in_vmem(*shape, dtype=BF16):
    return pltpu.VMEM(shape, dtype)


def here(value):
    return pltpu.with_memory_space_constraint(value, pltpu.VMEM)


def in_hbm(value):
    return pltpu.with_memory_space_constraint(value, pltpu.HBM)


def call(kernel, name, in_specs, out_shape, scratch, args, flops=0, bytes_accessed=0, limit=None, after=()):
    many = isinstance(out_shape, (list, tuple))
    count = len(in_specs)

    def body(*refs):
        kernel(*refs[:count], *refs[count + len(after) :])

    args = [*args, *after]
    return pl.pallas_call(
        body,
        name=name,
        in_specs=[*in_specs, *[ANY] * len(after)],
        out_specs=[VMEM] * len(out_shape) if many else VMEM,
        out_shape=out_shape,
        scratch_shapes=scratch,
        compiler_params=pltpu.CompilerParams(vmem_limit_bytes=limit or 8 * 2**20),
        cost_estimate=pl.CostEstimate(flops=flops, bytes_accessed=bytes_accessed, transcendentals=0),
    )(*args)


def partner(value, axis, mask):
    pairs = [(source, source ^ mask) for source in range(lax.axis_size(axis))]
    return lax.ppermute(value, axis, pairs)


def leaf_kernel(excite, leaves, blocks, index, first_ref, second_ref, next_ref, excite_v, leaves_v, blocks_v, index_s, coeff, sems):
    slots, rank = leaves.shape[0], leaves.shape[1]
    width = first_ref.shape[2]
    listing = pltpu.make_async_copy(index, index_s, sems.at[0])
    listing.start()
    loads = []
    for s in range(slots):
        a = pltpu.make_async_copy(leaves.at[s], leaves_v.at[s], sems.at[1 + s])
        b = pltpu.make_async_copy(excite.at[s], excite_v.at[s], sems.at[3 + s])
        a.start()
        b.start()
        loads.append((a, b))
    listing.wait()
    weights = []
    for s in range(slots):
        c = pltpu.make_async_copy(blocks.at[0, index_s[s, 0]], blocks_v.at[s], sems.at[5 + s])
        c.start()
        weights.append(c)
    later = []
    for s in range(slots):
        c = pltpu.make_async_copy(blocks.at[1, index_s[s, 1]], next_ref.at[s], sems.at[7 + s])
        c.start()
        later.append(c)
    for s in range(slots):
        for load in loads[s]:
            load.wait()
        coeff[s * rank : (s + 1) * rank, :] = dot(leaves_v[s], excite_v[s]).astype(BF16)
    for s in range(slots):
        weights[s].wait()
        out = dot(blocks_v[s], coeff[...]).astype(BF16)
        first_ref[s] = out[:, :width]
        second_ref[s] = out[:, width:]
    for c in later:
        c.wait()


def prefetch_kernel(blocks, basis, index, *refs):
    count = blocks.shape[0] - 2
    outs, basis_v, index_s, sems = refs[:count], refs[count], refs[count + 1], refs[count + 2]
    listing = pltpu.make_async_copy(index, index_s, sems.at[0])
    listing.start()
    listing.wait()
    copies = []
    for level in range(count):
        for s in range(2):
            c = pltpu.make_async_copy(
                blocks.at[level + 2, index_s[s, level + 2]], outs[level].at[s], sems.at[1 + 2 * level + s]
            )
            c.start()
            copies.append(c)
    c = pltpu.make_async_copy(basis, basis_v, sems.at[1 + 2 * count])
    c.start()
    copies.append(c)
    for c in copies:
        c.wait()


def mix(weights, own, other, bit, buf):
    rank = own.shape[0]
    upper = (lax.axis_index("box") >> bit) & 1
    buf[pl.ds(pl.multiple_of(upper * rank, rank), rank), :] = own
    buf[pl.ds(pl.multiple_of((1 - upper) * rank, rank), rank), :] = other
    return dot(weights, buf[...]).astype(BF16)


def first_kernel(bit, s, own, other, weights, out, buf):
    out[...] = mix(weights[s], own[s], other[s], bit, buf)


def level_kernel(bit, s, own, other, weights, out, buf):
    out[...] = mix(weights[s], own[...], other[...], bit, buf)


def pair_kernel(bit, s, bit_next, s_next, own, other, weights, own_n, other_n, weights_n, out, out_n, buf, buf_n):
    out[...] = mix(weights[s], own[...], other[...], bit, buf)
    out_n[...] = mix(weights_n[s_next], own_n[s_next], other_n[s_next], bit_next, buf_n)


def last_kernel(bit, s, own, other, weights, basis, *refs):
    pieces, mine, buf = refs[:-2], refs[-2], refs[-1]
    coeff = mix(weights[s], own[...], other[...], bit, buf)
    rows = mine.shape[0]
    me = lax.axis_index("blk")
    for d, piece in enumerate(pieces, 1):
        start = pl.multiple_of((me ^ d) * rows, rows)
        piece[...] = dot(basis[s, pl.ds(start, rows), :], coeff).astype(BF16)
    start = pl.multiple_of(me * rows, rows)
    mine[...] = dot(basis[s, pl.ds(start, rows), :], coeff)


def sum_kernel(places, per, *refs):
    out = refs[-1]
    for at, (s, start, width) in enumerate(places):
        group = refs[at * per : (at + 1) * per]
        total = group[0][...]
        for piece in group[1:]:
            total = total + piece[...].astype(jnp.float32)
        out[s, :, start : start + width] = total.astype(BF16)


def on_device(excitation, leaf_basis, transfer, transfer_index, out_basis):
    excite, leaves, blocks, basis = excitation[0], leaf_basis[0], transfer[0], out_basis[0]
    index = transfer_index[0].T
    slots, rank, points = leaves.shape
    levels = blocks.shape[0]
    columns = excite.shape[2]
    width = columns // HALVES
    n_blk = lax.axis_size("blk")
    rows = basis.shape[1] // n_blk
    nbits = lax.axis_size("box").bit_length() - 1
    bits = [None] + [(level - 1) % nbits for level in range(1, levels)]
    pair = (slots, rank, 2 * rank)

    *coeff1, weights1 = call(
        leaf_kernel,
        "leaf",
        [ANY] * 4,
        [in_vmem(slots, rank, width)] * 2 + [in_vmem(*pair)],
        [
            in_vmem(*excite.shape),
            in_vmem(*leaves.shape),
            in_vmem(*pair),
            pltpu.SMEM(index.shape, jnp.int32),
            in_vmem(2 * rank, columns),
            pltpu.SemaphoreType.DMA((9,)),
        ],
        [in_hbm(excite), in_hbm(leaves), in_hbm(blocks), in_hbm(index)],
        flops=2 * slots * rank * columns * (points + 2 * rank),
        bytes_accessed=6 * 2**20,
        limit=24 * 2**20,
    )
    near1 = [partner(c, "box", 2 ** bits[1]) for c in coeff1]

    chunks = [(h, s) for h in range(HALVES) for s in range(slots)]
    shape = in_vmem(rank, width)
    buf = in_vmem(2 * rank, width)
    work = 4 * rank * rank * width
    touched = 2 * (2 * rank * rank + 3 * rank * width)

    def step(level, j, own, other, after=()):
        return call(
            functools.partial(level_kernel, bits[level], chunks[j][1]),
            f"level{level}_{j}",
            [VMEM] * 3,
            shape,
            [buf],
            [here(own), here(other), here(weights[level])],
            flops=work,
            bytes_accessed=touched,
            after=after,
        )

    h, s = chunks[0]
    coeff2 = call(
        functools.partial(first_kernel, bits[1], s),
        "level1_0",
        [VMEM] * 3,
        shape,
        [buf],
        [here(coeff1[h]), here(near1[h]), here(weights1)],
        flops=work,
        bytes_accessed=touched,
    )
    near2 = partner(coeff2, "box", 2 ** bits[2])
    *weights, basis_v = call(
        prefetch_kernel,
        "prefetch",
        [ANY] * 3,
        [in_vmem(*pair)] * (levels - 2) + [in_vmem(*basis.shape)],
        [pltpu.SMEM(index.shape, jnp.int32), pltpu.SemaphoreType.DMA((2 * levels,))],
        [in_hbm(blocks), in_hbm(basis), in_hbm(index)],
        bytes_accessed=5 * 2**20,
        after=[coeff2],
    )
    weights = [None, weights1] + weights
    coeff3, near3, groups = {}, {}, []

    def finish(j):
        h, s = chunks[j]
        own, other = coeff3[j], near3[j]
        follow = [coeff3[j + 1]] if j + 1 < len(chunks) else []
        for level in range(3, levels - 1):
            own = step(level, j, own, other, follow)
            other = partner(own, "box", 2 ** bits[level + 1])
        *pieces, mine = call(
            functools.partial(last_kernel, bits[levels - 1], s),
            f"last_{j}",
            [VMEM] * 4,
            [in_vmem(rows, width)] * (n_blk - 1) + [in_vmem(rows, width, dtype=jnp.float32)],
            [buf],
            [here(own), here(other), here(weights[levels - 1]), here(basis_v)],
            flops=work + 2 * n_blk * rows * rank * width,
            bytes_accessed=touched + 2 * n_blk * rows * (rank + width),
        )
        got = {d: partner(pieces[d - 1], "blk", d) for d in range(n_blk - 1, 0, -1)}
        groups.extend([mine] + [got[d] for d in range(1, n_blk)])
        return mine

    done = []
    for j in range(len(chunks)):
        if j + 1 < len(chunks):
            h, s = chunks[j + 1]
            coeff3[j], coeff2_next = call(
                functools.partial(pair_kernel, bits[2], chunks[j][1], bits[1], s),
                f"level2_{j}_level1_{j + 1}",
                [VMEM] * 6,
                [shape] * 2,
                [buf] * 2,
                [here(coeff2), here(near2), here(weights[2]), here(coeff1[h]), here(near1[h]), here(weights1)],
                flops=2 * work,
                bytes_accessed=2 * touched,
                after=done[-1:],
            )
        else:
            coeff3[j] = step(2, j, coeff2, near2, done[-1:])
        near3[j] = partner(coeff3[j], "box", 2 ** bits[3])
        if j + 1 < len(chunks):
            coeff2 = coeff2_next
            near2 = partner(coeff2, "box", 2 ** bits[2])
        if j > 0:
            done.append(finish(j - 1))
    finish(len(chunks) - 1)
    return pl.pallas_call(
        functools.partial(sum_kernel, [(s, h * width, width) for h, s in chunks], n_blk),
        name="sum",
        in_specs=[VMEM] * len(groups),
        out_specs=VMEM,
        out_shape=jax.ShapeDtypeStruct((slots, rows, columns), BF16),
        compiler_params=pltpu.CompilerParams(vmem_limit_bytes=16 * 2**20),
    )(*[here(g) for g in groups])


def solution(mesh):
    in_specs = (
        P("blk", "box", None, None),
        P("blk", "box", None, None),
        P("blk", None, "box", None, None),
        P("blk", None, "box"),
        P("blk", "box", None, None),
    )
    out_specs = P("box", "blk", None)
    return jax.shard_map(
        on_device, mesh=mesh, in_specs=in_specs, out_specs=out_specs, check_vma=False
    )
```

time: 147 us -> 92.1 us (0.63)
  between operations: 32.5 us -> 0.19 us
  waiting for transfers between devices: 75.9 us -> 46.5 us
  starting transfers between devices: 7.05 us -> 29.7 us
  matrix products: 18.1 us -> 0 us
  Pallas kernels: 0 us -> 15.6 us
  local copies, waits for them, and re-layouts: 12.7 us -> 0 us
    reduce_scatter x1 -> x0, waiting for transfers between devices: 36.4 us -> none  [on_device(): lax.psum_scatter(jnp.einsum('bqr,brc->qbc', basis, coeff, preferred_eleme...]
    ppermute x8 -> x26, starting transfers between devices: 7.04 us -> 29.7 us  [partner(): return lax.ppermute(value, axis, pairs)]
    dot_general x22 -> x0, matrix products: 18.1 us -> none  [the longest x10 7.16 us: combine(): jnp.dot(matrix[:, rank:], second, preferred_element_type=jnp.float32)]
    pallas_call x0 -> x16, Pallas kernels: none -> 15.6 us  [the longest x15 14.6 us: call(): pl.pallas_call(body, name=name, in_specs=[*in_specs, *[ANY] * len(after)]...]
    ppermute x8 -> x26, waiting for transfers between devices: 39.4 us -> 46.5 us  [partner(): return lax.ppermute(value, axis, pairs)]
    slice x2 -> x0, local copies, waits for them, and re-layouts: 6.61 us -> none  [the longest x1 4.89 us: chosen(): blocks[level]]
    unnamed x10 -> x0, local copies, waits for them, and re-layouts: 2.26 us -> none
    convert_element_type x1 -> x0, local copies, waits for them, and re-layouts: 2.04 us -> none  [on_device(): return jnp.transpose(shares, (1, 0, 2)).astype(jnp.bfloat16)]
  transfers between devices with their start and end apart: 9 -> 26, of which waited for: 6 -> 15; matrix products, arithmetic and copies ran while one was open for 8% -> 0% of each run, Pallas kernels for 0% -> 11%
where the time goes in v2:
time: 92.1 us; the launch traced here: 91.9 us
  waiting for transfers between devices  46.5 us (50%)
  starting transfers between devices  29.7 us (32%)
  Pallas kernels  15.6 us (17%)
    ppermute x26, waiting for transfers between devices, partner(): return lax.ppermute(value, axis, pairs)  46.5 us
    ppermute x26, starting transfers between devices, partner(): return lax.ppermute(value, axis, pairs)  29.7 us
    pallas_call x15, Pallas kernels, call(): pl.pallas_call(body, name=name, in_specs=[*in_specs, *[ANY] * len(after)]...  14.6 us
  transfers between devices with their start and end apart: 26, of which 15 were waited for; matrix products, arithmetic and copies ran while one was open for 0% of the time, Pallas kernels for 11%

profile of v2, /device:TPU:0, one launch (start us, length us, event | category | flops | bytes accessed | tf_op | source)
XLA Modules:
  0.0 91.9 jit_solution(17920940029757447942)
XLA Ops:
  0.0 3.6 %leaf.1 = (bf16[2,384,256]{2,1,0:T(8,128)(2,1)S(1)}, bf16[2,384,256]{2,1,0:T(8,128)(2,1)S(1)}, bf16[2,384,768]{2,1,0:T(8,128)(2,1)S(1)}) custom-call(bf16[2,1024,512]{2,1,0:T(8,128)(2,1)} %bitcast.9, bf16[2,384,1024]{2,1,0:T(8,128)(2,1)} %bitcast.10, bf16[5,2,384,768]{3,2,1,0:T(8,128)(2,1)} %bitcast.7, s32[2,5]{1,0:T(2,128)} %bitcast.12), custom_call_target="tpu_custom_call" | custom-call | flops 1409286144 | bytes 6291456 | tf_op jit(solution)/shard_map/leaf/pallas_call | solution.py:40
  3.6 0.5 collective-permute-start
  4.2 1.3 %collective-permute-done.refs_1_.refs_4_ = bf16[2,384,256]{2,1,0:T(8,128)(2,1)S(1)} collective-permute-done((bf16[2,384,256]{2,1,0:T(8,128)(2,1)S(1)}, bf16[2,384,256]{2,1,0:T(8,128)(2,1)S(1)}, u32[]{:S(2)}, u32[]{:S(2)}) %collective-permute-start) | collective-permute-done | bytes 393248 | tf_op jit(solution)/shard_map/ppermute | solution.py:54
  5.5 0.4 level1_0.1.refs_3_.refs_0_
  5.9 3.0 %collective-permute-start.1 = (bf16[384,256]{1,0:T(8,128)(2,1)S(1)}, bf16[384,256]{1,0:T(8,128)(2,1)S(1)}, u32[]{:S(2)}, u32[]{:S(2)}) collective-permute-start(bf16[384,256]{1,0:T(8,128)(2,1)S(1)} %level1_0.1.refs_3_.refs_0_), channel_id=1, source_target_pairs={{0,2},{1,3},{2,0},{3,1},{4,6},{5,7},{6,4},{7,5},{8,10},{9,11},{10,... | collective-permute-start | bytes 589832 | tf_op jit(solution)/shard_map/ppermute | solution.py:54
  8.9 3.3 %prefetch.1 = (bf16[2,384,768]{2,1,0:T(8,128)(2,1)S(1)}, bf16[2,384,768]{2,1,0:T(8,128)(2,1)S(1)}, bf16[2,384,768]{2,1,0:T(8,128)(2,1)S(1)}, bf16[2,1024,384]{2,1,0:T(8,128)(2,1)S(1)}) custom-call(bf16[5,2,384,768]{3,2,1,0:T(8,128)(2,1)} %bitcast.8, bf16[2,1024,384]{2,1,0:T(8,128)(2,1)} %bitcast.11, s32[2,5]{1,0:T(2,128)} %bitcast.13, ...), custom_call_target="tpu_custom_call" | custom-call | bytes 5242880 | tf_op jit(solution)/shard_map/prefetch/pallas_call | solution.py:40
  12.2 1.9 %collective-permute-done.1.refs_1_ = bf16[384,256]{1,0:T(8,128)(2,1)S(1)} collective-permute-done((bf16[384,256]{1,0:T(8,128)(2,1)S(1)}, bf16[384,256]{1,0:T(8,128)(2,1)S(1)}, u32[]{:S(2)}, u32[]{:S(2)}) %collective-permute-start.1) | collective-permute-done | bytes 196640 | tf_op jit(solution)/shard_map/ppermute | solution.py:54
  14.1 0.5 level2_0_level1_1.1
  14.6 1.8 %collective-permute-start.3 = (bf16[384,256]{1,0:T(8,128)(2,1)S(1)}, bf16[384,256]{1,0:T(8,128)(2,1)S(1)}, u32[]{:S(2)}, u32[]{:S(2)}) collective-permute-start(bf16[384,256]{1,0:T(8,128)(2,1)S(1)} %get-tuple-element.39.refs_0_), channel_id=1, source_target_pairs={{0,2},{1,3},{2,0},{3,1},{4,6},{5,7},{6,4},{7,5},{8,10},{9,11},{10,... | collective-permute-start | bytes 589832 | tf_op jit(solution)/shard_map/ppermute | solution.py:54
  16.4 2.6 %collective-permute-start.2 = (bf16[384,256]{1,0:T(8,128)(2,1)S(1)}, bf16[384,256]{1,0:T(8,128)(2,1)S(1)}, u32[]{:S(2)}, u32[]{:S(2)}) collective-permute-start(bf16[384,256]{1,0:T(8,128)(2,1)S(1)} %get-tuple-element.37.refs_0_), channel_id=1, source_target_pairs={{0,4},{1,5},{2,6},{3,7},{4,0},{5,1},{6,2},{7,3},{8,12},{9,13},{10,... | collective-permute-start | bytes 589832 | tf_op jit(solution)/shard_map/ppermute | solution.py:54
  19.0 6.2 %collective-permute-done.3.refs_1_ = bf16[384,256]{1,0:T(8,128)(2,1)S(1)} collective-permute-done((bf16[384,256]{1,0:T(8,128)(2,1)S(1)}, bf16[384,256]{1,0:T(8,128)(2,1)S(1)}, u32[]{:S(2)}, u32[]{:S(2)}) %collective-permute-start.3) | collective-permute-done | bytes 196640 | tf_op jit(solution)/shard_map/ppermute | solution.py:54
  25.2 0.5 level2_1_level1_2.1
  25.7 1.7 %collective-permute-done.2.refs_1_ = bf16[384,256]{1,0:T(8,128)(2,1)S(1)} collective-permute-done((bf16[384,256]{1,0:T(8,128)(2,1)S(1)}, bf16[384,256]{1,0:T(8,128)(2,1)S(1)}, u32[]{:S(2)}, u32[]{:S(2)}) %collective-permute-start.2) | collective-permute-done | bytes 196640 | tf_op jit(solution)/shard_map/ppermute | solution.py:54
  27.4 0.4 level3_0.1.refs_0_
  27.8 0.5 collective-permute-start.10
  28.4 2.6 %collective-permute-start.9 = (bf16[384,256]{1,0:T(8,128)(2,1)S(1)}, bf16[384,256]{1,0:T(8,128)(2,1)S(1)}, u32[]{:S(2)}, u32[]{:S(2)}) collective-permute-start(bf16[384,256]{1,0:T(8,128)(2,1)S(1)} %get-tuple-element.41.refs_3_.refs_0_), channel_id=1, source_target_pairs={{0,4},{1,5},{2,6},{3,7},{4,0},{5,1},{6,2},{7,3},{8,12},{9,13},{10,... | collective-permute-start | bytes 589832 | tf_op jit(solution)/shard_map/ppermute | solution.py:54
  30.9 1.0 %last_0.1 = (bf16[256,256]{1,0:T(8,128)(2,1)S(1)}, bf16[256,256]{1,0:T(8,128)(2,1)S(1)}, bf16[256,256]{1,0:T(8,128)(2,1)S(1)}, f32[256,256]{1,0:T(8,128)S(1)}) custom-call(bf16[384,256]{1,0:T(8,128)(2,1)S(1)} %level3_0.1.refs_0_, bf16[384,256]{1,0:T(8,128)(2,1)S(1)} %collective-permute-done.5.refs_1_, bf16[2,384,768]{2,1,0:T(8,128)(2,1)S(1)} %get-tuple-element.42.refs_2_, ...), custom_call_target="tpu_custom_call" | custom-call | flops 352321536 | bytes 2490368 | tf_op jit(solution)/shard_map/last_0/pallas_call | solution.py:40
  31.9 7.1 %collective-permute-done.10.refs_1_ = bf16[384,256]{1,0:T(8,128)(2,1)S(1)} collective-permute-done((bf16[384,256]{1,0:T(8,128)(2,1)S(1)}, bf16[384,256]{1,0:T(8,128)(2,1)S(1)}, u32[]{:S(2)}, u32[]{:S(2)}) %collective-permute-start.10) | collective-permute-done | bytes 196640 | tf_op jit(solution)/shard_map/ppermute | solution.py:54
  39.1 0.5 level2_2_level1_3.1
  39.6 0.9 collective-permute-done.9.refs_1_
  40.5 0.4 level3_1.1.refs_0_
  41.3 2.6 %collective-permute-start.15 = (bf16[384,256]{1,0:T(8,128)(2,1)S(1)}, bf16[384,256]{1,0:T(8,128)(2,1)S(1)}, u32[]{:S(2)}, u32[]{:S(2)}) collective-permute-start(bf16[384,256]{1,0:T(8,128)(2,1)S(1)} %get-tuple-element.49.refs_3_.refs_0_), channel_id=1, source_target_pairs={{0,4},{1,5},{2,6},{3,7},{4,0},{5,1},{6,2},{7,3},{8,12},{9,13},{10,... | collective-permute-start | bytes 589832 | tf_op jit(solution)/shard_map/ppermute | solution.py:54
  43.8 1.0 %last_1.1 = (bf16[256,256]{1,0:T(8,128)(2,1)S(1)}, bf16[256,256]{1,0:T(8,128)(2,1)S(1)}, bf16[256,256]{1,0:T(8,128)(2,1)S(1)}, f32[256,256]{1,0:T(8,128)S(1)}) custom-call(bf16[384,256]{1,0:T(8,128)(2,1)S(1)} %level3_1.1.refs_0_, bf16[384,256]{1,0:T(8,128)(2,1)S(1)} %collective-permute-done.11.refs_1_, bf16[2,384,768]{2,1,0:T(8,128)(2,1)S(1)} %get-tuple-element.42.refs_2_, ...), custom_call_target="tpu_custom_call" | custom-call | flops 352321536 | bytes 2490368 | tf_op jit(solution)/shard_map/last_1/pallas_call | solution.py:40
  44.9 7.3 %collective-permute-done.16.refs_1_ = bf16[384,256]{1,0:T(8,128)(2,1)S(1)} collective-permute-done((bf16[384,256]{1,0:T(8,128)(2,1)S(1)}, bf16[384,256]{1,0:T(8,128)(2,1)S(1)}, u32[]{:S(2)}, u32[]{:S(2)}) %collective-permute-start.16) | collective-permute-done | bytes 196640 | tf_op jit(solution)/shard_map/ppermute | solution.py:54
  52.2 0.3 level2_3.1.refs_3_.refs_0_
  52.6 0.8 collective-permute-done.15.refs_1_
  53.4 0.4 level3_2.1.refs_0_
  53.8 9.3 %collective-permute-done.21.refs_1_ = bf16[384,256]{1,0:T(8,128)(2,1)S(1)} collective-permute-done((bf16[384,256]{1,0:T(8,128)(2,1)S(1)}, bf16[384,256]{1,0:T(8,128)(2,1)S(1)}, u32[]{:S(2)}, u32[]{:S(2)}) %collective-permute-start.21) | collective-permute-done | bytes 196640 | tf_op jit(solution)/shard_map/ppermute | solution.py:54
  63.1 0.4 level3_3.1.refs_0_
  63.6 1.6 %collective-permute-start.6 = (bf16[256,256]{1,0:T(8,128)(2,1)S(1)}, bf16[256,256]{1,0:T(8,128)(2,1)S(1)}, u32[]{:S(2)}, u32[]{:S(2)}) collective-permute-start(bf16[256,256]{1,0:T(8,128)(2,1)S(1)} %get-tuple-element.45), channel_id=1, source_target_pairs={{0,8},{8,0},{16,24},{24,16},{1,9},{9,1},{17,25},{25,17},{2,10},{10... | collective-permute-start | bytes 393224 | tf_op jit(solution)/shard_map/ppermute | solution.py:54
  65.1 1.5 %collective-permute-start.7 = (bf16[256,256]{1,0:T(8,128)(2,1)S(1)}, bf16[256,256]{1,0:T(8,128)(2,1)S(1)}, u32[]{:S(2)}, u32[]{:S(2)}) collective-permute-start(bf16[256,256]{1,0:T(8,128)(2,1)S(1)} %get-tuple-element.46), channel_id=1, source_target_pairs={{0,16},{8,24},{16,0},{24,8},{1,17},{9,25},{17,1},{25,9},{2,18},{10... | collective-permute-start | bytes 393224 | tf_op jit(solution)/shard_map/ppermute | solution.py:54
  66.7 0.5 collective-permute-start.8
  67.1 1.5 %collective-permute-start.12 = (bf16[256,256]{1,0:T(8,128)(2,1)S(1)}, bf16[256,256]{1,0:T(8,128)(2,1)S(1)}, u32[]{:S(2)}, u32[]{:S(2)}) collective-permute-start(bf16[256,256]{1,0:T(8,128)(2,1)S(1)} %get-tuple-element.51), channel_id=1, source_target_pairs={{0,8},{8,0},{16,24},{24,16},{1,9},{9,1},{17,25},{25,17},{2,10},{10... | collective-permute-start | bytes 393224 | tf_op jit(solution)/shard_map/ppermute | solution.py:54
  68.6 1.0 %last_2.1 = (bf16[256,256]{1,0:T(8,128)(2,1)S(1)}, bf16[256,256]{1,0:T(8,128)(2,1)S(1)}, bf16[256,256]{1,0:T(8,128)(2,1)S(1)}, f32[256,256]{1,0:T(8,128)S(1)}) custom-call(bf16[384,256]{1,0:T(8,128)(2,1)S(1)} %level3_2.1.refs_0_, bf16[384,256]{1,0:T(8,128)(2,1)S(1)} %collective-permute-done.17.refs_1_, bf16[2,384,768]{2,1,0:T(8,128)(2,1)S(1)} %get-tuple-element.42.refs_2_, ...), custom_call_target="tpu_custom_call" | custom-call | flops 352321536 | bytes 2490368 | tf_op jit(solution)/shard_map/last_2/pallas_call | solution.py:40
  69.8 1.5 %collective-permute-start.13 = (bf16[256,256]{1,0:T(8,128)(2,1)S(1)}, bf16[256,256]{1,0:T(8,128)(2,1)S(1)}, u32[]{:S(2)}, u32[]{:S(2)}) collective-permute-start(bf16[256,256]{1,0:T(8,128)(2,1)S(1)} %get-tuple-element.52), channel_id=1, source_target_pairs={{0,16},{8,24},{16,0},{24,8},{1,17},{9,25},{17,1},{25,9},{2,18},{10... | collective-permute-start | bytes 393224 | tf_op jit(solution)/shard_map/ppermute | solution.py:54
  71.4 2.0 %collective-permute-done.7.refs_2_ = bf16[256,256]{1,0:T(8,128)(2,1)S(1)} collective-permute-done((bf16[256,256]{1,0:T(8,128)(2,1)S(1)}, bf16[256,256]{1,0:T(8,128)(2,1)S(1)}, u32[]{:S(2)}, u32[]{:S(2)}) %collective-permute-start.7) | collective-permute-done | bytes 131104 | tf_op jit(solution)/shard_map/ppermute | solution.py:54
  73.3 1.8 %collective-permute-start.14 = (bf16[256,256]{1,0:T(8,128)(2,1)S(1)}, bf16[256,256]{1,0:T(8,128)(2,1)S(1)}, u32[]{:S(2)}, u32[]{:S(2)}) collective-permute-start(bf16[256,256]{1,0:T(8,128)(2,1)S(1)} %get-tuple-element.53), channel_id=1, source_target_pairs={{0,24},{8,16},{16,8},{24,0},{1,25},{9,17},{17,9},{25,1},{2,26},{10... | collective-permute-start | bytes 393224 | tf_op jit(solution)/shard_map/ppermute | solution.py:54
  75.1 2.2 %collective-permute-start.18 = (bf16[256,256]{1,0:T(8,128)(2,1)S(1)}, bf16[256,256]{1,0:T(8,128)(2,1)S(1)}, u32[]{:S(2)}, u32[]{:S(2)}) collective-permute-start(bf16[256,256]{1,0:T(8,128)(2,1)S(1)} %get-tuple-element.56), channel_id=1, source_target_pairs={{0,8},{8,0},{16,24},{24,16},{1,9},{9,1},{17,25},{25,17},{2,10},{10... | collective-permute-start | bytes 393224 | tf_op jit(solution)/shard_map/ppermute | solution.py:54
  77.3 1.0 %last_3.1 = (bf16[256,256]{1,0:T(8,128)(2,1)S(1)}, bf16[256,256]{1,0:T(8,128)(2,1)S(1)}, bf16[256,256]{1,0:T(8,128)(2,1)S(1)}, f32[256,256]{1,0:T(8,128)S(1)}) custom-call(bf16[384,256]{1,0:T(8,128)(2,1)S(1)} %level3_3.1.refs_0_, bf16[384,256]{1,0:T(8,128)(2,1)S(1)} %collective-permute-done.22.refs_1_, bf16[2,384,768]{2,1,0:T(8,128)(2,1)S(1)} %get-tuple-element.42.refs_2_, ...), custom_call_target="tpu_custom_call" | custom-call | flops 352321536 | bytes 2490368 | tf_op jit(solution)/shard_map/last_3/pallas_call | solution.py:40
  78.4 1.4 %collective-permute-start.20 = (bf16[256,256]{1,0:T(8,128)(2,1)S(1)}, bf16[256,256]{1,0:T(8,128)(2,1)S(1)}, u32[]{:S(2)}, u32[]{:S(2)}) collective-permute-start(bf16[256,256]{1,0:T(8,128)(2,1)S(1)} %get-tuple-element.58), channel_id=1, source_target_pairs={{0,24},{8,16},{16,8},{24,0},{1,25},{9,17},{17,9},{25,1},{2,26},{10... | collective-permute-start | bytes 393224 | tf_op jit(solution)/shard_map/ppermute | solution.py:54
  79.8 2.0 %collective-permute-start.23 = (bf16[256,256]{1,0:T(8,128)(2,1)S(1)}, bf16[256,256]{1,0:T(8,128)(2,1)S(1)}, u32[]{:S(2)}, u32[]{:S(2)}) collective-permute-start(bf16[256,256]{1,0:T(8,128)(2,1)S(1)} %get-tuple-element.60), channel_id=1, source_target_pairs={{0,8},{8,0},{16,24},{24,16},{1,9},{9,1},{17,25},{25,17},{2,10},{10... | collective-permute-start | bytes 393224 | tf_op jit(solution)/shard_map/ppermute | solution.py:54
  81.9 0.6 collective-permute-start.24
  82.5 1.3 %collective-permute-done.18.refs_9_ = bf16[256,256]{1,0:T(8,128)(2,1)S(1)} collective-permute-done((bf16[256,256]{1,0:T(8,128)(2,1)S(1)}, bf16[256,256]{1,0:T(8,128)(2,1)S(1)}, u32[]{:S(2)}, u32[]{:S(2)}) %collective-permute-start.18) | collective-permute-done | bytes 131104 | tf_op jit(solution)/shard_map/ppermute | solution.py:54
  83.8 0.7 collective-permute-start.25
  84.5 3.2 %collective-permute-done.19.refs_10_ = bf16[256,256]{1,0:T(8,128)(2,1)S(1)} collective-permute-done((bf16[256,256]{1,0:T(8,128)(2,1)S(1)}, bf16[256,256]{1,0:T(8,128)(2,1)S(1)}, u32[]{:S(2)}, u32[]{:S(2)}) %collective-permute-start.19) | collective-permute-done | bytes 131104 | tf_op jit(solution)/shard_map/ppermute | solution.py:54
  87.7 1.3 %collective-permute-done.23.refs_13_ = bf16[256,256]{1,0:T(8,128)(2,1)S(1)} collective-permute-done((bf16[256,256]{1,0:T(8,128)(2,1)S(1)}, bf16[256,256]{1,0:T(8,128)(2,1)S(1)}, u32[]{:S(2)}, u32[]{:S(2)}) %collective-permute-start.23) | collective-permute-done | bytes 131104 | tf_op jit(solution)/shard_map/ppermute | solution.py:54
  88.9 2.0 %collective-permute-done.24.refs_14_ = bf16[256,256]{1,0:T(8,128)(2,1)S(1)} collective-permute-done((bf16[256,256]{1,0:T(8,128)(2,1)S(1)}, bf16[256,256]{1,0:T(8,128)(2,1)S(1)}, u32[]{:S(2)}, u32[]{:S(2)}) %collective-permute-start.24) | collective-permute-done | bytes 131104 | tf_op jit(solution)/shard_map/ppermute | solution.py:54
  90.9 1.0 %sum.1 = bf16[2,256,512]{2,1,0:T(8,128)(2,1)} custom-call(f32[256,256]{1,0:T(8,128)S(1)} %get-tuple-element.44.refs_6_.refs_0_, bf16[256,256]{1,0:T(8,128)(2,1)S(1)} %collective-permute-done.6.refs_1_, bf16[256,256]{1,0:T(8,128)(2,1)S(1)} %collective-permute-done.7.refs_2_, bf16[256,256]{1,0:T(8,128)(2,1)S(1)} %collective-permute-done.8.refs_3_, ...), custom_call_target="tpu_custom_call" | custom-call | tf_op jit(solution)/shard_map/sum/pallas_call | solution.py:279
  (20 shorter events, 1.0 us)
Async XLA Ops:
  3.6 1.9 %collective-permute-start = (bf16[2,384,256]{2,1,0:T(8,128)(2,1)S(1)}, bf16[2,384,256]{2,1,0:T(8,128)(2,1)S(1)}, u32[]{:S(2)}, u32[]{:S(2)}) collective-permute-start(bf16[2,384,256]{2,1,0:T(8,128)(2,1)S(1)} %get-tuple-element.34.refs_0_.refs_3_), channel_id=1, source_target_pairs={{0,1},{1,0},{2,3},{3,2},{4,5},{5,4},{6,7},{7,6},{8,9},{9,8},{10,11... | collective-permute-start | bytes 1179656 | tf_op jit(solution)/shard_map/ppermute | solution.py:54
  5.9 8.2 %collective-permute-start.1 = (bf16[384,256]{1,0:T(8,128)(2,1)S(1)}, bf16[384,256]{1,0:T(8,128)(2,1)S(1)}, u32[]{:S(2)}, u32[]{:S(2)}) collective-permute-start(bf16[384,256]{1,0:T(8,128)(2,1)S(1)} %level1_0.1.refs_3_.refs_0_), channel_id=1, source_target_pairs={{0,2},{1,3},{2,0},{3,1},{4,6},{5,7},{6,4},{7,5},{8,10},{9,11},{10,... | collective-permute-start | bytes 589832 | tf_op jit(solution)/shard_map/ppermute | solution.py:54
  8.9 10.1 %collective-permute-start.4 = (bf16[2,384,256]{2,1,0:T(8,128)(2,1)S(1)}, bf16[2,384,256]{2,1,0:T(8,128)(2,1)S(1)}, u32[]{:S(2)}, u32[]{:S(2)}) collective-permute-start(bf16[2,384,256]{2,1,0:T(8,128)(2,1)S(1)} %get-tuple-element.40.refs_3_), channel_id=1, source_target_pairs={{0,1},{1,0},{2,3},{3,2},{4,5},{5,4},{6,7},{7,6},{8,9},{9,8},{10,11... | collective-permute-start | bytes 1179656 | tf_op jit(solution)/shard_map/ppermute | solution.py:54
  14.6 10.6 %collective-permute-start.3 = (bf16[384,256]{1,0:T(8,128)(2,1)S(1)}, bf16[384,256]{1,0:T(8,128)(2,1)S(1)}, u32[]{:S(2)}, u32[]{:S(2)}) collective-permute-start(bf16[384,256]{1,0:T(8,128)(2,1)S(1)} %get-tuple-element.39.refs_0_), channel_id=1, source_target_pairs={{0,2},{1,3},{2,0},{3,1},{4,6},{5,7},{6,4},{7,5},{8,10},{9,11},{10,... | collective-permute-start | bytes 589832 | tf_op jit(solution)/shard_map/ppermute | solution.py:54
  16.4 11.0 %collective-permute-start.2 = (bf16[384,256]{1,0:T(8,128)(2,1)S(1)}, bf16[384,256]{1,0:T(8,128)(2,1)S(1)}, u32[]{:S(2)}, u32[]{:S(2)}) collective-permute-start(bf16[384,256]{1,0:T(8,128)(2,1)S(1)} %get-tuple-element.37.refs_0_), channel_id=1, source_target_pairs={{0,4},{1,5},{2,6},{3,7},{4,0},{5,1},{6,2},{7,3},{8,12},{9,13},{10,... | collective-permute-start | bytes 589832 | tf_op jit(solution)/shard_map/ppermute | solution.py:54
  27.8 3.2 %collective-permute-start.5 = (bf16[384,256]{1,0:T(8,128)(2,1)S(1)}, bf16[384,256]{1,0:T(8,128)(2,1)S(1)}, u32[]{:S(2)}, u32[]{:S(2)}) collective-permute-start(bf16[384,256]{1,0:T(8,128)(2,1)S(1)} %level3_0.1.refs_0_), channel_id=1, source_target_pairs={{0,1},{1,0},{2,3},{3,2},{4,5},{5,4},{6,7},{7,6},{8,9},{9,8},{10,11... | collective-permute-start | bytes 589832 | tf_op jit(solution)/shard_map/ppermute | solution.py:54
  27.8 11.2 %collective-permute-start.10 = (bf16[384,256]{1,0:T(8,128)(2,1)S(1)}, bf16[384,256]{1,0:T(8,128)(2,1)S(1)}, u32[]{:S(2)}, u32[]{:S(2)}) collective-permute-start(bf16[384,256]{1,0:T(8,128)(2,1)S(1)} %get-tuple-element.48.refs_0_), channel_id=1, source_target_pairs={{0,2},{1,3},{2,0},{3,1},{4,6},{5,7},{6,4},{7,5},{8,10},{9,11},{10,... | collective-permute-start | bytes 589832 | tf_op jit(solution)/shard_map/ppermute | solution.py:54
  28.4 12.1 %collective-permute-start.9 = (bf16[384,256]{1,0:T(8,128)(2,1)S(1)}, bf16[384,256]{1,0:T(8,128)(2,1)S(1)}, u32[]{:S(2)}, u32[]{:S(2)}) collective-permute-start(bf16[384,256]{1,0:T(8,128)(2,1)S(1)} %get-tuple-element.41.refs_3_.refs_0_), channel_id=1, source_target_pairs={{0,4},{1,5},{2,6},{3,7},{4,0},{5,1},{6,2},{7,3},{8,12},{9,13},{10,... | collective-permute-start | bytes 589832 | tf_op jit(solution)/shard_map/ppermute | solution.py:54
  40.8 3.0 %collective-permute-start.11 = (bf16[384,256]{1,0:T(8,128)(2,1)S(1)}, bf16[384,256]{1,0:T(8,128)(2,1)S(1)}, u32[]{:S(2)}, u32[]{:S(2)}) collective-permute-start(bf16[384,256]{1,0:T(8,128)(2,1)S(1)} %level3_1.1.refs_0_), channel_id=1, source_target_pairs={{0,1},{1,0},{2,3},{3,2},{4,5},{5,4},{6,7},{7,6},{8,9},{9,8},{10,11... | collective-permute-start | bytes 589832 | tf_op jit(solution)/shard_map/ppermute | solution.py:54
  40.9 11.2 %collective-permute-start.16 = (bf16[384,256]{1,0:T(8,128)(2,1)S(1)}, bf16[384,256]{1,0:T(8,128)(2,1)S(1)}, u32[]{:S(2)}, u32[]{:S(2)}) collective-permute-start(bf16[384,256]{1,0:T(8,128)(2,1)S(1)} %get-tuple-element.54.refs_0_), channel_id=1, source_target_pairs={{0,2},{1,3},{2,0},{3,1},{4,6},{5,7},{6,4},{7,5},{8,10},{9,11},{10,... | collective-permute-start | bytes 589832 | tf_op jit(solution)/shard_map/ppermute | solution.py:54
  41.3 12.1 %collective-permute-start.15 = (bf16[384,256]{1,0:T(8,128)(2,1)S(1)}, bf16[384,256]{1,0:T(8,128)(2,1)S(1)}, u32[]{:S(2)}, u32[]{:S(2)}) collective-permute-start(bf16[384,256]{1,0:T(8,128)(2,1)S(1)} %get-tuple-element.49.refs_3_.refs_0_), channel_id=1, source_target_pairs={{0,4},{1,5},{2,6},{3,7},{4,0},{5,1},{6,2},{7,3},{8,12},{9,13},{10,... | collective-permute-start | bytes 589832 | tf_op jit(solution)/shard_map/ppermute | solution.py:54
  52.5 10.6 %collective-permute-start.21 = (bf16[384,256]{1,0:T(8,128)(2,1)S(1)}, bf16[384,256]{1,0:T(8,128)(2,1)S(1)}, u32[]{:S(2)}, u32[]{:S(2)}) collective-permute-start(bf16[384,256]{1,0:T(8,128)(2,1)S(1)} %level2_3.1.refs_3_.refs_0_), channel_id=1, source_target_pairs={{0,4},{1,5},{2,6},{3,7},{4,0},{5,1},{6,2},{7,3},{8,12},{9,13},{10,... | collective-permute-start | bytes 589832 | tf_op jit(solution)/shard_map/ppermute | solution.py:54
  53.7 13.4 %collective-permute-start.17 = (bf16[384,256]{1,0:T(8,128)(2,1)S(1)}, bf16[384,256]{1,0:T(8,128)(2,1)S(1)}, u32[]{:S(2)}, u32[]{:S(2)}) collective-permute-start(bf16[384,256]{1,0:T(8,128)(2,1)S(1)} %level3_2.1.refs_0_), channel_id=1, source_target_pairs={{0,1},{1,0},{2,3},{3,2},{4,5},{5,4},{6,7},{7,6},{8,9},{9,8},{10,11... | collective-permute-start | bytes 589832 | tf_op jit(solution)/shard_map/ppermute | solution.py:54
  63.5 11.6 %collective-permute-start.22 = (bf16[384,256]{1,0:T(8,128)(2,1)S(1)}, bf16[384,256]{1,0:T(8,128)(2,1)S(1)}, u32[]{:S(2)}, u32[]{:S(2)}) collective-permute-start(bf16[384,256]{1,0:T(8,128)(2,1)S(1)} %level3_3.1.refs_0_), channel_id=1, source_target_pairs={{0,1},{1,0},{2,3},{3,2},{4,5},{5,4},{6,7},{7,6},{8,9},{9,8},{10,11... | collective-permute-start | bytes 589832 | tf_op jit(solution)/shard_map/ppermute | solution.py:54
  63.6 6.3 %collective-permute-start.6 = (bf16[256,256]{1,0:T(8,128)(2,1)S(1)}, bf16[256,256]{1,0:T(8,128)(2,1)S(1)}, u32[]{:S(2)}, u32[]{:S(2)}) collective-permute-start(bf16[256,256]{1,0:T(8,128)(2,1)S(1)} %get-tuple-element.45), channel_id=1, source_target_pairs={{0,8},{8,0},{16,24},{24,16},{1,9},{9,1},{17,25},{25,17},{2,10},{10... | collective-permute-start | bytes 393224 | tf_op jit(solution)/shard_map/ppermute | solution.py:54
  65.1 8.2 %collective-permute-start.7 = (bf16[256,256]{1,0:T(8,128)(2,1)S(1)}, bf16[256,256]{1,0:T(8,128)(2,1)S(1)}, u32[]{:S(2)}, u32[]{:S(2)}) collective-permute-start(bf16[256,256]{1,0:T(8,128)(2,1)S(1)} %get-tuple-element.46), channel_id=1, source_target_pairs={{0,16},{8,24},{16,0},{24,8},{1,17},{9,25},{17,1},{25,9},{2,18},{10... | collective-permute-start | bytes 393224 | tf_op jit(solution)/shard_map/ppermute | solution.py:54
  66.7 11.6 %collective-permute-start.8 = (bf16[256,256]{1,0:T(8,128)(2,1)S(1)}, bf16[256,256]{1,0:T(8,128)(2,1)S(1)}, u32[]{:S(2)}, u32[]{:S(2)}) collective-permute-start(bf16[256,256]{1,0:T(8,128)(2,1)S(1)} %get-tuple-element.47), channel_id=1, source_target_pairs={{0,24},{8,16},{16,8},{24,0},{1,25},{9,17},{17,9},{25,1},{2,26},{10... | collective-permute-start | bytes 393224 | tf_op jit(solution)/shard_map/ppermute | solution.py:54
  67.1 11.2 %collective-permute-start.12 = (bf16[256,256]{1,0:T(8,128)(2,1)S(1)}, bf16[256,256]{1,0:T(8,128)(2,1)S(1)}, u32[]{:S(2)}, u32[]{:S(2)}) collective-permute-start(bf16[256,256]{1,0:T(8,128)(2,1)S(1)} %get-tuple-element.51), channel_id=1, source_target_pairs={{0,8},{8,0},{16,24},{24,16},{1,9},{9,1},{17,25},{25,17},{2,10},{10... | collective-permute-start | bytes 393224 | tf_op jit(solution)/shard_map/ppermute | solution.py:54
  69.8 10.0 %collective-permute-start.13 = (bf16[256,256]{1,0:T(8,128)(2,1)S(1)}, bf16[256,256]{1,0:T(8,128)(2,1)S(1)}, u32[]{:S(2)}, u32[]{:S(2)}) collective-permute-start(bf16[256,256]{1,0:T(8,128)(2,1)S(1)} %get-tuple-element.52), channel_id=1, source_target_pairs={{0,16},{8,24},{16,0},{24,8},{1,17},{9,25},{17,1},{25,9},{2,18},{10... | collective-permute-start | bytes 393224 | tf_op jit(solution)/shard_map/ppermute | solution.py:54
  73.3 8.5 %collective-permute-start.14 = (bf16[256,256]{1,0:T(8,128)(2,1)S(1)}, bf16[256,256]{1,0:T(8,128)(2,1)S(1)}, u32[]{:S(2)}, u32[]{:S(2)}) collective-permute-start(bf16[256,256]{1,0:T(8,128)(2,1)S(1)} %get-tuple-element.53), channel_id=1, source_target_pairs={{0,24},{8,16},{16,8},{24,0},{1,25},{9,17},{17,9},{25,1},{2,26},{10... | collective-permute-start | bytes 393224 | tf_op jit(solution)/shard_map/ppermute | solution.py:54
  75.1 8.7 %collective-permute-start.18 = (bf16[256,256]{1,0:T(8,128)(2,1)S(1)}, bf16[256,256]{1,0:T(8,128)(2,1)S(1)}, u32[]{:S(2)}, u32[]{:S(2)}) collective-permute-start(bf16[256,256]{1,0:T(8,128)(2,1)S(1)} %get-tuple-element.56), channel_id=1, source_target_pairs={{0,8},{8,0},{16,24},{24,16},{1,9},{9,1},{17,25},{25,17},{2,10},{10... | collective-permute-start | bytes 393224 | tf_op jit(solution)/shard_map/ppermute | solution.py:54
  78.3 9.4 %collective-permute-start.19 = (bf16[256,256]{1,0:T(8,128)(2,1)S(1)}, bf16[256,256]{1,0:T(8,128)(2,1)S(1)}, u32[]{:S(2)}, u32[]{:S(2)}) collective-permute-start(bf16[256,256]{1,0:T(8,128)(2,1)S(1)} %get-tuple-element.57), channel_id=1, source_target_pairs={{0,16},{8,24},{16,0},{24,8},{1,17},{9,25},{17,1},{25,9},{2,18},{10... | collective-permute-start | bytes 393224 | tf_op jit(solution)/shard_map/ppermute | solution.py:54
  78.4 9.3 %collective-permute-start.20 = (bf16[256,256]{1,0:T(8,128)(2,1)S(1)}, bf16[256,256]{1,0:T(8,128)(2,1)S(1)}, u32[]{:S(2)}, u32[]{:S(2)}) collective-permute-start(bf16[256,256]{1,0:T(8,128)(2,1)S(1)} %get-tuple-element.58), channel_id=1, source_target_pairs={{0,24},{8,16},{16,8},{24,0},{1,25},{9,17},{17,9},{25,1},{2,26},{10... | collective-permute-start | bytes 393224 | tf_op jit(solution)/shard_map/ppermute | solution.py:54
  79.8 9.1 %collective-permute-start.23 = (bf16[256,256]{1,0:T(8,128)(2,1)S(1)}, bf16[256,256]{1,0:T(8,128)(2,1)S(1)}, u32[]{:S(2)}, u32[]{:S(2)}) collective-permute-start(bf16[256,256]{1,0:T(8,128)(2,1)S(1)} %get-tuple-element.60), channel_id=1, source_target_pairs={{0,8},{8,0},{16,24},{24,16},{1,9},{9,1},{17,25},{25,17},{2,10},{10... | collective-permute-start | bytes 393224 | tf_op jit(solution)/shard_map/ppermute | solution.py:54
  81.9 9.1 %collective-permute-start.24 = (bf16[256,256]{1,0:T(8,128)(2,1)S(1)}, bf16[256,256]{1,0:T(8,128)(2,1)S(1)}, u32[]{:S(2)}, u32[]{:S(2)}) collective-permute-start(bf16[256,256]{1,0:T(8,128)(2,1)S(1)} %get-tuple-element.61), channel_id=1, source_target_pairs={{0,16},{8,24},{16,0},{24,8},{1,17},{9,25},{17,1},{25,9},{2,18},{10... | collective-permute-start | bytes 393224 | tf_op jit(solution)/shard_map/ppermute | solution.py:54
  83.8 7.2 %collective-permute-start.25 = (bf16[256,256]{1,0:T(8,128)(2,1)S(1)}, bf16[256,256]{1,0:T(8,128)(2,1)S(1)}, u32[]{:S(2)}, u32[]{:S(2)}) collective-permute-start(bf16[256,256]{1,0:T(8,128)(2,1)S(1)} %get-tuple-element.62), channel_id=1, source_target_pairs={{0,24},{8,16},{16,8},{24,0},{1,25},{9,17},{17,9},{25,1},{2,26},{10... | collective-permute-start | bytes 393224 | tf_op jit(solution)/shard_map/ppermute | solution.py:54

commit v3 on v2

v3 whole, which is shorter than its diff:
```python
import functools

import jax
import jax.numpy as jnp
from jax import lax
from jax.experimental import pallas as pl
from jax.experimental.pallas import tpu as pltpu
from jax.sharding import PartitionSpec as P

HALVES = 2
BF16 = jnp.bfloat16
F32 = jnp.float32
ANY = pl.BlockSpec(memory_space=pl.ANY)
VMEM = pl.BlockSpec(memory_space=pltpu.VMEM)


def dot(a, b):
    return jnp.dot(a, b, preferred_element_type=F32)


def in_vmem(*shape, dtype=BF16):
    return pltpu.VMEM(shape, dtype)


def here(value):
    return pltpu.with_memory_space_constraint(value, pltpu.VMEM)


def in_hbm(value):
    return pltpu.with_memory_space_constraint(value, pltpu.HBM)


def call(kernel, name, in_specs, out_shape, scratch, args, after=(), flops=6 * 10**9, limit=8 * 2**20):
    count = len(in_specs)

    def body(*refs):
        kernel(*refs[:count], *refs[count + len(after) :])

    return pl.pallas_call(
        body,
        name=name,
        in_specs=[*in_specs, *[ANY] * len(after)],
        out_specs=[VMEM] * len(out_shape),
        out_shape=out_shape,
        scratch_shapes=scratch,
        compiler_params=pltpu.CompilerParams(vmem_limit_bytes=limit),
        cost_estimate=pl.CostEstimate(flops=flops, bytes_accessed=0, transcendentals=0),
    )(*args, *after)


def partner(value, axis, mask):
    pairs = [(source, source ^ mask) for source in range(lax.axis_size(axis))]
    return lax.ppermute(value, axis, pairs)


def leaf_kernel(excite, leaves, blocks, index, *refs):
    firsts, next_ref = refs[:HALVES], refs[HALVES]
    excite_v, leaves_v, blocks_v, index_s, coeff, sems = refs[HALVES + 1 :]
    slots, rank = leaves.shape[0], leaves.shape[1]
    width = firsts[0].shape[2]
    listing = pltpu.make_async_copy(index, index_s, sems.at[0])
    listing.start()
    loads = []
    for s in range(slots):
        a = pltpu.make_async_copy(leaves.at[s], leaves_v.at[s], sems.at[1 + s])
        b = pltpu.make_async_copy(excite.at[s], excite_v.at[s], sems.at[3 + s])
        a.start()
        b.start()
        loads.append((a, b))
    listing.wait()
    weights, later = [], []
    for s in range(slots):
        c = pltpu.make_async_copy(blocks.at[0, index_s[s, 0]], blocks_v.at[s], sems.at[5 + s])
        c.start()
        weights.append(c)
    for s in range(slots):
        c = pltpu.make_async_copy(blocks.at[1, index_s[s, 1]], next_ref.at[s], sems.at[7 + s])
        c.start()
        later.append(c)
    for s in range(slots):
        for load in loads[s]:
            load.wait()
        coeff[s * rank : (s + 1) * rank, :] = dot(leaves_v[s], excite_v[s]).astype(BF16)
    for s in range(slots):
        weights[s].wait()
        out = dot(blocks_v[s], coeff[...]).astype(BF16)
        for h in range(HALVES):
            firsts[h][s] = out[:, h * width : (h + 1) * width]
    for c in later:
        c.wait()


def prefetch_kernel(blocks, basis, index, *refs):
    count = blocks.shape[0] - 2
    outs, basis_v, index_s, sems = refs[:count], refs[count], refs[count + 1], refs[count + 2]
    listing = pltpu.make_async_copy(index, index_s, sems.at[0])
    listing.start()
    listing.wait()
    copies = []
    for level in range(count):
        for s in range(2):
            c = pltpu.make_async_copy(
                blocks.at[level + 2, index_s[s, level + 2]], outs[level].at[s], sems.at[1 + 2 * level + s]
            )
            c.start()
            copies.append(c)
    c = pltpu.make_async_copy(basis, basis_v, sems.at[1 + 2 * count])
    c.start()
    copies.append(c)
    for c in copies:
        c.wait()


def upper_half(bit):
    return (lax.axis_index("box") >> bit) & 1


def mix(weights, own, other, bit, buf):
    rank = own.shape[0]
    upper = upper_half(bit)
    buf[pl.ds(pl.multiple_of(upper * rank, rank), rank), :] = own
    buf[pl.ds(pl.multiple_of((1 - upper) * rank, rank), rank), :] = other
    return dot(weights, buf[...]).astype(BF16)


def levels_kernel(jobs, *refs):
    count = len(jobs)
    ins, outs, bufs = refs[: 3 * count], refs[3 * count : 4 * count], refs[4 * count :]
    for at, (bit, s, both) in enumerate(jobs):
        own, other, weights = ins[3 * at : 3 * at + 3]
        own, other = (own[s], other[s]) if both else (own[...], other[...])
        outs[at][...] = mix(weights[s], own, other, bit, bufs[at])


def half_dot(weights, s, half, value):
    rank = value.shape[0]
    return dot(weights[s, :, pl.ds(pl.multiple_of(half * rank, 128), rank)], value)


def between_kernel(bit, s, fold, total, own, weights, *refs):
    refs = list(refs)
    ins = [refs.pop(0) for _ in range(2 * (fold + total))]
    partial = refs.pop(0)
    partial[...] = half_dot(weights, s, upper_half(bit), own[...])
    if fold:
        keep, got = ins.pop(0), ins.pop(0)
        send, rest = refs.pop(0), refs.pop(0)
        rows = rest.shape[0]
        rest[...] = keep[:rows] + got[:rows].astype(F32)
        send[...] = (keep[rows:] + got[rows:].astype(F32)).astype(BF16)
    if total:
        keep, got = ins.pop(0), ins.pop(0)
        refs.pop(0)[...] = (keep[...] + got[...].astype(F32)).astype(BF16)


def last_kernel(bit, s, order, partial, other, weights, basis, *refs):
    coeff = (partial[...] + half_dot(weights, s, 1 - upper_half(bit), other[...])).astype(BF16)
    rows = basis.shape[1] // lax.axis_size("blk")
    me = lax.axis_index("blk")
    for ref, distances in zip(refs, order):
        for at, d in enumerate(distances):
            start = pl.multiple_of((me ^ d) * rows, rows)
            piece = dot(basis[s, pl.ds(start, rows), :], coeff)
            ref[at * rows : (at + 1) * rows, :] = piece.astype(ref.dtype)


def fold_kernel(keep, got, send, rest):
    rows = rest.shape[0]
    rest[...] = keep[:rows] + got[:rows].astype(F32)
    send[...] = (keep[rows:] + got[rows:].astype(F32)).astype(BF16)


def end_kernel(places, counts, *refs):
    refs = list(refs)
    out = refs[-1]
    for (s, start, width), count in zip(places, counts):
        group = [refs.pop(0) for _ in range(count)]
        total = group[0][...].astype(F32)
        for piece in group[1:]:
            total = total + piece[...].astype(F32)
        out[s, :, start : start + width] = total.astype(BF16)


def on_device(excitation, leaf_basis, transfer, transfer_index, out_basis):
    excite, leaves, blocks, basis = excitation[0], leaf_basis[0], transfer[0], out_basis[0]
    index = transfer_index[0].T
    slots, rank, points = leaves.shape
    levels = blocks.shape[0]
    columns = excite.shape[2]
    width = columns // HALVES
    n_blk = lax.axis_size("blk")
    rows = basis.shape[1] // n_blk
    nbits = lax.axis_size("box").bit_length() - 1
    bits = [None] + [(level - 1) % nbits for level in range(1, levels)]
    pair = in_vmem(slots, rank, 2 * rank)
    shape = in_vmem(rank, width)
    buf = in_vmem(2 * rank, width)
    chunks = [(h, s) for h in range(HALVES) for s in range(slots)]

    *coeff1, weights1 = call(
        leaf_kernel,
        "leaf",
        [ANY] * 4,
        [in_vmem(slots, rank, width)] * HALVES + [pair],
        [
            in_vmem(*excite.shape),
            in_vmem(*leaves.shape),
            pair,
            pltpu.SMEM(index.shape, jnp.int32),
            in_vmem(2 * rank, columns),
            pltpu.SemaphoreType.DMA((9,)),
        ],
        [in_hbm(excite), in_hbm(leaves), in_hbm(blocks), in_hbm(index)],
        limit=24 * 2**20,
    )
    weights = [None, weights1]
    near1 = [partner(c, "box", 2 ** bits[1]) for c in coeff1]

    def cross(level, value):
        return partner(value, "box", 2 ** bits[level])

    def step(name, jobs, after=()):
        args = [here(v) for level, j, own, other in jobs for v in (own, other, weights[level])]
        return call(
            functools.partial(
                levels_kernel, [(bits[level], chunks[j][1], level == 1) for level, j, _, _ in jobs]
            ),
            name,
            [VMEM] * len(args),
            [shape] * len(jobs),
            [buf] * len(jobs),
            args,
            after,
        )

    def job1(j):
        h = chunks[j][0]
        return (1, j, coeff1[h], near1[h])

    coeff2, near2, coeff3, near3 = {}, {}, {}, {}
    coeff2[0], coeff2[1] = step("level1_a", [job1(0), job1(1)])
    for j in (0, 1):
        near2[j] = cross(2, coeff2[j])
    *more, basis_v = call(
        prefetch_kernel,
        "prefetch",
        [ANY] * 3,
        [pair] * (levels - 2) + [in_vmem(*basis.shape)],
        [pltpu.SMEM(index.shape, jnp.int32), pltpu.SemaphoreType.DMA((2 * levels,))],
        [in_hbm(blocks), in_hbm(basis), in_hbm(index)],
        [coeff2[0]],
    )
    weights += more
    (coeff3[0],) = step("level2_0", [(2, 0, coeff2[0], near2[0])])
    near3[0] = cross(3, coeff3[0])
    coeff3[1], coeff2[2], coeff2[3] = step(
        "level2_1", [(2, 1, coeff2[1], near2[1]), job1(2), job1(3)], [coeff3[0]]
    )
    near3[1] = cross(3, coeff3[1])
    for j in (2, 3):
        near2[j] = cross(2, coeff2[j])

    masks = [1 << b for b in range(n_blk.bit_length() - 1)]

    def halving(j):
        order = masks if j % 2 else masks[::-1]
        pieces = [0]
        for mask in order[::-1]:
            pieces = pieces + [d | mask for d in pieces]
        return order, pieces

    def result(count, dtype):
        return in_vmem(count * rows, width, dtype=dtype)

    def tail(j, after, folding, totalling):
        s = chunks[j][1]
        (coeff4,) = step(f"level3_{j}", [(3, j, coeff3[j], near3[j])], after)
        near4 = cross(4, coeff4)
        outs, extra = [in_vmem(rank, width, dtype=F32)], []
        if folding is not None:
            keep, got, count = folding
            extra += [keep, got]
            outs += [result(count // 2, BF16), result(count // 2, F32)]
        if totalling is not None:
            extra += totalling
            outs += [result(1, BF16)]
        partial, *rest = call(
            functools.partial(
                between_kernel, bits[4], s, folding is not None, totalling is not None
            ),
            f"between_{j}",
            [VMEM] * (2 + len(extra)),
            outs,
            [],
            [here(v) for v in (coeff4, weights[4], *extra)],
            flops=6 * 10**9,
        )
        if j == len(chunks) - 1:
            order = [[0]] + [[d] for d in range(1, n_blk)]
        else:
            pieces = halving(j)[1]
            order = [pieces[: n_blk // 2], pieces[n_blk // 2 :]]
        kinds = [F32] + [BF16] * (len(order) - 1)
        out = call(
            functools.partial(last_kernel, bits[4], s, order),
            f"last_{j}",
            [VMEM] * 4,
            [result(len(o), kind) for o, kind in zip(order, kinds)],
            [],
            [here(v) for v in (partial, near4, weights[4], basis_v)],
        )
        return out, rest

    def fold_all(j, keep, got, count):
        for mask in halving(j)[0][1:-1]:
            send, keep = call(
                fold_kernel,
                f"fold_{j}_{mask}",
                [VMEM] * 2,
                [result(count // 2, BF16), result(count // 2, F32)],
                [],
                [here(keep), here(got)],
            )
            got = partner(send, "blk", mask)
            count //= 2
        return keep, got, count

    def begin(j, out):
        keep, send = out
        return fold_all(j, keep, partner(send, "blk", halving(j)[0][0]), n_blk // 2)

    out0, _ = tail(0, [coeff3[1]], None, None)
    fold0 = begin(0, out0)
    (coeff3[2],) = step("level2_2", [(2, 2, coeff2[2], near2[2])], [out0[0]])
    near3[2] = cross(3, coeff3[2])
    (coeff3[3],) = step("level2_3", [(2, 3, coeff2[3], near2[3])], [coeff3[2]])
    near3[3] = cross(3, coeff3[3])
    out1, (send0, keep0) = tail(1, [coeff3[3]], fold0, None)
    got0 = partner(send0, "blk", halving(0)[0][-1])
    fold1 = begin(1, out1)
    out2, (send1, keep1, total0) = tail(2, [out1[0]], fold1, [keep0, got0])
    got1 = partner(send1, "blk", halving(1)[0][-1])
    fold2 = begin(2, out2)
    out3, (send2, keep2, total1) = tail(3, [out2[0]], fold2, [keep1, got1])
    got2 = partner(send2, "blk", halving(2)[0][-1])
    group3 = [out3[0]] + [partner(out3[d], "blk", d) for d in range(1, n_blk)]
    groups = [[total0], [total1], [keep2, got2], group3]
    flat = [here(v) for group in groups for v in group]
    return pl.pallas_call(
        functools.partial(
            end_kernel, [(s, h * width, width) for h, s in chunks], [len(group) for group in groups]
        ),
        name="end",
        in_specs=[VMEM] * len(flat),
        out_specs=VMEM,
        out_shape=jax.ShapeDtypeStruct((slots, rows, columns), BF16),
        compiler_params=pltpu.CompilerParams(vmem_limit_bytes=8 * 2**20),
    )(*flat)


def solution(mesh):
    in_specs = (
        P("blk", "box", None, None),
        P("blk", "box", None, None),
        P("blk", None, "box", None, None),
        P("blk", None, "box"),
        P("blk", "box", None, None),
    )
    out_specs = P("box", "blk", None)
    return jax.shard_map(
        on_device, mesh=mesh, in_specs=in_specs, out_specs=out_specs, check_vma=False
    )
```

time: 92.1 us -> 76.7 us (0.83)
  starting transfers between devices: 29.7 us -> 20.8 us
  waiting for transfers between devices: 46.5 us -> 39.8 us
    ppermute x26 -> x23, starting transfers between devices: 29.7 us -> 20.8 us  [partner(): return lax.ppermute(value, axis, pairs)]
    ppermute x26 -> x23, waiting for transfers between devices: 46.5 us -> 39.8 us  [partner(): return lax.ppermute(value, axis, pairs)]
    pallas_call x15 -> x19, Pallas kernels: 14.6 us -> 14.9 us  [call(): pl.pallas_call(body, name=name, in_specs=[*in_specs, *[ANY] * len(after)]...]
  transfers between devices with their start and end apart: 26 -> 23, of which waited for: 15 -> 16; matrix products, arithmetic and copies ran while one was open for 0% -> 0% of each run, Pallas kernels for 11% -> 15%
where the time goes in v3:
time: 76.7 us; the launch traced here: 76.6 us
  waiting for transfers between devices  39.8 us (52%)
  starting transfers between devices  20.8 us (27%)
  Pallas kernels  15.8 us (21%)
    ppermute x23, waiting for transfers between devices, partner(): return lax.ppermute(value, axis, pairs)  39.8 us
    ppermute x23, starting transfers between devices, partner(): return lax.ppermute(value, axis, pairs)  20.8 us
    pallas_call x19, Pallas kernels, call(): pl.pallas_call(body, name=name, in_specs=[*in_specs, *[ANY] * len(after)]...  14.9 us
  transfers between devices with their start and end apart: 23, of which 16 were waited for; matrix products, arithmetic and copies ran while one was open for 0% of the time, Pallas kernels for 15%

profile of v3, /device:TPU:0, one launch (start us, length us, event | category | flops | bytes accessed | tf_op | source)
XLA Modules:
  0.0 76.6 jit_solution(17767148309351584777)
XLA Ops:
  0.0 3.6 %leaf.1 = (bf16[2,384,256]{2,1,0:T(8,128)(2,1)S(1)}, bf16[2,384,256]{2,1,0:T(8,128)(2,1)S(1)}, bf16[2,384,768]{2,1,0:T(8,128)(2,1)S(1)}) custom-call(bf16[2,1024,512]{2,1,0:T(8,128)(2,1)} %bitcast.9, bf16[2,384,1024]{2,1,0:T(8,128)(2,1)} %bitcast.10, bf16[5,2,384,768]{3,2,1,0:T(8,128)(2,1)} %bitcast.7, s32[2,5]{1,0:T(2,128)} %bitcast.12), custom_call_target="tpu_custom_call" | custom-call | flops 6000000000 | tf_op jit(solution)/shard_map/leaf/pallas_call | solution.py:39
  3.6 0.5 collective-permute-start
  4.2 1.3 %collective-permute-done.refs_1_.refs_4_ = bf16[2,384,256]{2,1,0:T(8,128)(2,1)S(1)} collective-permute-done((bf16[2,384,256]{2,1,0:T(8,128)(2,1)S(1)}, bf16[2,384,256]{2,1,0:T(8,128)(2,1)S(1)}, u32[]{:S(2)}, u32[]{:S(2)}) %collective-permute-start) | collective-permute-done | bytes 393248 | tf_op jit(solution)/shard_map/ppermute | solution.py:53
  5.5 0.5 level1_a.1
  6.0 3.0 %collective-permute-start.1 = (bf16[384,256]{1,0:T(8,128)(2,1)S(1)}, bf16[384,256]{1,0:T(8,128)(2,1)S(1)}, u32[]{:S(2)}, u32[]{:S(2)}) collective-permute-start(bf16[384,256]{1,0:T(8,128)(2,1)S(1)} %get-tuple-element.40.refs_0_), channel_id=1, source_target_pairs={{0,2},{1,3},{2,0},{3,1},{4,6},{5,7},{6,4},{7,5},{8,10},{9,11},{10,... | collective-permute-start | bytes 589832 | tf_op jit(solution)/shard_map/ppermute | solution.py:53
  9.1 3.3 %prefetch.1 = (bf16[2,384,768]{2,1,0:T(8,128)(2,1)S(1)}, bf16[2,384,768]{2,1,0:T(8,128)(2,1)S(1)}, bf16[2,384,768]{2,1,0:T(8,128)(2,1)S(1)}, bf16[2,1024,384]{2,1,0:T(8,128)(2,1)S(1)}) custom-call(bf16[5,2,384,768]{3,2,1,0:T(8,128)(2,1)} %bitcast.8, bf16[2,1024,384]{2,1,0:T(8,128)(2,1)} %bitcast.11, s32[2,5]{1,0:T(2,128)} %bitcast.13, ...), custom_call_target="tpu_custom_call" | custom-call | flops 6000000000 | tf_op jit(solution)/shard_map/prefetch/pallas_call | solution.py:39
  12.4 6.1 %collective-permute-done.3.refs_1_ = bf16[384,256]{1,0:T(8,128)(2,1)S(1)} collective-permute-done((bf16[384,256]{1,0:T(8,128)(2,1)S(1)}, bf16[384,256]{1,0:T(8,128)(2,1)S(1)}, u32[]{:S(2)}, u32[]{:S(2)}) %collective-permute-start.3) | collective-permute-done | bytes 196640 | tf_op jit(solution)/shard_map/ppermute | solution.py:53
  18.5 0.4 level2_0.1.refs_9_.refs_0_
  18.8 2.8 %collective-permute-start.5 = (bf16[384,256]{1,0:T(8,128)(2,1)S(1)}, bf16[384,256]{1,0:T(8,128)(2,1)S(1)}, u32[]{:S(2)}, u32[]{:S(2)}) collective-permute-start(bf16[384,256]{1,0:T(8,128)(2,1)S(1)} %level2_0.1.refs_9_.refs_0_), channel_id=1, source_target_pairs={{0,4},{1,5},{2,6},{3,7},{4,0},{5,1},{6,2},{7,3},{8,12},{9,13},{10,... | collective-permute-start | bytes 589832 | tf_op jit(solution)/shard_map/ppermute | solution.py:53
  21.6 0.7 level2_1.1
  22.3 1.6 %collective-permute-start.4 = (bf16[384,256]{1,0:T(8,128)(2,1)S(1)}, bf16[384,256]{1,0:T(8,128)(2,1)S(1)}, u32[]{:S(2)}, u32[]{:S(2)}) collective-permute-start(bf16[384,256]{1,0:T(8,128)(2,1)S(1)} %get-tuple-element.44.refs_0_), channel_id=1, source_target_pairs={{0,2},{1,3},{2,0},{3,1},{4,6},{5,7},{6,4},{7,5},{8,10},{9,11},{10,... | collective-permute-start | bytes 589832 | tf_op jit(solution)/shard_map/ppermute | solution.py:53
  24.0 0.4 collective-permute-start.9
  24.6 7.0 %collective-permute-done.5.refs_1_ = bf16[384,256]{1,0:T(8,128)(2,1)S(1)} collective-permute-done((bf16[384,256]{1,0:T(8,128)(2,1)S(1)}, bf16[384,256]{1,0:T(8,128)(2,1)S(1)}, u32[]{:S(2)}, u32[]{:S(2)}) %collective-permute-start.5) | collective-permute-done | bytes 196640 | tf_op jit(solution)/shard_map/ppermute | solution.py:53
  31.5 0.4 level3_0.1.refs_0_
  32.2 1.2 %collective-permute-done.6.refs_1_ = bf16[384,256]{1,0:T(8,128)(2,1)S(1)} collective-permute-done((bf16[384,256]{1,0:T(8,128)(2,1)S(1)}, bf16[384,256]{1,0:T(8,128)(2,1)S(1)}, u32[]{:S(2)}, u32[]{:S(2)}) %collective-permute-start.6) | collective-permute-done | bytes 196640 | tf_op jit(solution)/shard_map/ppermute | solution.py:53
  33.4 0.8 %last_0.1 = (f32[512,256]{1,0:T(8,128)S(1)}, bf16[512,256]{1,0:T(8,128)(2,1)S(1)}) custom-call(f32[384,256]{1,0:T(8,128)S(1)} %between_0.1.refs_0_, bf16[384,256]{1,0:T(8,128)(2,1)S(1)} %collective-permute-done.6.refs_1_, bf16[2,384,768]{2,1,0:T(8,128)(2,1)S(1)} %get-tuple-element.47.refs_1_.refs_2_, bf16[2,1024,384]{2,1,0:T(8,128)(2,1)S(1)} %get-tuple-element.48.refs_3_), custom_call_target="tpu_custom_call" | custom-call | flops 6000000000 | tf_op jit(solution)/shard_map/last_0/pallas_call | solution.py:39
  34.2 3.3 %collective-permute-done.4.refs_1_ = bf16[384,256]{1,0:T(8,128)(2,1)S(1)} collective-permute-done((bf16[384,256]{1,0:T(8,128)(2,1)S(1)}, bf16[384,256]{1,0:T(8,128)(2,1)S(1)}, u32[]{:S(2)}, u32[]{:S(2)}) %collective-permute-start.4) | collective-permute-done | bytes 196640 | tf_op jit(solution)/shard_map/ppermute | solution.py:53
  37.5 0.4 level2_2.1.refs_3_.refs_0_
  38.1 1.9 %collective-permute-done.9.refs_1_ = bf16[384,256]{1,0:T(8,128)(2,1)S(1)} collective-permute-done((bf16[384,256]{1,0:T(8,128)(2,1)S(1)}, bf16[384,256]{1,0:T(8,128)(2,1)S(1)}, u32[]{:S(2)}, u32[]{:S(2)}) %collective-permute-start.9) | collective-permute-done | bytes 196640 | tf_op jit(solution)/shard_map/ppermute | solution.py:53
  40.0 0.4 level2_3.1.refs_3_.refs_0_
  40.4 0.9 %collective-permute-start.14 = (bf16[384,256]{1,0:T(8,128)(2,1)S(1)}, bf16[384,256]{1,0:T(8,128)(2,1)S(1)}, u32[]{:S(2)}, u32[]{:S(2)}) collective-permute-start(bf16[384,256]{1,0:T(8,128)(2,1)S(1)} %level2_3.1.refs_3_.refs_0_), channel_id=1, source_target_pairs={{0,4},{1,5},{2,6},{3,7},{4,0},{5,1},{6,2},{7,3},{8,12},{9,13},{10,... | collective-permute-start | bytes 589832 | tf_op jit(solution)/shard_map/ppermute | solution.py:53
  41.3 1.4 %collective-permute-start.10 = (bf16[512,256]{1,0:T(8,128)(2,1)S(1)}, bf16[512,256]{1,0:T(8,128)(2,1)S(1)}, u32[]{:S(2)}, u32[]{:S(2)}) collective-permute-start(bf16[512,256]{1,0:T(8,128)(2,1)S(1)} %get-tuple-element.51), channel_id=1, source_target_pairs={{0,16},{8,24},{16,0},{24,8},{1,17},{9,25},{17,1},{25,9},{2,18},{10... | collective-permute-start | bytes 786440 | tf_op jit(solution)/shard_map/ppermute | solution.py:53
  42.6 0.4 level3_1.1.refs_0_
  43.1 4.6 %collective-permute-done.10.refs_3_ = bf16[512,256]{1,0:T(8,128)(2,1)S(1)} collective-permute-done((bf16[512,256]{1,0:T(8,128)(2,1)S(1)}, bf16[512,256]{1,0:T(8,128)(2,1)S(1)}, u32[]{:S(2)}, u32[]{:S(2)}) %collective-permute-start.10) | collective-permute-done | bytes 262176 | tf_op jit(solution)/shard_map/ppermute | solution.py:53
  47.7 0.3 between_1.1
  47.9 1.4 %collective-permute-start.13 = (bf16[256,256]{1,0:T(8,128)(2,1)S(1)}, bf16[256,256]{1,0:T(8,128)(2,1)S(1)}, u32[]{:S(2)}, u32[]{:S(2)}) collective-permute-start(bf16[256,256]{1,0:T(8,128)(2,1)S(1)} %get-tuple-element.56), channel_id=1, source_target_pairs={{0,8},{8,0},{16,24},{24,16},{1,9},{9,1},{17,25},{25,17},{2,10},{10... | collective-permute-start | bytes 393224 | tf_op jit(solution)/shard_map/ppermute | solution.py:53
  49.3 0.8 %last_1.1 = (f32[512,256]{1,0:T(8,128)S(1)}, bf16[512,256]{1,0:T(8,128)(2,1)S(1)}) custom-call(f32[384,256]{1,0:T(8,128)S(1)} %get-tuple-element.52.refs_0_, bf16[384,256]{1,0:T(8,128)(2,1)S(1)} %collective-permute-done.11.refs_1_, bf16[2,384,768]{2,1,0:T(8,128)(2,1)S(1)} %get-tuple-element.47.refs_1_.refs_2_, ...), custom_call_target="tpu_custom_call" | custom-call | flops 6000000000 | tf_op jit(solution)/shard_map/last_1/pallas_call | solution.py:39
  50.2 0.8 collective-permute-start.12
  50.9 1.6 %collective-permute-done.7.refs_1_ = bf16[384,256]{1,0:T(8,128)(2,1)S(1)} collective-permute-done((bf16[384,256]{1,0:T(8,128)(2,1)S(1)}, bf16[384,256]{1,0:T(8,128)(2,1)S(1)}, u32[]{:S(2)}, u32[]{:S(2)}) %collective-permute-start.7) | collective-permute-done | bytes 196640 | tf_op jit(solution)/shard_map/ppermute | solution.py:53
  52.5 0.4 level3_2.1.refs_0_
  53.0 3.5 %collective-permute-done.12.refs_3_ = bf16[512,256]{1,0:T(8,128)(2,1)S(1)} collective-permute-done((bf16[512,256]{1,0:T(8,128)(2,1)S(1)}, bf16[512,256]{1,0:T(8,128)(2,1)S(1)}, u32[]{:S(2)}, u32[]{:S(2)}) %collective-permute-start.12) | collective-permute-done | bytes 262176 | tf_op jit(solution)/shard_map/ppermute | solution.py:53
  56.6 0.3 between_2.1
  56.9 1.6 %collective-permute-start.17 = (bf16[256,256]{1,0:T(8,128)(2,1)S(1)}, bf16[256,256]{1,0:T(8,128)(2,1)S(1)}, u32[]{:S(2)}, u32[]{:S(2)}) collective-permute-start(bf16[256,256]{1,0:T(8,128)(2,1)S(1)} %get-tuple-element.62), channel_id=1, source_target_pairs={{0,16},{8,24},{16,0},{24,8},{1,17},{9,25},{17,1},{25,9},{2,18},{10... | collective-permute-start | bytes 393224 | tf_op jit(solution)/shard_map/ppermute | solution.py:53
  58.5 0.8 %last_2.1 = (f32[512,256]{1,0:T(8,128)S(1)}, bf16[512,256]{1,0:T(8,128)(2,1)S(1)}) custom-call(f32[384,256]{1,0:T(8,128)S(1)} %get-tuple-element.58.refs_0_, bf16[384,256]{1,0:T(8,128)(2,1)S(1)} %collective-permute-done.15.refs_1_, bf16[2,384,768]{2,1,0:T(8,128)(2,1)S(1)} %get-tuple-element.47.refs_1_.refs_2_, ...), custom_call_target="tpu_custom_call" | custom-call | flops 6000000000 | tf_op jit(solution)/shard_map/last_2/pallas_call | solution.py:39
  59.3 0.6 collective-permute-start.16
  59.9 0.4 level3_3.1.refs_0_
  60.3 2.4 %collective-permute-done.17.refs_5_ = bf16[256,256]{1,0:T(8,128)(2,1)S(1)} collective-permute-done((bf16[256,256]{1,0:T(8,128)(2,1)S(1)}, bf16[256,256]{1,0:T(8,128)(2,1)S(1)}, u32[]{:S(2)}, u32[]{:S(2)}) %collective-permute-start.17) | collective-permute-done | bytes 131104 | tf_op jit(solution)/shard_map/ppermute | solution.py:53
  62.8 3.0 %collective-permute-done.16.refs_3_ = bf16[512,256]{1,0:T(8,128)(2,1)S(1)} collective-permute-done((bf16[512,256]{1,0:T(8,128)(2,1)S(1)}, bf16[512,256]{1,0:T(8,128)(2,1)S(1)}, u32[]{:S(2)}, u32[]{:S(2)}) %collective-permute-start.16) | collective-permute-done | bytes 262176 | tf_op jit(solution)/shard_map/ppermute | solution.py:53
  65.7 0.3 between_3.1
  66.1 1.4 %collective-permute-start.18 = (bf16[256,256]{1,0:T(8,128)(2,1)S(1)}, bf16[256,256]{1,0:T(8,128)(2,1)S(1)}, u32[]{:S(2)}, u32[]{:S(2)}) collective-permute-start(bf16[256,256]{1,0:T(8,128)(2,1)S(1)} %get-tuple-element.65), channel_id=1, source_target_pairs={{0,8},{8,0},{16,24},{24,16},{1,9},{9,1},{17,25},{25,17},{2,10},{10... | collective-permute-start | bytes 393224 | tf_op jit(solution)/shard_map/ppermute | solution.py:53
  67.4 0.8 %last_3.1 = (f32[256,256]{1,0:T(8,128)S(1)}, bf16[256,256]{1,0:T(8,128)(2,1)S(1)}, bf16[256,256]{1,0:T(8,128)(2,1)S(1)}, bf16[256,256]{1,0:T(8,128)(2,1)S(1)}) custom-call(f32[384,256]{1,0:T(8,128)S(1)} %get-tuple-element.66.refs_0_, bf16[384,256]{1,0:T(8,128)(2,1)S(1)} %collective-permute-done.19.refs_1_, ...), custom_call_target="tpu_custom_call" | custom-call | flops 6000000000 | tf_op jit(solution)/shard_map/last_3/pallas_call | solution.py:39
  68.3 0.8 %collective-permute-start.20 = (bf16[256,256]{1,0:T(8,128)(2,1)S(1)}, bf16[256,256]{1,0:T(8,128)(2,1)S(1)}, u32[]{:S(2)}, u32[]{:S(2)}) collective-permute-start(bf16[256,256]{1,0:T(8,128)(2,1)S(1)} %get-tuple-element.68), channel_id=1, source_target_pairs={{0,8},{8,0},{16,24},{24,16},{1,9},{9,1},{17,25},{25,17},{2,10},{10... | collective-permute-start | bytes 393224 | tf_op jit(solution)/shard_map/ppermute | solution.py:53
  69.0 0.8 %collective-permute-start.21 = (bf16[256,256]{1,0:T(8,128)(2,1)S(1)}, bf16[256,256]{1,0:T(8,128)(2,1)S(1)}, u32[]{:S(2)}, u32[]{:S(2)}) collective-permute-start(bf16[256,256]{1,0:T(8,128)(2,1)S(1)} %get-tuple-element.69), channel_id=1, source_target_pairs={{0,16},{8,24},{16,0},{24,8},{1,17},{9,25},{17,1},{25,9},{2,18},{10... | collective-permute-start | bytes 393224 | tf_op jit(solution)/shard_map/ppermute | solution.py:53
  69.8 2.0 %collective-permute-start.22 = (bf16[256,256]{1,0:T(8,128)(2,1)S(1)}, bf16[256,256]{1,0:T(8,128)(2,1)S(1)}, u32[]{:S(2)}, u32[]{:S(2)}) collective-permute-start(bf16[256,256]{1,0:T(8,128)(2,1)S(1)} %get-tuple-element.70), channel_id=1, source_target_pairs={{0,24},{8,16},{16,8},{24,0},{1,25},{9,17},{17,9},{25,1},{2,26},{10... | collective-permute-start | bytes 393224 | tf_op jit(solution)/shard_map/ppermute | solution.py:53
  71.8 0.5 collective-permute-done.18.refs_3_
  72.3 1.4 %collective-permute-done.20.refs_5_ = bf16[256,256]{1,0:T(8,128)(2,1)S(1)} collective-permute-done((bf16[256,256]{1,0:T(8,128)(2,1)S(1)}, bf16[256,256]{1,0:T(8,128)(2,1)S(1)}, u32[]{:S(2)}, u32[]{:S(2)}) %collective-permute-start.20) | collective-permute-done | bytes 131104 | tf_op jit(solution)/shard_map/ppermute | solution.py:53
  74.0 1.7 %collective-permute-done.22.refs_7_ = bf16[256,256]{1,0:T(8,128)(2,1)S(1)} collective-permute-done((bf16[256,256]{1,0:T(8,128)(2,1)S(1)}, bf16[256,256]{1,0:T(8,128)(2,1)S(1)}, u32[]{:S(2)}, u32[]{:S(2)}) %collective-permute-start.22) | collective-permute-done | bytes 131104 | tf_op jit(solution)/shard_map/ppermute | solution.py:53
  75.7 0.9 %end.1 = bf16[2,256,512]{2,1,0:T(8,128)(2,1)} custom-call(bf16[256,256]{1,0:T(8,128)(2,1)S(1)} %get-tuple-element.57.refs_0_, bf16[256,256]{1,0:T(8,128)(2,1)S(1)} %get-tuple-element.63.refs_1_, f32[256,256]{1,0:T(8,128)S(1)} %get-tuple-element.64.refs_2_, bf16[256,256]{1,0:T(8,128)(2,1)S(1)} %collective-permute-done.18.refs_3_, ...), custom_call_target="tpu_custom_call" | custom-call | tf_op jit(solution)/shard_map/end/pallas_call | solution.py:349
  (18 shorter events, 1.5 us)
Async XLA Ops:
  3.6 1.9 %collective-permute-start = (bf16[2,384,256]{2,1,0:T(8,128)(2,1)S(1)}, bf16[2,384,256]{2,1,0:T(8,128)(2,1)S(1)}, u32[]{:S(2)}, u32[]{:S(2)}) collective-permute-start(bf16[2,384,256]{2,1,0:T(8,128)(2,1)S(1)} %get-tuple-element.38.refs_0_.refs_3_), channel_id=1, source_target_pairs={{0,1},{1,0},{2,3},{3,2},{4,5},{5,4},{6,7},{7,6},{8,9},{9,8},{10,11... | collective-permute-start | bytes 1179656 | tf_op jit(solution)/shard_map/ppermute | solution.py:53
  4.2 17.5 %collective-permute-start.2 = (bf16[2,384,256]{2,1,0:T(8,128)(2,1)S(1)}, bf16[2,384,256]{2,1,0:T(8,128)(2,1)S(1)}, u32[]{:S(2)}, u32[]{:S(2)}) collective-permute-start(bf16[2,384,256]{2,1,0:T(8,128)(2,1)S(1)} %get-tuple-element.43.refs_3_.refs_6_), channel_id=1, source_target_pairs={{0,1},{1,0},{2,3},{3,2},{4,5},{5,4},{6,7},{7,6},{8,9},{9,8},{10,11... | collective-permute-start | bytes 1179656 | tf_op jit(solution)/shard_map/ppermute | solution.py:53
  6.0 15.6 %collective-permute-start.1 = (bf16[384,256]{1,0:T(8,128)(2,1)S(1)}, bf16[384,256]{1,0:T(8,128)(2,1)S(1)}, u32[]{:S(2)}, u32[]{:S(2)}) collective-permute-start(bf16[384,256]{1,0:T(8,128)(2,1)S(1)} %get-tuple-element.40.refs_0_), channel_id=1, source_target_pairs={{0,2},{1,3},{2,0},{3,1},{4,6},{5,7},{6,4},{7,5},{8,10},{9,11},{10,... | collective-permute-start | bytes 589832 | tf_op jit(solution)/shard_map/ppermute | solution.py:53
  9.0 9.4 %collective-permute-start.3 = (bf16[384,256]{1,0:T(8,128)(2,1)S(1)}, bf16[384,256]{1,0:T(8,128)(2,1)S(1)}, u32[]{:S(2)}, u32[]{:S(2)}) collective-permute-start(bf16[384,256]{1,0:T(8,128)(2,1)S(1)} %get-tuple-element.41.refs_3_.refs_0_), channel_id=1, source_target_pairs={{0,2},{1,3},{2,0},{3,1},{4,6},{5,7},{6,4},{7,5},{8,10},{9,11},{10,... | collective-permute-start | bytes 589832 | tf_op jit(solution)/shard_map/ppermute | solution.py:53
  18.8 12.7 %collective-permute-start.5 = (bf16[384,256]{1,0:T(8,128)(2,1)S(1)}, bf16[384,256]{1,0:T(8,128)(2,1)S(1)}, u32[]{:S(2)}, u32[]{:S(2)}) collective-permute-start(bf16[384,256]{1,0:T(8,128)(2,1)S(1)} %level2_0.1.refs_9_.refs_0_), channel_id=1, source_target_pairs={{0,4},{1,5},{2,6},{3,7},{4,0},{5,1},{6,2},{7,3},{8,12},{9,13},{10,... | collective-permute-start | bytes 589832 | tf_op jit(solution)/shard_map/ppermute | solution.py:53
  22.3 15.2 %collective-permute-start.4 = (bf16[384,256]{1,0:T(8,128)(2,1)S(1)}, bf16[384,256]{1,0:T(8,128)(2,1)S(1)}, u32[]{:S(2)}, u32[]{:S(2)}) collective-permute-start(bf16[384,256]{1,0:T(8,128)(2,1)S(1)} %get-tuple-element.44.refs_0_), channel_id=1, source_target_pairs={{0,2},{1,3},{2,0},{3,1},{4,6},{5,7},{6,4},{7,5},{8,10},{9,11},{10,... | collective-permute-start | bytes 589832 | tf_op jit(solution)/shard_map/ppermute | solution.py:53
  24.0 16.0 %collective-permute-start.9 = (bf16[384,256]{1,0:T(8,128)(2,1)S(1)}, bf16[384,256]{1,0:T(8,128)(2,1)S(1)}, u32[]{:S(2)}, u32[]{:S(2)}) collective-permute-start(bf16[384,256]{1,0:T(8,128)(2,1)S(1)} %get-tuple-element.50.refs_0_), channel_id=1, source_target_pairs={{0,2},{1,3},{2,0},{3,1},{4,6},{5,7},{6,4},{7,5},{8,10},{9,11},{10,... | collective-permute-start | bytes 589832 | tf_op jit(solution)/shard_map/ppermute | solution.py:53
  24.4 18.2 %collective-permute-start.8 = (bf16[384,256]{1,0:T(8,128)(2,1)S(1)}, bf16[384,256]{1,0:T(8,128)(2,1)S(1)}, u32[]{:S(2)}, u32[]{:S(2)}) collective-permute-start(bf16[384,256]{1,0:T(8,128)(2,1)S(1)} %get-tuple-element.46.refs_3_.refs_0_), channel_id=1, source_target_pairs={{0,4},{1,5},{2,6},{3,7},{4,0},{5,1},{6,2},{7,3},{8,12},{9,13},{10,... | collective-permute-start | bytes 589832 | tf_op jit(solution)/shard_map/ppermute | solution.py:53
  31.9 1.5 %collective-permute-start.6 = (bf16[384,256]{1,0:T(8,128)(2,1)S(1)}, bf16[384,256]{1,0:T(8,128)(2,1)S(1)}, u32[]{:S(2)}, u32[]{:S(2)}) collective-permute-start(bf16[384,256]{1,0:T(8,128)(2,1)S(1)} %level3_0.1.refs_0_), channel_id=1, source_target_pairs={{0,1},{1,0},{2,3},{3,2},{4,5},{5,4},{6,7},{7,6},{8,9},{9,8},{10,11... | collective-permute-start | bytes 589832 | tf_op jit(solution)/shard_map/ppermute | solution.py:53
  37.9 14.6 %collective-permute-start.7 = (bf16[384,256]{1,0:T(8,128)(2,1)S(1)}, bf16[384,256]{1,0:T(8,128)(2,1)S(1)}, u32[]{:S(2)}, u32[]{:S(2)}) collective-permute-start(bf16[384,256]{1,0:T(8,128)(2,1)S(1)} %level2_2.1.refs_3_.refs_0_), channel_id=1, source_target_pairs={{0,4},{1,5},{2,6},{3,7},{4,0},{5,1},{6,2},{7,3},{8,12},{9,13},{10,... | collective-permute-start | bytes 589832 | tf_op jit(solution)/shard_map/ppermute | solution.py:53
  40.4 19.5 %collective-permute-start.14 = (bf16[384,256]{1,0:T(8,128)(2,1)S(1)}, bf16[384,256]{1,0:T(8,128)(2,1)S(1)}, u32[]{:S(2)}, u32[]{:S(2)}) collective-permute-start(bf16[384,256]{1,0:T(8,128)(2,1)S(1)} %level2_3.1.refs_3_.refs_0_), channel_id=1, source_target_pairs={{0,4},{1,5},{2,6},{3,7},{4,0},{5,1},{6,2},{7,3},{8,12},{9,13},{10,... | collective-permute-start | bytes 589832 | tf_op jit(solution)/shard_map/ppermute | solution.py:53
  41.3 6.4 %collective-permute-start.10 = (bf16[512,256]{1,0:T(8,128)(2,1)S(1)}, bf16[512,256]{1,0:T(8,128)(2,1)S(1)}, u32[]{:S(2)}, u32[]{:S(2)}) collective-permute-start(bf16[512,256]{1,0:T(8,128)(2,1)S(1)} %get-tuple-element.51), channel_id=1, source_target_pairs={{0,16},{8,24},{16,0},{24,8},{1,17},{9,25},{17,1},{25,9},{2,18},{10... | collective-permute-start | bytes 786440 | tf_op jit(solution)/shard_map/ppermute | solution.py:53
  43.0 6.3 %collective-permute-start.11 = (bf16[384,256]{1,0:T(8,128)(2,1)S(1)}, bf16[384,256]{1,0:T(8,128)(2,1)S(1)}, u32[]{:S(2)}, u32[]{:S(2)}) collective-permute-start(bf16[384,256]{1,0:T(8,128)(2,1)S(1)} %level3_1.1.refs_0_), channel_id=1, source_target_pairs={{0,1},{1,0},{2,3},{3,2},{4,5},{5,4},{6,7},{7,6},{8,9},{9,8},{10,11... | collective-permute-start | bytes 589832 | tf_op jit(solution)/shard_map/ppermute | solution.py:53
  47.9 5.1 %collective-permute-start.13 = (bf16[256,256]{1,0:T(8,128)(2,1)S(1)}, bf16[256,256]{1,0:T(8,128)(2,1)S(1)}, u32[]{:S(2)}, u32[]{:S(2)}) collective-permute-start(bf16[256,256]{1,0:T(8,128)(2,1)S(1)} %get-tuple-element.56), channel_id=1, source_target_pairs={{0,8},{8,0},{16,24},{24,16},{1,9},{9,1},{17,25},{25,17},{2,10},{10... | collective-permute-start | bytes 393224 | tf_op jit(solution)/shard_map/ppermute | solution.py:53
  50.2 6.4 %collective-permute-start.12 = (bf16[512,256]{1,0:T(8,128)(2,1)S(1)}, bf16[512,256]{1,0:T(8,128)(2,1)S(1)}, u32[]{:S(2)}, u32[]{:S(2)}) collective-permute-start(bf16[512,256]{1,0:T(8,128)(2,1)S(1)} %get-tuple-element.54), channel_id=1, source_target_pairs={{0,8},{8,0},{16,24},{24,16},{1,9},{9,1},{17,25},{25,17},{2,10},{10... | collective-permute-start | bytes 786440 | tf_op jit(solution)/shard_map/ppermute | solution.py:53
  52.9 5.6 %collective-permute-start.15 = (bf16[384,256]{1,0:T(8,128)(2,1)S(1)}, bf16[384,256]{1,0:T(8,128)(2,1)S(1)}, u32[]{:S(2)}, u32[]{:S(2)}) collective-permute-start(bf16[384,256]{1,0:T(8,128)(2,1)S(1)} %level3_2.1.refs_0_), channel_id=1, source_target_pairs={{0,1},{1,0},{2,3},{3,2},{4,5},{5,4},{6,7},{7,6},{8,9},{9,8},{10,11... | collective-permute-start | bytes 589832 | tf_op jit(solution)/shard_map/ppermute | solution.py:53
  56.9 5.9 %collective-permute-start.17 = (bf16[256,256]{1,0:T(8,128)(2,1)S(1)}, bf16[256,256]{1,0:T(8,128)(2,1)S(1)}, u32[]{:S(2)}, u32[]{:S(2)}) collective-permute-start(bf16[256,256]{1,0:T(8,128)(2,1)S(1)} %get-tuple-element.62), channel_id=1, source_target_pairs={{0,16},{8,24},{16,0},{24,8},{1,17},{9,25},{17,1},{25,9},{2,18},{10... | collective-permute-start | bytes 393224 | tf_op jit(solution)/shard_map/ppermute | solution.py:53
  59.3 6.4 %collective-permute-start.16 = (bf16[512,256]{1,0:T(8,128)(2,1)S(1)}, bf16[512,256]{1,0:T(8,128)(2,1)S(1)}, u32[]{:S(2)}, u32[]{:S(2)}) collective-permute-start(bf16[512,256]{1,0:T(8,128)(2,1)S(1)} %get-tuple-element.60), channel_id=1, source_target_pairs={{0,16},{8,24},{16,0},{24,8},{1,17},{9,25},{17,1},{25,9},{2,18},{10... | collective-permute-start | bytes 786440 | tf_op jit(solution)/shard_map/ppermute | solution.py:53
  60.2 7.2 %collective-permute-start.19 = (bf16[384,256]{1,0:T(8,128)(2,1)S(1)}, bf16[384,256]{1,0:T(8,128)(2,1)S(1)}, u32[]{:S(2)}, u32[]{:S(2)}) collective-permute-start(bf16[384,256]{1,0:T(8,128)(2,1)S(1)} %level3_3.1.refs_0_), channel_id=1, source_target_pairs={{0,1},{1,0},{2,3},{3,2},{4,5},{5,4},{6,7},{7,6},{8,9},{9,8},{10,11... | collective-permute-start | bytes 589832 | tf_op jit(solution)/shard_map/ppermute | solution.py:53
  66.1 6.3 %collective-permute-start.18 = (bf16[256,256]{1,0:T(8,128)(2,1)S(1)}, bf16[256,256]{1,0:T(8,128)(2,1)S(1)}, u32[]{:S(2)}, u32[]{:S(2)}) collective-permute-start(bf16[256,256]{1,0:T(8,128)(2,1)S(1)} %get-tuple-element.65), channel_id=1, source_target_pairs={{0,8},{8,0},{16,24},{24,16},{1,9},{9,1},{17,25},{25,17},{2,10},{10... | collective-permute-start | bytes 393224 | tf_op jit(solution)/shard_map/ppermute | solution.py:53
  68.3 5.5 %collective-permute-start.20 = (bf16[256,256]{1,0:T(8,128)(2,1)S(1)}, bf16[256,256]{1,0:T(8,128)(2,1)S(1)}, u32[]{:S(2)}, u32[]{:S(2)}) collective-permute-start(bf16[256,256]{1,0:T(8,128)(2,1)S(1)} %get-tuple-element.68), channel_id=1, source_target_pairs={{0,8},{8,0},{16,24},{24,16},{1,9},{9,1},{17,25},{25,17},{2,10},{10... | collective-permute-start | bytes 393224 | tf_op jit(solution)/shard_map/ppermute | solution.py:53
  69.0 5.0 %collective-permute-start.21 = (bf16[256,256]{1,0:T(8,128)(2,1)S(1)}, bf16[256,256]{1,0:T(8,128)(2,1)S(1)}, u32[]{:S(2)}, u32[]{:S(2)}) collective-permute-start(bf16[256,256]{1,0:T(8,128)(2,1)S(1)} %get-tuple-element.69), channel_id=1, source_target_pairs={{0,16},{8,24},{16,0},{24,8},{1,17},{9,25},{17,1},{25,9},{2,18},{10... | collective-permute-start | bytes 393224 | tf_op jit(solution)/shard_map/ppermute | solution.py:53
  69.8 5.9 %collective-permute-start.22 = (bf16[256,256]{1,0:T(8,128)(2,1)S(1)}, bf16[256,256]{1,0:T(8,128)(2,1)S(1)}, u32[]{:S(2)}, u32[]{:S(2)}) collective-permute-start(bf16[256,256]{1,0:T(8,128)(2,1)S(1)} %get-tuple-element.70), channel_id=1, source_target_pairs={{0,24},{8,16},{16,8},{24,0},{1,25},{9,17},{17,9},{25,1},{2,26},{10... | collective-permute-start | bytes 393224 | tf_op jit(solution)/shard_map/ppermute | solution.py:53

commit v4 on v3

v4 whole, which is shorter than its diff:
```python
import functools

import jax
import jax.numpy as jnp
from jax import lax
from jax.experimental import pallas as pl
from jax.experimental.pallas import tpu as pltpu
from jax.sharding import PartitionSpec as P

SHARES = (1, 2, 3, 2)
PRELOADED = 2
COST = 6 * 10**9
BF16 = jnp.bfloat16
F32 = jnp.float32
ANY = pl.BlockSpec(memory_space=pl.ANY)
VMEM = pl.BlockSpec(memory_space=pltpu.VMEM)


def dot(a, b):
    return jnp.dot(a, b, preferred_element_type=F32)


def in_vmem(*shape, dtype=BF16):
    return pltpu.VMEM(shape, dtype)


def here(value):
    return pltpu.with_memory_space_constraint(value, pltpu.VMEM)


def in_hbm(value):
    return pltpu.with_memory_space_constraint(value, pltpu.HBM)


def call(kernel, name, in_specs, out_shape, scratch, args, after=(), flops=COST, limit=8 * 2**20):
    count = len(in_specs)

    def body(*refs):
        kernel(*refs[:count], *refs[count + len(after) :])

    return pl.pallas_call(
        body,
        name=name,
        in_specs=[*in_specs, *[ANY] * len(after)],
        out_specs=[VMEM] * len(out_shape),
        out_shape=out_shape,
        scratch_shapes=scratch,
        compiler_params=pltpu.CompilerParams(vmem_limit_bytes=limit),
        cost_estimate=pl.CostEstimate(flops=flops, bytes_accessed=0, transcendentals=0),
    )(*args, *after)


def partner(value, axis, mask):
    pairs = [(source, source ^ mask) for source in range(lax.axis_size(axis))]
    return lax.ppermute(value, axis, pairs)


def leaf_kernel(excite, leaves, blocks, index, first, rest, *refs):
    count = PRELOADED
    nexts = refs[:count]
    excite_v, leaves_v, blocks_v, index_s, coeff, sems = refs[count:]
    slots, rank = leaves.shape[0], leaves.shape[1]
    columns, width = excite.shape[2], first.shape[1]
    listing = pltpu.make_async_copy(index, index_s, sems.at[0])
    listing.start()
    loads = []
    for s in range(slots):
        a = pltpu.make_async_copy(leaves.at[s], leaves_v.at[s], sems.at[1 + s])
        b = pltpu.make_async_copy(excite.at[s], excite_v.at[s], sems.at[3 + s])
        a.start()
        b.start()
        loads.append((a, b))
    listing.wait()
    weights, later = [], []
    for s in range(slots):
        c = pltpu.make_async_copy(blocks.at[0, index_s[s, 0]], blocks_v.at[s], sems.at[5 + s])
        c.start()
        weights.append(c)
    for level in range(1, 1 + count):
        for s in range(slots):
            c = pltpu.make_async_copy(
                blocks.at[level, index_s[s, level]], nexts[level - 1].at[s], sems.at[5 + 2 * level + s]
            )
            c.start()
            later.append(c)
    for s in range(slots):
        for load in loads[s]:
            load.wait()
        coeff[s * rank : (s + 1) * rank, :] = dot(leaves_v[s], excite_v[s]).astype(BF16)
    for s in range(slots):
        weights[s].wait()
        out = dot(blocks_v[s], coeff[...]).astype(BF16)
        if s == 0:
            first[...] = out[:, :width]
            rest[:, : columns - width] = out[:, width:]
        else:
            rest[:, s * columns - width : (s + 1) * columns - width] = out
    for c in later:
        c.wait()


def prefetch_kernel(blocks, basis, index, *refs):
    count = blocks.shape[0] - 1 - PRELOADED
    outs, basis_v, index_s, sems = refs[:count], refs[count], refs[count + 1], refs[count + 2]
    listing = pltpu.make_async_copy(index, index_s, sems.at[0])
    listing.start()
    c = pltpu.make_async_copy(basis, basis_v, sems.at[1 + 2 * count])
    c.start()
    copies = [c]
    listing.wait()
    for at in range(count):
        level = at + 1 + PRELOADED
        for s in range(2):
            c = pltpu.make_async_copy(blocks.at[level, index_s[s, level]], outs[at].at[s], sems.at[1 + 2 * at + s])
            c.start()
            copies.append(c)
    for c in copies:
        c.wait()


def upper_half(bit):
    return (lax.axis_index("box") >> bit) & 1


def mix(weights, own, other, bit, buf, parts, out):
    rank = own.shape[0]
    upper = upper_half(bit)
    buf[pl.ds(pl.multiple_of(upper * rank, rank), rank), :] = own
    buf[pl.ds(pl.multiple_of((1 - upper) * rank, rank), rank), :] = other
    for s, start, stop in parts:
        out[:, start:stop] = dot(weights[s], buf[:, start:stop]).astype(BF16)


def levels_kernel(jobs, *refs):
    count = len(jobs)
    ins, outs, bufs = refs[: 3 * count], refs[3 * count : 4 * count], refs[4 * count :]
    for at, (bit, parts, lanes) in enumerate(jobs):
        own, other, weights = ins[3 * at : 3 * at + 3]
        mix(weights, own[:, lanes], other[:, lanes], bit, bufs[at], parts, outs[at])


def half_dot(weights, s, half, value):
    rank = value.shape[0]
    return dot(weights[s, :, pl.ds(pl.multiple_of(half * rank, 128), rank)], value)


def between_kernel(bit, parts, fold, total, own, weights, *refs):
    refs = list(refs)
    ins = [refs.pop(0) for _ in range(2 * (fold + total))]
    partial = refs.pop(0)
    for s, start, stop in parts:
        partial[:, start:stop] = half_dot(weights, s, upper_half(bit), own[:, start:stop])
    if fold:
        fold_kernel(ins.pop(0), ins.pop(0), refs.pop(0), refs.pop(0))
    if total:
        keep, got = ins.pop(0), ins.pop(0)
        refs.pop(0)[...] = (keep[...] + got[...].astype(F32)).astype(BF16)


def last_kernel(bit, parts, order, partial, other, weights, basis, *refs):
    rows = basis.shape[1] // lax.axis_size("blk")
    me = lax.axis_index("blk")
    for s, start, stop in parts:
        mixed = partial[:, start:stop] + half_dot(weights, s, 1 - upper_half(bit), other[:, start:stop])
        coeff = mixed.astype(BF16)
        for ref, distances in zip(refs, order):
            for at, d in enumerate(distances):
                row = pl.multiple_of((me ^ d) * rows, rows)
                piece = dot(basis[s, pl.ds(row, rows), :], coeff)
                ref[at * rows : (at + 1) * rows, start:stop] = piece.astype(ref.dtype)


def fold_kernel(keep, got, send, rest):
    rows = rest.shape[0]
    rest[...] = keep[:rows] + got[:rows].astype(F32)
    send[...] = (keep[rows:] + got[rows:].astype(F32)).astype(BF16)


def end_kernel(places, counts, *refs):
    refs = list(refs)
    out = refs[-1]
    for place, count in zip(places, counts):
        group = [refs.pop(0) for _ in range(count)]
        for s, column, start, stop in place:
            total = group[0][:, start:stop].astype(F32)
            for piece in group[1:]:
                total = total + piece[:, start:stop].astype(F32)
            out[s, :, column : column + stop - start] = total.astype(BF16)


def on_device(excitation, leaf_basis, transfer, transfer_index, out_basis):
    excite, leaves, blocks, basis = excitation[0], leaf_basis[0], transfer[0], out_basis[0]
    index = transfer_index[0].T
    slots, rank, points = leaves.shape
    levels = blocks.shape[0]
    columns = excite.shape[2]
    n_blk = lax.axis_size("blk")
    rows = basis.shape[1] // n_blk
    nbits = lax.axis_size("box").bit_length() - 1
    bits = [None] + [(level - 1) % nbits for level in range(1, levels)]
    pair = in_vmem(slots, rank, 2 * rank)

    unit = slots * columns // sum(SHARES)
    widths = [unit * share for share in SHARES]
    begins = [sum(widths[:j]) for j in range(len(widths))]
    parts, places = [], []
    for begin, width in zip(begins, widths):
        part, place, lane = [], [], 0
        while lane < width:
            s, column = divmod(begin + lane, columns)
            size = min(width - lane, columns - column)
            part.append((s, lane, lane + size))
            place.append((s, column, lane, lane + size))
            lane += size
        parts.append(part)
        places.append(place)

    first, rest, *weights = call(
        leaf_kernel,
        "leaf",
        [ANY] * 4,
        [in_vmem(rank, widths[0]), in_vmem(rank, slots * columns - widths[0])] + [pair] * PRELOADED,
        [
            in_vmem(*excite.shape),
            in_vmem(*leaves.shape),
            pair,
            pltpu.SMEM(index.shape, jnp.int32),
            in_vmem(2 * rank, columns),
            pltpu.SemaphoreType.DMA((7 + 2 * PRELOADED,)),
        ],
        [in_hbm(excite), in_hbm(leaves), in_hbm(blocks), in_hbm(index)],
        limit=24 * 2**20,
    )
    weights = [None, *weights]

    def cross(level, value):
        return partner(value, "box", 2 ** bits[level])

    near_first, near_rest = cross(1, first), cross(1, rest)

    def step(name, jobs, after=(), flops=COST):
        args = [here(v) for level, j, own, other in jobs for v in (own, other, weights[level])]
        described, sizes = [], []
        for level, j, _, _ in jobs:
            begin = begins[j] - widths[0] if level == 1 and j else 0
            described.append((bits[level], parts[j], slice(begin, begin + widths[j])))
            sizes.append(widths[j])
        return call(
            functools.partial(levels_kernel, described),
            name,
            [VMEM] * len(args),
            [in_vmem(rank, size) for size in sizes],
            [in_vmem(2 * rank, size) for size in sizes],
            args,
            after,
            flops,
        )

    def job1(j):
        return (1, j, rest, near_rest) if j else (1, j, first, near_first)

    coeff2, near2, coeff3, near3 = {}, {}, {}, {}

    def second(j, value):
        coeff2[j] = value
        near2[j] = cross(2, value)

    def third(j, value):
        coeff3[j] = value
        near3[j] = cross(3, value)

    (value,) = step("level1_0", [job1(0)])
    second(0, value)
    (value,) = step("level1_1", [job1(1)], [coeff2[0]])
    second(1, value)
    value, ahead = step("level2_0", [(2, 0, coeff2[0], near2[0]), job1(2)], [coeff2[1]])
    third(0, value)
    second(2, ahead)
    *more, basis_v = call(
        prefetch_kernel,
        "prefetch",
        [ANY] * 3,
        [pair] * (levels - 1 - PRELOADED) + [in_vmem(*basis.shape)],
        [pltpu.SMEM(index.shape, jnp.int32), pltpu.SemaphoreType.DMA((2 * levels,))],
        [in_hbm(blocks), in_hbm(basis), in_hbm(index)],
        [coeff3[0]],
    )
    weights += more
    value, ahead = step("level2_1", [(2, 1, coeff2[1], near2[1]), job1(3)], [basis_v])
    third(1, value)
    second(3, ahead)

    masks = [1 << b for b in range(n_blk.bit_length() - 1)]

    def halving(j):
        order = masks if j % 2 else masks[::-1]
        pieces = [0]
        for mask in order[::-1]:
            pieces = pieces + [d | mask for d in pieces]
        return order, pieces

    def result(j, count, dtype):
        return in_vmem(count * rows, widths[j], dtype=dtype)

    def tail(j, after, direct, folding=None, totalling=None):
        (coeff4,) = step(f"level3_{j}", [(3, j, coeff3[j], near3[j])], after, flops=0 if j == 1 else COST)
        near4 = cross(4, coeff4)
        outs, extra = [in_vmem(rank, widths[j], dtype=F32)], []
        if folding is not None:
            at, keep, got, count = folding
            extra += [keep, got]
            outs += [result(at, count // 2, BF16), result(at, count // 2, F32)]
        if totalling is not None:
            at, keep, got = totalling
            extra += [keep, got]
            outs += [result(at, 1, BF16)]
        partial, *more = call(
            functools.partial(
                between_kernel, bits[4], parts[j], folding is not None, totalling is not None
            ),
            f"between_{j}",
            [VMEM] * (2 + len(extra)),
            outs,
            [],
            [here(v) for v in (coeff4, weights[4], *extra)],
        )
        if direct:
            order = [[d] for d in range(n_blk)]
        else:
            pieces = halving(j)[1]
            order = [pieces[: n_blk // 2], pieces[n_blk // 2 :]]
        kinds = [F32] + [BF16] * (len(order) - 1)
        out = call(
            functools.partial(last_kernel, bits[4], parts[j], order),
            f"last_{j}",
            [VMEM] * 4,
            [result(j, len(o), kind) for o, kind in zip(order, kinds)],
            [],
            [here(v) for v in (partial, near4, weights[4], basis_v)],
        )
        return out, more

    def begin_sum(j, out):
        keep, send = out
        order = halving(j)[0]
        got, count = partner(send, "blk", order[0]), n_blk // 2
        for mask in order[1:-1]:
            send, keep = call(
                fold_kernel,
                f"fold_{j}_{mask}",
                [VMEM] * 2,
                [result(j, count // 2, BF16), result(j, count // 2, F32)],
                [],
                [here(keep), here(got)],
            )
            got, count = partner(send, "blk", mask), count // 2
        return j, keep, got, count

    def direct_sum(out):
        return [out[0]] + [partner(out[d], "blk", d) for d in range(n_blk - 1, 0, -1)]

    out0, _ = tail(0, [coeff3[1]], False)
    fold0 = begin_sum(0, out0)
    (value,) = step("level2_2", [(2, 2, coeff2[2], near2[2])], [out0[0]])
    third(2, value)
    (value,) = step("level2_3", [(2, 3, coeff2[3], near2[3])], [coeff3[2]])
    third(3, value)
    out1, (send0, keep0) = tail(1, [coeff3[3]], False, fold0)
    got0 = partner(send0, "blk", halving(0)[0][-1])
    fold1 = begin_sum(1, out1)
    out2, (send1, keep1, total0) = tail(2, [out1[0]], True, fold1, (0, keep0, got0))
    got1 = partner(send1, "blk", halving(1)[0][-1])
    group2 = direct_sum(out2)
    out3, (total1,) = tail(3, [out2[0]], True, None, (1, keep1, got1))
    group3 = direct_sum(out3)
    groups = [[total0], [total1], group2, group3]
    flat = [here(v) for group in groups for v in group]
    return pl.pallas_call(
        functools.partial(end_kernel, places, [len(group) for group in groups]),
        name="end",
        in_specs=[VMEM] * len(flat),
        out_specs=VMEM,
        out_shape=jax.ShapeDtypeStruct((slots, rows, columns), BF16),
        compiler_params=pltpu.CompilerParams(vmem_limit_bytes=8 * 2**20),
    )(*flat)


def solution(mesh):
    in_specs = (
        P("blk", "box", None, None),
        P("blk", "box", None, None),
        P("blk", None, "box", None, None),
        P("blk", None, "box"),
        P("blk", "box", None, None),
    )
    out_specs = P("box", "blk", None)
    return jax.shard_map(
        on_device, mesh=mesh, in_specs=in_specs, out_specs=out_specs, check_vma=False
    )
```

time: 76.7 us -> 75.1 us (0.979)
  waiting for transfers between devices: 39.8 us -> 33.3 us
  starting transfers between devices: 20.8 us -> 25.4 us
    ppermute x23 -> x24, waiting for transfers between devices: 39.8 us -> 33.3 us  [partner(): return lax.ppermute(value, axis, pairs)]
    ppermute x23 -> x24, starting transfers between devices: 20.8 us -> 25.4 us  [partner(): return lax.ppermute(value, axis, pairs)]
    pallas_call x19 -> x20, Pallas kernels: 14.9 us -> 15 us  [call(): pl.pallas_call(body, name=name, in_specs=[*in_specs, *[ANY] * len(after)]...]
  transfers between devices with their start and end apart: 23 -> 24, of which waited for: 16 -> 10; matrix products, arithmetic and copies ran while one was open for 0% -> 0% of each run, Pallas kernels for 15% -> 15%
where the time goes in v4:
time: 75.1 us; the launch traced here: 74.9 us
  waiting for transfers between devices  33.3 us (44%)
  starting transfers between devices  25.4 us (34%)
  Pallas kernels  16 us (21%)
    ppermute x24, waiting for transfers between devices, partner(): return lax.ppermute(value, axis, pairs)  33.3 us
    ppermute x24, starting transfers between devices, partner(): return lax.ppermute(value, axis, pairs)  25.4 us
    pallas_call x20, Pallas kernels, call(): pl.pallas_call(body, name=name, in_specs=[*in_specs, *[ANY] * len(after)]...  15 us
  transfers between devices with their start and end apart: 24, of which 10 were waited for; matrix products, arithmetic and copies ran while one was open for 0% of the time, Pallas kernels for 15%

profile of v4, /device:TPU:0, one launch (start us, length us, event | category | flops | bytes accessed | tf_op | source)
XLA Modules:
  0.0 74.9 jit_solution(15560563341505510751)
XLA Ops:
  0.0 3.7 %leaf.1 = (bf16[384,128]{1,0:T(8,128)(2,1)S(1)}, bf16[384,896]{1,0:T(8,128)(2,1)S(1)}, bf16[2,384,768]{2,1,0:T(8,128)(2,1)S(1)}, bf16[2,384,768]{2,1,0:T(8,128)(2,1)S(1)}) custom-call(bf16[2,1024,512]{2,1,0:T(8,128)(2,1)} %bitcast.9, bf16[2,384,1024]{2,1,0:T(8,128)(2,1)} %bitcast.10, bf16[5,2,384,768]{3,2,1,0:T(8,128)(2,1)} %bitcast.7, s32[2,5]{1,0:T(2,128)} %bitcast.12), custom_call_target="tpu_custom_call" | custom-call | flops 6000000000 | tf_op jit(solution)/shard_map/leaf/pallas_call | solution.py:41
  3.7 0.5 collective-permute-start.2
  4.3 1.8 %collective-permute-done.refs_1_ = bf16[384,128]{1,0:T(8,128)(2,1)S(1)} collective-permute-done((bf16[384,128]{1,0:T(8,128)(2,1)S(1)}, bf16[384,128]{1,0:T(8,128)(2,1)S(1)}, u32[]{:S(2)}, u32[]{:S(2)}) %collective-permute-start) | collective-permute-done | bytes 98336 | tf_op jit(solution)/shard_map/ppermute | solution.py:55
  6.1 0.3 level1_0.1.refs_3_.refs_0_
  6.4 3.0 %collective-permute-start.1 = (bf16[384,128]{1,0:T(8,128)(2,1)S(1)}, bf16[384,128]{1,0:T(8,128)(2,1)S(1)}, u32[]{:S(2)}, u32[]{:S(2)}) collective-permute-start(bf16[384,128]{1,0:T(8,128)(2,1)S(1)} %level1_0.1.refs_3_.refs_0_), channel_id=1, source_target_pairs={{0,2},{1,3},{2,0},{3,1},{4,6},{5,7},{6,4},{7,5},{8,10},{9,11},{10,... | collective-permute-start | bytes 294920 | tf_op jit(solution)/shard_map/ppermute | solution.py:55
  9.5 0.4 level1_1.1.refs_6_.refs_0_
  9.9 2.8 %collective-permute-done.1.refs_1_ = bf16[384,128]{1,0:T(8,128)(2,1)S(1)} collective-permute-done((bf16[384,128]{1,0:T(8,128)(2,1)S(1)}, bf16[384,128]{1,0:T(8,128)(2,1)S(1)}, u32[]{:S(2)}, u32[]{:S(2)}) %collective-permute-start.1) | collective-permute-done | bytes 98336 | tf_op jit(solution)/shard_map/ppermute | solution.py:55
  12.7 0.7 level2_0.1
  13.4 3.0 %collective-permute-start.4 = (bf16[384,128]{1,0:T(8,128)(2,1)S(1)}, bf16[384,128]{1,0:T(8,128)(2,1)S(1)}, u32[]{:S(2)}, u32[]{:S(2)}) collective-permute-start(bf16[384,128]{1,0:T(8,128)(2,1)S(1)} %get-tuple-element.42.refs_3_.refs_0_), channel_id=1, source_target_pairs={{0,4},{1,5},{2,6},{3,7},{4,0},{5,1},{6,2},{7,3},{8,12},{9,13},{10,... | collective-permute-start | bytes 294920 | tf_op jit(solution)/shard_map/ppermute | solution.py:55
  16.4 2.5 %prefetch.1 = (bf16[2,384,768]{2,1,0:T(8,128)(2,1)S(1)}, bf16[2,384,768]{2,1,0:T(8,128)(2,1)S(1)}, bf16[2,1024,384]{2,1,0:T(8,128)(2,1)S(1)}) custom-call(bf16[5,2,384,768]{3,2,1,0:T(8,128)(2,1)} %bitcast.8, bf16[2,1024,384]{2,1,0:T(8,128)(2,1)} %bitcast.11, s32[2,5]{1,0:T(2,128)} %bitcast.13, bf16[384,128]{1,0:T(8,128)(2,1)S(1)} %get-tuple-element.42.refs_3_.refs_0_), custom_call_target="tpu_custom_call" | custom-call | flops 6000000000 | tf_op jit(solution)/shard_map/prefetch/pallas_call | solution.py:41
  18.9 2.0 %collective-permute-start.3 = (bf16[384,384]{1,0:T(8,128)(2,1)S(1)}, bf16[384,384]{1,0:T(8,128)(2,1)S(1)}, u32[]{:S(2)}, u32[]{:S(2)}) collective-permute-start(bf16[384,384]{1,0:T(8,128)(2,1)S(1)} %get-tuple-element.41.refs_0_), channel_id=1, source_target_pairs={{0,2},{1,3},{2,0},{3,1},{4,6},{5,7},{6,4},{7,5},{8,10},{9,11},{10,... | collective-permute-start | bytes 884744 | tf_op jit(solution)/shard_map/ppermute | solution.py:55
  21.0 0.5 level2_1.1
  21.5 0.4 collective-permute-start.8
  21.9 0.3 level3_0.1.refs_0_
  22.6 0.6 collective-permute-start.9
  23.2 0.4 collective-permute-done.6.refs_1_
  23.6 0.6 last_0.1
  24.2 1.6 %collective-permute-start.10 = (bf16[512,128]{1,0:T(8,128)(2,1)S(1)}, bf16[512,128]{1,0:T(8,128)(2,1)S(1)}, u32[]{:S(2)}, u32[]{:S(2)}) collective-permute-start(bf16[512,128]{1,0:T(8,128)(2,1)S(1)} %get-tuple-element.49), channel_id=1, source_target_pairs={{0,16},{8,24},{16,0},{24,8},{1,17},{9,25},{17,1},{25,9},{2,18},{10... | collective-permute-start | bytes 393224 | tf_op jit(solution)/shard_map/ppermute | solution.py:55
  25.8 9.5 %collective-permute-done.3.refs_1_ = bf16[384,384]{1,0:T(8,128)(2,1)S(1)} collective-permute-done((bf16[384,384]{1,0:T(8,128)(2,1)S(1)}, bf16[384,384]{1,0:T(8,128)(2,1)S(1)}, u32[]{:S(2)}, u32[]{:S(2)}) %collective-permute-start.3) | collective-permute-done | bytes 294944 | tf_op jit(solution)/shard_map/ppermute | solution.py:55
  35.3 0.5 level2_2.1.refs_3_.refs_0_
  35.9 2.2 %collective-permute-done.9.refs_1_ = bf16[384,256]{1,0:T(8,128)(2,1)S(1)} collective-permute-done((bf16[384,256]{1,0:T(8,128)(2,1)S(1)}, bf16[384,256]{1,0:T(8,128)(2,1)S(1)}, u32[]{:S(2)}, u32[]{:S(2)}) %collective-permute-start.9) | collective-permute-done | bytes 196640 | tf_op jit(solution)/shard_map/ppermute | solution.py:55
  38.1 0.4 level2_3.1.refs_3_.refs_0_
  38.5 0.8 %collective-permute-start.14 = (bf16[384,256]{1,0:T(8,128)(2,1)S(1)}, bf16[384,256]{1,0:T(8,128)(2,1)S(1)}, u32[]{:S(2)}, u32[]{:S(2)}) collective-permute-start(bf16[384,256]{1,0:T(8,128)(2,1)S(1)} %level2_3.1.refs_3_.refs_0_), channel_id=1, source_target_pairs={{0,4},{1,5},{2,6},{3,7},{4,0},{5,1},{6,2},{7,3},{8,12},{9,13},{10,... | collective-permute-start | bytes 589832 | tf_op jit(solution)/shard_map/ppermute | solution.py:55
  39.3 0.4 level3_1.1.refs_0_
  39.7 0.3 between_1.1
  40.0 2.0 %collective-permute-start.13 = (bf16[256,128]{1,0:T(8,128)(2,1)S(1)}, bf16[256,128]{1,0:T(8,128)(2,1)S(1)}, u32[]{:S(2)}, u32[]{:S(2)}) collective-permute-start(bf16[256,128]{1,0:T(8,128)(2,1)S(1)} %get-tuple-element.54), channel_id=1, source_target_pairs={{0,8},{8,0},{16,24},{24,16},{1,9},{9,1},{17,25},{25,17},{2,10},{10... | collective-permute-start | bytes 196616 | tf_op jit(solution)/shard_map/ppermute | solution.py:55
  42.0 0.8 %last_1.1 = (f32[512,256]{1,0:T(8,128)S(1)}, bf16[512,256]{1,0:T(8,128)(2,1)S(1)}) custom-call(f32[384,256]{1,0:T(8,128)S(1)} %get-tuple-element.50.refs_0_, bf16[384,256]{1,0:T(8,128)(2,1)S(1)} %collective-permute-done.11.refs_1_, bf16[2,384,768]{2,1,0:T(8,128)(2,1)S(1)} %get-tuple-element.46.refs_1_.refs_2_, ...), custom_call_target="tpu_custom_call" | custom-call | flops 6000000000 | tf_op jit(solution)/shard_map/last_1/pallas_call | solution.py:41
  42.8 1.2 %collective-permute-start.12 = (bf16[512,256]{1,0:T(8,128)(2,1)S(1)}, bf16[512,256]{1,0:T(8,128)(2,1)S(1)}, u32[]{:S(2)}, u32[]{:S(2)}) collective-permute-start(bf16[512,256]{1,0:T(8,128)(2,1)S(1)} %get-tuple-element.52), channel_id=1, source_target_pairs={{0,8},{8,0},{16,24},{24,16},{1,9},{9,1},{17,25},{25,17},{2,10},{10... | collective-permute-start | bytes 786440 | tf_op jit(solution)/shard_map/ppermute | solution.py:55
  43.9 7.7 %collective-permute-done.7.refs_1_ = bf16[384,384]{1,0:T(8,128)(2,1)S(1)} collective-permute-done((bf16[384,384]{1,0:T(8,128)(2,1)S(1)}, bf16[384,384]{1,0:T(8,128)(2,1)S(1)}, u32[]{:S(2)}, u32[]{:S(2)}) %collective-permute-start.7) | collective-permute-done | bytes 294944 | tf_op jit(solution)/shard_map/ppermute | solution.py:55
  51.7 0.5 level3_2.1.refs_0_
  52.3 0.4 between_2.1
  52.6 1.6 %collective-permute-start.16 = (bf16[256,256]{1,0:T(8,128)(2,1)S(1)}, bf16[256,256]{1,0:T(8,128)(2,1)S(1)}, u32[]{:S(2)}, u32[]{:S(2)}) collective-permute-start(bf16[256,256]{1,0:T(8,128)(2,1)S(1)} %get-tuple-element.59), channel_id=1, source_target_pairs={{0,16},{8,24},{16,0},{24,8},{1,17},{9,25},{17,1},{25,9},{2,18},{10... | collective-permute-start | bytes 393224 | tf_op jit(solution)/shard_map/ppermute | solution.py:55
  54.2 1.2 %last_2.1 = (f32[256,384]{1,0:T(8,128)S(1)}, bf16[256,384]{1,0:T(8,128)(2,1)S(1)}, bf16[256,384]{1,0:T(8,128)(2,1)S(1)}, bf16[256,384]{1,0:T(8,128)(2,1)S(1)}) custom-call(f32[384,384]{1,0:T(8,128)S(1)} %get-tuple-element.56.refs_0_, bf16[384,384]{1,0:T(8,128)(2,1)S(1)} %collective-permute-done.15.refs_1_, ...), custom_call_target="tpu_custom_call" | custom-call | flops 6000000000 | tf_op jit(solution)/shard_map/last_2/pallas_call | solution.py:41
  55.5 0.4 level3_3.1.refs_0_
  55.8 0.3 collective-permute-start.20
  56.1 2.0 %collective-permute-start.17 = (bf16[256,384]{1,0:T(8,128)(2,1)S(1)}, bf16[256,384]{1,0:T(8,128)(2,1)S(1)}, u32[]{:S(2)}, u32[]{:S(2)}) collective-permute-start(bf16[256,384]{1,0:T(8,128)(2,1)S(1)} %get-tuple-element.61), channel_id=1, source_target_pairs={{0,24},{8,16},{16,8},{24,0},{1,25},{9,17},{17,9},{25,1},{2,26},{10... | collective-permute-start | bytes 589832 | tf_op jit(solution)/shard_map/ppermute | solution.py:55
  58.1 1.0 %collective-permute-start.18 = (bf16[256,384]{1,0:T(8,128)(2,1)S(1)}, bf16[256,384]{1,0:T(8,128)(2,1)S(1)}, u32[]{:S(2)}, u32[]{:S(2)}) collective-permute-start(bf16[256,384]{1,0:T(8,128)(2,1)S(1)} %get-tuple-element.62), channel_id=1, source_target_pairs={{0,16},{8,24},{16,0},{24,8},{1,17},{9,25},{17,1},{25,9},{2,18},{10... | collective-permute-start | bytes 589832 | tf_op jit(solution)/shard_map/ppermute | solution.py:55
  59.1 0.5 collective-permute-start.19
  59.6 0.3 between_3.1
  59.9 0.8 %last_3.1 = (f32[256,256]{1,0:T(8,128)S(1)}, bf16[256,256]{1,0:T(8,128)(2,1)S(1)}, bf16[256,256]{1,0:T(8,128)(2,1)S(1)}, bf16[256,256]{1,0:T(8,128)(2,1)S(1)}) custom-call(f32[384,256]{1,0:T(8,128)S(1)} %get-tuple-element.64.refs_0_, bf16[384,256]{1,0:T(8,128)(2,1)S(1)} %collective-permute-done.20.refs_1_, ...), custom_call_target="tpu_custom_call" | custom-call | flops 6000000000 | tf_op jit(solution)/shard_map/last_3/pallas_call | solution.py:41
  60.7 2.1 %collective-permute-start.21 = (bf16[256,256]{1,0:T(8,128)(2,1)S(1)}, bf16[256,256]{1,0:T(8,128)(2,1)S(1)}, u32[]{:S(2)}, u32[]{:S(2)}) collective-permute-start(bf16[256,256]{1,0:T(8,128)(2,1)S(1)} %get-tuple-element.66), channel_id=1, source_target_pairs={{0,24},{8,16},{16,8},{24,0},{1,25},{9,17},{17,9},{25,1},{2,26},{10... | collective-permute-start | bytes 393224 | tf_op jit(solution)/shard_map/ppermute | solution.py:55
  62.8 1.0 %collective-permute-start.22 = (bf16[256,256]{1,0:T(8,128)(2,1)S(1)}, bf16[256,256]{1,0:T(8,128)(2,1)S(1)}, u32[]{:S(2)}, u32[]{:S(2)}) collective-permute-start(bf16[256,256]{1,0:T(8,128)(2,1)S(1)} %get-tuple-element.67), channel_id=1, source_target_pairs={{0,16},{8,24},{16,0},{24,8},{1,17},{9,25},{17,1},{25,9},{2,18},{10... | collective-permute-start | bytes 393224 | tf_op jit(solution)/shard_map/ppermute | solution.py:55
  63.7 1.1 %collective-permute-done.17.refs_3_ = bf16[256,384]{1,0:T(8,128)(2,1)S(1)} collective-permute-done((bf16[256,384]{1,0:T(8,128)(2,1)S(1)}, bf16[256,384]{1,0:T(8,128)(2,1)S(1)}, u32[]{:S(2)}, u32[]{:S(2)}) %collective-permute-start.17) | collective-permute-done | bytes 196640 | tf_op jit(solution)/shard_map/ppermute | solution.py:55
  64.8 1.5 %collective-permute-start.23 = (bf16[256,256]{1,0:T(8,128)(2,1)S(1)}, bf16[256,256]{1,0:T(8,128)(2,1)S(1)}, u32[]{:S(2)}, u32[]{:S(2)}) collective-permute-start(bf16[256,256]{1,0:T(8,128)(2,1)S(1)} %get-tuple-element.68), channel_id=1, source_target_pairs={{0,8},{8,0},{16,24},{24,16},{1,9},{9,1},{17,25},{25,17},{2,10},{10... | collective-permute-start | bytes 393224 | tf_op jit(solution)/shard_map/ppermute | solution.py:55
  66.3 2.8 %collective-permute-done.18.refs_4_ = bf16[256,384]{1,0:T(8,128)(2,1)S(1)} collective-permute-done((bf16[256,384]{1,0:T(8,128)(2,1)S(1)}, bf16[256,384]{1,0:T(8,128)(2,1)S(1)}, u32[]{:S(2)}, u32[]{:S(2)}) %collective-permute-start.18) | collective-permute-done | bytes 196640 | tf_op jit(solution)/shard_map/ppermute | solution.py:55
  69.0 2.8 %collective-permute-done.21.refs_7_ = bf16[256,256]{1,0:T(8,128)(2,1)S(1)} collective-permute-done((bf16[256,256]{1,0:T(8,128)(2,1)S(1)}, bf16[256,256]{1,0:T(8,128)(2,1)S(1)}, u32[]{:S(2)}, u32[]{:S(2)}) %collective-permute-start.21) | collective-permute-done | bytes 131104 | tf_op jit(solution)/shard_map/ppermute | solution.py:55
  71.8 2.1 %collective-permute-done.22.refs_8_ = bf16[256,256]{1,0:T(8,128)(2,1)S(1)} collective-permute-done((bf16[256,256]{1,0:T(8,128)(2,1)S(1)}, bf16[256,256]{1,0:T(8,128)(2,1)S(1)}, u32[]{:S(2)}, u32[]{:S(2)}) %collective-permute-start.22) | collective-permute-done | bytes 131104 | tf_op jit(solution)/shard_map/ppermute | solution.py:55
  74.0 1.0 %end.1 = bf16[2,256,512]{2,1,0:T(8,128)(2,1)} custom-call(bf16[256,128]{1,0:T(8,128)(2,1)S(1)} %get-tuple-element.55.refs_0_, bf16[256,256]{1,0:T(8,128)(2,1)S(1)} %get-tuple-element.60.refs_1_, f32[256,384]{1,0:T(8,128)S(1)} %get-tuple-element.57.refs_3_.refs_2_, bf16[256,384]{1,0:T(8,128)(2,1)S(1)} %collective-permute-done.17.refs_3_, ...), custom_call_target="tpu_custom_call" | custom-call | tf_op jit(solution)/shard_map/end/pallas_call | solution.py:378
  (21 shorter events, 0.7 us)
Async XLA Ops:
  3.7 5.8 %collective-permute-start.2 = (bf16[384,896]{1,0:T(8,128)(2,1)S(1)}, bf16[384,896]{1,0:T(8,128)(2,1)S(1)}, u32[]{:S(2)}, u32[]{:S(2)}) collective-permute-start(bf16[384,896]{1,0:T(8,128)(2,1)S(1)} %get-tuple-element.40.refs_0_.refs_3_), channel_id=1, source_target_pairs={{0,1},{1,0},{2,3},{3,2},{4,5},{5,4},{6,7},{7,6},{8,9},{9,8},{10,11... | collective-permute-start | bytes 2064392 | tf_op jit(solution)/shard_map/ppermute | solution.py:55
  4.2 1.9 %collective-permute-start = (bf16[384,128]{1,0:T(8,128)(2,1)S(1)}, bf16[384,128]{1,0:T(8,128)(2,1)S(1)}, u32[]{:S(2)}, u32[]{:S(2)}) collective-permute-start(bf16[384,128]{1,0:T(8,128)(2,1)S(1)} %get-tuple-element.37.refs_0_), channel_id=1, source_target_pairs={{0,1},{1,0},{2,3},{3,2},{4,5},{5,4},{6,7},{7,6},{8,9},{9,8},{10,11... | collective-permute-start | bytes 294920 | tf_op jit(solution)/shard_map/ppermute | solution.py:55
  6.4 6.3 %collective-permute-start.1 = (bf16[384,128]{1,0:T(8,128)(2,1)S(1)}, bf16[384,128]{1,0:T(8,128)(2,1)S(1)}, u32[]{:S(2)}, u32[]{:S(2)}) collective-permute-start(bf16[384,128]{1,0:T(8,128)(2,1)S(1)} %level1_0.1.refs_3_.refs_0_), channel_id=1, source_target_pairs={{0,2},{1,3},{2,0},{3,1},{4,6},{5,7},{6,4},{7,5},{8,10},{9,11},{10,... | collective-permute-start | bytes 294920 | tf_op jit(solution)/shard_map/ppermute | solution.py:55
  9.8 11.2 %collective-permute-start.5 = (bf16[384,256]{1,0:T(8,128)(2,1)S(1)}, bf16[384,256]{1,0:T(8,128)(2,1)S(1)}, u32[]{:S(2)}, u32[]{:S(2)}) collective-permute-start(bf16[384,256]{1,0:T(8,128)(2,1)S(1)} %level1_1.1.refs_6_.refs_0_), channel_id=1, source_target_pairs={{0,2},{1,3},{2,0},{3,1},{4,6},{5,7},{6,4},{7,5},{8,10},{9,11},{10,... | collective-permute-start | bytes 589832 | tf_op jit(solution)/shard_map/ppermute | solution.py:55
  13.4 8.5 %collective-permute-start.4 = (bf16[384,128]{1,0:T(8,128)(2,1)S(1)}, bf16[384,128]{1,0:T(8,128)(2,1)S(1)}, u32[]{:S(2)}, u32[]{:S(2)}) collective-permute-start(bf16[384,128]{1,0:T(8,128)(2,1)S(1)} %get-tuple-element.42.refs_3_.refs_0_), channel_id=1, source_target_pairs={{0,4},{1,5},{2,6},{3,7},{4,0},{5,1},{6,2},{7,3},{8,12},{9,13},{10,... | collective-permute-start | bytes 294920 | tf_op jit(solution)/shard_map/ppermute | solution.py:55
  18.9 16.4 %collective-permute-start.3 = (bf16[384,384]{1,0:T(8,128)(2,1)S(1)}, bf16[384,384]{1,0:T(8,128)(2,1)S(1)}, u32[]{:S(2)}, u32[]{:S(2)}) collective-permute-start(bf16[384,384]{1,0:T(8,128)(2,1)S(1)} %get-tuple-element.41.refs_0_), channel_id=1, source_target_pairs={{0,2},{1,3},{2,0},{3,1},{4,6},{5,7},{6,4},{7,5},{8,10},{9,11},{10,... | collective-permute-start | bytes 884744 | tf_op jit(solution)/shard_map/ppermute | solution.py:55
  21.5 17.8 %collective-permute-start.8 = (bf16[384,256]{1,0:T(8,128)(2,1)S(1)}, bf16[384,256]{1,0:T(8,128)(2,1)S(1)}, u32[]{:S(2)}, u32[]{:S(2)}) collective-permute-start(bf16[384,256]{1,0:T(8,128)(2,1)S(1)} %get-tuple-element.45.refs_3_.refs_0_), channel_id=1, source_target_pairs={{0,4},{1,5},{2,6},{3,7},{4,0},{5,1},{6,2},{7,3},{8,12},{9,13},{10,... | collective-permute-start | bytes 589832 | tf_op jit(solution)/shard_map/ppermute | solution.py:55
  22.2 1.4 %collective-permute-start.6 = (bf16[384,128]{1,0:T(8,128)(2,1)S(1)}, bf16[384,128]{1,0:T(8,128)(2,1)S(1)}, u32[]{:S(2)}, u32[]{:S(2)}) collective-permute-start(bf16[384,128]{1,0:T(8,128)(2,1)S(1)} %level3_0.1.refs_0_), channel_id=1, source_target_pairs={{0,1},{1,0},{2,3},{3,2},{4,5},{5,4},{6,7},{7,6},{8,9},{9,8},{10,11... | collective-permute-start | bytes 294920 | tf_op jit(solution)/shard_map/ppermute | solution.py:55
  22.6 15.6 %collective-permute-start.9 = (bf16[384,256]{1,0:T(8,128)(2,1)S(1)}, bf16[384,256]{1,0:T(8,128)(2,1)S(1)}, u32[]{:S(2)}, u32[]{:S(2)}) collective-permute-start(bf16[384,256]{1,0:T(8,128)(2,1)S(1)} %get-tuple-element.48.refs_0_), channel_id=1, source_target_pairs={{0,2},{1,3},{2,0},{3,1},{4,6},{5,7},{6,4},{7,5},{8,10},{9,11},{10,... | collective-permute-start | bytes 589832 | tf_op jit(solution)/shard_map/ppermute | solution.py:55
  24.2 15.5 %collective-permute-start.10 = (bf16[512,128]{1,0:T(8,128)(2,1)S(1)}, bf16[512,128]{1,0:T(8,128)(2,1)S(1)}, u32[]{:S(2)}, u32[]{:S(2)}) collective-permute-start(bf16[512,128]{1,0:T(8,128)(2,1)S(1)} %get-tuple-element.49), channel_id=1, source_target_pairs={{0,16},{8,24},{16,0},{24,8},{1,17},{9,25},{17,1},{25,9},{2,18},{10... | collective-permute-start | bytes 393224 | tf_op jit(solution)/shard_map/ppermute | solution.py:55
  35.8 15.8 %collective-permute-start.7 = (bf16[384,384]{1,0:T(8,128)(2,1)S(1)}, bf16[384,384]{1,0:T(8,128)(2,1)S(1)}, u32[]{:S(2)}, u32[]{:S(2)}) collective-permute-start(bf16[384,384]{1,0:T(8,128)(2,1)S(1)} %level2_2.1.refs_3_.refs_0_), channel_id=1, source_target_pairs={{0,4},{1,5},{2,6},{3,7},{4,0},{5,1},{6,2},{7,3},{8,12},{9,13},{10,... | collective-permute-start | bytes 884744 | tf_op jit(solution)/shard_map/ppermute | solution.py:55
  38.5 17.0 %collective-permute-start.14 = (bf16[384,256]{1,0:T(8,128)(2,1)S(1)}, bf16[384,256]{1,0:T(8,128)(2,1)S(1)}, u32[]{:S(2)}, u32[]{:S(2)}) collective-permute-start(bf16[384,256]{1,0:T(8,128)(2,1)S(1)} %level2_3.1.refs_3_.refs_0_), channel_id=1, source_target_pairs={{0,4},{1,5},{2,6},{3,7},{4,0},{5,1},{6,2},{7,3},{8,12},{9,13},{10,... | collective-permute-start | bytes 589832 | tf_op jit(solution)/shard_map/ppermute | solution.py:55
  39.6 2.4 %collective-permute-start.11 = (bf16[384,256]{1,0:T(8,128)(2,1)S(1)}, bf16[384,256]{1,0:T(8,128)(2,1)S(1)}, u32[]{:S(2)}, u32[]{:S(2)}) collective-permute-start(bf16[384,256]{1,0:T(8,128)(2,1)S(1)} %level3_1.1.refs_0_), channel_id=1, source_target_pairs={{0,1},{1,0},{2,3},{3,2},{4,5},{5,4},{6,7},{7,6},{8,9},{9,8},{10,11... | collective-permute-start | bytes 589832 | tf_op jit(solution)/shard_map/ppermute | solution.py:55
  40.0 12.3 %collective-permute-start.13 = (bf16[256,128]{1,0:T(8,128)(2,1)S(1)}, bf16[256,128]{1,0:T(8,128)(2,1)S(1)}, u32[]{:S(2)}, u32[]{:S(2)}) collective-permute-start(bf16[256,128]{1,0:T(8,128)(2,1)S(1)} %get-tuple-element.54), channel_id=1, source_target_pairs={{0,8},{8,0},{16,24},{24,16},{1,9},{9,1},{17,25},{25,17},{2,10},{10... | collective-permute-start | bytes 196616 | tf_op jit(solution)/shard_map/ppermute | solution.py:55
  42.8 9.5 %collective-permute-start.12 = (bf16[512,256]{1,0:T(8,128)(2,1)S(1)}, bf16[512,256]{1,0:T(8,128)(2,1)S(1)}, u32[]{:S(2)}, u32[]{:S(2)}) collective-permute-start(bf16[512,256]{1,0:T(8,128)(2,1)S(1)} %get-tuple-element.52), channel_id=1, source_target_pairs={{0,8},{8,0},{16,24},{24,16},{1,9},{9,1},{17,25},{25,17},{2,10},{10... | collective-permute-start | bytes 786440 | tf_op jit(solution)/shard_map/ppermute | solution.py:55
  52.2 2.0 %collective-permute-start.15 = (bf16[384,384]{1,0:T(8,128)(2,1)S(1)}, bf16[384,384]{1,0:T(8,128)(2,1)S(1)}, u32[]{:S(2)}, u32[]{:S(2)}) collective-permute-start(bf16[384,384]{1,0:T(8,128)(2,1)S(1)} %level3_2.1.refs_0_), channel_id=1, source_target_pairs={{0,1},{1,0},{2,3},{3,2},{4,5},{5,4},{6,7},{7,6},{8,9},{9,8},{10,11... | collective-permute-start | bytes 884744 | tf_op jit(solution)/shard_map/ppermute | solution.py:55
  52.6 7.0 %collective-permute-start.16 = (bf16[256,256]{1,0:T(8,128)(2,1)S(1)}, bf16[256,256]{1,0:T(8,128)(2,1)S(1)}, u32[]{:S(2)}, u32[]{:S(2)}) collective-permute-start(bf16[256,256]{1,0:T(8,128)(2,1)S(1)} %get-tuple-element.59), channel_id=1, source_target_pairs={{0,16},{8,24},{16,0},{24,8},{1,17},{9,25},{17,1},{25,9},{2,18},{10... | collective-permute-start | bytes 393224 | tf_op jit(solution)/shard_map/ppermute | solution.py:55
  55.8 4.0 %collective-permute-start.20 = (bf16[384,256]{1,0:T(8,128)(2,1)S(1)}, bf16[384,256]{1,0:T(8,128)(2,1)S(1)}, u32[]{:S(2)}, u32[]{:S(2)}) collective-permute-start(bf16[384,256]{1,0:T(8,128)(2,1)S(1)} %level3_3.1.refs_0_), channel_id=1, source_target_pairs={{0,1},{1,0},{2,3},{3,2},{4,5},{5,4},{6,7},{7,6},{8,9},{9,8},{10,11... | collective-permute-start | bytes 589832 | tf_op jit(solution)/shard_map/ppermute | solution.py:55
  56.1 8.7 %collective-permute-start.17 = (bf16[256,384]{1,0:T(8,128)(2,1)S(1)}, bf16[256,384]{1,0:T(8,128)(2,1)S(1)}, u32[]{:S(2)}, u32[]{:S(2)}) collective-permute-start(bf16[256,384]{1,0:T(8,128)(2,1)S(1)} %get-tuple-element.61), channel_id=1, source_target_pairs={{0,24},{8,16},{16,8},{24,0},{1,25},{9,17},{17,9},{25,1},{2,26},{10... | collective-permute-start | bytes 589832 | tf_op jit(solution)/shard_map/ppermute | solution.py:55
  58.1 10.9 %collective-permute-start.18 = (bf16[256,384]{1,0:T(8,128)(2,1)S(1)}, bf16[256,384]{1,0:T(8,128)(2,1)S(1)}, u32[]{:S(2)}, u32[]{:S(2)}) collective-permute-start(bf16[256,384]{1,0:T(8,128)(2,1)S(1)} %get-tuple-element.62), channel_id=1, source_target_pairs={{0,16},{8,24},{16,0},{24,8},{1,17},{9,25},{17,1},{25,9},{2,18},{10... | collective-permute-start | bytes 589832 | tf_op jit(solution)/shard_map/ppermute | solution.py:55
  59.1 10.0 %collective-permute-start.19 = (bf16[256,384]{1,0:T(8,128)(2,1)S(1)}, bf16[256,384]{1,0:T(8,128)(2,1)S(1)}, u32[]{:S(2)}, u32[]{:S(2)}) collective-permute-start(bf16[256,384]{1,0:T(8,128)(2,1)S(1)} %get-tuple-element.63), channel_id=1, source_target_pairs={{0,8},{8,0},{16,24},{24,16},{1,9},{9,1},{17,25},{25,17},{2,10},{10... | collective-permute-start | bytes 589832 | tf_op jit(solution)/shard_map/ppermute | solution.py:55
  60.7 11.1 %collective-permute-start.21 = (bf16[256,256]{1,0:T(8,128)(2,1)S(1)}, bf16[256,256]{1,0:T(8,128)(2,1)S(1)}, u32[]{:S(2)}, u32[]{:S(2)}) collective-permute-start(bf16[256,256]{1,0:T(8,128)(2,1)S(1)} %get-tuple-element.66), channel_id=1, source_target_pairs={{0,24},{8,16},{16,8},{24,0},{1,25},{9,17},{17,9},{25,1},{2,26},{10... | collective-permute-start | bytes 393224 | tf_op jit(solution)/shard_map/ppermute | solution.py:55
  62.8 11.2 %collective-permute-start.22 = (bf16[256,256]{1,0:T(8,128)(2,1)S(1)}, bf16[256,256]{1,0:T(8,128)(2,1)S(1)}, u32[]{:S(2)}, u32[]{:S(2)}) collective-permute-start(bf16[256,256]{1,0:T(8,128)(2,1)S(1)} %get-tuple-element.67), channel_id=1, source_target_pairs={{0,16},{8,24},{16,0},{24,8},{1,17},{9,25},{17,1},{25,9},{2,18},{10... | collective-permute-start | bytes 393224 | tf_op jit(solution)/shard_map/ppermute | solution.py:55
  64.8 9.2 %collective-permute-start.23 = (bf16[256,256]{1,0:T(8,128)(2,1)S(1)}, bf16[256,256]{1,0:T(8,128)(2,1)S(1)}, u32[]{:S(2)}, u32[]{:S(2)}) collective-permute-start(bf16[256,256]{1,0:T(8,128)(2,1)S(1)} %get-tuple-element.68), channel_id=1, source_target_pairs={{0,8},{8,0},{16,24},{24,16},{1,9},{9,1},{17,25},{25,17},{2,10},{10... | collective-permute-start | bytes 393224 | tf_op jit(solution)/shard_map/ppermute | solution.py:55

commit v5 on v4

--- a/solution.py
+++ b/solution.py
@@ -144,47 +144,33 @@
     return dot(weights[s, :, pl.ds(pl.multiple_of(half * rank, 128), rank)], value)
 
 
-def between_kernel(bit, parts, fold, total, own, weights, *refs):
-    refs = list(refs)
-    ins = [refs.pop(0) for _ in range(2 * (fold + total))]
-    partial = refs.pop(0)
+def half_kernel(bit, parts, own, weights, partial):
     for s, start, stop in parts:
         partial[:, start:stop] = half_dot(weights, s, upper_half(bit), own[:, start:stop])
-    if fold:
-        fold_kernel(ins.pop(0), ins.pop(0), refs.pop(0), refs.pop(0))
-    if total:
-        keep, got = ins.pop(0), ins.pop(0)
-        refs.pop(0)[...] = (keep[...] + got[...].astype(F32)).astype(BF16)
-
-
-def last_kernel(bit, parts, order, partial, other, weights, basis, *refs):
-    rows = basis.shape[1] // lax.axis_size("blk")
-    me = lax.axis_index("blk")
+
+
+def last_kernel(bit, parts, partial, other, weights, basis, mine, pieces):
+    rows = mine.shape[0]
+    row = pl.multiple_of(lax.axis_index("blk") * rows, rows)
     for s, start, stop in parts:
         mixed = partial[:, start:stop] + half_dot(weights, s, 1 - upper_half(bit), other[:, start:stop])
         coeff = mixed.astype(BF16)
-        for ref, distances in zip(refs, order):
-            for at, d in enumerate(distances):
+        pieces[:, start:stop] = dot(basis[s], coeff).astype(BF16)
+        mine[:, start:stop] = dot(basis[s, pl.ds(row, rows), :], coeff)
+
+
+def end_kernel(places, *refs):
+    refs, out = list(refs[:-1]), refs[-1]
+    me = lax.axis_index("blk")
+    for place in places:
+        mine, got = refs.pop(0), refs.pop(0)
+        rows = mine.shape[0]
+        count = got.shape[0] // rows
+        for s, column, start, stop in place:
+            total = mine[:, start:stop]
+            for d in range(1, count):
                 row = pl.multiple_of((me ^ d) * rows, rows)
-                piece = dot(basis[s, pl.ds(row, rows), :], coeff)
-                ref[at * rows : (at + 1) * rows, start:stop] = piece.astype(ref.dtype)
-
-
-def fold_kernel(keep, got, send, rest):
-    rows = rest.shape[0]
-    rest[...] = keep[:rows] + got[:rows].astype(F32)
-    send[...] = (keep[rows:] + got[rows:].astype(F32)).astype(BF16)
-
-
-def end_kernel(places, counts, *refs):
-    refs = list(refs)
-    out = refs[-1]
-    for place, count in zip(places, counts):
-        group = [refs.pop(0) for _ in range(count)]
-        for s, column, start, stop in place:
-            total = group[0][:, start:stop].astype(F32)
-            for piece in group[1:]:
-                total = total + piece[:, start:stop].astype(F32)
+                total = total + got[pl.ds(row, rows), start:stop].astype(F32)
             out[s, :, column : column + stop - start] = total.astype(BF16)
 
 
@@ -290,93 +276,38 @@
     third(1, value)
     second(3, ahead)
 
-    masks = [1 << b for b in range(n_blk.bit_length() - 1)]
-
-    def halving(j):
-        order = masks if j % 2 else masks[::-1]
-        pieces = [0]
-        for mask in order[::-1]:
-            pieces = pieces + [d | mask for d in pieces]
-        return order, pieces
-
-    def result(j, count, dtype):
-        return in_vmem(count * rows, widths[j], dtype=dtype)
-
-    def tail(j, after, direct, folding=None, totalling=None):
-        (coeff4,) = step(f"level3_{j}", [(3, j, coeff3[j], near3[j])], after, flops=0 if j == 1 else COST)
+    def tail(j, after, flops=COST):
+        (coeff4,) = step(f"level3_{j}", [(3, j, coeff3[j], near3[j])], after, flops)
         near4 = cross(4, coeff4)
-        outs, extra = [in_vmem(rank, widths[j], dtype=F32)], []
-        if folding is not None:
-            at, keep, got, count = folding
-            extra += [keep, got]
-            outs += [result(at, count // 2, BF16), result(at, count // 2, F32)]
-        if totalling is not None:
-            at, keep, got = totalling
-            extra += [keep, got]
-            outs += [result(at, 1, BF16)]
-        partial, *more = call(
-            functools.partial(
-                between_kernel, bits[4], parts[j], folding is not None, totalling is not None
-            ),
-            f"between_{j}",
-            [VMEM] * (2 + len(extra)),
-            outs,
+        (partial,) = call(
+            functools.partial(half_kernel, bits[4], parts[j]),
+            f"half_{j}",
+            [VMEM] * 2,
+            [in_vmem(rank, widths[j], dtype=F32)],
             [],
-            [here(v) for v in (coeff4, weights[4], *extra)],
+            [here(coeff4), here(weights[4])],
         )
-        if direct:
-            order = [[d] for d in range(n_blk)]
-        else:
-            pieces = halving(j)[1]
-            order = [pieces[: n_blk // 2], pieces[n_blk // 2 :]]
-        kinds = [F32] + [BF16] * (len(order) - 1)
-        out = call(
-            functools.partial(last_kernel, bits[4], parts[j], order),
+        mine, pieces = call(
+            functools.partial(last_kernel, bits[4], parts[j]),
             f"last_{j}",
             [VMEM] * 4,
-            [result(j, len(o), kind) for o, kind in zip(order, kinds)],
+            [in_vmem(rows, widths[j], dtype=F32), in_vmem(n_blk * rows, widths[j])],
             [],
             [here(v) for v in (partial, near4, weights[4], basis_v)],
         )
-        return out, more
-
-    def begin_sum(j, out):
-        keep, send = out
-        order = halving(j)[0]
-        got, count = partner(send, "blk", order[0]), n_blk // 2
-        for mask in order[1:-1]:
-            send, keep = call(
-                fold_kernel,
-                f"fold_{j}_{mask}",
-                [VMEM] * 2,
-                [result(j, count // 2, BF16), result(j, count // 2, F32)],
-                [],
-                [here(keep), here(got)],
-            )
-            got, count = partner(send, "blk", mask), count // 2
-        return j, keep, got, count
-
-    def direct_sum(out):
-        return [out[0]] + [partner(out[d], "blk", d) for d in range(n_blk - 1, 0, -1)]
-
-    out0, _ = tail(0, [coeff3[1]], False)
-    fold0 = begin_sum(0, out0)
-    (value,) = step("level2_2", [(2, 2, coeff2[2], near2[2])], [out0[0]])
+        return mine, lax.all_to_all(pieces, "blk", 0, 0, tiled=True)
+
+    groups = [tail(0, [coeff3[1]])]
+    (value,) = step("level2_2", [(2, 2, coeff2[2], near2[2])], [groups[0][0]])
     third(2, value)
     (value,) = step("level2_3", [(2, 3, coeff2[3], near2[3])], [coeff3[2]])
     third(3, value)
-    out1, (send0, keep0) = tail(1, [coeff3[3]], False, fold0)
-    got0 = partner(send0, "blk", halving(0)[0][-1])
-    fold1 = begin_sum(1, out1)
-    out2, (send1, keep1, total0) = tail(2, [out1[0]], True, fold1, (0, keep0, got0))
-    got1 = partner(send1, "blk", halving(1)[0][-1])
-    group2 = direct_sum(out2)
-    out3, (total1,) = tail(3, [out2[0]], True, None, (1, keep1, got1))
-    group3 = direct_sum(out3)
-    groups = [[total0], [total1], group2, group3]
+    groups.append(tail(1, [coeff3[3]]))
+    groups.append(tail(2, [groups[1][0]]))
+    groups.append(tail(3, [groups[2][0]]))
     flat = [here(v) for group in groups for v in group]
     return pl.pallas_call(
-        functools.partial(end_kernel, places, [len(group) for group in groups]),
+        functools.partial(end_kernel, places),
         name="end",
         in_specs=[VMEM] * len(flat),
         out_specs=VMEM,

time: 75.1 us -> 92.5 us (1.23)
  blocking collectives: 0 us -> 22.6 us
  waiting for transfers between devices: 33.3 us -> 23.6 us
  local copies, waits for them, and re-layouts: 0 us -> 5.86 us
  starting transfers between devices: 25.4 us -> 21.7 us
  Pallas kernels: 16 us -> 18 us
    all_to_all x0 -> x2, blocking collectives: none -> 22.6 us  [tail(): return (mine, lax.all_to_all(pieces, 'blk', 0, 0, tiled=True))]
    ppermute x24 -> x14, waiting for transfers between devices: 33.3 us -> 19.5 us  [partner(): return lax.ppermute(value, axis, pairs)]
    ppermute x24 -> x14, starting transfers between devices: 25.4 us -> 13.4 us  [partner(): return lax.ppermute(value, axis, pairs)]
    all_to_all x0 -> x2, starting transfers between devices: none -> 8.37 us  [tail(): return (mine, lax.all_to_all(pieces, 'blk', 0, 0, tiled=True))]
    unnamed x0 -> x24, local copies, waits for them, and re-layouts: none -> 5.86 us
    all_to_all x0 -> x2, waiting for transfers between devices: none -> 4.03 us  [tail(): return (mine, lax.all_to_all(pieces, 'blk', 0, 0, tiled=True))]
    pallas_call x20, Pallas kernels: 15 us -> 17 us  [call(): pl.pallas_call(body, name=name, in_specs=[*in_specs, *[ANY] * len(after)]...]
  transfers between devices with their start and end apart: 24 -> 16, of which waited for: 10 -> 7; matrix products, arithmetic and copies ran while one was open for 0% -> 0% of each run, Pallas kernels for 15% -> 14%
where the time goes in v5:
time: 92.5 us; the launch traced here: 92 us
  waiting for transfers between devices  23.6 us (26%)
  blocking collectives  22.6 us (24%)
  starting transfers between devices  21.7 us (23%)
  Pallas kernels  18 us (19%)
  local copies, waits for them, and re-layouts  5.86 us (6%)
    all_to_all x2, blocking collectives, tail(): return (mine, lax.all_to_all(pieces, 'blk', 0, 0, tiled=True))  22.6 us
    ppermute x14, waiting for transfers between devices, partner(): return lax.ppermute(value, axis, pairs)  19.5 us
    pallas_call x20, Pallas kernels, call(): pl.pallas_call(body, name=name, in_specs=[*in_specs, *[ANY] * len(after)]...  17 us
    ppermute x14, starting transfers between devices, partner(): return lax.ppermute(value, axis, pairs)  13.4 us
    all_to_all x2, starting transfers between devices, tail(): return (mine, lax.all_to_all(pieces, 'blk', 0, 0, tiled=True))  8.37 us
    unnamed x24, local copies, waits for them, and re-layouts  5.86 us
    all_to_all x2, waiting for transfers between devices, tail(): return (mine, lax.all_to_all(pieces, 'blk', 0, 0, tiled=True))  4.03 us
  transfers between devices with their start and end apart: 16, of which 7 were waited for; matrix products, arithmetic and copies ran while one was open for 0% of the time, Pallas kernels for 14%

profile of v5, /device:TPU:0, one launch (start us, length us, event | category | flops | bytes accessed | tf_op | source)
XLA Modules:
  0.0 92.0 jit_solution(16001027103676802973)
XLA Ops:
  0.0 3.7 %leaf.1 = (bf16[384,128]{1,0:T(8,128)(2,1)S(1)}, bf16[384,896]{1,0:T(8,128)(2,1)S(1)}, bf16[2,384,768]{2,1,0:T(8,128)(2,1)S(1)}, bf16[2,384,768]{2,1,0:T(8,128)(2,1)S(1)}) custom-call(bf16[2,1024,512]{2,1,0:T(8,128)(2,1)} %bitcast.23, bf16[2,384,1024]{2,1,0:T(8,128)(2,1)} %bitcast.24, bf16[5,2,384,768]{3,2,1,0:T(8,128)(2,1)} %bitcast.21, s32[2,5]{1,0:T(2,128)} %bitcast.26), custom_call_target="tpu_custom_call" | custom-call | flops 6000000000 | tf_op jit(solution)/shard_map/leaf/pallas_call | solution.py:41
  3.7 0.5 collective-permute-start.2
  4.2 0.1 collective-permute-start
  4.3 1.8 %collective-permute-done.refs_1_ = bf16[384,128]{1,0:T(8,128)(2,1)S(1)} collective-permute-done((bf16[384,128]{1,0:T(8,128)(2,1)S(1)}, bf16[384,128]{1,0:T(8,128)(2,1)S(1)}, u32[]{:S(2)}, u32[]{:S(2)}) %collective-permute-start) | collective-permute-done | bytes 98336 | tf_op jit(solution)/shard_map/ppermute | solution.py:55
  6.1 0.3 level1_0.1.refs_3_.refs_0_
  6.5 3.0 %collective-permute-start.1 = (bf16[384,128]{1,0:T(8,128)(2,1)S(1)}, bf16[384,128]{1,0:T(8,128)(2,1)S(1)}, u32[]{:S(2)}, u32[]{:S(2)}) collective-permute-start(bf16[384,128]{1,0:T(8,128)(2,1)S(1)} %level1_0.1.refs_3_.refs_0_), channel_id=1, source_target_pairs={{0,2},{1,3},{2,0},{3,1},{4,6},{5,7},{6,4},{7,5},{8,10},{9,11},{10,... | collective-permute-start | bytes 294920 | tf_op jit(solution)/shard_map/ppermute | solution.py:55
  9.5 0.4 level1_1.1.refs_6_.refs_0_
  9.8 0.1 collective-permute-start.4
  9.9 2.8 %collective-permute-done.1.refs_1_ = bf16[384,128]{1,0:T(8,128)(2,1)S(1)} collective-permute-done((bf16[384,128]{1,0:T(8,128)(2,1)S(1)}, bf16[384,128]{1,0:T(8,128)(2,1)S(1)}, u32[]{:S(2)}, u32[]{:S(2)}) %collective-permute-start.1) | collective-permute-done | bytes 98336 | tf_op jit(solution)/shard_map/ppermute | solution.py:55
  12.7 0.7 level2_0.1
  13.4 3.0 %collective-permute-start.3 = (bf16[384,128]{1,0:T(8,128)(2,1)S(1)}, bf16[384,128]{1,0:T(8,128)(2,1)S(1)}, u32[]{:S(2)}, u32[]{:S(2)}) collective-permute-start(bf16[384,128]{1,0:T(8,128)(2,1)S(1)} %get-tuple-element.28.refs_3_.refs_0_), channel_id=1, source_target_pairs={{0,4},{1,5},{2,6},{3,7},{4,0},{5,1},{6,2},{7,3},{8,12},{9,13},{10,... | collective-permute-start | bytes 294920 | tf_op jit(solution)/shard_map/ppermute | solution.py:55
  16.4 2.5 %prefetch.1 = (bf16[2,384,768]{2,1,0:T(8,128)(2,1)S(1)}, bf16[2,384,768]{2,1,0:T(8,128)(2,1)S(1)}, bf16[2,1024,384]{2,1,0:T(8,128)(2,1)S(1)}) custom-call(bf16[5,2,384,768]{3,2,1,0:T(8,128)(2,1)} %bitcast.22, bf16[2,1024,384]{2,1,0:T(8,128)(2,1)} %bitcast.25, s32[2,5]{1,0:T(2,128)} %bitcast.27, bf16[384,128]{1,0:T(8,128)(2,1)S(1)} %get-tuple-element.28.refs_3_.refs_0_), custom_call_target="tpu_custom_call" | custom-call | flops 6000000000 | tf_op jit(solution)/shard_map/prefetch/pallas_call | solution.py:41
  19.0 2.0 %collective-permute-start.8 = (bf16[384,384]{1,0:T(8,128)(2,1)S(1)}, bf16[384,384]{1,0:T(8,128)(2,1)S(1)}, u32[]{:S(2)}, u32[]{:S(2)}) collective-permute-start(bf16[384,384]{1,0:T(8,128)(2,1)S(1)} %get-tuple-element.36.refs_0_), channel_id=1, source_target_pairs={{0,2},{1,3},{2,0},{3,1},{4,6},{5,7},{6,4},{7,5},{8,10},{9,11},{10,... | collective-permute-start | bytes 884744 | tf_op jit(solution)/shard_map/ppermute | solution.py:55
  21.0 0.5 level2_1.1
  21.5 0.4 collective-permute-start.6
  21.9 0.3 level3_0.1.refs_0_
  22.4 0.2 half_0.1.refs_0_
  22.6 0.6 collective-permute-start.7
  23.2 0.5 collective-permute-done.5.refs_1_
  23.7 1.4 %last_0.1 = (f32[256,128]{1,0:T(8,128)S(1)}, bf16[1024,128]{1,0:T(8,128)(2,1)}) custom-call(f32[384,128]{1,0:T(8,128)S(1)} %half_0.1.refs_0_, bf16[384,128]{1,0:T(8,128)(2,1)S(1)} %collective-permute-done.5.refs_1_, bf16[2,384,768]{2,1,0:T(8,128)(2,1)S(1)} %get-tuple-element.32.refs_1_.refs_2_, bf16[2,1024,384]{2,1,0:T(8,128)(2,1)S(1)} %get-tuple-element.30.refs_6_.refs_3_), custom_call_target="tpu_custom_call" | custom-call | flops 6000000000 | tf_op jit(solution)/shard_map/last_0/pallas_call | solution.py:41
  25.0 10.3 %collective-permute-done.8.refs_1_ = bf16[384,384]{1,0:T(8,128)(2,1)S(1)} collective-permute-done((bf16[384,384]{1,0:T(8,128)(2,1)S(1)}, bf16[384,384]{1,0:T(8,128)(2,1)S(1)}, u32[]{:S(2)}, u32[]{:S(2)}) %collective-permute-start.8) | collective-permute-done | bytes 294944 | tf_op jit(solution)/shard_map/ppermute | solution.py:55
  35.3 0.5 level2_2.1.refs_3_.refs_0_
  35.9 4.2 %all-to-all-start = ((bf16[4,256,128]{2,1,0:T(8,128)(2,1)}), bf16[4,256,128]{2,1,0:T(8,128)(2,1)S(1)}, u32[]{:S(2)}, u32[]{:S(2)}) async-start(bf16[4,256,128]{2,1,0:T(8,128)(2,1)} %bitcast.7), calls=%async_computation | async-start | bytes 524288 | tf_op jit(solution)/shard_map/all_to_all | solution.py:298
  40.1 1.3 %copy-done.1 = bf16[2,384,768]{2,1,0:T(8,128)(2,1)S(1)} copy-done((bf16[2,384,768]{2,1,0:T(8,128)(2,1)S(1)}, bf16[2,384,768]{2,1,0:T(8,128)(2,1)}, u32[]{:S(2)}) %copy-start.1) | copy-done | bytes 1179672
  41.4 0.4 level2_3.1.refs_3_.refs_0_
  41.7 0.9 copy-done.9
  42.6 0.4 level3_1.1.refs_0_
  43.1 0.3 half_1.1.refs_0_
  43.4 3.0 %collective-permute-start.12 = (bf16[384,256]{1,0:T(8,128)(2,1)S(1)}, bf16[384,256]{1,0:T(8,128)(2,1)S(1)}, u32[]{:S(2)}, u32[]{:S(2)}) collective-permute-start(bf16[384,256]{1,0:T(8,128)(2,1)S(1)} %level2_3.1.refs_3_.refs_0_), channel_id=1, source_target_pairs={{0,4},{1,5},{2,6},{3,7},{4,0},{5,1},{6,2},{7,3},{8,12},{9,13},{10,... | collective-permute-start | bytes 589832 | tf_op jit(solution)/shard_map/ppermute | solution.py:55
  46.3 1.7 %last_1.1 = (f32[256,256]{1,0:T(8,128)S(1)}, bf16[1024,256]{1,0:T(8,128)(2,1)}) custom-call(f32[384,256]{1,0:T(8,128)S(1)} %half_1.1.refs_0_, bf16[384,256]{1,0:T(8,128)(2,1)S(1)} %collective-permute-done.9.refs_1_, bf16[2,384,768]{2,1,0:T(8,128)(2,1)S(1)} %copy-done.6, bf16[2,1024,384]{2,1,0:T(8,128)(2,1)S(1)} %copy-done.3), custom_call_target="tpu_custom_call" | custom-call | flops 6000000000 | tf_op jit(solution)/shard_map/last_1/pallas_call | solution.py:41
  48.0 0.5 level3_2.1.refs_0_
  48.5 0.3 collective-permute-start.11
  48.8 0.3 half_2.1.refs_0_
  49.1 1.0 %collective-permute-done.11.refs_1_ = bf16[384,384]{1,0:T(8,128)(2,1)S(1)} collective-permute-done((bf16[384,384]{1,0:T(8,128)(2,1)S(1)}, bf16[384,384]{1,0:T(8,128)(2,1)S(1)}, u32[]{:S(2)}, u32[]{:S(2)}) %collective-permute-start.11) | collective-permute-done | bytes 294944 | tf_op jit(solution)/shard_map/ppermute | solution.py:55
  50.2 1.5 %last_2.1 = (f32[256,384]{1,0:T(8,128)S(1)}, bf16[1024,384]{1,0:T(8,128)(2,1)S(1)}) custom-call(f32[384,384]{1,0:T(8,128)S(1)} %half_2.1.refs_0_, bf16[384,384]{1,0:T(8,128)(2,1)S(1)} %collective-permute-done.11.refs_1_, bf16[2,384,768]{2,1,0:T(8,128)(2,1)S(1)} %copy-done.6, bf16[2,1024,384]{2,1,0:T(8,128)(2,1)S(1)} %copy-done.3), custom_call_target="tpu_custom_call" | custom-call | flops 6000000000 | tf_op jit(solution)/shard_map/last_2/pallas_call | solution.py:41
  51.7 3.1 %collective-permute-done.12.refs_1_ = bf16[384,256]{1,0:T(8,128)(2,1)S(1)} collective-permute-done((bf16[384,256]{1,0:T(8,128)(2,1)S(1)}, bf16[384,256]{1,0:T(8,128)(2,1)S(1)}, u32[]{:S(2)}, u32[]{:S(2)}) %collective-permute-start.12) | collective-permute-done | bytes 196640 | tf_op jit(solution)/shard_map/ppermute | solution.py:55
  54.8 0.4 level3_3.1.refs_0_
  55.1 0.2 collective-permute-start.13
  55.3 0.3 half_3.1.refs_0_
  55.6 4.2 %all-to-all-start.1 = ((bf16[4,256,256]{2,1,0:T(8,128)(2,1)}), bf16[4,256,256]{2,1,0:T(8,128)(2,1)S(1)}, u32[]{:S(2)}, u32[]{:S(2)}) async-start(bf16[4,256,256]{2,1,0:T(8,128)(2,1)} %bitcast.9), calls=%async_computation.1 | async-start | bytes 1048576 | tf_op jit(solution)/shard_map/all_to_all | solution.py:298
  59.8 1.4 %copy-done.4 = bf16[2,1024,384]{2,1,0:T(8,128)(2,1)S(1)} copy-done((bf16[2,1024,384]{2,1,0:T(8,128)(2,1)S(1)}, bf16[2,1024,384]{2,1,0:T(8,128)(2,1)}, u32[]{:S(2)}) %copy-start.4) | copy-done | bytes 1572888
  61.2 1.3 %copy-done.7 = bf16[2,384,768]{2,1,0:T(8,128)(2,1)S(1)} copy-done((bf16[2,384,768]{2,1,0:T(8,128)(2,1)S(1)}, bf16[2,384,768]{2,1,0:T(8,128)(2,1)}, u32[]{:S(2)}) %copy-start.7) | copy-done | bytes 1179672
  62.5 1.0 %copy-done.11 = f32[384,256]{1,0:T(8,128)S(1)} copy-done((f32[384,256]{1,0:T(8,128)S(1)}, f32[384,256]{1,0:T(8,128)}, u32[]{:S(2)}) %copy-start.11) | copy-done | bytes 393240
  63.5 0.9 last_3.1
  64.4 4.0 %all-to-all-done.1 = bf16[4,256,256]{2,1,0:T(8,128)(2,1)S(1)} async-done(((bf16[4,256,256]{2,1,0:T(8,128)(2,1)}), bf16[4,256,256]{2,1,0:T(8,128)(2,1)S(1)}, u32[]{:S(2)}, u32[]{:S(2)}) %all-to-all-start.1) | async-done | bytes 524320 | tf_op jit(solution)/shard_map/all_to_all | solution.py:298
  68.4 10.7 %all_to_all.44 = bf16[4,256,256]{2,1,0:T(8,128)(2,1)S(1)} all-to-all(bf16[4,256,256]{2,1,0:T(8,128)(2,1)S(1)} %bitcast.20), channel_id=1, replica_groups=mesh['blk'=4,'box'=8] {'blk'}, dimensions={0} | all-to-all | bytes 1048576 | tf_op jit(solution)/shard_map/all_to_all | solution.py:298
  79.1 11.9 %all_to_all.45 = bf16[4,256,384]{2,1,0:T(8,128)(2,1)S(1)} all-to-all(bf16[4,256,384]{2,1,0:T(8,128)(2,1)S(1)} %bitcast.19), channel_id=1, replica_groups=mesh['blk'=4,'box'=8] {'blk'}, dimensions={0} | all-to-all | bytes 1572864 | tf_op jit(solution)/shard_map/all_to_all | solution.py:298
  91.0 1.0 %end.1 = bf16[2,256,512]{2,1,0:T(8,128)(2,1)} custom-call(f32[256,128]{1,0:T(8,128)S(1)} %get-tuple-element.33.refs_3_.refs_0_, bf16[1024,128]{1,0:T(8,128)(2,1)S(1)} %bitcast.18, f32[256,256]{1,0:T(8,128)S(1)} %get-tuple-element.37.refs_3_.refs_2_, bf16[1024,256]{1,0:T(8,128)(2,1)S(1)} %bitcast.16, f32[256,384]{1,0:T(8,128)S(1)} %get-tuple-element.39.refs_3_.refs_4_, ...), custom_call_target="tpu_custom_call" | custom-call | tf_op jit(solution)/shard_map/end/pallas_call | solution.py:309
  (31 shorter events, 0.3 us)
Async XLA Ops:
  3.7 31.6 %copy-start = (bf16[2,384,768]{2,1,0:T(8,128)(2,1)}, bf16[2,384,768]{2,1,0:T(8,128)(2,1)S(1)}, u32[]{:S(2)}) copy-start(bf16[2,384,768]{2,1,0:T(8,128)(2,1)S(1)} %get-tuple-element.26.refs_2_) | copy-start | bytes 3538948
  3.7 5.8 %collective-permute-start.2 = (bf16[384,896]{1,0:T(8,128)(2,1)S(1)}, bf16[384,896]{1,0:T(8,128)(2,1)S(1)}, u32[]{:S(2)}, u32[]{:S(2)}) collective-permute-start(bf16[384,896]{1,0:T(8,128)(2,1)S(1)} %get-tuple-element.27.refs_0_.refs_3_), channel_id=1, source_target_pairs={{0,1},{1,0},{2,3},{3,2},{4,5},{5,4},{6,7},{7,6},{8,9},{9,8},{10,11... | collective-permute-start | bytes 2064392 | tf_op jit(solution)/shard_map/ppermute | solution.py:55
  4.2 1.9 %collective-permute-start = (bf16[384,128]{1,0:T(8,128)(2,1)S(1)}, bf16[384,128]{1,0:T(8,128)(2,1)S(1)}, u32[]{:S(2)}, u32[]{:S(2)}) collective-permute-start(bf16[384,128]{1,0:T(8,128)(2,1)S(1)} %get-tuple-element.24.refs_0_), channel_id=1, source_target_pairs={{0,1},{1,0},{2,3},{3,2},{4,5},{5,4},{6,7},{7,6},{8,9},{9,8},{10,11... | collective-permute-start | bytes 294920 | tf_op jit(solution)/shard_map/ppermute | solution.py:55
  6.5 6.3 %collective-permute-start.1 = (bf16[384,128]{1,0:T(8,128)(2,1)S(1)}, bf16[384,128]{1,0:T(8,128)(2,1)S(1)}, u32[]{:S(2)}, u32[]{:S(2)}) collective-permute-start(bf16[384,128]{1,0:T(8,128)(2,1)S(1)} %level1_0.1.refs_3_.refs_0_), channel_id=1, source_target_pairs={{0,2},{1,3},{2,0},{3,1},{4,6},{5,7},{6,4},{7,5},{8,10},{9,11},{10,... | collective-permute-start | bytes 294920 | tf_op jit(solution)/shard_map/ppermute | solution.py:55
  9.8 11.2 %collective-permute-start.4 = (bf16[384,256]{1,0:T(8,128)(2,1)S(1)}, bf16[384,256]{1,0:T(8,128)(2,1)S(1)}, u32[]{:S(2)}, u32[]{:S(2)}) collective-permute-start(bf16[384,256]{1,0:T(8,128)(2,1)S(1)} %level1_1.1.refs_6_.refs_0_), channel_id=1, source_target_pairs={{0,2},{1,3},{2,0},{3,1},{4,6},{5,7},{6,4},{7,5},{8,10},{9,11},{10,... | collective-permute-start | bytes 589832 | tf_op jit(solution)/shard_map/ppermute | solution.py:55
  13.4 8.6 %collective-permute-start.3 = (bf16[384,128]{1,0:T(8,128)(2,1)S(1)}, bf16[384,128]{1,0:T(8,128)(2,1)S(1)}, u32[]{:S(2)}, u32[]{:S(2)}) collective-permute-start(bf16[384,128]{1,0:T(8,128)(2,1)S(1)} %get-tuple-element.28.refs_3_.refs_0_), channel_id=1, source_target_pairs={{0,4},{1,5},{2,6},{3,7},{4,0},{5,1},{6,2},{7,3},{8,12},{9,13},{10,... | collective-permute-start | bytes 294920 | tf_op jit(solution)/shard_map/ppermute | solution.py:55
  18.9 3.0 %copy-start.8 = (bf16[2,384,768]{2,1,0:T(8,128)(2,1)}, bf16[2,384,768]{2,1,0:T(8,128)(2,1)S(1)}, u32[]{:S(2)}) copy-start(bf16[2,384,768]{2,1,0:T(8,128)(2,1)S(1)} %get-tuple-element.29.refs_2_) | copy-start | bytes 3538948
  18.9 4.7 %copy-start.2 = (bf16[2,1024,384]{2,1,0:T(8,128)(2,1)}, bf16[2,1024,384]{2,1,0:T(8,128)(2,1)S(1)}, u32[]{:S(2)}) copy-start(bf16[2,1024,384]{2,1,0:T(8,128)(2,1)S(1)} %get-tuple-element.30.refs_6_.refs_3_) | copy-start | bytes 4718596
  19.0 4.7 %copy-start.5 = (bf16[2,384,768]{2,1,0:T(8,128)(2,1)}, bf16[2,384,768]{2,1,0:T(8,128)(2,1)S(1)}, u32[]{:S(2)}) copy-start(bf16[2,384,768]{2,1,0:T(8,128)(2,1)S(1)} %get-tuple-element.32.refs_1_.refs_2_) | copy-start | bytes 3538948
  19.0 16.3 %collective-permute-start.8 = (bf16[384,384]{1,0:T(8,128)(2,1)S(1)}, bf16[384,384]{1,0:T(8,128)(2,1)S(1)}, u32[]{:S(2)}, u32[]{:S(2)}) collective-permute-start(bf16[384,384]{1,0:T(8,128)(2,1)S(1)} %get-tuple-element.36.refs_0_), channel_id=1, source_target_pairs={{0,2},{1,3},{2,0},{3,1},{4,6},{5,7},{6,4},{7,5},{8,10},{9,11},{10,... | collective-permute-start | bytes 884744 | tf_op jit(solution)/shard_map/ppermute | solution.py:55
  21.5 20.2 %collective-permute-start.6 = (bf16[384,256]{1,0:T(8,128)(2,1)S(1)}, bf16[384,256]{1,0:T(8,128)(2,1)S(1)}, u32[]{:S(2)}, u32[]{:S(2)}) collective-permute-start(bf16[384,256]{1,0:T(8,128)(2,1)S(1)} %get-tuple-element.31.refs_3_.refs_0_), channel_id=1, source_target_pairs={{0,4},{1,5},{2,6},{3,7},{4,0},{5,1},{6,2},{7,3},{8,12},{9,13},{10,... | collective-permute-start | bytes 589832 | tf_op jit(solution)/shard_map/ppermute | solution.py:55
  22.3 1.4 %collective-permute-start.5 = (bf16[384,128]{1,0:T(8,128)(2,1)S(1)}, bf16[384,128]{1,0:T(8,128)(2,1)S(1)}, u32[]{:S(2)}, u32[]{:S(2)}) collective-permute-start(bf16[384,128]{1,0:T(8,128)(2,1)S(1)} %level3_0.1.refs_0_), channel_id=1, source_target_pairs={{0,1},{1,0},{2,3},{3,2},{4,5},{5,4},{6,7},{7,6},{8,9},{9,8},{10,11... | collective-permute-start | bytes 294920 | tf_op jit(solution)/shard_map/ppermute | solution.py:55
  22.6 17.5 %collective-permute-start.7 = (bf16[384,256]{1,0:T(8,128)(2,1)S(1)}, bf16[384,256]{1,0:T(8,128)(2,1)S(1)}, u32[]{:S(2)}, u32[]{:S(2)}) collective-permute-start(bf16[384,256]{1,0:T(8,128)(2,1)S(1)} %get-tuple-element.35.refs_0_), channel_id=1, source_target_pairs={{0,2},{1,3},{2,0},{3,1},{4,6},{5,7},{6,4},{7,5},{8,10},{9,11},{10,... | collective-permute-start | bytes 589832 | tf_op jit(solution)/shard_map/ppermute | solution.py:55
  35.8 12.2 %collective-permute-start.10 = (bf16[384,384]{1,0:T(8,128)(2,1)S(1)}, bf16[384,384]{1,0:T(8,128)(2,1)S(1)}, u32[]{:S(2)}, u32[]{:S(2)}) collective-permute-start(bf16[384,384]{1,0:T(8,128)(2,1)S(1)} %level2_2.1.refs_3_.refs_0_), channel_id=1, source_target_pairs={{0,4},{1,5},{2,6},{3,7},{4,0},{5,1},{6,2},{7,3},{8,12},{9,13},{10,... | collective-permute-start | bytes 884744 | tf_op jit(solution)/shard_map/ppermute | solution.py:55
  35.9 19.7 %all-to-all-start = ((bf16[4,256,128]{2,1,0:T(8,128)(2,1)}), bf16[4,256,128]{2,1,0:T(8,128)(2,1)S(1)}, u32[]{:S(2)}, u32[]{:S(2)}) async-start(bf16[4,256,128]{2,1,0:T(8,128)(2,1)} %bitcast.7), calls=%async_computation | async-start | bytes 524288 | tf_op jit(solution)/shard_map/all_to_all | solution.py:298
  40.1 1.3 %copy-start.1 = (bf16[2,384,768]{2,1,0:T(8,128)(2,1)S(1)}, bf16[2,384,768]{2,1,0:T(8,128)(2,1)}, u32[]{:S(2)}) copy-start(bf16[2,384,768]{2,1,0:T(8,128)(2,1)} %copy-done) | copy-start | bytes 3538948
  41.4 1.3 %copy-start.9 = (bf16[2,384,768]{2,1,0:T(8,128)(2,1)S(1)}, bf16[2,384,768]{2,1,0:T(8,128)(2,1)}, u32[]{:S(2)}) copy-start(bf16[2,384,768]{2,1,0:T(8,128)(2,1)} %copy-done.8) | copy-start | bytes 3538948
  41.7 1.4 %copy-start.6 = (bf16[2,384,768]{2,1,0:T(8,128)(2,1)S(1)}, bf16[2,384,768]{2,1,0:T(8,128)(2,1)}, u32[]{:S(2)}) copy-start(bf16[2,384,768]{2,1,0:T(8,128)(2,1)} %copy-done.5) | copy-start | bytes 3538948
  43.0 3.3 %copy-start.3 = (bf16[2,1024,384]{2,1,0:T(8,128)(2,1)S(1)}, bf16[2,1024,384]{2,1,0:T(8,128)(2,1)}, u32[]{:S(2)}) copy-start(bf16[2,1024,384]{2,1,0:T(8,128)(2,1)} %copy-done.2) | copy-start | bytes 4718596
  43.0 3.3 %collective-permute-start.9 = (bf16[384,256]{1,0:T(8,128)(2,1)S(1)}, bf16[384,256]{1,0:T(8,128)(2,1)S(1)}, u32[]{:S(2)}, u32[]{:S(2)}) collective-permute-start(bf16[384,256]{1,0:T(8,128)(2,1)S(1)} %level3_1.1.refs_0_), channel_id=1, source_target_pairs={{0,1},{1,0},{2,3},{3,2},{4,5},{5,4},{6,7},{7,6},{8,9},{9,8},{10,11... | collective-permute-start | bytes 589832 | tf_op jit(solution)/shard_map/ppermute | solution.py:55
  43.4 11.4 %collective-permute-start.12 = (bf16[384,256]{1,0:T(8,128)(2,1)S(1)}, bf16[384,256]{1,0:T(8,128)(2,1)S(1)}, u32[]{:S(2)}, u32[]{:S(2)}) collective-permute-start(bf16[384,256]{1,0:T(8,128)(2,1)S(1)} %level2_3.1.refs_3_.refs_0_), channel_id=1, source_target_pairs={{0,4},{1,5},{2,6},{3,7},{4,0},{5,1},{6,2},{7,3},{8,12},{9,13},{10,... | collective-permute-start | bytes 589832 | tf_op jit(solution)/shard_map/ppermute | solution.py:55
  48.5 1.6 %collective-permute-start.11 = (bf16[384,384]{1,0:T(8,128)(2,1)S(1)}, bf16[384,384]{1,0:T(8,128)(2,1)S(1)}, u32[]{:S(2)}, u32[]{:S(2)}) collective-permute-start(bf16[384,384]{1,0:T(8,128)(2,1)S(1)} %level3_2.1.refs_0_), channel_id=1, source_target_pairs={{0,1},{1,0},{2,3},{3,2},{4,5},{5,4},{6,7},{7,6},{8,9},{9,8},{10,11... | collective-permute-start | bytes 884744 | tf_op jit(solution)/shard_map/ppermute | solution.py:55
  55.1 4.7 %collective-permute-start.13 = (bf16[384,256]{1,0:T(8,128)(2,1)S(1)}, bf16[384,256]{1,0:T(8,128)(2,1)S(1)}, u32[]{:S(2)}, u32[]{:S(2)}) collective-permute-start(bf16[384,256]{1,0:T(8,128)(2,1)S(1)} %level3_3.1.refs_0_), channel_id=1, source_target_pairs={{0,1},{1,0},{2,3},{3,2},{4,5},{5,4},{6,7},{7,6},{8,9},{9,8},{10,11... | collective-permute-start | bytes 589832 | tf_op jit(solution)/shard_map/ppermute | solution.py:55
  55.6 4.2 %copy-start.10 = (f32[384,256]{1,0:T(8,128)}, f32[384,256]{1,0:T(8,128)S(1)}, u32[]{:S(2)}) copy-start(f32[384,256]{1,0:T(8,128)S(1)} %half_3.1.refs_0_) | copy-start | bytes 1179652
  55.6 12.8 %all-to-all-start.1 = ((bf16[4,256,256]{2,1,0:T(8,128)(2,1)}), bf16[4,256,256]{2,1,0:T(8,128)(2,1)S(1)}, u32[]{:S(2)}, u32[]{:S(2)}) async-start(bf16[4,256,256]{2,1,0:T(8,128)(2,1)} %bitcast.9), calls=%async_computation.1 | async-start | bytes 1048576 | tf_op jit(solution)/shard_map/all_to_all | solution.py:298
  59.8 1.4 %copy-start.4 = (bf16[2,1024,384]{2,1,0:T(8,128)(2,1)S(1)}, bf16[2,1024,384]{2,1,0:T(8,128)(2,1)}, u32[]{:S(2)}) copy-start(bf16[2,1024,384]{2,1,0:T(8,128)(2,1)} %copy-done.2) | copy-start | bytes 4718596
  61.2 1.3 %copy-start.7 = (bf16[2,384,768]{2,1,0:T(8,128)(2,1)S(1)}, bf16[2,384,768]{2,1,0:T(8,128)(2,1)}, u32[]{:S(2)}) copy-start(bf16[2,384,768]{2,1,0:T(8,128)(2,1)} %copy-done.5) | copy-start | bytes 3538948
  62.5 1.0 %copy-start.11 = (f32[384,256]{1,0:T(8,128)S(1)}, f32[384,256]{1,0:T(8,128)}, u32[]{:S(2)}) copy-start(f32[384,256]{1,0:T(8,128)} %copy-done.10) | copy-start | bytes 1179652

commit v6 on v4

--- a/solution.py
+++ b/solution.py
@@ -286,9 +286,8 @@
         [coeff3[0]],
     )
     weights += more
-    value, ahead = step("level2_1", [(2, 1, coeff2[1], near2[1]), job1(3)], [basis_v])
+    (value,) = step("level2_1", [(2, 1, coeff2[1], near2[1])], [basis_v])
     third(1, value)
-    second(3, ahead)
 
     masks = [1 << b for b in range(n_blk.bit_length() - 1)]
 
@@ -361,14 +360,15 @@
 
     out0, _ = tail(0, [coeff3[1]], False)
     fold0 = begin_sum(0, out0)
-    (value,) = step("level2_2", [(2, 2, coeff2[2], near2[2])], [out0[0]])
+    value, ahead = step("level2_2", [(2, 2, coeff2[2], near2[2]), job1(3)], [out0[0]])
     third(2, value)
-    (value,) = step("level2_3", [(2, 3, coeff2[3], near2[3])], [coeff3[2]])
-    third(3, value)
-    out1, (send0, keep0) = tail(1, [coeff3[3]], False, fold0)
+    second(3, ahead)
+    out1, (send0, keep0) = tail(1, [coeff3[2]], False, fold0)
     got0 = partner(send0, "blk", halving(0)[0][-1])
     fold1 = begin_sum(1, out1)
-    out2, (send1, keep1, total0) = tail(2, [out1[0]], True, fold1, (0, keep0, got0))
+    (value,) = step("level2_3", [(2, 3, coeff2[3], near2[3])], [out1[0]])
+    third(3, value)
+    out2, (send1, keep1, total0) = tail(2, [coeff3[3]], True, fold1, (0, keep0, got0))
     got1 = partner(send1, "blk", halving(1)[0][-1])
     group2 = direct_sum(out2)
     out3, (total1,) = tail(3, [out2[0]], True, None, (1, keep1, got1))

time: 75.1 us -> 75.2 us (level)
  starting transfers between devices: 25.4 us -> 27.9 us
  waiting for transfers between devices: 33.3 us -> 30.9 us
    ppermute x24, starting transfers between devices: 25.4 us -> 27.9 us  [partner(): return lax.ppermute(value, axis, pairs)]
    ppermute x24, waiting for transfers between devices: 33.3 us -> 30.9 us  [partner(): return lax.ppermute(value, axis, pairs)]
where the time goes in v6:
time: 75.2 us; the launch traced here: 75 us
  waiting for transfers between devices  30.9 us (41%)
  starting transfers between devices  27.9 us (37%)
  Pallas kernels  16 us (21%)
    ppermute x24, waiting for transfers between devices, partner(): return lax.ppermute(value, axis, pairs)  30.9 us
    ppermute x24, starting transfers between devices, partner(): return lax.ppermute(value, axis, pairs)  27.9 us
    pallas_call x20, Pallas kernels, call(): pl.pallas_call(body, name=name, in_specs=[*in_specs, *[ANY] * len(after)]...  15 us
  transfers between devices with their start and end apart: 24, of which 10 were waited for; matrix products, arithmetic and copies ran while one was open for 0% of the time, Pallas kernels for 15%

profile of v6, /device:TPU:0, one launch (start us, length us, event | category | flops | bytes accessed | tf_op | source)
XLA Modules:
  0.0 75.0 jit_solution(63603266165625435)
XLA Ops:
  0.0 3.7 %leaf.1 = (bf16[384,128]{1,0:T(8,128)(2,1)S(1)}, bf16[384,896]{1,0:T(8,128)(2,1)S(1)}, bf16[2,384,768]{2,1,0:T(8,128)(2,1)S(1)}, bf16[2,384,768]{2,1,0:T(8,128)(2,1)S(1)}) custom-call(bf16[2,1024,512]{2,1,0:T(8,128)(2,1)} %bitcast.9, bf16[2,384,1024]{2,1,0:T(8,128)(2,1)} %bitcast.10, bf16[5,2,384,768]{3,2,1,0:T(8,128)(2,1)} %bitcast.7, s32[2,5]{1,0:T(2,128)} %bitcast.12), custom_call_target="tpu_custom_call" | custom-call | flops 6000000000 | tf_op jit(solution)/shard_map/leaf/pallas_call | solution.py:41
  3.7 0.5 collective-permute-start.2
  4.3 1.8 %collective-permute-done.refs_1_ = bf16[384,128]{1,0:T(8,128)(2,1)S(1)} collective-permute-done((bf16[384,128]{1,0:T(8,128)(2,1)S(1)}, bf16[384,128]{1,0:T(8,128)(2,1)S(1)}, u32[]{:S(2)}, u32[]{:S(2)}) %collective-permute-start) | collective-permute-done | bytes 98336 | tf_op jit(solution)/shard_map/ppermute | solution.py:55
  6.1 0.3 level1_0.1.refs_3_.refs_0_
  6.4 3.0 %collective-permute-start.1 = (bf16[384,128]{1,0:T(8,128)(2,1)S(1)}, bf16[384,128]{1,0:T(8,128)(2,1)S(1)}, u32[]{:S(2)}, u32[]{:S(2)}) collective-permute-start(bf16[384,128]{1,0:T(8,128)(2,1)S(1)} %level1_0.1.refs_3_.refs_0_), channel_id=1, source_target_pairs={{0,2},{1,3},{2,0},{3,1},{4,6},{5,7},{6,4},{7,5},{8,10},{9,11},{10,... | collective-permute-start | bytes 294920 | tf_op jit(solution)/shard_map/ppermute | solution.py:55
  9.5 0.4 level1_1.1.refs_6_.refs_0_
  9.9 2.8 %collective-permute-done.1.refs_1_ = bf16[384,128]{1,0:T(8,128)(2,1)S(1)} collective-permute-done((bf16[384,128]{1,0:T(8,128)(2,1)S(1)}, bf16[384,128]{1,0:T(8,128)(2,1)S(1)}, u32[]{:S(2)}, u32[]{:S(2)}) %collective-permute-start.1) | collective-permute-done | bytes 98336 | tf_op jit(solution)/shard_map/ppermute | solution.py:55
  12.7 0.7 level2_0.1
  13.4 3.0 %collective-permute-start.4 = (bf16[384,128]{1,0:T(8,128)(2,1)S(1)}, bf16[384,128]{1,0:T(8,128)(2,1)S(1)}, u32[]{:S(2)}, u32[]{:S(2)}) collective-permute-start(bf16[384,128]{1,0:T(8,128)(2,1)S(1)} %get-tuple-element.42.refs_3_.refs_0_), channel_id=1, source_target_pairs={{0,4},{1,5},{2,6},{3,7},{4,0},{5,1},{6,2},{7,3},{8,12},{9,13},{10,... | collective-permute-start | bytes 294920 | tf_op jit(solution)/shard_map/ppermute | solution.py:55
  16.4 2.0 %collective-permute-start.3 = (bf16[384,384]{1,0:T(8,128)(2,1)S(1)}, bf16[384,384]{1,0:T(8,128)(2,1)S(1)}, u32[]{:S(2)}, u32[]{:S(2)}) collective-permute-start(bf16[384,384]{1,0:T(8,128)(2,1)S(1)} %get-tuple-element.41.refs_0_), channel_id=1, source_target_pairs={{0,2},{1,3},{2,0},{3,1},{4,6},{5,7},{6,4},{7,5},{8,10},{9,11},{10,... | collective-permute-start | bytes 884744 | tf_op jit(solution)/shard_map/ppermute | solution.py:55
  18.4 2.5 %prefetch.1 = (bf16[2,384,768]{2,1,0:T(8,128)(2,1)S(1)}, bf16[2,384,768]{2,1,0:T(8,128)(2,1)S(1)}, bf16[2,1024,384]{2,1,0:T(8,128)(2,1)S(1)}) custom-call(bf16[5,2,384,768]{3,2,1,0:T(8,128)(2,1)} %bitcast.8, bf16[2,1024,384]{2,1,0:T(8,128)(2,1)} %bitcast.11, s32[2,5]{1,0:T(2,128)} %bitcast.13, bf16[384,128]{1,0:T(8,128)(2,1)S(1)} %get-tuple-element.42.refs_3_.refs_0_), custom_call_target="tpu_custom_call" | custom-call | flops 6000000000 | tf_op jit(solution)/shard_map/prefetch/pallas_call | solution.py:41
  20.9 0.4 level2_1.1.refs_3_.refs_0_
  21.3 0.4 collective-permute-start.9
  21.7 0.3 level3_0.1.refs_0_
  22.1 0.2 between_0.1.refs_0_
  22.3 1.0 %collective-permute-done.6.refs_1_ = bf16[384,128]{1,0:T(8,128)(2,1)S(1)} collective-permute-done((bf16[384,128]{1,0:T(8,128)(2,1)S(1)}, bf16[384,128]{1,0:T(8,128)(2,1)S(1)}, u32[]{:S(2)}, u32[]{:S(2)}) %collective-permute-start.6) | collective-permute-done | bytes 98336 | tf_op jit(solution)/shard_map/ppermute | solution.py:55
  23.4 0.6 last_0.1
  24.0 1.6 %collective-permute-start.10 = (bf16[512,128]{1,0:T(8,128)(2,1)S(1)}, bf16[512,128]{1,0:T(8,128)(2,1)S(1)}, u32[]{:S(2)}, u32[]{:S(2)}) collective-permute-start(bf16[512,128]{1,0:T(8,128)(2,1)S(1)} %get-tuple-element.49), channel_id=1, source_target_pairs={{0,16},{8,24},{16,0},{24,8},{1,17},{9,25},{17,1},{25,9},{2,18},{10... | collective-permute-start | bytes 393224 | tf_op jit(solution)/shard_map/ppermute | solution.py:55
  25.6 3.4 %collective-permute-done.3.refs_1_ = bf16[384,384]{1,0:T(8,128)(2,1)S(1)} collective-permute-done((bf16[384,384]{1,0:T(8,128)(2,1)S(1)}, bf16[384,384]{1,0:T(8,128)(2,1)S(1)}, u32[]{:S(2)}, u32[]{:S(2)}) %collective-permute-start.3) | collective-permute-done | bytes 294944 | tf_op jit(solution)/shard_map/ppermute | solution.py:55
  29.0 0.7 level2_2.1
  29.7 4.2 %collective-permute-start.7 = (bf16[384,384]{1,0:T(8,128)(2,1)S(1)}, bf16[384,384]{1,0:T(8,128)(2,1)S(1)}, u32[]{:S(2)}, u32[]{:S(2)}) collective-permute-start(bf16[384,384]{1,0:T(8,128)(2,1)S(1)} %get-tuple-element.47.refs_3_.refs_0_), channel_id=1, source_target_pairs={{0,4},{1,5},{2,6},{3,7},{4,0},{5,1},{6,2},{7,3},{8,12},{9,13},{10,... | collective-permute-start | bytes 884744 | tf_op jit(solution)/shard_map/ppermute | solution.py:55
  33.9 0.4 level3_1.1.refs_0_
  34.4 0.3 between_1.1
  34.7 1.6 %collective-permute-start.13 = (bf16[256,128]{1,0:T(8,128)(2,1)S(1)}, bf16[256,128]{1,0:T(8,128)(2,1)S(1)}, u32[]{:S(2)}, u32[]{:S(2)}) collective-permute-start(bf16[256,128]{1,0:T(8,128)(2,1)S(1)} %get-tuple-element.54), channel_id=1, source_target_pairs={{0,8},{8,0},{16,24},{24,16},{1,9},{9,1},{17,25},{25,17},{2,10},{10... | collective-permute-start | bytes 196616 | tf_op jit(solution)/shard_map/ppermute | solution.py:55
  36.2 0.8 %last_1.1 = (f32[512,256]{1,0:T(8,128)S(1)}, bf16[512,256]{1,0:T(8,128)(2,1)S(1)}) custom-call(f32[384,256]{1,0:T(8,128)S(1)} %get-tuple-element.50.refs_0_, bf16[384,256]{1,0:T(8,128)(2,1)S(1)} %collective-permute-done.11.refs_1_, bf16[2,384,768]{2,1,0:T(8,128)(2,1)S(1)} %get-tuple-element.45.refs_1_.refs_2_, ...), custom_call_target="tpu_custom_call" | custom-call | flops 6000000000 | tf_op jit(solution)/shard_map/last_1/pallas_call | solution.py:41
  37.0 2.3 %collective-permute-done.8.refs_1_ = bf16[384,256]{1,0:T(8,128)(2,1)S(1)} collective-permute-done((bf16[384,256]{1,0:T(8,128)(2,1)S(1)}, bf16[384,256]{1,0:T(8,128)(2,1)S(1)}, u32[]{:S(2)}, u32[]{:S(2)}) %collective-permute-start.8) | collective-permute-done | bytes 196640 | tf_op jit(solution)/shard_map/ppermute | solution.py:55
  39.4 0.4 level2_3.1.refs_3_.refs_0_
  39.7 0.5 collective-permute-start.14
  40.2 1.5 %collective-permute-start.12 = (bf16[512,256]{1,0:T(8,128)(2,1)S(1)}, bf16[512,256]{1,0:T(8,128)(2,1)S(1)}, u32[]{:S(2)}, u32[]{:S(2)}) collective-permute-start(bf16[512,256]{1,0:T(8,128)(2,1)S(1)} %get-tuple-element.52), channel_id=1, source_target_pairs={{0,8},{8,0},{16,24},{24,16},{1,9},{9,1},{17,25},{25,17},{2,10},{10... | collective-permute-start | bytes 786440 | tf_op jit(solution)/shard_map/ppermute | solution.py:55
  41.7 10.7 %collective-permute-done.7.refs_1_ = bf16[384,384]{1,0:T(8,128)(2,1)S(1)} collective-permute-done((bf16[384,384]{1,0:T(8,128)(2,1)S(1)}, bf16[384,384]{1,0:T(8,128)(2,1)S(1)}, u32[]{:S(2)}, u32[]{:S(2)}) %collective-permute-start.7) | collective-permute-done | bytes 294944 | tf_op jit(solution)/shard_map/ppermute | solution.py:55
  52.4 0.5 level3_2.1.refs_0_
  53.0 0.4 between_2.1
  53.4 1.6 %collective-permute-start.16 = (bf16[256,256]{1,0:T(8,128)(2,1)S(1)}, bf16[256,256]{1,0:T(8,128)(2,1)S(1)}, u32[]{:S(2)}, u32[]{:S(2)}) collective-permute-start(bf16[256,256]{1,0:T(8,128)(2,1)S(1)} %get-tuple-element.59), channel_id=1, source_target_pairs={{0,16},{8,24},{16,0},{24,8},{1,17},{9,25},{17,1},{25,9},{2,18},{10... | collective-permute-start | bytes 393224 | tf_op jit(solution)/shard_map/ppermute | solution.py:55
  55.0 1.2 %last_2.1 = (f32[256,384]{1,0:T(8,128)S(1)}, bf16[256,384]{1,0:T(8,128)(2,1)S(1)}, bf16[256,384]{1,0:T(8,128)(2,1)S(1)}, bf16[256,384]{1,0:T(8,128)(2,1)S(1)}) custom-call(f32[384,384]{1,0:T(8,128)S(1)} %get-tuple-element.56.refs_0_, bf16[384,384]{1,0:T(8,128)(2,1)S(1)} %collective-permute-done.15.refs_1_, ...), custom_call_target="tpu_custom_call" | custom-call | flops 6000000000 | tf_op jit(solution)/shard_map/last_2/pallas_call | solution.py:41
  56.2 2.1 %collective-permute-start.17 = (bf16[256,384]{1,0:T(8,128)(2,1)S(1)}, bf16[256,384]{1,0:T(8,128)(2,1)S(1)}, u32[]{:S(2)}, u32[]{:S(2)}) collective-permute-start(bf16[256,384]{1,0:T(8,128)(2,1)S(1)} %get-tuple-element.61), channel_id=1, source_target_pairs={{0,24},{8,16},{16,8},{24,0},{1,25},{9,17},{17,9},{25,1},{2,26},{10... | collective-permute-start | bytes 589832 | tf_op jit(solution)/shard_map/ppermute | solution.py:55
  58.3 0.9 %collective-permute-start.18 = (bf16[256,384]{1,0:T(8,128)(2,1)S(1)}, bf16[256,384]{1,0:T(8,128)(2,1)S(1)}, u32[]{:S(2)}, u32[]{:S(2)}) collective-permute-start(bf16[256,384]{1,0:T(8,128)(2,1)S(1)} %get-tuple-element.62), channel_id=1, source_target_pairs={{0,16},{8,24},{16,0},{24,8},{1,17},{9,25},{17,1},{25,9},{2,18},{10... | collective-permute-start | bytes 589832 | tf_op jit(solution)/shard_map/ppermute | solution.py:55
  59.2 0.6 collective-permute-start.19
  59.8 0.4 level3_3.1.refs_0_
  60.2 0.3 between_3.1
  60.5 1.2 %collective-permute-done.20.refs_1_ = bf16[384,256]{1,0:T(8,128)(2,1)S(1)} collective-permute-done((bf16[384,256]{1,0:T(8,128)(2,1)S(1)}, bf16[384,256]{1,0:T(8,128)(2,1)S(1)}, u32[]{:S(2)}, u32[]{:S(2)}) %collective-permute-start.20) | collective-permute-done | bytes 196640 | tf_op jit(solution)/shard_map/ppermute | solution.py:55
  61.7 0.8 %last_3.1 = (f32[256,256]{1,0:T(8,128)S(1)}, bf16[256,256]{1,0:T(8,128)(2,1)S(1)}, bf16[256,256]{1,0:T(8,128)(2,1)S(1)}, bf16[256,256]{1,0:T(8,128)(2,1)S(1)}) custom-call(f32[384,256]{1,0:T(8,128)S(1)} %get-tuple-element.64.refs_0_, bf16[384,256]{1,0:T(8,128)(2,1)S(1)} %collective-permute-done.20.refs_1_, ...), custom_call_target="tpu_custom_call" | custom-call | flops 6000000000 | tf_op jit(solution)/shard_map/last_3/pallas_call | solution.py:41
  62.5 2.1 %collective-permute-start.21 = (bf16[256,256]{1,0:T(8,128)(2,1)S(1)}, bf16[256,256]{1,0:T(8,128)(2,1)S(1)}, u32[]{:S(2)}, u32[]{:S(2)}) collective-permute-start(bf16[256,256]{1,0:T(8,128)(2,1)S(1)} %get-tuple-element.66), channel_id=1, source_target_pairs={{0,24},{8,16},{16,8},{24,0},{1,25},{9,17},{17,9},{25,1},{2,26},{10... | collective-permute-start | bytes 393224 | tf_op jit(solution)/shard_map/ppermute | solution.py:55
  64.6 0.9 %collective-permute-start.22 = (bf16[256,256]{1,0:T(8,128)(2,1)S(1)}, bf16[256,256]{1,0:T(8,128)(2,1)S(1)}, u32[]{:S(2)}, u32[]{:S(2)}) collective-permute-start(bf16[256,256]{1,0:T(8,128)(2,1)S(1)} %get-tuple-element.67), channel_id=1, source_target_pairs={{0,16},{8,24},{16,0},{24,8},{1,17},{9,25},{17,1},{25,9},{2,18},{10... | collective-permute-start | bytes 393224 | tf_op jit(solution)/shard_map/ppermute | solution.py:55
  65.5 1.0 %collective-permute-start.23 = (bf16[256,256]{1,0:T(8,128)(2,1)S(1)}, bf16[256,256]{1,0:T(8,128)(2,1)S(1)}, u32[]{:S(2)}, u32[]{:S(2)}) collective-permute-start(bf16[256,256]{1,0:T(8,128)(2,1)S(1)} %get-tuple-element.68), channel_id=1, source_target_pairs={{0,8},{8,0},{16,24},{24,16},{1,9},{9,1},{17,25},{25,17},{2,10},{10... | collective-permute-start | bytes 393224 | tf_op jit(solution)/shard_map/ppermute | solution.py:55
  66.5 2.8 %collective-permute-done.18.refs_4_ = bf16[256,384]{1,0:T(8,128)(2,1)S(1)} collective-permute-done((bf16[256,384]{1,0:T(8,128)(2,1)S(1)}, bf16[256,384]{1,0:T(8,128)(2,1)S(1)}, u32[]{:S(2)}, u32[]{:S(2)}) %collective-permute-start.18) | collective-permute-done | bytes 196640 | tf_op jit(solution)/shard_map/ppermute | solution.py:55
  69.3 2.8 %collective-permute-done.21.refs_7_ = bf16[256,256]{1,0:T(8,128)(2,1)S(1)} collective-permute-done((bf16[256,256]{1,0:T(8,128)(2,1)S(1)}, bf16[256,256]{1,0:T(8,128)(2,1)S(1)}, u32[]{:S(2)}, u32[]{:S(2)}) %collective-permute-start.21) | collective-permute-done | bytes 131104 | tf_op jit(solution)/shard_map/ppermute | solution.py:55
  72.0 2.0 %collective-permute-done.22.refs_8_ = bf16[256,256]{1,0:T(8,128)(2,1)S(1)} collective-permute-done((bf16[256,256]{1,0:T(8,128)(2,1)S(1)}, bf16[256,256]{1,0:T(8,128)(2,1)S(1)}, u32[]{:S(2)}, u32[]{:S(2)}) %collective-permute-start.22) | collective-permute-done | bytes 131104 | tf_op jit(solution)/shard_map/ppermute | solution.py:55
  74.0 1.0 %end.1 = bf16[2,256,512]{2,1,0:T(8,128)(2,1)} custom-call(bf16[256,128]{1,0:T(8,128)(2,1)S(1)} %get-tuple-element.55.refs_0_, bf16[256,256]{1,0:T(8,128)(2,1)S(1)} %get-tuple-element.60.refs_1_, f32[256,384]{1,0:T(8,128)S(1)} %get-tuple-element.57.refs_3_.refs_2_, bf16[256,384]{1,0:T(8,128)(2,1)S(1)} %collective-permute-done.17.refs_3_, ...), custom_call_target="tpu_custom_call" | custom-call | tf_op jit(solution)/shard_map/end/pallas_call | solution.py:378
  (21 shorter events, 0.6 us)
Async XLA Ops:
  3.7 5.8 %collective-permute-start.2 = (bf16[384,896]{1,0:T(8,128)(2,1)S(1)}, bf16[384,896]{1,0:T(8,128)(2,1)S(1)}, u32[]{:S(2)}, u32[]{:S(2)}) collective-permute-start(bf16[384,896]{1,0:T(8,128)(2,1)S(1)} %get-tuple-element.40.refs_0_.refs_3_), channel_id=1, source_target_pairs={{0,1},{1,0},{2,3},{3,2},{4,5},{5,4},{6,7},{7,6},{8,9},{9,8},{10,11... | collective-permute-start | bytes 2064392 | tf_op jit(solution)/shard_map/ppermute | solution.py:55
  4.2 1.9 %collective-permute-start = (bf16[384,128]{1,0:T(8,128)(2,1)S(1)}, bf16[384,128]{1,0:T(8,128)(2,1)S(1)}, u32[]{:S(2)}, u32[]{:S(2)}) collective-permute-start(bf16[384,128]{1,0:T(8,128)(2,1)S(1)} %get-tuple-element.37.refs_0_), channel_id=1, source_target_pairs={{0,1},{1,0},{2,3},{3,2},{4,5},{5,4},{6,7},{7,6},{8,9},{9,8},{10,11... | collective-permute-start | bytes 294920 | tf_op jit(solution)/shard_map/ppermute | solution.py:55
  6.4 6.3 %collective-permute-start.1 = (bf16[384,128]{1,0:T(8,128)(2,1)S(1)}, bf16[384,128]{1,0:T(8,128)(2,1)S(1)}, u32[]{:S(2)}, u32[]{:S(2)}) collective-permute-start(bf16[384,128]{1,0:T(8,128)(2,1)S(1)} %level1_0.1.refs_3_.refs_0_), channel_id=1, source_target_pairs={{0,2},{1,3},{2,0},{3,1},{4,6},{5,7},{6,4},{7,5},{8,10},{9,11},{10,... | collective-permute-start | bytes 294920 | tf_op jit(solution)/shard_map/ppermute | solution.py:55
  9.8 11.1 %collective-permute-start.5 = (bf16[384,256]{1,0:T(8,128)(2,1)S(1)}, bf16[384,256]{1,0:T(8,128)(2,1)S(1)}, u32[]{:S(2)}, u32[]{:S(2)}) collective-permute-start(bf16[384,256]{1,0:T(8,128)(2,1)S(1)} %level1_1.1.refs_6_.refs_0_), channel_id=1, source_target_pairs={{0,2},{1,3},{2,0},{3,1},{4,6},{5,7},{6,4},{7,5},{8,10},{9,11},{10,... | collective-permute-start | bytes 589832 | tf_op jit(solution)/shard_map/ppermute | solution.py:55
  13.4 8.3 %collective-permute-start.4 = (bf16[384,128]{1,0:T(8,128)(2,1)S(1)}, bf16[384,128]{1,0:T(8,128)(2,1)S(1)}, u32[]{:S(2)}, u32[]{:S(2)}) collective-permute-start(bf16[384,128]{1,0:T(8,128)(2,1)S(1)} %get-tuple-element.42.refs_3_.refs_0_), channel_id=1, source_target_pairs={{0,4},{1,5},{2,6},{3,7},{4,0},{5,1},{6,2},{7,3},{8,12},{9,13},{10,... | collective-permute-start | bytes 294920 | tf_op jit(solution)/shard_map/ppermute | solution.py:55
  16.4 12.5 %collective-permute-start.3 = (bf16[384,384]{1,0:T(8,128)(2,1)S(1)}, bf16[384,384]{1,0:T(8,128)(2,1)S(1)}, u32[]{:S(2)}, u32[]{:S(2)}) collective-permute-start(bf16[384,384]{1,0:T(8,128)(2,1)S(1)} %get-tuple-element.41.refs_0_), channel_id=1, source_target_pairs={{0,2},{1,3},{2,0},{3,1},{4,6},{5,7},{6,4},{7,5},{8,10},{9,11},{10,... | collective-permute-start | bytes 884744 | tf_op jit(solution)/shard_map/ppermute | solution.py:55
  21.3 12.7 %collective-permute-start.9 = (bf16[384,256]{1,0:T(8,128)(2,1)S(1)}, bf16[384,256]{1,0:T(8,128)(2,1)S(1)}, u32[]{:S(2)}, u32[]{:S(2)}) collective-permute-start(bf16[384,256]{1,0:T(8,128)(2,1)S(1)} %level2_1.1.refs_3_.refs_0_), channel_id=1, source_target_pairs={{0,4},{1,5},{2,6},{3,7},{4,0},{5,1},{6,2},{7,3},{8,12},{9,13},{10,... | collective-permute-start | bytes 589832 | tf_op jit(solution)/shard_map/ppermute | solution.py:55
  22.0 1.4 %collective-permute-start.6 = (bf16[384,128]{1,0:T(8,128)(2,1)S(1)}, bf16[384,128]{1,0:T(8,128)(2,1)S(1)}, u32[]{:S(2)}, u32[]{:S(2)}) collective-permute-start(bf16[384,128]{1,0:T(8,128)(2,1)S(1)} %level3_0.1.refs_0_), channel_id=1, source_target_pairs={{0,1},{1,0},{2,3},{3,2},{4,5},{5,4},{6,7},{7,6},{8,9},{9,8},{10,11... | collective-permute-start | bytes 294920 | tf_op jit(solution)/shard_map/ppermute | solution.py:55
  24.0 10.4 %collective-permute-start.10 = (bf16[512,128]{1,0:T(8,128)(2,1)S(1)}, bf16[512,128]{1,0:T(8,128)(2,1)S(1)}, u32[]{:S(2)}, u32[]{:S(2)}) collective-permute-start(bf16[512,128]{1,0:T(8,128)(2,1)S(1)} %get-tuple-element.49), channel_id=1, source_target_pairs={{0,16},{8,24},{16,0},{24,8},{1,17},{9,25},{17,1},{25,9},{2,18},{10... | collective-permute-start | bytes 393224 | tf_op jit(solution)/shard_map/ppermute | solution.py:55
  29.6 9.7 %collective-permute-start.8 = (bf16[384,256]{1,0:T(8,128)(2,1)S(1)}, bf16[384,256]{1,0:T(8,128)(2,1)S(1)}, u32[]{:S(2)}, u32[]{:S(2)}) collective-permute-start(bf16[384,256]{1,0:T(8,128)(2,1)S(1)} %get-tuple-element.48.refs_0_), channel_id=1, source_target_pairs={{0,2},{1,3},{2,0},{3,1},{4,6},{5,7},{6,4},{7,5},{8,10},{9,11},{10,... | collective-permute-start | bytes 589832 | tf_op jit(solution)/shard_map/ppermute | solution.py:55
  29.7 22.7 %collective-permute-start.7 = (bf16[384,384]{1,0:T(8,128)(2,1)S(1)}, bf16[384,384]{1,0:T(8,128)(2,1)S(1)}, u32[]{:S(2)}, u32[]{:S(2)}) collective-permute-start(bf16[384,384]{1,0:T(8,128)(2,1)S(1)} %get-tuple-element.47.refs_3_.refs_0_), channel_id=1, source_target_pairs={{0,4},{1,5},{2,6},{3,7},{4,0},{5,1},{6,2},{7,3},{8,12},{9,13},{10,... | collective-permute-start | bytes 884744 | tf_op jit(solution)/shard_map/ppermute | solution.py:55
  34.3 1.9 %collective-permute-start.11 = (bf16[384,256]{1,0:T(8,128)(2,1)S(1)}, bf16[384,256]{1,0:T(8,128)(2,1)S(1)}, u32[]{:S(2)}, u32[]{:S(2)}) collective-permute-start(bf16[384,256]{1,0:T(8,128)(2,1)S(1)} %level3_1.1.refs_0_), channel_id=1, source_target_pairs={{0,1},{1,0},{2,3},{3,2},{4,5},{5,4},{6,7},{7,6},{8,9},{9,8},{10,11... | collective-permute-start | bytes 589832 | tf_op jit(solution)/shard_map/ppermute | solution.py:55
  34.7 18.4 %collective-permute-start.13 = (bf16[256,128]{1,0:T(8,128)(2,1)S(1)}, bf16[256,128]{1,0:T(8,128)(2,1)S(1)}, u32[]{:S(2)}, u32[]{:S(2)}) collective-permute-start(bf16[256,128]{1,0:T(8,128)(2,1)S(1)} %get-tuple-element.54), channel_id=1, source_target_pairs={{0,8},{8,0},{16,24},{24,16},{1,9},{9,1},{17,25},{25,17},{2,10},{10... | collective-permute-start | bytes 196616 | tf_op jit(solution)/shard_map/ppermute | solution.py:55
  39.7 20.1 %collective-permute-start.14 = (bf16[384,256]{1,0:T(8,128)(2,1)S(1)}, bf16[384,256]{1,0:T(8,128)(2,1)S(1)}, u32[]{:S(2)}, u32[]{:S(2)}) collective-permute-start(bf16[384,256]{1,0:T(8,128)(2,1)S(1)} %level2_3.1.refs_3_.refs_0_), channel_id=1, source_target_pairs={{0,4},{1,5},{2,6},{3,7},{4,0},{5,1},{6,2},{7,3},{8,12},{9,13},{10,... | collective-permute-start | bytes 589832 | tf_op jit(solution)/shard_map/ppermute | solution.py:55
  40.2 12.8 %collective-permute-start.12 = (bf16[512,256]{1,0:T(8,128)(2,1)S(1)}, bf16[512,256]{1,0:T(8,128)(2,1)S(1)}, u32[]{:S(2)}, u32[]{:S(2)}) collective-permute-start(bf16[512,256]{1,0:T(8,128)(2,1)S(1)} %get-tuple-element.52), channel_id=1, source_target_pairs={{0,8},{8,0},{16,24},{24,16},{1,9},{9,1},{17,25},{25,17},{2,10},{10... | collective-permute-start | bytes 786440 | tf_op jit(solution)/shard_map/ppermute | solution.py:55
  52.9 2.0 %collective-permute-start.15 = (bf16[384,384]{1,0:T(8,128)(2,1)S(1)}, bf16[384,384]{1,0:T(8,128)(2,1)S(1)}, u32[]{:S(2)}, u32[]{:S(2)}) collective-permute-start(bf16[384,384]{1,0:T(8,128)(2,1)S(1)} %level3_2.1.refs_0_), channel_id=1, source_target_pairs={{0,1},{1,0},{2,3},{3,2},{4,5},{5,4},{6,7},{7,6},{8,9},{9,8},{10,11... | collective-permute-start | bytes 884744 | tf_op jit(solution)/shard_map/ppermute | solution.py:55
  53.4 6.8 %collective-permute-start.16 = (bf16[256,256]{1,0:T(8,128)(2,1)S(1)}, bf16[256,256]{1,0:T(8,128)(2,1)S(1)}, u32[]{:S(2)}, u32[]{:S(2)}) collective-permute-start(bf16[256,256]{1,0:T(8,128)(2,1)S(1)} %get-tuple-element.59), channel_id=1, source_target_pairs={{0,16},{8,24},{16,0},{24,8},{1,17},{9,25},{17,1},{25,9},{2,18},{10... | collective-permute-start | bytes 393224 | tf_op jit(solution)/shard_map/ppermute | solution.py:55
  56.2 9.3 %collective-permute-start.17 = (bf16[256,384]{1,0:T(8,128)(2,1)S(1)}, bf16[256,384]{1,0:T(8,128)(2,1)S(1)}, u32[]{:S(2)}, u32[]{:S(2)}) collective-permute-start(bf16[256,384]{1,0:T(8,128)(2,1)S(1)} %get-tuple-element.61), channel_id=1, source_target_pairs={{0,24},{8,16},{16,8},{24,0},{1,25},{9,17},{17,9},{25,1},{2,26},{10... | collective-permute-start | bytes 589832 | tf_op jit(solution)/shard_map/ppermute | solution.py:55
  58.3 10.9 %collective-permute-start.18 = (bf16[256,384]{1,0:T(8,128)(2,1)S(1)}, bf16[256,384]{1,0:T(8,128)(2,1)S(1)}, u32[]{:S(2)}, u32[]{:S(2)}) collective-permute-start(bf16[256,384]{1,0:T(8,128)(2,1)S(1)} %get-tuple-element.62), channel_id=1, source_target_pairs={{0,16},{8,24},{16,0},{24,8},{1,17},{9,25},{17,1},{25,9},{2,18},{10... | collective-permute-start | bytes 589832 | tf_op jit(solution)/shard_map/ppermute | solution.py:55
  59.2 10.0 %collective-permute-start.19 = (bf16[256,384]{1,0:T(8,128)(2,1)S(1)}, bf16[256,384]{1,0:T(8,128)(2,1)S(1)}, u32[]{:S(2)}, u32[]{:S(2)}) collective-permute-start(bf16[256,384]{1,0:T(8,128)(2,1)S(1)} %get-tuple-element.63), channel_id=1, source_target_pairs={{0,8},{8,0},{16,24},{24,16},{1,9},{9,1},{17,25},{25,17},{2,10},{10... | collective-permute-start | bytes 589832 | tf_op jit(solution)/shard_map/ppermute | solution.py:55
  60.1 1.5 %collective-permute-start.20 = (bf16[384,256]{1,0:T(8,128)(2,1)S(1)}, bf16[384,256]{1,0:T(8,128)(2,1)S(1)}, u32[]{:S(2)}, u32[]{:S(2)}) collective-permute-start(bf16[384,256]{1,0:T(8,128)(2,1)S(1)} %level3_3.1.refs_0_), channel_id=1, source_target_pairs={{0,1},{1,0},{2,3},{3,2},{4,5},{5,4},{6,7},{7,6},{8,9},{9,8},{10,11... | collective-permute-start | bytes 589832 | tf_op jit(solution)/shard_map/ppermute | solution.py:55
  62.5 9.6 %collective-permute-start.21 = (bf16[256,256]{1,0:T(8,128)(2,1)S(1)}, bf16[256,256]{1,0:T(8,128)(2,1)S(1)}, u32[]{:S(2)}, u32[]{:S(2)}) collective-permute-start(bf16[256,256]{1,0:T(8,128)(2,1)S(1)} %get-tuple-element.66), channel_id=1, source_target_pairs={{0,24},{8,16},{16,8},{24,0},{1,25},{9,17},{17,9},{25,1},{2,26},{10... | collective-permute-start | bytes 393224 | tf_op jit(solution)/shard_map/ppermute | solution.py:55
  64.6 9.5 %collective-permute-start.22 = (bf16[256,256]{1,0:T(8,128)(2,1)S(1)}, bf16[256,256]{1,0:T(8,128)(2,1)S(1)}, u32[]{:S(2)}, u32[]{:S(2)}) collective-permute-start(bf16[256,256]{1,0:T(8,128)(2,1)S(1)} %get-tuple-element.67), channel_id=1, source_target_pairs={{0,16},{8,24},{16,0},{24,8},{1,17},{9,25},{17,1},{25,9},{2,18},{10... | collective-permute-start | bytes 393224 | tf_op jit(solution)/shard_map/ppermute | solution.py:55
  65.5 8.5 %collective-permute-start.23 = (bf16[256,256]{1,0:T(8,128)(2,1)S(1)}, bf16[256,256]{1,0:T(8,128)(2,1)S(1)}, u32[]{:S(2)}, u32[]{:S(2)}) collective-permute-start(bf16[256,256]{1,0:T(8,128)(2,1)S(1)} %get-tuple-element.68), channel_id=1, source_target_pairs={{0,8},{8,0},{16,24},{24,16},{1,9},{9,1},{17,25},{25,17},{2,10},{10... | collective-permute-start | bytes 393224 | tf_op jit(solution)/shard_map/ppermute | solution.py:55

commit v7 on v6

--- a/solution.py
+++ b/solution.py
@@ -7,7 +7,7 @@
 from jax.experimental.pallas import tpu as pltpu
 from jax.sharding import PartitionSpec as P
 
-SHARES = (1, 2, 3, 2)
+SHARES = (1, 2, 2, 3)
 PRELOADED = 2
 COST = 6 * 10**9
 BF16 = jnp.bfloat16

time: 75.2 us -> 76.5 us (1.017)
  waiting for transfers between devices: 30.9 us -> 33.5 us
  starting transfers between devices: 27.9 us -> 26.3 us
    ppermute x24, waiting for transfers between devices: 30.9 us -> 33.5 us  [partner(): return lax.ppermute(value, axis, pairs)]
    ppermute x24, starting transfers between devices: 27.9 us -> 26.3 us  [partner(): return lax.ppermute(value, axis, pairs)]
  transfers between devices with their start and end apart: 24 -> 24, of which waited for: 10 -> 9; matrix products, arithmetic and copies ran while one was open for 0% -> 0% of each run, Pallas kernels for 15% -> 15%
where the time goes in v7:
time: 76.5 us; the launch traced here: 76.3 us
  waiting for transfers between devices  33.5 us (44%)
  starting transfers between devices  26.3 us (34%)
  Pallas kernels  16.3 us (21%)
    ppermute x24, waiting for transfers between devices, partner(): return lax.ppermute(value, axis, pairs)  33.5 us
    ppermute x24, starting transfers between devices, partner(): return lax.ppermute(value, axis, pairs)  26.3 us
    pallas_call x20, Pallas kernels, call(): pl.pallas_call(body, name=name, in_specs=[*in_specs, *[ANY] * len(after)]...  15.4 us
  transfers between devices with their start and end apart: 24, of which 9 were waited for; matrix products, arithmetic and copies ran while one was open for 0% of the time, Pallas kernels for 15%

profile of v7, /device:TPU:0, one launch (start us, length us, event | category | flops | bytes accessed | tf_op | source)
XLA Modules:
  0.0 76.3 jit_solution(677957122388387248)
XLA Ops:
  0.0 3.7 %leaf.1 = (bf16[384,128]{1,0:T(8,128)(2,1)S(1)}, bf16[384,896]{1,0:T(8,128)(2,1)S(1)}, bf16[2,384,768]{2,1,0:T(8,128)(2,1)S(1)}, bf16[2,384,768]{2,1,0:T(8,128)(2,1)S(1)}) custom-call(bf16[2,1024,512]{2,1,0:T(8,128)(2,1)} %bitcast.9, bf16[2,384,1024]{2,1,0:T(8,128)(2,1)} %bitcast.10, bf16[5,2,384,768]{3,2,1,0:T(8,128)(2,1)} %bitcast.7, s32[2,5]{1,0:T(2,128)} %bitcast.12), custom_call_target="tpu_custom_call" | custom-call | flops 6000000000 | tf_op jit(solution)/shard_map/leaf/pallas_call | solution.py:41
  3.7 0.5 collective-permute-start.2
  4.3 1.8 %collective-permute-done.refs_1_ = bf16[384,128]{1,0:T(8,128)(2,1)S(1)} collective-permute-done((bf16[384,128]{1,0:T(8,128)(2,1)S(1)}, bf16[384,128]{1,0:T(8,128)(2,1)S(1)}, u32[]{:S(2)}, u32[]{:S(2)}) %collective-permute-start) | collective-permute-done | bytes 98336 | tf_op jit(solution)/shard_map/ppermute | solution.py:55
  6.1 0.3 level1_0.1.refs_3_.refs_0_
  6.4 3.0 %collective-permute-start.1 = (bf16[384,128]{1,0:T(8,128)(2,1)S(1)}, bf16[384,128]{1,0:T(8,128)(2,1)S(1)}, u32[]{:S(2)}, u32[]{:S(2)}) collective-permute-start(bf16[384,128]{1,0:T(8,128)(2,1)S(1)} %level1_0.1.refs_3_.refs_0_), channel_id=1, source_target_pairs={{0,2},{1,3},{2,0},{3,1},{4,6},{5,7},{6,4},{7,5},{8,10},{9,11},{10,... | collective-permute-start | bytes 294920 | tf_op jit(solution)/shard_map/ppermute | solution.py:55
  9.5 0.4 level1_1.1.refs_6_.refs_0_
  9.9 2.8 %collective-permute-done.1.refs_1_ = bf16[384,128]{1,0:T(8,128)(2,1)S(1)} collective-permute-done((bf16[384,128]{1,0:T(8,128)(2,1)S(1)}, bf16[384,128]{1,0:T(8,128)(2,1)S(1)}, u32[]{:S(2)}, u32[]{:S(2)}) %collective-permute-start.1) | collective-permute-done | bytes 98336 | tf_op jit(solution)/shard_map/ppermute | solution.py:55
  12.7 0.7 level2_0.1
  13.4 3.0 %collective-permute-start.4 = (bf16[384,128]{1,0:T(8,128)(2,1)S(1)}, bf16[384,128]{1,0:T(8,128)(2,1)S(1)}, u32[]{:S(2)}, u32[]{:S(2)}) collective-permute-start(bf16[384,128]{1,0:T(8,128)(2,1)S(1)} %get-tuple-element.42.refs_3_.refs_0_), channel_id=1, source_target_pairs={{0,4},{1,5},{2,6},{3,7},{4,0},{5,1},{6,2},{7,3},{8,12},{9,13},{10,... | collective-permute-start | bytes 294920 | tf_op jit(solution)/shard_map/ppermute | solution.py:55
  16.4 2.0 %collective-permute-start.3 = (bf16[384,256]{1,0:T(8,128)(2,1)S(1)}, bf16[384,256]{1,0:T(8,128)(2,1)S(1)}, u32[]{:S(2)}, u32[]{:S(2)}) collective-permute-start(bf16[384,256]{1,0:T(8,128)(2,1)S(1)} %get-tuple-element.41.refs_0_), channel_id=1, source_target_pairs={{0,2},{1,3},{2,0},{3,1},{4,6},{5,7},{6,4},{7,5},{8,10},{9,11},{10,... | collective-permute-start | bytes 589832 | tf_op jit(solution)/shard_map/ppermute | solution.py:55
  18.4 2.5 %prefetch.1 = (bf16[2,384,768]{2,1,0:T(8,128)(2,1)S(1)}, bf16[2,384,768]{2,1,0:T(8,128)(2,1)S(1)}, bf16[2,1024,384]{2,1,0:T(8,128)(2,1)S(1)}) custom-call(bf16[5,2,384,768]{3,2,1,0:T(8,128)(2,1)} %bitcast.8, bf16[2,1024,384]{2,1,0:T(8,128)(2,1)} %bitcast.11, s32[2,5]{1,0:T(2,128)} %bitcast.13, bf16[384,128]{1,0:T(8,128)(2,1)S(1)} %get-tuple-element.42.refs_3_.refs_0_), custom_call_target="tpu_custom_call" | custom-call | flops 6000000000 | tf_op jit(solution)/shard_map/prefetch/pallas_call | solution.py:41
  20.9 0.4 level2_1.1.refs_3_.refs_0_
  21.3 0.4 collective-permute-start.9
  21.7 0.3 level3_0.1.refs_0_
  22.1 0.2 between_0.1.refs_0_
  22.3 1.0 %collective-permute-done.6.refs_1_ = bf16[384,128]{1,0:T(8,128)(2,1)S(1)} collective-permute-done((bf16[384,128]{1,0:T(8,128)(2,1)S(1)}, bf16[384,128]{1,0:T(8,128)(2,1)S(1)}, u32[]{:S(2)}, u32[]{:S(2)}) %collective-permute-start.6) | collective-permute-done | bytes 98336 | tf_op jit(solution)/shard_map/ppermute | solution.py:55
  23.4 0.6 last_0.1
  24.0 1.6 %collective-permute-start.10 = (bf16[512,128]{1,0:T(8,128)(2,1)S(1)}, bf16[512,128]{1,0:T(8,128)(2,1)S(1)}, u32[]{:S(2)}, u32[]{:S(2)}) collective-permute-start(bf16[512,128]{1,0:T(8,128)(2,1)S(1)} %get-tuple-element.49), channel_id=1, source_target_pairs={{0,16},{8,24},{16,0},{24,8},{1,17},{9,25},{17,1},{25,9},{2,18},{10... | collective-permute-start | bytes 393224 | tf_op jit(solution)/shard_map/ppermute | solution.py:55
  25.6 0.8 %level2_2.1 = (bf16[384,256]{1,0:T(8,128)(2,1)S(1)}, bf16[384,384]{1,0:T(8,128)(2,1)S(1)}) custom-call(bf16[384,256]{1,0:T(8,128)(2,1)S(1)} %get-tuple-element.41.refs_0_, bf16[384,256]{1,0:T(8,128)(2,1)S(1)} %collective-permute-done.3.refs_1_, bf16[2,384,768]{2,1,0:T(8,128)(2,1)S(1)} %get-tuple-element.39.refs_2_, ...), custom_call_target="tpu_custom_call" | custom-call | flops 6000000000 | tf_op jit(solution)/shard_map/level2_2/pallas_call | solution.py:41
  26.4 2.7 %collective-permute-start.7 = (bf16[384,256]{1,0:T(8,128)(2,1)S(1)}, bf16[384,256]{1,0:T(8,128)(2,1)S(1)}, u32[]{:S(2)}, u32[]{:S(2)}) collective-permute-start(bf16[384,256]{1,0:T(8,128)(2,1)S(1)} %get-tuple-element.47.refs_3_.refs_0_), channel_id=1, source_target_pairs={{0,4},{1,5},{2,6},{3,7},{4,0},{5,1},{6,2},{7,3},{8,12},{9,13},{10,... | collective-permute-start | bytes 589832 | tf_op jit(solution)/shard_map/ppermute | solution.py:55
  29.0 1.8 %collective-permute-start.8 = (bf16[384,384]{1,0:T(8,128)(2,1)S(1)}, bf16[384,384]{1,0:T(8,128)(2,1)S(1)}, u32[]{:S(2)}, u32[]{:S(2)}) collective-permute-start(bf16[384,384]{1,0:T(8,128)(2,1)S(1)} %get-tuple-element.48.refs_0_), channel_id=1, source_target_pairs={{0,2},{1,3},{2,0},{3,1},{4,6},{5,7},{6,4},{7,5},{8,10},{9,11},{10,... | collective-permute-start | bytes 884744 | tf_op jit(solution)/shard_map/ppermute | solution.py:55
  30.8 6.5 %collective-permute-done.9.refs_1_ = bf16[384,256]{1,0:T(8,128)(2,1)S(1)} collective-permute-done((bf16[384,256]{1,0:T(8,128)(2,1)S(1)}, bf16[384,256]{1,0:T(8,128)(2,1)S(1)}, u32[]{:S(2)}, u32[]{:S(2)}) %collective-permute-start.9) | collective-permute-done | bytes 196640 | tf_op jit(solution)/shard_map/ppermute | solution.py:55
  37.3 0.4 level3_1.1.refs_0_
  37.8 0.3 between_1.1
  38.0 1.5 %collective-permute-start.13 = (bf16[256,128]{1,0:T(8,128)(2,1)S(1)}, bf16[256,128]{1,0:T(8,128)(2,1)S(1)}, u32[]{:S(2)}, u32[]{:S(2)}) collective-permute-start(bf16[256,128]{1,0:T(8,128)(2,1)S(1)} %get-tuple-element.54), channel_id=1, source_target_pairs={{0,8},{8,0},{16,24},{24,16},{1,9},{9,1},{17,25},{25,17},{2,10},{10... | collective-permute-start | bytes 196616 | tf_op jit(solution)/shard_map/ppermute | solution.py:55
  39.6 0.8 %last_1.1 = (f32[512,256]{1,0:T(8,128)S(1)}, bf16[512,256]{1,0:T(8,128)(2,1)S(1)}) custom-call(f32[384,256]{1,0:T(8,128)S(1)} %get-tuple-element.50.refs_0_, bf16[384,256]{1,0:T(8,128)(2,1)S(1)} %collective-permute-done.11.refs_1_, bf16[2,384,768]{2,1,0:T(8,128)(2,1)S(1)} %get-tuple-element.45.refs_1_.refs_2_, ...), custom_call_target="tpu_custom_call" | custom-call | flops 6000000000 | tf_op jit(solution)/shard_map/last_1/pallas_call | solution.py:41
  40.4 1.2 %collective-permute-start.12 = (bf16[512,256]{1,0:T(8,128)(2,1)S(1)}, bf16[512,256]{1,0:T(8,128)(2,1)S(1)}, u32[]{:S(2)}, u32[]{:S(2)}) collective-permute-start(bf16[512,256]{1,0:T(8,128)(2,1)S(1)} %get-tuple-element.52), channel_id=1, source_target_pairs={{0,8},{8,0},{16,24},{24,16},{1,9},{9,1},{17,25},{25,17},{2,10},{10... | collective-permute-start | bytes 786440 | tf_op jit(solution)/shard_map/ppermute | solution.py:55
  41.5 0.5 collective-permute-done.8.refs_1_
  42.1 0.5 level2_3.1.refs_3_.refs_0_
  42.6 0.2 collective-permute-start.14
  42.8 0.5 level3_2.1.refs_0_
  43.3 5.5 %collective-permute-done.12.refs_3_ = bf16[512,256]{1,0:T(8,128)(2,1)S(1)} collective-permute-done((bf16[512,256]{1,0:T(8,128)(2,1)S(1)}, bf16[512,256]{1,0:T(8,128)(2,1)S(1)}, u32[]{:S(2)}, u32[]{:S(2)}) %collective-permute-start.12) | collective-permute-done | bytes 262176 | tf_op jit(solution)/shard_map/ppermute | solution.py:55
  48.9 0.3 between_2.1
  49.2 1.9 %collective-permute-start.16 = (bf16[256,256]{1,0:T(8,128)(2,1)S(1)}, bf16[256,256]{1,0:T(8,128)(2,1)S(1)}, u32[]{:S(2)}, u32[]{:S(2)}) collective-permute-start(bf16[256,256]{1,0:T(8,128)(2,1)S(1)} %get-tuple-element.59), channel_id=1, source_target_pairs={{0,16},{8,24},{16,0},{24,8},{1,17},{9,25},{17,1},{25,9},{2,18},{10... | collective-permute-start | bytes 393224 | tf_op jit(solution)/shard_map/ppermute | solution.py:55
  51.1 1.0 %last_2.1 = (f32[256,256]{1,0:T(8,128)S(1)}, bf16[256,256]{1,0:T(8,128)(2,1)S(1)}, bf16[256,256]{1,0:T(8,128)(2,1)S(1)}, bf16[256,256]{1,0:T(8,128)(2,1)S(1)}) custom-call(f32[384,256]{1,0:T(8,128)S(1)} %get-tuple-element.56.refs_0_, bf16[384,256]{1,0:T(8,128)(2,1)S(1)} %collective-permute-done.15.refs_1_, ...), custom_call_target="tpu_custom_call" | custom-call | flops 6000000000 | tf_op jit(solution)/shard_map/last_2/pallas_call | solution.py:41
  52.1 0.7 collective-permute-start.17
  52.8 4.5 %collective-permute-done.14.refs_1_ = bf16[384,384]{1,0:T(8,128)(2,1)S(1)} collective-permute-done((bf16[384,384]{1,0:T(8,128)(2,1)S(1)}, bf16[384,384]{1,0:T(8,128)(2,1)S(1)}, u32[]{:S(2)}, u32[]{:S(2)}) %collective-permute-start.14) | collective-permute-done | bytes 294944 | tf_op jit(solution)/shard_map/ppermute | solution.py:55
  57.3 0.5 level3_3.1.refs_0_
  57.9 0.3 between_3.1
  58.2 1.2 %collective-permute-done.20.refs_1_ = bf16[384,384]{1,0:T(8,128)(2,1)S(1)} collective-permute-done((bf16[384,384]{1,0:T(8,128)(2,1)S(1)}, bf16[384,384]{1,0:T(8,128)(2,1)S(1)}, u32[]{:S(2)}, u32[]{:S(2)}) %collective-permute-start.20) | collective-permute-done | bytes 294944 | tf_op jit(solution)/shard_map/ppermute | solution.py:55
  59.5 1.0 %last_3.1 = (f32[256,384]{1,0:T(8,128)S(1)}, bf16[256,384]{1,0:T(8,128)(2,1)S(1)}, bf16[256,384]{1,0:T(8,128)(2,1)S(1)}, bf16[256,384]{1,0:T(8,128)(2,1)S(1)}) custom-call(f32[384,384]{1,0:T(8,128)S(1)} %get-tuple-element.64.refs_0_, bf16[384,384]{1,0:T(8,128)(2,1)S(1)} %collective-permute-done.20.refs_1_, ...), custom_call_target="tpu_custom_call" | custom-call | flops 6000000000 | tf_op jit(solution)/shard_map/last_3/pallas_call | solution.py:41
  60.4 1.3 %collective-permute-start.21 = (bf16[256,384]{1,0:T(8,128)(2,1)S(1)}, bf16[256,384]{1,0:T(8,128)(2,1)S(1)}, u32[]{:S(2)}, u32[]{:S(2)}) collective-permute-start(bf16[256,384]{1,0:T(8,128)(2,1)S(1)} %get-tuple-element.66), channel_id=1, source_target_pairs={{0,24},{8,16},{16,8},{24,0},{1,25},{9,17},{17,9},{25,1},{2,26},{10... | collective-permute-start | bytes 589832 | tf_op jit(solution)/shard_map/ppermute | solution.py:55
  61.8 1.7 %collective-permute-start.22 = (bf16[256,384]{1,0:T(8,128)(2,1)S(1)}, bf16[256,384]{1,0:T(8,128)(2,1)S(1)}, u32[]{:S(2)}, u32[]{:S(2)}) collective-permute-start(bf16[256,384]{1,0:T(8,128)(2,1)S(1)} %get-tuple-element.67), channel_id=1, source_target_pairs={{0,16},{8,24},{16,0},{24,8},{1,17},{9,25},{17,1},{25,9},{2,18},{10... | collective-permute-start | bytes 589832 | tf_op jit(solution)/shard_map/ppermute | solution.py:55
  63.5 0.5 collective-permute-start.23
  64.0 0.3 collective-permute-start.18
  64.3 1.5 %collective-permute-start.19 = (bf16[256,256]{1,0:T(8,128)(2,1)S(1)}, bf16[256,256]{1,0:T(8,128)(2,1)S(1)}, u32[]{:S(2)}, u32[]{:S(2)}) collective-permute-start(bf16[256,256]{1,0:T(8,128)(2,1)S(1)} %get-tuple-element.63), channel_id=1, source_target_pairs={{0,8},{8,0},{16,24},{24,16},{1,9},{9,1},{17,25},{25,17},{2,10},{10... | collective-permute-start | bytes 393224 | tf_op jit(solution)/shard_map/ppermute | solution.py:55
  65.8 9.6 %collective-permute-done.18.refs_4_ = bf16[256,256]{1,0:T(8,128)(2,1)S(1)} collective-permute-done((bf16[256,256]{1,0:T(8,128)(2,1)S(1)}, bf16[256,256]{1,0:T(8,128)(2,1)S(1)}, u32[]{:S(2)}, u32[]{:S(2)}) %collective-permute-start.18) | collective-permute-done | bytes 131104 | tf_op jit(solution)/shard_map/ppermute | solution.py:55
  75.4 1.0 %end.1 = bf16[2,256,512]{2,1,0:T(8,128)(2,1)} custom-call(bf16[256,128]{1,0:T(8,128)(2,1)S(1)} %get-tuple-element.55.refs_0_, bf16[256,256]{1,0:T(8,128)(2,1)S(1)} %get-tuple-element.60.refs_1_, f32[256,256]{1,0:T(8,128)S(1)} %get-tuple-element.57.refs_3_.refs_2_, bf16[256,256]{1,0:T(8,128)(2,1)S(1)} %collective-permute-done.17.refs_3_, ...), custom_call_target="tpu_custom_call" | custom-call | tf_op jit(solution)/shard_map/end/pallas_call | solution.py:378
  (21 shorter events, 0.5 us)
Async XLA Ops:
  3.7 5.8 %collective-permute-start.2 = (bf16[384,896]{1,0:T(8,128)(2,1)S(1)}, bf16[384,896]{1,0:T(8,128)(2,1)S(1)}, u32[]{:S(2)}, u32[]{:S(2)}) collective-permute-start(bf16[384,896]{1,0:T(8,128)(2,1)S(1)} %get-tuple-element.40.refs_0_.refs_3_), channel_id=1, source_target_pairs={{0,1},{1,0},{2,3},{3,2},{4,5},{5,4},{6,7},{7,6},{8,9},{9,8},{10,11... | collective-permute-start | bytes 2064392 | tf_op jit(solution)/shard_map/ppermute | solution.py:55
  4.2 1.9 %collective-permute-start = (bf16[384,128]{1,0:T(8,128)(2,1)S(1)}, bf16[384,128]{1,0:T(8,128)(2,1)S(1)}, u32[]{:S(2)}, u32[]{:S(2)}) collective-permute-start(bf16[384,128]{1,0:T(8,128)(2,1)S(1)} %get-tuple-element.37.refs_0_), channel_id=1, source_target_pairs={{0,1},{1,0},{2,3},{3,2},{4,5},{5,4},{6,7},{7,6},{8,9},{9,8},{10,11... | collective-permute-start | bytes 294920 | tf_op jit(solution)/shard_map/ppermute | solution.py:55
  6.4 6.3 %collective-permute-start.1 = (bf16[384,128]{1,0:T(8,128)(2,1)S(1)}, bf16[384,128]{1,0:T(8,128)(2,1)S(1)}, u32[]{:S(2)}, u32[]{:S(2)}) collective-permute-start(bf16[384,128]{1,0:T(8,128)(2,1)S(1)} %level1_0.1.refs_3_.refs_0_), channel_id=1, source_target_pairs={{0,2},{1,3},{2,0},{3,1},{4,6},{5,7},{6,4},{7,5},{8,10},{9,11},{10,... | collective-permute-start | bytes 294920 | tf_op jit(solution)/shard_map/ppermute | solution.py:55
  9.8 11.1 %collective-permute-start.5 = (bf16[384,256]{1,0:T(8,128)(2,1)S(1)}, bf16[384,256]{1,0:T(8,128)(2,1)S(1)}, u32[]{:S(2)}, u32[]{:S(2)}) collective-permute-start(bf16[384,256]{1,0:T(8,128)(2,1)S(1)} %level1_1.1.refs_6_.refs_0_), channel_id=1, source_target_pairs={{0,2},{1,3},{2,0},{3,1},{4,6},{5,7},{6,4},{7,5},{8,10},{9,11},{10,... | collective-permute-start | bytes 589832 | tf_op jit(solution)/shard_map/ppermute | solution.py:55
  13.4 8.3 %collective-permute-start.4 = (bf16[384,128]{1,0:T(8,128)(2,1)S(1)}, bf16[384,128]{1,0:T(8,128)(2,1)S(1)}, u32[]{:S(2)}, u32[]{:S(2)}) collective-permute-start(bf16[384,128]{1,0:T(8,128)(2,1)S(1)} %get-tuple-element.42.refs_3_.refs_0_), channel_id=1, source_target_pairs={{0,4},{1,5},{2,6},{3,7},{4,0},{5,1},{6,2},{7,3},{8,12},{9,13},{10,... | collective-permute-start | bytes 294920 | tf_op jit(solution)/shard_map/ppermute | solution.py:55
  16.4 9.1 %collective-permute-start.3 = (bf16[384,256]{1,0:T(8,128)(2,1)S(1)}, bf16[384,256]{1,0:T(8,128)(2,1)S(1)}, u32[]{:S(2)}, u32[]{:S(2)}) collective-permute-start(bf16[384,256]{1,0:T(8,128)(2,1)S(1)} %get-tuple-element.41.refs_0_), channel_id=1, source_target_pairs={{0,2},{1,3},{2,0},{3,1},{4,6},{5,7},{6,4},{7,5},{8,10},{9,11},{10,... | collective-permute-start | bytes 589832 | tf_op jit(solution)/shard_map/ppermute | solution.py:55
  21.3 16.0 %collective-permute-start.9 = (bf16[384,256]{1,0:T(8,128)(2,1)S(1)}, bf16[384,256]{1,0:T(8,128)(2,1)S(1)}, u32[]{:S(2)}, u32[]{:S(2)}) collective-permute-start(bf16[384,256]{1,0:T(8,128)(2,1)S(1)} %level2_1.1.refs_3_.refs_0_), channel_id=1, source_target_pairs={{0,4},{1,5},{2,6},{3,7},{4,0},{5,1},{6,2},{7,3},{8,12},{9,13},{10,... | collective-permute-start | bytes 589832 | tf_op jit(solution)/shard_map/ppermute | solution.py:55
  22.0 1.4 %collective-permute-start.6 = (bf16[384,128]{1,0:T(8,128)(2,1)S(1)}, bf16[384,128]{1,0:T(8,128)(2,1)S(1)}, u32[]{:S(2)}, u32[]{:S(2)}) collective-permute-start(bf16[384,128]{1,0:T(8,128)(2,1)S(1)} %level3_0.1.refs_0_), channel_id=1, source_target_pairs={{0,1},{1,0},{2,3},{3,2},{4,5},{5,4},{6,7},{7,6},{8,9},{9,8},{10,11... | collective-permute-start | bytes 294920 | tf_op jit(solution)/shard_map/ppermute | solution.py:55
  24.0 13.8 %collective-permute-start.10 = (bf16[512,128]{1,0:T(8,128)(2,1)S(1)}, bf16[512,128]{1,0:T(8,128)(2,1)S(1)}, u32[]{:S(2)}, u32[]{:S(2)}) collective-permute-start(bf16[512,128]{1,0:T(8,128)(2,1)S(1)} %get-tuple-element.49), channel_id=1, source_target_pairs={{0,16},{8,24},{16,0},{24,8},{1,17},{9,25},{17,1},{25,9},{2,18},{10... | collective-permute-start | bytes 393224 | tf_op jit(solution)/shard_map/ppermute | solution.py:55
  26.4 16.4 %collective-permute-start.7 = (bf16[384,256]{1,0:T(8,128)(2,1)S(1)}, bf16[384,256]{1,0:T(8,128)(2,1)S(1)}, u32[]{:S(2)}, u32[]{:S(2)}) collective-permute-start(bf16[384,256]{1,0:T(8,128)(2,1)S(1)} %get-tuple-element.47.refs_3_.refs_0_), channel_id=1, source_target_pairs={{0,4},{1,5},{2,6},{3,7},{4,0},{5,1},{6,2},{7,3},{8,12},{9,13},{10,... | collective-permute-start | bytes 589832 | tf_op jit(solution)/shard_map/ppermute | solution.py:55
  29.0 13.0 %collective-permute-start.8 = (bf16[384,384]{1,0:T(8,128)(2,1)S(1)}, bf16[384,384]{1,0:T(8,128)(2,1)S(1)}, u32[]{:S(2)}, u32[]{:S(2)}) collective-permute-start(bf16[384,384]{1,0:T(8,128)(2,1)S(1)} %get-tuple-element.48.refs_0_), channel_id=1, source_target_pairs={{0,2},{1,3},{2,0},{3,1},{4,6},{5,7},{6,4},{7,5},{8,10},{9,11},{10,... | collective-permute-start | bytes 884744 | tf_op jit(solution)/shard_map/ppermute | solution.py:55
  37.7 1.9 %collective-permute-start.11 = (bf16[384,256]{1,0:T(8,128)(2,1)S(1)}, bf16[384,256]{1,0:T(8,128)(2,1)S(1)}, u32[]{:S(2)}, u32[]{:S(2)}) collective-permute-start(bf16[384,256]{1,0:T(8,128)(2,1)S(1)} %level3_1.1.refs_0_), channel_id=1, source_target_pairs={{0,1},{1,0},{2,3},{3,2},{4,5},{5,4},{6,7},{7,6},{8,9},{9,8},{10,11... | collective-permute-start | bytes 589832 | tf_op jit(solution)/shard_map/ppermute | solution.py:55
  38.0 5.3 %collective-permute-start.13 = (bf16[256,128]{1,0:T(8,128)(2,1)S(1)}, bf16[256,128]{1,0:T(8,128)(2,1)S(1)}, u32[]{:S(2)}, u32[]{:S(2)}) collective-permute-start(bf16[256,128]{1,0:T(8,128)(2,1)S(1)} %get-tuple-element.54), channel_id=1, source_target_pairs={{0,8},{8,0},{16,24},{24,16},{1,9},{9,1},{17,25},{25,17},{2,10},{10... | collective-permute-start | bytes 196616 | tf_op jit(solution)/shard_map/ppermute | solution.py:55
  40.4 8.5 %collective-permute-start.12 = (bf16[512,256]{1,0:T(8,128)(2,1)S(1)}, bf16[512,256]{1,0:T(8,128)(2,1)S(1)}, u32[]{:S(2)}, u32[]{:S(2)}) collective-permute-start(bf16[512,256]{1,0:T(8,128)(2,1)S(1)} %get-tuple-element.52), channel_id=1, source_target_pairs={{0,8},{8,0},{16,24},{24,16},{1,9},{9,1},{17,25},{25,17},{2,10},{10... | collective-permute-start | bytes 786440 | tf_op jit(solution)/shard_map/ppermute | solution.py:55
  42.6 14.7 %collective-permute-start.14 = (bf16[384,384]{1,0:T(8,128)(2,1)S(1)}, bf16[384,384]{1,0:T(8,128)(2,1)S(1)}, u32[]{:S(2)}, u32[]{:S(2)}) collective-permute-start(bf16[384,384]{1,0:T(8,128)(2,1)S(1)} %level2_3.1.refs_3_.refs_0_), channel_id=1, source_target_pairs={{0,4},{1,5},{2,6},{3,7},{4,0},{5,1},{6,2},{7,3},{8,12},{9,13},{10,... | collective-permute-start | bytes 884744 | tf_op jit(solution)/shard_map/ppermute | solution.py:55
  43.3 7.9 %collective-permute-start.15 = (bf16[384,256]{1,0:T(8,128)(2,1)S(1)}, bf16[384,256]{1,0:T(8,128)(2,1)S(1)}, u32[]{:S(2)}, u32[]{:S(2)}) collective-permute-start(bf16[384,256]{1,0:T(8,128)(2,1)S(1)} %level3_2.1.refs_0_), channel_id=1, source_target_pairs={{0,1},{1,0},{2,3},{3,2},{4,5},{5,4},{6,7},{7,6},{8,9},{9,8},{10,11... | collective-permute-start | bytes 589832 | tf_op jit(solution)/shard_map/ppermute | solution.py:55
  49.2 8.7 %collective-permute-start.16 = (bf16[256,256]{1,0:T(8,128)(2,1)S(1)}, bf16[256,256]{1,0:T(8,128)(2,1)S(1)}, u32[]{:S(2)}, u32[]{:S(2)}) collective-permute-start(bf16[256,256]{1,0:T(8,128)(2,1)S(1)} %get-tuple-element.59), channel_id=1, source_target_pairs={{0,16},{8,24},{16,0},{24,8},{1,17},{9,25},{17,1},{25,9},{2,18},{10... | collective-permute-start | bytes 393224 | tf_op jit(solution)/shard_map/ppermute | solution.py:55
  52.1 12.2 %collective-permute-start.17 = (bf16[256,256]{1,0:T(8,128)(2,1)S(1)}, bf16[256,256]{1,0:T(8,128)(2,1)S(1)}, u32[]{:S(2)}, u32[]{:S(2)}) collective-permute-start(bf16[256,256]{1,0:T(8,128)(2,1)S(1)} %get-tuple-element.61), channel_id=1, source_target_pairs={{0,24},{8,16},{16,8},{24,0},{1,25},{9,17},{17,9},{25,1},{2,26},{10... | collective-permute-start | bytes 393224 | tf_op jit(solution)/shard_map/ppermute | solution.py:55
  57.8 1.6 %collective-permute-start.20 = (bf16[384,384]{1,0:T(8,128)(2,1)S(1)}, bf16[384,384]{1,0:T(8,128)(2,1)S(1)}, u32[]{:S(2)}, u32[]{:S(2)}) collective-permute-start(bf16[384,384]{1,0:T(8,128)(2,1)S(1)} %level3_3.1.refs_0_), channel_id=1, source_target_pairs={{0,1},{1,0},{2,3},{3,2},{4,5},{5,4},{6,7},{7,6},{8,9},{9,8},{10,11... | collective-permute-start | bytes 884744 | tf_op jit(solution)/shard_map/ppermute | solution.py:55
  60.4 14.9 %collective-permute-start.21 = (bf16[256,384]{1,0:T(8,128)(2,1)S(1)}, bf16[256,384]{1,0:T(8,128)(2,1)S(1)}, u32[]{:S(2)}, u32[]{:S(2)}) collective-permute-start(bf16[256,384]{1,0:T(8,128)(2,1)S(1)} %get-tuple-element.66), channel_id=1, source_target_pairs={{0,24},{8,16},{16,8},{24,0},{1,25},{9,17},{17,9},{25,1},{2,26},{10... | collective-permute-start | bytes 589832 | tf_op jit(solution)/shard_map/ppermute | solution.py:55
  61.8 13.6 %collective-permute-start.22 = (bf16[256,384]{1,0:T(8,128)(2,1)S(1)}, bf16[256,384]{1,0:T(8,128)(2,1)S(1)}, u32[]{:S(2)}, u32[]{:S(2)}) collective-permute-start(bf16[256,384]{1,0:T(8,128)(2,1)S(1)} %get-tuple-element.67), channel_id=1, source_target_pairs={{0,16},{8,24},{16,0},{24,8},{1,17},{9,25},{17,1},{25,9},{2,18},{10... | collective-permute-start | bytes 589832 | tf_op jit(solution)/shard_map/ppermute | solution.py:55
  63.5 11.9 %collective-permute-start.23 = (bf16[256,384]{1,0:T(8,128)(2,1)S(1)}, bf16[256,384]{1,0:T(8,128)(2,1)S(1)}, u32[]{:S(2)}, u32[]{:S(2)}) collective-permute-start(bf16[256,384]{1,0:T(8,128)(2,1)S(1)} %get-tuple-element.68), channel_id=1, source_target_pairs={{0,8},{8,0},{16,24},{24,16},{1,9},{9,1},{17,25},{25,17},{2,10},{10... | collective-permute-start | bytes 589832 | tf_op jit(solution)/shard_map/ppermute | solution.py:55
  64.0 11.4 %collective-permute-start.18 = (bf16[256,256]{1,0:T(8,128)(2,1)S(1)}, bf16[256,256]{1,0:T(8,128)(2,1)S(1)}, u32[]{:S(2)}, u32[]{:S(2)}) collective-permute-start(bf16[256,256]{1,0:T(8,128)(2,1)S(1)} %get-tuple-element.62), channel_id=1, source_target_pairs={{0,16},{8,24},{16,0},{24,8},{1,17},{9,25},{17,1},{25,9},{2,18},{10... | collective-permute-start | bytes 393224 | tf_op jit(solution)/shard_map/ppermute | solution.py:55
  64.3 11.0 %collective-permute-start.19 = (bf16[256,256]{1,0:T(8,128)(2,1)S(1)}, bf16[256,256]{1,0:T(8,128)(2,1)S(1)}, u32[]{:S(2)}, u32[]{:S(2)}) collective-permute-start(bf16[256,256]{1,0:T(8,128)(2,1)S(1)} %get-tuple-element.63), channel_id=1, source_target_pairs={{0,8},{8,0},{16,24},{24,16},{1,9},{9,1},{17,25},{25,17},{2,10},{10... | collective-permute-start | bytes 393224 | tf_op jit(solution)/shard_map/ppermute | solution.py:55

commit v8 on v7

--- a/solution.py
+++ b/solution.py
@@ -7,7 +7,9 @@
 from jax.experimental.pallas import tpu as pltpu
 from jax.sharding import PartitionSpec as P
 
-SHARES = (1, 2, 2, 3)
+SHARES = (1, 2, 2, 2, 1)
+GROUPS = ((0, 1), (1, 1), (2, 1), (3, 2))
+DIRECT = 2
 PRELOADED = 2
 COST = 6 * 10**9
 BF16 = jnp.bfloat16
@@ -239,12 +241,12 @@
     near_first, near_rest = cross(1, first), cross(1, rest)
 
     def step(name, jobs, after=(), flops=COST):
-        args = [here(v) for level, j, own, other in jobs for v in (own, other, weights[level])]
+        args = [here(v) for level, _, _, own, other, _ in jobs for v in (own, other, weights[level])]
         described, sizes = [], []
-        for level, j, _, _ in jobs:
-            begin = begins[j] - widths[0] if level == 1 and j else 0
-            described.append((bits[level], parts[j], slice(begin, begin + widths[j])))
-            sizes.append(widths[j])
+        for level, j, many, _, _, begin in jobs:
+            part, size = spans(j, many)
+            described.append((bits[level], part, slice(begin, begin + size)))
+            sizes.append(size)
         return call(
             functools.partial(levels_kernel, described),
             name,
@@ -256,26 +258,43 @@
             flops,
         )
 
-    def job1(j):
-        return (1, j, rest, near_rest) if j else (1, j, first, near_first)
-
-    coeff2, near2, coeff3, near3 = {}, {}, {}, {}
-
-    def second(j, value):
-        coeff2[j] = value
-        near2[j] = cross(2, value)
+    def spans(j, many):
+        part, lane = [], 0
+        for at in range(j, j + many):
+            part += [(s, lane + start, lane + stop) for s, start, stop in parts[at]]
+            lane += widths[at]
+        return part, lane
+
+    def job1(group):
+        j, many = group
+        if j == 0:
+            return (1, j, many, first, near_first, 0)
+        return (1, j, many, rest, near_rest, begins[j] - widths[0])
+
+    def job2(j):
+        (start, many), own, other = next(
+            (group, own, other) for group, own, other in sent if group[0] <= j < sum(group)
+        )
+        return (2, j, 1, own, other, begins[j] - begins[start])
+
+    coeff3, near3 = {}, {}
+
+    sent = []
+
+    def second(group, value):
+        sent.append((group, value, cross(2, value)))
 
     def third(j, value):
         coeff3[j] = value
         near3[j] = cross(3, value)
 
-    (value,) = step("level1_0", [job1(0)])
-    second(0, value)
-    (value,) = step("level1_1", [job1(1)], [coeff2[0]])
-    second(1, value)
-    value, ahead = step("level2_0", [(2, 0, coeff2[0], near2[0]), job1(2)], [coeff2[1]])
+    (value,) = step("level1_0", [job1(GROUPS[0])])
+    second(GROUPS[0], value)
+    (value,) = step("level1_1", [job1(GROUPS[1])], [value])
+    second(GROUPS[1], value)
+    value, ahead = step("level2_0", [job2(0), job1(GROUPS[2])], [value])
     third(0, value)
-    second(2, ahead)
+    second(GROUPS[2], ahead)
     *more, basis_v = call(
         prefetch_kernel,
         "prefetch",
@@ -286,7 +305,7 @@
         [coeff3[0]],
     )
     weights += more
-    (value,) = step("level2_1", [(2, 1, coeff2[1], near2[1])], [basis_v])
+    (value,) = step("level2_1", [job2(1)], [basis_v])
     third(1, value)
 
     masks = [1 << b for b in range(n_blk.bit_length() - 1)]
@@ -302,7 +321,7 @@
         return in_vmem(count * rows, widths[j], dtype=dtype)
 
     def tail(j, after, direct, folding=None, totalling=None):
-        (coeff4,) = step(f"level3_{j}", [(3, j, coeff3[j], near3[j])], after, flops=0 if j == 1 else COST)
+        (coeff4,) = step(f"level3_{j}", [(3, j, 1, coeff3[j], near3[j], 0)], after)
         near4 = cross(4, coeff4)
         outs, extra = [in_vmem(rank, widths[j], dtype=F32)], []
         if folding is not None:
@@ -358,22 +377,31 @@
     def direct_sum(out):
         return [out[0]] + [partner(out[d], "blk", d) for d in range(n_blk - 1, 0, -1)]
 
-    out0, _ = tail(0, [coeff3[1]], False)
-    fold0 = begin_sum(0, out0)
-    value, ahead = step("level2_2", [(2, 2, coeff2[2], near2[2]), job1(3)], [out0[0]])
-    third(2, value)
-    second(3, ahead)
-    out1, (send0, keep0) = tail(1, [coeff3[2]], False, fold0)
-    got0 = partner(send0, "blk", halving(0)[0][-1])
-    fold1 = begin_sum(1, out1)
-    (value,) = step("level2_3", [(2, 3, coeff2[3], near2[3])], [out1[0]])
-    third(3, value)
-    out2, (send1, keep1, total0) = tail(2, [coeff3[3]], True, fold1, (0, keep0, got0))
-    got1 = partner(send1, "blk", halving(1)[0][-1])
-    group2 = direct_sum(out2)
-    out3, (total1,) = tail(3, [out2[0]], True, None, (1, keep1, got1))
-    group3 = direct_sum(out3)
-    groups = [[total0], [total1], group2, group3]
+    count = len(widths)
+    groups = {}
+    folding = totalling = out = None
+    for j in range(count):
+        after = [coeff3[j + 1]] if j + 1 < count else [out[0]]
+        out, more = tail(j, after, j >= count - DIRECT, folding, totalling)
+        if totalling is not None:
+            groups[totalling[0]] = [more.pop()]
+        totalling = None
+        if folding is not None:
+            at, (send, keep) = folding[0], more
+            totalling = (at, keep, partner(send, "blk", halving(at)[0][-1]))
+        folding = None
+        if j < count - DIRECT:
+            folding = begin_sum(j, out)
+        else:
+            groups[j] = direct_sum(out)
+        if j + 2 < count:
+            group = GROUPS[j + 3] if j + 3 < len(GROUPS) else None
+            jobs = [job2(j + 2)] + ([job1(group)] if group else [])
+            value, *ahead = step(f"level2_{j + 2}", jobs, [out[0]])
+            third(j + 2, value)
+            if group:
+                second(group, *ahead)
+    groups = [groups[j] for j in range(count)]
     flat = [here(v) for group in groups for v in group]
     return pl.pallas_call(
         functools.partial(end_kernel, places, [len(group) for group in groups]),

time: 76.5 us -> 76.3 us (level)
  waiting for transfers between devices: 33.5 us -> 29.7 us
  starting transfers between devices: 26.3 us -> 28.8 us
  Pallas kernels: 16.3 us -> 17.3 us
    ppermute x24 -> x28, waiting for transfers between devices: 33.5 us -> 29.7 us  [partner(): return lax.ppermute(value, axis, pairs)]
    ppermute x24 -> x28, starting transfers between devices: 26.3 us -> 28.8 us  [partner(): return lax.ppermute(value, axis, pairs)]
    pallas_call x20 -> x24, Pallas kernels: 15.4 us -> 16.4 us  [call(): pl.pallas_call(body, name=name, in_specs=[*in_specs, *[ANY] * len(after)]...]
  transfers between devices with their start and end apart: 24 -> 28, of which waited for: 9 -> 14; matrix products, arithmetic and copies ran while one was open for 0% -> 0% of each run, Pallas kernels for 15% -> 17%
where the time goes in v8:
time: 76.3 us; the launch traced here: 76.1 us
  waiting for transfers between devices  29.7 us (39%)
  starting transfers between devices  28.8 us (38%)
  Pallas kernels  17.3 us (23%)
    ppermute x28, waiting for transfers between devices, partner(): return lax.ppermute(value, axis, pairs)  29.7 us
    ppermute x28, starting transfers between devices, partner(): return lax.ppermute(value, axis, pairs)  28.8 us
    pallas_call x24, Pallas kernels, call(): pl.pallas_call(body, name=name, in_specs=[*in_specs, *[ANY] * len(after)]...  16.4 us
  transfers between devices with their start and end apart: 28, of which 14 were waited for; matrix products, arithmetic and copies ran while one was open for 0% of the time, Pallas kernels for 17%

profile of v8, /device:TPU:0, one launch (start us, length us, event | category | flops | bytes accessed | tf_op | source)
XLA Modules:
  0.0 76.1 jit_solution(2625999024959322168)
XLA Ops:
  0.0 3.7 %leaf.1 = (bf16[384,128]{1,0:T(8,128)(2,1)S(1)}, bf16[384,896]{1,0:T(8,128)(2,1)S(1)}, bf16[2,384,768]{2,1,0:T(8,128)(2,1)S(1)}, bf16[2,384,768]{2,1,0:T(8,128)(2,1)S(1)}) custom-call(bf16[2,1024,512]{2,1,0:T(8,128)(2,1)} %bitcast.9, bf16[2,384,1024]{2,1,0:T(8,128)(2,1)} %bitcast.10, bf16[5,2,384,768]{3,2,1,0:T(8,128)(2,1)} %bitcast.7, s32[2,5]{1,0:T(2,128)} %bitcast.12), custom_call_target="tpu_custom_call" | custom-call | flops 6000000000 | tf_op jit(solution)/shard_map/leaf/pallas_call | solution.py:43
  3.7 0.5 collective-permute-start.2
  4.3 1.8 %collective-permute-done.refs_1_ = bf16[384,128]{1,0:T(8,128)(2,1)S(1)} collective-permute-done((bf16[384,128]{1,0:T(8,128)(2,1)S(1)}, bf16[384,128]{1,0:T(8,128)(2,1)S(1)}, u32[]{:S(2)}, u32[]{:S(2)}) %collective-permute-start) | collective-permute-done | bytes 98336 | tf_op jit(solution)/shard_map/ppermute | solution.py:57
  6.1 0.3 level1_0.1.refs_3_.refs_0_
  6.4 3.0 %collective-permute-start.1 = (bf16[384,128]{1,0:T(8,128)(2,1)S(1)}, bf16[384,128]{1,0:T(8,128)(2,1)S(1)}, u32[]{:S(2)}, u32[]{:S(2)}) collective-permute-start(bf16[384,128]{1,0:T(8,128)(2,1)S(1)} %level1_0.1.refs_3_.refs_0_), channel_id=1, source_target_pairs={{0,2},{1,3},{2,0},{3,1},{4,6},{5,7},{6,4},{7,5},{8,10},{9,11},{10,... | collective-permute-start | bytes 294920 | tf_op jit(solution)/shard_map/ppermute | solution.py:57
  9.5 0.4 level1_1.1.refs_6_.refs_0_
  9.9 2.8 %collective-permute-done.1.refs_1_ = bf16[384,128]{1,0:T(8,128)(2,1)S(1)} collective-permute-done((bf16[384,128]{1,0:T(8,128)(2,1)S(1)}, bf16[384,128]{1,0:T(8,128)(2,1)S(1)}, u32[]{:S(2)}, u32[]{:S(2)}) %collective-permute-start.1) | collective-permute-done | bytes 98336 | tf_op jit(solution)/shard_map/ppermute | solution.py:57
  12.7 0.7 level2_0.1
  13.4 3.0 %collective-permute-start.4 = (bf16[384,128]{1,0:T(8,128)(2,1)S(1)}, bf16[384,128]{1,0:T(8,128)(2,1)S(1)}, u32[]{:S(2)}, u32[]{:S(2)}) collective-permute-start(bf16[384,128]{1,0:T(8,128)(2,1)S(1)} %get-tuple-element.48.refs_3_.refs_0_), channel_id=1, source_target_pairs={{0,4},{1,5},{2,6},{3,7},{4,0},{5,1},{6,2},{7,3},{8,12},{9,13},{10,... | collective-permute-start | bytes 294920 | tf_op jit(solution)/shard_map/ppermute | solution.py:57
  16.4 2.0 %collective-permute-start.3 = (bf16[384,256]{1,0:T(8,128)(2,1)S(1)}, bf16[384,256]{1,0:T(8,128)(2,1)S(1)}, u32[]{:S(2)}, u32[]{:S(2)}) collective-permute-start(bf16[384,256]{1,0:T(8,128)(2,1)S(1)} %get-tuple-element.47.refs_0_), channel_id=1, source_target_pairs={{0,2},{1,3},{2,0},{3,1},{4,6},{5,7},{6,4},{7,5},{8,10},{9,11},{10,... | collective-permute-start | bytes 589832 | tf_op jit(solution)/shard_map/ppermute | solution.py:57
  18.4 2.5 %prefetch.1 = (bf16[2,384,768]{2,1,0:T(8,128)(2,1)S(1)}, bf16[2,384,768]{2,1,0:T(8,128)(2,1)S(1)}, bf16[2,1024,384]{2,1,0:T(8,128)(2,1)S(1)}) custom-call(bf16[5,2,384,768]{3,2,1,0:T(8,128)(2,1)} %bitcast.8, bf16[2,1024,384]{2,1,0:T(8,128)(2,1)} %bitcast.11, s32[2,5]{1,0:T(2,128)} %bitcast.13, bf16[384,128]{1,0:T(8,128)(2,1)S(1)} %get-tuple-element.48.refs_3_.refs_0_), custom_call_target="tpu_custom_call" | custom-call | flops 6000000000 | tf_op jit(solution)/shard_map/prefetch/pallas_call | solution.py:43
  20.9 0.4 level2_1.1.refs_3_.refs_0_
  21.3 0.4 collective-permute-start.9
  21.7 0.3 level3_0.1.refs_0_
  22.3 1.0 %collective-permute-done.6.refs_1_ = bf16[384,128]{1,0:T(8,128)(2,1)S(1)} collective-permute-done((bf16[384,128]{1,0:T(8,128)(2,1)S(1)}, bf16[384,128]{1,0:T(8,128)(2,1)S(1)}, u32[]{:S(2)}, u32[]{:S(2)}) %collective-permute-start.6) | collective-permute-done | bytes 98336 | tf_op jit(solution)/shard_map/ppermute | solution.py:57
  23.4 0.6 last_0.1
  24.0 1.6 %collective-permute-start.10 = (bf16[512,128]{1,0:T(8,128)(2,1)S(1)}, bf16[512,128]{1,0:T(8,128)(2,1)S(1)}, u32[]{:S(2)}, u32[]{:S(2)}) collective-permute-start(bf16[512,128]{1,0:T(8,128)(2,1)S(1)} %get-tuple-element.55), channel_id=1, source_target_pairs={{0,16},{8,24},{16,0},{24,8},{1,17},{9,25},{17,1},{25,9},{2,18},{10... | collective-permute-start | bytes 393224 | tf_op jit(solution)/shard_map/ppermute | solution.py:57
  25.6 0.8 %level2_2.1 = (bf16[384,256]{1,0:T(8,128)(2,1)S(1)}, bf16[384,384]{1,0:T(8,128)(2,1)S(1)}) custom-call(bf16[384,256]{1,0:T(8,128)(2,1)S(1)} %get-tuple-element.47.refs_0_, bf16[384,256]{1,0:T(8,128)(2,1)S(1)} %collective-permute-done.3.refs_1_, bf16[2,384,768]{2,1,0:T(8,128)(2,1)S(1)} %get-tuple-element.45.refs_2_, ...), custom_call_target="tpu_custom_call" | custom-call | flops 6000000000 | tf_op jit(solution)/shard_map/level2_2/pallas_call | solution.py:43
  26.4 2.7 %collective-permute-start.7 = (bf16[384,256]{1,0:T(8,128)(2,1)S(1)}, bf16[384,256]{1,0:T(8,128)(2,1)S(1)}, u32[]{:S(2)}, u32[]{:S(2)}) collective-permute-start(bf16[384,256]{1,0:T(8,128)(2,1)S(1)} %get-tuple-element.53.refs_3_.refs_0_), channel_id=1, source_target_pairs={{0,4},{1,5},{2,6},{3,7},{4,0},{5,1},{6,2},{7,3},{8,12},{9,13},{10,... | collective-permute-start | bytes 589832 | tf_op jit(solution)/shard_map/ppermute | solution.py:57
  29.0 1.8 %collective-permute-start.8 = (bf16[384,384]{1,0:T(8,128)(2,1)S(1)}, bf16[384,384]{1,0:T(8,128)(2,1)S(1)}, u32[]{:S(2)}, u32[]{:S(2)}) collective-permute-start(bf16[384,384]{1,0:T(8,128)(2,1)S(1)} %get-tuple-element.54.refs_0_), channel_id=1, source_target_pairs={{0,2},{1,3},{2,0},{3,1},{4,6},{5,7},{6,4},{7,5},{8,10},{9,11},{10,... | collective-permute-start | bytes 884744 | tf_op jit(solution)/shard_map/ppermute | solution.py:57
  30.8 6.5 %collective-permute-done.9.refs_1_ = bf16[384,256]{1,0:T(8,128)(2,1)S(1)} collective-permute-done((bf16[384,256]{1,0:T(8,128)(2,1)S(1)}, bf16[384,256]{1,0:T(8,128)(2,1)S(1)}, u32[]{:S(2)}, u32[]{:S(2)}) %collective-permute-start.9) | collective-permute-done | bytes 196640 | tf_op jit(solution)/shard_map/ppermute | solution.py:57
  37.3 0.4 level3_1.1.refs_0_
  38.0 1.5 %collective-permute-start.13 = (bf16[256,128]{1,0:T(8,128)(2,1)S(1)}, bf16[256,128]{1,0:T(8,128)(2,1)S(1)}, u32[]{:S(2)}, u32[]{:S(2)}) collective-permute-start(bf16[256,128]{1,0:T(8,128)(2,1)S(1)} %get-tuple-element.60), channel_id=1, source_target_pairs={{0,8},{8,0},{16,24},{24,16},{1,9},{9,1},{17,25},{25,17},{2,10},{10... | collective-permute-start | bytes 196616 | tf_op jit(solution)/shard_map/ppermute | solution.py:57
  39.6 0.8 %last_1.1 = (f32[512,256]{1,0:T(8,128)S(1)}, bf16[512,256]{1,0:T(8,128)(2,1)S(1)}) custom-call(f32[384,256]{1,0:T(8,128)S(1)} %get-tuple-element.56.refs_0_, bf16[384,256]{1,0:T(8,128)(2,1)S(1)} %collective-permute-done.11.refs_1_, bf16[2,384,768]{2,1,0:T(8,128)(2,1)S(1)} %get-tuple-element.51.refs_1_.refs_2_, ...), custom_call_target="tpu_custom_call" | custom-call | flops 6000000000 | tf_op jit(solution)/shard_map/last_1/pallas_call | solution.py:43
  40.4 1.2 %collective-permute-start.12 = (bf16[512,256]{1,0:T(8,128)(2,1)S(1)}, bf16[512,256]{1,0:T(8,128)(2,1)S(1)}, u32[]{:S(2)}, u32[]{:S(2)}) collective-permute-start(bf16[512,256]{1,0:T(8,128)(2,1)S(1)} %get-tuple-element.58), channel_id=1, source_target_pairs={{0,8},{8,0},{16,24},{24,16},{1,9},{9,1},{17,25},{25,17},{2,10},{10... | collective-permute-start | bytes 786440 | tf_op jit(solution)/shard_map/ppermute | solution.py:57
  41.5 0.5 collective-permute-done.8.refs_1_
  42.1 0.4 level2_3.1.refs_3_.refs_0_
  42.6 0.5 level3_2.1.refs_0_
  43.2 5.7 %collective-permute-done.12.refs_3_ = bf16[512,256]{1,0:T(8,128)(2,1)S(1)} collective-permute-done((bf16[512,256]{1,0:T(8,128)(2,1)S(1)}, bf16[512,256]{1,0:T(8,128)(2,1)S(1)}, u32[]{:S(2)}, u32[]{:S(2)}) %collective-permute-start.12) | collective-permute-done | bytes 262176 | tf_op jit(solution)/shard_map/ppermute | solution.py:57
  49.2 1.9 %collective-permute-start.17 = (bf16[256,256]{1,0:T(8,128)(2,1)S(1)}, bf16[256,256]{1,0:T(8,128)(2,1)S(1)}, u32[]{:S(2)}, u32[]{:S(2)}) collective-permute-start(bf16[256,256]{1,0:T(8,128)(2,1)S(1)} %get-tuple-element.66), channel_id=1, source_target_pairs={{0,16},{8,24},{16,0},{24,8},{1,17},{9,25},{17,1},{25,9},{2,18},{10... | collective-permute-start | bytes 393224 | tf_op jit(solution)/shard_map/ppermute | solution.py:57
  51.1 1.0 %last_2.1 = (f32[512,256]{1,0:T(8,128)S(1)}, bf16[512,256]{1,0:T(8,128)(2,1)S(1)}) custom-call(f32[384,256]{1,0:T(8,128)S(1)} %get-tuple-element.62.refs_0_, bf16[384,256]{1,0:T(8,128)(2,1)S(1)} %collective-permute-done.15.refs_1_, bf16[2,384,768]{2,1,0:T(8,128)(2,1)S(1)} %get-tuple-element.51.refs_1_.refs_2_, ...), custom_call_target="tpu_custom_call" | custom-call | flops 6000000000 | tf_op jit(solution)/shard_map/last_2/pallas_call | solution.py:43
  52.1 0.4 level2_4.1.refs_3_.refs_0_
  52.8 2.2 %collective-permute-done.14.refs_1_ = bf16[384,256]{1,0:T(8,128)(2,1)S(1)} collective-permute-done((bf16[384,256]{1,0:T(8,128)(2,1)S(1)}, bf16[384,256]{1,0:T(8,128)(2,1)S(1)}, u32[]{:S(2)}, u32[]{:S(2)}) %collective-permute-start.14) | collective-permute-done | bytes 196640 | tf_op jit(solution)/shard_map/ppermute | solution.py:57
  55.0 0.4 level3_3.1.refs_0_
  55.5 4.5 %collective-permute-done.16.refs_3_ = bf16[512,256]{1,0:T(8,128)(2,1)S(1)} collective-permute-done((bf16[512,256]{1,0:T(8,128)(2,1)S(1)}, bf16[512,256]{1,0:T(8,128)(2,1)S(1)}, u32[]{:S(2)}, u32[]{:S(2)}) %collective-permute-start.16) | collective-permute-done | bytes 262176 | tf_op jit(solution)/shard_map/ppermute | solution.py:57
  60.2 1.0 %collective-permute-start.20 = (bf16[256,256]{1,0:T(8,128)(2,1)S(1)}, bf16[256,256]{1,0:T(8,128)(2,1)S(1)}, u32[]{:S(2)}, u32[]{:S(2)}) collective-permute-start(bf16[256,256]{1,0:T(8,128)(2,1)S(1)} %get-tuple-element.71), channel_id=1, source_target_pairs={{0,8},{8,0},{16,24},{24,16},{1,9},{9,1},{17,25},{25,17},{2,10},{10... | collective-permute-start | bytes 393224 | tf_op jit(solution)/shard_map/ppermute | solution.py:57
  61.3 0.8 %last_3.1 = (f32[256,256]{1,0:T(8,128)S(1)}, bf16[256,256]{1,0:T(8,128)(2,1)S(1)}, bf16[256,256]{1,0:T(8,128)(2,1)S(1)}, bf16[256,256]{1,0:T(8,128)(2,1)S(1)}) custom-call(f32[384,256]{1,0:T(8,128)S(1)} %get-tuple-element.68.refs_0_, bf16[384,256]{1,0:T(8,128)(2,1)S(1)} %collective-permute-done.19.refs_1_, ...), custom_call_target="tpu_custom_call" | custom-call | flops 6000000000 | tf_op jit(solution)/shard_map/last_3/pallas_call | solution.py:43
  62.1 0.3 level3_4.1.refs_0_
  62.5 2.3 %collective-permute-start.21 = (bf16[256,256]{1,0:T(8,128)(2,1)S(1)}, bf16[256,256]{1,0:T(8,128)(2,1)S(1)}, u32[]{:S(2)}, u32[]{:S(2)}) collective-permute-start(bf16[256,256]{1,0:T(8,128)(2,1)S(1)} %get-tuple-element.73), channel_id=1, source_target_pairs={{0,24},{8,16},{16,8},{24,0},{1,25},{9,17},{17,9},{25,1},{2,26},{10... | collective-permute-start | bytes 393224 | tf_op jit(solution)/shard_map/ppermute | solution.py:57
  64.8 0.3 collective-permute-start.22
  65.1 0.9 %collective-permute-start.23 = (bf16[256,256]{1,0:T(8,128)(2,1)S(1)}, bf16[256,256]{1,0:T(8,128)(2,1)S(1)}, u32[]{:S(2)}, u32[]{:S(2)}) collective-permute-start(bf16[256,256]{1,0:T(8,128)(2,1)S(1)} %get-tuple-element.75), channel_id=1, source_target_pairs={{0,8},{8,0},{16,24},{24,16},{1,9},{9,1},{17,25},{25,17},{2,10},{10... | collective-permute-start | bytes 393224 | tf_op jit(solution)/shard_map/ppermute | solution.py:57
  66.3 0.6 last_4.1
  66.9 2.3 %collective-permute-start.25 = (bf16[256,128]{1,0:T(8,128)(2,1)S(1)}, bf16[256,128]{1,0:T(8,128)(2,1)S(1)}, u32[]{:S(2)}, u32[]{:S(2)}) collective-permute-start(bf16[256,128]{1,0:T(8,128)(2,1)S(1)} %get-tuple-element.78), channel_id=1, source_target_pairs={{0,24},{8,16},{16,8},{24,0},{1,25},{9,17},{17,9},{25,1},{2,26},{10... | collective-permute-start | bytes 196616 | tf_op jit(solution)/shard_map/ppermute | solution.py:57
  69.8 1.1 %collective-permute-start.27 = (bf16[256,128]{1,0:T(8,128)(2,1)S(1)}, bf16[256,128]{1,0:T(8,128)(2,1)S(1)}, u32[]{:S(2)}, u32[]{:S(2)}) collective-permute-start(bf16[256,128]{1,0:T(8,128)(2,1)S(1)} %get-tuple-element.80), channel_id=1, source_target_pairs={{0,8},{8,0},{16,24},{24,16},{1,9},{9,1},{17,25},{25,17},{2,10},{10... | collective-permute-start | bytes 196616 | tf_op jit(solution)/shard_map/ppermute | solution.py:57
  70.9 1.9 %collective-permute-done.22.refs_5_ = bf16[256,256]{1,0:T(8,128)(2,1)S(1)} collective-permute-done((bf16[256,256]{1,0:T(8,128)(2,1)S(1)}, bf16[256,256]{1,0:T(8,128)(2,1)S(1)}, u32[]{:S(2)}, u32[]{:S(2)}) %collective-permute-start.22) | collective-permute-done | bytes 131104 | tf_op jit(solution)/shard_map/ppermute | solution.py:57
  72.9 1.2 %collective-permute-done.25.refs_8_ = bf16[256,128]{1,0:T(8,128)(2,1)S(1)} collective-permute-done((bf16[256,128]{1,0:T(8,128)(2,1)S(1)}, bf16[256,128]{1,0:T(8,128)(2,1)S(1)}, u32[]{:S(2)}, u32[]{:S(2)}) %collective-permute-start.25) | collective-permute-done | bytes 65568 | tf_op jit(solution)/shard_map/ppermute | solution.py:57
  74.1 0.8 %collective-permute-done.26.refs_9_ = bf16[256,128]{1,0:T(8,128)(2,1)S(1)} collective-permute-done((bf16[256,128]{1,0:T(8,128)(2,1)S(1)}, bf16[256,128]{1,0:T(8,128)(2,1)S(1)}, u32[]{:S(2)}, u32[]{:S(2)}) %collective-permute-start.26) | collective-permute-done | bytes 65568 | tf_op jit(solution)/shard_map/ppermute | solution.py:57
  75.2 0.9 %end.1 = bf16[2,256,512]{2,1,0:T(8,128)(2,1)} custom-call(bf16[256,128]{1,0:T(8,128)(2,1)S(1)} %get-tuple-element.61.refs_0_, bf16[256,256]{1,0:T(8,128)(2,1)S(1)} %get-tuple-element.67.refs_1_, bf16[256,256]{1,0:T(8,128)(2,1)S(1)} %get-tuple-element.72.refs_2_, f32[256,256]{1,0:T(8,128)S(1)} %get-tuple-element.69.refs_3_, ...), custom_call_target="tpu_custom_call" | custom-call | tf_op jit(solution)/shard_map/end/pallas_call | solution.py:406
  (33 shorter events, 3.3 us)
Async XLA Ops:
  3.7 5.8 %collective-permute-start.2 = (bf16[384,896]{1,0:T(8,128)(2,1)S(1)}, bf16[384,896]{1,0:T(8,128)(2,1)S(1)}, u32[]{:S(2)}, u32[]{:S(2)}) collective-permute-start(bf16[384,896]{1,0:T(8,128)(2,1)S(1)} %get-tuple-element.46.refs_0_.refs_3_), channel_id=1, source_target_pairs={{0,1},{1,0},{2,3},{3,2},{4,5},{5,4},{6,7},{7,6},{8,9},{9,8},{10,11... | collective-permute-start | bytes 2064392 | tf_op jit(solution)/shard_map/ppermute | solution.py:57
  4.2 1.9 %collective-permute-start = (bf16[384,128]{1,0:T(8,128)(2,1)S(1)}, bf16[384,128]{1,0:T(8,128)(2,1)S(1)}, u32[]{:S(2)}, u32[]{:S(2)}) collective-permute-start(bf16[384,128]{1,0:T(8,128)(2,1)S(1)} %get-tuple-element.43.refs_0_), channel_id=1, source_target_pairs={{0,1},{1,0},{2,3},{3,2},{4,5},{5,4},{6,7},{7,6},{8,9},{9,8},{10,11... | collective-permute-start | bytes 294920 | tf_op jit(solution)/shard_map/ppermute | solution.py:57
  6.4 6.3 %collective-permute-start.1 = (bf16[384,128]{1,0:T(8,128)(2,1)S(1)}, bf16[384,128]{1,0:T(8,128)(2,1)S(1)}, u32[]{:S(2)}, u32[]{:S(2)}) collective-permute-start(bf16[384,128]{1,0:T(8,128)(2,1)S(1)} %level1_0.1.refs_3_.refs_0_), channel_id=1, source_target_pairs={{0,2},{1,3},{2,0},{3,1},{4,6},{5,7},{6,4},{7,5},{8,10},{9,11},{10,... | collective-permute-start | bytes 294920 | tf_op jit(solution)/shard_map/ppermute | solution.py:57
  9.8 11.1 %collective-permute-start.5 = (bf16[384,256]{1,0:T(8,128)(2,1)S(1)}, bf16[384,256]{1,0:T(8,128)(2,1)S(1)}, u32[]{:S(2)}, u32[]{:S(2)}) collective-permute-start(bf16[384,256]{1,0:T(8,128)(2,1)S(1)} %level1_1.1.refs_6_.refs_0_), channel_id=1, source_target_pairs={{0,2},{1,3},{2,0},{3,1},{4,6},{5,7},{6,4},{7,5},{8,10},{9,11},{10,... | collective-permute-start | bytes 589832 | tf_op jit(solution)/shard_map/ppermute | solution.py:57
  13.4 8.3 %collective-permute-start.4 = (bf16[384,128]{1,0:T(8,128)(2,1)S(1)}, bf16[384,128]{1,0:T(8,128)(2,1)S(1)}, u32[]{:S(2)}, u32[]{:S(2)}) collective-permute-start(bf16[384,128]{1,0:T(8,128)(2,1)S(1)} %get-tuple-element.48.refs_3_.refs_0_), channel_id=1, source_target_pairs={{0,4},{1,5},{2,6},{3,7},{4,0},{5,1},{6,2},{7,3},{8,12},{9,13},{10,... | collective-permute-start | bytes 294920 | tf_op jit(solution)/shard_map/ppermute | solution.py:57
  16.4 9.1 %collective-permute-start.3 = (bf16[384,256]{1,0:T(8,128)(2,1)S(1)}, bf16[384,256]{1,0:T(8,128)(2,1)S(1)}, u32[]{:S(2)}, u32[]{:S(2)}) collective-permute-start(bf16[384,256]{1,0:T(8,128)(2,1)S(1)} %get-tuple-element.47.refs_0_), channel_id=1, source_target_pairs={{0,2},{1,3},{2,0},{3,1},{4,6},{5,7},{6,4},{7,5},{8,10},{9,11},{10,... | collective-permute-start | bytes 589832 | tf_op jit(solution)/shard_map/ppermute | solution.py:57
  21.3 16.0 %collective-permute-start.9 = (bf16[384,256]{1,0:T(8,128)(2,1)S(1)}, bf16[384,256]{1,0:T(8,128)(2,1)S(1)}, u32[]{:S(2)}, u32[]{:S(2)}) collective-permute-start(bf16[384,256]{1,0:T(8,128)(2,1)S(1)} %level2_1.1.refs_3_.refs_0_), channel_id=1, source_target_pairs={{0,4},{1,5},{2,6},{3,7},{4,0},{5,1},{6,2},{7,3},{8,12},{9,13},{10,... | collective-permute-start | bytes 589832 | tf_op jit(solution)/shard_map/ppermute | solution.py:57
  22.0 1.4 %collective-permute-start.6 = (bf16[384,128]{1,0:T(8,128)(2,1)S(1)}, bf16[384,128]{1,0:T(8,128)(2,1)S(1)}, u32[]{:S(2)}, u32[]{:S(2)}) collective-permute-start(bf16[384,128]{1,0:T(8,128)(2,1)S(1)} %level3_0.1.refs_0_), channel_id=1, source_target_pairs={{0,1},{1,0},{2,3},{3,2},{4,5},{5,4},{6,7},{7,6},{8,9},{9,8},{10,11... | collective-permute-start | bytes 294920 | tf_op jit(solution)/shard_map/ppermute | solution.py:57
  24.0 13.8 %collective-permute-start.10 = (bf16[512,128]{1,0:T(8,128)(2,1)S(1)}, bf16[512,128]{1,0:T(8,128)(2,1)S(1)}, u32[]{:S(2)}, u32[]{:S(2)}) collective-permute-start(bf16[512,128]{1,0:T(8,128)(2,1)S(1)} %get-tuple-element.55), channel_id=1, source_target_pairs={{0,16},{8,24},{16,0},{24,8},{1,17},{9,25},{17,1},{25,9},{2,18},{10... | collective-permute-start | bytes 393224 | tf_op jit(solution)/shard_map/ppermute | solution.py:57
  26.4 16.2 %collective-permute-start.7 = (bf16[384,256]{1,0:T(8,128)(2,1)S(1)}, bf16[384,256]{1,0:T(8,128)(2,1)S(1)}, u32[]{:S(2)}, u32[]{:S(2)}) collective-permute-start(bf16[384,256]{1,0:T(8,128)(2,1)S(1)} %get-tuple-element.53.refs_3_.refs_0_), channel_id=1, source_target_pairs={{0,4},{1,5},{2,6},{3,7},{4,0},{5,1},{6,2},{7,3},{8,12},{9,13},{10,... | collective-permute-start | bytes 589832 | tf_op jit(solution)/shard_map/ppermute | solution.py:57
  29.0 13.0 %collective-permute-start.8 = (bf16[384,384]{1,0:T(8,128)(2,1)S(1)}, bf16[384,384]{1,0:T(8,128)(2,1)S(1)}, u32[]{:S(2)}, u32[]{:S(2)}) collective-permute-start(bf16[384,384]{1,0:T(8,128)(2,1)S(1)} %get-tuple-element.54.refs_0_), channel_id=1, source_target_pairs={{0,2},{1,3},{2,0},{3,1},{4,6},{5,7},{6,4},{7,5},{8,10},{9,11},{10,... | collective-permute-start | bytes 884744 | tf_op jit(solution)/shard_map/ppermute | solution.py:57
  37.7 1.9 %collective-permute-start.11 = (bf16[384,256]{1,0:T(8,128)(2,1)S(1)}, bf16[384,256]{1,0:T(8,128)(2,1)S(1)}, u32[]{:S(2)}, u32[]{:S(2)}) collective-permute-start(bf16[384,256]{1,0:T(8,128)(2,1)S(1)} %level3_1.1.refs_0_), channel_id=1, source_target_pairs={{0,1},{1,0},{2,3},{3,2},{4,5},{5,4},{6,7},{7,6},{8,9},{9,8},{10,11... | collective-permute-start | bytes 589832 | tf_op jit(solution)/shard_map/ppermute | solution.py:57
  38.0 5.2 %collective-permute-start.13 = (bf16[256,128]{1,0:T(8,128)(2,1)S(1)}, bf16[256,128]{1,0:T(8,128)(2,1)S(1)}, u32[]{:S(2)}, u32[]{:S(2)}) collective-permute-start(bf16[256,128]{1,0:T(8,128)(2,1)S(1)} %get-tuple-element.60), channel_id=1, source_target_pairs={{0,8},{8,0},{16,24},{24,16},{1,9},{9,1},{17,25},{25,17},{2,10},{10... | collective-permute-start | bytes 196616 | tf_op jit(solution)/shard_map/ppermute | solution.py:57
  40.4 8.5 %collective-permute-start.12 = (bf16[512,256]{1,0:T(8,128)(2,1)S(1)}, bf16[512,256]{1,0:T(8,128)(2,1)S(1)}, u32[]{:S(2)}, u32[]{:S(2)}) collective-permute-start(bf16[512,256]{1,0:T(8,128)(2,1)S(1)} %get-tuple-element.58), channel_id=1, source_target_pairs={{0,8},{8,0},{16,24},{24,16},{1,9},{9,1},{17,25},{25,17},{2,10},{10... | collective-permute-start | bytes 786440 | tf_op jit(solution)/shard_map/ppermute | solution.py:57
  42.4 12.6 %collective-permute-start.14 = (bf16[384,256]{1,0:T(8,128)(2,1)S(1)}, bf16[384,256]{1,0:T(8,128)(2,1)S(1)}, u32[]{:S(2)}, u32[]{:S(2)}) collective-permute-start(bf16[384,256]{1,0:T(8,128)(2,1)S(1)} %level2_3.1.refs_3_.refs_0_), channel_id=1, source_target_pairs={{0,4},{1,5},{2,6},{3,7},{4,0},{5,1},{6,2},{7,3},{8,12},{9,13},{10,... | collective-permute-start | bytes 589832 | tf_op jit(solution)/shard_map/ppermute | solution.py:57
  43.1 8.0 %collective-permute-start.15 = (bf16[384,256]{1,0:T(8,128)(2,1)S(1)}, bf16[384,256]{1,0:T(8,128)(2,1)S(1)}, u32[]{:S(2)}, u32[]{:S(2)}) collective-permute-start(bf16[384,256]{1,0:T(8,128)(2,1)S(1)} %level3_2.1.refs_0_), channel_id=1, source_target_pairs={{0,1},{1,0},{2,3},{3,2},{4,5},{5,4},{6,7},{7,6},{8,9},{9,8},{10,11... | collective-permute-start | bytes 589832 | tf_op jit(solution)/shard_map/ppermute | solution.py:57
  49.2 6.3 %collective-permute-start.17 = (bf16[256,256]{1,0:T(8,128)(2,1)S(1)}, bf16[256,256]{1,0:T(8,128)(2,1)S(1)}, u32[]{:S(2)}, u32[]{:S(2)}) collective-permute-start(bf16[256,256]{1,0:T(8,128)(2,1)S(1)} %get-tuple-element.66), channel_id=1, source_target_pairs={{0,16},{8,24},{16,0},{24,8},{1,17},{9,25},{17,1},{25,9},{2,18},{10... | collective-permute-start | bytes 393224 | tf_op jit(solution)/shard_map/ppermute | solution.py:57
  52.5 9.6 %collective-permute-start.18 = (bf16[384,128]{1,0:T(8,128)(2,1)S(1)}, bf16[384,128]{1,0:T(8,128)(2,1)S(1)}, u32[]{:S(2)}, u32[]{:S(2)}) collective-permute-start(bf16[384,128]{1,0:T(8,128)(2,1)S(1)} %level2_4.1.refs_3_.refs_0_), channel_id=1, source_target_pairs={{0,4},{1,5},{2,6},{3,7},{4,0},{5,1},{6,2},{7,3},{8,12},{9,13},{10,... | collective-permute-start | bytes 294920 | tf_op jit(solution)/shard_map/ppermute | solution.py:57
  52.6 7.4 %collective-permute-start.16 = (bf16[512,256]{1,0:T(8,128)(2,1)S(1)}, bf16[512,256]{1,0:T(8,128)(2,1)S(1)}, u32[]{:S(2)}, u32[]{:S(2)}) collective-permute-start(bf16[512,256]{1,0:T(8,128)(2,1)S(1)} %get-tuple-element.64), channel_id=1, source_target_pairs={{0,16},{8,24},{16,0},{24,8},{1,17},{9,25},{17,1},{25,9},{2,18},{10... | collective-permute-start | bytes 786440 | tf_op jit(solution)/shard_map/ppermute | solution.py:57
  55.4 5.9 %collective-permute-start.19 = (bf16[384,256]{1,0:T(8,128)(2,1)S(1)}, bf16[384,256]{1,0:T(8,128)(2,1)S(1)}, u32[]{:S(2)}, u32[]{:S(2)}) collective-permute-start(bf16[384,256]{1,0:T(8,128)(2,1)S(1)} %level3_3.1.refs_0_), channel_id=1, source_target_pairs={{0,1},{1,0},{2,3},{3,2},{4,5},{5,4},{6,7},{7,6},{8,9},{9,8},{10,11... | collective-permute-start | bytes 589832 | tf_op jit(solution)/shard_map/ppermute | solution.py:57
  60.2 5.8 %collective-permute-start.20 = (bf16[256,256]{1,0:T(8,128)(2,1)S(1)}, bf16[256,256]{1,0:T(8,128)(2,1)S(1)}, u32[]{:S(2)}, u32[]{:S(2)}) collective-permute-start(bf16[256,256]{1,0:T(8,128)(2,1)S(1)} %get-tuple-element.71), channel_id=1, source_target_pairs={{0,8},{8,0},{16,24},{24,16},{1,9},{9,1},{17,25},{25,17},{2,10},{10... | collective-permute-start | bytes 393224 | tf_op jit(solution)/shard_map/ppermute | solution.py:57
  62.4 3.9 %collective-permute-start.24 = (bf16[384,128]{1,0:T(8,128)(2,1)S(1)}, bf16[384,128]{1,0:T(8,128)(2,1)S(1)}, u32[]{:S(2)}, u32[]{:S(2)}) collective-permute-start(bf16[384,128]{1,0:T(8,128)(2,1)S(1)} %level3_4.1.refs_0_), channel_id=1, source_target_pairs={{0,1},{1,0},{2,3},{3,2},{4,5},{5,4},{6,7},{7,6},{8,9},{9,8},{10,11... | collective-permute-start | bytes 294920 | tf_op jit(solution)/shard_map/ppermute | solution.py:57
  62.5 7.3 %collective-permute-start.21 = (bf16[256,256]{1,0:T(8,128)(2,1)S(1)}, bf16[256,256]{1,0:T(8,128)(2,1)S(1)}, u32[]{:S(2)}, u32[]{:S(2)}) collective-permute-start(bf16[256,256]{1,0:T(8,128)(2,1)S(1)} %get-tuple-element.73), channel_id=1, source_target_pairs={{0,24},{8,16},{16,8},{24,0},{1,25},{9,17},{17,9},{25,1},{2,26},{10... | collective-permute-start | bytes 393224 | tf_op jit(solution)/shard_map/ppermute | solution.py:57
  64.8 8.0 %collective-permute-start.22 = (bf16[256,256]{1,0:T(8,128)(2,1)S(1)}, bf16[256,256]{1,0:T(8,128)(2,1)S(1)}, u32[]{:S(2)}, u32[]{:S(2)}) collective-permute-start(bf16[256,256]{1,0:T(8,128)(2,1)S(1)} %get-tuple-element.74), channel_id=1, source_target_pairs={{0,16},{8,24},{16,0},{24,8},{1,17},{9,25},{17,1},{25,9},{2,18},{10... | collective-permute-start | bytes 393224 | tf_op jit(solution)/shard_map/ppermute | solution.py:57
  65.1 7.7 %collective-permute-start.23 = (bf16[256,256]{1,0:T(8,128)(2,1)S(1)}, bf16[256,256]{1,0:T(8,128)(2,1)S(1)}, u32[]{:S(2)}, u32[]{:S(2)}) collective-permute-start(bf16[256,256]{1,0:T(8,128)(2,1)S(1)} %get-tuple-element.75), channel_id=1, source_target_pairs={{0,8},{8,0},{16,24},{24,16},{1,9},{9,1},{17,25},{25,17},{2,10},{10... | collective-permute-start | bytes 393224 | tf_op jit(solution)/shard_map/ppermute | solution.py:57
  66.9 7.2 %collective-permute-start.25 = (bf16[256,128]{1,0:T(8,128)(2,1)S(1)}, bf16[256,128]{1,0:T(8,128)(2,1)S(1)}, u32[]{:S(2)}, u32[]{:S(2)}) collective-permute-start(bf16[256,128]{1,0:T(8,128)(2,1)S(1)} %get-tuple-element.78), channel_id=1, source_target_pairs={{0,24},{8,16},{16,8},{24,0},{1,25},{9,17},{17,9},{25,1},{2,26},{10... | collective-permute-start | bytes 196616 | tf_op jit(solution)/shard_map/ppermute | solution.py:57
  69.2 5.7 %collective-permute-start.26 = (bf16[256,128]{1,0:T(8,128)(2,1)S(1)}, bf16[256,128]{1,0:T(8,128)(2,1)S(1)}, u32[]{:S(2)}, u32[]{:S(2)}) collective-permute-start(bf16[256,128]{1,0:T(8,128)(2,1)S(1)} %get-tuple-element.79), channel_id=1, source_target_pairs={{0,16},{8,24},{16,0},{24,8},{1,17},{9,25},{17,1},{25,9},{2,18},{10... | collective-permute-start | bytes 196616 | tf_op jit(solution)/shard_map/ppermute | solution.py:57
  69.8 5.4 %collective-permute-start.27 = (bf16[256,128]{1,0:T(8,128)(2,1)S(1)}, bf16[256,128]{1,0:T(8,128)(2,1)S(1)}, u32[]{:S(2)}, u32[]{:S(2)}) collective-permute-start(bf16[256,128]{1,0:T(8,128)(2,1)S(1)} %get-tuple-element.80), channel_id=1, source_target_pairs={{0,8},{8,0},{16,24},{24,16},{1,9},{9,1},{17,25},{25,17},{2,10},{10... | collective-permute-start | bytes 196616 | tf_op jit(solution)/shard_map/ppermute | solution.py:57

commit v9 on v6

--- a/solution.py
+++ b/solution.py
@@ -176,6 +176,10 @@
     send[...] = (keep[rows:] + got[rows:].astype(F32)).astype(BF16)
 
 
+def sum_kernel(keep, got, total):
+    total[...] = (keep[...] + got[...].astype(F32)).astype(BF16)
+
+
 def end_kernel(places, counts, *refs):
     refs = list(refs)
     out = refs[-1]
@@ -366,9 +370,22 @@
     out1, (send0, keep0) = tail(1, [coeff3[2]], False, fold0)
     got0 = partner(send0, "blk", halving(0)[0][-1])
     fold1 = begin_sum(1, out1)
-    (value,) = step("level2_3", [(2, 3, coeff2[3], near2[3])], [out1[0]])
+    (total0,) = call(
+        sum_kernel, "sum_0", [VMEM] * 2, [result(0, 1, BF16)], [], [here(keep0), here(got0)], [out1[0]]
+    )
+    at, keep, got, count = fold1
+    send1, keep1 = call(
+        fold_kernel,
+        "fold_1",
+        [VMEM] * 2,
+        [result(1, count // 2, BF16), result(1, count // 2, F32)],
+        [],
+        [here(keep), here(got)],
+        [total0],
+    )
+    (value,) = step("level2_3", [(2, 3, coeff2[3], near2[3])], [keep1])
     third(3, value)
-    out2, (send1, keep1, total0) = tail(2, [coeff3[3]], True, fold1, (0, keep0, got0))
+    out2, _ = tail(2, [coeff3[3]], True, None, None)
     got1 = partner(send1, "blk", halving(1)[0][-1])
     group2 = direct_sum(out2)
     out3, (total1,) = tail(3, [out2[0]], True, None, (1, keep1, got1))

time: 75.2 us -> 71 us (0.944)
  waiting for transfers between devices: 30.9 us -> 27.8 us
  starting transfers between devices: 27.9 us -> 26.8 us
    ppermute x24, waiting for transfers between devices: 30.9 us -> 27.8 us  [partner(): return lax.ppermute(value, axis, pairs)]
    ppermute x24, starting transfers between devices: 27.9 us -> 26.8 us  [partner(): return lax.ppermute(value, axis, pairs)]
    pallas_call x20 -> x22, Pallas kernels: 15 us -> 15 us  [call(): pl.pallas_call(body, name=name, in_specs=[*in_specs, *[ANY] * len(after)]...]
  transfers between devices with their start and end apart: 24 -> 24, of which waited for: 10 -> 11; matrix products, arithmetic and copies ran while one was open for 0% -> 0% of each run, Pallas kernels for 15% -> 16%
where the time goes in v9:
time: 71 us; the launch traced here: 70.8 us
  waiting for transfers between devices  27.8 us (39%)
  starting transfers between devices  26.8 us (38%)
  Pallas kernels  16 us (23%)
    ppermute x24, waiting for transfers between devices, partner(): return lax.ppermute(value, axis, pairs)  27.8 us
    ppermute x24, starting transfers between devices, partner(): return lax.ppermute(value, axis, pairs)  26.8 us
    pallas_call x22, Pallas kernels, call(): pl.pallas_call(body, name=name, in_specs=[*in_specs, *[ANY] * len(after)]...  15 us
  transfers between devices with their start and end apart: 24, of which 11 were waited for; matrix products, arithmetic and copies ran while one was open for 0% of the time, Pallas kernels for 16%

profile of v9, /device:TPU:0, one launch (start us, length us, event | category | flops | bytes accessed | tf_op | source)
XLA Modules:
  0.0 70.8 jit_solution(12781312510746663379)
XLA Ops:
  0.0 3.7 %leaf.1 = (bf16[384,128]{1,0:T(8,128)(2,1)S(1)}, bf16[384,896]{1,0:T(8,128)(2,1)S(1)}, bf16[2,384,768]{2,1,0:T(8,128)(2,1)S(1)}, bf16[2,384,768]{2,1,0:T(8,128)(2,1)S(1)}) custom-call(bf16[2,1024,512]{2,1,0:T(8,128)(2,1)} %bitcast.9, bf16[2,384,1024]{2,1,0:T(8,128)(2,1)} %bitcast.10, bf16[5,2,384,768]{3,2,1,0:T(8,128)(2,1)} %bitcast.7, s32[2,5]{1,0:T(2,128)} %bitcast.12), custom_call_target="tpu_custom_call" | custom-call | flops 6000000000 | tf_op jit(solution)/shard_map/leaf/pallas_call | solution.py:41
  3.7 0.5 collective-permute-start
  4.3 1.8 %collective-permute-done.1.refs_1_ = bf16[384,128]{1,0:T(8,128)(2,1)S(1)} collective-permute-done((bf16[384,128]{1,0:T(8,128)(2,1)S(1)}, bf16[384,128]{1,0:T(8,128)(2,1)S(1)}, u32[]{:S(2)}, u32[]{:S(2)}) %collective-permute-start.1) | collective-permute-done | bytes 98336 | tf_op jit(solution)/shard_map/ppermute | solution.py:55
  6.1 0.3 level1_0.1.refs_3_.refs_0_
  6.4 3.0 %collective-permute-start.3 = (bf16[384,128]{1,0:T(8,128)(2,1)S(1)}, bf16[384,128]{1,0:T(8,128)(2,1)S(1)}, u32[]{:S(2)}, u32[]{:S(2)}) collective-permute-start(bf16[384,128]{1,0:T(8,128)(2,1)S(1)} %level1_0.1.refs_3_.refs_0_), channel_id=1, source_target_pairs={{0,2},{1,3},{2,0},{3,1},{4,6},{5,7},{6,4},{7,5},{8,10},{9,11},{10,... | collective-permute-start | bytes 294920 | tf_op jit(solution)/shard_map/ppermute | solution.py:55
  9.5 0.4 level1_1.1.refs_6_.refs_0_
  9.9 2.8 %collective-permute-done.3.refs_1_ = bf16[384,128]{1,0:T(8,128)(2,1)S(1)} collective-permute-done((bf16[384,128]{1,0:T(8,128)(2,1)S(1)}, bf16[384,128]{1,0:T(8,128)(2,1)S(1)}, u32[]{:S(2)}, u32[]{:S(2)}) %collective-permute-start.3) | collective-permute-done | bytes 98336 | tf_op jit(solution)/shard_map/ppermute | solution.py:55
  12.7 0.7 level2_0.1
  13.4 3.0 %collective-permute-start.6 = (bf16[384,128]{1,0:T(8,128)(2,1)S(1)}, bf16[384,128]{1,0:T(8,128)(2,1)S(1)}, u32[]{:S(2)}, u32[]{:S(2)}) collective-permute-start(bf16[384,128]{1,0:T(8,128)(2,1)S(1)} %get-tuple-element.39.refs_3_.refs_0_), channel_id=1, source_target_pairs={{0,4},{1,5},{2,6},{3,7},{4,0},{5,1},{6,2},{7,3},{8,12},{9,13},{10,... | collective-permute-start | bytes 294920 | tf_op jit(solution)/shard_map/ppermute | solution.py:55
  16.4 2.0 %collective-permute-start.5 = (bf16[384,384]{1,0:T(8,128)(2,1)S(1)}, bf16[384,384]{1,0:T(8,128)(2,1)S(1)}, u32[]{:S(2)}, u32[]{:S(2)}) collective-permute-start(bf16[384,384]{1,0:T(8,128)(2,1)S(1)} %get-tuple-element.42.refs_0_), channel_id=1, source_target_pairs={{0,2},{1,3},{2,0},{3,1},{4,6},{5,7},{6,4},{7,5},{8,10},{9,11},{10,... | collective-permute-start | bytes 884744 | tf_op jit(solution)/shard_map/ppermute | solution.py:55
  18.4 2.5 %prefetch.1 = (bf16[2,384,768]{2,1,0:T(8,128)(2,1)S(1)}, bf16[2,384,768]{2,1,0:T(8,128)(2,1)S(1)}, bf16[2,1024,384]{2,1,0:T(8,128)(2,1)S(1)}) custom-call(bf16[5,2,384,768]{3,2,1,0:T(8,128)(2,1)} %bitcast.8, bf16[2,1024,384]{2,1,0:T(8,128)(2,1)} %bitcast.11, s32[2,5]{1,0:T(2,128)} %bitcast.13, bf16[384,128]{1,0:T(8,128)(2,1)S(1)} %get-tuple-element.39.refs_3_.refs_0_), custom_call_target="tpu_custom_call" | custom-call | flops 6000000000 | tf_op jit(solution)/shard_map/prefetch/pallas_call | solution.py:41
  20.9 0.4 level2_1.1.refs_3_.refs_0_
  21.3 0.4 collective-permute-start.4
  21.7 0.3 level3_0.1.refs_0_
  22.1 0.2 between_0.1.refs_0_
  22.3 1.0 %collective-permute-done.7.refs_1_ = bf16[384,128]{1,0:T(8,128)(2,1)S(1)} collective-permute-done((bf16[384,128]{1,0:T(8,128)(2,1)S(1)}, bf16[384,128]{1,0:T(8,128)(2,1)S(1)}, u32[]{:S(2)}, u32[]{:S(2)}) %collective-permute-start.7) | collective-permute-done | bytes 98336 | tf_op jit(solution)/shard_map/ppermute | solution.py:55
  23.4 0.6 last_0.1
  24.0 1.6 %collective-permute-start.8 = (bf16[512,128]{1,0:T(8,128)(2,1)S(1)}, bf16[512,128]{1,0:T(8,128)(2,1)S(1)}, u32[]{:S(2)}, u32[]{:S(2)}) collective-permute-start(bf16[512,128]{1,0:T(8,128)(2,1)S(1)} %get-tuple-element.46), channel_id=1, source_target_pairs={{0,16},{8,24},{16,0},{24,8},{1,17},{9,25},{17,1},{25,9},{2,18},{10... | collective-permute-start | bytes 393224 | tf_op jit(solution)/shard_map/ppermute | solution.py:55
  25.6 3.4 %collective-permute-done.5.refs_1_ = bf16[384,384]{1,0:T(8,128)(2,1)S(1)} collective-permute-done((bf16[384,384]{1,0:T(8,128)(2,1)S(1)}, bf16[384,384]{1,0:T(8,128)(2,1)S(1)}, u32[]{:S(2)}, u32[]{:S(2)}) %collective-permute-start.5) | collective-permute-done | bytes 294944 | tf_op jit(solution)/shard_map/ppermute | solution.py:55
  29.0 0.7 level2_2.1
  29.7 4.2 %collective-permute-start.14 = (bf16[384,384]{1,0:T(8,128)(2,1)S(1)}, bf16[384,384]{1,0:T(8,128)(2,1)S(1)}, u32[]{:S(2)}, u32[]{:S(2)}) collective-permute-start(bf16[384,384]{1,0:T(8,128)(2,1)S(1)} %get-tuple-element.45.refs_3_.refs_0_), channel_id=1, source_target_pairs={{0,4},{1,5},{2,6},{3,7},{4,0},{5,1},{6,2},{7,3},{8,12},{9,13},{10,... | collective-permute-start | bytes 884744 | tf_op jit(solution)/shard_map/ppermute | solution.py:55
  33.9 0.4 level3_1.1.refs_0_
  34.4 0.3 between_1.1
  34.7 1.6 %collective-permute-start.9 = (bf16[256,128]{1,0:T(8,128)(2,1)S(1)}, bf16[256,128]{1,0:T(8,128)(2,1)S(1)}, u32[]{:S(2)}, u32[]{:S(2)}) collective-permute-start(bf16[256,128]{1,0:T(8,128)(2,1)S(1)} %get-tuple-element.48), channel_id=1, source_target_pairs={{0,8},{8,0},{16,24},{24,16},{1,9},{9,1},{17,25},{25,17},{2,10},{10... | collective-permute-start | bytes 196616 | tf_op jit(solution)/shard_map/ppermute | solution.py:55
  36.2 0.8 %last_1.1 = (f32[512,256]{1,0:T(8,128)S(1)}, bf16[512,256]{1,0:T(8,128)(2,1)S(1)}) custom-call(f32[384,256]{1,0:T(8,128)S(1)} %get-tuple-element.49.refs_0_, bf16[384,256]{1,0:T(8,128)(2,1)S(1)} %collective-permute-done.10.refs_1_, bf16[2,384,768]{2,1,0:T(8,128)(2,1)S(1)} %get-tuple-element.43.refs_1_.refs_2_, ...), custom_call_target="tpu_custom_call" | custom-call | flops 6000000000 | tf_op jit(solution)/shard_map/last_1/pallas_call | solution.py:41
  37.0 1.1 %collective-permute-start.12 = (bf16[512,256]{1,0:T(8,128)(2,1)S(1)}, bf16[512,256]{1,0:T(8,128)(2,1)S(1)}, u32[]{:S(2)}, u32[]{:S(2)}) collective-permute-start(bf16[512,256]{1,0:T(8,128)(2,1)S(1)} %get-tuple-element.52), channel_id=1, source_target_pairs={{0,8},{8,0},{16,24},{24,16},{1,9},{9,1},{17,25},{25,17},{2,10},{10... | collective-permute-start | bytes 786440 | tf_op jit(solution)/shard_map/ppermute | solution.py:55
  38.2 1.0 %collective-permute-done.9.refs_1_ = bf16[256,128]{1,0:T(8,128)(2,1)S(1)} collective-permute-done((bf16[256,128]{1,0:T(8,128)(2,1)S(1)}, bf16[256,128]{1,0:T(8,128)(2,1)S(1)}, u32[]{:S(2)}, u32[]{:S(2)}) %collective-permute-start.9) | collective-permute-done | bytes 65568 | tf_op jit(solution)/shard_map/ppermute | solution.py:55
  39.2 6.3 %collective-permute-done.12.refs_1_ = bf16[512,256]{1,0:T(8,128)(2,1)S(1)} collective-permute-done((bf16[512,256]{1,0:T(8,128)(2,1)S(1)}, bf16[512,256]{1,0:T(8,128)(2,1)S(1)}, u32[]{:S(2)}, u32[]{:S(2)}) %collective-permute-start.12) | collective-permute-done | bytes 262176 | tf_op jit(solution)/shard_map/ppermute | solution.py:55
  45.6 1.6 %collective-permute-start.16 = (bf16[256,256]{1,0:T(8,128)(2,1)S(1)}, bf16[256,256]{1,0:T(8,128)(2,1)S(1)}, u32[]{:S(2)}, u32[]{:S(2)}) collective-permute-start(bf16[256,256]{1,0:T(8,128)(2,1)S(1)} %get-tuple-element.55), channel_id=1, source_target_pairs={{0,16},{8,24},{16,0},{24,8},{1,17},{9,25},{17,1},{25,9},{2,18},{10... | collective-permute-start | bytes 393224 | tf_op jit(solution)/shard_map/ppermute | solution.py:55
  47.2 0.4 level2_3.1.refs_3_.refs_0_
  47.6 0.5 level3_2.1.refs_0_
  48.2 0.3 between_2.1.refs_0_
  48.5 1.2 %collective-permute-done.15.refs_1_ = bf16[384,384]{1,0:T(8,128)(2,1)S(1)} collective-permute-done((bf16[384,384]{1,0:T(8,128)(2,1)S(1)}, bf16[384,384]{1,0:T(8,128)(2,1)S(1)}, u32[]{:S(2)}, u32[]{:S(2)}) %collective-permute-start.15) | collective-permute-done | bytes 294944 | tf_op jit(solution)/shard_map/ppermute | solution.py:55
  49.8 1.2 %last_2.1 = (f32[256,384]{1,0:T(8,128)S(1)}, bf16[256,384]{1,0:T(8,128)(2,1)S(1)}, bf16[256,384]{1,0:T(8,128)(2,1)S(1)}, bf16[256,384]{1,0:T(8,128)(2,1)S(1)}) custom-call(f32[384,384]{1,0:T(8,128)S(1)} %between_2.1.refs_0_, bf16[384,384]{1,0:T(8,128)(2,1)S(1)} %collective-permute-done.15.refs_1_, ...), custom_call_target="tpu_custom_call" | custom-call | flops 6000000000 | tf_op jit(solution)/shard_map/last_2/pallas_call | solution.py:41
  51.0 1.4 %collective-permute-start.17 = (bf16[256,384]{1,0:T(8,128)(2,1)S(1)}, bf16[256,384]{1,0:T(8,128)(2,1)S(1)}, u32[]{:S(2)}, u32[]{:S(2)}) collective-permute-start(bf16[256,384]{1,0:T(8,128)(2,1)S(1)} %get-tuple-element.57), channel_id=1, source_target_pairs={{0,24},{8,16},{16,8},{24,0},{1,25},{9,17},{17,9},{25,1},{2,26},{10... | collective-permute-start | bytes 589832 | tf_op jit(solution)/shard_map/ppermute | solution.py:55
  52.4 1.1 %collective-permute-start.18 = (bf16[256,384]{1,0:T(8,128)(2,1)S(1)}, bf16[256,384]{1,0:T(8,128)(2,1)S(1)}, u32[]{:S(2)}, u32[]{:S(2)}) collective-permute-start(bf16[256,384]{1,0:T(8,128)(2,1)S(1)} %get-tuple-element.58), channel_id=1, source_target_pairs={{0,16},{8,24},{16,0},{24,8},{1,17},{9,25},{17,1},{25,9},{2,18},{10... | collective-permute-start | bytes 589832 | tf_op jit(solution)/shard_map/ppermute | solution.py:55
  53.6 1.0 %collective-permute-start.19 = (bf16[256,384]{1,0:T(8,128)(2,1)S(1)}, bf16[256,384]{1,0:T(8,128)(2,1)S(1)}, u32[]{:S(2)}, u32[]{:S(2)}) collective-permute-start(bf16[256,384]{1,0:T(8,128)(2,1)S(1)} %get-tuple-element.59), channel_id=1, source_target_pairs={{0,8},{8,0},{16,24},{24,16},{1,9},{9,1},{17,25},{25,17},{2,10},{10... | collective-permute-start | bytes 589832 | tf_op jit(solution)/shard_map/ppermute | solution.py:55
  54.6 3.5 %collective-permute-done.13.refs_1_ = bf16[384,256]{1,0:T(8,128)(2,1)S(1)} collective-permute-done((bf16[384,256]{1,0:T(8,128)(2,1)S(1)}, bf16[384,256]{1,0:T(8,128)(2,1)S(1)}, u32[]{:S(2)}, u32[]{:S(2)}) %collective-permute-start.13) | collective-permute-done | bytes 196640 | tf_op jit(solution)/shard_map/ppermute | solution.py:55
  58.1 0.4 level3_3.1.refs_0_
  58.6 0.3 between_3.1
  58.8 1.2 %collective-permute-done.20.refs_1_ = bf16[384,256]{1,0:T(8,128)(2,1)S(1)} collective-permute-done((bf16[384,256]{1,0:T(8,128)(2,1)S(1)}, bf16[384,256]{1,0:T(8,128)(2,1)S(1)}, u32[]{:S(2)}, u32[]{:S(2)}) %collective-permute-start.20) | collective-permute-done | bytes 196640 | tf_op jit(solution)/shard_map/ppermute | solution.py:55
  60.0 0.8 %last_3.1 = (f32[256,256]{1,0:T(8,128)S(1)}, bf16[256,256]{1,0:T(8,128)(2,1)S(1)}, bf16[256,256]{1,0:T(8,128)(2,1)S(1)}, bf16[256,256]{1,0:T(8,128)(2,1)S(1)}) custom-call(f32[384,256]{1,0:T(8,128)S(1)} %get-tuple-element.60.refs_0_, bf16[384,256]{1,0:T(8,128)(2,1)S(1)} %collective-permute-done.20.refs_1_, ...), custom_call_target="tpu_custom_call" | custom-call | flops 6000000000 | tf_op jit(solution)/shard_map/last_3/pallas_call | solution.py:41
  60.8 0.9 %collective-permute-start.21 = (bf16[256,256]{1,0:T(8,128)(2,1)S(1)}, bf16[256,256]{1,0:T(8,128)(2,1)S(1)}, u32[]{:S(2)}, u32[]{:S(2)}) collective-permute-start(bf16[256,256]{1,0:T(8,128)(2,1)S(1)} %get-tuple-element.62), channel_id=1, source_target_pairs={{0,24},{8,16},{16,8},{24,0},{1,25},{9,17},{17,9},{25,1},{2,26},{10... | collective-permute-start | bytes 393224 | tf_op jit(solution)/shard_map/ppermute | solution.py:55
  61.8 1.5 %collective-permute-start.22 = (bf16[256,256]{1,0:T(8,128)(2,1)S(1)}, bf16[256,256]{1,0:T(8,128)(2,1)S(1)}, u32[]{:S(2)}, u32[]{:S(2)}) collective-permute-start(bf16[256,256]{1,0:T(8,128)(2,1)S(1)} %get-tuple-element.63), channel_id=1, source_target_pairs={{0,16},{8,24},{16,0},{24,8},{1,17},{9,25},{17,1},{25,9},{2,18},{10... | collective-permute-start | bytes 393224 | tf_op jit(solution)/shard_map/ppermute | solution.py:55
  63.3 1.1 %collective-permute-start.23 = (bf16[256,256]{1,0:T(8,128)(2,1)S(1)}, bf16[256,256]{1,0:T(8,128)(2,1)S(1)}, u32[]{:S(2)}, u32[]{:S(2)}) collective-permute-start(bf16[256,256]{1,0:T(8,128)(2,1)S(1)} %get-tuple-element.64), channel_id=1, source_target_pairs={{0,8},{8,0},{16,24},{24,16},{1,9},{9,1},{17,25},{25,17},{2,10},{10... | collective-permute-start | bytes 393224 | tf_op jit(solution)/shard_map/ppermute | solution.py:55
  64.4 3.8 %collective-permute-done.21.refs_7_ = bf16[256,256]{1,0:T(8,128)(2,1)S(1)} collective-permute-done((bf16[256,256]{1,0:T(8,128)(2,1)S(1)}, bf16[256,256]{1,0:T(8,128)(2,1)S(1)}, u32[]{:S(2)}, u32[]{:S(2)}) %collective-permute-start.21) | collective-permute-done | bytes 131104 | tf_op jit(solution)/shard_map/ppermute | solution.py:55
  68.2 1.7 %collective-permute-done.22.refs_8_ = bf16[256,256]{1,0:T(8,128)(2,1)S(1)} collective-permute-done((bf16[256,256]{1,0:T(8,128)(2,1)S(1)}, bf16[256,256]{1,0:T(8,128)(2,1)S(1)}, u32[]{:S(2)}, u32[]{:S(2)}) %collective-permute-start.22) | collective-permute-done | bytes 131104 | tf_op jit(solution)/shard_map/ppermute | solution.py:55
  69.8 1.0 %end.1 = bf16[2,256,512]{2,1,0:T(8,128)(2,1)} custom-call(bf16[256,128]{1,0:T(8,128)(2,1)S(1)} %sum_0.1.refs_2_.refs_0_, bf16[256,256]{1,0:T(8,128)(2,1)S(1)} %get-tuple-element.56.refs_1_, f32[256,384]{1,0:T(8,128)S(1)} %get-tuple-element.54.refs_3_.refs_2_, bf16[256,384]{1,0:T(8,128)(2,1)S(1)} %collective-permute-done.17.refs_3_, ...), custom_call_target="tpu_custom_call" | custom-call | tf_op jit(solution)/shard_map/end/pallas_call | solution.py:395
  (23 shorter events, 0.7 us)
Async XLA Ops:
  3.7 5.8 %collective-permute-start = (bf16[384,896]{1,0:T(8,128)(2,1)S(1)}, bf16[384,896]{1,0:T(8,128)(2,1)S(1)}, u32[]{:S(2)}, u32[]{:S(2)}) collective-permute-start(bf16[384,896]{1,0:T(8,128)(2,1)S(1)} %get-tuple-element.35.refs_0_.refs_3_), channel_id=1, source_target_pairs={{0,1},{1,0},{2,3},{3,2},{4,5},{5,4},{6,7},{7,6},{8,9},{9,8},{10,11... | collective-permute-start | bytes 2064392 | tf_op jit(solution)/shard_map/ppermute | solution.py:55
  4.2 1.9 %collective-permute-start.1 = (bf16[384,128]{1,0:T(8,128)(2,1)S(1)}, bf16[384,128]{1,0:T(8,128)(2,1)S(1)}, u32[]{:S(2)}, u32[]{:S(2)}) collective-permute-start(bf16[384,128]{1,0:T(8,128)(2,1)S(1)} %get-tuple-element.37.refs_0_), channel_id=1, source_target_pairs={{0,1},{1,0},{2,3},{3,2},{4,5},{5,4},{6,7},{7,6},{8,9},{9,8},{10,11... | collective-permute-start | bytes 294920 | tf_op jit(solution)/shard_map/ppermute | solution.py:55
  6.4 6.3 %collective-permute-start.3 = (bf16[384,128]{1,0:T(8,128)(2,1)S(1)}, bf16[384,128]{1,0:T(8,128)(2,1)S(1)}, u32[]{:S(2)}, u32[]{:S(2)}) collective-permute-start(bf16[384,128]{1,0:T(8,128)(2,1)S(1)} %level1_0.1.refs_3_.refs_0_), channel_id=1, source_target_pairs={{0,2},{1,3},{2,0},{3,1},{4,6},{5,7},{6,4},{7,5},{8,10},{9,11},{10,... | collective-permute-start | bytes 294920 | tf_op jit(solution)/shard_map/ppermute | solution.py:55
  9.8 11.1 %collective-permute-start.2 = (bf16[384,256]{1,0:T(8,128)(2,1)S(1)}, bf16[384,256]{1,0:T(8,128)(2,1)S(1)}, u32[]{:S(2)}, u32[]{:S(2)}) collective-permute-start(bf16[384,256]{1,0:T(8,128)(2,1)S(1)} %level1_1.1.refs_6_.refs_0_), channel_id=1, source_target_pairs={{0,2},{1,3},{2,0},{3,1},{4,6},{5,7},{6,4},{7,5},{8,10},{9,11},{10,... | collective-permute-start | bytes 589832 | tf_op jit(solution)/shard_map/ppermute | solution.py:55
  13.4 8.3 %collective-permute-start.6 = (bf16[384,128]{1,0:T(8,128)(2,1)S(1)}, bf16[384,128]{1,0:T(8,128)(2,1)S(1)}, u32[]{:S(2)}, u32[]{:S(2)}) collective-permute-start(bf16[384,128]{1,0:T(8,128)(2,1)S(1)} %get-tuple-element.39.refs_3_.refs_0_), channel_id=1, source_target_pairs={{0,4},{1,5},{2,6},{3,7},{4,0},{5,1},{6,2},{7,3},{8,12},{9,13},{10,... | collective-permute-start | bytes 294920 | tf_op jit(solution)/shard_map/ppermute | solution.py:55
  16.4 12.5 %collective-permute-start.5 = (bf16[384,384]{1,0:T(8,128)(2,1)S(1)}, bf16[384,384]{1,0:T(8,128)(2,1)S(1)}, u32[]{:S(2)}, u32[]{:S(2)}) collective-permute-start(bf16[384,384]{1,0:T(8,128)(2,1)S(1)} %get-tuple-element.42.refs_0_), channel_id=1, source_target_pairs={{0,2},{1,3},{2,0},{3,1},{4,6},{5,7},{6,4},{7,5},{8,10},{9,11},{10,... | collective-permute-start | bytes 884744 | tf_op jit(solution)/shard_map/ppermute | solution.py:55
  21.3 12.7 %collective-permute-start.4 = (bf16[384,256]{1,0:T(8,128)(2,1)S(1)}, bf16[384,256]{1,0:T(8,128)(2,1)S(1)}, u32[]{:S(2)}, u32[]{:S(2)}) collective-permute-start(bf16[384,256]{1,0:T(8,128)(2,1)S(1)} %level2_1.1.refs_3_.refs_0_), channel_id=1, source_target_pairs={{0,4},{1,5},{2,6},{3,7},{4,0},{5,1},{6,2},{7,3},{8,12},{9,13},{10,... | collective-permute-start | bytes 589832 | tf_op jit(solution)/shard_map/ppermute | solution.py:55
  22.0 1.4 %collective-permute-start.7 = (bf16[384,128]{1,0:T(8,128)(2,1)S(1)}, bf16[384,128]{1,0:T(8,128)(2,1)S(1)}, u32[]{:S(2)}, u32[]{:S(2)}) collective-permute-start(bf16[384,128]{1,0:T(8,128)(2,1)S(1)} %level3_0.1.refs_0_), channel_id=1, source_target_pairs={{0,1},{1,0},{2,3},{3,2},{4,5},{5,4},{6,7},{7,6},{8,9},{9,8},{10,11... | collective-permute-start | bytes 294920 | tf_op jit(solution)/shard_map/ppermute | solution.py:55
  24.0 10.4 %collective-permute-start.8 = (bf16[512,128]{1,0:T(8,128)(2,1)S(1)}, bf16[512,128]{1,0:T(8,128)(2,1)S(1)}, u32[]{:S(2)}, u32[]{:S(2)}) collective-permute-start(bf16[512,128]{1,0:T(8,128)(2,1)S(1)} %get-tuple-element.46), channel_id=1, source_target_pairs={{0,16},{8,24},{16,0},{24,8},{1,17},{9,25},{17,1},{25,9},{2,18},{10... | collective-permute-start | bytes 393224 | tf_op jit(solution)/shard_map/ppermute | solution.py:55
  29.6 17.5 %collective-permute-start.11 = (bf16[384,256]{1,0:T(8,128)(2,1)S(1)}, bf16[384,256]{1,0:T(8,128)(2,1)S(1)}, u32[]{:S(2)}, u32[]{:S(2)}) collective-permute-start(bf16[384,256]{1,0:T(8,128)(2,1)S(1)} %get-tuple-element.51.refs_0_), channel_id=1, source_target_pairs={{0,2},{1,3},{2,0},{3,1},{4,6},{5,7},{6,4},{7,5},{8,10},{9,11},{10,... | collective-permute-start | bytes 589832 | tf_op jit(solution)/shard_map/ppermute | solution.py:55
  29.7 17.9 %collective-permute-start.14 = (bf16[384,384]{1,0:T(8,128)(2,1)S(1)}, bf16[384,384]{1,0:T(8,128)(2,1)S(1)}, u32[]{:S(2)}, u32[]{:S(2)}) collective-permute-start(bf16[384,384]{1,0:T(8,128)(2,1)S(1)} %get-tuple-element.45.refs_3_.refs_0_), channel_id=1, source_target_pairs={{0,4},{1,5},{2,6},{3,7},{4,0},{5,1},{6,2},{7,3},{8,12},{9,13},{10,... | collective-permute-start | bytes 884744 | tf_op jit(solution)/shard_map/ppermute | solution.py:55
  34.3 1.9 %collective-permute-start.10 = (bf16[384,256]{1,0:T(8,128)(2,1)S(1)}, bf16[384,256]{1,0:T(8,128)(2,1)S(1)}, u32[]{:S(2)}, u32[]{:S(2)}) collective-permute-start(bf16[384,256]{1,0:T(8,128)(2,1)S(1)} %level3_1.1.refs_0_), channel_id=1, source_target_pairs={{0,1},{1,0},{2,3},{3,2},{4,5},{5,4},{6,7},{7,6},{8,9},{9,8},{10,11... | collective-permute-start | bytes 589832 | tf_op jit(solution)/shard_map/ppermute | solution.py:55
  34.7 4.6 %collective-permute-start.9 = (bf16[256,128]{1,0:T(8,128)(2,1)S(1)}, bf16[256,128]{1,0:T(8,128)(2,1)S(1)}, u32[]{:S(2)}, u32[]{:S(2)}) collective-permute-start(bf16[256,128]{1,0:T(8,128)(2,1)S(1)} %get-tuple-element.48), channel_id=1, source_target_pairs={{0,8},{8,0},{16,24},{24,16},{1,9},{9,1},{17,25},{25,17},{2,10},{10... | collective-permute-start | bytes 196616 | tf_op jit(solution)/shard_map/ppermute | solution.py:55
  37.0 8.5 %collective-permute-start.12 = (bf16[512,256]{1,0:T(8,128)(2,1)S(1)}, bf16[512,256]{1,0:T(8,128)(2,1)S(1)}, u32[]{:S(2)}, u32[]{:S(2)}) collective-permute-start(bf16[512,256]{1,0:T(8,128)(2,1)S(1)} %get-tuple-element.52), channel_id=1, source_target_pairs={{0,8},{8,0},{16,24},{24,16},{1,9},{9,1},{17,25},{25,17},{2,10},{10... | collective-permute-start | bytes 786440 | tf_op jit(solution)/shard_map/ppermute | solution.py:55
  45.6 13.0 %collective-permute-start.16 = (bf16[256,256]{1,0:T(8,128)(2,1)S(1)}, bf16[256,256]{1,0:T(8,128)(2,1)S(1)}, u32[]{:S(2)}, u32[]{:S(2)}) collective-permute-start(bf16[256,256]{1,0:T(8,128)(2,1)S(1)} %get-tuple-element.55), channel_id=1, source_target_pairs={{0,16},{8,24},{16,0},{24,8},{1,17},{9,25},{17,1},{25,9},{2,18},{10... | collective-permute-start | bytes 393224 | tf_op jit(solution)/shard_map/ppermute | solution.py:55
  47.5 10.6 %collective-permute-start.13 = (bf16[384,256]{1,0:T(8,128)(2,1)S(1)}, bf16[384,256]{1,0:T(8,128)(2,1)S(1)}, u32[]{:S(2)}, u32[]{:S(2)}) collective-permute-start(bf16[384,256]{1,0:T(8,128)(2,1)S(1)} %level2_3.1.refs_3_.refs_0_), channel_id=1, source_target_pairs={{0,4},{1,5},{2,6},{3,7},{4,0},{5,1},{6,2},{7,3},{8,12},{9,13},{10,... | collective-permute-start | bytes 589832 | tf_op jit(solution)/shard_map/ppermute | solution.py:55
  48.1 1.6 %collective-permute-start.15 = (bf16[384,384]{1,0:T(8,128)(2,1)S(1)}, bf16[384,384]{1,0:T(8,128)(2,1)S(1)}, u32[]{:S(2)}, u32[]{:S(2)}) collective-permute-start(bf16[384,384]{1,0:T(8,128)(2,1)S(1)} %level3_2.1.refs_0_), channel_id=1, source_target_pairs={{0,1},{1,0},{2,3},{3,2},{4,5},{5,4},{6,7},{7,6},{8,9},{9,8},{10,11... | collective-permute-start | bytes 884744 | tf_op jit(solution)/shard_map/ppermute | solution.py:55
  51.0 12.3 %collective-permute-start.17 = (bf16[256,384]{1,0:T(8,128)(2,1)S(1)}, bf16[256,384]{1,0:T(8,128)(2,1)S(1)}, u32[]{:S(2)}, u32[]{:S(2)}) collective-permute-start(bf16[256,384]{1,0:T(8,128)(2,1)S(1)} %get-tuple-element.57), channel_id=1, source_target_pairs={{0,24},{8,16},{16,8},{24,0},{1,25},{9,17},{17,9},{25,1},{2,26},{10... | collective-permute-start | bytes 589832 | tf_op jit(solution)/shard_map/ppermute | solution.py:55
  52.4 11.9 %collective-permute-start.18 = (bf16[256,384]{1,0:T(8,128)(2,1)S(1)}, bf16[256,384]{1,0:T(8,128)(2,1)S(1)}, u32[]{:S(2)}, u32[]{:S(2)}) collective-permute-start(bf16[256,384]{1,0:T(8,128)(2,1)S(1)} %get-tuple-element.58), channel_id=1, source_target_pairs={{0,16},{8,24},{16,0},{24,8},{1,17},{9,25},{17,1},{25,9},{2,18},{10... | collective-permute-start | bytes 589832 | tf_op jit(solution)/shard_map/ppermute | solution.py:55
  53.6 10.8 %collective-permute-start.19 = (bf16[256,384]{1,0:T(8,128)(2,1)S(1)}, bf16[256,384]{1,0:T(8,128)(2,1)S(1)}, u32[]{:S(2)}, u32[]{:S(2)}) collective-permute-start(bf16[256,384]{1,0:T(8,128)(2,1)S(1)} %get-tuple-element.59), channel_id=1, source_target_pairs={{0,8},{8,0},{16,24},{24,16},{1,9},{9,1},{17,25},{25,17},{2,10},{10... | collective-permute-start | bytes 589832 | tf_op jit(solution)/shard_map/ppermute | solution.py:55
  58.5 1.5 %collective-permute-start.20 = (bf16[384,256]{1,0:T(8,128)(2,1)S(1)}, bf16[384,256]{1,0:T(8,128)(2,1)S(1)}, u32[]{:S(2)}, u32[]{:S(2)}) collective-permute-start(bf16[384,256]{1,0:T(8,128)(2,1)S(1)} %level3_3.1.refs_0_), channel_id=1, source_target_pairs={{0,1},{1,0},{2,3},{3,2},{4,5},{5,4},{6,7},{7,6},{8,9},{9,8},{10,11... | collective-permute-start | bytes 589832 | tf_op jit(solution)/shard_map/ppermute | solution.py:55
  60.8 7.4 %collective-permute-start.21 = (bf16[256,256]{1,0:T(8,128)(2,1)S(1)}, bf16[256,256]{1,0:T(8,128)(2,1)S(1)}, u32[]{:S(2)}, u32[]{:S(2)}) collective-permute-start(bf16[256,256]{1,0:T(8,128)(2,1)S(1)} %get-tuple-element.62), channel_id=1, source_target_pairs={{0,24},{8,16},{16,8},{24,0},{1,25},{9,17},{17,9},{25,1},{2,26},{10... | collective-permute-start | bytes 393224 | tf_op jit(solution)/shard_map/ppermute | solution.py:55
  61.8 8.1 %collective-permute-start.22 = (bf16[256,256]{1,0:T(8,128)(2,1)S(1)}, bf16[256,256]{1,0:T(8,128)(2,1)S(1)}, u32[]{:S(2)}, u32[]{:S(2)}) collective-permute-start(bf16[256,256]{1,0:T(8,128)(2,1)S(1)} %get-tuple-element.63), channel_id=1, source_target_pairs={{0,16},{8,24},{16,0},{24,8},{1,17},{9,25},{17,1},{25,9},{2,18},{10... | collective-permute-start | bytes 393224 | tf_op jit(solution)/shard_map/ppermute | solution.py:55
  63.3 6.6 %collective-permute-start.23 = (bf16[256,256]{1,0:T(8,128)(2,1)S(1)}, bf16[256,256]{1,0:T(8,128)(2,1)S(1)}, u32[]{:S(2)}, u32[]{:S(2)}) collective-permute-start(bf16[256,256]{1,0:T(8,128)(2,1)S(1)} %get-tuple-element.64), channel_id=1, source_target_pairs={{0,8},{8,0},{16,24},{24,16},{1,9},{9,1},{17,25},{25,17},{2,10},{10... | collective-permute-start | bytes 393224 | tf_op jit(solution)/shard_map/ppermute | solution.py:55

commit v10 on v9

--- a/solution.py
+++ b/solution.py
@@ -364,14 +364,15 @@
 
     out0, _ = tail(0, [coeff3[1]], False)
     fold0 = begin_sum(0, out0)
-    value, ahead = step("level2_2", [(2, 2, coeff2[2], near2[2]), job1(3)], [out0[0]])
+    (value,) = step("level2_2", [(2, 2, coeff2[2], near2[2])], [out0[0]])
     third(2, value)
-    second(3, ahead)
     out1, (send0, keep0) = tail(1, [coeff3[2]], False, fold0)
     got0 = partner(send0, "blk", halving(0)[0][-1])
     fold1 = begin_sum(1, out1)
+    (value,) = step("level1_3", [job1(3)], [out1[0]])
+    second(3, value)
     (total0,) = call(
-        sum_kernel, "sum_0", [VMEM] * 2, [result(0, 1, BF16)], [], [here(keep0), here(got0)], [out1[0]]
+        sum_kernel, "sum_0", [VMEM] * 2, [result(0, 1, BF16)], [], [here(keep0), here(got0)], [coeff2[3]]
     )
     at, keep, got, count = fold1
     send1, keep1 = call(
@@ -383,7 +384,7 @@
         [here(keep), here(got)],
         [total0],
     )
-    (value,) = step("level2_3", [(2, 3, coeff2[3], near2[3])], [keep1])
+    (value,) = step("level2_3", [(2, 3, coeff2[3], near2[3])], [total0])
     third(3, value)
     out2, _ = tail(2, [coeff3[3]], True, None, None)
     got1 = partner(send1, "blk", halving(1)[0][-1])

time: 71 us -> 72.7 us (1.024)
  waiting for transfers between devices: 27.8 us -> 30 us
    ppermute x24, waiting for transfers between devices: 27.8 us -> 30 us  [partner(): return lax.ppermute(value, axis, pairs)]
    pallas_call x22 -> x23, Pallas kernels: 15 us -> 15.2 us  [call(): pl.pallas_call(body, name=name, in_specs=[*in_specs, *[ANY] * len(after)]...]
where the time goes in v10:
time: 72.7 us; the launch traced here: 72.5 us
  waiting for transfers between devices  30 us (41%)
  starting transfers between devices  26.1 us (36%)
  Pallas kernels  16.2 us (22%)
    ppermute x24, waiting for transfers between devices, partner(): return lax.ppermute(value, axis, pairs)  30 us
    ppermute x24, starting transfers between devices, partner(): return lax.ppermute(value, axis, pairs)  26.1 us
    pallas_call x23, Pallas kernels, call(): pl.pallas_call(body, name=name, in_specs=[*in_specs, *[ANY] * len(after)]...  15.2 us
  transfers between devices with their start and end apart: 24, of which 11 were waited for; matrix products, arithmetic and copies ran while one was open for 0% of the time, Pallas kernels for 16%

profile of v10, /device:TPU:0, one launch (start us, length us, event | category | flops | bytes accessed | tf_op | source)
XLA Modules:
  0.0 72.5 jit_solution(731380916509112848)
XLA Ops:
  0.0 3.7 %leaf.1 = (bf16[384,128]{1,0:T(8,128)(2,1)S(1)}, bf16[384,896]{1,0:T(8,128)(2,1)S(1)}, bf16[2,384,768]{2,1,0:T(8,128)(2,1)S(1)}, bf16[2,384,768]{2,1,0:T(8,128)(2,1)S(1)}) custom-call(bf16[2,1024,512]{2,1,0:T(8,128)(2,1)} %bitcast.9, bf16[2,384,1024]{2,1,0:T(8,128)(2,1)} %bitcast.10, bf16[5,2,384,768]{3,2,1,0:T(8,128)(2,1)} %bitcast.7, s32[2,5]{1,0:T(2,128)} %bitcast.12), custom_call_target="tpu_custom_call" | custom-call | flops 6000000000 | tf_op jit(solution)/shard_map/leaf/pallas_call | solution.py:41
  3.7 0.5 collective-permute-start
  4.3 1.8 %collective-permute-done.1.refs_1_ = bf16[384,128]{1,0:T(8,128)(2,1)S(1)} collective-permute-done((bf16[384,128]{1,0:T(8,128)(2,1)S(1)}, bf16[384,128]{1,0:T(8,128)(2,1)S(1)}, u32[]{:S(2)}, u32[]{:S(2)}) %collective-permute-start.1) | collective-permute-done | bytes 98336 | tf_op jit(solution)/shard_map/ppermute | solution.py:55
  6.1 0.3 level1_0.1.refs_3_.refs_0_
  6.4 3.0 %collective-permute-start.3 = (bf16[384,128]{1,0:T(8,128)(2,1)S(1)}, bf16[384,128]{1,0:T(8,128)(2,1)S(1)}, u32[]{:S(2)}, u32[]{:S(2)}) collective-permute-start(bf16[384,128]{1,0:T(8,128)(2,1)S(1)} %level1_0.1.refs_3_.refs_0_), channel_id=1, source_target_pairs={{0,2},{1,3},{2,0},{3,1},{4,6},{5,7},{6,4},{7,5},{8,10},{9,11},{10,... | collective-permute-start | bytes 294920 | tf_op jit(solution)/shard_map/ppermute | solution.py:55
  9.5 0.4 level1_1.1.refs_6_.refs_0_
  9.9 2.8 %collective-permute-done.3.refs_1_ = bf16[384,128]{1,0:T(8,128)(2,1)S(1)} collective-permute-done((bf16[384,128]{1,0:T(8,128)(2,1)S(1)}, bf16[384,128]{1,0:T(8,128)(2,1)S(1)}, u32[]{:S(2)}, u32[]{:S(2)}) %collective-permute-start.3) | collective-permute-done | bytes 98336 | tf_op jit(solution)/shard_map/ppermute | solution.py:55
  12.7 0.7 level2_0.1
  13.4 3.0 %collective-permute-start.6 = (bf16[384,128]{1,0:T(8,128)(2,1)S(1)}, bf16[384,128]{1,0:T(8,128)(2,1)S(1)}, u32[]{:S(2)}, u32[]{:S(2)}) collective-permute-start(bf16[384,128]{1,0:T(8,128)(2,1)S(1)} %get-tuple-element.37.refs_3_.refs_0_), channel_id=1, source_target_pairs={{0,4},{1,5},{2,6},{3,7},{4,0},{5,1},{6,2},{7,3},{8,12},{9,13},{10,... | collective-permute-start | bytes 294920 | tf_op jit(solution)/shard_map/ppermute | solution.py:55
  16.4 2.0 %collective-permute-start.5 = (bf16[384,384]{1,0:T(8,128)(2,1)S(1)}, bf16[384,384]{1,0:T(8,128)(2,1)S(1)}, u32[]{:S(2)}, u32[]{:S(2)}) collective-permute-start(bf16[384,384]{1,0:T(8,128)(2,1)S(1)} %get-tuple-element.40.refs_0_), channel_id=1, source_target_pairs={{0,2},{1,3},{2,0},{3,1},{4,6},{5,7},{6,4},{7,5},{8,10},{9,11},{10,... | collective-permute-start | bytes 884744 | tf_op jit(solution)/shard_map/ppermute | solution.py:55
  18.4 2.5 %prefetch.1 = (bf16[2,384,768]{2,1,0:T(8,128)(2,1)S(1)}, bf16[2,384,768]{2,1,0:T(8,128)(2,1)S(1)}, bf16[2,1024,384]{2,1,0:T(8,128)(2,1)S(1)}) custom-call(bf16[5,2,384,768]{3,2,1,0:T(8,128)(2,1)} %bitcast.8, bf16[2,1024,384]{2,1,0:T(8,128)(2,1)} %bitcast.11, s32[2,5]{1,0:T(2,128)} %bitcast.13, bf16[384,128]{1,0:T(8,128)(2,1)S(1)} %get-tuple-element.37.refs_3_.refs_0_), custom_call_target="tpu_custom_call" | custom-call | flops 6000000000 | tf_op jit(solution)/shard_map/prefetch/pallas_call | solution.py:41
  20.9 0.4 level2_1.1.refs_3_.refs_0_
  21.3 0.4 collective-permute-start.4
  21.7 0.3 level3_0.1.refs_0_
  22.3 1.0 %collective-permute-done.7.refs_1_ = bf16[384,128]{1,0:T(8,128)(2,1)S(1)} collective-permute-done((bf16[384,128]{1,0:T(8,128)(2,1)S(1)}, bf16[384,128]{1,0:T(8,128)(2,1)S(1)}, u32[]{:S(2)}, u32[]{:S(2)}) %collective-permute-start.7) | collective-permute-done | bytes 98336 | tf_op jit(solution)/shard_map/ppermute | solution.py:55
  23.4 0.6 last_0.1
  24.0 1.6 %collective-permute-start.8 = (bf16[512,128]{1,0:T(8,128)(2,1)S(1)}, bf16[512,128]{1,0:T(8,128)(2,1)S(1)}, u32[]{:S(2)}, u32[]{:S(2)}) collective-permute-start(bf16[512,128]{1,0:T(8,128)(2,1)S(1)} %get-tuple-element.43), channel_id=1, source_target_pairs={{0,16},{8,24},{16,0},{24,8},{1,17},{9,25},{17,1},{25,9},{2,18},{10... | collective-permute-start | bytes 393224 | tf_op jit(solution)/shard_map/ppermute | solution.py:55
  25.6 3.4 %collective-permute-done.5.refs_1_ = bf16[384,384]{1,0:T(8,128)(2,1)S(1)} collective-permute-done((bf16[384,384]{1,0:T(8,128)(2,1)S(1)}, bf16[384,384]{1,0:T(8,128)(2,1)S(1)}, u32[]{:S(2)}, u32[]{:S(2)}) %collective-permute-start.5) | collective-permute-done | bytes 294944 | tf_op jit(solution)/shard_map/ppermute | solution.py:55
  29.0 0.5 level2_2.1.refs_3_.refs_0_
  29.5 1.8 %collective-permute-start.13 = (bf16[384,384]{1,0:T(8,128)(2,1)S(1)}, bf16[384,384]{1,0:T(8,128)(2,1)S(1)}, u32[]{:S(2)}, u32[]{:S(2)}) collective-permute-start(bf16[384,384]{1,0:T(8,128)(2,1)S(1)} %level2_2.1.refs_3_.refs_0_), channel_id=1, source_target_pairs={{0,4},{1,5},{2,6},{3,7},{4,0},{5,1},{6,2},{7,3},{8,12},{9,13},{10,... | collective-permute-start | bytes 884744 | tf_op jit(solution)/shard_map/ppermute | solution.py:55
  31.3 1.2 %collective-permute-done.4.refs_1_ = bf16[384,256]{1,0:T(8,128)(2,1)S(1)} collective-permute-done((bf16[384,256]{1,0:T(8,128)(2,1)S(1)}, bf16[384,256]{1,0:T(8,128)(2,1)S(1)}, u32[]{:S(2)}, u32[]{:S(2)}) %collective-permute-start.4) | collective-permute-done | bytes 196640 | tf_op jit(solution)/shard_map/ppermute | solution.py:55
  32.5 0.4 level3_1.1.refs_0_
  33.0 0.3 between_1.1
  33.2 1.6 %collective-permute-start.9 = (bf16[256,128]{1,0:T(8,128)(2,1)S(1)}, bf16[256,128]{1,0:T(8,128)(2,1)S(1)}, u32[]{:S(2)}, u32[]{:S(2)}) collective-permute-start(bf16[256,128]{1,0:T(8,128)(2,1)S(1)} %get-tuple-element.45), channel_id=1, source_target_pairs={{0,8},{8,0},{16,24},{24,16},{1,9},{9,1},{17,25},{25,17},{2,10},{10... | collective-permute-start | bytes 196616 | tf_op jit(solution)/shard_map/ppermute | solution.py:55
  34.8 0.8 %last_1.1 = (f32[512,256]{1,0:T(8,128)S(1)}, bf16[512,256]{1,0:T(8,128)(2,1)S(1)}) custom-call(f32[384,256]{1,0:T(8,128)S(1)} %get-tuple-element.46.refs_0_, bf16[384,256]{1,0:T(8,128)(2,1)S(1)} %collective-permute-done.10.refs_1_, bf16[2,384,768]{2,1,0:T(8,128)(2,1)S(1)} %get-tuple-element.41.refs_1_.refs_2_, ...), custom_call_target="tpu_custom_call" | custom-call | flops 6000000000 | tf_op jit(solution)/shard_map/last_1/pallas_call | solution.py:41
  35.6 0.4 level1_3.1.refs_2_.refs_0_
  36.0 1.4 %collective-permute-start.11 = (bf16[384,256]{1,0:T(8,128)(2,1)S(1)}, bf16[384,256]{1,0:T(8,128)(2,1)S(1)}, u32[]{:S(2)}, u32[]{:S(2)}) collective-permute-start(bf16[384,256]{1,0:T(8,128)(2,1)S(1)} %level1_3.1.refs_2_.refs_0_), channel_id=1, source_target_pairs={{0,2},{1,3},{2,0},{3,1},{4,6},{5,7},{6,4},{7,5},{8,10},{9,11},{10,... | collective-permute-start | bytes 589832 | tf_op jit(solution)/shard_map/ppermute | solution.py:55
  37.3 1.1 %collective-permute-start.15 = (bf16[512,256]{1,0:T(8,128)(2,1)S(1)}, bf16[512,256]{1,0:T(8,128)(2,1)S(1)}, u32[]{:S(2)}, u32[]{:S(2)}) collective-permute-start(bf16[512,256]{1,0:T(8,128)(2,1)S(1)} %get-tuple-element.49), channel_id=1, source_target_pairs={{0,8},{8,0},{16,24},{24,16},{1,9},{9,1},{17,25},{25,17},{2,10},{10... | collective-permute-start | bytes 786440 | tf_op jit(solution)/shard_map/ppermute | solution.py:55
  38.4 9.5 %collective-permute-done.11.refs_1_ = bf16[384,256]{1,0:T(8,128)(2,1)S(1)} collective-permute-done((bf16[384,256]{1,0:T(8,128)(2,1)S(1)}, bf16[384,256]{1,0:T(8,128)(2,1)S(1)}, u32[]{:S(2)}, u32[]{:S(2)}) %collective-permute-start.11) | collective-permute-done | bytes 196640 | tf_op jit(solution)/shard_map/ppermute | solution.py:55
  47.9 0.3 level2_3.1.refs_3_.refs_0_
  48.2 0.6 collective-permute-start.12
  48.8 0.5 level3_2.1.refs_0_
  49.5 0.3 between_2.1.refs_0_
  49.9 1.6 %collective-permute-start.16 = (bf16[256,256]{1,0:T(8,128)(2,1)S(1)}, bf16[256,256]{1,0:T(8,128)(2,1)S(1)}, u32[]{:S(2)}, u32[]{:S(2)}) collective-permute-start(bf16[256,256]{1,0:T(8,128)(2,1)S(1)} %get-tuple-element.51), channel_id=1, source_target_pairs={{0,16},{8,24},{16,0},{24,8},{1,17},{9,25},{17,1},{25,9},{2,18},{10... | collective-permute-start | bytes 393224 | tf_op jit(solution)/shard_map/ppermute | solution.py:55
  51.4 1.2 %last_2.1 = (f32[256,384]{1,0:T(8,128)S(1)}, bf16[256,384]{1,0:T(8,128)(2,1)S(1)}, bf16[256,384]{1,0:T(8,128)(2,1)S(1)}, bf16[256,384]{1,0:T(8,128)(2,1)S(1)}) custom-call(f32[384,384]{1,0:T(8,128)S(1)} %between_2.1.refs_0_, bf16[384,384]{1,0:T(8,128)(2,1)S(1)} %collective-permute-done.14.refs_1_, ...), custom_call_target="tpu_custom_call" | custom-call | flops 6000000000 | tf_op jit(solution)/shard_map/last_2/pallas_call | solution.py:41
  52.7 1.6 %collective-permute-start.17 = (bf16[256,384]{1,0:T(8,128)(2,1)S(1)}, bf16[256,384]{1,0:T(8,128)(2,1)S(1)}, u32[]{:S(2)}, u32[]{:S(2)}) collective-permute-start(bf16[256,384]{1,0:T(8,128)(2,1)S(1)} %get-tuple-element.53), channel_id=1, source_target_pairs={{0,24},{8,16},{16,8},{24,0},{1,25},{9,17},{17,9},{25,1},{2,26},{10... | collective-permute-start | bytes 589832 | tf_op jit(solution)/shard_map/ppermute | solution.py:55
  54.3 0.9 %collective-permute-start.18 = (bf16[256,384]{1,0:T(8,128)(2,1)S(1)}, bf16[256,384]{1,0:T(8,128)(2,1)S(1)}, u32[]{:S(2)}, u32[]{:S(2)}) collective-permute-start(bf16[256,384]{1,0:T(8,128)(2,1)S(1)} %get-tuple-element.54), channel_id=1, source_target_pairs={{0,16},{8,24},{16,0},{24,8},{1,17},{9,25},{17,1},{25,9},{2,18},{10... | collective-permute-start | bytes 589832 | tf_op jit(solution)/shard_map/ppermute | solution.py:55
  55.2 1.0 %collective-permute-start.19 = (bf16[256,384]{1,0:T(8,128)(2,1)S(1)}, bf16[256,384]{1,0:T(8,128)(2,1)S(1)}, u32[]{:S(2)}, u32[]{:S(2)}) collective-permute-start(bf16[256,384]{1,0:T(8,128)(2,1)S(1)} %get-tuple-element.55), channel_id=1, source_target_pairs={{0,8},{8,0},{16,24},{24,16},{1,9},{9,1},{17,25},{25,17},{2,10},{10... | collective-permute-start | bytes 589832 | tf_op jit(solution)/shard_map/ppermute | solution.py:55
  56.3 3.2 %collective-permute-done.12.refs_1_ = bf16[384,256]{1,0:T(8,128)(2,1)S(1)} collective-permute-done((bf16[384,256]{1,0:T(8,128)(2,1)S(1)}, bf16[384,256]{1,0:T(8,128)(2,1)S(1)}, u32[]{:S(2)}, u32[]{:S(2)}) %collective-permute-start.12) | collective-permute-done | bytes 196640 | tf_op jit(solution)/shard_map/ppermute | solution.py:55
  59.4 0.4 level3_3.1.refs_0_
  60.1 1.2 %collective-permute-done.20.refs_1_ = bf16[384,256]{1,0:T(8,128)(2,1)S(1)} collective-permute-done((bf16[384,256]{1,0:T(8,128)(2,1)S(1)}, bf16[384,256]{1,0:T(8,128)(2,1)S(1)}, u32[]{:S(2)}, u32[]{:S(2)}) %collective-permute-start.20) | collective-permute-done | bytes 196640 | tf_op jit(solution)/shard_map/ppermute | solution.py:55
  61.3 0.8 %last_3.1 = (f32[256,256]{1,0:T(8,128)S(1)}, bf16[256,256]{1,0:T(8,128)(2,1)S(1)}, bf16[256,256]{1,0:T(8,128)(2,1)S(1)}, bf16[256,256]{1,0:T(8,128)(2,1)S(1)}) custom-call(f32[384,256]{1,0:T(8,128)S(1)} %get-tuple-element.56.refs_0_, bf16[384,256]{1,0:T(8,128)(2,1)S(1)} %collective-permute-done.20.refs_1_, ...), custom_call_target="tpu_custom_call" | custom-call | flops 6000000000 | tf_op jit(solution)/shard_map/last_3/pallas_call | solution.py:41
  62.1 2.0 %collective-permute-start.21 = (bf16[256,256]{1,0:T(8,128)(2,1)S(1)}, bf16[256,256]{1,0:T(8,128)(2,1)S(1)}, u32[]{:S(2)}, u32[]{:S(2)}) collective-permute-start(bf16[256,256]{1,0:T(8,128)(2,1)S(1)} %get-tuple-element.58), channel_id=1, source_target_pairs={{0,24},{8,16},{16,8},{24,0},{1,25},{9,17},{17,9},{25,1},{2,26},{10... | collective-permute-start | bytes 393224 | tf_op jit(solution)/shard_map/ppermute | solution.py:55
  64.1 0.5 collective-permute-start.22
  64.6 1.1 %collective-permute-start.23 = (bf16[256,256]{1,0:T(8,128)(2,1)S(1)}, bf16[256,256]{1,0:T(8,128)(2,1)S(1)}, u32[]{:S(2)}, u32[]{:S(2)}) collective-permute-start(bf16[256,256]{1,0:T(8,128)(2,1)S(1)} %get-tuple-element.60), channel_id=1, source_target_pairs={{0,8},{8,0},{16,24},{24,16},{1,9},{9,1},{17,25},{25,17},{2,10},{10... | collective-permute-start | bytes 393224 | tf_op jit(solution)/shard_map/ppermute | solution.py:55
  65.7 3.7 %collective-permute-done.21.refs_7_ = bf16[256,256]{1,0:T(8,128)(2,1)S(1)} collective-permute-done((bf16[256,256]{1,0:T(8,128)(2,1)S(1)}, bf16[256,256]{1,0:T(8,128)(2,1)S(1)}, u32[]{:S(2)}, u32[]{:S(2)}) %collective-permute-start.21) | collective-permute-done | bytes 131104 | tf_op jit(solution)/shard_map/ppermute | solution.py:55
  69.4 2.0 %collective-permute-done.22.refs_8_ = bf16[256,256]{1,0:T(8,128)(2,1)S(1)} collective-permute-done((bf16[256,256]{1,0:T(8,128)(2,1)S(1)}, bf16[256,256]{1,0:T(8,128)(2,1)S(1)}, u32[]{:S(2)}, u32[]{:S(2)}) %collective-permute-start.22) | collective-permute-done | bytes 131104 | tf_op jit(solution)/shard_map/ppermute | solution.py:55
  71.6 1.0 %end.1 = bf16[2,256,512]{2,1,0:T(8,128)(2,1)} custom-call(bf16[256,128]{1,0:T(8,128)(2,1)S(1)} %sum_0.1.refs_3_.refs_2_.refs_0_, bf16[256,256]{1,0:T(8,128)(2,1)S(1)} %get-tuple-element.52.refs_1_, f32[256,384]{1,0:T(8,128)S(1)} %get-tuple-element.48.refs_3_.refs_2_, bf16[256,384]{1,0:T(8,128)(2,1)S(1)} %collective-permute-done.17.refs_3_, ...), custom_call_target="tpu_custom_call" | custom-call | tf_op jit(solution)/shard_map/end/pallas_call | solution.py:396
  (24 shorter events, 1.2 us)
Async XLA Ops:
  3.7 5.8 %collective-permute-start = (bf16[384,896]{1,0:T(8,128)(2,1)S(1)}, bf16[384,896]{1,0:T(8,128)(2,1)S(1)}, u32[]{:S(2)}, u32[]{:S(2)}) collective-permute-start(bf16[384,896]{1,0:T(8,128)(2,1)S(1)} %get-tuple-element.33.refs_0_.refs_3_), channel_id=1, source_target_pairs={{0,1},{1,0},{2,3},{3,2},{4,5},{5,4},{6,7},{7,6},{8,9},{9,8},{10,11... | collective-permute-start | bytes 2064392 | tf_op jit(solution)/shard_map/ppermute | solution.py:55
  4.2 1.9 %collective-permute-start.1 = (bf16[384,128]{1,0:T(8,128)(2,1)S(1)}, bf16[384,128]{1,0:T(8,128)(2,1)S(1)}, u32[]{:S(2)}, u32[]{:S(2)}) collective-permute-start(bf16[384,128]{1,0:T(8,128)(2,1)S(1)} %get-tuple-element.35.refs_0_), channel_id=1, source_target_pairs={{0,1},{1,0},{2,3},{3,2},{4,5},{5,4},{6,7},{7,6},{8,9},{9,8},{10,11... | collective-permute-start | bytes 294920 | tf_op jit(solution)/shard_map/ppermute | solution.py:55
  6.4 6.3 %collective-permute-start.3 = (bf16[384,128]{1,0:T(8,128)(2,1)S(1)}, bf16[384,128]{1,0:T(8,128)(2,1)S(1)}, u32[]{:S(2)}, u32[]{:S(2)}) collective-permute-start(bf16[384,128]{1,0:T(8,128)(2,1)S(1)} %level1_0.1.refs_3_.refs_0_), channel_id=1, source_target_pairs={{0,2},{1,3},{2,0},{3,1},{4,6},{5,7},{6,4},{7,5},{8,10},{9,11},{10,... | collective-permute-start | bytes 294920 | tf_op jit(solution)/shard_map/ppermute | solution.py:55
  9.8 11.1 %collective-permute-start.2 = (bf16[384,256]{1,0:T(8,128)(2,1)S(1)}, bf16[384,256]{1,0:T(8,128)(2,1)S(1)}, u32[]{:S(2)}, u32[]{:S(2)}) collective-permute-start(bf16[384,256]{1,0:T(8,128)(2,1)S(1)} %level1_1.1.refs_6_.refs_0_), channel_id=1, source_target_pairs={{0,2},{1,3},{2,0},{3,1},{4,6},{5,7},{6,4},{7,5},{8,10},{9,11},{10,... | collective-permute-start | bytes 589832 | tf_op jit(solution)/shard_map/ppermute | solution.py:55
  13.4 8.3 %collective-permute-start.6 = (bf16[384,128]{1,0:T(8,128)(2,1)S(1)}, bf16[384,128]{1,0:T(8,128)(2,1)S(1)}, u32[]{:S(2)}, u32[]{:S(2)}) collective-permute-start(bf16[384,128]{1,0:T(8,128)(2,1)S(1)} %get-tuple-element.37.refs_3_.refs_0_), channel_id=1, source_target_pairs={{0,4},{1,5},{2,6},{3,7},{4,0},{5,1},{6,2},{7,3},{8,12},{9,13},{10,... | collective-permute-start | bytes 294920 | tf_op jit(solution)/shard_map/ppermute | solution.py:55
  16.4 12.5 %collective-permute-start.5 = (bf16[384,384]{1,0:T(8,128)(2,1)S(1)}, bf16[384,384]{1,0:T(8,128)(2,1)S(1)}, u32[]{:S(2)}, u32[]{:S(2)}) collective-permute-start(bf16[384,384]{1,0:T(8,128)(2,1)S(1)} %get-tuple-element.40.refs_0_), channel_id=1, source_target_pairs={{0,2},{1,3},{2,0},{3,1},{4,6},{5,7},{6,4},{7,5},{8,10},{9,11},{10,... | collective-permute-start | bytes 884744 | tf_op jit(solution)/shard_map/ppermute | solution.py:55
  21.3 11.2 %collective-permute-start.4 = (bf16[384,256]{1,0:T(8,128)(2,1)S(1)}, bf16[384,256]{1,0:T(8,128)(2,1)S(1)}, u32[]{:S(2)}, u32[]{:S(2)}) collective-permute-start(bf16[384,256]{1,0:T(8,128)(2,1)S(1)} %level2_1.1.refs_3_.refs_0_), channel_id=1, source_target_pairs={{0,4},{1,5},{2,6},{3,7},{4,0},{5,1},{6,2},{7,3},{8,12},{9,13},{10,... | collective-permute-start | bytes 589832 | tf_op jit(solution)/shard_map/ppermute | solution.py:55
  22.0 1.4 %collective-permute-start.7 = (bf16[384,128]{1,0:T(8,128)(2,1)S(1)}, bf16[384,128]{1,0:T(8,128)(2,1)S(1)}, u32[]{:S(2)}, u32[]{:S(2)}) collective-permute-start(bf16[384,128]{1,0:T(8,128)(2,1)S(1)} %level3_0.1.refs_0_), channel_id=1, source_target_pairs={{0,1},{1,0},{2,3},{3,2},{4,5},{5,4},{6,7},{7,6},{8,9},{9,8},{10,11... | collective-permute-start | bytes 294920 | tf_op jit(solution)/shard_map/ppermute | solution.py:55
  24.0 8.9 %collective-permute-start.8 = (bf16[512,128]{1,0:T(8,128)(2,1)S(1)}, bf16[512,128]{1,0:T(8,128)(2,1)S(1)}, u32[]{:S(2)}, u32[]{:S(2)}) collective-permute-start(bf16[512,128]{1,0:T(8,128)(2,1)S(1)} %get-tuple-element.43), channel_id=1, source_target_pairs={{0,16},{8,24},{16,0},{24,8},{1,17},{9,25},{17,1},{25,9},{2,18},{10... | collective-permute-start | bytes 393224 | tf_op jit(solution)/shard_map/ppermute | solution.py:55
  29.5 19.4 %collective-permute-start.13 = (bf16[384,384]{1,0:T(8,128)(2,1)S(1)}, bf16[384,384]{1,0:T(8,128)(2,1)S(1)}, u32[]{:S(2)}, u32[]{:S(2)}) collective-permute-start(bf16[384,384]{1,0:T(8,128)(2,1)S(1)} %level2_2.1.refs_3_.refs_0_), channel_id=1, source_target_pairs={{0,4},{1,5},{2,6},{3,7},{4,0},{5,1},{6,2},{7,3},{8,12},{9,13},{10,... | collective-permute-start | bytes 884744 | tf_op jit(solution)/shard_map/ppermute | solution.py:55
  32.9 1.9 %collective-permute-start.10 = (bf16[384,256]{1,0:T(8,128)(2,1)S(1)}, bf16[384,256]{1,0:T(8,128)(2,1)S(1)}, u32[]{:S(2)}, u32[]{:S(2)}) collective-permute-start(bf16[384,256]{1,0:T(8,128)(2,1)S(1)} %level3_1.1.refs_0_), channel_id=1, source_target_pairs={{0,1},{1,0},{2,3},{3,2},{4,5},{5,4},{6,7},{7,6},{8,9},{9,8},{10,11... | collective-permute-start | bytes 589832 | tf_op jit(solution)/shard_map/ppermute | solution.py:55
  33.2 5.2 %collective-permute-start.9 = (bf16[256,128]{1,0:T(8,128)(2,1)S(1)}, bf16[256,128]{1,0:T(8,128)(2,1)S(1)}, u32[]{:S(2)}, u32[]{:S(2)}) collective-permute-start(bf16[256,128]{1,0:T(8,128)(2,1)S(1)} %get-tuple-element.45), channel_id=1, source_target_pairs={{0,8},{8,0},{16,24},{24,16},{1,9},{9,1},{17,25},{25,17},{2,10},{10... | collective-permute-start | bytes 196616 | tf_op jit(solution)/shard_map/ppermute | solution.py:55
  36.0 11.9 %collective-permute-start.11 = (bf16[384,256]{1,0:T(8,128)(2,1)S(1)}, bf16[384,256]{1,0:T(8,128)(2,1)S(1)}, u32[]{:S(2)}, u32[]{:S(2)}) collective-permute-start(bf16[384,256]{1,0:T(8,128)(2,1)S(1)} %level1_3.1.refs_2_.refs_0_), channel_id=1, source_target_pairs={{0,2},{1,3},{2,0},{3,1},{4,6},{5,7},{6,4},{7,5},{8,10},{9,11},{10,... | collective-permute-start | bytes 589832 | tf_op jit(solution)/shard_map/ppermute | solution.py:55
  37.3 12.5 %collective-permute-start.15 = (bf16[512,256]{1,0:T(8,128)(2,1)S(1)}, bf16[512,256]{1,0:T(8,128)(2,1)S(1)}, u32[]{:S(2)}, u32[]{:S(2)}) collective-permute-start(bf16[512,256]{1,0:T(8,128)(2,1)S(1)} %get-tuple-element.49), channel_id=1, source_target_pairs={{0,8},{8,0},{16,24},{24,16},{1,9},{9,1},{17,25},{25,17},{2,10},{10... | collective-permute-start | bytes 786440 | tf_op jit(solution)/shard_map/ppermute | solution.py:55
  48.2 11.2 %collective-permute-start.12 = (bf16[384,256]{1,0:T(8,128)(2,1)S(1)}, bf16[384,256]{1,0:T(8,128)(2,1)S(1)}, u32[]{:S(2)}, u32[]{:S(2)}) collective-permute-start(bf16[384,256]{1,0:T(8,128)(2,1)S(1)} %level2_3.1.refs_3_.refs_0_), channel_id=1, source_target_pairs={{0,4},{1,5},{2,6},{3,7},{4,0},{5,1},{6,2},{7,3},{8,12},{9,13},{10,... | collective-permute-start | bytes 589832 | tf_op jit(solution)/shard_map/ppermute | solution.py:55
  49.4 2.1 %collective-permute-start.14 = (bf16[384,384]{1,0:T(8,128)(2,1)S(1)}, bf16[384,384]{1,0:T(8,128)(2,1)S(1)}, u32[]{:S(2)}, u32[]{:S(2)}) collective-permute-start(bf16[384,384]{1,0:T(8,128)(2,1)S(1)} %level3_2.1.refs_0_), channel_id=1, source_target_pairs={{0,1},{1,0},{2,3},{3,2},{4,5},{5,4},{6,7},{7,6},{8,9},{9,8},{10,11... | collective-permute-start | bytes 884744 | tf_op jit(solution)/shard_map/ppermute | solution.py:55
  49.9 10.0 %collective-permute-start.16 = (bf16[256,256]{1,0:T(8,128)(2,1)S(1)}, bf16[256,256]{1,0:T(8,128)(2,1)S(1)}, u32[]{:S(2)}, u32[]{:S(2)}) collective-permute-start(bf16[256,256]{1,0:T(8,128)(2,1)S(1)} %get-tuple-element.51), channel_id=1, source_target_pairs={{0,16},{8,24},{16,0},{24,8},{1,17},{9,25},{17,1},{25,9},{2,18},{10... | collective-permute-start | bytes 393224 | tf_op jit(solution)/shard_map/ppermute | solution.py:55
  52.7 11.9 %collective-permute-start.17 = (bf16[256,384]{1,0:T(8,128)(2,1)S(1)}, bf16[256,384]{1,0:T(8,128)(2,1)S(1)}, u32[]{:S(2)}, u32[]{:S(2)}) collective-permute-start(bf16[256,384]{1,0:T(8,128)(2,1)S(1)} %get-tuple-element.53), channel_id=1, source_target_pairs={{0,24},{8,16},{16,8},{24,0},{1,25},{9,17},{17,9},{25,1},{2,26},{10... | collective-permute-start | bytes 589832 | tf_op jit(solution)/shard_map/ppermute | solution.py:55
  54.3 11.4 %collective-permute-start.18 = (bf16[256,384]{1,0:T(8,128)(2,1)S(1)}, bf16[256,384]{1,0:T(8,128)(2,1)S(1)}, u32[]{:S(2)}, u32[]{:S(2)}) collective-permute-start(bf16[256,384]{1,0:T(8,128)(2,1)S(1)} %get-tuple-element.54), channel_id=1, source_target_pairs={{0,16},{8,24},{16,0},{24,8},{1,17},{9,25},{17,1},{25,9},{2,18},{10... | collective-permute-start | bytes 589832 | tf_op jit(solution)/shard_map/ppermute | solution.py:55
  55.2 10.4 %collective-permute-start.19 = (bf16[256,384]{1,0:T(8,128)(2,1)S(1)}, bf16[256,384]{1,0:T(8,128)(2,1)S(1)}, u32[]{:S(2)}, u32[]{:S(2)}) collective-permute-start(bf16[256,384]{1,0:T(8,128)(2,1)S(1)} %get-tuple-element.55), channel_id=1, source_target_pairs={{0,8},{8,0},{16,24},{24,16},{1,9},{9,1},{17,25},{25,17},{2,10},{10... | collective-permute-start | bytes 589832 | tf_op jit(solution)/shard_map/ppermute | solution.py:55
  59.8 1.5 %collective-permute-start.20 = (bf16[384,256]{1,0:T(8,128)(2,1)S(1)}, bf16[384,256]{1,0:T(8,128)(2,1)S(1)}, u32[]{:S(2)}, u32[]{:S(2)}) collective-permute-start(bf16[384,256]{1,0:T(8,128)(2,1)S(1)} %level3_3.1.refs_0_), channel_id=1, source_target_pairs={{0,1},{1,0},{2,3},{3,2},{4,5},{5,4},{6,7},{7,6},{8,9},{9,8},{10,11... | collective-permute-start | bytes 589832 | tf_op jit(solution)/shard_map/ppermute | solution.py:55
  62.1 7.3 %collective-permute-start.21 = (bf16[256,256]{1,0:T(8,128)(2,1)S(1)}, bf16[256,256]{1,0:T(8,128)(2,1)S(1)}, u32[]{:S(2)}, u32[]{:S(2)}) collective-permute-start(bf16[256,256]{1,0:T(8,128)(2,1)S(1)} %get-tuple-element.58), channel_id=1, source_target_pairs={{0,24},{8,16},{16,8},{24,0},{1,25},{9,17},{17,9},{25,1},{2,26},{10... | collective-permute-start | bytes 393224 | tf_op jit(solution)/shard_map/ppermute | solution.py:55
  64.1 7.4 %collective-permute-start.22 = (bf16[256,256]{1,0:T(8,128)(2,1)S(1)}, bf16[256,256]{1,0:T(8,128)(2,1)S(1)}, u32[]{:S(2)}, u32[]{:S(2)}) collective-permute-start(bf16[256,256]{1,0:T(8,128)(2,1)S(1)} %get-tuple-element.59), channel_id=1, source_target_pairs={{0,16},{8,24},{16,0},{24,8},{1,17},{9,25},{17,1},{25,9},{2,18},{10... | collective-permute-start | bytes 393224 | tf_op jit(solution)/shard_map/ppermute | solution.py:55
  64.6 7.0 %collective-permute-start.23 = (bf16[256,256]{1,0:T(8,128)(2,1)S(1)}, bf16[256,256]{1,0:T(8,128)(2,1)S(1)}, u32[]{:S(2)}, u32[]{:S(2)}) collective-permute-start(bf16[256,256]{1,0:T(8,128)(2,1)S(1)} %get-tuple-element.60), channel_id=1, source_target_pairs={{0,8},{8,0},{16,24},{24,16},{1,9},{9,1},{17,25},{25,17},{2,10},{10... | collective-permute-start | bytes 393224 | tf_op jit(solution)/shard_map/ppermute | solution.py:55

commit v11 on v6

--- a/solution.py
+++ b/solution.py
@@ -176,6 +176,10 @@
     send[...] = (keep[rows:] + got[rows:].astype(F32)).astype(BF16)
 
 
+def sum_kernel(keep, got, total):
+    total[...] = (keep[...] + got[...].astype(F32)).astype(BF16)
+
+
 def end_kernel(places, counts, *refs):
     refs = list(refs)
     out = refs[-1]
@@ -360,16 +364,30 @@
 
     out0, _ = tail(0, [coeff3[1]], False)
     fold0 = begin_sum(0, out0)
-    value, ahead = step("level2_2", [(2, 2, coeff2[2], near2[2]), job1(3)], [out0[0]])
+    (value,) = step("level2_2", [(2, 2, coeff2[2], near2[2])], [out0[0]])
     third(2, value)
-    second(3, ahead)
-    out1, (send0, keep0) = tail(1, [coeff3[2]], False, fold0)
-    got0 = partner(send0, "blk", halving(0)[0][-1])
+    (value,) = step("level1_3", [job1(3)], [coeff3[2]])
+    second(3, value)
+    def fold(held, after=()):
+        at, keep, got, count = held
+        send, keep = call(
+            fold_kernel,
+            f"fold_{at}",
+            [VMEM] * 2,
+            [result(at, count // 2, BF16), result(at, count // 2, F32)],
+            [],
+            [here(keep), here(got)],
+            after,
+        )
+        return keep, partner(send, "blk", halving(at)[0][-1])
+
+    out1, _ = tail(1, [coeff2[3]], False)
     fold1 = begin_sum(1, out1)
-    (value,) = step("level2_3", [(2, 3, coeff2[3], near2[3])], [out1[0]])
+    keep0, got0 = fold(fold0, [out1[0]])
+    keep1, got1 = fold(fold1, [keep0])
+    (value,) = step("level2_3", [(2, 3, coeff2[3], near2[3])], [keep1])
     third(3, value)
-    out2, (send1, keep1, total0) = tail(2, [coeff3[3]], True, fold1, (0, keep0, got0))
-    got1 = partner(send1, "blk", halving(1)[0][-1])
+    out2, (total0,) = tail(2, [coeff3[3]], True, None, (0, keep0, got0))
     group2 = direct_sum(out2)
     out3, (total1,) = tail(3, [out2[0]], True, None, (1, keep1, got1))
     group3 = direct_sum(out3)

time: 75.2 us -> 70.9 us (0.943)
  waiting for transfers between devices: 30.9 us -> 28 us
  starting transfers between devices: 27.9 us -> 26.3 us
    ppermute x24, waiting for transfers between devices: 30.9 us -> 28 us  [partner(): return lax.ppermute(value, axis, pairs)]
    ppermute x24, starting transfers between devices: 27.9 us -> 26.3 us  [partner(): return lax.ppermute(value, axis, pairs)]
    pallas_call x20 -> x23, Pallas kernels: 15 us -> 15.3 us  [call(): pl.pallas_call(body, name=name, in_specs=[*in_specs, *[ANY] * len(after)]...]
  transfers between devices with their start and end apart: 24 -> 24, of which waited for: 10 -> 11; matrix products, arithmetic and copies ran while one was open for 0% -> 0% of each run, Pallas kernels for 15% -> 16%
where the time goes in v11:
time: 70.9 us; the launch traced here: 70.8 us
  waiting for transfers between devices  28 us (39%)
  starting transfers between devices  26.3 us (37%)
  Pallas kernels  16.2 us (23%)
    ppermute x24, waiting for transfers between devices, partner(): return lax.ppermute(value, axis, pairs)  28 us
    ppermute x24, starting transfers between devices, partner(): return lax.ppermute(value, axis, pairs)  26.3 us
    pallas_call x23, Pallas kernels, call(): pl.pallas_call(body, name=name, in_specs=[*in_specs, *[ANY] * len(after)]...  15.3 us
  transfers between devices with their start and end apart: 24, of which 11 were waited for; matrix products, arithmetic and copies ran while one was open for 0% of the time, Pallas kernels for 16%

profile of v11, /device:TPU:0, one launch (start us, length us, event | category | flops | bytes accessed | tf_op | source)
XLA Modules:
  0.0 70.8 jit_solution(17068137736053628564)
XLA Ops:
  0.0 3.7 %leaf.1 = (bf16[384,128]{1,0:T(8,128)(2,1)S(1)}, bf16[384,896]{1,0:T(8,128)(2,1)S(1)}, bf16[2,384,768]{2,1,0:T(8,128)(2,1)S(1)}, bf16[2,384,768]{2,1,0:T(8,128)(2,1)S(1)}) custom-call(bf16[2,1024,512]{2,1,0:T(8,128)(2,1)} %bitcast.9, bf16[2,384,1024]{2,1,0:T(8,128)(2,1)} %bitcast.10, bf16[5,2,384,768]{3,2,1,0:T(8,128)(2,1)} %bitcast.7, s32[2,5]{1,0:T(2,128)} %bitcast.12), custom_call_target="tpu_custom_call" | custom-call | flops 6000000000 | tf_op jit(solution)/shard_map/leaf/pallas_call | solution.py:41
  3.7 0.5 collective-permute-start.2
  4.3 1.8 %collective-permute-done.refs_1_ = bf16[384,128]{1,0:T(8,128)(2,1)S(1)} collective-permute-done((bf16[384,128]{1,0:T(8,128)(2,1)S(1)}, bf16[384,128]{1,0:T(8,128)(2,1)S(1)}, u32[]{:S(2)}, u32[]{:S(2)}) %collective-permute-start) | collective-permute-done | bytes 98336 | tf_op jit(solution)/shard_map/ppermute | solution.py:55
  6.1 0.3 level1_0.1.refs_3_.refs_0_
  6.4 3.0 %collective-permute-start.1 = (bf16[384,128]{1,0:T(8,128)(2,1)S(1)}, bf16[384,128]{1,0:T(8,128)(2,1)S(1)}, u32[]{:S(2)}, u32[]{:S(2)}) collective-permute-start(bf16[384,128]{1,0:T(8,128)(2,1)S(1)} %level1_0.1.refs_3_.refs_0_), channel_id=1, source_target_pairs={{0,2},{1,3},{2,0},{3,1},{4,6},{5,7},{6,4},{7,5},{8,10},{9,11},{10,... | collective-permute-start | bytes 294920 | tf_op jit(solution)/shard_map/ppermute | solution.py:55
  9.5 0.4 level1_1.1.refs_6_.refs_0_
  9.9 2.8 %collective-permute-done.1.refs_1_ = bf16[384,128]{1,0:T(8,128)(2,1)S(1)} collective-permute-done((bf16[384,128]{1,0:T(8,128)(2,1)S(1)}, bf16[384,128]{1,0:T(8,128)(2,1)S(1)}, u32[]{:S(2)}, u32[]{:S(2)}) %collective-permute-start.1) | collective-permute-done | bytes 98336 | tf_op jit(solution)/shard_map/ppermute | solution.py:55
  12.7 0.7 level2_0.1
  13.4 3.0 %collective-permute-start.4 = (bf16[384,128]{1,0:T(8,128)(2,1)S(1)}, bf16[384,128]{1,0:T(8,128)(2,1)S(1)}, u32[]{:S(2)}, u32[]{:S(2)}) collective-permute-start(bf16[384,128]{1,0:T(8,128)(2,1)S(1)} %get-tuple-element.39.refs_3_.refs_0_), channel_id=1, source_target_pairs={{0,4},{1,5},{2,6},{3,7},{4,0},{5,1},{6,2},{7,3},{8,12},{9,13},{10,... | collective-permute-start | bytes 294920 | tf_op jit(solution)/shard_map/ppermute | solution.py:55
  16.4 2.0 %collective-permute-start.3 = (bf16[384,384]{1,0:T(8,128)(2,1)S(1)}, bf16[384,384]{1,0:T(8,128)(2,1)S(1)}, u32[]{:S(2)}, u32[]{:S(2)}) collective-permute-start(bf16[384,384]{1,0:T(8,128)(2,1)S(1)} %get-tuple-element.38.refs_0_), channel_id=1, source_target_pairs={{0,2},{1,3},{2,0},{3,1},{4,6},{5,7},{6,4},{7,5},{8,10},{9,11},{10,... | collective-permute-start | bytes 884744 | tf_op jit(solution)/shard_map/ppermute | solution.py:55
  18.4 2.5 %prefetch.1 = (bf16[2,384,768]{2,1,0:T(8,128)(2,1)S(1)}, bf16[2,384,768]{2,1,0:T(8,128)(2,1)S(1)}, bf16[2,1024,384]{2,1,0:T(8,128)(2,1)S(1)}) custom-call(bf16[5,2,384,768]{3,2,1,0:T(8,128)(2,1)} %bitcast.8, bf16[2,1024,384]{2,1,0:T(8,128)(2,1)} %bitcast.11, s32[2,5]{1,0:T(2,128)} %bitcast.13, bf16[384,128]{1,0:T(8,128)(2,1)S(1)} %get-tuple-element.39.refs_3_.refs_0_), custom_call_target="tpu_custom_call" | custom-call | flops 6000000000 | tf_op jit(solution)/shard_map/prefetch/pallas_call | solution.py:41
  20.9 0.4 level2_1.1.refs_3_.refs_0_
  21.3 0.4 collective-permute-start.9
  21.7 0.3 level3_0.1.refs_0_
  22.3 1.0 %collective-permute-done.6.refs_1_ = bf16[384,128]{1,0:T(8,128)(2,1)S(1)} collective-permute-done((bf16[384,128]{1,0:T(8,128)(2,1)S(1)}, bf16[384,128]{1,0:T(8,128)(2,1)S(1)}, u32[]{:S(2)}, u32[]{:S(2)}) %collective-permute-start.6) | collective-permute-done | bytes 98336 | tf_op jit(solution)/shard_map/ppermute | solution.py:55
  23.4 0.6 last_0.1
  24.0 1.6 %collective-permute-start.12 = (bf16[512,128]{1,0:T(8,128)(2,1)S(1)}, bf16[512,128]{1,0:T(8,128)(2,1)S(1)}, u32[]{:S(2)}, u32[]{:S(2)}) collective-permute-start(bf16[512,128]{1,0:T(8,128)(2,1)S(1)} %get-tuple-element.46), channel_id=1, source_target_pairs={{0,16},{8,24},{16,0},{24,8},{1,17},{9,25},{17,1},{25,9},{2,18},{10... | collective-permute-start | bytes 393224 | tf_op jit(solution)/shard_map/ppermute | solution.py:55
  25.6 3.4 %collective-permute-done.3.refs_1_ = bf16[384,384]{1,0:T(8,128)(2,1)S(1)} collective-permute-done((bf16[384,384]{1,0:T(8,128)(2,1)S(1)}, bf16[384,384]{1,0:T(8,128)(2,1)S(1)}, u32[]{:S(2)}, u32[]{:S(2)}) %collective-permute-start.3) | collective-permute-done | bytes 294944 | tf_op jit(solution)/shard_map/ppermute | solution.py:55
  29.0 0.5 level2_2.1.refs_3_.refs_0_
  29.5 1.8 %collective-permute-start.7 = (bf16[384,384]{1,0:T(8,128)(2,1)S(1)}, bf16[384,384]{1,0:T(8,128)(2,1)S(1)}, u32[]{:S(2)}, u32[]{:S(2)}) collective-permute-start(bf16[384,384]{1,0:T(8,128)(2,1)S(1)} %level2_2.1.refs_3_.refs_0_), channel_id=1, source_target_pairs={{0,4},{1,5},{2,6},{3,7},{4,0},{5,1},{6,2},{7,3},{8,12},{9,13},{10,... | collective-permute-start | bytes 884744 | tf_op jit(solution)/shard_map/ppermute | solution.py:55
  31.3 0.4 level1_3.1.refs_3_.refs_0_
  31.7 2.5 %collective-permute-start.8 = (bf16[384,256]{1,0:T(8,128)(2,1)S(1)}, bf16[384,256]{1,0:T(8,128)(2,1)S(1)}, u32[]{:S(2)}, u32[]{:S(2)}) collective-permute-start(bf16[384,256]{1,0:T(8,128)(2,1)S(1)} %level1_3.1.refs_3_.refs_0_), channel_id=1, source_target_pairs={{0,2},{1,3},{2,0},{3,1},{4,6},{5,7},{6,4},{7,5},{8,10},{9,11},{10,... | collective-permute-start | bytes 589832 | tf_op jit(solution)/shard_map/ppermute | solution.py:55
  34.2 0.4 level3_1.1.refs_0_
  34.7 0.3 between_1.1.refs_0_
  34.9 1.2 %collective-permute-done.10.refs_1_ = bf16[384,256]{1,0:T(8,128)(2,1)S(1)} collective-permute-done((bf16[384,256]{1,0:T(8,128)(2,1)S(1)}, bf16[384,256]{1,0:T(8,128)(2,1)S(1)}, u32[]{:S(2)}, u32[]{:S(2)}) %collective-permute-start.10) | collective-permute-done | bytes 196640 | tf_op jit(solution)/shard_map/ppermute | solution.py:55
  36.1 0.8 %last_1.1 = (f32[512,256]{1,0:T(8,128)S(1)}, bf16[512,256]{1,0:T(8,128)(2,1)S(1)}) custom-call(f32[384,256]{1,0:T(8,128)S(1)} %between_1.1.refs_0_, bf16[384,256]{1,0:T(8,128)(2,1)S(1)} %collective-permute-done.10.refs_1_, bf16[2,384,768]{2,1,0:T(8,128)(2,1)S(1)} %get-tuple-element.42.refs_1_.refs_2_, bf16[2,1024,384]{2,1,0:T(8,128)(2,1)S(1)} %get-tuple-element.41.refs_3_), custom_call_target="tpu_custom_call" | custom-call | flops 6000000000 | tf_op jit(solution)/shard_map/last_1/pallas_call | solution.py:41
  36.9 1.6 %collective-permute-start.11 = (bf16[512,256]{1,0:T(8,128)(2,1)S(1)}, bf16[512,256]{1,0:T(8,128)(2,1)S(1)}, u32[]{:S(2)}, u32[]{:S(2)}) collective-permute-start(bf16[512,256]{1,0:T(8,128)(2,1)S(1)} %get-tuple-element.45), channel_id=1, source_target_pairs={{0,8},{8,0},{16,24},{24,16},{1,9},{9,1},{17,25},{25,17},{2,10},{10... | collective-permute-start | bytes 786440 | tf_op jit(solution)/shard_map/ppermute | solution.py:55
  38.5 0.6 collective-permute-start.13
  39.1 6.9 %collective-permute-done.11.refs_1_ = bf16[512,256]{1,0:T(8,128)(2,1)S(1)} collective-permute-done((bf16[512,256]{1,0:T(8,128)(2,1)S(1)}, bf16[512,256]{1,0:T(8,128)(2,1)S(1)}, u32[]{:S(2)}, u32[]{:S(2)}) %collective-permute-start.11) | collective-permute-done | bytes 262176 | tf_op jit(solution)/shard_map/ppermute | solution.py:55
  46.1 1.6 %collective-permute-start.16 = (bf16[256,256]{1,0:T(8,128)(2,1)S(1)}, bf16[256,256]{1,0:T(8,128)(2,1)S(1)}, u32[]{:S(2)}, u32[]{:S(2)}) collective-permute-start(bf16[256,256]{1,0:T(8,128)(2,1)S(1)} %get-tuple-element.53), channel_id=1, source_target_pairs={{0,16},{8,24},{16,0},{24,8},{1,17},{9,25},{17,1},{25,9},{2,18},{10... | collective-permute-start | bytes 393224 | tf_op jit(solution)/shard_map/ppermute | solution.py:55
  47.7 0.4 level2_3.1.refs_3_.refs_0_
  48.1 0.5 level3_2.1.refs_0_
  48.7 0.3 between_2.1
  49.1 1.2 %collective-permute-done.15.refs_1_ = bf16[384,384]{1,0:T(8,128)(2,1)S(1)} collective-permute-done((bf16[384,384]{1,0:T(8,128)(2,1)S(1)}, bf16[384,384]{1,0:T(8,128)(2,1)S(1)}, u32[]{:S(2)}, u32[]{:S(2)}) %collective-permute-start.15) | collective-permute-done | bytes 294944 | tf_op jit(solution)/shard_map/ppermute | solution.py:55
  50.3 1.2 %last_2.1 = (f32[256,384]{1,0:T(8,128)S(1)}, bf16[256,384]{1,0:T(8,128)(2,1)S(1)}, bf16[256,384]{1,0:T(8,128)(2,1)S(1)}, bf16[256,384]{1,0:T(8,128)(2,1)S(1)}) custom-call(f32[384,384]{1,0:T(8,128)S(1)} %get-tuple-element.51.refs_0_, bf16[384,384]{1,0:T(8,128)(2,1)S(1)} %collective-permute-done.15.refs_1_, ...), custom_call_target="tpu_custom_call" | custom-call | flops 6000000000 | tf_op jit(solution)/shard_map/last_2/pallas_call | solution.py:41
  51.5 1.5 %collective-permute-start.17 = (bf16[256,384]{1,0:T(8,128)(2,1)S(1)}, bf16[256,384]{1,0:T(8,128)(2,1)S(1)}, u32[]{:S(2)}, u32[]{:S(2)}) collective-permute-start(bf16[256,384]{1,0:T(8,128)(2,1)S(1)} %get-tuple-element.55), channel_id=1, source_target_pairs={{0,24},{8,16},{16,8},{24,0},{1,25},{9,17},{17,9},{25,1},{2,26},{10... | collective-permute-start | bytes 589832 | tf_op jit(solution)/shard_map/ppermute | solution.py:55
  53.0 1.5 %collective-permute-start.18 = (bf16[256,384]{1,0:T(8,128)(2,1)S(1)}, bf16[256,384]{1,0:T(8,128)(2,1)S(1)}, u32[]{:S(2)}, u32[]{:S(2)}) collective-permute-start(bf16[256,384]{1,0:T(8,128)(2,1)S(1)} %get-tuple-element.56), channel_id=1, source_target_pairs={{0,16},{8,24},{16,0},{24,8},{1,17},{9,25},{17,1},{25,9},{2,18},{10... | collective-permute-start | bytes 589832 | tf_op jit(solution)/shard_map/ppermute | solution.py:55
  54.6 0.5 collective-permute-start.19
  55.1 2.7 %collective-permute-done.14.refs_1_ = bf16[384,256]{1,0:T(8,128)(2,1)S(1)} collective-permute-done((bf16[384,256]{1,0:T(8,128)(2,1)S(1)}, bf16[384,256]{1,0:T(8,128)(2,1)S(1)}, u32[]{:S(2)}, u32[]{:S(2)}) %collective-permute-start.14) | collective-permute-done | bytes 196640 | tf_op jit(solution)/shard_map/ppermute | solution.py:55
  57.8 0.4 level3_3.1.refs_0_
  58.5 1.2 %collective-permute-done.20.refs_1_ = bf16[384,256]{1,0:T(8,128)(2,1)S(1)} collective-permute-done((bf16[384,256]{1,0:T(8,128)(2,1)S(1)}, bf16[384,256]{1,0:T(8,128)(2,1)S(1)}, u32[]{:S(2)}, u32[]{:S(2)}) %collective-permute-start.20) | collective-permute-done | bytes 196640 | tf_op jit(solution)/shard_map/ppermute | solution.py:55
  59.7 0.8 %last_3.1 = (f32[256,256]{1,0:T(8,128)S(1)}, bf16[256,256]{1,0:T(8,128)(2,1)S(1)}, bf16[256,256]{1,0:T(8,128)(2,1)S(1)}, bf16[256,256]{1,0:T(8,128)(2,1)S(1)}) custom-call(f32[384,256]{1,0:T(8,128)S(1)} %get-tuple-element.58.refs_0_, bf16[384,256]{1,0:T(8,128)(2,1)S(1)} %collective-permute-done.20.refs_1_, ...), custom_call_target="tpu_custom_call" | custom-call | flops 6000000000 | tf_op jit(solution)/shard_map/last_3/pallas_call | solution.py:41
  60.5 1.5 %collective-permute-start.21 = (bf16[256,256]{1,0:T(8,128)(2,1)S(1)}, bf16[256,256]{1,0:T(8,128)(2,1)S(1)}, u32[]{:S(2)}, u32[]{:S(2)}) collective-permute-start(bf16[256,256]{1,0:T(8,128)(2,1)S(1)} %get-tuple-element.60), channel_id=1, source_target_pairs={{0,24},{8,16},{16,8},{24,0},{1,25},{9,17},{17,9},{25,1},{2,26},{10... | collective-permute-start | bytes 393224 | tf_op jit(solution)/shard_map/ppermute | solution.py:55
  62.0 1.5 %collective-permute-start.22 = (bf16[256,256]{1,0:T(8,128)(2,1)S(1)}, bf16[256,256]{1,0:T(8,128)(2,1)S(1)}, u32[]{:S(2)}, u32[]{:S(2)}) collective-permute-start(bf16[256,256]{1,0:T(8,128)(2,1)S(1)} %get-tuple-element.61), channel_id=1, source_target_pairs={{0,16},{8,24},{16,0},{24,8},{1,17},{9,25},{17,1},{25,9},{2,18},{10... | collective-permute-start | bytes 393224 | tf_op jit(solution)/shard_map/ppermute | solution.py:55
  63.5 0.5 collective-permute-start.23
  64.1 3.8 %collective-permute-done.21.refs_7_ = bf16[256,256]{1,0:T(8,128)(2,1)S(1)} collective-permute-done((bf16[256,256]{1,0:T(8,128)(2,1)S(1)}, bf16[256,256]{1,0:T(8,128)(2,1)S(1)}, u32[]{:S(2)}, u32[]{:S(2)}) %collective-permute-start.21) | collective-permute-done | bytes 131104 | tf_op jit(solution)/shard_map/ppermute | solution.py:55
  67.8 2.0 %collective-permute-done.22.refs_8_ = bf16[256,256]{1,0:T(8,128)(2,1)S(1)} collective-permute-done((bf16[256,256]{1,0:T(8,128)(2,1)S(1)}, bf16[256,256]{1,0:T(8,128)(2,1)S(1)}, u32[]{:S(2)}, u32[]{:S(2)}) %collective-permute-start.22) | collective-permute-done | bytes 131104 | tf_op jit(solution)/shard_map/ppermute | solution.py:55
  69.8 1.0 %end.1 = bf16[2,256,512]{2,1,0:T(8,128)(2,1)} custom-call(bf16[256,128]{1,0:T(8,128)(2,1)S(1)} %get-tuple-element.50.refs_0_, bf16[256,256]{1,0:T(8,128)(2,1)S(1)} %get-tuple-element.54.refs_1_, f32[256,384]{1,0:T(8,128)S(1)} %get-tuple-element.52.refs_3_.refs_2_, bf16[256,384]{1,0:T(8,128)(2,1)S(1)} %collective-permute-done.17.refs_3_, ...), custom_call_target="tpu_custom_call" | custom-call | tf_op jit(solution)/shard_map/end/pallas_call | solution.py:396
  (24 shorter events, 1.1 us)
Async XLA Ops:
  3.7 5.8 %collective-permute-start.2 = (bf16[384,896]{1,0:T(8,128)(2,1)S(1)}, bf16[384,896]{1,0:T(8,128)(2,1)S(1)}, u32[]{:S(2)}, u32[]{:S(2)}) collective-permute-start(bf16[384,896]{1,0:T(8,128)(2,1)S(1)} %get-tuple-element.37.refs_0_.refs_3_), channel_id=1, source_target_pairs={{0,1},{1,0},{2,3},{3,2},{4,5},{5,4},{6,7},{7,6},{8,9},{9,8},{10,11... | collective-permute-start | bytes 2064392 | tf_op jit(solution)/shard_map/ppermute | solution.py:55
  4.2 1.9 %collective-permute-start = (bf16[384,128]{1,0:T(8,128)(2,1)S(1)}, bf16[384,128]{1,0:T(8,128)(2,1)S(1)}, u32[]{:S(2)}, u32[]{:S(2)}) collective-permute-start(bf16[384,128]{1,0:T(8,128)(2,1)S(1)} %get-tuple-element.34.refs_0_), channel_id=1, source_target_pairs={{0,1},{1,0},{2,3},{3,2},{4,5},{5,4},{6,7},{7,6},{8,9},{9,8},{10,11... | collective-permute-start | bytes 294920 | tf_op jit(solution)/shard_map/ppermute | solution.py:55
  6.4 6.3 %collective-permute-start.1 = (bf16[384,128]{1,0:T(8,128)(2,1)S(1)}, bf16[384,128]{1,0:T(8,128)(2,1)S(1)}, u32[]{:S(2)}, u32[]{:S(2)}) collective-permute-start(bf16[384,128]{1,0:T(8,128)(2,1)S(1)} %level1_0.1.refs_3_.refs_0_), channel_id=1, source_target_pairs={{0,2},{1,3},{2,0},{3,1},{4,6},{5,7},{6,4},{7,5},{8,10},{9,11},{10,... | collective-permute-start | bytes 294920 | tf_op jit(solution)/shard_map/ppermute | solution.py:55
  9.8 11.1 %collective-permute-start.5 = (bf16[384,256]{1,0:T(8,128)(2,1)S(1)}, bf16[384,256]{1,0:T(8,128)(2,1)S(1)}, u32[]{:S(2)}, u32[]{:S(2)}) collective-permute-start(bf16[384,256]{1,0:T(8,128)(2,1)S(1)} %level1_1.1.refs_6_.refs_0_), channel_id=1, source_target_pairs={{0,2},{1,3},{2,0},{3,1},{4,6},{5,7},{6,4},{7,5},{8,10},{9,11},{10,... | collective-permute-start | bytes 589832 | tf_op jit(solution)/shard_map/ppermute | solution.py:55
  13.4 8.3 %collective-permute-start.4 = (bf16[384,128]{1,0:T(8,128)(2,1)S(1)}, bf16[384,128]{1,0:T(8,128)(2,1)S(1)}, u32[]{:S(2)}, u32[]{:S(2)}) collective-permute-start(bf16[384,128]{1,0:T(8,128)(2,1)S(1)} %get-tuple-element.39.refs_3_.refs_0_), channel_id=1, source_target_pairs={{0,4},{1,5},{2,6},{3,7},{4,0},{5,1},{6,2},{7,3},{8,12},{9,13},{10,... | collective-permute-start | bytes 294920 | tf_op jit(solution)/shard_map/ppermute | solution.py:55
  16.4 12.5 %collective-permute-start.3 = (bf16[384,384]{1,0:T(8,128)(2,1)S(1)}, bf16[384,384]{1,0:T(8,128)(2,1)S(1)}, u32[]{:S(2)}, u32[]{:S(2)}) collective-permute-start(bf16[384,384]{1,0:T(8,128)(2,1)S(1)} %get-tuple-element.38.refs_0_), channel_id=1, source_target_pairs={{0,2},{1,3},{2,0},{3,1},{4,6},{5,7},{6,4},{7,5},{8,10},{9,11},{10,... | collective-permute-start | bytes 884744 | tf_op jit(solution)/shard_map/ppermute | solution.py:55
  21.3 12.9 %collective-permute-start.9 = (bf16[384,256]{1,0:T(8,128)(2,1)S(1)}, bf16[384,256]{1,0:T(8,128)(2,1)S(1)}, u32[]{:S(2)}, u32[]{:S(2)}) collective-permute-start(bf16[384,256]{1,0:T(8,128)(2,1)S(1)} %level2_1.1.refs_3_.refs_0_), channel_id=1, source_target_pairs={{0,4},{1,5},{2,6},{3,7},{4,0},{5,1},{6,2},{7,3},{8,12},{9,13},{10,... | collective-permute-start | bytes 589832 | tf_op jit(solution)/shard_map/ppermute | solution.py:55
  22.0 1.4 %collective-permute-start.6 = (bf16[384,128]{1,0:T(8,128)(2,1)S(1)}, bf16[384,128]{1,0:T(8,128)(2,1)S(1)}, u32[]{:S(2)}, u32[]{:S(2)}) collective-permute-start(bf16[384,128]{1,0:T(8,128)(2,1)S(1)} %level3_0.1.refs_0_), channel_id=1, source_target_pairs={{0,1},{1,0},{2,3},{3,2},{4,5},{5,4},{6,7},{7,6},{8,9},{9,8},{10,11... | collective-permute-start | bytes 294920 | tf_op jit(solution)/shard_map/ppermute | solution.py:55
  24.0 14.5 %collective-permute-start.12 = (bf16[512,128]{1,0:T(8,128)(2,1)S(1)}, bf16[512,128]{1,0:T(8,128)(2,1)S(1)}, u32[]{:S(2)}, u32[]{:S(2)}) collective-permute-start(bf16[512,128]{1,0:T(8,128)(2,1)S(1)} %get-tuple-element.46), channel_id=1, source_target_pairs={{0,16},{8,24},{16,0},{24,8},{1,17},{9,25},{17,1},{25,9},{2,18},{10... | collective-permute-start | bytes 393224 | tf_op jit(solution)/shard_map/ppermute | solution.py:55
  29.5 18.6 %collective-permute-start.7 = (bf16[384,384]{1,0:T(8,128)(2,1)S(1)}, bf16[384,384]{1,0:T(8,128)(2,1)S(1)}, u32[]{:S(2)}, u32[]{:S(2)}) collective-permute-start(bf16[384,384]{1,0:T(8,128)(2,1)S(1)} %level2_2.1.refs_3_.refs_0_), channel_id=1, source_target_pairs={{0,4},{1,5},{2,6},{3,7},{4,0},{5,1},{6,2},{7,3},{8,12},{9,13},{10,... | collective-permute-start | bytes 884744 | tf_op jit(solution)/shard_map/ppermute | solution.py:55
  31.7 16.0 %collective-permute-start.8 = (bf16[384,256]{1,0:T(8,128)(2,1)S(1)}, bf16[384,256]{1,0:T(8,128)(2,1)S(1)}, u32[]{:S(2)}, u32[]{:S(2)}) collective-permute-start(bf16[384,256]{1,0:T(8,128)(2,1)S(1)} %level1_3.1.refs_3_.refs_0_), channel_id=1, source_target_pairs={{0,2},{1,3},{2,0},{3,1},{4,6},{5,7},{6,4},{7,5},{8,10},{9,11},{10,... | collective-permute-start | bytes 589832 | tf_op jit(solution)/shard_map/ppermute | solution.py:55
  34.6 1.5 %collective-permute-start.10 = (bf16[384,256]{1,0:T(8,128)(2,1)S(1)}, bf16[384,256]{1,0:T(8,128)(2,1)S(1)}, u32[]{:S(2)}, u32[]{:S(2)}) collective-permute-start(bf16[384,256]{1,0:T(8,128)(2,1)S(1)} %level3_1.1.refs_0_), channel_id=1, source_target_pairs={{0,1},{1,0},{2,3},{3,2},{4,5},{5,4},{6,7},{7,6},{8,9},{9,8},{10,11... | collective-permute-start | bytes 589832 | tf_op jit(solution)/shard_map/ppermute | solution.py:55
  36.9 9.1 %collective-permute-start.11 = (bf16[512,256]{1,0:T(8,128)(2,1)S(1)}, bf16[512,256]{1,0:T(8,128)(2,1)S(1)}, u32[]{:S(2)}, u32[]{:S(2)}) collective-permute-start(bf16[512,256]{1,0:T(8,128)(2,1)S(1)} %get-tuple-element.45), channel_id=1, source_target_pairs={{0,8},{8,0},{16,24},{24,16},{1,9},{9,1},{17,25},{25,17},{2,10},{10... | collective-permute-start | bytes 786440 | tf_op jit(solution)/shard_map/ppermute | solution.py:55
  38.5 10.2 %collective-permute-start.13 = (bf16[256,128]{1,0:T(8,128)(2,1)S(1)}, bf16[256,128]{1,0:T(8,128)(2,1)S(1)}, u32[]{:S(2)}, u32[]{:S(2)}) collective-permute-start(bf16[256,128]{1,0:T(8,128)(2,1)S(1)} %get-tuple-element.49), channel_id=1, source_target_pairs={{0,8},{8,0},{16,24},{24,16},{1,9},{9,1},{17,25},{25,17},{2,10},{10... | collective-permute-start | bytes 196616 | tf_op jit(solution)/shard_map/ppermute | solution.py:55
  46.1 12.2 %collective-permute-start.16 = (bf16[256,256]{1,0:T(8,128)(2,1)S(1)}, bf16[256,256]{1,0:T(8,128)(2,1)S(1)}, u32[]{:S(2)}, u32[]{:S(2)}) collective-permute-start(bf16[256,256]{1,0:T(8,128)(2,1)S(1)} %get-tuple-element.53), channel_id=1, source_target_pairs={{0,16},{8,24},{16,0},{24,8},{1,17},{9,25},{17,1},{25,9},{2,18},{10... | collective-permute-start | bytes 393224 | tf_op jit(solution)/shard_map/ppermute | solution.py:55
  48.0 9.8 %collective-permute-start.14 = (bf16[384,256]{1,0:T(8,128)(2,1)S(1)}, bf16[384,256]{1,0:T(8,128)(2,1)S(1)}, u32[]{:S(2)}, u32[]{:S(2)}) collective-permute-start(bf16[384,256]{1,0:T(8,128)(2,1)S(1)} %level2_3.1.refs_3_.refs_0_), channel_id=1, source_target_pairs={{0,4},{1,5},{2,6},{3,7},{4,0},{5,1},{6,2},{7,3},{8,12},{9,13},{10,... | collective-permute-start | bytes 589832 | tf_op jit(solution)/shard_map/ppermute | solution.py:55
  48.6 1.6 %collective-permute-start.15 = (bf16[384,384]{1,0:T(8,128)(2,1)S(1)}, bf16[384,384]{1,0:T(8,128)(2,1)S(1)}, u32[]{:S(2)}, u32[]{:S(2)}) collective-permute-start(bf16[384,384]{1,0:T(8,128)(2,1)S(1)} %level3_2.1.refs_0_), channel_id=1, source_target_pairs={{0,1},{1,0},{2,3},{3,2},{4,5},{5,4},{6,7},{7,6},{8,9},{9,8},{10,11... | collective-permute-start | bytes 884744 | tf_op jit(solution)/shard_map/ppermute | solution.py:55
  51.5 12.0 %collective-permute-start.17 = (bf16[256,384]{1,0:T(8,128)(2,1)S(1)}, bf16[256,384]{1,0:T(8,128)(2,1)S(1)}, u32[]{:S(2)}, u32[]{:S(2)}) collective-permute-start(bf16[256,384]{1,0:T(8,128)(2,1)S(1)} %get-tuple-element.55), channel_id=1, source_target_pairs={{0,24},{8,16},{16,8},{24,0},{1,25},{9,17},{17,9},{25,1},{2,26},{10... | collective-permute-start | bytes 589832 | tf_op jit(solution)/shard_map/ppermute | solution.py:55
  53.0 11.0 %collective-permute-start.18 = (bf16[256,384]{1,0:T(8,128)(2,1)S(1)}, bf16[256,384]{1,0:T(8,128)(2,1)S(1)}, u32[]{:S(2)}, u32[]{:S(2)}) collective-permute-start(bf16[256,384]{1,0:T(8,128)(2,1)S(1)} %get-tuple-element.56), channel_id=1, source_target_pairs={{0,16},{8,24},{16,0},{24,8},{1,17},{9,25},{17,1},{25,9},{2,18},{10... | collective-permute-start | bytes 589832 | tf_op jit(solution)/shard_map/ppermute | solution.py:55
  54.6 9.5 %collective-permute-start.19 = (bf16[256,384]{1,0:T(8,128)(2,1)S(1)}, bf16[256,384]{1,0:T(8,128)(2,1)S(1)}, u32[]{:S(2)}, u32[]{:S(2)}) collective-permute-start(bf16[256,384]{1,0:T(8,128)(2,1)S(1)} %get-tuple-element.57), channel_id=1, source_target_pairs={{0,8},{8,0},{16,24},{24,16},{1,9},{9,1},{17,25},{25,17},{2,10},{10... | collective-permute-start | bytes 589832 | tf_op jit(solution)/shard_map/ppermute | solution.py:55
  58.2 1.5 %collective-permute-start.20 = (bf16[384,256]{1,0:T(8,128)(2,1)S(1)}, bf16[384,256]{1,0:T(8,128)(2,1)S(1)}, u32[]{:S(2)}, u32[]{:S(2)}) collective-permute-start(bf16[384,256]{1,0:T(8,128)(2,1)S(1)} %level3_3.1.refs_0_), channel_id=1, source_target_pairs={{0,1},{1,0},{2,3},{3,2},{4,5},{5,4},{6,7},{7,6},{8,9},{9,8},{10,11... | collective-permute-start | bytes 589832 | tf_op jit(solution)/shard_map/ppermute | solution.py:55
  60.5 7.3 %collective-permute-start.21 = (bf16[256,256]{1,0:T(8,128)(2,1)S(1)}, bf16[256,256]{1,0:T(8,128)(2,1)S(1)}, u32[]{:S(2)}, u32[]{:S(2)}) collective-permute-start(bf16[256,256]{1,0:T(8,128)(2,1)S(1)} %get-tuple-element.60), channel_id=1, source_target_pairs={{0,24},{8,16},{16,8},{24,0},{1,25},{9,17},{17,9},{25,1},{2,26},{10... | collective-permute-start | bytes 393224 | tf_op jit(solution)/shard_map/ppermute | solution.py:55
  62.0 7.8 %collective-permute-start.22 = (bf16[256,256]{1,0:T(8,128)(2,1)S(1)}, bf16[256,256]{1,0:T(8,128)(2,1)S(1)}, u32[]{:S(2)}, u32[]{:S(2)}) collective-permute-start(bf16[256,256]{1,0:T(8,128)(2,1)S(1)} %get-tuple-element.61), channel_id=1, source_target_pairs={{0,16},{8,24},{16,0},{24,8},{1,17},{9,25},{17,1},{25,9},{2,18},{10... | collective-permute-start | bytes 393224 | tf_op jit(solution)/shard_map/ppermute | solution.py:55
  63.5 6.3 %collective-permute-start.23 = (bf16[256,256]{1,0:T(8,128)(2,1)S(1)}, bf16[256,256]{1,0:T(8,128)(2,1)S(1)}, u32[]{:S(2)}, u32[]{:S(2)}) collective-permute-start(bf16[256,256]{1,0:T(8,128)(2,1)S(1)} %get-tuple-element.62), channel_id=1, source_target_pairs={{0,8},{8,0},{16,24},{24,16},{1,9},{9,1},{17,25},{25,17},{2,10},{10... | collective-permute-start | bytes 393224 | tf_op jit(solution)/shard_map/ppermute | solution.py:55

commit v12 on v11

--- a/solution.py
+++ b/solution.py
@@ -384,10 +384,10 @@
     out1, _ = tail(1, [coeff2[3]], False)
     fold1 = begin_sum(1, out1)
     keep0, got0 = fold(fold0, [out1[0]])
-    keep1, got1 = fold(fold1, [keep0])
-    (value,) = step("level2_3", [(2, 3, coeff2[3], near2[3])], [keep1])
+    (value,) = step("level2_3", [(2, 3, coeff2[3], near2[3])], [keep0])
     third(3, value)
-    out2, (total0,) = tail(2, [coeff3[3]], True, None, (0, keep0, got0))
+    keep1, got1 = fold(fold1, [coeff3[3]])
+    out2, (total0,) = tail(2, [keep1], True, None, (0, keep0, got0))
     group2 = direct_sum(out2)
     out3, (total1,) = tail(3, [out2[0]], True, None, (1, keep1, got1))
     group3 = direct_sum(out3)

time: 70.9 us -> 70.8 us (level)
  waiting for transfers between devices: 28 us -> 24.5 us
  starting transfers between devices: 26.3 us -> 29.7 us
    ppermute x24, waiting for transfers between devices: 28 us -> 24.5 us  [partner(): return lax.ppermute(value, axis, pairs)]
    ppermute x24, starting transfers between devices: 26.3 us -> 29.7 us  [partner(): return lax.ppermute(value, axis, pairs)]
  transfers between devices with their start and end apart: 24 -> 24, of which waited for: 11 -> 12; matrix products, arithmetic and copies ran while one was open for 0% -> 0% of each run, Pallas kernels for 16% -> 16%
where the time goes in v12:
time: 70.8 us; the launch traced here: 70.7 us
  starting transfers between devices  29.7 us (42%)
  waiting for transfers between devices  24.5 us (35%)
  Pallas kernels  16.2 us (23%)
    ppermute x24, starting transfers between devices, partner(): return lax.ppermute(value, axis, pairs)  29.7 us
    ppermute x24, waiting for transfers between devices, partner(): return lax.ppermute(value, axis, pairs)  24.5 us
    pallas_call x23, Pallas kernels, call(): pl.pallas_call(body, name=name, in_specs=[*in_specs, *[ANY] * len(after)]...  15.3 us
  transfers between devices with their start and end apart: 24, of which 12 were waited for; matrix products, arithmetic and copies ran while one was open for 0% of the time, Pallas kernels for 16%

profile of v12, /device:TPU:0, one launch (start us, length us, event | category | flops | bytes accessed | tf_op | source)
XLA Modules:
  0.0 70.7 jit_solution(4377250831377176526)
XLA Ops:
  0.0 3.7 %leaf.1 = (bf16[384,128]{1,0:T(8,128)(2,1)S(1)}, bf16[384,896]{1,0:T(8,128)(2,1)S(1)}, bf16[2,384,768]{2,1,0:T(8,128)(2,1)S(1)}, bf16[2,384,768]{2,1,0:T(8,128)(2,1)S(1)}) custom-call(bf16[2,1024,512]{2,1,0:T(8,128)(2,1)} %bitcast.9, bf16[2,384,1024]{2,1,0:T(8,128)(2,1)} %bitcast.10, bf16[5,2,384,768]{3,2,1,0:T(8,128)(2,1)} %bitcast.7, s32[2,5]{1,0:T(2,128)} %bitcast.12), custom_call_target="tpu_custom_call" | custom-call | flops 6000000000 | tf_op jit(solution)/shard_map/leaf/pallas_call | solution.py:41
  3.7 0.5 collective-permute-start.2
  4.3 1.8 %collective-permute-done.refs_1_ = bf16[384,128]{1,0:T(8,128)(2,1)S(1)} collective-permute-done((bf16[384,128]{1,0:T(8,128)(2,1)S(1)}, bf16[384,128]{1,0:T(8,128)(2,1)S(1)}, u32[]{:S(2)}, u32[]{:S(2)}) %collective-permute-start) | collective-permute-done | bytes 98336 | tf_op jit(solution)/shard_map/ppermute | solution.py:55
  6.1 0.3 level1_0.1.refs_3_.refs_0_
  6.4 3.0 %collective-permute-start.1 = (bf16[384,128]{1,0:T(8,128)(2,1)S(1)}, bf16[384,128]{1,0:T(8,128)(2,1)S(1)}, u32[]{:S(2)}, u32[]{:S(2)}) collective-permute-start(bf16[384,128]{1,0:T(8,128)(2,1)S(1)} %level1_0.1.refs_3_.refs_0_), channel_id=1, source_target_pairs={{0,2},{1,3},{2,0},{3,1},{4,6},{5,7},{6,4},{7,5},{8,10},{9,11},{10,... | collective-permute-start | bytes 294920 | tf_op jit(solution)/shard_map/ppermute | solution.py:55
  9.5 0.4 level1_1.1.refs_6_.refs_0_
  9.9 2.8 %collective-permute-done.1.refs_1_ = bf16[384,128]{1,0:T(8,128)(2,1)S(1)} collective-permute-done((bf16[384,128]{1,0:T(8,128)(2,1)S(1)}, bf16[384,128]{1,0:T(8,128)(2,1)S(1)}, u32[]{:S(2)}, u32[]{:S(2)}) %collective-permute-start.1) | collective-permute-done | bytes 98336 | tf_op jit(solution)/shard_map/ppermute | solution.py:55
  12.7 0.7 level2_0.1
  13.4 3.0 %collective-permute-start.4 = (bf16[384,128]{1,0:T(8,128)(2,1)S(1)}, bf16[384,128]{1,0:T(8,128)(2,1)S(1)}, u32[]{:S(2)}, u32[]{:S(2)}) collective-permute-start(bf16[384,128]{1,0:T(8,128)(2,1)S(1)} %get-tuple-element.39.refs_3_.refs_0_), channel_id=1, source_target_pairs={{0,4},{1,5},{2,6},{3,7},{4,0},{5,1},{6,2},{7,3},{8,12},{9,13},{10,... | collective-permute-start | bytes 294920 | tf_op jit(solution)/shard_map/ppermute | solution.py:55
  16.4 2.0 %collective-permute-start.3 = (bf16[384,384]{1,0:T(8,128)(2,1)S(1)}, bf16[384,384]{1,0:T(8,128)(2,1)S(1)}, u32[]{:S(2)}, u32[]{:S(2)}) collective-permute-start(bf16[384,384]{1,0:T(8,128)(2,1)S(1)} %get-tuple-element.38.refs_0_), channel_id=1, source_target_pairs={{0,2},{1,3},{2,0},{3,1},{4,6},{5,7},{6,4},{7,5},{8,10},{9,11},{10,... | collective-permute-start | bytes 884744 | tf_op jit(solution)/shard_map/ppermute | solution.py:55
  18.4 2.5 %prefetch.1 = (bf16[2,384,768]{2,1,0:T(8,128)(2,1)S(1)}, bf16[2,384,768]{2,1,0:T(8,128)(2,1)S(1)}, bf16[2,1024,384]{2,1,0:T(8,128)(2,1)S(1)}) custom-call(bf16[5,2,384,768]{3,2,1,0:T(8,128)(2,1)} %bitcast.8, bf16[2,1024,384]{2,1,0:T(8,128)(2,1)} %bitcast.11, s32[2,5]{1,0:T(2,128)} %bitcast.13, bf16[384,128]{1,0:T(8,128)(2,1)S(1)} %get-tuple-element.39.refs_3_.refs_0_), custom_call_target="tpu_custom_call" | custom-call | flops 6000000000 | tf_op jit(solution)/shard_map/prefetch/pallas_call | solution.py:41
  20.9 0.4 level2_1.1.refs_3_.refs_0_
  21.3 0.4 collective-permute-start.8
  21.7 0.3 level3_0.1.refs_0_
  22.4 1.0 %collective-permute-done.6.refs_1_ = bf16[384,128]{1,0:T(8,128)(2,1)S(1)} collective-permute-done((bf16[384,128]{1,0:T(8,128)(2,1)S(1)}, bf16[384,128]{1,0:T(8,128)(2,1)S(1)}, u32[]{:S(2)}, u32[]{:S(2)}) %collective-permute-start.6) | collective-permute-done | bytes 98336 | tf_op jit(solution)/shard_map/ppermute | solution.py:55
  23.4 0.6 last_0.1
  24.0 1.6 %collective-permute-start.12 = (bf16[512,128]{1,0:T(8,128)(2,1)S(1)}, bf16[512,128]{1,0:T(8,128)(2,1)S(1)}, u32[]{:S(2)}, u32[]{:S(2)}) collective-permute-start(bf16[512,128]{1,0:T(8,128)(2,1)S(1)} %get-tuple-element.46), channel_id=1, source_target_pairs={{0,16},{8,24},{16,0},{24,8},{1,17},{9,25},{17,1},{25,9},{2,18},{10... | collective-permute-start | bytes 393224 | tf_op jit(solution)/shard_map/ppermute | solution.py:55
  25.6 3.4 %collective-permute-done.3.refs_1_ = bf16[384,384]{1,0:T(8,128)(2,1)S(1)} collective-permute-done((bf16[384,384]{1,0:T(8,128)(2,1)S(1)}, bf16[384,384]{1,0:T(8,128)(2,1)S(1)}, u32[]{:S(2)}, u32[]{:S(2)}) %collective-permute-start.3) | collective-permute-done | bytes 294944 | tf_op jit(solution)/shard_map/ppermute | solution.py:55
  29.0 0.5 level2_2.1.refs_3_.refs_0_
  29.5 1.8 %collective-permute-start.7 = (bf16[384,384]{1,0:T(8,128)(2,1)S(1)}, bf16[384,384]{1,0:T(8,128)(2,1)S(1)}, u32[]{:S(2)}, u32[]{:S(2)}) collective-permute-start(bf16[384,384]{1,0:T(8,128)(2,1)S(1)} %level2_2.1.refs_3_.refs_0_), channel_id=1, source_target_pairs={{0,4},{1,5},{2,6},{3,7},{4,0},{5,1},{6,2},{7,3},{8,12},{9,13},{10,... | collective-permute-start | bytes 884744 | tf_op jit(solution)/shard_map/ppermute | solution.py:55
  31.3 0.4 level1_3.1.refs_3_.refs_0_
  31.7 2.5 %collective-permute-start.11 = (bf16[384,256]{1,0:T(8,128)(2,1)S(1)}, bf16[384,256]{1,0:T(8,128)(2,1)S(1)}, u32[]{:S(2)}, u32[]{:S(2)}) collective-permute-start(bf16[384,256]{1,0:T(8,128)(2,1)S(1)} %level1_3.1.refs_3_.refs_0_), channel_id=1, source_target_pairs={{0,2},{1,3},{2,0},{3,1},{4,6},{5,7},{6,4},{7,5},{8,10},{9,11},{10,... | collective-permute-start | bytes 589832 | tf_op jit(solution)/shard_map/ppermute | solution.py:55
  34.2 0.4 level3_1.1.refs_0_
  34.9 1.2 %collective-permute-done.9.refs_1_ = bf16[384,256]{1,0:T(8,128)(2,1)S(1)} collective-permute-done((bf16[384,256]{1,0:T(8,128)(2,1)S(1)}, bf16[384,256]{1,0:T(8,128)(2,1)S(1)}, u32[]{:S(2)}, u32[]{:S(2)}) %collective-permute-start.9) | collective-permute-done | bytes 196640 | tf_op jit(solution)/shard_map/ppermute | solution.py:55
  36.1 0.8 %last_1.1 = (f32[512,256]{1,0:T(8,128)S(1)}, bf16[512,256]{1,0:T(8,128)(2,1)S(1)}) custom-call(f32[384,256]{1,0:T(8,128)S(1)} %between_1.1.refs_0_, bf16[384,256]{1,0:T(8,128)(2,1)S(1)} %collective-permute-done.9.refs_1_, bf16[2,384,768]{2,1,0:T(8,128)(2,1)S(1)} %get-tuple-element.42.refs_1_.refs_2_, bf16[2,1024,384]{2,1,0:T(8,128)(2,1)S(1)} %get-tuple-element.41.refs_3_), custom_call_target="tpu_custom_call" | custom-call | flops 6000000000 | tf_op jit(solution)/shard_map/last_1/pallas_call | solution.py:41
  37.0 1.6 %collective-permute-start.13 = (bf16[256,128]{1,0:T(8,128)(2,1)S(1)}, bf16[256,128]{1,0:T(8,128)(2,1)S(1)}, u32[]{:S(2)}, u32[]{:S(2)}) collective-permute-start(bf16[256,128]{1,0:T(8,128)(2,1)S(1)} %get-tuple-element.49), channel_id=1, source_target_pairs={{0,8},{8,0},{16,24},{24,16},{1,9},{9,1},{17,25},{25,17},{2,10},{10... | collective-permute-start | bytes 196616 | tf_op jit(solution)/shard_map/ppermute | solution.py:55
  38.5 0.5 collective-permute-start.10
  39.0 2.3 %collective-permute-done.11.refs_1_ = bf16[384,256]{1,0:T(8,128)(2,1)S(1)} collective-permute-done((bf16[384,256]{1,0:T(8,128)(2,1)S(1)}, bf16[384,256]{1,0:T(8,128)(2,1)S(1)}, u32[]{:S(2)}, u32[]{:S(2)}) %collective-permute-start.11) | collective-permute-done | bytes 196640 | tf_op jit(solution)/shard_map/ppermute | solution.py:55
  41.3 0.3 level2_3.1.refs_2_.refs_0_
  41.7 3.3 %collective-permute-start.14 = (bf16[384,256]{1,0:T(8,128)(2,1)S(1)}, bf16[384,256]{1,0:T(8,128)(2,1)S(1)}, u32[]{:S(2)}, u32[]{:S(2)}) collective-permute-start(bf16[384,256]{1,0:T(8,128)(2,1)S(1)} %level2_3.1.refs_2_.refs_0_), channel_id=1, source_target_pairs={{0,4},{1,5},{2,6},{3,7},{4,0},{5,1},{6,2},{7,3},{8,12},{9,13},{10,... | collective-permute-start | bytes 589832 | tf_op jit(solution)/shard_map/ppermute | solution.py:55
  45.0 2.0 %collective-permute-done.10.refs_1_ = bf16[512,256]{1,0:T(8,128)(2,1)S(1)} collective-permute-done((bf16[512,256]{1,0:T(8,128)(2,1)S(1)}, bf16[512,256]{1,0:T(8,128)(2,1)S(1)}, u32[]{:S(2)}, u32[]{:S(2)}) %collective-permute-start.10) | collective-permute-done | bytes 262176 | tf_op jit(solution)/shard_map/ppermute | solution.py:55
  47.0 1.6 %collective-permute-start.16 = (bf16[256,256]{1,0:T(8,128)(2,1)S(1)}, bf16[256,256]{1,0:T(8,128)(2,1)S(1)}, u32[]{:S(2)}, u32[]{:S(2)}) collective-permute-start(bf16[256,256]{1,0:T(8,128)(2,1)S(1)} %get-tuple-element.53), channel_id=1, source_target_pairs={{0,16},{8,24},{16,0},{24,8},{1,17},{9,25},{17,1},{25,9},{2,18},{10... | collective-permute-start | bytes 393224 | tf_op jit(solution)/shard_map/ppermute | solution.py:55
  48.5 0.5 level3_2.1.refs_0_
  49.5 1.2 %collective-permute-done.15.refs_1_ = bf16[384,384]{1,0:T(8,128)(2,1)S(1)} collective-permute-done((bf16[384,384]{1,0:T(8,128)(2,1)S(1)}, bf16[384,384]{1,0:T(8,128)(2,1)S(1)}, u32[]{:S(2)}, u32[]{:S(2)}) %collective-permute-start.15) | collective-permute-done | bytes 294944 | tf_op jit(solution)/shard_map/ppermute | solution.py:55
  50.7 1.2 %last_2.1 = (f32[256,384]{1,0:T(8,128)S(1)}, bf16[256,384]{1,0:T(8,128)(2,1)S(1)}, bf16[256,384]{1,0:T(8,128)(2,1)S(1)}, bf16[256,384]{1,0:T(8,128)(2,1)S(1)}) custom-call(f32[384,384]{1,0:T(8,128)S(1)} %get-tuple-element.51.refs_0_, bf16[384,384]{1,0:T(8,128)(2,1)S(1)} %collective-permute-done.15.refs_1_, ...), custom_call_target="tpu_custom_call" | custom-call | flops 6000000000 | tf_op jit(solution)/shard_map/last_2/pallas_call | solution.py:41
  52.0 1.4 %collective-permute-start.17 = (bf16[256,384]{1,0:T(8,128)(2,1)S(1)}, bf16[256,384]{1,0:T(8,128)(2,1)S(1)}, u32[]{:S(2)}, u32[]{:S(2)}) collective-permute-start(bf16[256,384]{1,0:T(8,128)(2,1)S(1)} %get-tuple-element.55), channel_id=1, source_target_pairs={{0,24},{8,16},{16,8},{24,0},{1,25},{9,17},{17,9},{25,1},{2,26},{10... | collective-permute-start | bytes 589832 | tf_op jit(solution)/shard_map/ppermute | solution.py:55
  53.3 1.5 %collective-permute-start.18 = (bf16[256,384]{1,0:T(8,128)(2,1)S(1)}, bf16[256,384]{1,0:T(8,128)(2,1)S(1)}, u32[]{:S(2)}, u32[]{:S(2)}) collective-permute-start(bf16[256,384]{1,0:T(8,128)(2,1)S(1)} %get-tuple-element.56), channel_id=1, source_target_pairs={{0,16},{8,24},{16,0},{24,8},{1,17},{9,25},{17,1},{25,9},{2,18},{10... | collective-permute-start | bytes 589832 | tf_op jit(solution)/shard_map/ppermute | solution.py:55
  54.9 0.7 collective-permute-start.19
  55.5 0.4 level3_3.1.refs_0_
  56.2 1.2 %collective-permute-done.20.refs_1_ = bf16[384,256]{1,0:T(8,128)(2,1)S(1)} collective-permute-done((bf16[384,256]{1,0:T(8,128)(2,1)S(1)}, bf16[384,256]{1,0:T(8,128)(2,1)S(1)}, u32[]{:S(2)}, u32[]{:S(2)}) %collective-permute-start.20) | collective-permute-done | bytes 196640 | tf_op jit(solution)/shard_map/ppermute | solution.py:55
  57.4 0.8 %last_3.1 = (f32[256,256]{1,0:T(8,128)S(1)}, bf16[256,256]{1,0:T(8,128)(2,1)S(1)}, bf16[256,256]{1,0:T(8,128)(2,1)S(1)}, bf16[256,256]{1,0:T(8,128)(2,1)S(1)}) custom-call(f32[384,256]{1,0:T(8,128)S(1)} %get-tuple-element.58.refs_0_, bf16[384,256]{1,0:T(8,128)(2,1)S(1)} %collective-permute-done.20.refs_1_, ...), custom_call_target="tpu_custom_call" | custom-call | flops 6000000000 | tf_op jit(solution)/shard_map/last_3/pallas_call | solution.py:41
  58.2 1.4 %collective-permute-start.21 = (bf16[256,256]{1,0:T(8,128)(2,1)S(1)}, bf16[256,256]{1,0:T(8,128)(2,1)S(1)}, u32[]{:S(2)}, u32[]{:S(2)}) collective-permute-start(bf16[256,256]{1,0:T(8,128)(2,1)S(1)} %get-tuple-element.60), channel_id=1, source_target_pairs={{0,24},{8,16},{16,8},{24,0},{1,25},{9,17},{17,9},{25,1},{2,26},{10... | collective-permute-start | bytes 393224 | tf_op jit(solution)/shard_map/ppermute | solution.py:55
  59.6 1.5 %collective-permute-start.22 = (bf16[256,256]{1,0:T(8,128)(2,1)S(1)}, bf16[256,256]{1,0:T(8,128)(2,1)S(1)}, u32[]{:S(2)}, u32[]{:S(2)}) collective-permute-start(bf16[256,256]{1,0:T(8,128)(2,1)S(1)} %get-tuple-element.61), channel_id=1, source_target_pairs={{0,16},{8,24},{16,0},{24,8},{1,17},{9,25},{17,1},{25,9},{2,18},{10... | collective-permute-start | bytes 393224 | tf_op jit(solution)/shard_map/ppermute | solution.py:55
  61.1 1.0 %collective-permute-start.23 = (bf16[256,256]{1,0:T(8,128)(2,1)S(1)}, bf16[256,256]{1,0:T(8,128)(2,1)S(1)}, u32[]{:S(2)}, u32[]{:S(2)}) collective-permute-start(bf16[256,256]{1,0:T(8,128)(2,1)S(1)} %get-tuple-element.62), channel_id=1, source_target_pairs={{0,8},{8,0},{16,24},{24,16},{1,9},{9,1},{17,25},{25,17},{2,10},{10... | collective-permute-start | bytes 393224 | tf_op jit(solution)/shard_map/ppermute | solution.py:55
  62.1 2.9 %collective-permute-done.18.refs_4_ = bf16[256,384]{1,0:T(8,128)(2,1)S(1)} collective-permute-done((bf16[256,384]{1,0:T(8,128)(2,1)S(1)}, bf16[256,384]{1,0:T(8,128)(2,1)S(1)}, u32[]{:S(2)}, u32[]{:S(2)}) %collective-permute-start.18) | collective-permute-done | bytes 196640 | tf_op jit(solution)/shard_map/ppermute | solution.py:55
  65.0 2.8 %collective-permute-done.21.refs_7_ = bf16[256,256]{1,0:T(8,128)(2,1)S(1)} collective-permute-done((bf16[256,256]{1,0:T(8,128)(2,1)S(1)}, bf16[256,256]{1,0:T(8,128)(2,1)S(1)}, u32[]{:S(2)}, u32[]{:S(2)}) %collective-permute-start.21) | collective-permute-done | bytes 131104 | tf_op jit(solution)/shard_map/ppermute | solution.py:55
  67.8 1.9 %collective-permute-done.22.refs_8_ = bf16[256,256]{1,0:T(8,128)(2,1)S(1)} collective-permute-done((bf16[256,256]{1,0:T(8,128)(2,1)S(1)}, bf16[256,256]{1,0:T(8,128)(2,1)S(1)}, u32[]{:S(2)}, u32[]{:S(2)}) %collective-permute-start.22) | collective-permute-done | bytes 131104 | tf_op jit(solution)/shard_map/ppermute | solution.py:55
  69.7 1.0 %end.1 = bf16[2,256,512]{2,1,0:T(8,128)(2,1)} custom-call(bf16[256,128]{1,0:T(8,128)(2,1)S(1)} %get-tuple-element.50.refs_0_, bf16[256,256]{1,0:T(8,128)(2,1)S(1)} %get-tuple-element.54.refs_1_, f32[256,384]{1,0:T(8,128)S(1)} %get-tuple-element.52.refs_3_.refs_2_, bf16[256,384]{1,0:T(8,128)(2,1)S(1)} %collective-permute-done.17.refs_3_, ...), custom_call_target="tpu_custom_call" | custom-call | tf_op jit(solution)/shard_map/end/pallas_call | solution.py:396
  (24 shorter events, 1.6 us)
Async XLA Ops:
  3.7 5.8 %collective-permute-start.2 = (bf16[384,896]{1,0:T(8,128)(2,1)S(1)}, bf16[384,896]{1,0:T(8,128)(2,1)S(1)}, u32[]{:S(2)}, u32[]{:S(2)}) collective-permute-start(bf16[384,896]{1,0:T(8,128)(2,1)S(1)} %get-tuple-element.37.refs_0_.refs_3_), channel_id=1, source_target_pairs={{0,1},{1,0},{2,3},{3,2},{4,5},{5,4},{6,7},{7,6},{8,9},{9,8},{10,11... | collective-permute-start | bytes 2064392 | tf_op jit(solution)/shard_map/ppermute | solution.py:55
  4.2 1.9 %collective-permute-start = (bf16[384,128]{1,0:T(8,128)(2,1)S(1)}, bf16[384,128]{1,0:T(8,128)(2,1)S(1)}, u32[]{:S(2)}, u32[]{:S(2)}) collective-permute-start(bf16[384,128]{1,0:T(8,128)(2,1)S(1)} %get-tuple-element.34.refs_0_), channel_id=1, source_target_pairs={{0,1},{1,0},{2,3},{3,2},{4,5},{5,4},{6,7},{7,6},{8,9},{9,8},{10,11... | collective-permute-start | bytes 294920 | tf_op jit(solution)/shard_map/ppermute | solution.py:55
  6.4 6.3 %collective-permute-start.1 = (bf16[384,128]{1,0:T(8,128)(2,1)S(1)}, bf16[384,128]{1,0:T(8,128)(2,1)S(1)}, u32[]{:S(2)}, u32[]{:S(2)}) collective-permute-start(bf16[384,128]{1,0:T(8,128)(2,1)S(1)} %level1_0.1.refs_3_.refs_0_), channel_id=1, source_target_pairs={{0,2},{1,3},{2,0},{3,1},{4,6},{5,7},{6,4},{7,5},{8,10},{9,11},{10,... | collective-permute-start | bytes 294920 | tf_op jit(solution)/shard_map/ppermute | solution.py:55
  9.8 11.1 %collective-permute-start.5 = (bf16[384,256]{1,0:T(8,128)(2,1)S(1)}, bf16[384,256]{1,0:T(8,128)(2,1)S(1)}, u32[]{:S(2)}, u32[]{:S(2)}) collective-permute-start(bf16[384,256]{1,0:T(8,128)(2,1)S(1)} %level1_1.1.refs_6_.refs_0_), channel_id=1, source_target_pairs={{0,2},{1,3},{2,0},{3,1},{4,6},{5,7},{6,4},{7,5},{8,10},{9,11},{10,... | collective-permute-start | bytes 589832 | tf_op jit(solution)/shard_map/ppermute | solution.py:55
  13.4 8.3 %collective-permute-start.4 = (bf16[384,128]{1,0:T(8,128)(2,1)S(1)}, bf16[384,128]{1,0:T(8,128)(2,1)S(1)}, u32[]{:S(2)}, u32[]{:S(2)}) collective-permute-start(bf16[384,128]{1,0:T(8,128)(2,1)S(1)} %get-tuple-element.39.refs_3_.refs_0_), channel_id=1, source_target_pairs={{0,4},{1,5},{2,6},{3,7},{4,0},{5,1},{6,2},{7,3},{8,12},{9,13},{10,... | collective-permute-start | bytes 294920 | tf_op jit(solution)/shard_map/ppermute | solution.py:55
  16.4 12.5 %collective-permute-start.3 = (bf16[384,384]{1,0:T(8,128)(2,1)S(1)}, bf16[384,384]{1,0:T(8,128)(2,1)S(1)}, u32[]{:S(2)}, u32[]{:S(2)}) collective-permute-start(bf16[384,384]{1,0:T(8,128)(2,1)S(1)} %get-tuple-element.38.refs_0_), channel_id=1, source_target_pairs={{0,2},{1,3},{2,0},{3,1},{4,6},{5,7},{6,4},{7,5},{8,10},{9,11},{10,... | collective-permute-start | bytes 884744 | tf_op jit(solution)/shard_map/ppermute | solution.py:55
  21.3 12.9 %collective-permute-start.8 = (bf16[384,256]{1,0:T(8,128)(2,1)S(1)}, bf16[384,256]{1,0:T(8,128)(2,1)S(1)}, u32[]{:S(2)}, u32[]{:S(2)}) collective-permute-start(bf16[384,256]{1,0:T(8,128)(2,1)S(1)} %level2_1.1.refs_3_.refs_0_), channel_id=1, source_target_pairs={{0,4},{1,5},{2,6},{3,7},{4,0},{5,1},{6,2},{7,3},{8,12},{9,13},{10,... | collective-permute-start | bytes 589832 | tf_op jit(solution)/shard_map/ppermute | solution.py:55
  22.1 1.4 %collective-permute-start.6 = (bf16[384,128]{1,0:T(8,128)(2,1)S(1)}, bf16[384,128]{1,0:T(8,128)(2,1)S(1)}, u32[]{:S(2)}, u32[]{:S(2)}) collective-permute-start(bf16[384,128]{1,0:T(8,128)(2,1)S(1)} %level3_0.1.refs_0_), channel_id=1, source_target_pairs={{0,1},{1,0},{2,3},{3,2},{4,5},{5,4},{6,7},{7,6},{8,9},{9,8},{10,11... | collective-permute-start | bytes 294920 | tf_op jit(solution)/shard_map/ppermute | solution.py:55
  24.0 12.9 %collective-permute-start.12 = (bf16[512,128]{1,0:T(8,128)(2,1)S(1)}, bf16[512,128]{1,0:T(8,128)(2,1)S(1)}, u32[]{:S(2)}, u32[]{:S(2)}) collective-permute-start(bf16[512,128]{1,0:T(8,128)(2,1)S(1)} %get-tuple-element.46), channel_id=1, source_target_pairs={{0,16},{8,24},{16,0},{24,8},{1,17},{9,25},{17,1},{25,9},{2,18},{10... | collective-permute-start | bytes 393224 | tf_op jit(solution)/shard_map/ppermute | solution.py:55
  29.5 19.1 %collective-permute-start.7 = (bf16[384,384]{1,0:T(8,128)(2,1)S(1)}, bf16[384,384]{1,0:T(8,128)(2,1)S(1)}, u32[]{:S(2)}, u32[]{:S(2)}) collective-permute-start(bf16[384,384]{1,0:T(8,128)(2,1)S(1)} %level2_2.1.refs_3_.refs_0_), channel_id=1, source_target_pairs={{0,4},{1,5},{2,6},{3,7},{4,0},{5,1},{6,2},{7,3},{8,12},{9,13},{10,... | collective-permute-start | bytes 884744 | tf_op jit(solution)/shard_map/ppermute | solution.py:55
  31.7 9.6 %collective-permute-start.11 = (bf16[384,256]{1,0:T(8,128)(2,1)S(1)}, bf16[384,256]{1,0:T(8,128)(2,1)S(1)}, u32[]{:S(2)}, u32[]{:S(2)}) collective-permute-start(bf16[384,256]{1,0:T(8,128)(2,1)S(1)} %level1_3.1.refs_3_.refs_0_), channel_id=1, source_target_pairs={{0,2},{1,3},{2,0},{3,1},{4,6},{5,7},{6,4},{7,5},{8,10},{9,11},{10,... | collective-permute-start | bytes 589832 | tf_op jit(solution)/shard_map/ppermute | solution.py:55
  34.6 1.5 %collective-permute-start.9 = (bf16[384,256]{1,0:T(8,128)(2,1)S(1)}, bf16[384,256]{1,0:T(8,128)(2,1)S(1)}, u32[]{:S(2)}, u32[]{:S(2)}) collective-permute-start(bf16[384,256]{1,0:T(8,128)(2,1)S(1)} %level3_1.1.refs_0_), channel_id=1, source_target_pairs={{0,1},{1,0},{2,3},{3,2},{4,5},{5,4},{6,7},{7,6},{8,9},{9,8},{10,11... | collective-permute-start | bytes 589832 | tf_op jit(solution)/shard_map/ppermute | solution.py:55
  37.0 12.2 %collective-permute-start.13 = (bf16[256,128]{1,0:T(8,128)(2,1)S(1)}, bf16[256,128]{1,0:T(8,128)(2,1)S(1)}, u32[]{:S(2)}, u32[]{:S(2)}) collective-permute-start(bf16[256,128]{1,0:T(8,128)(2,1)S(1)} %get-tuple-element.49), channel_id=1, source_target_pairs={{0,8},{8,0},{16,24},{24,16},{1,9},{9,1},{17,25},{25,17},{2,10},{10... | collective-permute-start | bytes 196616 | tf_op jit(solution)/shard_map/ppermute | solution.py:55
  38.5 8.4 %collective-permute-start.10 = (bf16[512,256]{1,0:T(8,128)(2,1)S(1)}, bf16[512,256]{1,0:T(8,128)(2,1)S(1)}, u32[]{:S(2)}, u32[]{:S(2)}) collective-permute-start(bf16[512,256]{1,0:T(8,128)(2,1)S(1)} %get-tuple-element.45), channel_id=1, source_target_pairs={{0,8},{8,0},{16,24},{24,16},{1,9},{9,1},{17,25},{25,17},{2,10},{10... | collective-permute-start | bytes 786440 | tf_op jit(solution)/shard_map/ppermute | solution.py:55
  41.7 13.9 %collective-permute-start.14 = (bf16[384,256]{1,0:T(8,128)(2,1)S(1)}, bf16[384,256]{1,0:T(8,128)(2,1)S(1)}, u32[]{:S(2)}, u32[]{:S(2)}) collective-permute-start(bf16[384,256]{1,0:T(8,128)(2,1)S(1)} %level2_3.1.refs_2_.refs_0_), channel_id=1, source_target_pairs={{0,4},{1,5},{2,6},{3,7},{4,0},{5,1},{6,2},{7,3},{8,12},{9,13},{10,... | collective-permute-start | bytes 589832 | tf_op jit(solution)/shard_map/ppermute | solution.py:55
  47.0 9.0 %collective-permute-start.16 = (bf16[256,256]{1,0:T(8,128)(2,1)S(1)}, bf16[256,256]{1,0:T(8,128)(2,1)S(1)}, u32[]{:S(2)}, u32[]{:S(2)}) collective-permute-start(bf16[256,256]{1,0:T(8,128)(2,1)S(1)} %get-tuple-element.53), channel_id=1, source_target_pairs={{0,16},{8,24},{16,0},{24,8},{1,17},{9,25},{17,1},{25,9},{2,18},{10... | collective-permute-start | bytes 393224 | tf_op jit(solution)/shard_map/ppermute | solution.py:55
  49.1 1.6 %collective-permute-start.15 = (bf16[384,384]{1,0:T(8,128)(2,1)S(1)}, bf16[384,384]{1,0:T(8,128)(2,1)S(1)}, u32[]{:S(2)}, u32[]{:S(2)}) collective-permute-start(bf16[384,384]{1,0:T(8,128)(2,1)S(1)} %level3_2.1.refs_0_), channel_id=1, source_target_pairs={{0,1},{1,0},{2,3},{3,2},{4,5},{5,4},{6,7},{7,6},{8,9},{9,8},{10,11... | collective-permute-start | bytes 884744 | tf_op jit(solution)/shard_map/ppermute | solution.py:55
  52.0 9.1 %collective-permute-start.17 = (bf16[256,384]{1,0:T(8,128)(2,1)S(1)}, bf16[256,384]{1,0:T(8,128)(2,1)S(1)}, u32[]{:S(2)}, u32[]{:S(2)}) collective-permute-start(bf16[256,384]{1,0:T(8,128)(2,1)S(1)} %get-tuple-element.55), channel_id=1, source_target_pairs={{0,24},{8,16},{16,8},{24,0},{1,25},{9,17},{17,9},{25,1},{2,26},{10... | collective-permute-start | bytes 589832 | tf_op jit(solution)/shard_map/ppermute | solution.py:55
  53.3 11.7 %collective-permute-start.18 = (bf16[256,384]{1,0:T(8,128)(2,1)S(1)}, bf16[256,384]{1,0:T(8,128)(2,1)S(1)}, u32[]{:S(2)}, u32[]{:S(2)}) collective-permute-start(bf16[256,384]{1,0:T(8,128)(2,1)S(1)} %get-tuple-element.56), channel_id=1, source_target_pairs={{0,16},{8,24},{16,0},{24,8},{1,17},{9,25},{17,1},{25,9},{2,18},{10... | collective-permute-start | bytes 589832 | tf_op jit(solution)/shard_map/ppermute | solution.py:55
  54.9 10.1 %collective-permute-start.19 = (bf16[256,384]{1,0:T(8,128)(2,1)S(1)}, bf16[256,384]{1,0:T(8,128)(2,1)S(1)}, u32[]{:S(2)}, u32[]{:S(2)}) collective-permute-start(bf16[256,384]{1,0:T(8,128)(2,1)S(1)} %get-tuple-element.57), channel_id=1, source_target_pairs={{0,8},{8,0},{16,24},{24,16},{1,9},{9,1},{17,25},{25,17},{2,10},{10... | collective-permute-start | bytes 589832 | tf_op jit(solution)/shard_map/ppermute | solution.py:55
  55.9 1.5 %collective-permute-start.20 = (bf16[384,256]{1,0:T(8,128)(2,1)S(1)}, bf16[384,256]{1,0:T(8,128)(2,1)S(1)}, u32[]{:S(2)}, u32[]{:S(2)}) collective-permute-start(bf16[384,256]{1,0:T(8,128)(2,1)S(1)} %level3_3.1.refs_0_), channel_id=1, source_target_pairs={{0,1},{1,0},{2,3},{3,2},{4,5},{5,4},{6,7},{7,6},{8,9},{9,8},{10,11... | collective-permute-start | bytes 589832 | tf_op jit(solution)/shard_map/ppermute | solution.py:55
  58.2 9.6 %collective-permute-start.21 = (bf16[256,256]{1,0:T(8,128)(2,1)S(1)}, bf16[256,256]{1,0:T(8,128)(2,1)S(1)}, u32[]{:S(2)}, u32[]{:S(2)}) collective-permute-start(bf16[256,256]{1,0:T(8,128)(2,1)S(1)} %get-tuple-element.60), channel_id=1, source_target_pairs={{0,24},{8,16},{16,8},{24,0},{1,25},{9,17},{17,9},{25,1},{2,26},{10... | collective-permute-start | bytes 393224 | tf_op jit(solution)/shard_map/ppermute | solution.py:55
  59.6 10.1 %collective-permute-start.22 = (bf16[256,256]{1,0:T(8,128)(2,1)S(1)}, bf16[256,256]{1,0:T(8,128)(2,1)S(1)}, u32[]{:S(2)}, u32[]{:S(2)}) collective-permute-start(bf16[256,256]{1,0:T(8,128)(2,1)S(1)} %get-tuple-element.61), channel_id=1, source_target_pairs={{0,16},{8,24},{16,0},{24,8},{1,17},{9,25},{17,1},{25,9},{2,18},{10... | collective-permute-start | bytes 393224 | tf_op jit(solution)/shard_map/ppermute | solution.py:55
  61.1 8.6 %collective-permute-start.23 = (bf16[256,256]{1,0:T(8,128)(2,1)S(1)}, bf16[256,256]{1,0:T(8,128)(2,1)S(1)}, u32[]{:S(2)}, u32[]{:S(2)}) collective-permute-start(bf16[256,256]{1,0:T(8,128)(2,1)S(1)} %get-tuple-element.62), channel_id=1, source_target_pairs={{0,8},{8,0},{16,24},{24,16},{1,9},{9,1},{17,25},{25,17},{2,10},{10... | collective-permute-start | bytes 393224 | tf_op jit(solution)/shard_map/ppermute | solution.py:55

commit v13 on v5

--- a/solution.py
+++ b/solution.py
@@ -144,33 +144,43 @@
     return dot(weights[s, :, pl.ds(pl.multiple_of(half * rank, 128), rank)], value)
 
 
-def half_kernel(bit, parts, own, weights, partial):
+def sum_kernel(mine, *refs):
+    total = mine[...]
+    for piece in refs[:-1]:
+        total = total + piece[...].astype(F32)
+    refs[-1][...] = total.astype(BF16)
+
+
+def between_kernel(bit, parts, counts, own, weights, *refs):
+    refs = list(refs)
+    groups = [[refs.pop(0) for _ in range(count)] for count in counts]
+    partial = refs.pop(0)
     for s, start, stop in parts:
         partial[:, start:stop] = half_dot(weights, s, upper_half(bit), own[:, start:stop])
-
-
-def last_kernel(bit, parts, partial, other, weights, basis, mine, pieces):
-    rows = mine.shape[0]
-    row = pl.multiple_of(lax.axis_index("blk") * rows, rows)
+    for group, out in zip(groups, refs):
+        sum_kernel(*group, out)
+
+
+def last_kernel(bit, parts, partial, other, weights, basis, *refs):
+    rows = refs[0].shape[0]
+    me = lax.axis_index("blk")
     for s, start, stop in parts:
         mixed = partial[:, start:stop] + half_dot(weights, s, 1 - upper_half(bit), other[:, start:stop])
         coeff = mixed.astype(BF16)
-        pieces[:, start:stop] = dot(basis[s], coeff).astype(BF16)
-        mine[:, start:stop] = dot(basis[s, pl.ds(row, rows), :], coeff)
-
-
-def end_kernel(places, *refs):
-    refs, out = list(refs[:-1]), refs[-1]
-    me = lax.axis_index("blk")
-    for place in places:
-        mine, got = refs.pop(0), refs.pop(0)
-        rows = mine.shape[0]
-        count = got.shape[0] // rows
+        for d, ref in enumerate(refs):
+            row = pl.multiple_of((me ^ d) * rows, rows)
+            ref[:, start:stop] = dot(basis[s, pl.ds(row, rows), :], coeff).astype(ref.dtype)
+
+
+def end_kernel(places, counts, *refs):
+    refs = list(refs)
+    out = refs[-1]
+    for place, count in zip(places, counts):
+        group = [refs.pop(0) for _ in range(count)]
         for s, column, start, stop in place:
-            total = mine[:, start:stop]
-            for d in range(1, count):
-                row = pl.multiple_of((me ^ d) * rows, rows)
-                total = total + got[pl.ds(row, rows), start:stop].astype(F32)
+            total = group[0][:, start:stop].astype(F32)
+            for piece in group[1:]:
+                total = total + piece[:, start:stop].astype(F32)
             out[s, :, column : column + stop - start] = total.astype(BF16)
 
 
@@ -259,9 +269,10 @@
     second(0, value)
     (value,) = step("level1_1", [job1(1)], [coeff2[0]])
     second(1, value)
-    value, ahead = step("level2_0", [(2, 0, coeff2[0], near2[0]), job1(2)], [coeff2[1]])
+    (value,) = step("level2_0", [(2, 0, coeff2[0], near2[0])], [coeff2[1]])
     third(0, value)
-    second(2, ahead)
+    (value,) = step("level1_2", [job1(2)], [coeff3[0]])
+    second(2, value)
     *more, basis_v = call(
         prefetch_kernel,
         "prefetch",
@@ -269,45 +280,58 @@
         [pair] * (levels - 1 - PRELOADED) + [in_vmem(*basis.shape)],
         [pltpu.SMEM(index.shape, jnp.int32), pltpu.SemaphoreType.DMA((2 * levels,))],
         [in_hbm(blocks), in_hbm(basis), in_hbm(index)],
-        [coeff3[0]],
+        [coeff2[2]],
     )
     weights += more
-    value, ahead = step("level2_1", [(2, 1, coeff2[1], near2[1]), job1(3)], [basis_v])
+    (value,) = step("level2_1", [(2, 1, coeff2[1], near2[1])], [basis_v])
     third(1, value)
-    second(3, ahead)
-
-    def tail(j, after, flops=COST):
-        (coeff4,) = step(f"level3_{j}", [(3, j, coeff3[j], near3[j])], after, flops)
+
+    def tail(j, after, arrived=()):
+        (coeff4,) = step(f"level3_{j}", [(3, j, coeff3[j], near3[j])], after)
         near4 = cross(4, coeff4)
-        (partial,) = call(
-            functools.partial(half_kernel, bits[4], parts[j]),
-            f"half_{j}",
-            [VMEM] * 2,
-            [in_vmem(rank, widths[j], dtype=F32)],
+        partial, *totals = call(
+            functools.partial(between_kernel, bits[4], parts[j], [len(group) for _, group in arrived]),
+            f"between_{j}",
+            [VMEM] * (2 + sum(len(group) for _, group in arrived)),
+            [in_vmem(rank, widths[j], dtype=F32)] + [in_vmem(rows, widths[at]) for at, _ in arrived],
             [],
-            [here(coeff4), here(weights[4])],
+            [here(v) for v in (coeff4, weights[4], *(v for _, group in arrived for v in group))],
         )
-        mine, pieces = call(
+        out = call(
             functools.partial(last_kernel, bits[4], parts[j]),
             f"last_{j}",
             [VMEM] * 4,
-            [in_vmem(rows, widths[j], dtype=F32), in_vmem(n_blk * rows, widths[j])],
+            [in_vmem(rows, widths[j], dtype=F32)] + [in_vmem(rows, widths[j])] * (n_blk - 1),
             [],
             [here(v) for v in (partial, near4, weights[4], basis_v)],
+            flops=COST if j < len(widths) - 1 else 0,
         )
-        return mine, lax.all_to_all(pieces, "blk", 0, 0, tiled=True)
-
-    groups = [tail(0, [coeff3[1]])]
-    (value,) = step("level2_2", [(2, 2, coeff2[2], near2[2])], [groups[0][0]])
+        group = [out[0]] + [partner(out[d], "blk", d) for d in range(n_blk - 1, 0, -1)]
+        return group, totals
+
+    group0, _ = tail(0, [coeff3[1]])
+    (value,) = step("level2_2", [(2, 2, coeff2[2], near2[2])], [group0[0]])
     third(2, value)
-    (value,) = step("level2_3", [(2, 3, coeff2[3], near2[3])], [coeff3[2]])
+    (total0,) = call(
+        sum_kernel,
+        "sum_0",
+        [VMEM] * n_blk,
+        [in_vmem(rows, widths[0])],
+        [],
+        [here(v) for v in group0],
+        [coeff3[2]],
+    )
+    (value,) = step("level1_3", [job1(3)], [total0])
+    second(3, value)
+    group1, _ = tail(1, [coeff2[3]])
+    (value,) = step("level2_3", [(2, 3, coeff2[3], near2[3])], [group1[0]])
     third(3, value)
-    groups.append(tail(1, [coeff3[3]]))
-    groups.append(tail(2, [groups[1][0]]))
-    groups.append(tail(3, [groups[2][0]]))
+    group2, (total1,) = tail(2, [coeff3[3]], [(1, group1)])
+    group3, _ = tail(3, [group2[0]])
+    groups = [[total0], [total1], group2, group3]
     flat = [here(v) for group in groups for v in group]
     return pl.pallas_call(
-        functools.partial(end_kernel, places),
+        functools.partial(end_kernel, places, [len(group) for group in groups]),
         name="end",
         in_specs=[VMEM] * len(flat),
         out_specs=VMEM,

time: 92.5 us -> 70.1 us (0.76)
  blocking collectives: 22.6 us -> 0 us
  starting transfers between devices: 21.7 us -> 31.6 us
  local copies, waits for them, and re-layouts: 5.86 us -> 0 us
  waiting for transfers between devices: 23.6 us -> 21.6 us
  Pallas kernels: 18 us -> 16.4 us
    all_to_all x2 -> x0, blocking collectives: 22.6 us -> none  [tail(): return (mine, lax.all_to_all(pieces, 'blk', 0, 0, tiled=True))]
    ppermute x14 -> x26, starting transfers between devices: 13.4 us -> 31.6 us  [partner(): return lax.ppermute(value, axis, pairs)]
    all_to_all x2 -> x0, starting transfers between devices: 8.37 us -> none  [tail(): return (mine, lax.all_to_all(pieces, 'blk', 0, 0, tiled=True))]
    unnamed x24 -> x0, local copies, waits for them, and re-layouts: 5.86 us -> none
    all_to_all x2 -> x0, waiting for transfers between devices: 4.03 us -> none  [tail(): return (mine, lax.all_to_all(pieces, 'blk', 0, 0, tiled=True))]
    ppermute x14 -> x26, waiting for transfers between devices: 19.5 us -> 21.6 us  [partner(): return lax.ppermute(value, axis, pairs)]
    pallas_call x20 -> x23, Pallas kernels: 17 us -> 15.5 us  [call(): pl.pallas_call(body, name=name, in_specs=[*in_specs, *[ANY] * len(after)]...]
  transfers between devices with their start and end apart: 16 -> 26, of which waited for: 7 -> 14; matrix products, arithmetic and copies ran while one was open for 0% -> 0% of each run, Pallas kernels for 14% -> 17%
where the time goes in v13:
time: 70.1 us; the launch traced here: 69.9 us
  starting transfers between devices  31.6 us (45%)
  waiting for transfers between devices  21.6 us (31%)
  Pallas kernels  16.4 us (23%)
    ppermute x26, starting transfers between devices, partner(): return lax.ppermute(value, axis, pairs)  31.6 us
    ppermute x26, waiting for transfers between devices, partner(): return lax.ppermute(value, axis, pairs)  21.6 us
    pallas_call x23, Pallas kernels, call(): pl.pallas_call(body, name=name, in_specs=[*in_specs, *[ANY] * len(after)]...  15.5 us
  transfers between devices with their start and end apart: 26, of which 14 were waited for; matrix products, arithmetic and copies ran while one was open for 0% of the time, Pallas kernels for 17%

profile of v13, /device:TPU:0, one launch (start us, length us, event | category | flops | bytes accessed | tf_op | source)
XLA Modules:
  0.0 69.9 jit_solution(11393031174351648190)
XLA Ops:
  0.0 3.7 %leaf.1 = (bf16[384,128]{1,0:T(8,128)(2,1)S(1)}, bf16[384,896]{1,0:T(8,128)(2,1)S(1)}, bf16[2,384,768]{2,1,0:T(8,128)(2,1)S(1)}, bf16[2,384,768]{2,1,0:T(8,128)(2,1)S(1)}) custom-call(bf16[2,1024,512]{2,1,0:T(8,128)(2,1)} %bitcast.9, bf16[2,384,1024]{2,1,0:T(8,128)(2,1)} %bitcast.10, bf16[5,2,384,768]{3,2,1,0:T(8,128)(2,1)} %bitcast.7, s32[2,5]{1,0:T(2,128)} %bitcast.12), custom_call_target="tpu_custom_call" | custom-call | flops 6000000000 | tf_op jit(solution)/shard_map/leaf/pallas_call | solution.py:41
  3.7 0.5 collective-permute-start.2
  4.3 1.8 %collective-permute-done.refs_1_ = bf16[384,128]{1,0:T(8,128)(2,1)S(1)} collective-permute-done((bf16[384,128]{1,0:T(8,128)(2,1)S(1)}, bf16[384,128]{1,0:T(8,128)(2,1)S(1)}, u32[]{:S(2)}, u32[]{:S(2)}) %collective-permute-start) | collective-permute-done | bytes 98336 | tf_op jit(solution)/shard_map/ppermute | solution.py:55
  6.4 3.0 %collective-permute-start.1 = (bf16[384,128]{1,0:T(8,128)(2,1)S(1)}, bf16[384,128]{1,0:T(8,128)(2,1)S(1)}, u32[]{:S(2)}, u32[]{:S(2)}) collective-permute-start(bf16[384,128]{1,0:T(8,128)(2,1)S(1)} %level1_0.1.refs_3_.refs_0_), channel_id=1, source_target_pairs={{0,2},{1,3},{2,0},{3,1},{4,6},{5,7},{6,4},{7,5},{8,10},{9,11},{10,... | collective-permute-start | bytes 294920 | tf_op jit(solution)/shard_map/ppermute | solution.py:55
  9.5 0.4 level1_1.1.refs_3_.refs_0_
  9.9 2.8 %collective-permute-done.1.refs_1_ = bf16[384,128]{1,0:T(8,128)(2,1)S(1)} collective-permute-done((bf16[384,128]{1,0:T(8,128)(2,1)S(1)}, bf16[384,128]{1,0:T(8,128)(2,1)S(1)}, u32[]{:S(2)}, u32[]{:S(2)}) %collective-permute-start.1) | collective-permute-done | bytes 98336 | tf_op jit(solution)/shard_map/ppermute | solution.py:55
  13.1 3.0 %collective-permute-start.3 = (bf16[384,128]{1,0:T(8,128)(2,1)S(1)}, bf16[384,128]{1,0:T(8,128)(2,1)S(1)}, u32[]{:S(2)}, u32[]{:S(2)}) collective-permute-start(bf16[384,128]{1,0:T(8,128)(2,1)S(1)} %level2_0.1.refs_3_.refs_0_), channel_id=1, source_target_pairs={{0,4},{1,5},{2,6},{3,7},{4,0},{5,1},{6,2},{7,3},{8,12},{9,13},{10,... | collective-permute-start | bytes 294920 | tf_op jit(solution)/shard_map/ppermute | solution.py:55
  16.1 0.5 level1_2.1.refs_3_.refs_0_
  16.6 2.0 %collective-permute-start.9 = (bf16[384,384]{1,0:T(8,128)(2,1)S(1)}, bf16[384,384]{1,0:T(8,128)(2,1)S(1)}, u32[]{:S(2)}, u32[]{:S(2)}) collective-permute-start(bf16[384,384]{1,0:T(8,128)(2,1)S(1)} %level1_2.1.refs_3_.refs_0_), channel_id=1, source_target_pairs={{0,2},{1,3},{2,0},{3,1},{4,6},{5,7},{6,4},{7,5},{8,10},{9,11},{10,... | collective-permute-start | bytes 884744 | tf_op jit(solution)/shard_map/ppermute | solution.py:55
  18.7 2.5 %prefetch.1 = (bf16[2,384,768]{2,1,0:T(8,128)(2,1)S(1)}, bf16[2,384,768]{2,1,0:T(8,128)(2,1)S(1)}, bf16[2,1024,384]{2,1,0:T(8,128)(2,1)S(1)}) custom-call(bf16[5,2,384,768]{3,2,1,0:T(8,128)(2,1)} %bitcast.8, bf16[2,1024,384]{2,1,0:T(8,128)(2,1)} %bitcast.11, s32[2,5]{1,0:T(2,128)} %bitcast.13, bf16[384,384]{1,0:T(8,128)(2,1)S(1)} %level1_2.1.refs_3_.refs_0_), custom_call_target="tpu_custom_call" | custom-call | flops 6000000000 | tf_op jit(solution)/shard_map/prefetch/pallas_call | solution.py:41
  21.2 0.4 level2_1.1.refs_3_.refs_0_
  21.6 0.4 collective-permute-start.12
  22.6 1.0 %collective-permute-done.5.refs_1_ = bf16[384,128]{1,0:T(8,128)(2,1)S(1)} collective-permute-done((bf16[384,128]{1,0:T(8,128)(2,1)S(1)}, bf16[384,128]{1,0:T(8,128)(2,1)S(1)}, u32[]{:S(2)}, u32[]{:S(2)}) %collective-permute-start.5) | collective-permute-done | bytes 98336 | tf_op jit(solution)/shard_map/ppermute | solution.py:55
  23.7 0.6 last_0.1
  24.3 2.5 %collective-permute-start.6 = (bf16[256,128]{1,0:T(8,128)(2,1)S(1)}, bf16[256,128]{1,0:T(8,128)(2,1)S(1)}, u32[]{:S(2)}, u32[]{:S(2)}) collective-permute-start(bf16[256,128]{1,0:T(8,128)(2,1)S(1)} %get-tuple-element.38), channel_id=1, source_target_pairs={{0,24},{8,16},{16,8},{24,0},{1,25},{9,17},{17,9},{25,1},{2,26},{10... | collective-permute-start | bytes 196616 | tf_op jit(solution)/shard_map/ppermute | solution.py:55
  26.8 0.5 collective-permute-start.7
  27.3 0.5 collective-permute-start.8
  27.8 0.9 %collective-permute-done.9.refs_1_ = bf16[384,384]{1,0:T(8,128)(2,1)S(1)} collective-permute-done((bf16[384,384]{1,0:T(8,128)(2,1)S(1)}, bf16[384,384]{1,0:T(8,128)(2,1)S(1)}, u32[]{:S(2)}, u32[]{:S(2)}) %collective-permute-start.9) | collective-permute-done | bytes 294944 | tf_op jit(solution)/shard_map/ppermute | solution.py:55
  28.7 0.5 level2_2.1.refs_4_.refs_0_
  29.2 2.0 %collective-permute-start.10 = (bf16[384,384]{1,0:T(8,128)(2,1)S(1)}, bf16[384,384]{1,0:T(8,128)(2,1)S(1)}, u32[]{:S(2)}, u32[]{:S(2)}) collective-permute-start(bf16[384,384]{1,0:T(8,128)(2,1)S(1)} %level2_2.1.refs_4_.refs_0_), channel_id=1, source_target_pairs={{0,4},{1,5},{2,6},{3,7},{4,0},{5,1},{6,2},{7,3},{8,12},{9,13},{10,... | collective-permute-start | bytes 884744 | tf_op jit(solution)/shard_map/ppermute | solution.py:55
  31.6 0.4 level1_3.1.refs_3_.refs_0_
  31.9 2.2 %collective-permute-start.11 = (bf16[384,256]{1,0:T(8,128)(2,1)S(1)}, bf16[384,256]{1,0:T(8,128)(2,1)S(1)}, u32[]{:S(2)}, u32[]{:S(2)}) collective-permute-start(bf16[384,256]{1,0:T(8,128)(2,1)S(1)} %level1_3.1.refs_3_.refs_0_), channel_id=1, source_target_pairs={{0,2},{1,3},{2,0},{3,1},{4,6},{5,7},{6,4},{7,5},{8,10},{9,11},{10,... | collective-permute-start | bytes 589832 | tf_op jit(solution)/shard_map/ppermute | solution.py:55
  34.2 0.4 level3_1.1.refs_0_
  34.9 1.2 %collective-permute-done.13.refs_1_ = bf16[384,256]{1,0:T(8,128)(2,1)S(1)} collective-permute-done((bf16[384,256]{1,0:T(8,128)(2,1)S(1)}, bf16[384,256]{1,0:T(8,128)(2,1)S(1)}, u32[]{:S(2)}, u32[]{:S(2)}) %collective-permute-start.13) | collective-permute-done | bytes 196640 | tf_op jit(solution)/shard_map/ppermute | solution.py:55
  36.1 0.8 %last_1.1 = (f32[256,256]{1,0:T(8,128)S(1)}, bf16[256,256]{1,0:T(8,128)(2,1)S(1)}, bf16[256,256]{1,0:T(8,128)(2,1)S(1)}, bf16[256,256]{1,0:T(8,128)(2,1)S(1)}) custom-call(f32[384,256]{1,0:T(8,128)S(1)} %between_1.1.refs_0_, bf16[384,256]{1,0:T(8,128)(2,1)S(1)} %collective-permute-done.13.refs_1_, ...), custom_call_target="tpu_custom_call" | custom-call | flops 6000000000 | tf_op jit(solution)/shard_map/last_1/pallas_call | solution.py:41
  36.9 2.5 %collective-permute-start.14 = (bf16[256,256]{1,0:T(8,128)(2,1)S(1)}, bf16[256,256]{1,0:T(8,128)(2,1)S(1)}, u32[]{:S(2)}, u32[]{:S(2)}) collective-permute-start(bf16[256,256]{1,0:T(8,128)(2,1)S(1)} %get-tuple-element.42), channel_id=1, source_target_pairs={{0,24},{8,16},{16,8},{24,0},{1,25},{9,17},{17,9},{25,1},{2,26},{10... | collective-permute-start | bytes 393224 | tf_op jit(solution)/shard_map/ppermute | solution.py:55
  39.4 0.5 collective-permute-start.15
  39.9 0.5 collective-permute-start.16
  40.4 0.8 %collective-permute-done.11.refs_1_ = bf16[384,256]{1,0:T(8,128)(2,1)S(1)} collective-permute-done((bf16[384,256]{1,0:T(8,128)(2,1)S(1)}, bf16[384,256]{1,0:T(8,128)(2,1)S(1)}, u32[]{:S(2)}, u32[]{:S(2)}) %collective-permute-start.11) | collective-permute-done | bytes 196640 | tf_op jit(solution)/shard_map/ppermute | solution.py:55
  41.6 3.3 %collective-permute-start.21 = (bf16[384,256]{1,0:T(8,128)(2,1)S(1)}, bf16[384,256]{1,0:T(8,128)(2,1)S(1)}, u32[]{:S(2)}, u32[]{:S(2)}) collective-permute-start(bf16[384,256]{1,0:T(8,128)(2,1)S(1)} %level2_3.1.refs_3_.refs_0_), channel_id=1, source_target_pairs={{0,4},{1,5},{2,6},{3,7},{4,0},{5,1},{6,2},{7,3},{8,12},{9,13},{10,... | collective-permute-start | bytes 589832 | tf_op jit(solution)/shard_map/ppermute | solution.py:55
  44.9 2.8 %collective-permute-done.10.refs_1_ = bf16[384,384]{1,0:T(8,128)(2,1)S(1)} collective-permute-done((bf16[384,384]{1,0:T(8,128)(2,1)S(1)}, bf16[384,384]{1,0:T(8,128)(2,1)S(1)}, u32[]{:S(2)}, u32[]{:S(2)}) %collective-permute-start.10) | collective-permute-done | bytes 294944 | tf_op jit(solution)/shard_map/ppermute | solution.py:55
  47.7 0.5 level3_2.1.refs_0_
  48.3 0.4 between_2.1
  48.7 1.2 %collective-permute-done.17.refs_1_ = bf16[384,384]{1,0:T(8,128)(2,1)S(1)} collective-permute-done((bf16[384,384]{1,0:T(8,128)(2,1)S(1)}, bf16[384,384]{1,0:T(8,128)(2,1)S(1)}, u32[]{:S(2)}, u32[]{:S(2)}) %collective-permute-start.17) | collective-permute-done | bytes 294944 | tf_op jit(solution)/shard_map/ppermute | solution.py:55
  49.8 1.2 %last_2.1 = (f32[256,384]{1,0:T(8,128)S(1)}, bf16[256,384]{1,0:T(8,128)(2,1)S(1)}, bf16[256,384]{1,0:T(8,128)(2,1)S(1)}, bf16[256,384]{1,0:T(8,128)(2,1)S(1)}) custom-call(f32[384,384]{1,0:T(8,128)S(1)} %get-tuple-element.46.refs_0_, bf16[384,384]{1,0:T(8,128)(2,1)S(1)} %collective-permute-done.17.refs_1_, ...), custom_call_target="tpu_custom_call" | custom-call | flops 6000000000 | tf_op jit(solution)/shard_map/last_2/pallas_call | solution.py:41
  51.1 2.5 %collective-permute-start.18 = (bf16[256,384]{1,0:T(8,128)(2,1)S(1)}, bf16[256,384]{1,0:T(8,128)(2,1)S(1)}, u32[]{:S(2)}, u32[]{:S(2)}) collective-permute-start(bf16[256,384]{1,0:T(8,128)(2,1)S(1)} %get-tuple-element.48), channel_id=1, source_target_pairs={{0,24},{8,16},{16,8},{24,0},{1,25},{9,17},{17,9},{25,1},{2,26},{10... | collective-permute-start | bytes 589832 | tf_op jit(solution)/shard_map/ppermute | solution.py:55
  53.6 0.5 collective-permute-start.19
  54.1 0.5 collective-permute-start.20
  54.7 0.4 level3_3.1.refs_0_
  55.4 1.2 %collective-permute-done.22.refs_1_ = bf16[384,256]{1,0:T(8,128)(2,1)S(1)} collective-permute-done((bf16[384,256]{1,0:T(8,128)(2,1)S(1)}, bf16[384,256]{1,0:T(8,128)(2,1)S(1)}, u32[]{:S(2)}, u32[]{:S(2)}) %collective-permute-start.22) | collective-permute-done | bytes 196640 | tf_op jit(solution)/shard_map/ppermute | solution.py:55
  56.5 0.8 %last_3.1 = (f32[256,256]{1,0:T(8,128)S(1)}, bf16[256,256]{1,0:T(8,128)(2,1)S(1)}, bf16[256,256]{1,0:T(8,128)(2,1)S(1)}, bf16[256,256]{1,0:T(8,128)(2,1)S(1)}) custom-call(f32[384,256]{1,0:T(8,128)S(1)} %between_3.1.refs_0_, bf16[384,256]{1,0:T(8,128)(2,1)S(1)} %collective-permute-done.22.refs_1_, ...), custom_call_target="tpu_custom_call" | custom-call | tf_op jit(solution)/shard_map/last_3/pallas_call | solution.py:41
  57.4 2.5 %collective-permute-start.23 = (bf16[256,256]{1,0:T(8,128)(2,1)S(1)}, bf16[256,256]{1,0:T(8,128)(2,1)S(1)}, u32[]{:S(2)}, u32[]{:S(2)}) collective-permute-start(bf16[256,256]{1,0:T(8,128)(2,1)S(1)} %get-tuple-element.52), channel_id=1, source_target_pairs={{0,24},{8,16},{16,8},{24,0},{1,25},{9,17},{17,9},{25,1},{2,26},{10... | collective-permute-start | bytes 393224 | tf_op jit(solution)/shard_map/ppermute | solution.py:55
  59.9 0.5 collective-permute-start.24
  60.4 1.0 %collective-permute-start.25 = (bf16[256,256]{1,0:T(8,128)(2,1)S(1)}, bf16[256,256]{1,0:T(8,128)(2,1)S(1)}, u32[]{:S(2)}, u32[]{:S(2)}) collective-permute-start(bf16[256,256]{1,0:T(8,128)(2,1)S(1)} %get-tuple-element.54), channel_id=1, source_target_pairs={{0,8},{8,0},{16,24},{24,16},{1,9},{9,1},{17,25},{25,17},{2,10},{10... | collective-permute-start | bytes 393224 | tf_op jit(solution)/shard_map/ppermute | solution.py:55
  61.3 2.8 %collective-permute-done.19.refs_4_ = bf16[256,384]{1,0:T(8,128)(2,1)S(1)} collective-permute-done((bf16[256,384]{1,0:T(8,128)(2,1)S(1)}, bf16[256,384]{1,0:T(8,128)(2,1)S(1)}, u32[]{:S(2)}, u32[]{:S(2)}) %collective-permute-start.19) | collective-permute-done | bytes 196640 | tf_op jit(solution)/shard_map/ppermute | solution.py:55
  64.1 2.8 %collective-permute-done.23.refs_7_ = bf16[256,256]{1,0:T(8,128)(2,1)S(1)} collective-permute-done((bf16[256,256]{1,0:T(8,128)(2,1)S(1)}, bf16[256,256]{1,0:T(8,128)(2,1)S(1)}, u32[]{:S(2)}, u32[]{:S(2)}) %collective-permute-start.23) | collective-permute-done | bytes 131104 | tf_op jit(solution)/shard_map/ppermute | solution.py:55
  66.9 1.9 %collective-permute-done.24.refs_8_ = bf16[256,256]{1,0:T(8,128)(2,1)S(1)} collective-permute-done((bf16[256,256]{1,0:T(8,128)(2,1)S(1)}, bf16[256,256]{1,0:T(8,128)(2,1)S(1)}, u32[]{:S(2)}, u32[]{:S(2)}) %collective-permute-start.24) | collective-permute-done | bytes 131104 | tf_op jit(solution)/shard_map/ppermute | solution.py:55
  69.0 1.0 %end.1 = bf16[2,256,512]{2,1,0:T(8,128)(2,1)} custom-call(bf16[256,128]{1,0:T(8,128)(2,1)S(1)} %sum_0.1.refs_3_.refs_0_, bf16[256,256]{1,0:T(8,128)(2,1)S(1)} %get-tuple-element.45.refs_1_, f32[256,384]{1,0:T(8,128)S(1)} %get-tuple-element.47.refs_3_.refs_2_, bf16[256,384]{1,0:T(8,128)(2,1)S(1)} %collective-permute-done.18.refs_3_, ...), custom_call_target="tpu_custom_call" | custom-call | tf_op jit(solution)/shard_map/end/pallas_call | solution.py:333
  (28 shorter events, 3.1 us)
Async XLA Ops:
  3.7 5.8 %collective-permute-start.2 = (bf16[384,896]{1,0:T(8,128)(2,1)S(1)}, bf16[384,896]{1,0:T(8,128)(2,1)S(1)}, u32[]{:S(2)}, u32[]{:S(2)}) collective-permute-start(bf16[384,896]{1,0:T(8,128)(2,1)S(1)} %get-tuple-element.33.refs_0_), channel_id=1, source_target_pairs={{0,1},{1,0},{2,3},{3,2},{4,5},{5,4},{6,7},{7,6},{8,9},{9,8},{10,11... | collective-permute-start | bytes 2064392 | tf_op jit(solution)/shard_map/ppermute | solution.py:55
  4.2 1.9 %collective-permute-start = (bf16[384,128]{1,0:T(8,128)(2,1)S(1)}, bf16[384,128]{1,0:T(8,128)(2,1)S(1)}, u32[]{:S(2)}, u32[]{:S(2)}) collective-permute-start(bf16[384,128]{1,0:T(8,128)(2,1)S(1)} %get-tuple-element.30.refs_0_), channel_id=1, source_target_pairs={{0,1},{1,0},{2,3},{3,2},{4,5},{5,4},{6,7},{7,6},{8,9},{9,8},{10,11... | collective-permute-start | bytes 294920 | tf_op jit(solution)/shard_map/ppermute | solution.py:55
  6.4 6.3 %collective-permute-start.1 = (bf16[384,128]{1,0:T(8,128)(2,1)S(1)}, bf16[384,128]{1,0:T(8,128)(2,1)S(1)}, u32[]{:S(2)}, u32[]{:S(2)}) collective-permute-start(bf16[384,128]{1,0:T(8,128)(2,1)S(1)} %level1_0.1.refs_3_.refs_0_), channel_id=1, source_target_pairs={{0,2},{1,3},{2,0},{3,1},{4,6},{5,7},{6,4},{7,5},{8,10},{9,11},{10,... | collective-permute-start | bytes 294920 | tf_op jit(solution)/shard_map/ppermute | solution.py:55
  9.8 11.4 %collective-permute-start.4 = (bf16[384,256]{1,0:T(8,128)(2,1)S(1)}, bf16[384,256]{1,0:T(8,128)(2,1)S(1)}, u32[]{:S(2)}, u32[]{:S(2)}) collective-permute-start(bf16[384,256]{1,0:T(8,128)(2,1)S(1)} %level1_1.1.refs_3_.refs_0_), channel_id=1, source_target_pairs={{0,2},{1,3},{2,0},{3,1},{4,6},{5,7},{6,4},{7,5},{8,10},{9,11},{10,... | collective-permute-start | bytes 589832 | tf_op jit(solution)/shard_map/ppermute | solution.py:55
  13.1 8.9 %collective-permute-start.3 = (bf16[384,128]{1,0:T(8,128)(2,1)S(1)}, bf16[384,128]{1,0:T(8,128)(2,1)S(1)}, u32[]{:S(2)}, u32[]{:S(2)}) collective-permute-start(bf16[384,128]{1,0:T(8,128)(2,1)S(1)} %level2_0.1.refs_3_.refs_0_), channel_id=1, source_target_pairs={{0,4},{1,5},{2,6},{3,7},{4,0},{5,1},{6,2},{7,3},{8,12},{9,13},{10,... | collective-permute-start | bytes 294920 | tf_op jit(solution)/shard_map/ppermute | solution.py:55
  16.6 12.1 %collective-permute-start.9 = (bf16[384,384]{1,0:T(8,128)(2,1)S(1)}, bf16[384,384]{1,0:T(8,128)(2,1)S(1)}, u32[]{:S(2)}, u32[]{:S(2)}) collective-permute-start(bf16[384,384]{1,0:T(8,128)(2,1)S(1)} %level1_2.1.refs_3_.refs_0_), channel_id=1, source_target_pairs={{0,2},{1,3},{2,0},{3,1},{4,6},{5,7},{6,4},{7,5},{8,10},{9,11},{10,... | collective-permute-start | bytes 884744 | tf_op jit(solution)/shard_map/ppermute | solution.py:55
  21.6 12.6 %collective-permute-start.12 = (bf16[384,256]{1,0:T(8,128)(2,1)S(1)}, bf16[384,256]{1,0:T(8,128)(2,1)S(1)}, u32[]{:S(2)}, u32[]{:S(2)}) collective-permute-start(bf16[384,256]{1,0:T(8,128)(2,1)S(1)} %level2_1.1.refs_3_.refs_0_), channel_id=1, source_target_pairs={{0,4},{1,5},{2,6},{3,7},{4,0},{5,1},{6,2},{7,3},{8,12},{9,13},{10,... | collective-permute-start | bytes 589832 | tf_op jit(solution)/shard_map/ppermute | solution.py:55
  22.3 1.4 %collective-permute-start.5 = (bf16[384,128]{1,0:T(8,128)(2,1)S(1)}, bf16[384,128]{1,0:T(8,128)(2,1)S(1)}, u32[]{:S(2)}, u32[]{:S(2)}) collective-permute-start(bf16[384,128]{1,0:T(8,128)(2,1)S(1)} %level3_0.1.refs_0_), channel_id=1, source_target_pairs={{0,1},{1,0},{2,3},{3,2},{4,5},{5,4},{6,7},{7,6},{8,9},{9,8},{10,11... | collective-permute-start | bytes 294920 | tf_op jit(solution)/shard_map/ppermute | solution.py:55
  24.3 7.0 %collective-permute-start.6 = (bf16[256,128]{1,0:T(8,128)(2,1)S(1)}, bf16[256,128]{1,0:T(8,128)(2,1)S(1)}, u32[]{:S(2)}, u32[]{:S(2)}) collective-permute-start(bf16[256,128]{1,0:T(8,128)(2,1)S(1)} %get-tuple-element.38), channel_id=1, source_target_pairs={{0,24},{8,16},{16,8},{24,0},{1,25},{9,17},{17,9},{25,1},{2,26},{10... | collective-permute-start | bytes 196616 | tf_op jit(solution)/shard_map/ppermute | solution.py:55
  26.8 4.4 %collective-permute-start.7 = (bf16[256,128]{1,0:T(8,128)(2,1)S(1)}, bf16[256,128]{1,0:T(8,128)(2,1)S(1)}, u32[]{:S(2)}, u32[]{:S(2)}) collective-permute-start(bf16[256,128]{1,0:T(8,128)(2,1)S(1)} %get-tuple-element.39), channel_id=1, source_target_pairs={{0,16},{8,24},{16,0},{24,8},{1,17},{9,25},{17,1},{25,9},{2,18},{10... | collective-permute-start | bytes 196616 | tf_op jit(solution)/shard_map/ppermute | solution.py:55
  27.3 4.3 %collective-permute-start.8 = (bf16[256,128]{1,0:T(8,128)(2,1)S(1)}, bf16[256,128]{1,0:T(8,128)(2,1)S(1)}, u32[]{:S(2)}, u32[]{:S(2)}) collective-permute-start(bf16[256,128]{1,0:T(8,128)(2,1)S(1)} %get-tuple-element.40), channel_id=1, source_target_pairs={{0,8},{8,0},{16,24},{24,16},{1,9},{9,1},{17,25},{25,17},{2,10},{10... | collective-permute-start | bytes 196616 | tf_op jit(solution)/shard_map/ppermute | solution.py:55
  29.2 18.5 %collective-permute-start.10 = (bf16[384,384]{1,0:T(8,128)(2,1)S(1)}, bf16[384,384]{1,0:T(8,128)(2,1)S(1)}, u32[]{:S(2)}, u32[]{:S(2)}) collective-permute-start(bf16[384,384]{1,0:T(8,128)(2,1)S(1)} %level2_2.1.refs_4_.refs_0_), channel_id=1, source_target_pairs={{0,4},{1,5},{2,6},{3,7},{4,0},{5,1},{6,2},{7,3},{8,12},{9,13},{10,... | collective-permute-start | bytes 884744 | tf_op jit(solution)/shard_map/ppermute | solution.py:55
  31.9 9.3 %collective-permute-start.11 = (bf16[384,256]{1,0:T(8,128)(2,1)S(1)}, bf16[384,256]{1,0:T(8,128)(2,1)S(1)}, u32[]{:S(2)}, u32[]{:S(2)}) collective-permute-start(bf16[384,256]{1,0:T(8,128)(2,1)S(1)} %level1_3.1.refs_3_.refs_0_), channel_id=1, source_target_pairs={{0,2},{1,3},{2,0},{3,1},{4,6},{5,7},{6,4},{7,5},{8,10},{9,11},{10,... | collective-permute-start | bytes 589832 | tf_op jit(solution)/shard_map/ppermute | solution.py:55
  34.5 1.5 %collective-permute-start.13 = (bf16[384,256]{1,0:T(8,128)(2,1)S(1)}, bf16[384,256]{1,0:T(8,128)(2,1)S(1)}, u32[]{:S(2)}, u32[]{:S(2)}) collective-permute-start(bf16[384,256]{1,0:T(8,128)(2,1)S(1)} %level3_1.1.refs_0_), channel_id=1, source_target_pairs={{0,1},{1,0},{2,3},{3,2},{4,5},{5,4},{6,7},{7,6},{8,9},{9,8},{10,11... | collective-permute-start | bytes 589832 | tf_op jit(solution)/shard_map/ppermute | solution.py:55
  36.9 11.4 %collective-permute-start.14 = (bf16[256,256]{1,0:T(8,128)(2,1)S(1)}, bf16[256,256]{1,0:T(8,128)(2,1)S(1)}, u32[]{:S(2)}, u32[]{:S(2)}) collective-permute-start(bf16[256,256]{1,0:T(8,128)(2,1)S(1)} %get-tuple-element.42), channel_id=1, source_target_pairs={{0,24},{8,16},{16,8},{24,0},{1,25},{9,17},{17,9},{25,1},{2,26},{10... | collective-permute-start | bytes 393224 | tf_op jit(solution)/shard_map/ppermute | solution.py:55
  39.4 8.9 %collective-permute-start.15 = (bf16[256,256]{1,0:T(8,128)(2,1)S(1)}, bf16[256,256]{1,0:T(8,128)(2,1)S(1)}, u32[]{:S(2)}, u32[]{:S(2)}) collective-permute-start(bf16[256,256]{1,0:T(8,128)(2,1)S(1)} %get-tuple-element.43), channel_id=1, source_target_pairs={{0,16},{8,24},{16,0},{24,8},{1,17},{9,25},{17,1},{25,9},{2,18},{10... | collective-permute-start | bytes 393224 | tf_op jit(solution)/shard_map/ppermute | solution.py:55
  39.9 8.4 %collective-permute-start.16 = (bf16[256,256]{1,0:T(8,128)(2,1)S(1)}, bf16[256,256]{1,0:T(8,128)(2,1)S(1)}, u32[]{:S(2)}, u32[]{:S(2)}) collective-permute-start(bf16[256,256]{1,0:T(8,128)(2,1)S(1)} %get-tuple-element.44), channel_id=1, source_target_pairs={{0,8},{8,0},{16,24},{24,16},{1,9},{9,1},{17,25},{25,17},{2,10},{10... | collective-permute-start | bytes 393224 | tf_op jit(solution)/shard_map/ppermute | solution.py:55
  41.6 13.1 %collective-permute-start.21 = (bf16[384,256]{1,0:T(8,128)(2,1)S(1)}, bf16[384,256]{1,0:T(8,128)(2,1)S(1)}, u32[]{:S(2)}, u32[]{:S(2)}) collective-permute-start(bf16[384,256]{1,0:T(8,128)(2,1)S(1)} %level2_3.1.refs_3_.refs_0_), channel_id=1, source_target_pairs={{0,4},{1,5},{2,6},{3,7},{4,0},{5,1},{6,2},{7,3},{8,12},{9,13},{10,... | collective-permute-start | bytes 589832 | tf_op jit(solution)/shard_map/ppermute | solution.py:55
  48.2 1.6 %collective-permute-start.17 = (bf16[384,384]{1,0:T(8,128)(2,1)S(1)}, bf16[384,384]{1,0:T(8,128)(2,1)S(1)}, u32[]{:S(2)}, u32[]{:S(2)}) collective-permute-start(bf16[384,384]{1,0:T(8,128)(2,1)S(1)} %level3_2.1.refs_0_), channel_id=1, source_target_pairs={{0,1},{1,0},{2,3},{3,2},{4,5},{5,4},{6,7},{7,6},{8,9},{9,8},{10,11... | collective-permute-start | bytes 884744 | tf_op jit(solution)/shard_map/ppermute | solution.py:55
  51.1 9.3 %collective-permute-start.18 = (bf16[256,384]{1,0:T(8,128)(2,1)S(1)}, bf16[256,384]{1,0:T(8,128)(2,1)S(1)}, u32[]{:S(2)}, u32[]{:S(2)}) collective-permute-start(bf16[256,384]{1,0:T(8,128)(2,1)S(1)} %get-tuple-element.48), channel_id=1, source_target_pairs={{0,24},{8,16},{16,8},{24,0},{1,25},{9,17},{17,9},{25,1},{2,26},{10... | collective-permute-start | bytes 589832 | tf_op jit(solution)/shard_map/ppermute | solution.py:55
  53.6 10.5 %collective-permute-start.19 = (bf16[256,384]{1,0:T(8,128)(2,1)S(1)}, bf16[256,384]{1,0:T(8,128)(2,1)S(1)}, u32[]{:S(2)}, u32[]{:S(2)}) collective-permute-start(bf16[256,384]{1,0:T(8,128)(2,1)S(1)} %get-tuple-element.49), channel_id=1, source_target_pairs={{0,16},{8,24},{16,0},{24,8},{1,17},{9,25},{17,1},{25,9},{2,18},{10... | collective-permute-start | bytes 589832 | tf_op jit(solution)/shard_map/ppermute | solution.py:55
  54.1 10.0 %collective-permute-start.20 = (bf16[256,384]{1,0:T(8,128)(2,1)S(1)}, bf16[256,384]{1,0:T(8,128)(2,1)S(1)}, u32[]{:S(2)}, u32[]{:S(2)}) collective-permute-start(bf16[256,384]{1,0:T(8,128)(2,1)S(1)} %get-tuple-element.50), channel_id=1, source_target_pairs={{0,8},{8,0},{16,24},{24,16},{1,9},{9,1},{17,25},{25,17},{2,10},{10... | collective-permute-start | bytes 589832 | tf_op jit(solution)/shard_map/ppermute | solution.py:55
  55.0 1.5 %collective-permute-start.22 = (bf16[384,256]{1,0:T(8,128)(2,1)S(1)}, bf16[384,256]{1,0:T(8,128)(2,1)S(1)}, u32[]{:S(2)}, u32[]{:S(2)}) collective-permute-start(bf16[384,256]{1,0:T(8,128)(2,1)S(1)} %level3_3.1.refs_0_), channel_id=1, source_target_pairs={{0,1},{1,0},{2,3},{3,2},{4,5},{5,4},{6,7},{7,6},{8,9},{9,8},{10,11... | collective-permute-start | bytes 589832 | tf_op jit(solution)/shard_map/ppermute | solution.py:55
  57.4 9.6 %collective-permute-start.23 = (bf16[256,256]{1,0:T(8,128)(2,1)S(1)}, bf16[256,256]{1,0:T(8,128)(2,1)S(1)}, u32[]{:S(2)}, u32[]{:S(2)}) collective-permute-start(bf16[256,256]{1,0:T(8,128)(2,1)S(1)} %get-tuple-element.52), channel_id=1, source_target_pairs={{0,24},{8,16},{16,8},{24,0},{1,25},{9,17},{17,9},{25,1},{2,26},{10... | collective-permute-start | bytes 393224 | tf_op jit(solution)/shard_map/ppermute | solution.py:55
  59.9 9.0 %collective-permute-start.24 = (bf16[256,256]{1,0:T(8,128)(2,1)S(1)}, bf16[256,256]{1,0:T(8,128)(2,1)S(1)}, u32[]{:S(2)}, u32[]{:S(2)}) collective-permute-start(bf16[256,256]{1,0:T(8,128)(2,1)S(1)} %get-tuple-element.53), channel_id=1, source_target_pairs={{0,16},{8,24},{16,0},{24,8},{1,17},{9,25},{17,1},{25,9},{2,18},{10... | collective-permute-start | bytes 393224 | tf_op jit(solution)/shard_map/ppermute | solution.py:55
  60.4 8.6 %collective-permute-start.25 = (bf16[256,256]{1,0:T(8,128)(2,1)S(1)}, bf16[256,256]{1,0:T(8,128)(2,1)S(1)}, u32[]{:S(2)}, u32[]{:S(2)}) collective-permute-start(bf16[256,256]{1,0:T(8,128)(2,1)S(1)} %get-tuple-element.54), channel_id=1, source_target_pairs={{0,8},{8,0},{16,24},{24,16},{1,9},{9,1},{17,25},{25,17},{2,10},{10... | collective-permute-start | bytes 393224 | tf_op jit(solution)/shard_map/ppermute | solution.py:55

commit v14 on v13

--- a/solution.py
+++ b/solution.py
@@ -7,7 +7,7 @@
 from jax.experimental.pallas import tpu as pltpu
 from jax.sharding import PartitionSpec as P
 
-SHARES = (1, 2, 3, 2)
+SHARES = (1, 3, 2, 2)
 PRELOADED = 2
 COST = 6 * 10**9
 BF16 = jnp.bfloat16
@@ -151,25 +151,36 @@
     refs[-1][...] = total.astype(BF16)
 
 
-def between_kernel(bit, parts, counts, own, weights, *refs):
+def between_kernel(bit, parts, counts, fold, own, weights, *refs):
     refs = list(refs)
     groups = [[refs.pop(0) for _ in range(count)] for count in counts]
+    halves = [refs.pop(0) for _ in range(2 * fold)]
     partial = refs.pop(0)
     for s, start, stop in parts:
         partial[:, start:stop] = half_dot(weights, s, upper_half(bit), own[:, start:stop])
-    for group, out in zip(groups, refs):
-        sum_kernel(*group, out)
-
-
-def last_kernel(bit, parts, partial, other, weights, basis, *refs):
-    rows = refs[0].shape[0]
+    for group in groups:
+        sum_kernel(*group, refs.pop(0))
+    if fold:
+        fold_kernel(*halves, *refs)
+
+
+def fold_kernel(keep, got, send, rest):
+    rows = rest.shape[0]
+    rest[...] = keep[:rows] + got[:rows].astype(F32)
+    send[...] = (keep[rows:] + got[rows:].astype(F32)).astype(BF16)
+
+
+def last_kernel(bit, parts, order, partial, other, weights, basis, *refs):
+    rows = basis.shape[1] // lax.axis_size("blk")
     me = lax.axis_index("blk")
     for s, start, stop in parts:
         mixed = partial[:, start:stop] + half_dot(weights, s, 1 - upper_half(bit), other[:, start:stop])
         coeff = mixed.astype(BF16)
-        for d, ref in enumerate(refs):
-            row = pl.multiple_of((me ^ d) * rows, rows)
-            ref[:, start:stop] = dot(basis[s, pl.ds(row, rows), :], coeff).astype(ref.dtype)
+        for ref, distances in zip(refs, order):
+            for at, d in enumerate(distances):
+                row = pl.multiple_of((me ^ d) * rows, rows)
+                piece = dot(basis[s, pl.ds(row, rows), :], coeff)
+                ref[at * rows : (at + 1) * rows, start:stop] = piece.astype(ref.dtype)
 
 
 def end_kernel(places, counts, *refs):
@@ -286,49 +297,86 @@
     (value,) = step("level2_1", [(2, 1, coeff2[1], near2[1])], [basis_v])
     third(1, value)
 
-    def tail(j, after, arrived=()):
+    def result(j, count, dtype):
+        return in_vmem(count * rows, widths[j], dtype=dtype)
+
+    direct = [[d] for d in range(n_blk)]
+
+    def tail(j, after, order, arrived=(), folding=None):
         (coeff4,) = step(f"level3_{j}", [(3, j, coeff3[j], near3[j])], after)
         near4 = cross(4, coeff4)
-        partial, *totals = call(
-            functools.partial(between_kernel, bits[4], parts[j], [len(group) for _, group in arrived]),
+        extra = [v for _, group in arrived for v in group]
+        outs = [in_vmem(rank, widths[j], dtype=F32)] + [result(at, 1, BF16) for at, _ in arrived]
+        if folding is not None:
+            at, keep, got, count = folding
+            extra += [keep, got]
+            outs += [result(at, count // 2, BF16), result(at, count // 2, F32)]
+        partial, *more = call(
+            functools.partial(
+                between_kernel, bits[4], parts[j], [len(group) for _, group in arrived], folding is not None
+            ),
             f"between_{j}",
-            [VMEM] * (2 + sum(len(group) for _, group in arrived)),
-            [in_vmem(rank, widths[j], dtype=F32)] + [in_vmem(rows, widths[at]) for at, _ in arrived],
+            [VMEM] * (2 + len(extra)),
+            outs,
             [],
-            [here(v) for v in (coeff4, weights[4], *(v for _, group in arrived for v in group))],
+            [here(v) for v in (coeff4, weights[4], *extra)],
         )
         out = call(
-            functools.partial(last_kernel, bits[4], parts[j]),
+            functools.partial(last_kernel, bits[4], parts[j], order),
             f"last_{j}",
             [VMEM] * 4,
-            [in_vmem(rows, widths[j], dtype=F32)] + [in_vmem(rows, widths[j])] * (n_blk - 1),
+            [result(j, len(o), BF16 if at else F32) for at, o in enumerate(order)],
             [],
             [here(v) for v in (partial, near4, weights[4], basis_v)],
             flops=COST if j < len(widths) - 1 else 0,
         )
-        group = [out[0]] + [partner(out[d], "blk", d) for d in range(n_blk - 1, 0, -1)]
-        return group, totals
-
-    group0, _ = tail(0, [coeff3[1]])
-    (value,) = step("level2_2", [(2, 2, coeff2[2], near2[2])], [group0[0]])
+        return out, more
+
+    def direct_sum(out):
+        return [out[0]] + [partner(out[d], "blk", d) for d in range(n_blk - 1, 0, -1)]
+
+    masks = [1 << b for b in range(n_blk.bit_length() - 1)]
+    halves = [0]
+    for mask in masks[::-1]:
+        halves = halves + [d | mask for d in halves]
+
+    def begin_sum(j, out):
+        keep, send = out
+        got, count = partner(send, "blk", masks[0]), n_blk // 2
+        for mask in masks[1:-1]:
+            send, keep = call(
+                fold_kernel,
+                f"fold_{j}_{mask}",
+                [VMEM] * 2,
+                [result(j, count // 2, BF16), result(j, count // 2, F32)],
+                [],
+                [here(keep), here(got)],
+            )
+            got, count = partner(send, "blk", mask), count // 2
+        return j, keep, got, count
+
+    out0, _ = tail(0, [coeff3[1]], direct)
+    group0 = direct_sum(out0)
+    (value,) = step("level2_2", [(2, 2, coeff2[2], near2[2])], [out0[0]])
     third(2, value)
     (total0,) = call(
-        sum_kernel,
-        "sum_0",
-        [VMEM] * n_blk,
-        [in_vmem(rows, widths[0])],
-        [],
-        [here(v) for v in group0],
-        [coeff3[2]],
+        sum_kernel, "sum_0", [VMEM] * n_blk, [result(0, 1, BF16)], [], [here(v) for v in group0], [coeff3[2]]
     )
     (value,) = step("level1_3", [job1(3)], [total0])
     second(3, value)
-    group1, _ = tail(1, [coeff2[3]])
-    (value,) = step("level2_3", [(2, 3, coeff2[3], near2[3])], [group1[0]])
+    out1, _ = tail(1, [coeff2[3]], direct)
+    group1 = direct_sum(out1)
+    (value,) = step("level2_3", [(2, 3, coeff2[3], near2[3])], [out1[0]])
     third(3, value)
-    group2, (total1,) = tail(2, [coeff3[3]], [(1, group1)])
-    group3, _ = tail(3, [group2[0]])
-    groups = [[total0], [total1], group2, group3]
+    out2, (total1,) = tail(
+        2, [coeff3[3]], [halves[: n_blk // 2], halves[n_blk // 2 :]], [(1, group1)]
+    )
+    fold2 = begin_sum(2, out2)
+    out3, (send2, keep2) = tail(3, [out2[0]], direct, (), fold2)
+    got2 = partner(send2, "blk", masks[-1])
+    group3 = direct_sum(out3)
+    (total2,) = call(sum_kernel, "sum_2", [VMEM] * 2, [result(2, 1, BF16)], [], [here(keep2), here(got2)], [out3[0]], 0)
+    groups = [[total0], [total1], [total2], group3]
     flat = [here(v) for group in groups for v in group]
     return pl.pallas_call(
         functools.partial(end_kernel, places, [len(group) for group in groups]),

time: 70.1 us -> 80.1 us (1.14)
  waiting for transfers between devices: 21.6 us -> 34.7 us
  starting transfers between devices: 31.6 us -> 28.9 us
    ppermute x26 -> x25, waiting for transfers between devices: 21.6 us -> 34.7 us  [partner(): return lax.ppermute(value, axis, pairs)]
    ppermute x26 -> x25, starting transfers between devices: 31.6 us -> 28.9 us  [partner(): return lax.ppermute(value, axis, pairs)]
    pallas_call x23 -> x24, Pallas kernels: 15.5 us -> 15.3 us  [call(): pl.pallas_call(body, name=name, in_specs=[*in_specs, *[ANY] * len(after)]...]
  transfers between devices with their start and end apart: 26 -> 25, of which waited for: 14 -> 15; matrix products, arithmetic and copies ran while one was open for 0% -> 0% of each run, Pallas kernels for 17% -> 15%
where the time goes in v14:
time: 80.1 us; the launch traced here: 79.9 us
  waiting for transfers between devices  34.7 us (43%)
  starting transfers between devices  28.9 us (36%)
  Pallas kernels  16.2 us (20%)
    ppermute x25, waiting for transfers between devices, partner(): return lax.ppermute(value, axis, pairs)  34.7 us
    ppermute x25, starting transfers between devices, partner(): return lax.ppermute(value, axis, pairs)  28.9 us
    pallas_call x24, Pallas kernels, call(): pl.pallas_call(body, name=name, in_specs=[*in_specs, *[ANY] * len(after)]...  15.3 us
  transfers between devices with their start and end apart: 25, of which 15 were waited for; matrix products, arithmetic and copies ran while one was open for 0% of the time, Pallas kernels for 15%

profile of v14, /device:TPU:0, one launch (start us, length us, event | category | flops | bytes accessed | tf_op | source)
XLA Modules:
  0.0 79.9 jit_solution(5689708699765639836)
XLA Ops:
  0.0 3.7 %leaf.1 = (bf16[384,128]{1,0:T(8,128)(2,1)S(1)}, bf16[384,896]{1,0:T(8,128)(2,1)S(1)}, bf16[2,384,768]{2,1,0:T(8,128)(2,1)S(1)}, bf16[2,384,768]{2,1,0:T(8,128)(2,1)S(1)}) custom-call(bf16[2,1024,512]{2,1,0:T(8,128)(2,1)} %bitcast.9, bf16[2,384,1024]{2,1,0:T(8,128)(2,1)} %bitcast.10, bf16[5,2,384,768]{3,2,1,0:T(8,128)(2,1)} %bitcast.7, s32[2,5]{1,0:T(2,128)} %bitcast.12), custom_call_target="tpu_custom_call" | custom-call | flops 6000000000 | tf_op jit(solution)/shard_map/leaf/pallas_call | solution.py:41
  3.7 0.5 collective-permute-start.2
  4.3 1.8 %collective-permute-done.refs_1_ = bf16[384,128]{1,0:T(8,128)(2,1)S(1)} collective-permute-done((bf16[384,128]{1,0:T(8,128)(2,1)S(1)}, bf16[384,128]{1,0:T(8,128)(2,1)S(1)}, u32[]{:S(2)}, u32[]{:S(2)}) %collective-permute-start) | collective-permute-done | bytes 98336 | tf_op jit(solution)/shard_map/ppermute | solution.py:55
  6.4 3.0 %collective-permute-start.1 = (bf16[384,128]{1,0:T(8,128)(2,1)S(1)}, bf16[384,128]{1,0:T(8,128)(2,1)S(1)}, u32[]{:S(2)}, u32[]{:S(2)}) collective-permute-start(bf16[384,128]{1,0:T(8,128)(2,1)S(1)} %level1_0.1.refs_3_.refs_0_), channel_id=1, source_target_pairs={{0,2},{1,3},{2,0},{3,1},{4,6},{5,7},{6,4},{7,5},{8,10},{9,11},{10,... | collective-permute-start | bytes 294920 | tf_op jit(solution)/shard_map/ppermute | solution.py:55
  9.5 0.5 level1_1.1.refs_3_.refs_0_
  10.1 2.5 %collective-permute-done.1.refs_1_ = bf16[384,128]{1,0:T(8,128)(2,1)S(1)} collective-permute-done((bf16[384,128]{1,0:T(8,128)(2,1)S(1)}, bf16[384,128]{1,0:T(8,128)(2,1)S(1)}, u32[]{:S(2)}, u32[]{:S(2)}) %collective-permute-start.1) | collective-permute-done | bytes 98336 | tf_op jit(solution)/shard_map/ppermute | solution.py:55
  13.0 3.0 %collective-permute-start.3 = (bf16[384,128]{1,0:T(8,128)(2,1)S(1)}, bf16[384,128]{1,0:T(8,128)(2,1)S(1)}, u32[]{:S(2)}, u32[]{:S(2)}) collective-permute-start(bf16[384,128]{1,0:T(8,128)(2,1)S(1)} %level2_0.1.refs_3_.refs_0_), channel_id=1, source_target_pairs={{0,4},{1,5},{2,6},{3,7},{4,0},{5,1},{6,2},{7,3},{8,12},{9,13},{10,... | collective-permute-start | bytes 294920 | tf_op jit(solution)/shard_map/ppermute | solution.py:55
  15.9 0.4 level1_2.1.refs_3_.refs_0_
  16.3 2.2 %collective-permute-start.9 = (bf16[384,256]{1,0:T(8,128)(2,1)S(1)}, bf16[384,256]{1,0:T(8,128)(2,1)S(1)}, u32[]{:S(2)}, u32[]{:S(2)}) collective-permute-start(bf16[384,256]{1,0:T(8,128)(2,1)S(1)} %level1_2.1.refs_3_.refs_0_), channel_id=1, source_target_pairs={{0,2},{1,3},{2,0},{3,1},{4,6},{5,7},{6,4},{7,5},{8,10},{9,11},{10,... | collective-permute-start | bytes 589832 | tf_op jit(solution)/shard_map/ppermute | solution.py:55
  18.5 2.5 %prefetch.1 = (bf16[2,384,768]{2,1,0:T(8,128)(2,1)S(1)}, bf16[2,384,768]{2,1,0:T(8,128)(2,1)S(1)}, bf16[2,1024,384]{2,1,0:T(8,128)(2,1)S(1)}) custom-call(bf16[5,2,384,768]{3,2,1,0:T(8,128)(2,1)} %bitcast.8, bf16[2,1024,384]{2,1,0:T(8,128)(2,1)} %bitcast.11, s32[2,5]{1,0:T(2,128)} %bitcast.13, bf16[384,256]{1,0:T(8,128)(2,1)S(1)} %level1_2.1.refs_3_.refs_0_), custom_call_target="tpu_custom_call" | custom-call | flops 6000000000 | tf_op jit(solution)/shard_map/prefetch/pallas_call | solution.py:41
  21.0 1.0 %collective-permute-done.4.refs_1_ = bf16[384,384]{1,0:T(8,128)(2,1)S(1)} collective-permute-done((bf16[384,384]{1,0:T(8,128)(2,1)S(1)}, bf16[384,384]{1,0:T(8,128)(2,1)S(1)}, u32[]{:S(2)}, u32[]{:S(2)}) %collective-permute-start.4) | collective-permute-done | bytes 294944 | tf_op jit(solution)/shard_map/ppermute | solution.py:55
  22.0 0.5 level2_1.1.refs_3_.refs_0_
  22.6 1.6 %collective-permute-start.12 = (bf16[384,384]{1,0:T(8,128)(2,1)S(1)}, bf16[384,384]{1,0:T(8,128)(2,1)S(1)}, u32[]{:S(2)}, u32[]{:S(2)}) collective-permute-start(bf16[384,384]{1,0:T(8,128)(2,1)S(1)} %level2_1.1.refs_3_.refs_0_), channel_id=1, source_target_pairs={{0,4},{1,5},{2,6},{3,7},{4,0},{5,1},{6,2},{7,3},{8,12},{9,13},{10,... | collective-permute-start | bytes 884744 | tf_op jit(solution)/shard_map/ppermute | solution.py:55
  24.2 0.3 level3_0.1.refs_0_
  24.9 1.0 %collective-permute-done.5.refs_1_ = bf16[384,128]{1,0:T(8,128)(2,1)S(1)} collective-permute-done((bf16[384,128]{1,0:T(8,128)(2,1)S(1)}, bf16[384,128]{1,0:T(8,128)(2,1)S(1)}, u32[]{:S(2)}, u32[]{:S(2)}) %collective-permute-start.5) | collective-permute-done | bytes 98336 | tf_op jit(solution)/shard_map/ppermute | solution.py:55
  25.9 0.6 last_0.1
  26.5 2.5 %collective-permute-start.6 = (bf16[256,128]{1,0:T(8,128)(2,1)S(1)}, bf16[256,128]{1,0:T(8,128)(2,1)S(1)}, u32[]{:S(2)}, u32[]{:S(2)}) collective-permute-start(bf16[256,128]{1,0:T(8,128)(2,1)S(1)} %get-tuple-element.39), channel_id=1, source_target_pairs={{0,24},{8,16},{16,8},{24,0},{1,25},{9,17},{17,9},{25,1},{2,26},{10... | collective-permute-start | bytes 196616 | tf_op jit(solution)/shard_map/ppermute | solution.py:55
  29.0 0.5 collective-permute-start.7
  29.5 0.5 collective-permute-start.8
  30.1 0.4 level2_2.1.refs_4_.refs_0_
  30.4 1.4 %collective-permute-start.10 = (bf16[384,256]{1,0:T(8,128)(2,1)S(1)}, bf16[384,256]{1,0:T(8,128)(2,1)S(1)}, u32[]{:S(2)}, u32[]{:S(2)}) collective-permute-start(bf16[384,256]{1,0:T(8,128)(2,1)S(1)} %level2_2.1.refs_4_.refs_0_), channel_id=1, source_target_pairs={{0,4},{1,5},{2,6},{3,7},{4,0},{5,1},{6,2},{7,3},{8,12},{9,13},{10,... | collective-permute-start | bytes 589832 | tf_op jit(solution)/shard_map/ppermute | solution.py:55
  31.8 1.5 %collective-permute-done.7.refs_2_ = bf16[256,128]{1,0:T(8,128)(2,1)S(1)} collective-permute-done((bf16[256,128]{1,0:T(8,128)(2,1)S(1)}, bf16[256,128]{1,0:T(8,128)(2,1)S(1)}, u32[]{:S(2)}, u32[]{:S(2)}) %collective-permute-start.7) | collective-permute-done | bytes 65568 | tf_op jit(solution)/shard_map/ppermute | solution.py:55
  33.3 0.5 collective-permute-done.8.refs_3_
  33.8 0.4 level1_3.1.refs_3_.refs_0_
  34.2 2.5 %collective-permute-start.11 = (bf16[384,256]{1,0:T(8,128)(2,1)S(1)}, bf16[384,256]{1,0:T(8,128)(2,1)S(1)}, u32[]{:S(2)}, u32[]{:S(2)}) collective-permute-start(bf16[384,256]{1,0:T(8,128)(2,1)S(1)} %level1_3.1.refs_3_.refs_0_), channel_id=1, source_target_pairs={{0,2},{1,3},{2,0},{3,1},{4,6},{5,7},{6,4},{7,5},{8,10},{9,11},{10,... | collective-permute-start | bytes 589832 | tf_op jit(solution)/shard_map/ppermute | solution.py:55
  36.7 6.5 %collective-permute-done.12.refs_1_ = bf16[384,384]{1,0:T(8,128)(2,1)S(1)} collective-permute-done((bf16[384,384]{1,0:T(8,128)(2,1)S(1)}, bf16[384,384]{1,0:T(8,128)(2,1)S(1)}, u32[]{:S(2)}, u32[]{:S(2)}) %collective-permute-start.12) | collective-permute-done | bytes 294944 | tf_op jit(solution)/shard_map/ppermute | solution.py:55
  43.2 0.5 level3_1.1.refs_0_
  44.1 1.2 %collective-permute-done.13.refs_1_ = bf16[384,384]{1,0:T(8,128)(2,1)S(1)} collective-permute-done((bf16[384,384]{1,0:T(8,128)(2,1)S(1)}, bf16[384,384]{1,0:T(8,128)(2,1)S(1)}, u32[]{:S(2)}, u32[]{:S(2)}) %collective-permute-start.13) | collective-permute-done | bytes 294944 | tf_op jit(solution)/shard_map/ppermute | solution.py:55
  45.4 1.0 %last_1.1 = (f32[256,384]{1,0:T(8,128)S(1)}, bf16[256,384]{1,0:T(8,128)(2,1)S(1)}, bf16[256,384]{1,0:T(8,128)(2,1)S(1)}, bf16[256,384]{1,0:T(8,128)(2,1)S(1)}) custom-call(f32[384,384]{1,0:T(8,128)S(1)} %between_1.1.refs_0_, bf16[384,384]{1,0:T(8,128)(2,1)S(1)} %collective-permute-done.13.refs_1_, ...), custom_call_target="tpu_custom_call" | custom-call | flops 6000000000 | tf_op jit(solution)/shard_map/last_1/pallas_call | solution.py:41
  46.3 2.8 %collective-permute-start.14 = (bf16[256,384]{1,0:T(8,128)(2,1)S(1)}, bf16[256,384]{1,0:T(8,128)(2,1)S(1)}, u32[]{:S(2)}, u32[]{:S(2)}) collective-permute-start(bf16[256,384]{1,0:T(8,128)(2,1)S(1)} %get-tuple-element.43), channel_id=1, source_target_pairs={{0,24},{8,16},{16,8},{24,0},{1,25},{9,17},{17,9},{25,1},{2,26},{10... | collective-permute-start | bytes 589832 | tf_op jit(solution)/shard_map/ppermute | solution.py:55
  49.2 0.5 collective-permute-start.15
  49.9 0.4 level2_3.1.refs_3_.refs_0_
  50.3 0.4 level3_2.1.refs_0_
  50.8 4.3 %collective-permute-done.14.refs_3_ = bf16[256,384]{1,0:T(8,128)(2,1)S(1)} collective-permute-done((bf16[256,384]{1,0:T(8,128)(2,1)S(1)}, bf16[256,384]{1,0:T(8,128)(2,1)S(1)}, u32[]{:S(2)}, u32[]{:S(2)}) %collective-permute-start.14) | collective-permute-done | bytes 196640 | tf_op jit(solution)/shard_map/ppermute | solution.py:55
  55.1 3.5 %collective-permute-done.15.refs_4_ = bf16[256,384]{1,0:T(8,128)(2,1)S(1)} collective-permute-done((bf16[256,384]{1,0:T(8,128)(2,1)S(1)}, bf16[256,384]{1,0:T(8,128)(2,1)S(1)}, u32[]{:S(2)}, u32[]{:S(2)}) %collective-permute-start.15) | collective-permute-done | bytes 196640 | tf_op jit(solution)/shard_map/ppermute | solution.py:55
  58.9 0.3 between_2.1
  59.2 0.8 %last_2.1 = (f32[512,256]{1,0:T(8,128)S(1)}, bf16[512,256]{1,0:T(8,128)(2,1)S(1)}) custom-call(f32[384,256]{1,0:T(8,128)S(1)} %get-tuple-element.47.refs_0_, bf16[384,256]{1,0:T(8,128)(2,1)S(1)} %collective-permute-done.18.refs_1_, bf16[2,384,768]{2,1,0:T(8,128)(2,1)S(1)} %get-tuple-element.37.refs_1_.refs_2_, ...), custom_call_target="tpu_custom_call" | custom-call | flops 6000000000 | tf_op jit(solution)/shard_map/last_2/pallas_call | solution.py:41
  60.1 1.5 %collective-permute-start.19 = (bf16[512,256]{1,0:T(8,128)(2,1)S(1)}, bf16[512,256]{1,0:T(8,128)(2,1)S(1)}, u32[]{:S(2)}, u32[]{:S(2)}) collective-permute-start(bf16[512,256]{1,0:T(8,128)(2,1)S(1)} %get-tuple-element.49), channel_id=1, source_target_pairs={{0,8},{8,0},{16,24},{24,16},{1,9},{9,1},{17,25},{25,17},{2,10},{10... | collective-permute-start | bytes 786440 | tf_op jit(solution)/shard_map/ppermute | solution.py:55
  61.6 0.4 level3_3.1.refs_0_
  62.1 6.0 %collective-permute-done.19.refs_3_ = bf16[512,256]{1,0:T(8,128)(2,1)S(1)} collective-permute-done((bf16[512,256]{1,0:T(8,128)(2,1)S(1)}, bf16[512,256]{1,0:T(8,128)(2,1)S(1)}, u32[]{:S(2)}, u32[]{:S(2)}) %collective-permute-start.19) | collective-permute-done | bytes 262176 | tf_op jit(solution)/shard_map/ppermute | solution.py:55
  68.3 1.8 %collective-permute-start.20 = (bf16[256,256]{1,0:T(8,128)(2,1)S(1)}, bf16[256,256]{1,0:T(8,128)(2,1)S(1)}, u32[]{:S(2)}, u32[]{:S(2)}) collective-permute-start(bf16[256,256]{1,0:T(8,128)(2,1)S(1)} %get-tuple-element.51), channel_id=1, source_target_pairs={{0,16},{8,24},{16,0},{24,8},{1,17},{9,25},{17,1},{25,9},{2,18},{10... | collective-permute-start | bytes 393224 | tf_op jit(solution)/shard_map/ppermute | solution.py:55
  70.1 0.8 %last_3.1 = (f32[256,256]{1,0:T(8,128)S(1)}, bf16[256,256]{1,0:T(8,128)(2,1)S(1)}, bf16[256,256]{1,0:T(8,128)(2,1)S(1)}, bf16[256,256]{1,0:T(8,128)(2,1)S(1)}) custom-call(f32[384,256]{1,0:T(8,128)S(1)} %get-tuple-element.52.refs_0_, bf16[384,256]{1,0:T(8,128)(2,1)S(1)} %collective-permute-done.21.refs_1_, ...), custom_call_target="tpu_custom_call" | custom-call | tf_op jit(solution)/shard_map/last_3/pallas_call | solution.py:41
  71.0 1.5 %collective-permute-start.22 = (bf16[256,256]{1,0:T(8,128)(2,1)S(1)}, bf16[256,256]{1,0:T(8,128)(2,1)S(1)}, u32[]{:S(2)}, u32[]{:S(2)}) collective-permute-start(bf16[256,256]{1,0:T(8,128)(2,1)S(1)} %get-tuple-element.54), channel_id=1, source_target_pairs={{0,24},{8,16},{16,8},{24,0},{1,25},{9,17},{17,9},{25,1},{2,26},{10... | collective-permute-start | bytes 393224 | tf_op jit(solution)/shard_map/ppermute | solution.py:55
  72.8 1.7 %collective-permute-start.24 = (bf16[256,256]{1,0:T(8,128)(2,1)S(1)}, bf16[256,256]{1,0:T(8,128)(2,1)S(1)}, u32[]{:S(2)}, u32[]{:S(2)}) collective-permute-start(bf16[256,256]{1,0:T(8,128)(2,1)S(1)} %get-tuple-element.56), channel_id=1, source_target_pairs={{0,8},{8,0},{16,24},{24,16},{1,9},{9,1},{17,25},{25,17},{2,10},{10... | collective-permute-start | bytes 393224 | tf_op jit(solution)/shard_map/ppermute | solution.py:55
  74.5 2.2 %collective-permute-done.20.refs_1_ = bf16[256,256]{1,0:T(8,128)(2,1)S(1)} collective-permute-done((bf16[256,256]{1,0:T(8,128)(2,1)S(1)}, bf16[256,256]{1,0:T(8,128)(2,1)S(1)}, u32[]{:S(2)}, u32[]{:S(2)}) %collective-permute-start.20) | collective-permute-done | bytes 131104 | tf_op jit(solution)/shard_map/ppermute | solution.py:55
  76.7 1.0 %collective-permute-done.22.refs_4_ = bf16[256,256]{1,0:T(8,128)(2,1)S(1)} collective-permute-done((bf16[256,256]{1,0:T(8,128)(2,1)S(1)}, bf16[256,256]{1,0:T(8,128)(2,1)S(1)}, u32[]{:S(2)}, u32[]{:S(2)}) %collective-permute-start.22) | collective-permute-done | bytes 131104 | tf_op jit(solution)/shard_map/ppermute | solution.py:55
  77.7 1.3 %collective-permute-done.23.refs_5_ = bf16[256,256]{1,0:T(8,128)(2,1)S(1)} collective-permute-done((bf16[256,256]{1,0:T(8,128)(2,1)S(1)}, bf16[256,256]{1,0:T(8,128)(2,1)S(1)}, u32[]{:S(2)}, u32[]{:S(2)}) %collective-permute-start.23) | collective-permute-done | bytes 131104 | tf_op jit(solution)/shard_map/ppermute | solution.py:55
  79.0 0.9 %end.1 = bf16[2,256,512]{2,1,0:T(8,128)(2,1)} custom-call(bf16[256,128]{1,0:T(8,128)(2,1)S(1)} %sum_0.1.refs_3_.refs_0_, bf16[256,384]{1,0:T(8,128)(2,1)S(1)} %get-tuple-element.46.refs_1_, bf16[256,256]{1,0:T(8,128)(2,1)S(1)} %sum_2.1.refs_2_, f32[256,256]{1,0:T(8,128)S(1)} %get-tuple-element.53.refs_2_.refs_3_, ...), custom_call_target="tpu_custom_call" | custom-call | tf_op jit(solution)/shard_map/end/pallas_call | solution.py:381
  (27 shorter events, 2.9 us)
Async XLA Ops:
  3.7 5.8 %collective-permute-start.2 = (bf16[384,896]{1,0:T(8,128)(2,1)S(1)}, bf16[384,896]{1,0:T(8,128)(2,1)S(1)}, u32[]{:S(2)}, u32[]{:S(2)}) collective-permute-start(bf16[384,896]{1,0:T(8,128)(2,1)S(1)} %get-tuple-element.34.refs_0_), channel_id=1, source_target_pairs={{0,1},{1,0},{2,3},{3,2},{4,5},{5,4},{6,7},{7,6},{8,9},{9,8},{10,11... | collective-permute-start | bytes 2064392 | tf_op jit(solution)/shard_map/ppermute | solution.py:55
  4.2 1.9 %collective-permute-start = (bf16[384,128]{1,0:T(8,128)(2,1)S(1)}, bf16[384,128]{1,0:T(8,128)(2,1)S(1)}, u32[]{:S(2)}, u32[]{:S(2)}) collective-permute-start(bf16[384,128]{1,0:T(8,128)(2,1)S(1)} %get-tuple-element.31.refs_0_), channel_id=1, source_target_pairs={{0,1},{1,0},{2,3},{3,2},{4,5},{5,4},{6,7},{7,6},{8,9},{9,8},{10,11... | collective-permute-start | bytes 294920 | tf_op jit(solution)/shard_map/ppermute | solution.py:55
  6.4 6.2 %collective-permute-start.1 = (bf16[384,128]{1,0:T(8,128)(2,1)S(1)}, bf16[384,128]{1,0:T(8,128)(2,1)S(1)}, u32[]{:S(2)}, u32[]{:S(2)}) collective-permute-start(bf16[384,128]{1,0:T(8,128)(2,1)S(1)} %level1_0.1.refs_3_.refs_0_), channel_id=1, source_target_pairs={{0,2},{1,3},{2,0},{3,1},{4,6},{5,7},{6,4},{7,5},{8,10},{9,11},{10,... | collective-permute-start | bytes 294920 | tf_op jit(solution)/shard_map/ppermute | solution.py:55
  10.0 12.1 %collective-permute-start.4 = (bf16[384,384]{1,0:T(8,128)(2,1)S(1)}, bf16[384,384]{1,0:T(8,128)(2,1)S(1)}, u32[]{:S(2)}, u32[]{:S(2)}) collective-permute-start(bf16[384,384]{1,0:T(8,128)(2,1)S(1)} %level1_1.1.refs_3_.refs_0_), channel_id=1, source_target_pairs={{0,2},{1,3},{2,0},{3,1},{4,6},{5,7},{6,4},{7,5},{8,10},{9,11},{10,... | collective-permute-start | bytes 884744 | tf_op jit(solution)/shard_map/ppermute | solution.py:55
  13.0 11.3 %collective-permute-start.3 = (bf16[384,128]{1,0:T(8,128)(2,1)S(1)}, bf16[384,128]{1,0:T(8,128)(2,1)S(1)}, u32[]{:S(2)}, u32[]{:S(2)}) collective-permute-start(bf16[384,128]{1,0:T(8,128)(2,1)S(1)} %level2_0.1.refs_3_.refs_0_), channel_id=1, source_target_pairs={{0,4},{1,5},{2,6},{3,7},{4,0},{5,1},{6,2},{7,3},{8,12},{9,13},{10,... | collective-permute-start | bytes 294920 | tf_op jit(solution)/shard_map/ppermute | solution.py:55
  16.3 13.8 %collective-permute-start.9 = (bf16[384,256]{1,0:T(8,128)(2,1)S(1)}, bf16[384,256]{1,0:T(8,128)(2,1)S(1)}, u32[]{:S(2)}, u32[]{:S(2)}) collective-permute-start(bf16[384,256]{1,0:T(8,128)(2,1)S(1)} %level1_2.1.refs_3_.refs_0_), channel_id=1, source_target_pairs={{0,2},{1,3},{2,0},{3,1},{4,6},{5,7},{6,4},{7,5},{8,10},{9,11},{10,... | collective-permute-start | bytes 589832 | tf_op jit(solution)/shard_map/ppermute | solution.py:55
  22.6 20.6 %collective-permute-start.12 = (bf16[384,384]{1,0:T(8,128)(2,1)S(1)}, bf16[384,384]{1,0:T(8,128)(2,1)S(1)}, u32[]{:S(2)}, u32[]{:S(2)}) collective-permute-start(bf16[384,384]{1,0:T(8,128)(2,1)S(1)} %level2_1.1.refs_3_.refs_0_), channel_id=1, source_target_pairs={{0,4},{1,5},{2,6},{3,7},{4,0},{5,1},{6,2},{7,3},{8,12},{9,13},{10,... | collective-permute-start | bytes 884744 | tf_op jit(solution)/shard_map/ppermute | solution.py:55
  24.6 1.4 %collective-permute-start.5 = (bf16[384,128]{1,0:T(8,128)(2,1)S(1)}, bf16[384,128]{1,0:T(8,128)(2,1)S(1)}, u32[]{:S(2)}, u32[]{:S(2)}) collective-permute-start(bf16[384,128]{1,0:T(8,128)(2,1)S(1)} %level3_0.1.refs_0_), channel_id=1, source_target_pairs={{0,1},{1,0},{2,3},{3,2},{4,5},{5,4},{6,7},{7,6},{8,9},{9,8},{10,11... | collective-permute-start | bytes 294920 | tf_op jit(solution)/shard_map/ppermute | solution.py:55
  26.5 5.3 %collective-permute-start.6 = (bf16[256,128]{1,0:T(8,128)(2,1)S(1)}, bf16[256,128]{1,0:T(8,128)(2,1)S(1)}, u32[]{:S(2)}, u32[]{:S(2)}) collective-permute-start(bf16[256,128]{1,0:T(8,128)(2,1)S(1)} %get-tuple-element.39), channel_id=1, source_target_pairs={{0,24},{8,16},{16,8},{24,0},{1,25},{9,17},{17,9},{25,1},{2,26},{10... | collective-permute-start | bytes 196616 | tf_op jit(solution)/shard_map/ppermute | solution.py:55
  29.0 4.3 %collective-permute-start.7 = (bf16[256,128]{1,0:T(8,128)(2,1)S(1)}, bf16[256,128]{1,0:T(8,128)(2,1)S(1)}, u32[]{:S(2)}, u32[]{:S(2)}) collective-permute-start(bf16[256,128]{1,0:T(8,128)(2,1)S(1)} %get-tuple-element.40), channel_id=1, source_target_pairs={{0,16},{8,24},{16,0},{24,8},{1,17},{9,25},{17,1},{25,9},{2,18},{10... | collective-permute-start | bytes 196616 | tf_op jit(solution)/shard_map/ppermute | solution.py:55
  29.5 4.3 %collective-permute-start.8 = (bf16[256,128]{1,0:T(8,128)(2,1)S(1)}, bf16[256,128]{1,0:T(8,128)(2,1)S(1)}, u32[]{:S(2)}, u32[]{:S(2)}) collective-permute-start(bf16[256,128]{1,0:T(8,128)(2,1)S(1)} %get-tuple-element.41), channel_id=1, source_target_pairs={{0,8},{8,0},{16,24},{24,16},{1,9},{9,1},{17,25},{25,17},{2,10},{10... | collective-permute-start | bytes 196616 | tf_op jit(solution)/shard_map/ppermute | solution.py:55
  30.4 19.9 %collective-permute-start.10 = (bf16[384,256]{1,0:T(8,128)(2,1)S(1)}, bf16[384,256]{1,0:T(8,128)(2,1)S(1)}, u32[]{:S(2)}, u32[]{:S(2)}) collective-permute-start(bf16[384,256]{1,0:T(8,128)(2,1)S(1)} %level2_2.1.refs_4_.refs_0_), channel_id=1, source_target_pairs={{0,4},{1,5},{2,6},{3,7},{4,0},{5,1},{6,2},{7,3},{8,12},{9,13},{10,... | collective-permute-start | bytes 589832 | tf_op jit(solution)/shard_map/ppermute | solution.py:55
  34.2 15.7 %collective-permute-start.11 = (bf16[384,256]{1,0:T(8,128)(2,1)S(1)}, bf16[384,256]{1,0:T(8,128)(2,1)S(1)}, u32[]{:S(2)}, u32[]{:S(2)}) collective-permute-start(bf16[384,256]{1,0:T(8,128)(2,1)S(1)} %level1_3.1.refs_3_.refs_0_), channel_id=1, source_target_pairs={{0,2},{1,3},{2,0},{3,1},{4,6},{5,7},{6,4},{7,5},{8,10},{9,11},{10,... | collective-permute-start | bytes 589832 | tf_op jit(solution)/shard_map/ppermute | solution.py:55
  43.7 1.6 %collective-permute-start.13 = (bf16[384,384]{1,0:T(8,128)(2,1)S(1)}, bf16[384,384]{1,0:T(8,128)(2,1)S(1)}, u32[]{:S(2)}, u32[]{:S(2)}) collective-permute-start(bf16[384,384]{1,0:T(8,128)(2,1)S(1)} %level3_1.1.refs_0_), channel_id=1, source_target_pairs={{0,1},{1,0},{2,3},{3,2},{4,5},{5,4},{6,7},{7,6},{8,9},{9,8},{10,11... | collective-permute-start | bytes 884744 | tf_op jit(solution)/shard_map/ppermute | solution.py:55
  46.3 8.7 %collective-permute-start.14 = (bf16[256,384]{1,0:T(8,128)(2,1)S(1)}, bf16[256,384]{1,0:T(8,128)(2,1)S(1)}, u32[]{:S(2)}, u32[]{:S(2)}) collective-permute-start(bf16[256,384]{1,0:T(8,128)(2,1)S(1)} %get-tuple-element.43), channel_id=1, source_target_pairs={{0,24},{8,16},{16,8},{24,0},{1,25},{9,17},{17,9},{25,1},{2,26},{10... | collective-permute-start | bytes 589832 | tf_op jit(solution)/shard_map/ppermute | solution.py:55
  49.2 9.4 %collective-permute-start.15 = (bf16[256,384]{1,0:T(8,128)(2,1)S(1)}, bf16[256,384]{1,0:T(8,128)(2,1)S(1)}, u32[]{:S(2)}, u32[]{:S(2)}) collective-permute-start(bf16[256,384]{1,0:T(8,128)(2,1)S(1)} %get-tuple-element.44), channel_id=1, source_target_pairs={{0,16},{8,24},{16,0},{24,8},{1,17},{9,25},{17,1},{25,9},{2,18},{10... | collective-permute-start | bytes 589832 | tf_op jit(solution)/shard_map/ppermute | solution.py:55
  49.7 9.2 %collective-permute-start.16 = (bf16[256,384]{1,0:T(8,128)(2,1)S(1)}, bf16[256,384]{1,0:T(8,128)(2,1)S(1)}, u32[]{:S(2)}, u32[]{:S(2)}) collective-permute-start(bf16[256,384]{1,0:T(8,128)(2,1)S(1)} %get-tuple-element.45), channel_id=1, source_target_pairs={{0,8},{8,0},{16,24},{24,16},{1,9},{9,1},{17,25},{25,17},{2,10},{10... | collective-permute-start | bytes 589832 | tf_op jit(solution)/shard_map/ppermute | solution.py:55
  50.3 11.4 %collective-permute-start.17 = (bf16[384,256]{1,0:T(8,128)(2,1)S(1)}, bf16[384,256]{1,0:T(8,128)(2,1)S(1)}, u32[]{:S(2)}, u32[]{:S(2)}) collective-permute-start(bf16[384,256]{1,0:T(8,128)(2,1)S(1)} %level2_3.1.refs_3_.refs_0_), channel_id=1, source_target_pairs={{0,4},{1,5},{2,6},{3,7},{4,0},{5,1},{6,2},{7,3},{8,12},{9,13},{10,... | collective-permute-start | bytes 589832 | tf_op jit(solution)/shard_map/ppermute | solution.py:55
  50.7 8.5 %collective-permute-start.18 = (bf16[384,256]{1,0:T(8,128)(2,1)S(1)}, bf16[384,256]{1,0:T(8,128)(2,1)S(1)}, u32[]{:S(2)}, u32[]{:S(2)}) collective-permute-start(bf16[384,256]{1,0:T(8,128)(2,1)S(1)} %level3_2.1.refs_0_), channel_id=1, source_target_pairs={{0,1},{1,0},{2,3},{3,2},{4,5},{5,4},{6,7},{7,6},{8,9},{9,8},{10,11... | collective-permute-start | bytes 589832 | tf_op jit(solution)/shard_map/ppermute | solution.py:55
  60.1 8.0 %collective-permute-start.19 = (bf16[512,256]{1,0:T(8,128)(2,1)S(1)}, bf16[512,256]{1,0:T(8,128)(2,1)S(1)}, u32[]{:S(2)}, u32[]{:S(2)}) collective-permute-start(bf16[512,256]{1,0:T(8,128)(2,1)S(1)} %get-tuple-element.49), channel_id=1, source_target_pairs={{0,8},{8,0},{16,24},{24,16},{1,9},{9,1},{17,25},{25,17},{2,10},{10... | collective-permute-start | bytes 786440 | tf_op jit(solution)/shard_map/ppermute | solution.py:55
  62.0 8.2 %collective-permute-start.21 = (bf16[384,256]{1,0:T(8,128)(2,1)S(1)}, bf16[384,256]{1,0:T(8,128)(2,1)S(1)}, u32[]{:S(2)}, u32[]{:S(2)}) collective-permute-start(bf16[384,256]{1,0:T(8,128)(2,1)S(1)} %level3_3.1.refs_0_), channel_id=1, source_target_pairs={{0,1},{1,0},{2,3},{3,2},{4,5},{5,4},{6,7},{7,6},{8,9},{9,8},{10,11... | collective-permute-start | bytes 589832 | tf_op jit(solution)/shard_map/ppermute | solution.py:55
  68.3 8.4 %collective-permute-start.20 = (bf16[256,256]{1,0:T(8,128)(2,1)S(1)}, bf16[256,256]{1,0:T(8,128)(2,1)S(1)}, u32[]{:S(2)}, u32[]{:S(2)}) collective-permute-start(bf16[256,256]{1,0:T(8,128)(2,1)S(1)} %get-tuple-element.51), channel_id=1, source_target_pairs={{0,16},{8,24},{16,0},{24,8},{1,17},{9,25},{17,1},{25,9},{2,18},{10... | collective-permute-start | bytes 393224 | tf_op jit(solution)/shard_map/ppermute | solution.py:55
  71.0 6.8 %collective-permute-start.22 = (bf16[256,256]{1,0:T(8,128)(2,1)S(1)}, bf16[256,256]{1,0:T(8,128)(2,1)S(1)}, u32[]{:S(2)}, u32[]{:S(2)}) collective-permute-start(bf16[256,256]{1,0:T(8,128)(2,1)S(1)} %get-tuple-element.54), channel_id=1, source_target_pairs={{0,24},{8,16},{16,8},{24,0},{1,25},{9,17},{17,9},{25,1},{2,26},{10... | collective-permute-start | bytes 393224 | tf_op jit(solution)/shard_map/ppermute | solution.py:55
  72.5 6.6 %collective-permute-start.23 = (bf16[256,256]{1,0:T(8,128)(2,1)S(1)}, bf16[256,256]{1,0:T(8,128)(2,1)S(1)}, u32[]{:S(2)}, u32[]{:S(2)}) collective-permute-start(bf16[256,256]{1,0:T(8,128)(2,1)S(1)} %get-tuple-element.55), channel_id=1, source_target_pairs={{0,16},{8,24},{16,0},{24,8},{1,17},{9,25},{17,1},{25,9},{2,18},{10... | collective-permute-start | bytes 393224 | tf_op jit(solution)/shard_map/ppermute | solution.py:55
  72.8 6.3 %collective-permute-start.24 = (bf16[256,256]{1,0:T(8,128)(2,1)S(1)}, bf16[256,256]{1,0:T(8,128)(2,1)S(1)}, u32[]{:S(2)}, u32[]{:S(2)}) collective-permute-start(bf16[256,256]{1,0:T(8,128)(2,1)S(1)} %get-tuple-element.56), channel_id=1, source_target_pairs={{0,8},{8,0},{16,24},{24,16},{1,9},{9,1},{17,25},{25,17},{2,10},{10... | collective-permute-start | bytes 393224 | tf_op jit(solution)/shard_map/ppermute | solution.py:55

commit v15 on v13

--- a/solution.py
+++ b/solution.py
@@ -9,6 +9,7 @@
 
 SHARES = (1, 2, 3, 2)
 PRELOADED = 2
+DEPTHS = 2
 COST = 6 * 10**9
 BF16 = jnp.bfloat16
 F32 = jnp.float32
@@ -32,22 +33,24 @@
     return pltpu.with_memory_space_constraint(value, pltpu.HBM)
 
 
-def call(kernel, name, in_specs, out_shape, scratch, args, after=(), flops=COST, limit=8 * 2**20):
-    count = len(in_specs)
+def call(kernel, name, in_specs, out_shape, scratch, args, after=(), flops=COST, limit=8 * 2**20, through=()):
+    count, outs = len(in_specs), len(out_shape)
 
     def body(*refs):
-        kernel(*refs[:count], *refs[count + len(after) :])
+        held = refs[count + len(after) + len(through) :]
+        kernel(*refs[:count], *held[:outs], *held[outs + len(through) :])
 
     return pl.pallas_call(
         body,
         name=name,
-        in_specs=[*in_specs, *[ANY] * len(after)],
-        out_specs=[VMEM] * len(out_shape),
-        out_shape=out_shape,
+        in_specs=[*in_specs, *[ANY] * (len(after) + len(through))],
+        out_specs=[VMEM] * outs + [ANY] * len(through),
+        out_shape=[*out_shape, *[in_vmem(*v.shape, dtype=v.dtype) for v in through]],
         scratch_shapes=scratch,
+        input_output_aliases={count + len(after) + at: outs + at for at in range(len(through))},
         compiler_params=pltpu.CompilerParams(vmem_limit_bytes=limit),
         cost_estimate=pl.CostEstimate(flops=flops, bytes_accessed=0, transcendentals=0),
-    )(*args, *after)
+    )(*args, *after, *[here(v) for v in through])
 
 
 def partner(value, axis, mask):
@@ -61,32 +64,41 @@
     excite_v, leaves_v, blocks_v, index_s, coeff, sems = refs[count:]
     slots, rank = leaves.shape[0], leaves.shape[1]
     columns, width = excite.shape[2], first.shape[1]
+    base = 1 + 2 * (1 + count)
     listing = pltpu.make_async_copy(index, index_s, sems.at[0])
     listing.start()
     loads = []
+    depth = leaves.shape[2] // DEPTHS
+    spans = [pl.ds(k * depth, depth) for k in range(DEPTHS)]
     for s in range(slots):
-        a = pltpu.make_async_copy(leaves.at[s], leaves_v.at[s], sems.at[1 + s])
-        b = pltpu.make_async_copy(excite.at[s], excite_v.at[s], sems.at[3 + s])
-        a.start()
-        b.start()
-        loads.append((a, b))
+        for k, span in enumerate(spans):
+            at = base + 2 * (s * DEPTHS + k)
+            a = pltpu.make_async_copy(leaves.at[s, :, span], leaves_v.at[s, :, span], sems.at[at])
+            b = pltpu.make_async_copy(excite.at[s, span], excite_v.at[s, span], sems.at[at + 1])
+            a.start()
+            b.start()
+            loads.append((a, b))
     listing.wait()
     weights, later = [], []
     for s in range(slots):
-        c = pltpu.make_async_copy(blocks.at[0, index_s[s, 0]], blocks_v.at[s], sems.at[5 + s])
+        c = pltpu.make_async_copy(blocks.at[0, index_s[s, 0]], blocks_v.at[s], sems.at[1 + s])
         c.start()
         weights.append(c)
     for level in range(1, 1 + count):
         for s in range(slots):
             c = pltpu.make_async_copy(
-                blocks.at[level, index_s[s, level]], nexts[level - 1].at[s], sems.at[5 + 2 * level + s]
+                blocks.at[level, index_s[s, level]], nexts[level - 1].at[s], sems.at[1 + 2 * level + s]
             )
             c.start()
             later.append(c)
     for s in range(slots):
-        for load in loads[s]:
-            load.wait()
-        coeff[s * rank : (s + 1) * rank, :] = dot(leaves_v[s], excite_v[s]).astype(BF16)
+        total = None
+        for k, span in enumerate(spans):
+            for load in loads[s * DEPTHS + k]:
+                load.wait()
+            part = dot(leaves_v[s, :, span], excite_v[s, span])
+            total = part if total is None else total + part
+        coeff[s * rank : (s + 1) * rank, :] = total.astype(BF16)
     for s in range(slots):
         weights[s].wait()
         out = dot(blocks_v[s], coeff[...]).astype(BF16)
@@ -222,7 +234,7 @@
             pair,
             pltpu.SMEM(index.shape, jnp.int32),
             in_vmem(2 * rank, columns),
-            pltpu.SemaphoreType.DMA((7 + 2 * PRELOADED,)),
+            pltpu.SemaphoreType.DMA((1 + 2 * (1 + PRELOADED) + 2 * slots * DEPTHS,)),
         ],
         [in_hbm(excite), in_hbm(leaves), in_hbm(blocks), in_hbm(index)],
         limit=24 * 2**20,
@@ -232,9 +244,9 @@
     def cross(level, value):
         return partner(value, "box", 2 ** bits[level])
 
-    near_first, near_rest = cross(1, first), cross(1, rest)
-
-    def step(name, jobs, after=(), flops=COST):
+    near_first = cross(1, first)
+
+    def step(name, jobs, after=(), flops=COST, through=()):
         args = [here(v) for level, j, own, other in jobs for v in (own, other, weights[level])]
         described, sizes = [], []
         for level, j, _, _ in jobs:
@@ -250,6 +262,7 @@
             args,
             after,
             flops,
+            through=through,
         )
 
     def job1(j):
@@ -265,14 +278,11 @@
         coeff3[j] = value
         near3[j] = cross(3, value)
 
-    (value,) = step("level1_0", [job1(0)])
+    value, rest = step("level1_0", [job1(0)], through=[rest])
+    near_rest = cross(1, rest)
     second(0, value)
     (value,) = step("level1_1", [job1(1)], [coeff2[0]])
     second(1, value)
-    (value,) = step("level2_0", [(2, 0, coeff2[0], near2[0])], [coeff2[1]])
-    third(0, value)
-    (value,) = step("level1_2", [job1(2)], [coeff3[0]])
-    second(2, value)
     *more, basis_v = call(
         prefetch_kernel,
         "prefetch",
@@ -280,10 +290,14 @@
         [pair] * (levels - 1 - PRELOADED) + [in_vmem(*basis.shape)],
         [pltpu.SMEM(index.shape, jnp.int32), pltpu.SemaphoreType.DMA((2 * levels,))],
         [in_hbm(blocks), in_hbm(basis), in_hbm(index)],
-        [coeff2[2]],
+        [coeff2[1]],
     )
     weights += more
-    (value,) = step("level2_1", [(2, 1, coeff2[1], near2[1])], [basis_v])
+    (value,) = step("level2_0", [(2, 0, coeff2[0], near2[0])], [basis_v])
+    third(0, value)
+    (value,) = step("level1_2", [job1(2)], [coeff3[0]])
+    second(2, value)
+    (value,) = step("level2_1", [(2, 1, coeff2[1], near2[1])], [coeff2[2]])
     third(1, value)
 
     def tail(j, after, arrived=()):

time: 70.1 us -> 73.3 us (1.046)
  waiting for transfers between devices: 21.6 us -> 24.6 us
    ppermute x26, waiting for transfers between devices: 21.6 us -> 24.6 us  [partner(): return lax.ppermute(value, axis, pairs)]
  transfers between devices with their start and end apart: 26 -> 26, of which waited for: 14 -> 14; matrix products, arithmetic and copies ran while one was open for 0% -> 0% of each run, Pallas kernels for 17% -> 16%
where the time goes in v15:
time: 73.3 us; the launch traced here: 73.1 us
  starting transfers between devices  31.7 us (43%)
  waiting for transfers between devices  24.6 us (34%)
  Pallas kernels  16.5 us (23%)
    ppermute x26, starting transfers between devices, partner(): return lax.ppermute(value, axis, pairs)  31.7 us
    ppermute x26, waiting for transfers between devices, partner(): return lax.ppermute(value, axis, pairs)  24.6 us
    pallas_call x23, Pallas kernels, call(): pl.pallas_call(body, name=name, in_specs=[*in_specs, *[ANY] * (len(after)...  15.5 us
  transfers between devices with their start and end apart: 26, of which 14 were waited for; matrix products, arithmetic and copies ran while one was open for 0% of the time, Pallas kernels for 16%

profile of v15, /device:TPU:0, one launch (start us, length us, event | category | flops | bytes accessed | tf_op | source)
XLA Modules:
  0.0 73.1 jit_solution(29593597484889925)
XLA Ops:
  0.0 3.7 %leaf.1 = (bf16[384,128]{1,0:T(8,128)(2,1)S(1)}, bf16[384,896]{1,0:T(8,128)(2,1)S(1)}, bf16[2,384,768]{2,1,0:T(8,128)(2,1)S(1)}, bf16[2,384,768]{2,1,0:T(8,128)(2,1)S(1)}) custom-call(bf16[2,1024,512]{2,1,0:T(8,128)(2,1)} %bitcast.9, bf16[2,384,1024]{2,1,0:T(8,128)(2,1)} %bitcast.10, bf16[5,2,384,768]{3,2,1,0:T(8,128)(2,1)} %bitcast.7, s32[2,5]{1,0:T(2,128)} %bitcast.12), custom_call_target="tpu_custom_call" | custom-call | flops 6000000000 | tf_op jit(solution)/shard_map/leaf/pallas_call | solution.py:43
  3.7 0.5 collective-permute-start
  4.2 0.9 %collective-permute-done.refs_1_ = bf16[384,128]{1,0:T(8,128)(2,1)S(1)} collective-permute-done((bf16[384,128]{1,0:T(8,128)(2,1)S(1)}, bf16[384,128]{1,0:T(8,128)(2,1)S(1)}, u32[]{:S(2)}, u32[]{:S(2)}) %collective-permute-start) | collective-permute-done | bytes 98336 | tf_op jit(solution)/shard_map/ppermute | solution.py:58
  5.5 0.4 collective-permute-start.2
  6.0 2.7 %collective-permute-start.1 = (bf16[384,128]{1,0:T(8,128)(2,1)S(1)}, bf16[384,128]{1,0:T(8,128)(2,1)S(1)}, u32[]{:S(2)}, u32[]{:S(2)}) collective-permute-start(bf16[384,128]{1,0:T(8,128)(2,1)S(1)} %get-tuple-element.35.refs_3_.refs_0_), channel_id=1, source_target_pairs={{0,2},{1,3},{2,0},{3,1},{4,6},{5,7},{6,4},{7,5},{8,10},{9,11},{10,... | collective-permute-start | bytes 294920 | tf_op jit(solution)/shard_map/ppermute | solution.py:58
  8.7 0.4 level1_1.1.refs_3_.refs_0_
  9.1 2.0 %collective-permute-start.4 = (bf16[384,256]{1,0:T(8,128)(2,1)S(1)}, bf16[384,256]{1,0:T(8,128)(2,1)S(1)}, u32[]{:S(2)}, u32[]{:S(2)}) collective-permute-start(bf16[384,256]{1,0:T(8,128)(2,1)S(1)} %level1_1.1.refs_3_.refs_0_), channel_id=1, source_target_pairs={{0,2},{1,3},{2,0},{3,1},{4,6},{5,7},{6,4},{7,5},{8,10},{9,11},{10,... | collective-permute-start | bytes 589832 | tf_op jit(solution)/shard_map/ppermute | solution.py:58
  11.1 2.5 %prefetch.1 = (bf16[2,384,768]{2,1,0:T(8,128)(2,1)S(1)}, bf16[2,384,768]{2,1,0:T(8,128)(2,1)S(1)}, bf16[2,1024,384]{2,1,0:T(8,128)(2,1)S(1)}) custom-call(bf16[5,2,384,768]{3,2,1,0:T(8,128)(2,1)} %bitcast.8, bf16[2,1024,384]{2,1,0:T(8,128)(2,1)} %bitcast.11, s32[2,5]{1,0:T(2,128)} %bitcast.13, bf16[384,256]{1,0:T(8,128)(2,1)S(1)} %level1_1.1.refs_3_.refs_0_), custom_call_target="tpu_custom_call" | custom-call | flops 6000000000 | tf_op jit(solution)/shard_map/prefetch/pallas_call | solution.py:43
  14.0 2.7 %collective-permute-start.3 = (bf16[384,128]{1,0:T(8,128)(2,1)S(1)}, bf16[384,128]{1,0:T(8,128)(2,1)S(1)}, u32[]{:S(2)}, u32[]{:S(2)}) collective-permute-start(bf16[384,128]{1,0:T(8,128)(2,1)S(1)} %level2_0.1.refs_3_.refs_0_), channel_id=1, source_target_pairs={{0,4},{1,5},{2,6},{3,7},{4,0},{5,1},{6,2},{7,3},{8,12},{9,13},{10,... | collective-permute-start | bytes 294920 | tf_op jit(solution)/shard_map/ppermute | solution.py:58
  16.6 0.5 level1_2.1.refs_3_.refs_0_
  17.1 0.5 collective-permute-start.9
  17.7 0.4 level2_1.1.refs_3_.refs_0_
  18.0 2.3 %collective-permute-start.12 = (bf16[384,256]{1,0:T(8,128)(2,1)S(1)}, bf16[384,256]{1,0:T(8,128)(2,1)S(1)}, u32[]{:S(2)}, u32[]{:S(2)}) collective-permute-start(bf16[384,256]{1,0:T(8,128)(2,1)S(1)} %level2_1.1.refs_3_.refs_0_), channel_id=1, source_target_pairs={{0,4},{1,5},{2,6},{3,7},{4,0},{5,1},{6,2},{7,3},{8,12},{9,13},{10,... | collective-permute-start | bytes 589832 | tf_op jit(solution)/shard_map/ppermute | solution.py:58
  20.3 1.8 %collective-permute-done.3.refs_1_ = bf16[384,128]{1,0:T(8,128)(2,1)S(1)} collective-permute-done((bf16[384,128]{1,0:T(8,128)(2,1)S(1)}, bf16[384,128]{1,0:T(8,128)(2,1)S(1)}, u32[]{:S(2)}, u32[]{:S(2)}) %collective-permute-start.3) | collective-permute-done | bytes 98336 | tf_op jit(solution)/shard_map/ppermute | solution.py:58
  22.7 1.0 %collective-permute-done.5.refs_1_ = bf16[384,128]{1,0:T(8,128)(2,1)S(1)} collective-permute-done((bf16[384,128]{1,0:T(8,128)(2,1)S(1)}, bf16[384,128]{1,0:T(8,128)(2,1)S(1)}, u32[]{:S(2)}, u32[]{:S(2)}) %collective-permute-start.5) | collective-permute-done | bytes 98336 | tf_op jit(solution)/shard_map/ppermute | solution.py:58
  23.8 0.6 last_0.1
  24.4 2.5 %collective-permute-start.6 = (bf16[256,128]{1,0:T(8,128)(2,1)S(1)}, bf16[256,128]{1,0:T(8,128)(2,1)S(1)}, u32[]{:S(2)}, u32[]{:S(2)}) collective-permute-start(bf16[256,128]{1,0:T(8,128)(2,1)S(1)} %get-tuple-element.42), channel_id=1, source_target_pairs={{0,24},{8,16},{16,8},{24,0},{1,25},{9,17},{17,9},{25,1},{2,26},{10... | collective-permute-start | bytes 196616 | tf_op jit(solution)/shard_map/ppermute | solution.py:58
  26.9 0.5 collective-permute-start.7
  27.4 0.5 collective-permute-start.8
  27.9 2.9 %collective-permute-done.9.refs_1_ = bf16[384,384]{1,0:T(8,128)(2,1)S(1)} collective-permute-done((bf16[384,384]{1,0:T(8,128)(2,1)S(1)}, bf16[384,384]{1,0:T(8,128)(2,1)S(1)}, u32[]{:S(2)}, u32[]{:S(2)}) %collective-permute-start.9) | collective-permute-done | bytes 294944 | tf_op jit(solution)/shard_map/ppermute | solution.py:58
  30.8 0.5 level2_2.1.refs_4_.refs_0_
  31.7 0.4 level1_3.1.refs_3_.refs_0_
  32.1 2.3 %collective-permute-start.11 = (bf16[384,256]{1,0:T(8,128)(2,1)S(1)}, bf16[384,256]{1,0:T(8,128)(2,1)S(1)}, u32[]{:S(2)}, u32[]{:S(2)}) collective-permute-start(bf16[384,256]{1,0:T(8,128)(2,1)S(1)} %level1_3.1.refs_3_.refs_0_), channel_id=1, source_target_pairs={{0,2},{1,3},{2,0},{3,1},{4,6},{5,7},{6,4},{7,5},{8,10},{9,11},{10,... | collective-permute-start | bytes 589832 | tf_op jit(solution)/shard_map/ppermute | solution.py:58
  35.1 1.2 %collective-permute-done.13.refs_1_ = bf16[384,256]{1,0:T(8,128)(2,1)S(1)} collective-permute-done((bf16[384,256]{1,0:T(8,128)(2,1)S(1)}, bf16[384,256]{1,0:T(8,128)(2,1)S(1)}, u32[]{:S(2)}, u32[]{:S(2)}) %collective-permute-start.13) | collective-permute-done | bytes 196640 | tf_op jit(solution)/shard_map/ppermute | solution.py:58
  36.2 0.8 %last_1.1 = (f32[256,256]{1,0:T(8,128)S(1)}, bf16[256,256]{1,0:T(8,128)(2,1)S(1)}, bf16[256,256]{1,0:T(8,128)(2,1)S(1)}, bf16[256,256]{1,0:T(8,128)(2,1)S(1)}) custom-call(f32[384,256]{1,0:T(8,128)S(1)} %between_1.1.refs_0_, bf16[384,256]{1,0:T(8,128)(2,1)S(1)} %collective-permute-done.13.refs_1_, ...), custom_call_target="tpu_custom_call" | custom-call | flops 6000000000 | tf_op jit(solution)/shard_map/last_1/pallas_call | solution.py:43
  37.1 2.5 %collective-permute-start.14 = (bf16[256,256]{1,0:T(8,128)(2,1)S(1)}, bf16[256,256]{1,0:T(8,128)(2,1)S(1)}, u32[]{:S(2)}, u32[]{:S(2)}) collective-permute-start(bf16[256,256]{1,0:T(8,128)(2,1)S(1)} %get-tuple-element.46), channel_id=1, source_target_pairs={{0,24},{8,16},{16,8},{24,0},{1,25},{9,17},{17,9},{25,1},{2,26},{10... | collective-permute-start | bytes 393224 | tf_op jit(solution)/shard_map/ppermute | solution.py:58
  39.6 0.5 collective-permute-start.15
  40.1 0.5 collective-permute-start.16
  40.6 1.2 %collective-permute-done.11.refs_1_ = bf16[384,256]{1,0:T(8,128)(2,1)S(1)} collective-permute-done((bf16[384,256]{1,0:T(8,128)(2,1)S(1)}, bf16[384,256]{1,0:T(8,128)(2,1)S(1)}, u32[]{:S(2)}, u32[]{:S(2)}) %collective-permute-start.11) | collective-permute-done | bytes 196640 | tf_op jit(solution)/shard_map/ppermute | solution.py:58
  41.8 0.4 level2_3.1.refs_3_.refs_0_
  42.1 3.3 %collective-permute-start.21 = (bf16[384,256]{1,0:T(8,128)(2,1)S(1)}, bf16[384,256]{1,0:T(8,128)(2,1)S(1)}, u32[]{:S(2)}, u32[]{:S(2)}) collective-permute-start(bf16[384,256]{1,0:T(8,128)(2,1)S(1)} %level2_3.1.refs_3_.refs_0_), channel_id=1, source_target_pairs={{0,4},{1,5},{2,6},{3,7},{4,0},{5,1},{6,2},{7,3},{8,12},{9,13},{10,... | collective-permute-start | bytes 589832 | tf_op jit(solution)/shard_map/ppermute | solution.py:58
  45.4 5.4 %collective-permute-done.10.refs_1_ = bf16[384,384]{1,0:T(8,128)(2,1)S(1)} collective-permute-done((bf16[384,384]{1,0:T(8,128)(2,1)S(1)}, bf16[384,384]{1,0:T(8,128)(2,1)S(1)}, u32[]{:S(2)}, u32[]{:S(2)}) %collective-permute-start.10) | collective-permute-done | bytes 294944 | tf_op jit(solution)/shard_map/ppermute | solution.py:58
  50.8 0.5 level3_2.1.refs_0_
  51.5 0.4 between_2.1
  51.8 1.2 %collective-permute-done.17.refs_1_ = bf16[384,384]{1,0:T(8,128)(2,1)S(1)} collective-permute-done((bf16[384,384]{1,0:T(8,128)(2,1)S(1)}, bf16[384,384]{1,0:T(8,128)(2,1)S(1)}, u32[]{:S(2)}, u32[]{:S(2)}) %collective-permute-start.17) | collective-permute-done | bytes 294944 | tf_op jit(solution)/shard_map/ppermute | solution.py:58
  53.0 1.2 %last_2.1 = (f32[256,384]{1,0:T(8,128)S(1)}, bf16[256,384]{1,0:T(8,128)(2,1)S(1)}, bf16[256,384]{1,0:T(8,128)(2,1)S(1)}, bf16[256,384]{1,0:T(8,128)(2,1)S(1)}) custom-call(f32[384,384]{1,0:T(8,128)S(1)} %get-tuple-element.50.refs_0_, bf16[384,384]{1,0:T(8,128)(2,1)S(1)} %collective-permute-done.17.refs_1_, ...), custom_call_target="tpu_custom_call" | custom-call | flops 6000000000 | tf_op jit(solution)/shard_map/last_2/pallas_call | solution.py:43
  54.2 2.5 %collective-permute-start.18 = (bf16[256,384]{1,0:T(8,128)(2,1)S(1)}, bf16[256,384]{1,0:T(8,128)(2,1)S(1)}, u32[]{:S(2)}, u32[]{:S(2)}) collective-permute-start(bf16[256,384]{1,0:T(8,128)(2,1)S(1)} %get-tuple-element.52), channel_id=1, source_target_pairs={{0,24},{8,16},{16,8},{24,0},{1,25},{9,17},{17,9},{25,1},{2,26},{10... | collective-permute-start | bytes 589832 | tf_op jit(solution)/shard_map/ppermute | solution.py:58
  56.8 0.5 collective-permute-start.19
  57.3 0.5 collective-permute-start.20
  58.5 1.2 %collective-permute-done.22.refs_1_ = bf16[384,256]{1,0:T(8,128)(2,1)S(1)} collective-permute-done((bf16[384,256]{1,0:T(8,128)(2,1)S(1)}, bf16[384,256]{1,0:T(8,128)(2,1)S(1)}, u32[]{:S(2)}, u32[]{:S(2)}) %collective-permute-start.22) | collective-permute-done | bytes 196640 | tf_op jit(solution)/shard_map/ppermute | solution.py:58
  59.7 0.8 %last_3.1 = (f32[256,256]{1,0:T(8,128)S(1)}, bf16[256,256]{1,0:T(8,128)(2,1)S(1)}, bf16[256,256]{1,0:T(8,128)(2,1)S(1)}, bf16[256,256]{1,0:T(8,128)(2,1)S(1)}) custom-call(f32[384,256]{1,0:T(8,128)S(1)} %between_3.1.refs_0_, bf16[384,256]{1,0:T(8,128)(2,1)S(1)} %collective-permute-done.22.refs_1_, ...), custom_call_target="tpu_custom_call" | custom-call | tf_op jit(solution)/shard_map/last_3/pallas_call | solution.py:43
  60.5 2.5 %collective-permute-start.23 = (bf16[256,256]{1,0:T(8,128)(2,1)S(1)}, bf16[256,256]{1,0:T(8,128)(2,1)S(1)}, u32[]{:S(2)}, u32[]{:S(2)}) collective-permute-start(bf16[256,256]{1,0:T(8,128)(2,1)S(1)} %get-tuple-element.56), channel_id=1, source_target_pairs={{0,24},{8,16},{16,8},{24,0},{1,25},{9,17},{17,9},{25,1},{2,26},{10... | collective-permute-start | bytes 393224 | tf_op jit(solution)/shard_map/ppermute | solution.py:58
  63.0 0.5 collective-permute-start.24
  63.5 1.0 %collective-permute-start.25 = (bf16[256,256]{1,0:T(8,128)(2,1)S(1)}, bf16[256,256]{1,0:T(8,128)(2,1)S(1)}, u32[]{:S(2)}, u32[]{:S(2)}) collective-permute-start(bf16[256,256]{1,0:T(8,128)(2,1)S(1)} %get-tuple-element.58), channel_id=1, source_target_pairs={{0,8},{8,0},{16,24},{24,16},{1,9},{9,1},{17,25},{25,17},{2,10},{10... | collective-permute-start | bytes 393224 | tf_op jit(solution)/shard_map/ppermute | solution.py:58
  64.5 2.8 %collective-permute-done.19.refs_4_ = bf16[256,384]{1,0:T(8,128)(2,1)S(1)} collective-permute-done((bf16[256,384]{1,0:T(8,128)(2,1)S(1)}, bf16[256,384]{1,0:T(8,128)(2,1)S(1)}, u32[]{:S(2)}, u32[]{:S(2)}) %collective-permute-start.19) | collective-permute-done | bytes 196640 | tf_op jit(solution)/shard_map/ppermute | solution.py:58
  67.3 2.8 %collective-permute-done.23.refs_7_ = bf16[256,256]{1,0:T(8,128)(2,1)S(1)} collective-permute-done((bf16[256,256]{1,0:T(8,128)(2,1)S(1)}, bf16[256,256]{1,0:T(8,128)(2,1)S(1)}, u32[]{:S(2)}, u32[]{:S(2)}) %collective-permute-start.23) | collective-permute-done | bytes 131104 | tf_op jit(solution)/shard_map/ppermute | solution.py:58
  70.1 1.9 %collective-permute-done.24.refs_8_ = bf16[256,256]{1,0:T(8,128)(2,1)S(1)} collective-permute-done((bf16[256,256]{1,0:T(8,128)(2,1)S(1)}, bf16[256,256]{1,0:T(8,128)(2,1)S(1)}, u32[]{:S(2)}, u32[]{:S(2)}) %collective-permute-start.24) | collective-permute-done | bytes 131104 | tf_op jit(solution)/shard_map/ppermute | solution.py:58
  72.1 1.0 %end.1 = bf16[2,256,512]{2,1,0:T(8,128)(2,1)} custom-call(bf16[256,128]{1,0:T(8,128)(2,1)S(1)} %sum_0.1.refs_3_.refs_0_, bf16[256,256]{1,0:T(8,128)(2,1)S(1)} %get-tuple-element.49.refs_1_, f32[256,384]{1,0:T(8,128)S(1)} %get-tuple-element.51.refs_3_.refs_2_, bf16[256,384]{1,0:T(8,128)(2,1)S(1)} %collective-permute-done.18.refs_3_, ...), custom_call_target="tpu_custom_call" | custom-call | tf_op jit(solution)/shard_map/end/pallas_call | solution.py:347
  (28 shorter events, 3.3 us)
Async XLA Ops:
  3.7 1.5 %collective-permute-start = (bf16[384,128]{1,0:T(8,128)(2,1)S(1)}, bf16[384,128]{1,0:T(8,128)(2,1)S(1)}, u32[]{:S(2)}, u32[]{:S(2)}) collective-permute-start(bf16[384,128]{1,0:T(8,128)(2,1)S(1)} %get-tuple-element.32.refs_0_), channel_id=1, source_target_pairs={{0,1},{1,0},{2,3},{3,2},{4,5},{5,4},{6,7},{7,6},{8,9},{9,8},{10,11... | collective-permute-start | bytes 294920 | tf_op jit(solution)/shard_map/ppermute | solution.py:58
  5.5 3.2 %collective-permute-start.2 = (bf16[384,896]{1,0:T(8,128)(2,1)S(1)}, bf16[384,896]{1,0:T(8,128)(2,1)S(1)}, u32[]{:S(2)}, u32[]{:S(2)}) collective-permute-start(bf16[384,896]{1,0:T(8,128)(2,1)S(1)} %get-tuple-element.37.refs_0_), channel_id=1, source_target_pairs={{0,1},{1,0},{2,3},{3,2},{4,5},{5,4},{6,7},{7,6},{8,9},{9,8},{10,11... | collective-permute-start | bytes 2064392 | tf_op jit(solution)/shard_map/ppermute | solution.py:58
  6.0 7.6 %collective-permute-start.1 = (bf16[384,128]{1,0:T(8,128)(2,1)S(1)}, bf16[384,128]{1,0:T(8,128)(2,1)S(1)}, u32[]{:S(2)}, u32[]{:S(2)}) collective-permute-start(bf16[384,128]{1,0:T(8,128)(2,1)S(1)} %get-tuple-element.35.refs_3_.refs_0_), channel_id=1, source_target_pairs={{0,2},{1,3},{2,0},{3,1},{4,6},{5,7},{6,4},{7,5},{8,10},{9,11},{10,... | collective-permute-start | bytes 294920 | tf_op jit(solution)/shard_map/ppermute | solution.py:58
  9.1 8.6 %collective-permute-start.4 = (bf16[384,256]{1,0:T(8,128)(2,1)S(1)}, bf16[384,256]{1,0:T(8,128)(2,1)S(1)}, u32[]{:S(2)}, u32[]{:S(2)}) collective-permute-start(bf16[384,256]{1,0:T(8,128)(2,1)S(1)} %level1_1.1.refs_3_.refs_0_), channel_id=1, source_target_pairs={{0,2},{1,3},{2,0},{3,1},{4,6},{5,7},{6,4},{7,5},{8,10},{9,11},{10,... | collective-permute-start | bytes 589832 | tf_op jit(solution)/shard_map/ppermute | solution.py:58
  14.0 8.1 %collective-permute-start.3 = (bf16[384,128]{1,0:T(8,128)(2,1)S(1)}, bf16[384,128]{1,0:T(8,128)(2,1)S(1)}, u32[]{:S(2)}, u32[]{:S(2)}) collective-permute-start(bf16[384,128]{1,0:T(8,128)(2,1)S(1)} %level2_0.1.refs_3_.refs_0_), channel_id=1, source_target_pairs={{0,4},{1,5},{2,6},{3,7},{4,0},{5,1},{6,2},{7,3},{8,12},{9,13},{10,... | collective-permute-start | bytes 294920 | tf_op jit(solution)/shard_map/ppermute | solution.py:58
  17.1 13.7 %collective-permute-start.9 = (bf16[384,384]{1,0:T(8,128)(2,1)S(1)}, bf16[384,384]{1,0:T(8,128)(2,1)S(1)}, u32[]{:S(2)}, u32[]{:S(2)}) collective-permute-start(bf16[384,384]{1,0:T(8,128)(2,1)S(1)} %level1_2.1.refs_3_.refs_0_), channel_id=1, source_target_pairs={{0,2},{1,3},{2,0},{3,1},{4,6},{5,7},{6,4},{7,5},{8,10},{9,11},{10,... | collective-permute-start | bytes 884744 | tf_op jit(solution)/shard_map/ppermute | solution.py:58
  18.0 16.3 %collective-permute-start.12 = (bf16[384,256]{1,0:T(8,128)(2,1)S(1)}, bf16[384,256]{1,0:T(8,128)(2,1)S(1)}, u32[]{:S(2)}, u32[]{:S(2)}) collective-permute-start(bf16[384,256]{1,0:T(8,128)(2,1)S(1)} %level2_1.1.refs_3_.refs_0_), channel_id=1, source_target_pairs={{0,4},{1,5},{2,6},{3,7},{4,0},{5,1},{6,2},{7,3},{8,12},{9,13},{10,... | collective-permute-start | bytes 589832 | tf_op jit(solution)/shard_map/ppermute | solution.py:58
  22.4 1.4 %collective-permute-start.5 = (bf16[384,128]{1,0:T(8,128)(2,1)S(1)}, bf16[384,128]{1,0:T(8,128)(2,1)S(1)}, u32[]{:S(2)}, u32[]{:S(2)}) collective-permute-start(bf16[384,128]{1,0:T(8,128)(2,1)S(1)} %level3_0.1.refs_0_), channel_id=1, source_target_pairs={{0,1},{1,0},{2,3},{3,2},{4,5},{5,4},{6,7},{7,6},{8,9},{9,8},{10,11... | collective-permute-start | bytes 294920 | tf_op jit(solution)/shard_map/ppermute | solution.py:58
  24.4 7.0 %collective-permute-start.6 = (bf16[256,128]{1,0:T(8,128)(2,1)S(1)}, bf16[256,128]{1,0:T(8,128)(2,1)S(1)}, u32[]{:S(2)}, u32[]{:S(2)}) collective-permute-start(bf16[256,128]{1,0:T(8,128)(2,1)S(1)} %get-tuple-element.42), channel_id=1, source_target_pairs={{0,24},{8,16},{16,8},{24,0},{1,25},{9,17},{17,9},{25,1},{2,26},{10... | collective-permute-start | bytes 196616 | tf_op jit(solution)/shard_map/ppermute | solution.py:58
  26.9 4.5 %collective-permute-start.7 = (bf16[256,128]{1,0:T(8,128)(2,1)S(1)}, bf16[256,128]{1,0:T(8,128)(2,1)S(1)}, u32[]{:S(2)}, u32[]{:S(2)}) collective-permute-start(bf16[256,128]{1,0:T(8,128)(2,1)S(1)} %get-tuple-element.43), channel_id=1, source_target_pairs={{0,16},{8,24},{16,0},{24,8},{1,17},{9,25},{17,1},{25,9},{2,18},{10... | collective-permute-start | bytes 196616 | tf_op jit(solution)/shard_map/ppermute | solution.py:58
  27.4 4.3 %collective-permute-start.8 = (bf16[256,128]{1,0:T(8,128)(2,1)S(1)}, bf16[256,128]{1,0:T(8,128)(2,1)S(1)}, u32[]{:S(2)}, u32[]{:S(2)}) collective-permute-start(bf16[256,128]{1,0:T(8,128)(2,1)S(1)} %get-tuple-element.44), channel_id=1, source_target_pairs={{0,8},{8,0},{16,24},{24,16},{1,9},{9,1},{17,25},{25,17},{2,10},{10... | collective-permute-start | bytes 196616 | tf_op jit(solution)/shard_map/ppermute | solution.py:58
  31.4 19.5 %collective-permute-start.10 = (bf16[384,384]{1,0:T(8,128)(2,1)S(1)}, bf16[384,384]{1,0:T(8,128)(2,1)S(1)}, u32[]{:S(2)}, u32[]{:S(2)}) collective-permute-start(bf16[384,384]{1,0:T(8,128)(2,1)S(1)} %level2_2.1.refs_4_.refs_0_), channel_id=1, source_target_pairs={{0,4},{1,5},{2,6},{3,7},{4,0},{5,1},{6,2},{7,3},{8,12},{9,13},{10,... | collective-permute-start | bytes 884744 | tf_op jit(solution)/shard_map/ppermute | solution.py:58
  32.1 9.7 %collective-permute-start.11 = (bf16[384,256]{1,0:T(8,128)(2,1)S(1)}, bf16[384,256]{1,0:T(8,128)(2,1)S(1)}, u32[]{:S(2)}, u32[]{:S(2)}) collective-permute-start(bf16[384,256]{1,0:T(8,128)(2,1)S(1)} %level1_3.1.refs_3_.refs_0_), channel_id=1, source_target_pairs={{0,2},{1,3},{2,0},{3,1},{4,6},{5,7},{6,4},{7,5},{8,10},{9,11},{10,... | collective-permute-start | bytes 589832 | tf_op jit(solution)/shard_map/ppermute | solution.py:58
  34.7 1.5 %collective-permute-start.13 = (bf16[384,256]{1,0:T(8,128)(2,1)S(1)}, bf16[384,256]{1,0:T(8,128)(2,1)S(1)}, u32[]{:S(2)}, u32[]{:S(2)}) collective-permute-start(bf16[384,256]{1,0:T(8,128)(2,1)S(1)} %level3_1.1.refs_0_), channel_id=1, source_target_pairs={{0,1},{1,0},{2,3},{3,2},{4,5},{5,4},{6,7},{7,6},{8,9},{9,8},{10,11... | collective-permute-start | bytes 589832 | tf_op jit(solution)/shard_map/ppermute | solution.py:58
  37.1 14.4 %collective-permute-start.14 = (bf16[256,256]{1,0:T(8,128)(2,1)S(1)}, bf16[256,256]{1,0:T(8,128)(2,1)S(1)}, u32[]{:S(2)}, u32[]{:S(2)}) collective-permute-start(bf16[256,256]{1,0:T(8,128)(2,1)S(1)} %get-tuple-element.46), channel_id=1, source_target_pairs={{0,24},{8,16},{16,8},{24,0},{1,25},{9,17},{17,9},{25,1},{2,26},{10... | collective-permute-start | bytes 393224 | tf_op jit(solution)/shard_map/ppermute | solution.py:58
  39.6 11.9 %collective-permute-start.15 = (bf16[256,256]{1,0:T(8,128)(2,1)S(1)}, bf16[256,256]{1,0:T(8,128)(2,1)S(1)}, u32[]{:S(2)}, u32[]{:S(2)}) collective-permute-start(bf16[256,256]{1,0:T(8,128)(2,1)S(1)} %get-tuple-element.47), channel_id=1, source_target_pairs={{0,16},{8,24},{16,0},{24,8},{1,17},{9,25},{17,1},{25,9},{2,18},{10... | collective-permute-start | bytes 393224 | tf_op jit(solution)/shard_map/ppermute | solution.py:58
  40.1 11.4 %collective-permute-start.16 = (bf16[256,256]{1,0:T(8,128)(2,1)S(1)}, bf16[256,256]{1,0:T(8,128)(2,1)S(1)}, u32[]{:S(2)}, u32[]{:S(2)}) collective-permute-start(bf16[256,256]{1,0:T(8,128)(2,1)S(1)} %get-tuple-element.48), channel_id=1, source_target_pairs={{0,8},{8,0},{16,24},{24,16},{1,9},{9,1},{17,25},{25,17},{2,10},{10... | collective-permute-start | bytes 393224 | tf_op jit(solution)/shard_map/ppermute | solution.py:58
  42.1 15.6 %collective-permute-start.21 = (bf16[384,256]{1,0:T(8,128)(2,1)S(1)}, bf16[384,256]{1,0:T(8,128)(2,1)S(1)}, u32[]{:S(2)}, u32[]{:S(2)}) collective-permute-start(bf16[384,256]{1,0:T(8,128)(2,1)S(1)} %level2_3.1.refs_3_.refs_0_), channel_id=1, source_target_pairs={{0,4},{1,5},{2,6},{3,7},{4,0},{5,1},{6,2},{7,3},{8,12},{9,13},{10,... | collective-permute-start | bytes 589832 | tf_op jit(solution)/shard_map/ppermute | solution.py:58
  51.3 1.6 %collective-permute-start.17 = (bf16[384,384]{1,0:T(8,128)(2,1)S(1)}, bf16[384,384]{1,0:T(8,128)(2,1)S(1)}, u32[]{:S(2)}, u32[]{:S(2)}) collective-permute-start(bf16[384,384]{1,0:T(8,128)(2,1)S(1)} %level3_2.1.refs_0_), channel_id=1, source_target_pairs={{0,1},{1,0},{2,3},{3,2},{4,5},{5,4},{6,7},{7,6},{8,9},{9,8},{10,11... | collective-permute-start | bytes 884744 | tf_op jit(solution)/shard_map/ppermute | solution.py:58
  54.2 9.3 %collective-permute-start.18 = (bf16[256,384]{1,0:T(8,128)(2,1)S(1)}, bf16[256,384]{1,0:T(8,128)(2,1)S(1)}, u32[]{:S(2)}, u32[]{:S(2)}) collective-permute-start(bf16[256,384]{1,0:T(8,128)(2,1)S(1)} %get-tuple-element.52), channel_id=1, source_target_pairs={{0,24},{8,16},{16,8},{24,0},{1,25},{9,17},{17,9},{25,1},{2,26},{10... | collective-permute-start | bytes 589832 | tf_op jit(solution)/shard_map/ppermute | solution.py:58
  56.8 10.5 %collective-permute-start.19 = (bf16[256,384]{1,0:T(8,128)(2,1)S(1)}, bf16[256,384]{1,0:T(8,128)(2,1)S(1)}, u32[]{:S(2)}, u32[]{:S(2)}) collective-permute-start(bf16[256,384]{1,0:T(8,128)(2,1)S(1)} %get-tuple-element.53), channel_id=1, source_target_pairs={{0,16},{8,24},{16,0},{24,8},{1,17},{9,25},{17,1},{25,9},{2,18},{10... | collective-permute-start | bytes 589832 | tf_op jit(solution)/shard_map/ppermute | solution.py:58
  57.3 10.0 %collective-permute-start.20 = (bf16[256,384]{1,0:T(8,128)(2,1)S(1)}, bf16[256,384]{1,0:T(8,128)(2,1)S(1)}, u32[]{:S(2)}, u32[]{:S(2)}) collective-permute-start(bf16[256,384]{1,0:T(8,128)(2,1)S(1)} %get-tuple-element.54), channel_id=1, source_target_pairs={{0,8},{8,0},{16,24},{24,16},{1,9},{9,1},{17,25},{25,17},{2,10},{10... | collective-permute-start | bytes 589832 | tf_op jit(solution)/shard_map/ppermute | solution.py:58
  58.2 1.5 %collective-permute-start.22 = (bf16[384,256]{1,0:T(8,128)(2,1)S(1)}, bf16[384,256]{1,0:T(8,128)(2,1)S(1)}, u32[]{:S(2)}, u32[]{:S(2)}) collective-permute-start(bf16[384,256]{1,0:T(8,128)(2,1)S(1)} %level3_3.1.refs_0_), channel_id=1, source_target_pairs={{0,1},{1,0},{2,3},{3,2},{4,5},{5,4},{6,7},{7,6},{8,9},{9,8},{10,11... | collective-permute-start | bytes 589832 | tf_op jit(solution)/shard_map/ppermute | solution.py:58
  60.5 9.6 %collective-permute-start.23 = (bf16[256,256]{1,0:T(8,128)(2,1)S(1)}, bf16[256,256]{1,0:T(8,128)(2,1)S(1)}, u32[]{:S(2)}, u32[]{:S(2)}) collective-permute-start(bf16[256,256]{1,0:T(8,128)(2,1)S(1)} %get-tuple-element.56), channel_id=1, source_target_pairs={{0,24},{8,16},{16,8},{24,0},{1,25},{9,17},{17,9},{25,1},{2,26},{10... | collective-permute-start | bytes 393224 | tf_op jit(solution)/shard_map/ppermute | solution.py:58
  63.0 9.0 %collective-permute-start.24 = (bf16[256,256]{1,0:T(8,128)(2,1)S(1)}, bf16[256,256]{1,0:T(8,128)(2,1)S(1)}, u32[]{:S(2)}, u32[]{:S(2)}) collective-permute-start(bf16[256,256]{1,0:T(8,128)(2,1)S(1)} %get-tuple-element.57), channel_id=1, source_target_pairs={{0,16},{8,24},{16,0},{24,8},{1,17},{9,25},{17,1},{25,9},{2,18},{10... | collective-permute-start | bytes 393224 | tf_op jit(solution)/shard_map/ppermute | solution.py:58
  63.5 8.6 %collective-permute-start.25 = (bf16[256,256]{1,0:T(8,128)(2,1)S(1)}, bf16[256,256]{1,0:T(8,128)(2,1)S(1)}, u32[]{:S(2)}, u32[]{:S(2)}) collective-permute-start(bf16[256,256]{1,0:T(8,128)(2,1)S(1)} %get-tuple-element.58), channel_id=1, source_target_pairs={{0,8},{8,0},{16,24},{24,16},{1,9},{9,1},{17,25},{25,17},{2,10},{10... | collective-permute-start | bytes 393224 | tf_op jit(solution)/shard_map/ppermute | solution.py:58

commit v16 on v15

--- a/solution.py
+++ b/solution.py
@@ -9,7 +9,7 @@
 
 SHARES = (1, 2, 3, 2)
 PRELOADED = 2
-DEPTHS = 2
+DEPTHS = 1
 COST = 6 * 10**9
 BF16 = jnp.bfloat16
 F32 = jnp.float32
@@ -283,6 +283,8 @@
     second(0, value)
     (value,) = step("level1_1", [job1(1)], [coeff2[0]])
     second(1, value)
+    (value,) = step("level1_2", [job1(2)], [coeff2[1]])
+    second(2, value)
     *more, basis_v = call(
         prefetch_kernel,
         "prefetch",
@@ -290,14 +292,12 @@
         [pair] * (levels - 1 - PRELOADED) + [in_vmem(*basis.shape)],
         [pltpu.SMEM(index.shape, jnp.int32), pltpu.SemaphoreType.DMA((2 * levels,))],
         [in_hbm(blocks), in_hbm(basis), in_hbm(index)],
-        [coeff2[1]],
+        [coeff2[2]],
     )
     weights += more
     (value,) = step("level2_0", [(2, 0, coeff2[0], near2[0])], [basis_v])
     third(0, value)
-    (value,) = step("level1_2", [job1(2)], [coeff3[0]])
-    second(2, value)
-    (value,) = step("level2_1", [(2, 1, coeff2[1], near2[1])], [coeff2[2]])
+    (value,) = step("level2_1", [(2, 1, coeff2[1], near2[1])], [coeff3[0]])
     third(1, value)
 
     def tail(j, after, arrived=()):

time: 73.3 us -> 71 us (0.969)
  waiting for transfers between devices: 24.6 us -> 18.2 us
  starting transfers between devices: 31.7 us -> 36 us
    ppermute x26, waiting for transfers between devices: 24.6 us -> 18.2 us  [partner(): return lax.ppermute(value, axis, pairs)]
    ppermute x26, starting transfers between devices: 31.7 us -> 36 us  [partner(): return lax.ppermute(value, axis, pairs)]
  transfers between devices with their start and end apart: 26 -> 26, of which waited for: 14 -> 12; matrix products, arithmetic and copies ran while one was open for 0% -> 0% of each run, Pallas kernels for 16% -> 16%
where the time goes in v16:
time: 71 us; the launch traced here: 70.9 us
  starting transfers between devices  36 us (51%)
  waiting for transfers between devices  18.2 us (26%)
  Pallas kernels  16.4 us (23%)
    ppermute x26, starting transfers between devices, partner(): return lax.ppermute(value, axis, pairs)  36 us
    ppermute x26, waiting for transfers between devices, partner(): return lax.ppermute(value, axis, pairs)  18.2 us
    pallas_call x23, Pallas kernels, call(): pl.pallas_call(body, name=name, in_specs=[*in_specs, *[ANY] * (len(after)...  15.4 us
  transfers between devices with their start and end apart: 26, of which 12 were waited for; matrix products, arithmetic and copies ran while one was open for 0% of the time, Pallas kernels for 16%

profile of v16, /device:TPU:0, one launch (start us, length us, event | category | flops | bytes accessed | tf_op | source)
XLA Modules:
  0.0 70.9 jit_solution(6160439534917851319)
XLA Ops:
  0.0 3.7 %leaf.1 = (bf16[384,128]{1,0:T(8,128)(2,1)S(1)}, bf16[384,896]{1,0:T(8,128)(2,1)S(1)}, bf16[2,384,768]{2,1,0:T(8,128)(2,1)S(1)}, bf16[2,384,768]{2,1,0:T(8,128)(2,1)S(1)}) custom-call(bf16[2,1024,512]{2,1,0:T(8,128)(2,1)} %bitcast.9, bf16[2,384,1024]{2,1,0:T(8,128)(2,1)} %bitcast.10, bf16[5,2,384,768]{3,2,1,0:T(8,128)(2,1)} %bitcast.7, s32[2,5]{1,0:T(2,128)} %bitcast.12), custom_call_target="tpu_custom_call" | custom-call | flops 6000000000 | tf_op jit(solution)/shard_map/leaf/pallas_call | solution.py:43
  3.7 0.5 collective-permute-start
  4.2 0.9 %collective-permute-done.refs_1_ = bf16[384,128]{1,0:T(8,128)(2,1)S(1)} collective-permute-done((bf16[384,128]{1,0:T(8,128)(2,1)S(1)}, bf16[384,128]{1,0:T(8,128)(2,1)S(1)}, u32[]{:S(2)}, u32[]{:S(2)}) %collective-permute-start) | collective-permute-done | bytes 98336 | tf_op jit(solution)/shard_map/ppermute | solution.py:58
  5.5 0.4 collective-permute-start.2
  5.9 2.7 %collective-permute-start.1 = (bf16[384,128]{1,0:T(8,128)(2,1)S(1)}, bf16[384,128]{1,0:T(8,128)(2,1)S(1)}, u32[]{:S(2)}, u32[]{:S(2)}) collective-permute-start(bf16[384,128]{1,0:T(8,128)(2,1)S(1)} %get-tuple-element.35.refs_3_.refs_0_), channel_id=1, source_target_pairs={{0,2},{1,3},{2,0},{3,1},{4,6},{5,7},{6,4},{7,5},{8,10},{9,11},{10,... | collective-permute-start | bytes 294920 | tf_op jit(solution)/shard_map/ppermute | solution.py:58
  8.6 0.4 level1_1.1.refs_3_.refs_0_
  9.0 2.1 %collective-permute-start.4 = (bf16[384,256]{1,0:T(8,128)(2,1)S(1)}, bf16[384,256]{1,0:T(8,128)(2,1)S(1)}, u32[]{:S(2)}, u32[]{:S(2)}) collective-permute-start(bf16[384,256]{1,0:T(8,128)(2,1)S(1)} %level1_1.1.refs_3_.refs_0_), channel_id=1, source_target_pairs={{0,2},{1,3},{2,0},{3,1},{4,6},{5,7},{6,4},{7,5},{8,10},{9,11},{10,... | collective-permute-start | bytes 589832 | tf_op jit(solution)/shard_map/ppermute | solution.py:58
  11.0 0.5 level1_2.1.refs_3_.refs_0_
  11.7 2.5 %prefetch.1 = (bf16[2,384,768]{2,1,0:T(8,128)(2,1)S(1)}, bf16[2,384,768]{2,1,0:T(8,128)(2,1)S(1)}, bf16[2,1024,384]{2,1,0:T(8,128)(2,1)S(1)}) custom-call(bf16[5,2,384,768]{3,2,1,0:T(8,128)(2,1)} %bitcast.8, bf16[2,1024,384]{2,1,0:T(8,128)(2,1)} %bitcast.11, s32[2,5]{1,0:T(2,128)} %bitcast.13, bf16[384,384]{1,0:T(8,128)(2,1)S(1)} %level1_2.1.refs_3_.refs_0_), custom_call_target="tpu_custom_call" | custom-call | flops 6000000000 | tf_op jit(solution)/shard_map/prefetch/pallas_call | solution.py:43
  14.5 3.1 %collective-permute-start.3 = (bf16[384,128]{1,0:T(8,128)(2,1)S(1)}, bf16[384,128]{1,0:T(8,128)(2,1)S(1)}, u32[]{:S(2)}, u32[]{:S(2)}) collective-permute-start(bf16[384,128]{1,0:T(8,128)(2,1)S(1)} %level2_0.1.refs_3_.refs_0_), channel_id=1, source_target_pairs={{0,4},{1,5},{2,6},{3,7},{4,0},{5,1},{6,2},{7,3},{8,12},{9,13},{10,... | collective-permute-start | bytes 294920 | tf_op jit(solution)/shard_map/ppermute | solution.py:58
  17.6 0.4 level2_1.1.refs_3_.refs_0_
  18.0 2.3 %collective-permute-start.12 = (bf16[384,256]{1,0:T(8,128)(2,1)S(1)}, bf16[384,256]{1,0:T(8,128)(2,1)S(1)}, u32[]{:S(2)}, u32[]{:S(2)}) collective-permute-start(bf16[384,256]{1,0:T(8,128)(2,1)S(1)} %level2_1.1.refs_3_.refs_0_), channel_id=1, source_target_pairs={{0,4},{1,5},{2,6},{3,7},{4,0},{5,1},{6,2},{7,3},{8,12},{9,13},{10,... | collective-permute-start | bytes 589832 | tf_op jit(solution)/shard_map/ppermute | solution.py:58
  20.2 4.6 %collective-permute-done.3.refs_1_ = bf16[384,128]{1,0:T(8,128)(2,1)S(1)} collective-permute-done((bf16[384,128]{1,0:T(8,128)(2,1)S(1)}, bf16[384,128]{1,0:T(8,128)(2,1)S(1)}, u32[]{:S(2)}, u32[]{:S(2)}) %collective-permute-start.3) | collective-permute-done | bytes 98336 | tf_op jit(solution)/shard_map/ppermute | solution.py:58
  25.4 1.0 %collective-permute-done.5.refs_1_ = bf16[384,128]{1,0:T(8,128)(2,1)S(1)} collective-permute-done((bf16[384,128]{1,0:T(8,128)(2,1)S(1)}, bf16[384,128]{1,0:T(8,128)(2,1)S(1)}, u32[]{:S(2)}, u32[]{:S(2)}) %collective-permute-start.5) | collective-permute-done | bytes 98336 | tf_op jit(solution)/shard_map/ppermute | solution.py:58
  26.5 0.6 last_0.1
  27.1 2.5 %collective-permute-start.6 = (bf16[256,128]{1,0:T(8,128)(2,1)S(1)}, bf16[256,128]{1,0:T(8,128)(2,1)S(1)}, u32[]{:S(2)}, u32[]{:S(2)}) collective-permute-start(bf16[256,128]{1,0:T(8,128)(2,1)S(1)} %get-tuple-element.42), channel_id=1, source_target_pairs={{0,24},{8,16},{16,8},{24,0},{1,25},{9,17},{17,9},{25,1},{2,26},{10... | collective-permute-start | bytes 196616 | tf_op jit(solution)/shard_map/ppermute | solution.py:58
  29.6 0.5 collective-permute-start.7
  30.1 0.5 collective-permute-start.8
  30.6 0.5 level2_2.1.refs_4_.refs_0_
  31.2 3.5 %collective-permute-start.10 = (bf16[384,384]{1,0:T(8,128)(2,1)S(1)}, bf16[384,384]{1,0:T(8,128)(2,1)S(1)}, u32[]{:S(2)}, u32[]{:S(2)}) collective-permute-start(bf16[384,384]{1,0:T(8,128)(2,1)S(1)} %level2_2.1.refs_4_.refs_0_), channel_id=1, source_target_pairs={{0,4},{1,5},{2,6},{3,7},{4,0},{5,1},{6,2},{7,3},{8,12},{9,13},{10,... | collective-permute-start | bytes 884744 | tf_op jit(solution)/shard_map/ppermute | solution.py:58
  34.7 0.4 level1_3.1.refs_3_.refs_0_
  35.1 3.3 %collective-permute-start.11 = (bf16[384,256]{1,0:T(8,128)(2,1)S(1)}, bf16[384,256]{1,0:T(8,128)(2,1)S(1)}, u32[]{:S(2)}, u32[]{:S(2)}) collective-permute-start(bf16[384,256]{1,0:T(8,128)(2,1)S(1)} %level1_3.1.refs_3_.refs_0_), channel_id=1, source_target_pairs={{0,2},{1,3},{2,0},{3,1},{4,6},{5,7},{6,4},{7,5},{8,10},{9,11},{10,... | collective-permute-start | bytes 589832 | tf_op jit(solution)/shard_map/ppermute | solution.py:58
  38.4 0.4 level3_1.1.refs_0_
  39.1 1.2 %collective-permute-done.13.refs_1_ = bf16[384,256]{1,0:T(8,128)(2,1)S(1)} collective-permute-done((bf16[384,256]{1,0:T(8,128)(2,1)S(1)}, bf16[384,256]{1,0:T(8,128)(2,1)S(1)}, u32[]{:S(2)}, u32[]{:S(2)}) %collective-permute-start.13) | collective-permute-done | bytes 196640 | tf_op jit(solution)/shard_map/ppermute | solution.py:58
  40.3 0.8 %last_1.1 = (f32[256,256]{1,0:T(8,128)S(1)}, bf16[256,256]{1,0:T(8,128)(2,1)S(1)}, bf16[256,256]{1,0:T(8,128)(2,1)S(1)}, bf16[256,256]{1,0:T(8,128)(2,1)S(1)}) custom-call(f32[384,256]{1,0:T(8,128)S(1)} %between_1.1.refs_0_, bf16[384,256]{1,0:T(8,128)(2,1)S(1)} %collective-permute-done.13.refs_1_, ...), custom_call_target="tpu_custom_call" | custom-call | flops 6000000000 | tf_op jit(solution)/shard_map/last_1/pallas_call | solution.py:43
  41.1 1.6 %collective-permute-start.14 = (bf16[256,256]{1,0:T(8,128)(2,1)S(1)}, bf16[256,256]{1,0:T(8,128)(2,1)S(1)}, u32[]{:S(2)}, u32[]{:S(2)}) collective-permute-start(bf16[256,256]{1,0:T(8,128)(2,1)S(1)} %get-tuple-element.46), channel_id=1, source_target_pairs={{0,24},{8,16},{16,8},{24,0},{1,25},{9,17},{17,9},{25,1},{2,26},{10... | collective-permute-start | bytes 393224 | tf_op jit(solution)/shard_map/ppermute | solution.py:58
  42.6 0.7 %collective-permute-start.15 = (bf16[256,256]{1,0:T(8,128)(2,1)S(1)}, bf16[256,256]{1,0:T(8,128)(2,1)S(1)}, u32[]{:S(2)}, u32[]{:S(2)}) collective-permute-start(bf16[256,256]{1,0:T(8,128)(2,1)S(1)} %get-tuple-element.47), channel_id=1, source_target_pairs={{0,16},{8,24},{16,0},{24,8},{1,17},{9,25},{17,1},{25,9},{2,18},{10... | collective-permute-start | bytes 393224 | tf_op jit(solution)/shard_map/ppermute | solution.py:58
  43.4 1.3 %collective-permute-start.16 = (bf16[256,256]{1,0:T(8,128)(2,1)S(1)}, bf16[256,256]{1,0:T(8,128)(2,1)S(1)}, u32[]{:S(2)}, u32[]{:S(2)}) collective-permute-start(bf16[256,256]{1,0:T(8,128)(2,1)S(1)} %get-tuple-element.48), channel_id=1, source_target_pairs={{0,8},{8,0},{16,24},{24,16},{1,9},{9,1},{17,25},{25,17},{2,10},{10... | collective-permute-start | bytes 393224 | tf_op jit(solution)/shard_map/ppermute | solution.py:58
  44.7 0.4 level2_3.1.refs_3_.refs_0_
  45.0 3.6 %collective-permute-start.21 = (bf16[384,256]{1,0:T(8,128)(2,1)S(1)}, bf16[384,256]{1,0:T(8,128)(2,1)S(1)}, u32[]{:S(2)}, u32[]{:S(2)}) collective-permute-start(bf16[384,256]{1,0:T(8,128)(2,1)S(1)} %level2_3.1.refs_3_.refs_0_), channel_id=1, source_target_pairs={{0,4},{1,5},{2,6},{3,7},{4,0},{5,1},{6,2},{7,3},{8,12},{9,13},{10,... | collective-permute-start | bytes 589832 | tf_op jit(solution)/shard_map/ppermute | solution.py:58
  48.6 0.5 level3_2.1.refs_0_
  49.2 1.2 %collective-permute-done.15.refs_4_ = bf16[256,256]{1,0:T(8,128)(2,1)S(1)} collective-permute-done((bf16[256,256]{1,0:T(8,128)(2,1)S(1)}, bf16[256,256]{1,0:T(8,128)(2,1)S(1)}, u32[]{:S(2)}, u32[]{:S(2)}) %collective-permute-start.15) | collective-permute-done | bytes 131104 | tf_op jit(solution)/shard_map/ppermute | solution.py:58
  50.5 0.4 between_2.1
  50.9 1.2 %last_2.1 = (f32[256,384]{1,0:T(8,128)S(1)}, bf16[256,384]{1,0:T(8,128)(2,1)S(1)}, bf16[256,384]{1,0:T(8,128)(2,1)S(1)}, bf16[256,384]{1,0:T(8,128)(2,1)S(1)}) custom-call(f32[384,384]{1,0:T(8,128)S(1)} %get-tuple-element.50.refs_0_, bf16[384,384]{1,0:T(8,128)(2,1)S(1)} %collective-permute-done.17.refs_1_, ...), custom_call_target="tpu_custom_call" | custom-call | flops 6000000000 | tf_op jit(solution)/shard_map/last_2/pallas_call | solution.py:43
  52.1 2.4 %collective-permute-start.18 = (bf16[256,384]{1,0:T(8,128)(2,1)S(1)}, bf16[256,384]{1,0:T(8,128)(2,1)S(1)}, u32[]{:S(2)}, u32[]{:S(2)}) collective-permute-start(bf16[256,384]{1,0:T(8,128)(2,1)S(1)} %get-tuple-element.52), channel_id=1, source_target_pairs={{0,24},{8,16},{16,8},{24,0},{1,25},{9,17},{17,9},{25,1},{2,26},{10... | collective-permute-start | bytes 589832 | tf_op jit(solution)/shard_map/ppermute | solution.py:58
  54.5 0.5 collective-permute-start.19
  55.0 0.6 collective-permute-start.20
  55.7 0.6 collective-permute-done.21.refs_1_
  56.3 0.4 level3_3.1.refs_0_
  57.0 1.2 %collective-permute-done.22.refs_1_ = bf16[384,256]{1,0:T(8,128)(2,1)S(1)} collective-permute-done((bf16[384,256]{1,0:T(8,128)(2,1)S(1)}, bf16[384,256]{1,0:T(8,128)(2,1)S(1)}, u32[]{:S(2)}, u32[]{:S(2)}) %collective-permute-start.22) | collective-permute-done | bytes 196640 | tf_op jit(solution)/shard_map/ppermute | solution.py:58
  58.2 0.8 %last_3.1 = (f32[256,256]{1,0:T(8,128)S(1)}, bf16[256,256]{1,0:T(8,128)(2,1)S(1)}, bf16[256,256]{1,0:T(8,128)(2,1)S(1)}, bf16[256,256]{1,0:T(8,128)(2,1)S(1)}) custom-call(f32[384,256]{1,0:T(8,128)S(1)} %between_3.1.refs_0_, bf16[384,256]{1,0:T(8,128)(2,1)S(1)} %collective-permute-done.22.refs_1_, ...), custom_call_target="tpu_custom_call" | custom-call | tf_op jit(solution)/shard_map/last_3/pallas_call | solution.py:43
  59.0 2.5 %collective-permute-start.23 = (bf16[256,256]{1,0:T(8,128)(2,1)S(1)}, bf16[256,256]{1,0:T(8,128)(2,1)S(1)}, u32[]{:S(2)}, u32[]{:S(2)}) collective-permute-start(bf16[256,256]{1,0:T(8,128)(2,1)S(1)} %get-tuple-element.56), channel_id=1, source_target_pairs={{0,24},{8,16},{16,8},{24,0},{1,25},{9,17},{17,9},{25,1},{2,26},{10... | collective-permute-start | bytes 393224 | tf_op jit(solution)/shard_map/ppermute | solution.py:58
  61.5 0.5 collective-permute-start.24
  62.0 0.5 collective-permute-start.25
  62.5 2.6 %collective-permute-done.19.refs_4_ = bf16[256,384]{1,0:T(8,128)(2,1)S(1)} collective-permute-done((bf16[256,384]{1,0:T(8,128)(2,1)S(1)}, bf16[256,384]{1,0:T(8,128)(2,1)S(1)}, u32[]{:S(2)}, u32[]{:S(2)}) %collective-permute-start.19) | collective-permute-done | bytes 196640 | tf_op jit(solution)/shard_map/ppermute | solution.py:58
  65.2 2.8 %collective-permute-done.23.refs_7_ = bf16[256,256]{1,0:T(8,128)(2,1)S(1)} collective-permute-done((bf16[256,256]{1,0:T(8,128)(2,1)S(1)}, bf16[256,256]{1,0:T(8,128)(2,1)S(1)}, u32[]{:S(2)}, u32[]{:S(2)}) %collective-permute-start.23) | collective-permute-done | bytes 131104 | tf_op jit(solution)/shard_map/ppermute | solution.py:58
  67.9 1.8 %collective-permute-done.24.refs_8_ = bf16[256,256]{1,0:T(8,128)(2,1)S(1)} collective-permute-done((bf16[256,256]{1,0:T(8,128)(2,1)S(1)}, bf16[256,256]{1,0:T(8,128)(2,1)S(1)}, u32[]{:S(2)}, u32[]{:S(2)}) %collective-permute-start.24) | collective-permute-done | bytes 131104 | tf_op jit(solution)/shard_map/ppermute | solution.py:58
  69.9 1.0 %end.1 = bf16[2,256,512]{2,1,0:T(8,128)(2,1)} custom-call(bf16[256,128]{1,0:T(8,128)(2,1)S(1)} %sum_0.1.refs_3_.refs_0_, bf16[256,256]{1,0:T(8,128)(2,1)S(1)} %get-tuple-element.49.refs_1_, f32[256,384]{1,0:T(8,128)S(1)} %get-tuple-element.51.refs_3_.refs_2_, bf16[256,384]{1,0:T(8,128)(2,1)S(1)} %collective-permute-done.18.refs_3_, ...), custom_call_target="tpu_custom_call" | custom-call | tf_op jit(solution)/shard_map/end/pallas_call | solution.py:347
  (28 shorter events, 2.5 us)
Async XLA Ops:
  3.7 1.5 %collective-permute-start = (bf16[384,128]{1,0:T(8,128)(2,1)S(1)}, bf16[384,128]{1,0:T(8,128)(2,1)S(1)}, u32[]{:S(2)}, u32[]{:S(2)}) collective-permute-start(bf16[384,128]{1,0:T(8,128)(2,1)S(1)} %get-tuple-element.32.refs_0_), channel_id=1, source_target_pairs={{0,1},{1,0},{2,3},{3,2},{4,5},{5,4},{6,7},{7,6},{8,9},{9,8},{10,11... | collective-permute-start | bytes 294920 | tf_op jit(solution)/shard_map/ppermute | solution.py:58
  5.5 3.1 %collective-permute-start.2 = (bf16[384,896]{1,0:T(8,128)(2,1)S(1)}, bf16[384,896]{1,0:T(8,128)(2,1)S(1)}, u32[]{:S(2)}, u32[]{:S(2)}) collective-permute-start(bf16[384,896]{1,0:T(8,128)(2,1)S(1)} %get-tuple-element.37.refs_0_), channel_id=1, source_target_pairs={{0,1},{1,0},{2,3},{3,2},{4,5},{5,4},{6,7},{7,6},{8,9},{9,8},{10,11... | collective-permute-start | bytes 2064392 | tf_op jit(solution)/shard_map/ppermute | solution.py:58
  5.9 8.3 %collective-permute-start.1 = (bf16[384,128]{1,0:T(8,128)(2,1)S(1)}, bf16[384,128]{1,0:T(8,128)(2,1)S(1)}, u32[]{:S(2)}, u32[]{:S(2)}) collective-permute-start(bf16[384,128]{1,0:T(8,128)(2,1)S(1)} %get-tuple-element.35.refs_3_.refs_0_), channel_id=1, source_target_pairs={{0,2},{1,3},{2,0},{3,1},{4,6},{5,7},{6,4},{7,5},{8,10},{9,11},{10,... | collective-permute-start | bytes 294920 | tf_op jit(solution)/shard_map/ppermute | solution.py:58
  9.0 8.6 %collective-permute-start.4 = (bf16[384,256]{1,0:T(8,128)(2,1)S(1)}, bf16[384,256]{1,0:T(8,128)(2,1)S(1)}, u32[]{:S(2)}, u32[]{:S(2)}) collective-permute-start(bf16[384,256]{1,0:T(8,128)(2,1)S(1)} %level1_1.1.refs_3_.refs_0_), channel_id=1, source_target_pairs={{0,2},{1,3},{2,0},{3,1},{4,6},{5,7},{6,4},{7,5},{8,10},{9,11},{10,... | collective-permute-start | bytes 589832 | tf_op jit(solution)/shard_map/ppermute | solution.py:58
  11.6 19.1 %collective-permute-start.9 = (bf16[384,384]{1,0:T(8,128)(2,1)S(1)}, bf16[384,384]{1,0:T(8,128)(2,1)S(1)}, u32[]{:S(2)}, u32[]{:S(2)}) collective-permute-start(bf16[384,384]{1,0:T(8,128)(2,1)S(1)} %level1_2.1.refs_3_.refs_0_), channel_id=1, source_target_pairs={{0,2},{1,3},{2,0},{3,1},{4,6},{5,7},{6,4},{7,5},{8,10},{9,11},{10,... | collective-permute-start | bytes 884744 | tf_op jit(solution)/shard_map/ppermute | solution.py:58
  14.5 10.2 %collective-permute-start.3 = (bf16[384,128]{1,0:T(8,128)(2,1)S(1)}, bf16[384,128]{1,0:T(8,128)(2,1)S(1)}, u32[]{:S(2)}, u32[]{:S(2)}) collective-permute-start(bf16[384,128]{1,0:T(8,128)(2,1)S(1)} %level2_0.1.refs_3_.refs_0_), channel_id=1, source_target_pairs={{0,4},{1,5},{2,6},{3,7},{4,0},{5,1},{6,2},{7,3},{8,12},{9,13},{10,... | collective-permute-start | bytes 294920 | tf_op jit(solution)/shard_map/ppermute | solution.py:58
  18.0 20.4 %collective-permute-start.12 = (bf16[384,256]{1,0:T(8,128)(2,1)S(1)}, bf16[384,256]{1,0:T(8,128)(2,1)S(1)}, u32[]{:S(2)}, u32[]{:S(2)}) collective-permute-start(bf16[384,256]{1,0:T(8,128)(2,1)S(1)} %level2_1.1.refs_3_.refs_0_), channel_id=1, source_target_pairs={{0,4},{1,5},{2,6},{3,7},{4,0},{5,1},{6,2},{7,3},{8,12},{9,13},{10,... | collective-permute-start | bytes 589832 | tf_op jit(solution)/shard_map/ppermute | solution.py:58
  25.1 1.4 %collective-permute-start.5 = (bf16[384,128]{1,0:T(8,128)(2,1)S(1)}, bf16[384,128]{1,0:T(8,128)(2,1)S(1)}, u32[]{:S(2)}, u32[]{:S(2)}) collective-permute-start(bf16[384,128]{1,0:T(8,128)(2,1)S(1)} %level3_0.1.refs_0_), channel_id=1, source_target_pairs={{0,1},{1,0},{2,3},{3,2},{4,5},{5,4},{6,7},{7,6},{8,9},{9,8},{10,11... | collective-permute-start | bytes 294920 | tf_op jit(solution)/shard_map/ppermute | solution.py:58
  27.1 7.6 %collective-permute-start.6 = (bf16[256,128]{1,0:T(8,128)(2,1)S(1)}, bf16[256,128]{1,0:T(8,128)(2,1)S(1)}, u32[]{:S(2)}, u32[]{:S(2)}) collective-permute-start(bf16[256,128]{1,0:T(8,128)(2,1)S(1)} %get-tuple-element.42), channel_id=1, source_target_pairs={{0,24},{8,16},{16,8},{24,0},{1,25},{9,17},{17,9},{25,1},{2,26},{10... | collective-permute-start | bytes 196616 | tf_op jit(solution)/shard_map/ppermute | solution.py:58
  29.6 5.1 %collective-permute-start.7 = (bf16[256,128]{1,0:T(8,128)(2,1)S(1)}, bf16[256,128]{1,0:T(8,128)(2,1)S(1)}, u32[]{:S(2)}, u32[]{:S(2)}) collective-permute-start(bf16[256,128]{1,0:T(8,128)(2,1)S(1)} %get-tuple-element.43), channel_id=1, source_target_pairs={{0,16},{8,24},{16,0},{24,8},{1,17},{9,25},{17,1},{25,9},{2,18},{10... | collective-permute-start | bytes 196616 | tf_op jit(solution)/shard_map/ppermute | solution.py:58
  30.1 4.6 %collective-permute-start.8 = (bf16[256,128]{1,0:T(8,128)(2,1)S(1)}, bf16[256,128]{1,0:T(8,128)(2,1)S(1)}, u32[]{:S(2)}, u32[]{:S(2)}) collective-permute-start(bf16[256,128]{1,0:T(8,128)(2,1)S(1)} %get-tuple-element.44), channel_id=1, source_target_pairs={{0,8},{8,0},{16,24},{24,16},{1,9},{9,1},{17,25},{25,17},{2,10},{10... | collective-permute-start | bytes 196616 | tf_op jit(solution)/shard_map/ppermute | solution.py:58
  31.2 17.4 %collective-permute-start.10 = (bf16[384,384]{1,0:T(8,128)(2,1)S(1)}, bf16[384,384]{1,0:T(8,128)(2,1)S(1)}, u32[]{:S(2)}, u32[]{:S(2)}) collective-permute-start(bf16[384,384]{1,0:T(8,128)(2,1)S(1)} %level2_2.1.refs_4_.refs_0_), channel_id=1, source_target_pairs={{0,4},{1,5},{2,6},{3,7},{4,0},{5,1},{6,2},{7,3},{8,12},{9,13},{10,... | collective-permute-start | bytes 884744 | tf_op jit(solution)/shard_map/ppermute | solution.py:58
  35.1 9.6 %collective-permute-start.11 = (bf16[384,256]{1,0:T(8,128)(2,1)S(1)}, bf16[384,256]{1,0:T(8,128)(2,1)S(1)}, u32[]{:S(2)}, u32[]{:S(2)}) collective-permute-start(bf16[384,256]{1,0:T(8,128)(2,1)S(1)} %level1_3.1.refs_3_.refs_0_), channel_id=1, source_target_pairs={{0,2},{1,3},{2,0},{3,1},{4,6},{5,7},{6,4},{7,5},{8,10},{9,11},{10,... | collective-permute-start | bytes 589832 | tf_op jit(solution)/shard_map/ppermute | solution.py:58
  38.7 1.5 %collective-permute-start.13 = (bf16[384,256]{1,0:T(8,128)(2,1)S(1)}, bf16[384,256]{1,0:T(8,128)(2,1)S(1)}, u32[]{:S(2)}, u32[]{:S(2)}) collective-permute-start(bf16[384,256]{1,0:T(8,128)(2,1)S(1)} %level3_1.1.refs_0_), channel_id=1, source_target_pairs={{0,1},{1,0},{2,3},{3,2},{4,5},{5,4},{6,7},{7,6},{8,9},{9,8},{10,11... | collective-permute-start | bytes 589832 | tf_op jit(solution)/shard_map/ppermute | solution.py:58
  41.1 8.1 %collective-permute-start.14 = (bf16[256,256]{1,0:T(8,128)(2,1)S(1)}, bf16[256,256]{1,0:T(8,128)(2,1)S(1)}, u32[]{:S(2)}, u32[]{:S(2)}) collective-permute-start(bf16[256,256]{1,0:T(8,128)(2,1)S(1)} %get-tuple-element.46), channel_id=1, source_target_pairs={{0,24},{8,16},{16,8},{24,0},{1,25},{9,17},{17,9},{25,1},{2,26},{10... | collective-permute-start | bytes 393224 | tf_op jit(solution)/shard_map/ppermute | solution.py:58
  42.6 7.8 %collective-permute-start.15 = (bf16[256,256]{1,0:T(8,128)(2,1)S(1)}, bf16[256,256]{1,0:T(8,128)(2,1)S(1)}, u32[]{:S(2)}, u32[]{:S(2)}) collective-permute-start(bf16[256,256]{1,0:T(8,128)(2,1)S(1)} %get-tuple-element.47), channel_id=1, source_target_pairs={{0,16},{8,24},{16,0},{24,8},{1,17},{9,25},{17,1},{25,9},{2,18},{10... | collective-permute-start | bytes 393224 | tf_op jit(solution)/shard_map/ppermute | solution.py:58
  43.4 7.1 %collective-permute-start.16 = (bf16[256,256]{1,0:T(8,128)(2,1)S(1)}, bf16[256,256]{1,0:T(8,128)(2,1)S(1)}, u32[]{:S(2)}, u32[]{:S(2)}) collective-permute-start(bf16[256,256]{1,0:T(8,128)(2,1)S(1)} %get-tuple-element.48), channel_id=1, source_target_pairs={{0,8},{8,0},{16,24},{24,16},{1,9},{9,1},{17,25},{25,17},{2,10},{10... | collective-permute-start | bytes 393224 | tf_op jit(solution)/shard_map/ppermute | solution.py:58
  45.0 11.3 %collective-permute-start.21 = (bf16[384,256]{1,0:T(8,128)(2,1)S(1)}, bf16[384,256]{1,0:T(8,128)(2,1)S(1)}, u32[]{:S(2)}, u32[]{:S(2)}) collective-permute-start(bf16[384,256]{1,0:T(8,128)(2,1)S(1)} %level2_3.1.refs_3_.refs_0_), channel_id=1, source_target_pairs={{0,4},{1,5},{2,6},{3,7},{4,0},{5,1},{6,2},{7,3},{8,12},{9,13},{10,... | collective-permute-start | bytes 589832 | tf_op jit(solution)/shard_map/ppermute | solution.py:58
  49.1 1.8 %collective-permute-start.17 = (bf16[384,384]{1,0:T(8,128)(2,1)S(1)}, bf16[384,384]{1,0:T(8,128)(2,1)S(1)}, u32[]{:S(2)}, u32[]{:S(2)}) collective-permute-start(bf16[384,384]{1,0:T(8,128)(2,1)S(1)} %level3_2.1.refs_0_), channel_id=1, source_target_pairs={{0,1},{1,0},{2,3},{3,2},{4,5},{5,4},{6,7},{7,6},{8,9},{9,8},{10,11... | collective-permute-start | bytes 884744 | tf_op jit(solution)/shard_map/ppermute | solution.py:58
  52.1 9.9 %collective-permute-start.18 = (bf16[256,384]{1,0:T(8,128)(2,1)S(1)}, bf16[256,384]{1,0:T(8,128)(2,1)S(1)}, u32[]{:S(2)}, u32[]{:S(2)}) collective-permute-start(bf16[256,384]{1,0:T(8,128)(2,1)S(1)} %get-tuple-element.52), channel_id=1, source_target_pairs={{0,24},{8,16},{16,8},{24,0},{1,25},{9,17},{17,9},{25,1},{2,26},{10... | collective-permute-start | bytes 589832 | tf_op jit(solution)/shard_map/ppermute | solution.py:58
  54.5 10.7 %collective-permute-start.19 = (bf16[256,384]{1,0:T(8,128)(2,1)S(1)}, bf16[256,384]{1,0:T(8,128)(2,1)S(1)}, u32[]{:S(2)}, u32[]{:S(2)}) collective-permute-start(bf16[256,384]{1,0:T(8,128)(2,1)S(1)} %get-tuple-element.53), channel_id=1, source_target_pairs={{0,16},{8,24},{16,0},{24,8},{1,17},{9,25},{17,1},{25,9},{2,18},{10... | collective-permute-start | bytes 589832 | tf_op jit(solution)/shard_map/ppermute | solution.py:58
  55.0 10.1 %collective-permute-start.20 = (bf16[256,384]{1,0:T(8,128)(2,1)S(1)}, bf16[256,384]{1,0:T(8,128)(2,1)S(1)}, u32[]{:S(2)}, u32[]{:S(2)}) collective-permute-start(bf16[256,384]{1,0:T(8,128)(2,1)S(1)} %get-tuple-element.54), channel_id=1, source_target_pairs={{0,8},{8,0},{16,24},{24,16},{1,9},{9,1},{17,25},{25,17},{2,10},{10... | collective-permute-start | bytes 589832 | tf_op jit(solution)/shard_map/ppermute | solution.py:58
  56.7 1.5 %collective-permute-start.22 = (bf16[384,256]{1,0:T(8,128)(2,1)S(1)}, bf16[384,256]{1,0:T(8,128)(2,1)S(1)}, u32[]{:S(2)}, u32[]{:S(2)}) collective-permute-start(bf16[384,256]{1,0:T(8,128)(2,1)S(1)} %level3_3.1.refs_0_), channel_id=1, source_target_pairs={{0,1},{1,0},{2,3},{3,2},{4,5},{5,4},{6,7},{7,6},{8,9},{9,8},{10,11... | collective-permute-start | bytes 589832 | tf_op jit(solution)/shard_map/ppermute | solution.py:58
  59.0 9.0 %collective-permute-start.23 = (bf16[256,256]{1,0:T(8,128)(2,1)S(1)}, bf16[256,256]{1,0:T(8,128)(2,1)S(1)}, u32[]{:S(2)}, u32[]{:S(2)}) collective-permute-start(bf16[256,256]{1,0:T(8,128)(2,1)S(1)} %get-tuple-element.56), channel_id=1, source_target_pairs={{0,24},{8,16},{16,8},{24,0},{1,25},{9,17},{17,9},{25,1},{2,26},{10... | collective-permute-start | bytes 393224 | tf_op jit(solution)/shard_map/ppermute | solution.py:58
  61.5 8.3 %collective-permute-start.24 = (bf16[256,256]{1,0:T(8,128)(2,1)S(1)}, bf16[256,256]{1,0:T(8,128)(2,1)S(1)}, u32[]{:S(2)}, u32[]{:S(2)}) collective-permute-start(bf16[256,256]{1,0:T(8,128)(2,1)S(1)} %get-tuple-element.57), channel_id=1, source_target_pairs={{0,16},{8,24},{16,0},{24,8},{1,17},{9,25},{17,1},{25,9},{2,18},{10... | collective-permute-start | bytes 393224 | tf_op jit(solution)/shard_map/ppermute | solution.py:58
  62.0 7.9 %collective-permute-start.25 = (bf16[256,256]{1,0:T(8,128)(2,1)S(1)}, bf16[256,256]{1,0:T(8,128)(2,1)S(1)}, u32[]{:S(2)}, u32[]{:S(2)}) collective-permute-start(bf16[256,256]{1,0:T(8,128)(2,1)S(1)} %get-tuple-element.58), channel_id=1, source_target_pairs={{0,8},{8,0},{16,24},{24,16},{1,9},{9,1},{17,25},{25,17},{2,10},{10... | collective-permute-start | bytes 393224 | tf_op jit(solution)/shard_map/ppermute | solution.py:58

commit v17 on v16

--- a/solution.py
+++ b/solution.py
@@ -163,25 +163,32 @@
     refs[-1][...] = total.astype(BF16)
 
 
-def between_kernel(bit, parts, counts, own, weights, *refs):
+def between_kernel(bit, cuts, counts, weights, *refs):
     refs = list(refs)
+    owns = [refs.pop(0) for _ in cuts]
     groups = [[refs.pop(0) for _ in range(count)] for count in counts]
     partial = refs.pop(0)
-    for s, start, stop in parts:
-        partial[:, start:stop] = half_dot(weights, s, upper_half(bit), own[:, start:stop])
+    for own, (begin, parts) in zip(owns, cuts):
+        for s, start, stop in parts:
+            partial[:, begin + start : begin + stop] = half_dot(
+                weights, s, upper_half(bit), own[:, start:stop]
+            )
     for group, out in zip(groups, refs):
         sum_kernel(*group, out)
 
 
-def last_kernel(bit, parts, partial, other, weights, basis, *refs):
+def last_kernel(bit, cuts, partial, weights, basis, *refs):
+    others, refs = refs[: len(cuts)], refs[len(cuts) :]
     rows = refs[0].shape[0]
     me = lax.axis_index("blk")
-    for s, start, stop in parts:
-        mixed = partial[:, start:stop] + half_dot(weights, s, 1 - upper_half(bit), other[:, start:stop])
-        coeff = mixed.astype(BF16)
-        for d, ref in enumerate(refs):
-            row = pl.multiple_of((me ^ d) * rows, rows)
-            ref[:, start:stop] = dot(basis[s, pl.ds(row, rows), :], coeff).astype(ref.dtype)
+    for other, (begin, parts) in zip(others, cuts):
+        for s, start, stop in parts:
+            lanes = slice(begin + start, begin + stop)
+            mixed = partial[:, lanes] + half_dot(weights, s, 1 - upper_half(bit), other[:, start:stop])
+            coeff = mixed.astype(BF16)
+            for d, ref in enumerate(refs):
+                row = pl.multiple_of((me ^ d) * rows, rows)
+                ref[:, lanes] = dot(basis[s, pl.ds(row, rows), :], coeff).astype(ref.dtype)
 
 
 def end_kernel(places, counts, *refs):
@@ -246,13 +253,24 @@
 
     near_first = cross(1, first)
 
+    def within(j, begin, size):
+        found = []
+        for s, start, stop in parts[j]:
+            start, stop = max(start - begin, 0), min(stop - begin, size)
+            if start < stop:
+                found.append((s, start, stop))
+        return found
+
     def step(name, jobs, after=(), flops=COST, through=()):
-        args = [here(v) for level, j, own, other in jobs for v in (own, other, weights[level])]
+        args = [here(v) for level, _, own, other, *_ in jobs for v in (own, other, weights[level])]
         described, sizes = [], []
-        for level, j, _, _ in jobs:
-            begin = begins[j] - widths[0] if level == 1 and j else 0
-            described.append((bits[level], parts[j], slice(begin, begin + widths[j])))
-            sizes.append(widths[j])
+        for level, j, _, _, *lanes in jobs:
+            begin, size = lanes or (0, widths[j])
+            part = within(j, begin, size)
+            if level == 1 and j:
+                begin += begins[j] - widths[0]
+            described.append((bits[level], part, slice(begin, begin + size)))
+            sizes.append(size)
         return call(
             functools.partial(levels_kernel, described),
             name,
@@ -300,49 +318,55 @@
     (value,) = step("level2_1", [(2, 1, coeff2[1], near2[1])], [coeff3[0]])
     third(1, value)
 
-    def tail(j, after, arrived=()):
-        (coeff4,) = step(f"level3_{j}", [(3, j, coeff3[j], near3[j])], after)
-        near4 = cross(4, coeff4)
+    def tail(name, members, after, arrived=(), flops=COST, beside=COST, pieces=1):
+        size = sum(widths[j] for j in members)
+        cuts, jobs = [], []
+        for j in members:
+            lanes = widths[j] // pieces
+            for at in range(0, widths[j], lanes):
+                cuts.append((begins[j] - begins[members[0]] + at, within(j, at, lanes)))
+                jobs.append((3, j, coeff3[j], near3[j], at, lanes))
+        coeff4 = step(f"level3_{name}", jobs, after)
+        near4 = [cross(4, value) for value in coeff4]
         partial, *totals = call(
-            functools.partial(between_kernel, bits[4], parts[j], [len(group) for _, group in arrived]),
-            f"between_{j}",
-            [VMEM] * (2 + sum(len(group) for _, group in arrived)),
-            [in_vmem(rank, widths[j], dtype=F32)] + [in_vmem(rows, widths[at]) for at, _ in arrived],
+            functools.partial(between_kernel, bits[4], cuts, [len(group) for _, group in arrived]),
+            f"between_{name}",
+            [VMEM] * (1 + len(cuts) + sum(len(group) for _, group in arrived)),
+            [in_vmem(rank, size, dtype=F32)] + [in_vmem(rows, lanes) for lanes, _ in arrived],
             [],
-            [here(v) for v in (coeff4, weights[4], *(v for _, group in arrived for v in group))],
+            [here(v) for v in (weights[4], *coeff4, *(v for _, group in arrived for v in group))],
+            flops=beside,
         )
         out = call(
-            functools.partial(last_kernel, bits[4], parts[j]),
-            f"last_{j}",
-            [VMEM] * 4,
-            [in_vmem(rows, widths[j], dtype=F32)] + [in_vmem(rows, widths[j])] * (n_blk - 1),
+            functools.partial(last_kernel, bits[4], cuts),
+            f"last_{name}",
+            [VMEM] * (3 + len(cuts)),
+            [in_vmem(rows, size, dtype=F32)] + [in_vmem(rows, size)] * (n_blk - 1),
             [],
-            [here(v) for v in (partial, near4, weights[4], basis_v)],
-            flops=COST if j < len(widths) - 1 else 0,
+            [here(v) for v in (partial, weights[4], basis_v, *near4)],
+            flops=flops,
         )
         group = [out[0]] + [partner(out[d], "blk", d) for d in range(n_blk - 1, 0, -1)]
-        return group, totals
-
-    group0, _ = tail(0, [coeff3[1]])
-    (value,) = step("level2_2", [(2, 2, coeff2[2], near2[2])], [group0[0]])
+        return (size, group), totals
+
+    (value,) = step("level2_2", [(2, 2, coeff2[2], near2[2])], [coeff3[1]])
     third(2, value)
-    (total0,) = call(
-        sum_kernel,
-        "sum_0",
-        [VMEM] * n_blk,
-        [in_vmem(rows, widths[0])],
-        [],
-        [here(v) for v in group0],
-        [coeff3[2]],
-    )
-    (value,) = step("level1_3", [job1(3)], [total0])
+    (value,) = step("level1_3", [job1(3)], [coeff3[2]])
     second(3, value)
-    group1, _ = tail(1, [coeff2[3]])
-    (value,) = step("level2_3", [(2, 3, coeff2[3], near2[3])], [group1[0]])
+    group1, _ = tail("1", (0, 1), [coeff2[3]])
+    (value,) = step("level2_3", [(2, 3, coeff2[3], near2[3])], [group1[1][0]])
     third(3, value)
-    group2, (total1,) = tail(2, [coeff3[3]], [(1, group1)])
-    group3, _ = tail(3, [group2[0]])
-    groups = [[total0], [total1], group2, group3]
+    group2, (total1,) = tail("2", (2,), [coeff3[3]], [group1])
+    group3, _ = tail("3", (3,), [group2[1][0]], flops=0, beside=10**9, pieces=2)
+    places = [
+        [
+            (s, column, begins[j] - begins[members[0]] + start, begins[j] - begins[members[0]] + stop)
+            for j in members
+            for s, column, start, stop in places[j]
+        ]
+        for members in ((0, 1), (2,), (3,))
+    ]
+    groups = [[total1], group2[1], group3[1]]
     flat = [here(v) for group in groups for v in group]
     return pl.pallas_call(
         functools.partial(end_kernel, places, [len(group) for group in groups]),

time: 71 us -> 73.2 us (1.031)
  waiting for transfers between devices: 18.2 us -> 30 us
  starting transfers between devices: 36 us -> 25.9 us
    ppermute x26 -> x24, waiting for transfers between devices: 18.2 us -> 30 us  [partner(): return lax.ppermute(value, axis, pairs)]
    ppermute x26 -> x24, starting transfers between devices: 36 us -> 25.9 us  [partner(): return lax.ppermute(value, axis, pairs)]
    pallas_call x23 -> x19, Pallas kernels: 15.4 us -> 15.3 us  [call(): pl.pallas_call(body, name=name, in_specs=[*in_specs, *[ANY] * (len(after)...]
  transfers between devices with their start and end apart: 26 -> 24, of which waited for: 12 -> 11; matrix products, arithmetic and copies ran while one was open for 0% -> 0% of each run, Pallas kernels for 16% -> 16%
where the time goes in v17:
time: 73.2 us; the launch traced here: 72.4 us
  waiting for transfers between devices  30 us (41%)
  starting transfers between devices  25.9 us (35%)
  Pallas kernels  16.3 us (22%)
    ppermute x24, waiting for transfers between devices, partner(): return lax.ppermute(value, axis, pairs)  30 us
    ppermute x24, starting transfers between devices, partner(): return lax.ppermute(value, axis, pairs)  25.9 us
    pallas_call x19, Pallas kernels, call(): pl.pallas_call(body, name=name, in_specs=[*in_specs, *[ANY] * (len(after)...  15.3 us
  transfers between devices with their start and end apart: 24, of which 11 were waited for; matrix products, arithmetic and copies ran while one was open for 0% of the time, Pallas kernels for 16%

profile of v17, /device:TPU:0, one launch (start us, length us, event | category | flops | bytes accessed | tf_op | source)
XLA Modules:
  0.0 72.4 jit_solution(5314860297037355631)
XLA Ops:
  0.0 3.7 %leaf.1 = (bf16[384,128]{1,0:T(8,128)(2,1)S(1)}, bf16[384,896]{1,0:T(8,128)(2,1)S(1)}, bf16[2,384,768]{2,1,0:T(8,128)(2,1)S(1)}, bf16[2,384,768]{2,1,0:T(8,128)(2,1)S(1)}) custom-call(bf16[2,1024,512]{2,1,0:T(8,128)(2,1)} %bitcast.9, bf16[2,384,1024]{2,1,0:T(8,128)(2,1)} %bitcast.10, bf16[5,2,384,768]{3,2,1,0:T(8,128)(2,1)} %bitcast.7, s32[2,5]{1,0:T(2,128)} %bitcast.12), custom_call_target="tpu_custom_call" | custom-call | flops 6000000000 | tf_op jit(solution)/shard_map/leaf/pallas_call | solution.py:43
  3.7 0.5 collective-permute-start
  4.2 0.9 %collective-permute-done.refs_1_ = bf16[384,128]{1,0:T(8,128)(2,1)S(1)} collective-permute-done((bf16[384,128]{1,0:T(8,128)(2,1)S(1)}, bf16[384,128]{1,0:T(8,128)(2,1)S(1)}, u32[]{:S(2)}, u32[]{:S(2)}) %collective-permute-start) | collective-permute-done | bytes 98336 | tf_op jit(solution)/shard_map/ppermute | solution.py:58
  5.1 0.3 level1_0.1
  5.5 0.4 collective-permute-start.1
  5.9 2.7 %collective-permute-start.4 = (bf16[384,128]{1,0:T(8,128)(2,1)S(1)}, bf16[384,128]{1,0:T(8,128)(2,1)S(1)}, u32[]{:S(2)}, u32[]{:S(2)}) collective-permute-start(bf16[384,128]{1,0:T(8,128)(2,1)S(1)} %get-tuple-element.36.refs_3_.refs_0_), channel_id=1, source_target_pairs={{0,2},{1,3},{2,0},{3,1},{4,6},{5,7},{6,4},{7,5},{8,10},{9,11},{10,... | collective-permute-start | bytes 294920 | tf_op jit(solution)/shard_map/ppermute | solution.py:58
  8.6 0.4 level1_1.1.refs_3_.refs_0_
  9.0 2.1 %collective-permute-start.3 = (bf16[384,256]{1,0:T(8,128)(2,1)S(1)}, bf16[384,256]{1,0:T(8,128)(2,1)S(1)}, u32[]{:S(2)}, u32[]{:S(2)}) collective-permute-start(bf16[384,256]{1,0:T(8,128)(2,1)S(1)} %level1_1.1.refs_3_.refs_0_), channel_id=1, source_target_pairs={{0,2},{1,3},{2,0},{3,1},{4,6},{5,7},{6,4},{7,5},{8,10},{9,11},{10,... | collective-permute-start | bytes 589832 | tf_op jit(solution)/shard_map/ppermute | solution.py:58
  11.0 0.5 level1_2.1.refs_3_.refs_0_
  11.7 2.5 %prefetch.1 = (bf16[2,384,768]{2,1,0:T(8,128)(2,1)S(1)}, bf16[2,384,768]{2,1,0:T(8,128)(2,1)S(1)}, bf16[2,1024,384]{2,1,0:T(8,128)(2,1)S(1)}) custom-call(bf16[5,2,384,768]{3,2,1,0:T(8,128)(2,1)} %bitcast.8, bf16[2,1024,384]{2,1,0:T(8,128)(2,1)} %bitcast.11, s32[2,5]{1,0:T(2,128)} %bitcast.13, bf16[384,384]{1,0:T(8,128)(2,1)S(1)} %level1_2.1.refs_3_.refs_0_), custom_call_target="tpu_custom_call" | custom-call | flops 6000000000 | tf_op jit(solution)/shard_map/prefetch/pallas_call | solution.py:43
  14.2 0.3 level2_0.1.refs_3_.refs_0_
  14.5 3.1 %collective-permute-start.7 = (bf16[384,128]{1,0:T(8,128)(2,1)S(1)}, bf16[384,128]{1,0:T(8,128)(2,1)S(1)}, u32[]{:S(2)}, u32[]{:S(2)}) collective-permute-start(bf16[384,128]{1,0:T(8,128)(2,1)S(1)} %level2_0.1.refs_3_.refs_0_), channel_id=1, source_target_pairs={{0,4},{1,5},{2,6},{3,7},{4,0},{5,1},{6,2},{7,3},{8,12},{9,13},{10,... | collective-permute-start | bytes 294920 | tf_op jit(solution)/shard_map/ppermute | solution.py:58
  17.6 0.4 level2_1.1.refs_3_
  18.0 2.3 %collective-permute-start.8 = (bf16[384,256]{1,0:T(8,128)(2,1)S(1)}, bf16[384,256]{1,0:T(8,128)(2,1)S(1)}, u32[]{:S(2)}, u32[]{:S(2)}) collective-permute-start(bf16[384,256]{1,0:T(8,128)(2,1)S(1)} %level2_1.1.refs_3_), channel_id=1, source_target_pairs={{0,4},{1,5},{2,6},{3,7},{4,0},{5,1},{6,2},{7,3},{8,12},{9,13},{10,... | collective-permute-start | bytes 589832 | tf_op jit(solution)/shard_map/ppermute | solution.py:58
  20.2 8.4 %collective-permute-done.2.refs_1_ = bf16[384,384]{1,0:T(8,128)(2,1)S(1)} collective-permute-done((bf16[384,384]{1,0:T(8,128)(2,1)S(1)}, bf16[384,384]{1,0:T(8,128)(2,1)S(1)}, u32[]{:S(2)}, u32[]{:S(2)}) %collective-permute-start.2) | collective-permute-done | bytes 294944 | tf_op jit(solution)/shard_map/ppermute | solution.py:58
  28.7 0.5 level2_2.1.refs_3_.refs_0_
  29.3 0.4 level1_3.1.refs_6_.refs_0_
  29.6 2.5 %collective-permute-start.6 = (bf16[384,256]{1,0:T(8,128)(2,1)S(1)}, bf16[384,256]{1,0:T(8,128)(2,1)S(1)}, u32[]{:S(2)}, u32[]{:S(2)}) collective-permute-start(bf16[384,256]{1,0:T(8,128)(2,1)S(1)} %level1_3.1.refs_6_.refs_0_), channel_id=1, source_target_pairs={{0,2},{1,3},{2,0},{3,1},{4,6},{5,7},{6,4},{7,5},{8,10},{9,11},{10,... | collective-permute-start | bytes 589832 | tf_op jit(solution)/shard_map/ppermute | solution.py:58
  32.1 4.4 %collective-permute-done.8.refs_4_ = bf16[384,256]{1,0:T(8,128)(2,1)S(1)} collective-permute-done((bf16[384,256]{1,0:T(8,128)(2,1)S(1)}, bf16[384,256]{1,0:T(8,128)(2,1)S(1)}, u32[]{:S(2)}, u32[]{:S(2)}) %collective-permute-start.8) | collective-permute-done | bytes 196640 | tf_op jit(solution)/shard_map/ppermute | solution.py:58
  36.5 0.5 level3_1.1
  37.1 0.5 collective-permute-start.9
  37.6 0.3 between_1.1.refs_0_
  37.9 0.7 %collective-permute-done.9.refs_3_ = bf16[384,128]{1,0:T(8,128)(2,1)S(1)} collective-permute-done((bf16[384,128]{1,0:T(8,128)(2,1)S(1)}, bf16[384,128]{1,0:T(8,128)(2,1)S(1)}, u32[]{:S(2)}, u32[]{:S(2)}) %collective-permute-start.9) | collective-permute-done | bytes 98336 | tf_op jit(solution)/shard_map/ppermute | solution.py:58
  38.7 1.2 %last_1.1 = (f32[256,384]{1,0:T(8,128)S(1)}, bf16[256,384]{1,0:T(8,128)(2,1)S(1)}, bf16[256,384]{1,0:T(8,128)(2,1)S(1)}, bf16[256,384]{1,0:T(8,128)(2,1)S(1)}) custom-call(f32[384,384]{1,0:T(8,128)S(1)} %between_1.1.refs_0_, bf16[2,384,768]{2,1,0:T(8,128)(2,1)S(1)} %get-tuple-element.37.refs_0_.refs_1_, ...), custom_call_target="tpu_custom_call" | custom-call | flops 6000000000 | tf_op jit(solution)/shard_map/last_1/pallas_call | solution.py:43
  39.9 2.0 %collective-permute-start.11 = (bf16[256,384]{1,0:T(8,128)(2,1)S(1)}, bf16[256,384]{1,0:T(8,128)(2,1)S(1)}, u32[]{:S(2)}, u32[]{:S(2)}) collective-permute-start(bf16[256,384]{1,0:T(8,128)(2,1)S(1)} %get-tuple-element.44), channel_id=1, source_target_pairs={{0,24},{8,16},{16,8},{24,0},{1,25},{9,17},{17,9},{25,1},{2,26},{10... | collective-permute-start | bytes 589832 | tf_op jit(solution)/shard_map/ppermute | solution.py:58
  42.0 0.5 collective-permute-start.12
  42.5 1.0 %collective-permute-start.13 = (bf16[256,384]{1,0:T(8,128)(2,1)S(1)}, bf16[256,384]{1,0:T(8,128)(2,1)S(1)}, u32[]{:S(2)}, u32[]{:S(2)}) collective-permute-start(bf16[256,384]{1,0:T(8,128)(2,1)S(1)} %get-tuple-element.46), channel_id=1, source_target_pairs={{0,8},{8,0},{16,24},{24,16},{1,9},{9,1},{17,25},{25,17},{2,10},{10... | collective-permute-start | bytes 589832 | tf_op jit(solution)/shard_map/ppermute | solution.py:58
  43.5 0.4 level2_3.1.refs_3_.refs_0_
  43.9 0.1 collective-permute-done.5.refs_1_
  44.1 0.5 level3_2.1.refs_1_
  44.7 3.9 %collective-permute-done.11.refs_3_ = bf16[256,384]{1,0:T(8,128)(2,1)S(1)} collective-permute-done((bf16[256,384]{1,0:T(8,128)(2,1)S(1)}, bf16[256,384]{1,0:T(8,128)(2,1)S(1)}, u32[]{:S(2)}, u32[]{:S(2)}) %collective-permute-start.11) | collective-permute-done | bytes 196640 | tf_op jit(solution)/shard_map/ppermute | solution.py:58
  48.7 3.5 %collective-permute-done.12.refs_4_ = bf16[256,384]{1,0:T(8,128)(2,1)S(1)} collective-permute-done((bf16[256,384]{1,0:T(8,128)(2,1)S(1)}, bf16[256,384]{1,0:T(8,128)(2,1)S(1)}, u32[]{:S(2)}, u32[]{:S(2)}) %collective-permute-start.12) | collective-permute-done | bytes 196640 | tf_op jit(solution)/shard_map/ppermute | solution.py:58
  52.1 0.4 between_2.1
  52.6 1.2 %last_2.1 = (f32[256,384]{1,0:T(8,128)S(1)}, bf16[256,384]{1,0:T(8,128)(2,1)S(1)}, bf16[256,384]{1,0:T(8,128)(2,1)S(1)}, bf16[256,384]{1,0:T(8,128)(2,1)S(1)}) custom-call(f32[384,384]{1,0:T(8,128)S(1)} %get-tuple-element.48.refs_0_, bf16[2,384,768]{2,1,0:T(8,128)(2,1)S(1)} %get-tuple-element.37.refs_0_.refs_1_, ...), custom_call_target="tpu_custom_call" | custom-call | flops 6000000000 | tf_op jit(solution)/shard_map/last_2/pallas_call | solution.py:43
  53.8 1.8 %collective-permute-start.15 = (bf16[256,384]{1,0:T(8,128)(2,1)S(1)}, bf16[256,384]{1,0:T(8,128)(2,1)S(1)}, u32[]{:S(2)}, u32[]{:S(2)}) collective-permute-start(bf16[256,384]{1,0:T(8,128)(2,1)S(1)} %get-tuple-element.50), channel_id=1, source_target_pairs={{0,24},{8,16},{16,8},{24,0},{1,25},{9,17},{17,9},{25,1},{2,26},{10... | collective-permute-start | bytes 589832 | tf_op jit(solution)/shard_map/ppermute | solution.py:58
  55.7 0.5 level3_3.1
  56.2 0.5 collective-permute-start.20
  56.7 0.8 %collective-permute-start.16 = (bf16[256,384]{1,0:T(8,128)(2,1)S(1)}, bf16[256,384]{1,0:T(8,128)(2,1)S(1)}, u32[]{:S(2)}, u32[]{:S(2)}) collective-permute-start(bf16[256,384]{1,0:T(8,128)(2,1)S(1)} %get-tuple-element.51), channel_id=1, source_target_pairs={{0,16},{8,24},{16,0},{24,8},{1,17},{9,25},{17,1},{25,9},{2,18},{10... | collective-permute-start | bytes 589832 | tf_op jit(solution)/shard_map/ppermute | solution.py:58
  57.6 1.3 %collective-permute-start.17 = (bf16[256,384]{1,0:T(8,128)(2,1)S(1)}, bf16[256,384]{1,0:T(8,128)(2,1)S(1)}, u32[]{:S(2)}, u32[]{:S(2)}) collective-permute-start(bf16[256,384]{1,0:T(8,128)(2,1)S(1)} %get-tuple-element.52), channel_id=1, source_target_pairs={{0,8},{8,0},{16,24},{24,16},{1,9},{9,1},{17,25},{25,17},{2,10},{10... | collective-permute-start | bytes 589832 | tf_op jit(solution)/shard_map/ppermute | solution.py:58
  58.8 0.3 between_3.1.refs_0_
  59.2 1.0 %last_3.1 = (f32[256,256]{1,0:T(8,128)S(1)}, bf16[256,256]{1,0:T(8,128)(2,1)S(1)}, bf16[256,256]{1,0:T(8,128)(2,1)S(1)}, bf16[256,256]{1,0:T(8,128)(2,1)S(1)}) custom-call(f32[384,256]{1,0:T(8,128)S(1)} %between_3.1.refs_0_, bf16[2,384,768]{2,1,0:T(8,128)(2,1)S(1)} %get-tuple-element.37.refs_0_.refs_1_, ...), custom_call_target="tpu_custom_call" | custom-call | tf_op jit(solution)/shard_map/last_3/pallas_call | solution.py:43
  60.1 1.5 %collective-permute-start.21 = (bf16[256,256]{1,0:T(8,128)(2,1)S(1)}, bf16[256,256]{1,0:T(8,128)(2,1)S(1)}, u32[]{:S(2)}, u32[]{:S(2)}) collective-permute-start(bf16[256,256]{1,0:T(8,128)(2,1)S(1)} %get-tuple-element.56), channel_id=1, source_target_pairs={{0,24},{8,16},{16,8},{24,0},{1,25},{9,17},{17,9},{25,1},{2,26},{10... | collective-permute-start | bytes 393224 | tf_op jit(solution)/shard_map/ppermute | solution.py:58
  61.6 0.8 %collective-permute-start.22 = (bf16[256,256]{1,0:T(8,128)(2,1)S(1)}, bf16[256,256]{1,0:T(8,128)(2,1)S(1)}, u32[]{:S(2)}, u32[]{:S(2)}) collective-permute-start(bf16[256,256]{1,0:T(8,128)(2,1)S(1)} %get-tuple-element.57), channel_id=1, source_target_pairs={{0,16},{8,24},{16,0},{24,8},{1,17},{9,25},{17,1},{25,9},{2,18},{10... | collective-permute-start | bytes 393224 | tf_op jit(solution)/shard_map/ppermute | solution.py:58
  62.6 1.1 %collective-permute-start.23 = (bf16[256,256]{1,0:T(8,128)(2,1)S(1)}, bf16[256,256]{1,0:T(8,128)(2,1)S(1)}, u32[]{:S(2)}, u32[]{:S(2)}) collective-permute-start(bf16[256,256]{1,0:T(8,128)(2,1)S(1)} %get-tuple-element.58), channel_id=1, source_target_pairs={{0,8},{8,0},{16,24},{24,16},{1,9},{9,1},{17,25},{25,17},{2,10},{10... | collective-permute-start | bytes 393224 | tf_op jit(solution)/shard_map/ppermute | solution.py:58
  63.7 3.2 %collective-permute-done.16.refs_3_ = bf16[256,384]{1,0:T(8,128)(2,1)S(1)} collective-permute-done((bf16[256,384]{1,0:T(8,128)(2,1)S(1)}, bf16[256,384]{1,0:T(8,128)(2,1)S(1)}, u32[]{:S(2)}, u32[]{:S(2)}) %collective-permute-start.16) | collective-permute-done | bytes 196640 | tf_op jit(solution)/shard_map/ppermute | solution.py:58
  66.9 2.7 %collective-permute-done.21.refs_6_ = bf16[256,256]{1,0:T(8,128)(2,1)S(1)} collective-permute-done((bf16[256,256]{1,0:T(8,128)(2,1)S(1)}, bf16[256,256]{1,0:T(8,128)(2,1)S(1)}, u32[]{:S(2)}, u32[]{:S(2)}) %collective-permute-start.21) | collective-permute-done | bytes 131104 | tf_op jit(solution)/shard_map/ppermute | solution.py:58
  69.6 1.9 %collective-permute-done.22.refs_7_ = bf16[256,256]{1,0:T(8,128)(2,1)S(1)} collective-permute-done((bf16[256,256]{1,0:T(8,128)(2,1)S(1)}, bf16[256,256]{1,0:T(8,128)(2,1)S(1)}, u32[]{:S(2)}, u32[]{:S(2)}) %collective-permute-start.22) | collective-permute-done | bytes 131104 | tf_op jit(solution)/shard_map/ppermute | solution.py:58
  71.5 1.0 %end.1 = bf16[2,256,512]{2,1,0:T(8,128)(2,1)} custom-call(bf16[256,384]{1,0:T(8,128)(2,1)S(1)} %get-tuple-element.47.refs_0_, f32[256,384]{1,0:T(8,128)S(1)} %get-tuple-element.49.refs_6_.refs_1_, bf16[256,384]{1,0:T(8,128)(2,1)S(1)} %collective-permute-done.15.refs_2_, bf16[256,384]{1,0:T(8,128)(2,1)S(1)} %collective-permute-done.16.refs_3_, ...), custom_call_target="tpu_custom_call" | custom-call | tf_op jit(solution)/shard_map/end/pallas_call | solution.py:371
  (20 shorter events, 0.7 us)
Async XLA Ops:
  3.7 1.5 %collective-permute-start = (bf16[384,128]{1,0:T(8,128)(2,1)S(1)}, bf16[384,128]{1,0:T(8,128)(2,1)S(1)}, u32[]{:S(2)}, u32[]{:S(2)}) collective-permute-start(bf16[384,128]{1,0:T(8,128)(2,1)S(1)} %get-tuple-element.32.refs_0_), channel_id=1, source_target_pairs={{0,1},{1,0},{2,3},{3,2},{4,5},{5,4},{6,7},{7,6},{8,9},{9,8},{10,11... | collective-permute-start | bytes 294920 | tf_op jit(solution)/shard_map/ppermute | solution.py:58
  5.5 3.1 %collective-permute-start.1 = (bf16[384,896]{1,0:T(8,128)(2,1)S(1)}, bf16[384,896]{1,0:T(8,128)(2,1)S(1)}, u32[]{:S(2)}, u32[]{:S(2)}) collective-permute-start(bf16[384,896]{1,0:T(8,128)(2,1)S(1)} %get-tuple-element.35.refs_0_), channel_id=1, source_target_pairs={{0,1},{1,0},{2,3},{3,2},{4,5},{5,4},{6,7},{7,6},{8,9},{9,8},{10,11... | collective-permute-start | bytes 2064392 | tf_op jit(solution)/shard_map/ppermute | solution.py:58
  5.9 8.3 %collective-permute-start.4 = (bf16[384,128]{1,0:T(8,128)(2,1)S(1)}, bf16[384,128]{1,0:T(8,128)(2,1)S(1)}, u32[]{:S(2)}, u32[]{:S(2)}) collective-permute-start(bf16[384,128]{1,0:T(8,128)(2,1)S(1)} %get-tuple-element.36.refs_3_.refs_0_), channel_id=1, source_target_pairs={{0,2},{1,3},{2,0},{3,1},{4,6},{5,7},{6,4},{7,5},{8,10},{9,11},{10,... | collective-permute-start | bytes 294920 | tf_op jit(solution)/shard_map/ppermute | solution.py:58
  9.0 8.6 %collective-permute-start.3 = (bf16[384,256]{1,0:T(8,128)(2,1)S(1)}, bf16[384,256]{1,0:T(8,128)(2,1)S(1)}, u32[]{:S(2)}, u32[]{:S(2)}) collective-permute-start(bf16[384,256]{1,0:T(8,128)(2,1)S(1)} %level1_1.1.refs_3_.refs_0_), channel_id=1, source_target_pairs={{0,2},{1,3},{2,0},{3,1},{4,6},{5,7},{6,4},{7,5},{8,10},{9,11},{10,... | collective-permute-start | bytes 589832 | tf_op jit(solution)/shard_map/ppermute | solution.py:58
  11.6 17.1 %collective-permute-start.2 = (bf16[384,384]{1,0:T(8,128)(2,1)S(1)}, bf16[384,384]{1,0:T(8,128)(2,1)S(1)}, u32[]{:S(2)}, u32[]{:S(2)}) collective-permute-start(bf16[384,384]{1,0:T(8,128)(2,1)S(1)} %level1_2.1.refs_3_.refs_0_), channel_id=1, source_target_pairs={{0,2},{1,3},{2,0},{3,1},{4,6},{5,7},{6,4},{7,5},{8,10},{9,11},{10,... | collective-permute-start | bytes 884744 | tf_op jit(solution)/shard_map/ppermute | solution.py:58
  14.5 17.6 %collective-permute-start.7 = (bf16[384,128]{1,0:T(8,128)(2,1)S(1)}, bf16[384,128]{1,0:T(8,128)(2,1)S(1)}, u32[]{:S(2)}, u32[]{:S(2)}) collective-permute-start(bf16[384,128]{1,0:T(8,128)(2,1)S(1)} %level2_0.1.refs_3_.refs_0_), channel_id=1, source_target_pairs={{0,4},{1,5},{2,6},{3,7},{4,0},{5,1},{6,2},{7,3},{8,12},{9,13},{10,... | collective-permute-start | bytes 294920 | tf_op jit(solution)/shard_map/ppermute | solution.py:58
  18.0 18.6 %collective-permute-start.8 = (bf16[384,256]{1,0:T(8,128)(2,1)S(1)}, bf16[384,256]{1,0:T(8,128)(2,1)S(1)}, u32[]{:S(2)}, u32[]{:S(2)}) collective-permute-start(bf16[384,256]{1,0:T(8,128)(2,1)S(1)} %level2_1.1.refs_3_), channel_id=1, source_target_pairs={{0,4},{1,5},{2,6},{3,7},{4,0},{5,1},{6,2},{7,3},{8,12},{9,13},{10,... | collective-permute-start | bytes 589832 | tf_op jit(solution)/shard_map/ppermute | solution.py:58
  29.2 14.9 %collective-permute-start.5 = (bf16[384,384]{1,0:T(8,128)(2,1)S(1)}, bf16[384,384]{1,0:T(8,128)(2,1)S(1)}, u32[]{:S(2)}, u32[]{:S(2)}) collective-permute-start(bf16[384,384]{1,0:T(8,128)(2,1)S(1)} %level2_2.1.refs_3_.refs_0_), channel_id=1, source_target_pairs={{0,4},{1,5},{2,6},{3,7},{4,0},{5,1},{6,2},{7,3},{8,12},{9,13},{10,... | collective-permute-start | bytes 884744 | tf_op jit(solution)/shard_map/ppermute | solution.py:58
  29.6 13.9 %collective-permute-start.6 = (bf16[384,256]{1,0:T(8,128)(2,1)S(1)}, bf16[384,256]{1,0:T(8,128)(2,1)S(1)}, u32[]{:S(2)}, u32[]{:S(2)}) collective-permute-start(bf16[384,256]{1,0:T(8,128)(2,1)S(1)} %level1_3.1.refs_6_.refs_0_), channel_id=1, source_target_pairs={{0,2},{1,3},{2,0},{3,1},{4,6},{5,7},{6,4},{7,5},{8,10},{9,11},{10,... | collective-permute-start | bytes 589832 | tf_op jit(solution)/shard_map/ppermute | solution.py:58
  37.0 1.7 %collective-permute-start.10 = (bf16[384,256]{1,0:T(8,128)(2,1)S(1)}, bf16[384,256]{1,0:T(8,128)(2,1)S(1)}, u32[]{:S(2)}, u32[]{:S(2)}) collective-permute-start(bf16[384,256]{1,0:T(8,128)(2,1)S(1)} %get-tuple-element.42.refs_2_), channel_id=1, source_target_pairs={{0,1},{1,0},{2,3},{3,2},{4,5},{5,4},{6,7},{7,6},{8,9},{9,8},{10,11... | collective-permute-start | bytes 589832 | tf_op jit(solution)/shard_map/ppermute | solution.py:58
  37.1 1.6 %collective-permute-start.9 = (bf16[384,128]{1,0:T(8,128)(2,1)S(1)}, bf16[384,128]{1,0:T(8,128)(2,1)S(1)}, u32[]{:S(2)}, u32[]{:S(2)}) collective-permute-start(bf16[384,128]{1,0:T(8,128)(2,1)S(1)} %get-tuple-element.41.refs_1_), channel_id=1, source_target_pairs={{0,1},{1,0},{2,3},{3,2},{4,5},{5,4},{6,7},{7,6},{8,9},{9,8},{10,11... | collective-permute-start | bytes 294920 | tf_op jit(solution)/shard_map/ppermute | solution.py:58
  39.9 8.7 %collective-permute-start.11 = (bf16[256,384]{1,0:T(8,128)(2,1)S(1)}, bf16[256,384]{1,0:T(8,128)(2,1)S(1)}, u32[]{:S(2)}, u32[]{:S(2)}) collective-permute-start(bf16[256,384]{1,0:T(8,128)(2,1)S(1)} %get-tuple-element.44), channel_id=1, source_target_pairs={{0,24},{8,16},{16,8},{24,0},{1,25},{9,17},{17,9},{25,1},{2,26},{10... | collective-permute-start | bytes 589832 | tf_op jit(solution)/shard_map/ppermute | solution.py:58
  42.0 10.2 %collective-permute-start.12 = (bf16[256,384]{1,0:T(8,128)(2,1)S(1)}, bf16[256,384]{1,0:T(8,128)(2,1)S(1)}, u32[]{:S(2)}, u32[]{:S(2)}) collective-permute-start(bf16[256,384]{1,0:T(8,128)(2,1)S(1)} %get-tuple-element.45), channel_id=1, source_target_pairs={{0,16},{8,24},{16,0},{24,8},{1,17},{9,25},{17,1},{25,9},{2,18},{10... | collective-permute-start | bytes 589832 | tf_op jit(solution)/shard_map/ppermute | solution.py:58
  42.5 9.7 %collective-permute-start.13 = (bf16[256,384]{1,0:T(8,128)(2,1)S(1)}, bf16[256,384]{1,0:T(8,128)(2,1)S(1)}, u32[]{:S(2)}, u32[]{:S(2)}) collective-permute-start(bf16[256,384]{1,0:T(8,128)(2,1)S(1)} %get-tuple-element.46), channel_id=1, source_target_pairs={{0,8},{8,0},{16,24},{24,16},{1,9},{9,1},{17,25},{25,17},{2,10},{10... | collective-permute-start | bytes 589832 | tf_op jit(solution)/shard_map/ppermute | solution.py:58
  43.9 11.8 %collective-permute-start.18 = (bf16[384,256]{1,0:T(8,128)(2,1)S(1)}, bf16[384,256]{1,0:T(8,128)(2,1)S(1)}, u32[]{:S(2)}, u32[]{:S(2)}) collective-permute-start(bf16[384,256]{1,0:T(8,128)(2,1)S(1)} %level2_3.1.refs_3_.refs_0_), channel_id=1, source_target_pairs={{0,4},{1,5},{2,6},{3,7},{4,0},{5,1},{6,2},{7,3},{8,12},{9,13},{10,... | collective-permute-start | bytes 589832 | tf_op jit(solution)/shard_map/ppermute | solution.py:58
  44.6 8.0 %collective-permute-start.14 = (bf16[384,384]{1,0:T(8,128)(2,1)S(1)}, bf16[384,384]{1,0:T(8,128)(2,1)S(1)}, u32[]{:S(2)}, u32[]{:S(2)}) collective-permute-start(bf16[384,384]{1,0:T(8,128)(2,1)S(1)} %level3_2.1.refs_1_), channel_id=1, source_target_pairs={{0,1},{1,0},{2,3},{3,2},{4,5},{5,4},{6,7},{7,6},{8,9},{9,8},{10,11... | collective-permute-start | bytes 884744 | tf_op jit(solution)/shard_map/ppermute | solution.py:58
  53.8 8.7 %collective-permute-start.15 = (bf16[256,384]{1,0:T(8,128)(2,1)S(1)}, bf16[256,384]{1,0:T(8,128)(2,1)S(1)}, u32[]{:S(2)}, u32[]{:S(2)}) collective-permute-start(bf16[256,384]{1,0:T(8,128)(2,1)S(1)} %get-tuple-element.50), channel_id=1, source_target_pairs={{0,24},{8,16},{16,8},{24,0},{1,25},{9,17},{17,9},{25,1},{2,26},{10... | collective-permute-start | bytes 589832 | tf_op jit(solution)/shard_map/ppermute | solution.py:58
  56.2 3.0 %collective-permute-start.19 = (bf16[384,128]{1,0:T(8,128)(2,1)S(1)}, bf16[384,128]{1,0:T(8,128)(2,1)S(1)}, u32[]{:S(2)}, u32[]{:S(2)}) collective-permute-start(bf16[384,128]{1,0:T(8,128)(2,1)S(1)} %get-tuple-element.53.refs_1_), channel_id=1, source_target_pairs={{0,1},{1,0},{2,3},{3,2},{4,5},{5,4},{6,7},{7,6},{8,9},{9,8},{10,11... | collective-permute-start | bytes 294920 | tf_op jit(solution)/shard_map/ppermute | solution.py:58
  56.2 2.9 %collective-permute-start.20 = (bf16[384,128]{1,0:T(8,128)(2,1)S(1)}, bf16[384,128]{1,0:T(8,128)(2,1)S(1)}, u32[]{:S(2)}, u32[]{:S(2)}) collective-permute-start(bf16[384,128]{1,0:T(8,128)(2,1)S(1)} %get-tuple-element.54.refs_2_), channel_id=1, source_target_pairs={{0,1},{1,0},{2,3},{3,2},{4,5},{5,4},{6,7},{7,6},{8,9},{9,8},{10,11... | collective-permute-start | bytes 294920 | tf_op jit(solution)/shard_map/ppermute | solution.py:58
  56.7 10.1 %collective-permute-start.16 = (bf16[256,384]{1,0:T(8,128)(2,1)S(1)}, bf16[256,384]{1,0:T(8,128)(2,1)S(1)}, u32[]{:S(2)}, u32[]{:S(2)}) collective-permute-start(bf16[256,384]{1,0:T(8,128)(2,1)S(1)} %get-tuple-element.51), channel_id=1, source_target_pairs={{0,16},{8,24},{16,0},{24,8},{1,17},{9,25},{17,1},{25,9},{2,18},{10... | collective-permute-start | bytes 589832 | tf_op jit(solution)/shard_map/ppermute | solution.py:58
  57.6 9.3 %collective-permute-start.17 = (bf16[256,384]{1,0:T(8,128)(2,1)S(1)}, bf16[256,384]{1,0:T(8,128)(2,1)S(1)}, u32[]{:S(2)}, u32[]{:S(2)}) collective-permute-start(bf16[256,384]{1,0:T(8,128)(2,1)S(1)} %get-tuple-element.52), channel_id=1, source_target_pairs={{0,8},{8,0},{16,24},{24,16},{1,9},{9,1},{17,25},{25,17},{2,10},{10... | collective-permute-start | bytes 589832 | tf_op jit(solution)/shard_map/ppermute | solution.py:58
  60.1 9.5 %collective-permute-start.21 = (bf16[256,256]{1,0:T(8,128)(2,1)S(1)}, bf16[256,256]{1,0:T(8,128)(2,1)S(1)}, u32[]{:S(2)}, u32[]{:S(2)}) collective-permute-start(bf16[256,256]{1,0:T(8,128)(2,1)S(1)} %get-tuple-element.56), channel_id=1, source_target_pairs={{0,24},{8,16},{16,8},{24,0},{1,25},{9,17},{17,9},{25,1},{2,26},{10... | collective-permute-start | bytes 393224 | tf_op jit(solution)/shard_map/ppermute | solution.py:58
  61.6 9.8 %collective-permute-start.22 = (bf16[256,256]{1,0:T(8,128)(2,1)S(1)}, bf16[256,256]{1,0:T(8,128)(2,1)S(1)}, u32[]{:S(2)}, u32[]{:S(2)}) collective-permute-start(bf16[256,256]{1,0:T(8,128)(2,1)S(1)} %get-tuple-element.57), channel_id=1, source_target_pairs={{0,16},{8,24},{16,0},{24,8},{1,17},{9,25},{17,1},{25,9},{2,18},{10... | collective-permute-start | bytes 393224 | tf_op jit(solution)/shard_map/ppermute | solution.py:58
  62.6 8.9 %collective-permute-start.23 = (bf16[256,256]{1,0:T(8,128)(2,1)S(1)}, bf16[256,256]{1,0:T(8,128)(2,1)S(1)}, u32[]{:S(2)}, u32[]{:S(2)}) collective-permute-start(bf16[256,256]{1,0:T(8,128)(2,1)S(1)} %get-tuple-element.58), channel_id=1, source_target_pairs={{0,8},{8,0},{16,24},{24,16},{1,9},{9,1},{17,25},{25,17},{2,10},{10... | collective-permute-start | bytes 393224 | tf_op jit(solution)/shard_map/ppermute | solution.py:58

commit v18 on v17

--- a/solution.py
+++ b/solution.py
@@ -349,11 +349,11 @@
         group = [out[0]] + [partner(out[d], "blk", d) for d in range(n_blk - 1, 0, -1)]
         return (size, group), totals
 
-    (value,) = step("level2_2", [(2, 2, coeff2[2], near2[2])], [coeff3[1]])
+    (value,) = step("level1_3", [job1(3)], [coeff3[1], near2[2]])
+    second(3, value)
+    (value,) = step("level2_2", [(2, 2, coeff2[2], near2[2])], [coeff2[3]])
     third(2, value)
-    (value,) = step("level1_3", [job1(3)], [coeff3[2]])
-    second(3, value)
-    group1, _ = tail("1", (0, 1), [coeff2[3]])
+    group1, _ = tail("1", (0, 1), [coeff3[2]])
     (value,) = step("level2_3", [(2, 3, coeff2[3], near2[3])], [group1[1][0]])
     third(3, value)
     group2, (total1,) = tail("2", (2,), [coeff3[3]], [group1])

time: 73.2 us -> 73.5 us (level)
  starting transfers between devices: 25.9 us -> 27.3 us
    ppermute x24, starting transfers between devices: 25.9 us -> 27.3 us  [partner(): return lax.ppermute(value, axis, pairs)]
  transfers between devices with their start and end apart: 24 -> 24, of which waited for: 11 -> 10; matrix products, arithmetic and copies ran while one was open for 0% -> 0% of each run, Pallas kernels for 16% -> 15%
where the time goes in v18:
time: 73.5 us; the launch traced here: 73.3 us
  waiting for transfers between devices  29.6 us (40%)
  starting transfers between devices  27.3 us (37%)
  Pallas kernels  16.3 us (22%)
    ppermute x24, waiting for transfers between devices, partner(): return lax.ppermute(value, axis, pairs)  29.6 us
    ppermute x24, starting transfers between devices, partner(): return lax.ppermute(value, axis, pairs)  27.3 us
    pallas_call x19, Pallas kernels, call(): pl.pallas_call(body, name=name, in_specs=[*in_specs, *[ANY] * (len(after)...  15.3 us
  transfers between devices with their start and end apart: 24, of which 10 were waited for; matrix products, arithmetic and copies ran while one was open for 0% of the time, Pallas kernels for 15%

profile of v18, /device:TPU:0, one launch (start us, length us, event | category | flops | bytes accessed | tf_op | source)
XLA Modules:
  0.0 73.3 jit_solution(8550760673031327622)
XLA Ops:
  0.0 3.7 %leaf.1 = (bf16[384,128]{1,0:T(8,128)(2,1)S(1)}, bf16[384,896]{1,0:T(8,128)(2,1)S(1)}, bf16[2,384,768]{2,1,0:T(8,128)(2,1)S(1)}, bf16[2,384,768]{2,1,0:T(8,128)(2,1)S(1)}) custom-call(bf16[2,1024,512]{2,1,0:T(8,128)(2,1)} %bitcast.9, bf16[2,384,1024]{2,1,0:T(8,128)(2,1)} %bitcast.10, bf16[5,2,384,768]{3,2,1,0:T(8,128)(2,1)} %bitcast.7, s32[2,5]{1,0:T(2,128)} %bitcast.12), custom_call_target="tpu_custom_call" | custom-call | flops 6000000000 | tf_op jit(solution)/shard_map/leaf/pallas_call | solution.py:43
  3.7 0.5 collective-permute-start
  4.2 0.9 %collective-permute-done.refs_1_ = bf16[384,128]{1,0:T(8,128)(2,1)S(1)} collective-permute-done((bf16[384,128]{1,0:T(8,128)(2,1)S(1)}, bf16[384,128]{1,0:T(8,128)(2,1)S(1)}, u32[]{:S(2)}, u32[]{:S(2)}) %collective-permute-start) | collective-permute-done | bytes 98336 | tf_op jit(solution)/shard_map/ppermute | solution.py:58
  5.1 0.3 level1_0.1
  5.5 0.4 collective-permute-start.1
  5.9 2.7 %collective-permute-start.4 = (bf16[384,128]{1,0:T(8,128)(2,1)S(1)}, bf16[384,128]{1,0:T(8,128)(2,1)S(1)}, u32[]{:S(2)}, u32[]{:S(2)}) collective-permute-start(bf16[384,128]{1,0:T(8,128)(2,1)S(1)} %get-tuple-element.36.refs_3_.refs_0_), channel_id=1, source_target_pairs={{0,2},{1,3},{2,0},{3,1},{4,6},{5,7},{6,4},{7,5},{8,10},{9,11},{10,... | collective-permute-start | bytes 294920 | tf_op jit(solution)/shard_map/ppermute | solution.py:58
  8.6 0.4 level1_1.1.refs_3_.refs_0_
  9.0 2.1 %collective-permute-start.3 = (bf16[384,256]{1,0:T(8,128)(2,1)S(1)}, bf16[384,256]{1,0:T(8,128)(2,1)S(1)}, u32[]{:S(2)}, u32[]{:S(2)}) collective-permute-start(bf16[384,256]{1,0:T(8,128)(2,1)S(1)} %level1_1.1.refs_3_.refs_0_), channel_id=1, source_target_pairs={{0,2},{1,3},{2,0},{3,1},{4,6},{5,7},{6,4},{7,5},{8,10},{9,11},{10,... | collective-permute-start | bytes 589832 | tf_op jit(solution)/shard_map/ppermute | solution.py:58
  11.0 0.5 level1_2.1.refs_3_.refs_0_
  11.7 2.5 %prefetch.1 = (bf16[2,384,768]{2,1,0:T(8,128)(2,1)S(1)}, bf16[2,384,768]{2,1,0:T(8,128)(2,1)S(1)}, bf16[2,1024,384]{2,1,0:T(8,128)(2,1)S(1)}) custom-call(bf16[5,2,384,768]{3,2,1,0:T(8,128)(2,1)} %bitcast.8, bf16[2,1024,384]{2,1,0:T(8,128)(2,1)} %bitcast.11, s32[2,5]{1,0:T(2,128)} %bitcast.13, bf16[384,384]{1,0:T(8,128)(2,1)S(1)} %level1_2.1.refs_3_.refs_0_), custom_call_target="tpu_custom_call" | custom-call | flops 6000000000 | tf_op jit(solution)/shard_map/prefetch/pallas_call | solution.py:43
  14.2 0.3 level2_0.1.refs_3_.refs_0_
  14.5 3.1 %collective-permute-start.7 = (bf16[384,128]{1,0:T(8,128)(2,1)S(1)}, bf16[384,128]{1,0:T(8,128)(2,1)S(1)}, u32[]{:S(2)}, u32[]{:S(2)}) collective-permute-start(bf16[384,128]{1,0:T(8,128)(2,1)S(1)} %level2_0.1.refs_3_.refs_0_), channel_id=1, source_target_pairs={{0,4},{1,5},{2,6},{3,7},{4,0},{5,1},{6,2},{7,3},{8,12},{9,13},{10,... | collective-permute-start | bytes 294920 | tf_op jit(solution)/shard_map/ppermute | solution.py:58
  17.6 0.4 level2_1.1.refs_3_
  18.0 2.3 %collective-permute-start.8 = (bf16[384,256]{1,0:T(8,128)(2,1)S(1)}, bf16[384,256]{1,0:T(8,128)(2,1)S(1)}, u32[]{:S(2)}, u32[]{:S(2)}) collective-permute-start(bf16[384,256]{1,0:T(8,128)(2,1)S(1)} %level2_1.1.refs_3_), channel_id=1, source_target_pairs={{0,4},{1,5},{2,6},{3,7},{4,0},{5,1},{6,2},{7,3},{8,12},{9,13},{10,... | collective-permute-start | bytes 589832 | tf_op jit(solution)/shard_map/ppermute | solution.py:58
  20.2 8.5 %collective-permute-done.2.refs_4_.refs_1_ = bf16[384,384]{1,0:T(8,128)(2,1)S(1)} collective-permute-done((bf16[384,384]{1,0:T(8,128)(2,1)S(1)}, bf16[384,384]{1,0:T(8,128)(2,1)S(1)}, u32[]{:S(2)}, u32[]{:S(2)}) %collective-permute-start.2) | collective-permute-done | bytes 294944 | tf_op jit(solution)/shard_map/ppermute | solution.py:58
  28.7 0.4 level1_3.1.refs_3_.refs_0_
  29.1 0.5 level2_2.1.refs_6_.refs_0_
  29.6 2.5 %collective-permute-start.5 = (bf16[384,384]{1,0:T(8,128)(2,1)S(1)}, bf16[384,384]{1,0:T(8,128)(2,1)S(1)}, u32[]{:S(2)}, u32[]{:S(2)}) collective-permute-start(bf16[384,384]{1,0:T(8,128)(2,1)S(1)} %level2_2.1.refs_6_.refs_0_), channel_id=1, source_target_pairs={{0,4},{1,5},{2,6},{3,7},{4,0},{5,1},{6,2},{7,3},{8,12},{9,13},{10,... | collective-permute-start | bytes 884744 | tf_op jit(solution)/shard_map/ppermute | solution.py:58
  32.1 0.5 level3_1.1
  32.7 0.5 collective-permute-start.9
  33.2 0.3 between_1.1.refs_0_
  33.6 0.7 %collective-permute-done.9.refs_3_ = bf16[384,128]{1,0:T(8,128)(2,1)S(1)} collective-permute-done((bf16[384,128]{1,0:T(8,128)(2,1)S(1)}, bf16[384,128]{1,0:T(8,128)(2,1)S(1)}, u32[]{:S(2)}, u32[]{:S(2)}) %collective-permute-start.9) | collective-permute-done | bytes 98336 | tf_op jit(solution)/shard_map/ppermute | solution.py:58
  34.3 1.2 %last_1.1 = (f32[256,384]{1,0:T(8,128)S(1)}, bf16[256,384]{1,0:T(8,128)(2,1)S(1)}, bf16[256,384]{1,0:T(8,128)(2,1)S(1)}, bf16[256,384]{1,0:T(8,128)(2,1)S(1)}) custom-call(f32[384,384]{1,0:T(8,128)S(1)} %between_1.1.refs_0_, bf16[2,384,768]{2,1,0:T(8,128)(2,1)S(1)} %get-tuple-element.37.refs_0_.refs_1_, ...), custom_call_target="tpu_custom_call" | custom-call | flops 6000000000 | tf_op jit(solution)/shard_map/last_1/pallas_call | solution.py:43
  35.6 2.5 %collective-permute-start.11 = (bf16[256,384]{1,0:T(8,128)(2,1)S(1)}, bf16[256,384]{1,0:T(8,128)(2,1)S(1)}, u32[]{:S(2)}, u32[]{:S(2)}) collective-permute-start(bf16[256,384]{1,0:T(8,128)(2,1)S(1)} %get-tuple-element.44), channel_id=1, source_target_pairs={{0,24},{8,16},{16,8},{24,0},{1,25},{9,17},{17,9},{25,1},{2,26},{10... | collective-permute-start | bytes 589832 | tf_op jit(solution)/shard_map/ppermute | solution.py:58
  38.1 0.5 collective-permute-start.12
  38.6 0.5 collective-permute-start.13
  39.1 0.4 level2_3.1.refs_3_.refs_0_
  39.5 0.9 %collective-permute-start.18 = (bf16[384,256]{1,0:T(8,128)(2,1)S(1)}, bf16[384,256]{1,0:T(8,128)(2,1)S(1)}, u32[]{:S(2)}, u32[]{:S(2)}) collective-permute-start(bf16[384,256]{1,0:T(8,128)(2,1)S(1)} %level2_3.1.refs_3_.refs_0_), channel_id=1, source_target_pairs={{0,4},{1,5},{2,6},{3,7},{4,0},{5,1},{6,2},{7,3},{8,12},{9,13},{10,... | collective-permute-start | bytes 589832 | tf_op jit(solution)/shard_map/ppermute | solution.py:58
  40.4 10.6 %collective-permute-done.5.refs_1_ = bf16[384,384]{1,0:T(8,128)(2,1)S(1)} collective-permute-done((bf16[384,384]{1,0:T(8,128)(2,1)S(1)}, bf16[384,384]{1,0:T(8,128)(2,1)S(1)}, u32[]{:S(2)}, u32[]{:S(2)}) %collective-permute-start.5) | collective-permute-done | bytes 294944 | tf_op jit(solution)/shard_map/ppermute | solution.py:58
  51.0 0.5 level3_2.1.refs_1_
  51.6 0.4 between_2.1
  52.1 1.1 %collective-permute-done.14.refs_3_ = bf16[384,384]{1,0:T(8,128)(2,1)S(1)} collective-permute-done((bf16[384,384]{1,0:T(8,128)(2,1)S(1)}, bf16[384,384]{1,0:T(8,128)(2,1)S(1)}, u32[]{:S(2)}, u32[]{:S(2)}) %collective-permute-start.14) | collective-permute-done | bytes 294944 | tf_op jit(solution)/shard_map/ppermute | solution.py:58
  53.2 1.2 %last_2.1 = (f32[256,384]{1,0:T(8,128)S(1)}, bf16[256,384]{1,0:T(8,128)(2,1)S(1)}, bf16[256,384]{1,0:T(8,128)(2,1)S(1)}, bf16[256,384]{1,0:T(8,128)(2,1)S(1)}) custom-call(f32[384,384]{1,0:T(8,128)S(1)} %get-tuple-element.48.refs_0_, bf16[2,384,768]{2,1,0:T(8,128)(2,1)S(1)} %get-tuple-element.37.refs_0_.refs_1_, ...), custom_call_target="tpu_custom_call" | custom-call | flops 6000000000 | tf_op jit(solution)/shard_map/last_2/pallas_call | solution.py:43
  54.4 2.6 %collective-permute-start.15 = (bf16[256,384]{1,0:T(8,128)(2,1)S(1)}, bf16[256,384]{1,0:T(8,128)(2,1)S(1)}, u32[]{:S(2)}, u32[]{:S(2)}) collective-permute-start(bf16[256,384]{1,0:T(8,128)(2,1)S(1)} %get-tuple-element.50), channel_id=1, source_target_pairs={{0,24},{8,16},{16,8},{24,0},{1,25},{9,17},{17,9},{25,1},{2,26},{10... | collective-permute-start | bytes 589832 | tf_op jit(solution)/shard_map/ppermute | solution.py:58
  57.0 0.5 level3_3.1
  57.6 0.5 collective-permute-start.20
  58.1 0.5 collective-permute-start.16
  58.6 0.5 collective-permute-start.17
  59.1 0.3 between_3.1.refs_0_
  59.4 1.0 %last_3.1 = (f32[256,256]{1,0:T(8,128)S(1)}, bf16[256,256]{1,0:T(8,128)(2,1)S(1)}, bf16[256,256]{1,0:T(8,128)(2,1)S(1)}, bf16[256,256]{1,0:T(8,128)(2,1)S(1)}) custom-call(f32[384,256]{1,0:T(8,128)S(1)} %between_3.1.refs_0_, bf16[2,384,768]{2,1,0:T(8,128)(2,1)S(1)} %get-tuple-element.37.refs_0_.refs_1_, ...), custom_call_target="tpu_custom_call" | custom-call | tf_op jit(solution)/shard_map/last_3/pallas_call | solution.py:43
  60.4 2.6 %collective-permute-start.21 = (bf16[256,256]{1,0:T(8,128)(2,1)S(1)}, bf16[256,256]{1,0:T(8,128)(2,1)S(1)}, u32[]{:S(2)}, u32[]{:S(2)}) collective-permute-start(bf16[256,256]{1,0:T(8,128)(2,1)S(1)} %get-tuple-element.56), channel_id=1, source_target_pairs={{0,24},{8,16},{16,8},{24,0},{1,25},{9,17},{17,9},{25,1},{2,26},{10... | collective-permute-start | bytes 393224 | tf_op jit(solution)/shard_map/ppermute | solution.py:58
  63.0 0.5 collective-permute-start.22
  63.5 1.2 %collective-permute-start.23 = (bf16[256,256]{1,0:T(8,128)(2,1)S(1)}, bf16[256,256]{1,0:T(8,128)(2,1)S(1)}, u32[]{:S(2)}, u32[]{:S(2)}) collective-permute-start(bf16[256,256]{1,0:T(8,128)(2,1)S(1)} %get-tuple-element.58), channel_id=1, source_target_pairs={{0,8},{8,0},{16,24},{24,16},{1,9},{9,1},{17,25},{25,17},{2,10},{10... | collective-permute-start | bytes 393224 | tf_op jit(solution)/shard_map/ppermute | solution.py:58
  64.7 2.7 %collective-permute-done.16.refs_3_ = bf16[256,384]{1,0:T(8,128)(2,1)S(1)} collective-permute-done((bf16[256,384]{1,0:T(8,128)(2,1)S(1)}, bf16[256,384]{1,0:T(8,128)(2,1)S(1)}, u32[]{:S(2)}, u32[]{:S(2)}) %collective-permute-start.16) | collective-permute-done | bytes 196640 | tf_op jit(solution)/shard_map/ppermute | solution.py:58
  67.5 2.7 %collective-permute-done.21.refs_6_ = bf16[256,256]{1,0:T(8,128)(2,1)S(1)} collective-permute-done((bf16[256,256]{1,0:T(8,128)(2,1)S(1)}, bf16[256,256]{1,0:T(8,128)(2,1)S(1)}, u32[]{:S(2)}, u32[]{:S(2)}) %collective-permute-start.21) | collective-permute-done | bytes 131104 | tf_op jit(solution)/shard_map/ppermute | solution.py:58
  70.2 1.9 %collective-permute-done.22.refs_7_ = bf16[256,256]{1,0:T(8,128)(2,1)S(1)} collective-permute-done((bf16[256,256]{1,0:T(8,128)(2,1)S(1)}, bf16[256,256]{1,0:T(8,128)(2,1)S(1)}, u32[]{:S(2)}, u32[]{:S(2)}) %collective-permute-start.22) | collective-permute-done | bytes 131104 | tf_op jit(solution)/shard_map/ppermute | solution.py:58
  72.2 0.2 collective-permute-done.23.refs_8_
  72.4 1.0 %end.1 = bf16[2,256,512]{2,1,0:T(8,128)(2,1)} custom-call(bf16[256,384]{1,0:T(8,128)(2,1)S(1)} %get-tuple-element.47.refs_0_, f32[256,384]{1,0:T(8,128)S(1)} %get-tuple-element.49.refs_6_.refs_1_, bf16[256,384]{1,0:T(8,128)(2,1)S(1)} %collective-permute-done.15.refs_2_, bf16[256,384]{1,0:T(8,128)(2,1)S(1)} %collective-permute-done.16.refs_3_, ...), custom_call_target="tpu_custom_call" | custom-call | tf_op jit(solution)/shard_map/end/pallas_call | solution.py:371
  (20 shorter events, 0.5 us)
Async XLA Ops:
  3.7 1.5 %collective-permute-start = (bf16[384,128]{1,0:T(8,128)(2,1)S(1)}, bf16[384,128]{1,0:T(8,128)(2,1)S(1)}, u32[]{:S(2)}, u32[]{:S(2)}) collective-permute-start(bf16[384,128]{1,0:T(8,128)(2,1)S(1)} %get-tuple-element.32.refs_0_), channel_id=1, source_target_pairs={{0,1},{1,0},{2,3},{3,2},{4,5},{5,4},{6,7},{7,6},{8,9},{9,8},{10,11... | collective-permute-start | bytes 294920 | tf_op jit(solution)/shard_map/ppermute | solution.py:58
  5.5 3.1 %collective-permute-start.1 = (bf16[384,896]{1,0:T(8,128)(2,1)S(1)}, bf16[384,896]{1,0:T(8,128)(2,1)S(1)}, u32[]{:S(2)}, u32[]{:S(2)}) collective-permute-start(bf16[384,896]{1,0:T(8,128)(2,1)S(1)} %get-tuple-element.35.refs_0_), channel_id=1, source_target_pairs={{0,1},{1,0},{2,3},{3,2},{4,5},{5,4},{6,7},{7,6},{8,9},{9,8},{10,11... | collective-permute-start | bytes 2064392 | tf_op jit(solution)/shard_map/ppermute | solution.py:58
  5.9 8.3 %collective-permute-start.4 = (bf16[384,128]{1,0:T(8,128)(2,1)S(1)}, bf16[384,128]{1,0:T(8,128)(2,1)S(1)}, u32[]{:S(2)}, u32[]{:S(2)}) collective-permute-start(bf16[384,128]{1,0:T(8,128)(2,1)S(1)} %get-tuple-element.36.refs_3_.refs_0_), channel_id=1, source_target_pairs={{0,2},{1,3},{2,0},{3,1},{4,6},{5,7},{6,4},{7,5},{8,10},{9,11},{10,... | collective-permute-start | bytes 294920 | tf_op jit(solution)/shard_map/ppermute | solution.py:58
  9.0 8.6 %collective-permute-start.3 = (bf16[384,256]{1,0:T(8,128)(2,1)S(1)}, bf16[384,256]{1,0:T(8,128)(2,1)S(1)}, u32[]{:S(2)}, u32[]{:S(2)}) collective-permute-start(bf16[384,256]{1,0:T(8,128)(2,1)S(1)} %level1_1.1.refs_3_.refs_0_), channel_id=1, source_target_pairs={{0,2},{1,3},{2,0},{3,1},{4,6},{5,7},{6,4},{7,5},{8,10},{9,11},{10,... | collective-permute-start | bytes 589832 | tf_op jit(solution)/shard_map/ppermute | solution.py:58
  11.6 17.1 %collective-permute-start.2 = (bf16[384,384]{1,0:T(8,128)(2,1)S(1)}, bf16[384,384]{1,0:T(8,128)(2,1)S(1)}, u32[]{:S(2)}, u32[]{:S(2)}) collective-permute-start(bf16[384,384]{1,0:T(8,128)(2,1)S(1)} %level1_2.1.refs_3_.refs_0_), channel_id=1, source_target_pairs={{0,2},{1,3},{2,0},{3,1},{4,6},{5,7},{6,4},{7,5},{8,10},{9,11},{10,... | collective-permute-start | bytes 884744 | tf_op jit(solution)/shard_map/ppermute | solution.py:58
  14.5 17.6 %collective-permute-start.7 = (bf16[384,128]{1,0:T(8,128)(2,1)S(1)}, bf16[384,128]{1,0:T(8,128)(2,1)S(1)}, u32[]{:S(2)}, u32[]{:S(2)}) collective-permute-start(bf16[384,128]{1,0:T(8,128)(2,1)S(1)} %level2_0.1.refs_3_.refs_0_), channel_id=1, source_target_pairs={{0,4},{1,5},{2,6},{3,7},{4,0},{5,1},{6,2},{7,3},{8,12},{9,13},{10,... | collective-permute-start | bytes 294920 | tf_op jit(solution)/shard_map/ppermute | solution.py:58
  18.0 14.2 %collective-permute-start.8 = (bf16[384,256]{1,0:T(8,128)(2,1)S(1)}, bf16[384,256]{1,0:T(8,128)(2,1)S(1)}, u32[]{:S(2)}, u32[]{:S(2)}) collective-permute-start(bf16[384,256]{1,0:T(8,128)(2,1)S(1)} %level2_1.1.refs_3_), channel_id=1, source_target_pairs={{0,4},{1,5},{2,6},{3,7},{4,0},{5,1},{6,2},{7,3},{8,12},{9,13},{10,... | collective-permute-start | bytes 589832 | tf_op jit(solution)/shard_map/ppermute | solution.py:58
  29.0 10.1 %collective-permute-start.6 = (bf16[384,256]{1,0:T(8,128)(2,1)S(1)}, bf16[384,256]{1,0:T(8,128)(2,1)S(1)}, u32[]{:S(2)}, u32[]{:S(2)}) collective-permute-start(bf16[384,256]{1,0:T(8,128)(2,1)S(1)} %level1_3.1.refs_3_.refs_0_), channel_id=1, source_target_pairs={{0,2},{1,3},{2,0},{3,1},{4,6},{5,7},{6,4},{7,5},{8,10},{9,11},{10,... | collective-permute-start | bytes 589832 | tf_op jit(solution)/shard_map/ppermute | solution.py:58
  29.6 21.4 %collective-permute-start.5 = (bf16[384,384]{1,0:T(8,128)(2,1)S(1)}, bf16[384,384]{1,0:T(8,128)(2,1)S(1)}, u32[]{:S(2)}, u32[]{:S(2)}) collective-permute-start(bf16[384,384]{1,0:T(8,128)(2,1)S(1)} %level2_2.1.refs_6_.refs_0_), channel_id=1, source_target_pairs={{0,4},{1,5},{2,6},{3,7},{4,0},{5,1},{6,2},{7,3},{8,12},{9,13},{10,... | collective-permute-start | bytes 884744 | tf_op jit(solution)/shard_map/ppermute | solution.py:58
  32.6 1.7 %collective-permute-start.10 = (bf16[384,256]{1,0:T(8,128)(2,1)S(1)}, bf16[384,256]{1,0:T(8,128)(2,1)S(1)}, u32[]{:S(2)}, u32[]{:S(2)}) collective-permute-start(bf16[384,256]{1,0:T(8,128)(2,1)S(1)} %get-tuple-element.42.refs_2_), channel_id=1, source_target_pairs={{0,1},{1,0},{2,3},{3,2},{4,5},{5,4},{6,7},{7,6},{8,9},{9,8},{10,11... | collective-permute-start | bytes 589832 | tf_op jit(solution)/shard_map/ppermute | solution.py:58
  32.7 1.6 %collective-permute-start.9 = (bf16[384,128]{1,0:T(8,128)(2,1)S(1)}, bf16[384,128]{1,0:T(8,128)(2,1)S(1)}, u32[]{:S(2)}, u32[]{:S(2)}) collective-permute-start(bf16[384,128]{1,0:T(8,128)(2,1)S(1)} %get-tuple-element.41.refs_1_), channel_id=1, source_target_pairs={{0,1},{1,0},{2,3},{3,2},{4,5},{5,4},{6,7},{7,6},{8,9},{9,8},{10,11... | collective-permute-start | bytes 294920 | tf_op jit(solution)/shard_map/ppermute | solution.py:58
  35.6 16.1 %collective-permute-start.11 = (bf16[256,384]{1,0:T(8,128)(2,1)S(1)}, bf16[256,384]{1,0:T(8,128)(2,1)S(1)}, u32[]{:S(2)}, u32[]{:S(2)}) collective-permute-start(bf16[256,384]{1,0:T(8,128)(2,1)S(1)} %get-tuple-element.44), channel_id=1, source_target_pairs={{0,24},{8,16},{16,8},{24,0},{1,25},{9,17},{17,9},{25,1},{2,26},{10... | collective-permute-start | bytes 589832 | tf_op jit(solution)/shard_map/ppermute | solution.py:58
  38.1 13.6 %collective-permute-start.12 = (bf16[256,384]{1,0:T(8,128)(2,1)S(1)}, bf16[256,384]{1,0:T(8,128)(2,1)S(1)}, u32[]{:S(2)}, u32[]{:S(2)}) collective-permute-start(bf16[256,384]{1,0:T(8,128)(2,1)S(1)} %get-tuple-element.45), channel_id=1, source_target_pairs={{0,16},{8,24},{16,0},{24,8},{1,17},{9,25},{17,1},{25,9},{2,18},{10... | collective-permute-start | bytes 589832 | tf_op jit(solution)/shard_map/ppermute | solution.py:58
  38.6 13.1 %collective-permute-start.13 = (bf16[256,384]{1,0:T(8,128)(2,1)S(1)}, bf16[256,384]{1,0:T(8,128)(2,1)S(1)}, u32[]{:S(2)}, u32[]{:S(2)}) collective-permute-start(bf16[256,384]{1,0:T(8,128)(2,1)S(1)} %get-tuple-element.46), channel_id=1, source_target_pairs={{0,8},{8,0},{16,24},{24,16},{1,9},{9,1},{17,25},{25,17},{2,10},{10... | collective-permute-start | bytes 589832 | tf_op jit(solution)/shard_map/ppermute | solution.py:58
  39.5 17.6 %collective-permute-start.18 = (bf16[384,256]{1,0:T(8,128)(2,1)S(1)}, bf16[384,256]{1,0:T(8,128)(2,1)S(1)}, u32[]{:S(2)}, u32[]{:S(2)}) collective-permute-start(bf16[384,256]{1,0:T(8,128)(2,1)S(1)} %level2_3.1.refs_3_.refs_0_), channel_id=1, source_target_pairs={{0,4},{1,5},{2,6},{3,7},{4,0},{5,1},{6,2},{7,3},{8,12},{9,13},{10,... | collective-permute-start | bytes 589832 | tf_op jit(solution)/shard_map/ppermute | solution.py:58
  51.5 1.6 %collective-permute-start.14 = (bf16[384,384]{1,0:T(8,128)(2,1)S(1)}, bf16[384,384]{1,0:T(8,128)(2,1)S(1)}, u32[]{:S(2)}, u32[]{:S(2)}) collective-permute-start(bf16[384,384]{1,0:T(8,128)(2,1)S(1)} %level3_2.1.refs_1_), channel_id=1, source_target_pairs={{0,1},{1,0},{2,3},{3,2},{4,5},{5,4},{6,7},{7,6},{8,9},{9,8},{10,11... | collective-permute-start | bytes 884744 | tf_op jit(solution)/shard_map/ppermute | solution.py:58
  54.4 9.1 %collective-permute-start.15 = (bf16[256,384]{1,0:T(8,128)(2,1)S(1)}, bf16[256,384]{1,0:T(8,128)(2,1)S(1)}, u32[]{:S(2)}, u32[]{:S(2)}) collective-permute-start(bf16[256,384]{1,0:T(8,128)(2,1)S(1)} %get-tuple-element.50), channel_id=1, source_target_pairs={{0,24},{8,16},{16,8},{24,0},{1,25},{9,17},{17,9},{25,1},{2,26},{10... | collective-permute-start | bytes 589832 | tf_op jit(solution)/shard_map/ppermute | solution.py:58
  57.5 1.8 %collective-permute-start.19 = (bf16[384,128]{1,0:T(8,128)(2,1)S(1)}, bf16[384,128]{1,0:T(8,128)(2,1)S(1)}, u32[]{:S(2)}, u32[]{:S(2)}) collective-permute-start(bf16[384,128]{1,0:T(8,128)(2,1)S(1)} %get-tuple-element.53.refs_1_), channel_id=1, source_target_pairs={{0,1},{1,0},{2,3},{3,2},{4,5},{5,4},{6,7},{7,6},{8,9},{9,8},{10,11... | collective-permute-start | bytes 294920 | tf_op jit(solution)/shard_map/ppermute | solution.py:58
  57.6 1.8 %collective-permute-start.20 = (bf16[384,128]{1,0:T(8,128)(2,1)S(1)}, bf16[384,128]{1,0:T(8,128)(2,1)S(1)}, u32[]{:S(2)}, u32[]{:S(2)}) collective-permute-start(bf16[384,128]{1,0:T(8,128)(2,1)S(1)} %get-tuple-element.54.refs_2_), channel_id=1, source_target_pairs={{0,1},{1,0},{2,3},{3,2},{4,5},{5,4},{6,7},{7,6},{8,9},{9,8},{10,11... | collective-permute-start | bytes 294920 | tf_op jit(solution)/shard_map/ppermute | solution.py:58
  58.1 9.4 %collective-permute-start.16 = (bf16[256,384]{1,0:T(8,128)(2,1)S(1)}, bf16[256,384]{1,0:T(8,128)(2,1)S(1)}, u32[]{:S(2)}, u32[]{:S(2)}) collective-permute-start(bf16[256,384]{1,0:T(8,128)(2,1)S(1)} %get-tuple-element.51), channel_id=1, source_target_pairs={{0,16},{8,24},{16,0},{24,8},{1,17},{9,25},{17,1},{25,9},{2,18},{10... | collective-permute-start | bytes 589832 | tf_op jit(solution)/shard_map/ppermute | solution.py:58
  58.6 8.9 %collective-permute-start.17 = (bf16[256,384]{1,0:T(8,128)(2,1)S(1)}, bf16[256,384]{1,0:T(8,128)(2,1)S(1)}, u32[]{:S(2)}, u32[]{:S(2)}) collective-permute-start(bf16[256,384]{1,0:T(8,128)(2,1)S(1)} %get-tuple-element.52), channel_id=1, source_target_pairs={{0,8},{8,0},{16,24},{24,16},{1,9},{9,1},{17,25},{25,17},{2,10},{10... | collective-permute-start | bytes 589832 | tf_op jit(solution)/shard_map/ppermute | solution.py:58
  60.4 9.8 %collective-permute-start.21 = (bf16[256,256]{1,0:T(8,128)(2,1)S(1)}, bf16[256,256]{1,0:T(8,128)(2,1)S(1)}, u32[]{:S(2)}, u32[]{:S(2)}) collective-permute-start(bf16[256,256]{1,0:T(8,128)(2,1)S(1)} %get-tuple-element.56), channel_id=1, source_target_pairs={{0,24},{8,16},{16,8},{24,0},{1,25},{9,17},{17,9},{25,1},{2,26},{10... | collective-permute-start | bytes 393224 | tf_op jit(solution)/shard_map/ppermute | solution.py:58
  63.0 9.2 %collective-permute-start.22 = (bf16[256,256]{1,0:T(8,128)(2,1)S(1)}, bf16[256,256]{1,0:T(8,128)(2,1)S(1)}, u32[]{:S(2)}, u32[]{:S(2)}) collective-permute-start(bf16[256,256]{1,0:T(8,128)(2,1)S(1)} %get-tuple-element.57), channel_id=1, source_target_pairs={{0,16},{8,24},{16,0},{24,8},{1,17},{9,25},{17,1},{25,9},{2,18},{10... | collective-permute-start | bytes 393224 | tf_op jit(solution)/shard_map/ppermute | solution.py:58
  63.5 8.9 %collective-permute-start.23 = (bf16[256,256]{1,0:T(8,128)(2,1)S(1)}, bf16[256,256]{1,0:T(8,128)(2,1)S(1)}, u32[]{:S(2)}, u32[]{:S(2)}) collective-permute-start(bf16[256,256]{1,0:T(8,128)(2,1)S(1)} %get-tuple-element.58), channel_id=1, source_target_pairs={{0,8},{8,0},{16,24},{24,16},{1,9},{9,1},{17,25},{25,17},{2,10},{10... | collective-permute-start | bytes 393224 | tf_op jit(solution)/shard_map/ppermute | solution.py:58

commit v19 on v13

--- a/solution.py
+++ b/solution.py
@@ -7,7 +7,7 @@
 from jax.experimental.pallas import tpu as pltpu
 from jax.sharding import PartitionSpec as P
 
-SHARES = (1, 2, 3, 2)
+SHARES = (1, 3, 3, 1)
 PRELOADED = 2
 COST = 6 * 10**9
 BF16 = jnp.bfloat16
@@ -328,7 +328,17 @@
     third(3, value)
     group2, (total1,) = tail(2, [coeff3[3]], [(1, group1)])
     group3, _ = tail(3, [group2[0]])
-    groups = [[total0], [total1], group2, group3]
+    (total2,) = call(
+        sum_kernel,
+        "sum_2",
+        [VMEM] * n_blk,
+        [in_vmem(rows, widths[2])],
+        [],
+        [here(v) for v in group2],
+        [group3[0]],
+        0,
+    )
+    groups = [[total0], [total1], [total2], group3]
     flat = [here(v) for group in groups for v in group]
     return pl.pallas_call(
         functools.partial(end_kernel, places, [len(group) for group in groups]),

time: 70.1 us -> 77.2 us (1.10)
  waiting for transfers between devices: 21.6 us -> 31.3 us
  starting transfers between devices: 31.6 us -> 28.9 us
    ppermute x26, waiting for transfers between devices: 21.6 us -> 31.3 us  [partner(): return lax.ppermute(value, axis, pairs)]
    ppermute x26, starting transfers between devices: 31.6 us -> 28.9 us  [partner(): return lax.ppermute(value, axis, pairs)]
    pallas_call x23 -> x24, Pallas kernels: 15.5 us -> 15.7 us  [call(): pl.pallas_call(body, name=name, in_specs=[*in_specs, *[ANY] * len(after)]...]
  transfers between devices with their start and end apart: 26 -> 26, of which waited for: 14 -> 17; matrix products, arithmetic and copies ran while one was open for 0% -> 0% of each run, Pallas kernels for 17% -> 16%
where the time goes in v19:
time: 77.2 us; the launch traced here: 77 us
  waiting for transfers between devices  31.3 us (41%)
  starting transfers between devices  28.9 us (37%)
  Pallas kernels  16.6 us (22%)
    ppermute x26, waiting for transfers between devices, partner(): return lax.ppermute(value, axis, pairs)  31.3 us
    ppermute x26, starting transfers between devices, partner(): return lax.ppermute(value, axis, pairs)  28.9 us
    pallas_call x24, Pallas kernels, call(): pl.pallas_call(body, name=name, in_specs=[*in_specs, *[ANY] * len(after)]...  15.7 us
  transfers between devices with their start and end apart: 26, of which 17 were waited for; matrix products, arithmetic and copies ran while one was open for 0% of the time, Pallas kernels for 16%

profile of v19, /device:TPU:0, one launch (start us, length us, event | category | flops | bytes accessed | tf_op | source)
XLA Modules:
  0.0 77.0 jit_solution(17831264397254704352)
XLA Ops:
  0.0 3.7 %leaf.1 = (bf16[384,128]{1,0:T(8,128)(2,1)S(1)}, bf16[384,896]{1,0:T(8,128)(2,1)S(1)}, bf16[2,384,768]{2,1,0:T(8,128)(2,1)S(1)}, bf16[2,384,768]{2,1,0:T(8,128)(2,1)S(1)}) custom-call(bf16[2,1024,512]{2,1,0:T(8,128)(2,1)} %bitcast.9, bf16[2,384,1024]{2,1,0:T(8,128)(2,1)} %bitcast.10, bf16[5,2,384,768]{3,2,1,0:T(8,128)(2,1)} %bitcast.7, s32[2,5]{1,0:T(2,128)} %bitcast.12), custom_call_target="tpu_custom_call" | custom-call | flops 6000000000 | tf_op jit(solution)/shard_map/leaf/pallas_call | solution.py:41
  3.7 0.5 collective-permute-start.2
  4.3 1.8 %collective-permute-done.refs_1_ = bf16[384,128]{1,0:T(8,128)(2,1)S(1)} collective-permute-done((bf16[384,128]{1,0:T(8,128)(2,1)S(1)}, bf16[384,128]{1,0:T(8,128)(2,1)S(1)}, u32[]{:S(2)}, u32[]{:S(2)}) %collective-permute-start) | collective-permute-done | bytes 98336 | tf_op jit(solution)/shard_map/ppermute | solution.py:55
  6.4 3.0 %collective-permute-start.1 = (bf16[384,128]{1,0:T(8,128)(2,1)S(1)}, bf16[384,128]{1,0:T(8,128)(2,1)S(1)}, u32[]{:S(2)}, u32[]{:S(2)}) collective-permute-start(bf16[384,128]{1,0:T(8,128)(2,1)S(1)} %level1_0.1.refs_3_.refs_0_), channel_id=1, source_target_pairs={{0,2},{1,3},{2,0},{3,1},{4,6},{5,7},{6,4},{7,5},{8,10},{9,11},{10,... | collective-permute-start | bytes 294920 | tf_op jit(solution)/shard_map/ppermute | solution.py:55
  9.5 0.5 level1_1.1.refs_3_.refs_0_
  10.1 2.5 %collective-permute-done.1.refs_1_ = bf16[384,128]{1,0:T(8,128)(2,1)S(1)} collective-permute-done((bf16[384,128]{1,0:T(8,128)(2,1)S(1)}, bf16[384,128]{1,0:T(8,128)(2,1)S(1)}, u32[]{:S(2)}, u32[]{:S(2)}) %collective-permute-start.1) | collective-permute-done | bytes 98336 | tf_op jit(solution)/shard_map/ppermute | solution.py:55
  13.0 3.0 %collective-permute-start.3 = (bf16[384,128]{1,0:T(8,128)(2,1)S(1)}, bf16[384,128]{1,0:T(8,128)(2,1)S(1)}, u32[]{:S(2)}, u32[]{:S(2)}) collective-permute-start(bf16[384,128]{1,0:T(8,128)(2,1)S(1)} %level2_0.1.refs_3_.refs_0_), channel_id=1, source_target_pairs={{0,4},{1,5},{2,6},{3,7},{4,0},{5,1},{6,2},{7,3},{8,12},{9,13},{10,... | collective-permute-start | bytes 294920 | tf_op jit(solution)/shard_map/ppermute | solution.py:55
  15.9 0.5 level1_2.1.refs_3_.refs_0_
  16.4 2.2 %collective-permute-start.9 = (bf16[384,384]{1,0:T(8,128)(2,1)S(1)}, bf16[384,384]{1,0:T(8,128)(2,1)S(1)}, u32[]{:S(2)}, u32[]{:S(2)}) collective-permute-start(bf16[384,384]{1,0:T(8,128)(2,1)S(1)} %level1_2.1.refs_3_.refs_0_), channel_id=1, source_target_pairs={{0,2},{1,3},{2,0},{3,1},{4,6},{5,7},{6,4},{7,5},{8,10},{9,11},{10,... | collective-permute-start | bytes 884744 | tf_op jit(solution)/shard_map/ppermute | solution.py:55
  18.7 2.5 %prefetch.1 = (bf16[2,384,768]{2,1,0:T(8,128)(2,1)S(1)}, bf16[2,384,768]{2,1,0:T(8,128)(2,1)S(1)}, bf16[2,1024,384]{2,1,0:T(8,128)(2,1)S(1)}) custom-call(bf16[5,2,384,768]{3,2,1,0:T(8,128)(2,1)} %bitcast.8, bf16[2,1024,384]{2,1,0:T(8,128)(2,1)} %bitcast.11, s32[2,5]{1,0:T(2,128)} %bitcast.13, bf16[384,384]{1,0:T(8,128)(2,1)S(1)} %level1_2.1.refs_3_.refs_0_), custom_call_target="tpu_custom_call" | custom-call | flops 6000000000 | tf_op jit(solution)/shard_map/prefetch/pallas_call | solution.py:41
  21.2 0.9 %collective-permute-done.4.refs_1_ = bf16[384,384]{1,0:T(8,128)(2,1)S(1)} collective-permute-done((bf16[384,384]{1,0:T(8,128)(2,1)S(1)}, bf16[384,384]{1,0:T(8,128)(2,1)S(1)}, u32[]{:S(2)}, u32[]{:S(2)}) %collective-permute-start.4) | collective-permute-done | bytes 294944 | tf_op jit(solution)/shard_map/ppermute | solution.py:55
  22.0 0.5 level2_1.1.refs_3_.refs_0_
  22.6 1.6 %collective-permute-start.12 = (bf16[384,384]{1,0:T(8,128)(2,1)S(1)}, bf16[384,384]{1,0:T(8,128)(2,1)S(1)}, u32[]{:S(2)}, u32[]{:S(2)}) collective-permute-start(bf16[384,384]{1,0:T(8,128)(2,1)S(1)} %level2_1.1.refs_3_.refs_0_), channel_id=1, source_target_pairs={{0,4},{1,5},{2,6},{3,7},{4,0},{5,1},{6,2},{7,3},{8,12},{9,13},{10,... | collective-permute-start | bytes 884744 | tf_op jit(solution)/shard_map/ppermute | solution.py:55
  24.2 0.3 level3_0.1.refs_0_
  24.9 1.0 %collective-permute-done.5.refs_1_ = bf16[384,128]{1,0:T(8,128)(2,1)S(1)} collective-permute-done((bf16[384,128]{1,0:T(8,128)(2,1)S(1)}, bf16[384,128]{1,0:T(8,128)(2,1)S(1)}, u32[]{:S(2)}, u32[]{:S(2)}) %collective-permute-start.5) | collective-permute-done | bytes 98336 | tf_op jit(solution)/shard_map/ppermute | solution.py:55
  25.9 0.6 last_0.1
  26.5 2.5 %collective-permute-start.6 = (bf16[256,128]{1,0:T(8,128)(2,1)S(1)}, bf16[256,128]{1,0:T(8,128)(2,1)S(1)}, u32[]{:S(2)}, u32[]{:S(2)}) collective-permute-start(bf16[256,128]{1,0:T(8,128)(2,1)S(1)} %get-tuple-element.38), channel_id=1, source_target_pairs={{0,24},{8,16},{16,8},{24,0},{1,25},{9,17},{17,9},{25,1},{2,26},{10... | collective-permute-start | bytes 196616 | tf_op jit(solution)/shard_map/ppermute | solution.py:55
  29.0 0.5 collective-permute-start.7
  29.5 0.5 collective-permute-start.8
  30.1 2.7 %collective-permute-done.9.refs_1_ = bf16[384,384]{1,0:T(8,128)(2,1)S(1)} collective-permute-done((bf16[384,384]{1,0:T(8,128)(2,1)S(1)}, bf16[384,384]{1,0:T(8,128)(2,1)S(1)}, u32[]{:S(2)}, u32[]{:S(2)}) %collective-permute-start.9) | collective-permute-done | bytes 294944 | tf_op jit(solution)/shard_map/ppermute | solution.py:55
  32.7 0.5 level2_2.1.refs_4_.refs_0_
  33.4 0.4 collective-permute-done.8.refs_3_
  33.8 0.4 level1_3.1.refs_3_.refs_0_
  34.2 2.5 %collective-permute-start.11 = (bf16[384,128]{1,0:T(8,128)(2,1)S(1)}, bf16[384,128]{1,0:T(8,128)(2,1)S(1)}, u32[]{:S(2)}, u32[]{:S(2)}) collective-permute-start(bf16[384,128]{1,0:T(8,128)(2,1)S(1)} %level1_3.1.refs_3_.refs_0_), channel_id=1, source_target_pairs={{0,2},{1,3},{2,0},{3,1},{4,6},{5,7},{6,4},{7,5},{8,10},{9,11},{10,... | collective-permute-start | bytes 294920 | tf_op jit(solution)/shard_map/ppermute | solution.py:55
  36.7 7.2 %collective-permute-done.12.refs_1_ = bf16[384,384]{1,0:T(8,128)(2,1)S(1)} collective-permute-done((bf16[384,384]{1,0:T(8,128)(2,1)S(1)}, bf16[384,384]{1,0:T(8,128)(2,1)S(1)}, u32[]{:S(2)}, u32[]{:S(2)}) %collective-permute-start.12) | collective-permute-done | bytes 294944 | tf_op jit(solution)/shard_map/ppermute | solution.py:55
  43.9 0.5 level3_1.1.refs_0_
  44.8 1.2 %collective-permute-done.13.refs_1_ = bf16[384,384]{1,0:T(8,128)(2,1)S(1)} collective-permute-done((bf16[384,384]{1,0:T(8,128)(2,1)S(1)}, bf16[384,384]{1,0:T(8,128)(2,1)S(1)}, u32[]{:S(2)}, u32[]{:S(2)}) %collective-permute-start.13) | collective-permute-done | bytes 294944 | tf_op jit(solution)/shard_map/ppermute | solution.py:55
  46.1 1.0 %last_1.1 = (f32[256,384]{1,0:T(8,128)S(1)}, bf16[256,384]{1,0:T(8,128)(2,1)S(1)}, bf16[256,384]{1,0:T(8,128)(2,1)S(1)}, bf16[256,384]{1,0:T(8,128)(2,1)S(1)}) custom-call(f32[384,384]{1,0:T(8,128)S(1)} %between_1.1.refs_0_, bf16[384,384]{1,0:T(8,128)(2,1)S(1)} %collective-permute-done.13.refs_1_, ...), custom_call_target="tpu_custom_call" | custom-call | flops 6000000000 | tf_op jit(solution)/shard_map/last_1/pallas_call | solution.py:41
  47.0 3.2 %collective-permute-start.14 = (bf16[256,384]{1,0:T(8,128)(2,1)S(1)}, bf16[256,384]{1,0:T(8,128)(2,1)S(1)}, u32[]{:S(2)}, u32[]{:S(2)}) collective-permute-start(bf16[256,384]{1,0:T(8,128)(2,1)S(1)} %get-tuple-element.42), channel_id=1, source_target_pairs={{0,24},{8,16},{16,8},{24,0},{1,25},{9,17},{17,9},{25,1},{2,26},{10... | collective-permute-start | bytes 589832 | tf_op jit(solution)/shard_map/ppermute | solution.py:55
  50.2 0.5 collective-permute-start.15
  51.3 0.5 level3_2.1.refs_0_
  51.9 4.1 %collective-permute-done.14.refs_3_ = bf16[256,384]{1,0:T(8,128)(2,1)S(1)} collective-permute-done((bf16[256,384]{1,0:T(8,128)(2,1)S(1)}, bf16[256,384]{1,0:T(8,128)(2,1)S(1)}, u32[]{:S(2)}, u32[]{:S(2)}) %collective-permute-start.14) | collective-permute-done | bytes 196640 | tf_op jit(solution)/shard_map/ppermute | solution.py:55
  56.0 3.7 %collective-permute-done.15.refs_4_ = bf16[256,384]{1,0:T(8,128)(2,1)S(1)} collective-permute-done((bf16[256,384]{1,0:T(8,128)(2,1)S(1)}, bf16[256,384]{1,0:T(8,128)(2,1)S(1)}, u32[]{:S(2)}, u32[]{:S(2)}) %collective-permute-start.15) | collective-permute-done | bytes 196640 | tf_op jit(solution)/shard_map/ppermute | solution.py:55
  59.9 0.4 between_2.1
  60.4 1.0 %last_2.1 = (f32[256,384]{1,0:T(8,128)S(1)}, bf16[256,384]{1,0:T(8,128)(2,1)S(1)}, bf16[256,384]{1,0:T(8,128)(2,1)S(1)}, bf16[256,384]{1,0:T(8,128)(2,1)S(1)}) custom-call(f32[384,384]{1,0:T(8,128)S(1)} %get-tuple-element.46.refs_0_, bf16[384,384]{1,0:T(8,128)(2,1)S(1)} %collective-permute-done.17.refs_1_, ...), custom_call_target="tpu_custom_call" | custom-call | flops 6000000000 | tf_op jit(solution)/shard_map/last_2/pallas_call | solution.py:41
  61.3 1.6 %collective-permute-start.18 = (bf16[256,384]{1,0:T(8,128)(2,1)S(1)}, bf16[256,384]{1,0:T(8,128)(2,1)S(1)}, u32[]{:S(2)}, u32[]{:S(2)}) collective-permute-start(bf16[256,384]{1,0:T(8,128)(2,1)S(1)} %get-tuple-element.48), channel_id=1, source_target_pairs={{0,24},{8,16},{16,8},{24,0},{1,25},{9,17},{17,9},{25,1},{2,26},{10... | collective-permute-start | bytes 589832 | tf_op jit(solution)/shard_map/ppermute | solution.py:55
  63.0 1.4 %collective-permute-start.19 = (bf16[256,384]{1,0:T(8,128)(2,1)S(1)}, bf16[256,384]{1,0:T(8,128)(2,1)S(1)}, u32[]{:S(2)}, u32[]{:S(2)}) collective-permute-start(bf16[256,384]{1,0:T(8,128)(2,1)S(1)} %get-tuple-element.49), channel_id=1, source_target_pairs={{0,16},{8,24},{16,0},{24,8},{1,17},{9,25},{17,1},{25,9},{2,18},{10... | collective-permute-start | bytes 589832 | tf_op jit(solution)/shard_map/ppermute | solution.py:55
  64.4 0.5 collective-permute-start.20
  65.6 1.0 %collective-permute-done.22.refs_1_ = bf16[384,128]{1,0:T(8,128)(2,1)S(1)} collective-permute-done((bf16[384,128]{1,0:T(8,128)(2,1)S(1)}, bf16[384,128]{1,0:T(8,128)(2,1)S(1)}, u32[]{:S(2)}, u32[]{:S(2)}) %collective-permute-start.22) | collective-permute-done | bytes 98336 | tf_op jit(solution)/shard_map/ppermute | solution.py:55
  66.6 0.6 last_3.1
  67.2 1.6 %collective-permute-start.23 = (bf16[256,128]{1,0:T(8,128)(2,1)S(1)}, bf16[256,128]{1,0:T(8,128)(2,1)S(1)}, u32[]{:S(2)}, u32[]{:S(2)}) collective-permute-start(bf16[256,128]{1,0:T(8,128)(2,1)S(1)} %get-tuple-element.52), channel_id=1, source_target_pairs={{0,24},{8,16},{16,8},{24,0},{1,25},{9,17},{17,9},{25,1},{2,26},{10... | collective-permute-start | bytes 196616 | tf_op jit(solution)/shard_map/ppermute | solution.py:55
  68.8 1.4 %collective-permute-start.24 = (bf16[256,128]{1,0:T(8,128)(2,1)S(1)}, bf16[256,128]{1,0:T(8,128)(2,1)S(1)}, u32[]{:S(2)}, u32[]{:S(2)}) collective-permute-start(bf16[256,128]{1,0:T(8,128)(2,1)S(1)} %get-tuple-element.53), channel_id=1, source_target_pairs={{0,16},{8,24},{16,0},{24,8},{1,17},{9,25},{17,1},{25,9},{2,18},{10... | collective-permute-start | bytes 196616 | tf_op jit(solution)/shard_map/ppermute | solution.py:55
  70.3 1.4 %collective-permute-start.25 = (bf16[256,128]{1,0:T(8,128)(2,1)S(1)}, bf16[256,128]{1,0:T(8,128)(2,1)S(1)}, u32[]{:S(2)}, u32[]{:S(2)}) collective-permute-start(bf16[256,128]{1,0:T(8,128)(2,1)S(1)} %get-tuple-element.54), channel_id=1, source_target_pairs={{0,8},{8,0},{16,24},{24,16},{1,9},{9,1},{17,25},{25,17},{2,10},{10... | collective-permute-start | bytes 196616 | tf_op jit(solution)/shard_map/ppermute | solution.py:55
  71.6 2.2 %collective-permute-done.19.refs_2_ = bf16[256,384]{1,0:T(8,128)(2,1)S(1)} collective-permute-done((bf16[256,384]{1,0:T(8,128)(2,1)S(1)}, bf16[256,384]{1,0:T(8,128)(2,1)S(1)}, u32[]{:S(2)}, u32[]{:S(2)}) %collective-permute-start.19) | collective-permute-done | bytes 196640 | tf_op jit(solution)/shard_map/ppermute | solution.py:55
  73.9 0.4 collective-permute-done.20.refs_3_
  74.4 0.9 %collective-permute-done.23.refs_4_ = bf16[256,128]{1,0:T(8,128)(2,1)S(1)} collective-permute-done((bf16[256,128]{1,0:T(8,128)(2,1)S(1)}, bf16[256,128]{1,0:T(8,128)(2,1)S(1)}, u32[]{:S(2)}, u32[]{:S(2)}) %collective-permute-start.23) | collective-permute-done | bytes 65568 | tf_op jit(solution)/shard_map/ppermute | solution.py:55
  75.3 0.6 collective-permute-done.24.refs_5_
  76.2 0.9 %end.1 = bf16[2,256,512]{2,1,0:T(8,128)(2,1)} custom-call(bf16[256,128]{1,0:T(8,128)(2,1)S(1)} %sum_0.1.refs_3_.refs_0_, bf16[256,384]{1,0:T(8,128)(2,1)S(1)} %get-tuple-element.45.refs_1_, bf16[256,384]{1,0:T(8,128)(2,1)S(1)} %sum_2.1.refs_2_, f32[256,128]{1,0:T(8,128)S(1)} %get-tuple-element.51.refs_4_.refs_3_, ...), custom_call_target="tpu_custom_call" | custom-call | tf_op jit(solution)/shard_map/end/pallas_call | solution.py:343
  (29 shorter events, 3.6 us)
Async XLA Ops:
  3.7 5.8 %collective-permute-start.2 = (bf16[384,896]{1,0:T(8,128)(2,1)S(1)}, bf16[384,896]{1,0:T(8,128)(2,1)S(1)}, u32[]{:S(2)}, u32[]{:S(2)}) collective-permute-start(bf16[384,896]{1,0:T(8,128)(2,1)S(1)} %get-tuple-element.33.refs_0_), channel_id=1, source_target_pairs={{0,1},{1,0},{2,3},{3,2},{4,5},{5,4},{6,7},{7,6},{8,9},{9,8},{10,11... | collective-permute-start | bytes 2064392 | tf_op jit(solution)/shard_map/ppermute | solution.py:55
  4.2 1.9 %collective-permute-start = (bf16[384,128]{1,0:T(8,128)(2,1)S(1)}, bf16[384,128]{1,0:T(8,128)(2,1)S(1)}, u32[]{:S(2)}, u32[]{:S(2)}) collective-permute-start(bf16[384,128]{1,0:T(8,128)(2,1)S(1)} %get-tuple-element.30.refs_0_), channel_id=1, source_target_pairs={{0,1},{1,0},{2,3},{3,2},{4,5},{5,4},{6,7},{7,6},{8,9},{9,8},{10,11... | collective-permute-start | bytes 294920 | tf_op jit(solution)/shard_map/ppermute | solution.py:55
  6.4 6.2 %collective-permute-start.1 = (bf16[384,128]{1,0:T(8,128)(2,1)S(1)}, bf16[384,128]{1,0:T(8,128)(2,1)S(1)}, u32[]{:S(2)}, u32[]{:S(2)}) collective-permute-start(bf16[384,128]{1,0:T(8,128)(2,1)S(1)} %level1_0.1.refs_3_.refs_0_), channel_id=1, source_target_pairs={{0,2},{1,3},{2,0},{3,1},{4,6},{5,7},{6,4},{7,5},{8,10},{9,11},{10,... | collective-permute-start | bytes 294920 | tf_op jit(solution)/shard_map/ppermute | solution.py:55
  10.0 12.1 %collective-permute-start.4 = (bf16[384,384]{1,0:T(8,128)(2,1)S(1)}, bf16[384,384]{1,0:T(8,128)(2,1)S(1)}, u32[]{:S(2)}, u32[]{:S(2)}) collective-permute-start(bf16[384,384]{1,0:T(8,128)(2,1)S(1)} %level1_1.1.refs_3_.refs_0_), channel_id=1, source_target_pairs={{0,2},{1,3},{2,0},{3,1},{4,6},{5,7},{6,4},{7,5},{8,10},{9,11},{10,... | collective-permute-start | bytes 884744 | tf_op jit(solution)/shard_map/ppermute | solution.py:55
  13.0 11.3 %collective-permute-start.3 = (bf16[384,128]{1,0:T(8,128)(2,1)S(1)}, bf16[384,128]{1,0:T(8,128)(2,1)S(1)}, u32[]{:S(2)}, u32[]{:S(2)}) collective-permute-start(bf16[384,128]{1,0:T(8,128)(2,1)S(1)} %level2_0.1.refs_3_.refs_0_), channel_id=1, source_target_pairs={{0,4},{1,5},{2,6},{3,7},{4,0},{5,1},{6,2},{7,3},{8,12},{9,13},{10,... | collective-permute-start | bytes 294920 | tf_op jit(solution)/shard_map/ppermute | solution.py:55
  16.4 16.3 %collective-permute-start.9 = (bf16[384,384]{1,0:T(8,128)(2,1)S(1)}, bf16[384,384]{1,0:T(8,128)(2,1)S(1)}, u32[]{:S(2)}, u32[]{:S(2)}) collective-permute-start(bf16[384,384]{1,0:T(8,128)(2,1)S(1)} %level1_2.1.refs_3_.refs_0_), channel_id=1, source_target_pairs={{0,2},{1,3},{2,0},{3,1},{4,6},{5,7},{6,4},{7,5},{8,10},{9,11},{10,... | collective-permute-start | bytes 884744 | tf_op jit(solution)/shard_map/ppermute | solution.py:55
  22.6 21.3 %collective-permute-start.12 = (bf16[384,384]{1,0:T(8,128)(2,1)S(1)}, bf16[384,384]{1,0:T(8,128)(2,1)S(1)}, u32[]{:S(2)}, u32[]{:S(2)}) collective-permute-start(bf16[384,384]{1,0:T(8,128)(2,1)S(1)} %level2_1.1.refs_3_.refs_0_), channel_id=1, source_target_pairs={{0,4},{1,5},{2,6},{3,7},{4,0},{5,1},{6,2},{7,3},{8,12},{9,13},{10,... | collective-permute-start | bytes 884744 | tf_op jit(solution)/shard_map/ppermute | solution.py:55
  24.6 1.4 %collective-permute-start.5 = (bf16[384,128]{1,0:T(8,128)(2,1)S(1)}, bf16[384,128]{1,0:T(8,128)(2,1)S(1)}, u32[]{:S(2)}, u32[]{:S(2)}) collective-permute-start(bf16[384,128]{1,0:T(8,128)(2,1)S(1)} %level3_0.1.refs_0_), channel_id=1, source_target_pairs={{0,1},{1,0},{2,3},{3,2},{4,5},{5,4},{6,7},{7,6},{8,9},{9,8},{10,11... | collective-permute-start | bytes 294920 | tf_op jit(solution)/shard_map/ppermute | solution.py:55
  26.5 6.8 %collective-permute-start.6 = (bf16[256,128]{1,0:T(8,128)(2,1)S(1)}, bf16[256,128]{1,0:T(8,128)(2,1)S(1)}, u32[]{:S(2)}, u32[]{:S(2)}) collective-permute-start(bf16[256,128]{1,0:T(8,128)(2,1)S(1)} %get-tuple-element.38), channel_id=1, source_target_pairs={{0,24},{8,16},{16,8},{24,0},{1,25},{9,17},{17,9},{25,1},{2,26},{10... | collective-permute-start | bytes 196616 | tf_op jit(solution)/shard_map/ppermute | solution.py:55
  29.0 4.3 %collective-permute-start.7 = (bf16[256,128]{1,0:T(8,128)(2,1)S(1)}, bf16[256,128]{1,0:T(8,128)(2,1)S(1)}, u32[]{:S(2)}, u32[]{:S(2)}) collective-permute-start(bf16[256,128]{1,0:T(8,128)(2,1)S(1)} %get-tuple-element.39), channel_id=1, source_target_pairs={{0,16},{8,24},{16,0},{24,8},{1,17},{9,25},{17,1},{25,9},{2,18},{10... | collective-permute-start | bytes 196616 | tf_op jit(solution)/shard_map/ppermute | solution.py:55
  29.5 4.3 %collective-permute-start.8 = (bf16[256,128]{1,0:T(8,128)(2,1)S(1)}, bf16[256,128]{1,0:T(8,128)(2,1)S(1)}, u32[]{:S(2)}, u32[]{:S(2)}) collective-permute-start(bf16[256,128]{1,0:T(8,128)(2,1)S(1)} %get-tuple-element.40), channel_id=1, source_target_pairs={{0,8},{8,0},{16,24},{24,16},{1,9},{9,1},{17,25},{25,17},{2,10},{10... | collective-permute-start | bytes 196616 | tf_op jit(solution)/shard_map/ppermute | solution.py:55
  33.3 18.0 %collective-permute-start.10 = (bf16[384,384]{1,0:T(8,128)(2,1)S(1)}, bf16[384,384]{1,0:T(8,128)(2,1)S(1)}, u32[]{:S(2)}, u32[]{:S(2)}) collective-permute-start(bf16[384,384]{1,0:T(8,128)(2,1)S(1)} %level2_2.1.refs_4_.refs_0_), channel_id=1, source_target_pairs={{0,4},{1,5},{2,6},{3,7},{4,0},{5,1},{6,2},{7,3},{8,12},{9,13},{10,... | collective-permute-start | bytes 884744 | tf_op jit(solution)/shard_map/ppermute | solution.py:55
  34.2 16.7 %collective-permute-start.11 = (bf16[384,128]{1,0:T(8,128)(2,1)S(1)}, bf16[384,128]{1,0:T(8,128)(2,1)S(1)}, u32[]{:S(2)}, u32[]{:S(2)}) collective-permute-start(bf16[384,128]{1,0:T(8,128)(2,1)S(1)} %level1_3.1.refs_3_.refs_0_), channel_id=1, source_target_pairs={{0,2},{1,3},{2,0},{3,1},{4,6},{5,7},{6,4},{7,5},{8,10},{9,11},{10,... | collective-permute-start | bytes 294920 | tf_op jit(solution)/shard_map/ppermute | solution.py:55
  44.4 1.6 %collective-permute-start.13 = (bf16[384,384]{1,0:T(8,128)(2,1)S(1)}, bf16[384,384]{1,0:T(8,128)(2,1)S(1)}, u32[]{:S(2)}, u32[]{:S(2)}) collective-permute-start(bf16[384,384]{1,0:T(8,128)(2,1)S(1)} %level3_1.1.refs_0_), channel_id=1, source_target_pairs={{0,1},{1,0},{2,3},{3,2},{4,5},{5,4},{6,7},{7,6},{8,9},{9,8},{10,11... | collective-permute-start | bytes 884744 | tf_op jit(solution)/shard_map/ppermute | solution.py:55
  47.0 8.9 %collective-permute-start.14 = (bf16[256,384]{1,0:T(8,128)(2,1)S(1)}, bf16[256,384]{1,0:T(8,128)(2,1)S(1)}, u32[]{:S(2)}, u32[]{:S(2)}) collective-permute-start(bf16[256,384]{1,0:T(8,128)(2,1)S(1)} %get-tuple-element.42), channel_id=1, source_target_pairs={{0,24},{8,16},{16,8},{24,0},{1,25},{9,17},{17,9},{25,1},{2,26},{10... | collective-permute-start | bytes 589832 | tf_op jit(solution)/shard_map/ppermute | solution.py:55
  50.2 9.4 %collective-permute-start.15 = (bf16[256,384]{1,0:T(8,128)(2,1)S(1)}, bf16[256,384]{1,0:T(8,128)(2,1)S(1)}, u32[]{:S(2)}, u32[]{:S(2)}) collective-permute-start(bf16[256,384]{1,0:T(8,128)(2,1)S(1)} %get-tuple-element.43), channel_id=1, source_target_pairs={{0,16},{8,24},{16,0},{24,8},{1,17},{9,25},{17,1},{25,9},{2,18},{10... | collective-permute-start | bytes 589832 | tf_op jit(solution)/shard_map/ppermute | solution.py:55
  50.7 9.2 %collective-permute-start.16 = (bf16[256,384]{1,0:T(8,128)(2,1)S(1)}, bf16[256,384]{1,0:T(8,128)(2,1)S(1)}, u32[]{:S(2)}, u32[]{:S(2)}) collective-permute-start(bf16[256,384]{1,0:T(8,128)(2,1)S(1)} %get-tuple-element.44), channel_id=1, source_target_pairs={{0,8},{8,0},{16,24},{24,16},{1,9},{9,1},{17,25},{25,17},{2,10},{10... | collective-permute-start | bytes 589832 | tf_op jit(solution)/shard_map/ppermute | solution.py:55
  51.2 13.7 %collective-permute-start.21 = (bf16[384,128]{1,0:T(8,128)(2,1)S(1)}, bf16[384,128]{1,0:T(8,128)(2,1)S(1)}, u32[]{:S(2)}, u32[]{:S(2)}) collective-permute-start(bf16[384,128]{1,0:T(8,128)(2,1)S(1)} %level2_3.1.refs_3_.refs_0_), channel_id=1, source_target_pairs={{0,4},{1,5},{2,6},{3,7},{4,0},{5,1},{6,2},{7,3},{8,12},{9,13},{10,... | collective-permute-start | bytes 294920 | tf_op jit(solution)/shard_map/ppermute | solution.py:55
  51.8 8.5 %collective-permute-start.17 = (bf16[384,384]{1,0:T(8,128)(2,1)S(1)}, bf16[384,384]{1,0:T(8,128)(2,1)S(1)}, u32[]{:S(2)}, u32[]{:S(2)}) collective-permute-start(bf16[384,384]{1,0:T(8,128)(2,1)S(1)} %level3_2.1.refs_0_), channel_id=1, source_target_pairs={{0,1},{1,0},{2,3},{3,2},{4,5},{5,4},{6,7},{7,6},{8,9},{9,8},{10,11... | collective-permute-start | bytes 884744 | tf_op jit(solution)/shard_map/ppermute | solution.py:55
  61.3 8.9 %collective-permute-start.18 = (bf16[256,384]{1,0:T(8,128)(2,1)S(1)}, bf16[256,384]{1,0:T(8,128)(2,1)S(1)}, u32[]{:S(2)}, u32[]{:S(2)}) collective-permute-start(bf16[256,384]{1,0:T(8,128)(2,1)S(1)} %get-tuple-element.48), channel_id=1, source_target_pairs={{0,24},{8,16},{16,8},{24,0},{1,25},{9,17},{17,9},{25,1},{2,26},{10... | collective-permute-start | bytes 589832 | tf_op jit(solution)/shard_map/ppermute | solution.py:55
  63.0 10.9 %collective-permute-start.19 = (bf16[256,384]{1,0:T(8,128)(2,1)S(1)}, bf16[256,384]{1,0:T(8,128)(2,1)S(1)}, u32[]{:S(2)}, u32[]{:S(2)}) collective-permute-start(bf16[256,384]{1,0:T(8,128)(2,1)S(1)} %get-tuple-element.49), channel_id=1, source_target_pairs={{0,16},{8,24},{16,0},{24,8},{1,17},{9,25},{17,1},{25,9},{2,18},{10... | collective-permute-start | bytes 589832 | tf_op jit(solution)/shard_map/ppermute | solution.py:55
  64.4 9.9 %collective-permute-start.20 = (bf16[256,384]{1,0:T(8,128)(2,1)S(1)}, bf16[256,384]{1,0:T(8,128)(2,1)S(1)}, u32[]{:S(2)}, u32[]{:S(2)}) collective-permute-start(bf16[256,384]{1,0:T(8,128)(2,1)S(1)} %get-tuple-element.50), channel_id=1, source_target_pairs={{0,8},{8,0},{16,24},{24,16},{1,9},{9,1},{17,25},{25,17},{2,10},{10... | collective-permute-start | bytes 589832 | tf_op jit(solution)/shard_map/ppermute | solution.py:55
  65.2 1.4 %collective-permute-start.22 = (bf16[384,128]{1,0:T(8,128)(2,1)S(1)}, bf16[384,128]{1,0:T(8,128)(2,1)S(1)}, u32[]{:S(2)}, u32[]{:S(2)}) collective-permute-start(bf16[384,128]{1,0:T(8,128)(2,1)S(1)} %level3_3.1.refs_0_), channel_id=1, source_target_pairs={{0,1},{1,0},{2,3},{3,2},{4,5},{5,4},{6,7},{7,6},{8,9},{9,8},{10,11... | collective-permute-start | bytes 294920 | tf_op jit(solution)/shard_map/ppermute | solution.py:55
  67.2 8.1 %collective-permute-start.23 = (bf16[256,128]{1,0:T(8,128)(2,1)S(1)}, bf16[256,128]{1,0:T(8,128)(2,1)S(1)}, u32[]{:S(2)}, u32[]{:S(2)}) collective-permute-start(bf16[256,128]{1,0:T(8,128)(2,1)S(1)} %get-tuple-element.52), channel_id=1, source_target_pairs={{0,24},{8,16},{16,8},{24,0},{1,25},{9,17},{17,9},{25,1},{2,26},{10... | collective-permute-start | bytes 196616 | tf_op jit(solution)/shard_map/ppermute | solution.py:55
  68.8 7.0 %collective-permute-start.24 = (bf16[256,128]{1,0:T(8,128)(2,1)S(1)}, bf16[256,128]{1,0:T(8,128)(2,1)S(1)}, u32[]{:S(2)}, u32[]{:S(2)}) collective-permute-start(bf16[256,128]{1,0:T(8,128)(2,1)S(1)} %get-tuple-element.53), channel_id=1, source_target_pairs={{0,16},{8,24},{16,0},{24,8},{1,17},{9,25},{17,1},{25,9},{2,18},{10... | collective-permute-start | bytes 196616 | tf_op jit(solution)/shard_map/ppermute | solution.py:55
  70.3 5.9 %collective-permute-start.25 = (bf16[256,128]{1,0:T(8,128)(2,1)S(1)}, bf16[256,128]{1,0:T(8,128)(2,1)S(1)}, u32[]{:S(2)}, u32[]{:S(2)}) collective-permute-start(bf16[256,128]{1,0:T(8,128)(2,1)S(1)} %get-tuple-element.54), channel_id=1, source_target_pairs={{0,8},{8,0},{16,24},{24,16},{1,9},{9,1},{17,25},{25,17},{2,10},{10... | collective-permute-start | bytes 196616 | tf_op jit(solution)/shard_map/ppermute | solution.py:55

commit v20 on v19

--- a/solution.py
+++ b/solution.py
@@ -7,7 +7,7 @@
 from jax.experimental.pallas import tpu as pltpu
 from jax.sharding import PartitionSpec as P
 
-SHARES = (1, 3, 3, 1)
+SHARES = (1, 2, 3, 2)
 PRELOADED = 2
 COST = 6 * 10**9
 BF16 = jnp.bfloat16
@@ -151,25 +151,46 @@
     refs[-1][...] = total.astype(BF16)
 
 
-def between_kernel(bit, parts, counts, own, weights, *refs):
+def between_kernel(bit, parts, counts, folds, own, weights, *refs):
     refs = list(refs)
     groups = [[refs.pop(0) for _ in range(count)] for count in counts]
+    held = [refs.pop(0) for _ in range(2 * folds)]
     partial = refs.pop(0)
     for s, start, stop in parts:
         partial[:, start:stop] = half_dot(weights, s, upper_half(bit), own[:, start:stop])
-    for group, out in zip(groups, refs):
-        sum_kernel(*group, out)
-
-
-def last_kernel(bit, parts, partial, other, weights, basis, *refs):
-    rows = refs[0].shape[0]
+    for group in groups:
+        sum_kernel(*group, refs.pop(0))
+    fold_kernel(*held, *refs)
+
+
+def fold_kernel(*refs):
+    half = len(refs) // 2
+    for at in range(0, half, 2):
+        keep, got, rest, send = refs[at], refs[at + 1], refs[half + at], refs[half + at + 1]
+        rows = rest.shape[0]
+        rest[...] = keep[:rows] + got[:rows].astype(F32)
+        send[...] = (keep[rows:] + got[rows:].astype(F32)).astype(BF16)
+
+
+def join_kernel(*refs):
+    out, row = refs[-1], 0
+    for keep, got in zip(refs[:-1:2], refs[1:-1:2]):
+        out[row : row + keep.shape[0], :] = (keep[...] + got[...].astype(F32)).astype(BF16)
+        row += keep.shape[0]
+
+
+def last_kernel(bit, parts, homes, partial, other, weights, basis, *refs):
+    rows = basis.shape[1] // lax.axis_size("blk")
     me = lax.axis_index("blk")
     for s, start, stop in parts:
         mixed = partial[:, start:stop] + half_dot(weights, s, 1 - upper_half(bit), other[:, start:stop])
         coeff = mixed.astype(BF16)
-        for d, ref in enumerate(refs):
+        for d, home in enumerate(homes):
             row = pl.multiple_of((me ^ d) * rows, rows)
-            ref[:, start:stop] = dot(basis[s, pl.ds(row, rows), :], coeff).astype(ref.dtype)
+            piece = dot(basis[s, pl.ds(row, rows), :], coeff)
+            for begin, size, at, to in home:
+                ref = refs[at]
+                ref[to : to + size, start:stop] = piece[begin : begin + size].astype(ref.dtype)
 
 
 def end_kernel(places, counts, *refs):
@@ -286,30 +307,75 @@
     (value,) = step("level2_1", [(2, 1, coeff2[1], near2[1])], [basis_v])
     third(1, value)
 
-    def tail(j, after, arrived=()):
+    masks = [1 << b for b in range(n_blk.bit_length() - 1)]
+    orders = [masks, masks[::-1]]
+    half = rows // 2
+    whole = [[(0, rows, d, 0)] for d in range(n_blk)]
+    halved = [[] for _ in range(n_blk)]
+    for side, order in enumerate(orders):
+        pieces = [0]
+        for mask in order[::-1]:
+            pieces = pieces + [d | mask for d in pieces]
+        for at, d in enumerate(pieces):
+            sent, to = divmod(at, n_blk // 2)
+            halved[d].append((side * half, half, 2 * side + sent, to * half))
+
+    def halves(j, count):
+        shape = (count * half, widths[j])
+        return [in_vmem(*shape, dtype=kind) for _ in orders for kind in (F32, BF16)]
+
+    def exchange(values, at):
+        return [
+            v
+            for side, order in enumerate(orders)
+            for v in (values[2 * side], partner(values[2 * side + 1], "blk", order[at]))
+        ]
+
+    def begin_sum(j, out):
+        held, count = exchange(out, 0), n_blk // 2
+        for at in range(1, len(masks) - 1):
+            count //= 2
+            out = call(
+                fold_kernel, f"fold_{j}_{at}", [VMEM] * 4, halves(j, count), [], [here(v) for v in held]
+            )
+            held = exchange(out, at)
+        return held
+
+    def tail(j, after, arrived=(), folding=(), halving=False):
         (coeff4,) = step(f"level3_{j}", [(3, j, coeff3[j], near3[j])], after)
         near4 = cross(4, coeff4)
-        partial, *totals = call(
-            functools.partial(between_kernel, bits[4], parts[j], [len(group) for _, group in arrived]),
+        held = folding[1] if folding else []
+        extra = [v for _, group in arrived for v in group] + held
+        partial, *more = call(
+            functools.partial(
+                between_kernel, bits[4], parts[j], [len(group) for _, group in arrived], len(held) // 2
+            ),
             f"between_{j}",
-            [VMEM] * (2 + sum(len(group) for _, group in arrived)),
-            [in_vmem(rank, widths[j], dtype=F32)] + [in_vmem(rows, widths[at]) for at, _ in arrived],
+            [VMEM] * (2 + len(extra)),
+            [in_vmem(rank, widths[j], dtype=F32)]
+            + [in_vmem(rows, widths[at]) for at, _ in arrived]
+            + (halves(folding[0], 1) if folding else []),
             [],
-            [here(v) for v in (coeff4, weights[4], *(v for _, group in arrived for v in group))],
+            [here(v) for v in (coeff4, weights[4], *extra)],
         )
+        if halving:
+            outs = halves(j, n_blk // 2)
+        else:
+            outs = [in_vmem(rows, widths[j], dtype=BF16 if d else F32) for d in range(n_blk)]
         out = call(
-            functools.partial(last_kernel, bits[4], parts[j]),
+            functools.partial(last_kernel, bits[4], parts[j], halved if halving else whole),
             f"last_{j}",
             [VMEM] * 4,
-            [in_vmem(rows, widths[j], dtype=F32)] + [in_vmem(rows, widths[j])] * (n_blk - 1),
+            outs,
             [],
             [here(v) for v in (partial, near4, weights[4], basis_v)],
             flops=COST if j < len(widths) - 1 else 0,
         )
-        group = [out[0]] + [partner(out[d], "blk", d) for d in range(n_blk - 1, 0, -1)]
-        return group, totals
-
-    group0, _ = tail(0, [coeff3[1]])
+        if halving:
+            return out, begin_sum(j, out), more
+        return out, [out[0]] + [partner(out[d], "blk", d) for d in range(n_blk - 1, 0, -1)], more
+
+    _, group0, _ = tail(0, [coeff3[1]])
     (value,) = step("level2_2", [(2, 2, coeff2[2], near2[2])], [group0[0]])
     third(2, value)
     (total0,) = call(
@@ -323,20 +389,20 @@
     )
     (value,) = step("level1_3", [job1(3)], [total0])
     second(3, value)
-    group1, _ = tail(1, [coeff2[3]])
+    _, group1, _ = tail(1, [coeff2[3]])
     (value,) = step("level2_3", [(2, 3, coeff2[3], near2[3])], [group1[0]])
     third(3, value)
-    group2, (total1,) = tail(2, [coeff3[3]], [(1, group1)])
-    group3, _ = tail(3, [group2[0]])
+    out2, held2, (total1,) = tail(2, [coeff3[3]], [(1, group1)], halving=True)
+    out3, group3, more = tail(3, [out2[0]], folding=(2, held2))
+    held2 = exchange(more, len(masks) - 1)
     (total2,) = call(
-        sum_kernel,
+        join_kernel,
         "sum_2",
-        [VMEM] * n_blk,
+        [VMEM] * 4,
         [in_vmem(rows, widths[2])],
         [],
-        [here(v) for v in group2],
-        [group3[0]],
-        0,
+        [here(v) for v in held2],
+        [out3[0]],
     )
     groups = [[total0], [total1], [total2], group3]
     flat = [here(v) for group in groups for v in group]

time: 77.2 us -> 71.6 us (0.927)
  waiting for transfers between devices: 31.3 us -> 22 us
  starting transfers between devices: 28.9 us -> 32.8 us
    ppermute x26 -> x27, waiting for transfers between devices: 31.3 us -> 22 us  [partner(): return lax.ppermute(value, axis, pairs)]
    ppermute x26 -> x27, starting transfers between devices: 28.9 us -> 32.8 us  [partner(): return lax.ppermute(value, axis, pairs)]
  transfers between devices with their start and end apart: 26 -> 27, of which waited for: 17 -> 15; matrix products, arithmetic and copies ran while one was open for 0% -> 0% of each run, Pallas kernels for 16% -> 17%
where the time goes in v20:
time: 71.6 us; the launch traced here: 71.4 us
  starting transfers between devices  32.8 us (46%)
  waiting for transfers between devices  22 us (31%)
  Pallas kernels  16.4 us (23%)
    ppermute x27, starting transfers between devices, partner(): return lax.ppermute(value, axis, pairs)  32.8 us
    ppermute x27, waiting for transfers between devices, partner(): return lax.ppermute(value, axis, pairs)  22 us
    pallas_call x24, Pallas kernels, call(): pl.pallas_call(body, name=name, in_specs=[*in_specs, *[ANY] * len(after)]...  15.5 us
  transfers between devices with their start and end apart: 27, of which 15 were waited for; matrix products, arithmetic and copies ran while one was open for 0% of the time, Pallas kernels for 17%

profile of v20, /device:TPU:0, one launch (start us, length us, event | category | flops | bytes accessed | tf_op | source)
XLA Modules:
  0.0 71.4 jit_solution(2056167171680161032)
XLA Ops:
  0.0 3.7 %leaf.1 = (bf16[384,128]{1,0:T(8,128)(2,1)S(1)}, bf16[384,896]{1,0:T(8,128)(2,1)S(1)}, bf16[2,384,768]{2,1,0:T(8,128)(2,1)S(1)}, bf16[2,384,768]{2,1,0:T(8,128)(2,1)S(1)}) custom-call(bf16[2,1024,512]{2,1,0:T(8,128)(2,1)} %bitcast.9, bf16[2,384,1024]{2,1,0:T(8,128)(2,1)} %bitcast.10, bf16[5,2,384,768]{3,2,1,0:T(8,128)(2,1)} %bitcast.7, s32[2,5]{1,0:T(2,128)} %bitcast.12), custom_call_target="tpu_custom_call" | custom-call | flops 6000000000 | tf_op jit(solution)/shard_map/leaf/pallas_call | solution.py:41
  3.7 0.5 collective-permute-start.2
  4.3 1.8 %collective-permute-done.refs_1_ = bf16[384,128]{1,0:T(8,128)(2,1)S(1)} collective-permute-done((bf16[384,128]{1,0:T(8,128)(2,1)S(1)}, bf16[384,128]{1,0:T(8,128)(2,1)S(1)}, u32[]{:S(2)}, u32[]{:S(2)}) %collective-permute-start) | collective-permute-done | bytes 98336 | tf_op jit(solution)/shard_map/ppermute | solution.py:55
  6.4 3.0 %collective-permute-start.1 = (bf16[384,128]{1,0:T(8,128)(2,1)S(1)}, bf16[384,128]{1,0:T(8,128)(2,1)S(1)}, u32[]{:S(2)}, u32[]{:S(2)}) collective-permute-start(bf16[384,128]{1,0:T(8,128)(2,1)S(1)} %level1_0.1.refs_3_.refs_0_), channel_id=1, source_target_pairs={{0,2},{1,3},{2,0},{3,1},{4,6},{5,7},{6,4},{7,5},{8,10},{9,11},{10,... | collective-permute-start | bytes 294920 | tf_op jit(solution)/shard_map/ppermute | solution.py:55
  9.5 0.4 level1_1.1.refs_3_.refs_0_
  9.9 2.8 %collective-permute-done.1.refs_1_ = bf16[384,128]{1,0:T(8,128)(2,1)S(1)} collective-permute-done((bf16[384,128]{1,0:T(8,128)(2,1)S(1)}, bf16[384,128]{1,0:T(8,128)(2,1)S(1)}, u32[]{:S(2)}, u32[]{:S(2)}) %collective-permute-start.1) | collective-permute-done | bytes 98336 | tf_op jit(solution)/shard_map/ppermute | solution.py:55
  13.1 3.0 %collective-permute-start.3 = (bf16[384,128]{1,0:T(8,128)(2,1)S(1)}, bf16[384,128]{1,0:T(8,128)(2,1)S(1)}, u32[]{:S(2)}, u32[]{:S(2)}) collective-permute-start(bf16[384,128]{1,0:T(8,128)(2,1)S(1)} %level2_0.1.refs_3_.refs_0_), channel_id=1, source_target_pairs={{0,4},{1,5},{2,6},{3,7},{4,0},{5,1},{6,2},{7,3},{8,12},{9,13},{10,... | collective-permute-start | bytes 294920 | tf_op jit(solution)/shard_map/ppermute | solution.py:55
  16.1 0.5 level1_2.1.refs_3_.refs_0_
  16.6 2.0 %collective-permute-start.9 = (bf16[384,384]{1,0:T(8,128)(2,1)S(1)}, bf16[384,384]{1,0:T(8,128)(2,1)S(1)}, u32[]{:S(2)}, u32[]{:S(2)}) collective-permute-start(bf16[384,384]{1,0:T(8,128)(2,1)S(1)} %level1_2.1.refs_3_.refs_0_), channel_id=1, source_target_pairs={{0,2},{1,3},{2,0},{3,1},{4,6},{5,7},{6,4},{7,5},{8,10},{9,11},{10,... | collective-permute-start | bytes 884744 | tf_op jit(solution)/shard_map/ppermute | solution.py:55
  18.7 2.5 %prefetch.1 = (bf16[2,384,768]{2,1,0:T(8,128)(2,1)S(1)}, bf16[2,384,768]{2,1,0:T(8,128)(2,1)S(1)}, bf16[2,1024,384]{2,1,0:T(8,128)(2,1)S(1)}) custom-call(bf16[5,2,384,768]{3,2,1,0:T(8,128)(2,1)} %bitcast.8, bf16[2,1024,384]{2,1,0:T(8,128)(2,1)} %bitcast.11, s32[2,5]{1,0:T(2,128)} %bitcast.13, bf16[384,384]{1,0:T(8,128)(2,1)S(1)} %level1_2.1.refs_3_.refs_0_), custom_call_target="tpu_custom_call" | custom-call | flops 6000000000 | tf_op jit(solution)/shard_map/prefetch/pallas_call | solution.py:41
  21.6 0.4 collective-permute-start.12
  22.6 1.0 %collective-permute-done.5.refs_1_ = bf16[384,128]{1,0:T(8,128)(2,1)S(1)} collective-permute-done((bf16[384,128]{1,0:T(8,128)(2,1)S(1)}, bf16[384,128]{1,0:T(8,128)(2,1)S(1)}, u32[]{:S(2)}, u32[]{:S(2)}) %collective-permute-start.5) | collective-permute-done | bytes 98336 | tf_op jit(solution)/shard_map/ppermute | solution.py:55
  23.7 0.6 last_0.1
  24.3 2.5 %collective-permute-start.6 = (bf16[256,128]{1,0:T(8,128)(2,1)S(1)}, bf16[256,128]{1,0:T(8,128)(2,1)S(1)}, u32[]{:S(2)}, u32[]{:S(2)}) collective-permute-start(bf16[256,128]{1,0:T(8,128)(2,1)S(1)} %get-tuple-element.43), channel_id=1, source_target_pairs={{0,24},{8,16},{16,8},{24,0},{1,25},{9,17},{17,9},{25,1},{2,26},{10... | collective-permute-start | bytes 196616 | tf_op jit(solution)/shard_map/ppermute | solution.py:55
  26.8 0.5 collective-permute-start.7
  27.3 0.5 collective-permute-start.8
  27.8 0.9 %collective-permute-done.9.refs_1_ = bf16[384,384]{1,0:T(8,128)(2,1)S(1)} collective-permute-done((bf16[384,384]{1,0:T(8,128)(2,1)S(1)}, bf16[384,384]{1,0:T(8,128)(2,1)S(1)}, u32[]{:S(2)}, u32[]{:S(2)}) %collective-permute-start.9) | collective-permute-done | bytes 294944 | tf_op jit(solution)/shard_map/ppermute | solution.py:55
  28.7 0.5 level2_2.1.refs_4_.refs_0_
  29.2 2.0 %collective-permute-start.10 = (bf16[384,384]{1,0:T(8,128)(2,1)S(1)}, bf16[384,384]{1,0:T(8,128)(2,1)S(1)}, u32[]{:S(2)}, u32[]{:S(2)}) collective-permute-start(bf16[384,384]{1,0:T(8,128)(2,1)S(1)} %level2_2.1.refs_4_.refs_0_), channel_id=1, source_target_pairs={{0,4},{1,5},{2,6},{3,7},{4,0},{5,1},{6,2},{7,3},{8,12},{9,13},{10,... | collective-permute-start | bytes 884744 | tf_op jit(solution)/shard_map/ppermute | solution.py:55
  31.2 0.4 collective-permute-done.8.refs_3_
  31.6 0.4 level1_3.1.refs_3_.refs_0_
  32.0 2.2 %collective-permute-start.11 = (bf16[384,256]{1,0:T(8,128)(2,1)S(1)}, bf16[384,256]{1,0:T(8,128)(2,1)S(1)}, u32[]{:S(2)}, u32[]{:S(2)}) collective-permute-start(bf16[384,256]{1,0:T(8,128)(2,1)S(1)} %level1_3.1.refs_3_.refs_0_), channel_id=1, source_target_pairs={{0,2},{1,3},{2,0},{3,1},{4,6},{5,7},{6,4},{7,5},{8,10},{9,11},{10,... | collective-permute-start | bytes 589832 | tf_op jit(solution)/shard_map/ppermute | solution.py:55
  34.2 0.4 level3_1.1.refs_0_
  34.9 1.2 %collective-permute-done.13.refs_1_ = bf16[384,256]{1,0:T(8,128)(2,1)S(1)} collective-permute-done((bf16[384,256]{1,0:T(8,128)(2,1)S(1)}, bf16[384,256]{1,0:T(8,128)(2,1)S(1)}, u32[]{:S(2)}, u32[]{:S(2)}) %collective-permute-start.13) | collective-permute-done | bytes 196640 | tf_op jit(solution)/shard_map/ppermute | solution.py:55
  36.1 0.8 %last_1.1 = (f32[256,256]{1,0:T(8,128)S(1)}, bf16[256,256]{1,0:T(8,128)(2,1)S(1)}, bf16[256,256]{1,0:T(8,128)(2,1)S(1)}, bf16[256,256]{1,0:T(8,128)(2,1)S(1)}) custom-call(f32[384,256]{1,0:T(8,128)S(1)} %between_1.1.refs_0_, bf16[384,256]{1,0:T(8,128)(2,1)S(1)} %collective-permute-done.13.refs_1_, ...), custom_call_target="tpu_custom_call" | custom-call | flops 6000000000 | tf_op jit(solution)/shard_map/last_1/pallas_call | solution.py:41
  36.9 2.5 %collective-permute-start.14 = (bf16[256,256]{1,0:T(8,128)(2,1)S(1)}, bf16[256,256]{1,0:T(8,128)(2,1)S(1)}, u32[]{:S(2)}, u32[]{:S(2)}) collective-permute-start(bf16[256,256]{1,0:T(8,128)(2,1)S(1)} %get-tuple-element.47), channel_id=1, source_target_pairs={{0,24},{8,16},{16,8},{24,0},{1,25},{9,17},{17,9},{25,1},{2,26},{10... | collective-permute-start | bytes 393224 | tf_op jit(solution)/shard_map/ppermute | solution.py:55
  39.4 0.5 collective-permute-start.15
  39.9 0.5 collective-permute-start.16
  40.4 0.8 %collective-permute-done.11.refs_1_ = bf16[384,256]{1,0:T(8,128)(2,1)S(1)} collective-permute-done((bf16[384,256]{1,0:T(8,128)(2,1)S(1)}, bf16[384,256]{1,0:T(8,128)(2,1)S(1)}, u32[]{:S(2)}, u32[]{:S(2)}) %collective-permute-start.11) | collective-permute-done | bytes 196640 | tf_op jit(solution)/shard_map/ppermute | solution.py:55
  41.6 3.3 %collective-permute-start.17 = (bf16[384,256]{1,0:T(8,128)(2,1)S(1)}, bf16[384,256]{1,0:T(8,128)(2,1)S(1)}, u32[]{:S(2)}, u32[]{:S(2)}) collective-permute-start(bf16[384,256]{1,0:T(8,128)(2,1)S(1)} %level2_3.1.refs_3_.refs_0_), channel_id=1, source_target_pairs={{0,4},{1,5},{2,6},{3,7},{4,0},{5,1},{6,2},{7,3},{8,12},{9,13},{10,... | collective-permute-start | bytes 589832 | tf_op jit(solution)/shard_map/ppermute | solution.py:55
  44.9 2.8 %collective-permute-done.10.refs_1_ = bf16[384,384]{1,0:T(8,128)(2,1)S(1)} collective-permute-done((bf16[384,384]{1,0:T(8,128)(2,1)S(1)}, bf16[384,384]{1,0:T(8,128)(2,1)S(1)}, u32[]{:S(2)}, u32[]{:S(2)}) %collective-permute-start.10) | collective-permute-done | bytes 294944 | tf_op jit(solution)/shard_map/ppermute | solution.py:55
  47.7 0.5 level3_2.1.refs_0_
  48.3 0.4 between_2.1
  48.7 1.2 %collective-permute-done.18.refs_1_ = bf16[384,384]{1,0:T(8,128)(2,1)S(1)} collective-permute-done((bf16[384,384]{1,0:T(8,128)(2,1)S(1)}, bf16[384,384]{1,0:T(8,128)(2,1)S(1)}, u32[]{:S(2)}, u32[]{:S(2)}) %collective-permute-start.18) | collective-permute-done | bytes 294944 | tf_op jit(solution)/shard_map/ppermute | solution.py:55
  49.8 1.2 %last_2.1 = (f32[256,384]{1,0:T(8,128)S(1)}, bf16[256,384]{1,0:T(8,128)(2,1)S(1)}, f32[256,384]{1,0:T(8,128)S(1)}, bf16[256,384]{1,0:T(8,128)(2,1)S(1)}) custom-call(f32[384,384]{1,0:T(8,128)S(1)} %get-tuple-element.51.refs_0_, bf16[384,384]{1,0:T(8,128)(2,1)S(1)} %collective-permute-done.18.refs_1_, ...), custom_call_target="tpu_custom_call" | custom-call | flops 6000000000 | tf_op jit(solution)/shard_map/last_2/pallas_call | solution.py:41
  51.1 1.6 %collective-permute-start.19 = (bf16[256,384]{1,0:T(8,128)(2,1)S(1)}, bf16[256,384]{1,0:T(8,128)(2,1)S(1)}, u32[]{:S(2)}, u32[]{:S(2)}) collective-permute-start(bf16[256,384]{1,0:T(8,128)(2,1)S(1)} %get-tuple-element.53), channel_id=1, source_target_pairs={{0,8},{8,0},{16,24},{24,16},{1,9},{9,1},{17,25},{25,17},{2,10},{10... | collective-permute-start | bytes 589832 | tf_op jit(solution)/shard_map/ppermute | solution.py:55
  52.7 1.5 %collective-permute-start.20 = (bf16[256,384]{1,0:T(8,128)(2,1)S(1)}, bf16[256,384]{1,0:T(8,128)(2,1)S(1)}, u32[]{:S(2)}, u32[]{:S(2)}) collective-permute-start(bf16[256,384]{1,0:T(8,128)(2,1)S(1)} %get-tuple-element.55), channel_id=1, source_target_pairs={{0,16},{8,24},{16,0},{24,8},{1,17},{9,25},{17,1},{25,9},{2,18},{10... | collective-permute-start | bytes 589832 | tf_op jit(solution)/shard_map/ppermute | solution.py:55
  54.6 3.5 %collective-permute-done.19.refs_3_ = bf16[256,384]{1,0:T(8,128)(2,1)S(1)} collective-permute-done((bf16[256,384]{1,0:T(8,128)(2,1)S(1)}, bf16[256,384]{1,0:T(8,128)(2,1)S(1)}, u32[]{:S(2)}, u32[]{:S(2)}) %collective-permute-start.19) | collective-permute-done | bytes 196640 | tf_op jit(solution)/shard_map/ppermute | solution.py:55
  58.1 1.2 %collective-permute-done.20.refs_5_ = bf16[256,384]{1,0:T(8,128)(2,1)S(1)} collective-permute-done((bf16[256,384]{1,0:T(8,128)(2,1)S(1)}, bf16[256,384]{1,0:T(8,128)(2,1)S(1)}, u32[]{:S(2)}, u32[]{:S(2)}) %collective-permute-start.20) | collective-permute-done | bytes 196640 | tf_op jit(solution)/shard_map/ppermute | solution.py:55
  59.6 1.6 %collective-permute-start.21 = (bf16[128,384]{1,0:T(8,128)(2,1)S(1)}, bf16[128,384]{1,0:T(8,128)(2,1)S(1)}, u32[]{:S(2)}, u32[]{:S(2)}) collective-permute-start(bf16[128,384]{1,0:T(8,128)(2,1)S(1)} %get-tuple-element.57), channel_id=1, source_target_pairs={{0,16},{8,24},{16,0},{24,8},{1,17},{9,25},{17,1},{25,9},{2,18},{10... | collective-permute-start | bytes 294920 | tf_op jit(solution)/shard_map/ppermute | solution.py:55
  61.2 0.5 collective-permute-start.22
  61.7 0.8 %last_3.1 = (f32[256,256]{1,0:T(8,128)S(1)}, bf16[256,256]{1,0:T(8,128)(2,1)S(1)}, bf16[256,256]{1,0:T(8,128)(2,1)S(1)}, bf16[256,256]{1,0:T(8,128)(2,1)S(1)}) custom-call(f32[384,256]{1,0:T(8,128)S(1)} %get-tuple-element.60.refs_0_, bf16[384,256]{1,0:T(8,128)(2,1)S(1)} %collective-permute-done.23.refs_1_, ...), custom_call_target="tpu_custom_call" | custom-call | tf_op jit(solution)/shard_map/last_3/pallas_call | solution.py:41
  62.6 1.5 %collective-permute-start.24 = (bf16[256,256]{1,0:T(8,128)(2,1)S(1)}, bf16[256,256]{1,0:T(8,128)(2,1)S(1)}, u32[]{:S(2)}, u32[]{:S(2)}) collective-permute-start(bf16[256,256]{1,0:T(8,128)(2,1)S(1)} %get-tuple-element.62), channel_id=1, source_target_pairs={{0,24},{8,16},{16,8},{24,0},{1,25},{9,17},{17,9},{25,1},{2,26},{10... | collective-permute-start | bytes 393224 | tf_op jit(solution)/shard_map/ppermute | solution.py:55
  64.1 1.5 %collective-permute-start.25 = (bf16[256,256]{1,0:T(8,128)(2,1)S(1)}, bf16[256,256]{1,0:T(8,128)(2,1)S(1)}, u32[]{:S(2)}, u32[]{:S(2)}) collective-permute-start(bf16[256,256]{1,0:T(8,128)(2,1)S(1)} %get-tuple-element.63), channel_id=1, source_target_pairs={{0,16},{8,24},{16,0},{24,8},{1,17},{9,25},{17,1},{25,9},{2,18},{10... | collective-permute-start | bytes 393224 | tf_op jit(solution)/shard_map/ppermute | solution.py:55
  65.6 0.5 collective-permute-start.26
  66.3 3.6 %collective-permute-done.24.refs_4_ = bf16[256,256]{1,0:T(8,128)(2,1)S(1)} collective-permute-done((bf16[256,256]{1,0:T(8,128)(2,1)S(1)}, bf16[256,256]{1,0:T(8,128)(2,1)S(1)}, u32[]{:S(2)}, u32[]{:S(2)}) %collective-permute-start.24) | collective-permute-done | bytes 131104 | tf_op jit(solution)/shard_map/ppermute | solution.py:55
  69.9 0.4 collective-permute-done.25.refs_5_
  70.5 0.9 %end.1 = bf16[2,256,512]{2,1,0:T(8,128)(2,1)} custom-call(bf16[256,128]{1,0:T(8,128)(2,1)S(1)} %sum_0.1.refs_3_.refs_0_, bf16[256,256]{1,0:T(8,128)(2,1)S(1)} %get-tuple-element.50.refs_1_, bf16[256,384]{1,0:T(8,128)(2,1)S(1)} %sum_2.1.refs_2_, f32[256,256]{1,0:T(8,128)S(1)} %get-tuple-element.61.refs_4_.refs_3_, ...), custom_call_target="tpu_custom_call" | custom-call | tf_op jit(solution)/shard_map/end/pallas_call | solution.py:409
  (31 shorter events, 3.8 us)
Async XLA Ops:
  3.7 5.8 %collective-permute-start.2 = (bf16[384,896]{1,0:T(8,128)(2,1)S(1)}, bf16[384,896]{1,0:T(8,128)(2,1)S(1)}, u32[]{:S(2)}, u32[]{:S(2)}) collective-permute-start(bf16[384,896]{1,0:T(8,128)(2,1)S(1)} %get-tuple-element.38.refs_0_), channel_id=1, source_target_pairs={{0,1},{1,0},{2,3},{3,2},{4,5},{5,4},{6,7},{7,6},{8,9},{9,8},{10,11... | collective-permute-start | bytes 2064392 | tf_op jit(solution)/shard_map/ppermute | solution.py:55
  4.2 1.9 %collective-permute-start = (bf16[384,128]{1,0:T(8,128)(2,1)S(1)}, bf16[384,128]{1,0:T(8,128)(2,1)S(1)}, u32[]{:S(2)}, u32[]{:S(2)}) collective-permute-start(bf16[384,128]{1,0:T(8,128)(2,1)S(1)} %get-tuple-element.35.refs_0_), channel_id=1, source_target_pairs={{0,1},{1,0},{2,3},{3,2},{4,5},{5,4},{6,7},{7,6},{8,9},{9,8},{10,11... | collective-permute-start | bytes 294920 | tf_op jit(solution)/shard_map/ppermute | solution.py:55
  6.4 6.3 %collective-permute-start.1 = (bf16[384,128]{1,0:T(8,128)(2,1)S(1)}, bf16[384,128]{1,0:T(8,128)(2,1)S(1)}, u32[]{:S(2)}, u32[]{:S(2)}) collective-permute-start(bf16[384,128]{1,0:T(8,128)(2,1)S(1)} %level1_0.1.refs_3_.refs_0_), channel_id=1, source_target_pairs={{0,2},{1,3},{2,0},{3,1},{4,6},{5,7},{6,4},{7,5},{8,10},{9,11},{10,... | collective-permute-start | bytes 294920 | tf_op jit(solution)/shard_map/ppermute | solution.py:55
  9.8 11.4 %collective-permute-start.4 = (bf16[384,256]{1,0:T(8,128)(2,1)S(1)}, bf16[384,256]{1,0:T(8,128)(2,1)S(1)}, u32[]{:S(2)}, u32[]{:S(2)}) collective-permute-start(bf16[384,256]{1,0:T(8,128)(2,1)S(1)} %level1_1.1.refs_3_.refs_0_), channel_id=1, source_target_pairs={{0,2},{1,3},{2,0},{3,1},{4,6},{5,7},{6,4},{7,5},{8,10},{9,11},{10,... | collective-permute-start | bytes 589832 | tf_op jit(solution)/shard_map/ppermute | solution.py:55
  13.1 8.9 %collective-permute-start.3 = (bf16[384,128]{1,0:T(8,128)(2,1)S(1)}, bf16[384,128]{1,0:T(8,128)(2,1)S(1)}, u32[]{:S(2)}, u32[]{:S(2)}) collective-permute-start(bf16[384,128]{1,0:T(8,128)(2,1)S(1)} %level2_0.1.refs_3_.refs_0_), channel_id=1, source_target_pairs={{0,4},{1,5},{2,6},{3,7},{4,0},{5,1},{6,2},{7,3},{8,12},{9,13},{10,... | collective-permute-start | bytes 294920 | tf_op jit(solution)/shard_map/ppermute | solution.py:55
  16.6 12.1 %collective-permute-start.9 = (bf16[384,384]{1,0:T(8,128)(2,1)S(1)}, bf16[384,384]{1,0:T(8,128)(2,1)S(1)}, u32[]{:S(2)}, u32[]{:S(2)}) collective-permute-start(bf16[384,384]{1,0:T(8,128)(2,1)S(1)} %level1_2.1.refs_3_.refs_0_), channel_id=1, source_target_pairs={{0,2},{1,3},{2,0},{3,1},{4,6},{5,7},{6,4},{7,5},{8,10},{9,11},{10,... | collective-permute-start | bytes 884744 | tf_op jit(solution)/shard_map/ppermute | solution.py:55
  21.6 12.6 %collective-permute-start.12 = (bf16[384,256]{1,0:T(8,128)(2,1)S(1)}, bf16[384,256]{1,0:T(8,128)(2,1)S(1)}, u32[]{:S(2)}, u32[]{:S(2)}) collective-permute-start(bf16[384,256]{1,0:T(8,128)(2,1)S(1)} %level2_1.1.refs_3_.refs_0_), channel_id=1, source_target_pairs={{0,4},{1,5},{2,6},{3,7},{4,0},{5,1},{6,2},{7,3},{8,12},{9,13},{10,... | collective-permute-start | bytes 589832 | tf_op jit(solution)/shard_map/ppermute | solution.py:55
  22.3 1.4 %collective-permute-start.5 = (bf16[384,128]{1,0:T(8,128)(2,1)S(1)}, bf16[384,128]{1,0:T(8,128)(2,1)S(1)}, u32[]{:S(2)}, u32[]{:S(2)}) collective-permute-start(bf16[384,128]{1,0:T(8,128)(2,1)S(1)} %level3_0.1.refs_0_), channel_id=1, source_target_pairs={{0,1},{1,0},{2,3},{3,2},{4,5},{5,4},{6,7},{7,6},{8,9},{9,8},{10,11... | collective-permute-start | bytes 294920 | tf_op jit(solution)/shard_map/ppermute | solution.py:55
  24.3 7.0 %collective-permute-start.6 = (bf16[256,128]{1,0:T(8,128)(2,1)S(1)}, bf16[256,128]{1,0:T(8,128)(2,1)S(1)}, u32[]{:S(2)}, u32[]{:S(2)}) collective-permute-start(bf16[256,128]{1,0:T(8,128)(2,1)S(1)} %get-tuple-element.43), channel_id=1, source_target_pairs={{0,24},{8,16},{16,8},{24,0},{1,25},{9,17},{17,9},{25,1},{2,26},{10... | collective-permute-start | bytes 196616 | tf_op jit(solution)/shard_map/ppermute | solution.py:55
  26.8 4.4 %collective-permute-start.7 = (bf16[256,128]{1,0:T(8,128)(2,1)S(1)}, bf16[256,128]{1,0:T(8,128)(2,1)S(1)}, u32[]{:S(2)}, u32[]{:S(2)}) collective-permute-start(bf16[256,128]{1,0:T(8,128)(2,1)S(1)} %get-tuple-element.44), channel_id=1, source_target_pairs={{0,16},{8,24},{16,0},{24,8},{1,17},{9,25},{17,1},{25,9},{2,18},{10... | collective-permute-start | bytes 196616 | tf_op jit(solution)/shard_map/ppermute | solution.py:55
  27.3 4.3 %collective-permute-start.8 = (bf16[256,128]{1,0:T(8,128)(2,1)S(1)}, bf16[256,128]{1,0:T(8,128)(2,1)S(1)}, u32[]{:S(2)}, u32[]{:S(2)}) collective-permute-start(bf16[256,128]{1,0:T(8,128)(2,1)S(1)} %get-tuple-element.45), channel_id=1, source_target_pairs={{0,8},{8,0},{16,24},{24,16},{1,9},{9,1},{17,25},{25,17},{2,10},{10... | collective-permute-start | bytes 196616 | tf_op jit(solution)/shard_map/ppermute | solution.py:55
  29.2 18.5 %collective-permute-start.10 = (bf16[384,384]{1,0:T(8,128)(2,1)S(1)}, bf16[384,384]{1,0:T(8,128)(2,1)S(1)}, u32[]{:S(2)}, u32[]{:S(2)}) collective-permute-start(bf16[384,384]{1,0:T(8,128)(2,1)S(1)} %level2_2.1.refs_4_.refs_0_), channel_id=1, source_target_pairs={{0,4},{1,5},{2,6},{3,7},{4,0},{5,1},{6,2},{7,3},{8,12},{9,13},{10,... | collective-permute-start | bytes 884744 | tf_op jit(solution)/shard_map/ppermute | solution.py:55
  32.0 9.2 %collective-permute-start.11 = (bf16[384,256]{1,0:T(8,128)(2,1)S(1)}, bf16[384,256]{1,0:T(8,128)(2,1)S(1)}, u32[]{:S(2)}, u32[]{:S(2)}) collective-permute-start(bf16[384,256]{1,0:T(8,128)(2,1)S(1)} %level1_3.1.refs_3_.refs_0_), channel_id=1, source_target_pairs={{0,2},{1,3},{2,0},{3,1},{4,6},{5,7},{6,4},{7,5},{8,10},{9,11},{10,... | collective-permute-start | bytes 589832 | tf_op jit(solution)/shard_map/ppermute | solution.py:55
  34.5 1.5 %collective-permute-start.13 = (bf16[384,256]{1,0:T(8,128)(2,1)S(1)}, bf16[384,256]{1,0:T(8,128)(2,1)S(1)}, u32[]{:S(2)}, u32[]{:S(2)}) collective-permute-start(bf16[384,256]{1,0:T(8,128)(2,1)S(1)} %level3_1.1.refs_0_), channel_id=1, source_target_pairs={{0,1},{1,0},{2,3},{3,2},{4,5},{5,4},{6,7},{7,6},{8,9},{9,8},{10,11... | collective-permute-start | bytes 589832 | tf_op jit(solution)/shard_map/ppermute | solution.py:55
  36.9 11.4 %collective-permute-start.14 = (bf16[256,256]{1,0:T(8,128)(2,1)S(1)}, bf16[256,256]{1,0:T(8,128)(2,1)S(1)}, u32[]{:S(2)}, u32[]{:S(2)}) collective-permute-start(bf16[256,256]{1,0:T(8,128)(2,1)S(1)} %get-tuple-element.47), channel_id=1, source_target_pairs={{0,24},{8,16},{16,8},{24,0},{1,25},{9,17},{17,9},{25,1},{2,26},{10... | collective-permute-start | bytes 393224 | tf_op jit(solution)/shard_map/ppermute | solution.py:55
  39.4 8.9 %collective-permute-start.15 = (bf16[256,256]{1,0:T(8,128)(2,1)S(1)}, bf16[256,256]{1,0:T(8,128)(2,1)S(1)}, u32[]{:S(2)}, u32[]{:S(2)}) collective-permute-start(bf16[256,256]{1,0:T(8,128)(2,1)S(1)} %get-tuple-element.48), channel_id=1, source_target_pairs={{0,16},{8,24},{16,0},{24,8},{1,17},{9,25},{17,1},{25,9},{2,18},{10... | collective-permute-start | bytes 393224 | tf_op jit(solution)/shard_map/ppermute | solution.py:55
  39.9 8.4 %collective-permute-start.16 = (bf16[256,256]{1,0:T(8,128)(2,1)S(1)}, bf16[256,256]{1,0:T(8,128)(2,1)S(1)}, u32[]{:S(2)}, u32[]{:S(2)}) collective-permute-start(bf16[256,256]{1,0:T(8,128)(2,1)S(1)} %get-tuple-element.49), channel_id=1, source_target_pairs={{0,8},{8,0},{16,24},{24,16},{1,9},{9,1},{17,25},{25,17},{2,10},{10... | collective-permute-start | bytes 393224 | tf_op jit(solution)/shard_map/ppermute | solution.py:55
  41.6 12.6 %collective-permute-start.17 = (bf16[384,256]{1,0:T(8,128)(2,1)S(1)}, bf16[384,256]{1,0:T(8,128)(2,1)S(1)}, u32[]{:S(2)}, u32[]{:S(2)}) collective-permute-start(bf16[384,256]{1,0:T(8,128)(2,1)S(1)} %level2_3.1.refs_3_.refs_0_), channel_id=1, source_target_pairs={{0,4},{1,5},{2,6},{3,7},{4,0},{5,1},{6,2},{7,3},{8,12},{9,13},{10,... | collective-permute-start | bytes 589832 | tf_op jit(solution)/shard_map/ppermute | solution.py:55
  48.2 1.6 %collective-permute-start.18 = (bf16[384,384]{1,0:T(8,128)(2,1)S(1)}, bf16[384,384]{1,0:T(8,128)(2,1)S(1)}, u32[]{:S(2)}, u32[]{:S(2)}) collective-permute-start(bf16[384,384]{1,0:T(8,128)(2,1)S(1)} %level3_2.1.refs_0_), channel_id=1, source_target_pairs={{0,1},{1,0},{2,3},{3,2},{4,5},{5,4},{6,7},{7,6},{8,9},{9,8},{10,11... | collective-permute-start | bytes 884744 | tf_op jit(solution)/shard_map/ppermute | solution.py:55
  51.1 7.0 %collective-permute-start.19 = (bf16[256,384]{1,0:T(8,128)(2,1)S(1)}, bf16[256,384]{1,0:T(8,128)(2,1)S(1)}, u32[]{:S(2)}, u32[]{:S(2)}) collective-permute-start(bf16[256,384]{1,0:T(8,128)(2,1)S(1)} %get-tuple-element.53), channel_id=1, source_target_pairs={{0,8},{8,0},{16,24},{24,16},{1,9},{9,1},{17,25},{25,17},{2,10},{10... | collective-permute-start | bytes 589832 | tf_op jit(solution)/shard_map/ppermute | solution.py:55
  52.7 6.7 %collective-permute-start.20 = (bf16[256,384]{1,0:T(8,128)(2,1)S(1)}, bf16[256,384]{1,0:T(8,128)(2,1)S(1)}, u32[]{:S(2)}, u32[]{:S(2)}) collective-permute-start(bf16[256,384]{1,0:T(8,128)(2,1)S(1)} %get-tuple-element.55), channel_id=1, source_target_pairs={{0,16},{8,24},{16,0},{24,8},{1,17},{9,25},{17,1},{25,9},{2,18},{10... | collective-permute-start | bytes 589832 | tf_op jit(solution)/shard_map/ppermute | solution.py:55
  54.5 7.2 %collective-permute-start.23 = (bf16[384,256]{1,0:T(8,128)(2,1)S(1)}, bf16[384,256]{1,0:T(8,128)(2,1)S(1)}, u32[]{:S(2)}, u32[]{:S(2)}) collective-permute-start(bf16[384,256]{1,0:T(8,128)(2,1)S(1)} %level3_3.1.refs_0_), channel_id=1, source_target_pairs={{0,1},{1,0},{2,3},{3,2},{4,5},{5,4},{6,7},{7,6},{8,9},{9,8},{10,11... | collective-permute-start | bytes 589832 | tf_op jit(solution)/shard_map/ppermute | solution.py:55
  59.6 6.5 %collective-permute-start.21 = (bf16[128,384]{1,0:T(8,128)(2,1)S(1)}, bf16[128,384]{1,0:T(8,128)(2,1)S(1)}, u32[]{:S(2)}, u32[]{:S(2)}) collective-permute-start(bf16[128,384]{1,0:T(8,128)(2,1)S(1)} %get-tuple-element.57), channel_id=1, source_target_pairs={{0,16},{8,24},{16,0},{24,8},{1,17},{9,25},{17,1},{25,9},{2,18},{10... | collective-permute-start | bytes 294920 | tf_op jit(solution)/shard_map/ppermute | solution.py:55
  61.2 5.1 %collective-permute-start.22 = (bf16[128,384]{1,0:T(8,128)(2,1)S(1)}, bf16[128,384]{1,0:T(8,128)(2,1)S(1)}, u32[]{:S(2)}, u32[]{:S(2)}) collective-permute-start(bf16[128,384]{1,0:T(8,128)(2,1)S(1)} %get-tuple-element.59), channel_id=1, source_target_pairs={{0,8},{8,0},{16,24},{24,16},{1,9},{9,1},{17,25},{25,17},{2,10},{10... | collective-permute-start | bytes 294920 | tf_op jit(solution)/shard_map/ppermute | solution.py:55
  62.6 7.3 %collective-permute-start.24 = (bf16[256,256]{1,0:T(8,128)(2,1)S(1)}, bf16[256,256]{1,0:T(8,128)(2,1)S(1)}, u32[]{:S(2)}, u32[]{:S(2)}) collective-permute-start(bf16[256,256]{1,0:T(8,128)(2,1)S(1)} %get-tuple-element.62), channel_id=1, source_target_pairs={{0,24},{8,16},{16,8},{24,0},{1,25},{9,17},{17,9},{25,1},{2,26},{10... | collective-permute-start | bytes 393224 | tf_op jit(solution)/shard_map/ppermute | solution.py:55
  64.1 6.2 %collective-permute-start.25 = (bf16[256,256]{1,0:T(8,128)(2,1)S(1)}, bf16[256,256]{1,0:T(8,128)(2,1)S(1)}, u32[]{:S(2)}, u32[]{:S(2)}) collective-permute-start(bf16[256,256]{1,0:T(8,128)(2,1)S(1)} %get-tuple-element.63), channel_id=1, source_target_pairs={{0,16},{8,24},{16,0},{24,8},{1,17},{9,25},{17,1},{25,9},{2,18},{10... | collective-permute-start | bytes 393224 | tf_op jit(solution)/shard_map/ppermute | solution.py:55
  65.6 5.0 %collective-permute-start.26 = (bf16[256,256]{1,0:T(8,128)(2,1)S(1)}, bf16[256,256]{1,0:T(8,128)(2,1)S(1)}, u32[]{:S(2)}, u32[]{:S(2)}) collective-permute-start(bf16[256,256]{1,0:T(8,128)(2,1)S(1)} %get-tuple-element.64), channel_id=1, source_target_pairs={{0,8},{8,0},{16,24},{24,16},{1,9},{9,1},{17,25},{25,17},{2,10},{10... | collective-permute-start | bytes 393224 | tf_op jit(solution)/shard_map/ppermute | solution.py:55

commit v21 on v20

--- a/solution.py
+++ b/solution.py
@@ -393,7 +393,10 @@
     (value,) = step("level2_3", [(2, 3, coeff2[3], near2[3])], [group1[0]])
     third(3, value)
     out2, held2, (total1,) = tail(2, [coeff3[3]], [(1, group1)], halving=True)
-    out3, group3, more = tail(3, [out2[0]], folding=(2, held2))
+    out3, group3, _ = tail(3, [out2[0]])
+    more = call(
+        fold_kernel, "fold_2", [VMEM] * 4, halves(2, 1), [], [here(v) for v in held2], [out3[0]], 0
+    )
     held2 = exchange(more, len(masks) - 1)
     (total2,) = call(
         join_kernel,
@@ -403,6 +406,7 @@
         [],
         [here(v) for v in held2],
         [out3[0]],
+        0,
     )
     groups = [[total0], [total1], [total2], group3]
     flat = [here(v) for group in groups for v in group]

time: 71.6 us -> 69.5 us (0.971)
  waiting for transfers between devices: 22 us -> 19.4 us
    ppermute x27, waiting for transfers between devices: 22 us -> 19.4 us  [partner(): return lax.ppermute(value, axis, pairs)]
    pallas_call x24 -> x25, Pallas kernels: 15.5 us -> 15.5 us  [call(): pl.pallas_call(body, name=name, in_specs=[*in_specs, *[ANY] * len(after)]...]
  transfers between devices with their start and end apart: 27 -> 27, of which waited for: 15 -> 11; matrix products, arithmetic and copies ran while one was open for 0% -> 0% of each run, Pallas kernels for 17% -> 17%
where the time goes in v21:
time: 69.5 us; the launch traced here: 69.3 us
  starting transfers between devices  33.1 us (48%)
  waiting for transfers between devices  19.4 us (28%)
  Pallas kernels  16.4 us (24%)
    ppermute x27, starting transfers between devices, partner(): return lax.ppermute(value, axis, pairs)  33.1 us
    ppermute x27, waiting for transfers between devices, partner(): return lax.ppermute(value, axis, pairs)  19.4 us
    pallas_call x25, Pallas kernels, call(): pl.pallas_call(body, name=name, in_specs=[*in_specs, *[ANY] * len(after)]...  15.5 us
  transfers between devices with their start and end apart: 27, of which 11 were waited for; matrix products, arithmetic and copies ran while one was open for 0% of the time, Pallas kernels for 17%

profile of v21, /device:TPU:0, one launch (start us, length us, event | category | flops | bytes accessed | tf_op | source)
XLA Modules:
  0.0 69.3 jit_solution(11538951631061437567)
XLA Ops:
  0.0 3.7 %leaf.1 = (bf16[384,128]{1,0:T(8,128)(2,1)S(1)}, bf16[384,896]{1,0:T(8,128)(2,1)S(1)}, bf16[2,384,768]{2,1,0:T(8,128)(2,1)S(1)}, bf16[2,384,768]{2,1,0:T(8,128)(2,1)S(1)}) custom-call(bf16[2,1024,512]{2,1,0:T(8,128)(2,1)} %bitcast.9, bf16[2,384,1024]{2,1,0:T(8,128)(2,1)} %bitcast.10, bf16[5,2,384,768]{3,2,1,0:T(8,128)(2,1)} %bitcast.7, s32[2,5]{1,0:T(2,128)} %bitcast.12), custom_call_target="tpu_custom_call" | custom-call | flops 6000000000 | tf_op jit(solution)/shard_map/leaf/pallas_call | solution.py:41
  3.7 0.5 collective-permute-start.2
  4.3 1.8 %collective-permute-done.refs_1_ = bf16[384,128]{1,0:T(8,128)(2,1)S(1)} collective-permute-done((bf16[384,128]{1,0:T(8,128)(2,1)S(1)}, bf16[384,128]{1,0:T(8,128)(2,1)S(1)}, u32[]{:S(2)}, u32[]{:S(2)}) %collective-permute-start) | collective-permute-done | bytes 98336 | tf_op jit(solution)/shard_map/ppermute | solution.py:55
  6.4 3.0 %collective-permute-start.1 = (bf16[384,128]{1,0:T(8,128)(2,1)S(1)}, bf16[384,128]{1,0:T(8,128)(2,1)S(1)}, u32[]{:S(2)}, u32[]{:S(2)}) collective-permute-start(bf16[384,128]{1,0:T(8,128)(2,1)S(1)} %level1_0.1.refs_3_.refs_0_), channel_id=1, source_target_pairs={{0,2},{1,3},{2,0},{3,1},{4,6},{5,7},{6,4},{7,5},{8,10},{9,11},{10,... | collective-permute-start | bytes 294920 | tf_op jit(solution)/shard_map/ppermute | solution.py:55
  9.5 0.4 level1_1.1.refs_3_.refs_0_
  9.9 2.8 %collective-permute-done.1.refs_1_ = bf16[384,128]{1,0:T(8,128)(2,1)S(1)} collective-permute-done((bf16[384,128]{1,0:T(8,128)(2,1)S(1)}, bf16[384,128]{1,0:T(8,128)(2,1)S(1)}, u32[]{:S(2)}, u32[]{:S(2)}) %collective-permute-start.1) | collective-permute-done | bytes 98336 | tf_op jit(solution)/shard_map/ppermute | solution.py:55
  13.1 3.0 %collective-permute-start.3 = (bf16[384,128]{1,0:T(8,128)(2,1)S(1)}, bf16[384,128]{1,0:T(8,128)(2,1)S(1)}, u32[]{:S(2)}, u32[]{:S(2)}) collective-permute-start(bf16[384,128]{1,0:T(8,128)(2,1)S(1)} %level2_0.1.refs_3_.refs_0_), channel_id=1, source_target_pairs={{0,4},{1,5},{2,6},{3,7},{4,0},{5,1},{6,2},{7,3},{8,12},{9,13},{10,... | collective-permute-start | bytes 294920 | tf_op jit(solution)/shard_map/ppermute | solution.py:55
  16.1 0.5 level1_2.1.refs_3_.refs_0_
  16.6 2.0 %collective-permute-start.9 = (bf16[384,384]{1,0:T(8,128)(2,1)S(1)}, bf16[384,384]{1,0:T(8,128)(2,1)S(1)}, u32[]{:S(2)}, u32[]{:S(2)}) collective-permute-start(bf16[384,384]{1,0:T(8,128)(2,1)S(1)} %level1_2.1.refs_3_.refs_0_), channel_id=1, source_target_pairs={{0,2},{1,3},{2,0},{3,1},{4,6},{5,7},{6,4},{7,5},{8,10},{9,11},{10,... | collective-permute-start | bytes 884744 | tf_op jit(solution)/shard_map/ppermute | solution.py:55
  18.7 2.5 %prefetch.1 = (bf16[2,384,768]{2,1,0:T(8,128)(2,1)S(1)}, bf16[2,384,768]{2,1,0:T(8,128)(2,1)S(1)}, bf16[2,1024,384]{2,1,0:T(8,128)(2,1)S(1)}) custom-call(bf16[5,2,384,768]{3,2,1,0:T(8,128)(2,1)} %bitcast.8, bf16[2,1024,384]{2,1,0:T(8,128)(2,1)} %bitcast.11, s32[2,5]{1,0:T(2,128)} %bitcast.13, bf16[384,384]{1,0:T(8,128)(2,1)S(1)} %level1_2.1.refs_3_.refs_0_), custom_call_target="tpu_custom_call" | custom-call | flops 6000000000 | tf_op jit(solution)/shard_map/prefetch/pallas_call | solution.py:41
  21.2 0.4 level2_1.1.refs_3_.refs_0_
  21.6 0.4 collective-permute-start.12
  22.6 1.0 %collective-permute-done.5.refs_1_ = bf16[384,128]{1,0:T(8,128)(2,1)S(1)} collective-permute-done((bf16[384,128]{1,0:T(8,128)(2,1)S(1)}, bf16[384,128]{1,0:T(8,128)(2,1)S(1)}, u32[]{:S(2)}, u32[]{:S(2)}) %collective-permute-start.5) | collective-permute-done | bytes 98336 | tf_op jit(solution)/shard_map/ppermute | solution.py:55
  23.7 0.6 last_0.1
  24.3 2.5 %collective-permute-start.6 = (bf16[256,128]{1,0:T(8,128)(2,1)S(1)}, bf16[256,128]{1,0:T(8,128)(2,1)S(1)}, u32[]{:S(2)}, u32[]{:S(2)}) collective-permute-start(bf16[256,128]{1,0:T(8,128)(2,1)S(1)} %get-tuple-element.42), channel_id=1, source_target_pairs={{0,24},{8,16},{16,8},{24,0},{1,25},{9,17},{17,9},{25,1},{2,26},{10... | collective-permute-start | bytes 196616 | tf_op jit(solution)/shard_map/ppermute | solution.py:55
  26.8 0.5 collective-permute-start.7
  27.3 0.5 collective-permute-start.8
  27.8 0.9 %collective-permute-done.9.refs_1_ = bf16[384,384]{1,0:T(8,128)(2,1)S(1)} collective-permute-done((bf16[384,384]{1,0:T(8,128)(2,1)S(1)}, bf16[384,384]{1,0:T(8,128)(2,1)S(1)}, u32[]{:S(2)}, u32[]{:S(2)}) %collective-permute-start.9) | collective-permute-done | bytes 294944 | tf_op jit(solution)/shard_map/ppermute | solution.py:55
  28.7 0.5 level2_2.1.refs_4_.refs_0_
  29.2 2.0 %collective-permute-start.10 = (bf16[384,384]{1,0:T(8,128)(2,1)S(1)}, bf16[384,384]{1,0:T(8,128)(2,1)S(1)}, u32[]{:S(2)}, u32[]{:S(2)}) collective-permute-start(bf16[384,384]{1,0:T(8,128)(2,1)S(1)} %level2_2.1.refs_4_.refs_0_), channel_id=1, source_target_pairs={{0,4},{1,5},{2,6},{3,7},{4,0},{5,1},{6,2},{7,3},{8,12},{9,13},{10,... | collective-permute-start | bytes 884744 | tf_op jit(solution)/shard_map/ppermute | solution.py:55
  31.6 0.4 level1_3.1.refs_3_.refs_0_
  31.9 2.2 %collective-permute-start.11 = (bf16[384,256]{1,0:T(8,128)(2,1)S(1)}, bf16[384,256]{1,0:T(8,128)(2,1)S(1)}, u32[]{:S(2)}, u32[]{:S(2)}) collective-permute-start(bf16[384,256]{1,0:T(8,128)(2,1)S(1)} %level1_3.1.refs_3_.refs_0_), channel_id=1, source_target_pairs={{0,2},{1,3},{2,0},{3,1},{4,6},{5,7},{6,4},{7,5},{8,10},{9,11},{10,... | collective-permute-start | bytes 589832 | tf_op jit(solution)/shard_map/ppermute | solution.py:55
  34.2 0.4 level3_1.1.refs_0_
  34.9 1.2 %collective-permute-done.13.refs_1_ = bf16[384,256]{1,0:T(8,128)(2,1)S(1)} collective-permute-done((bf16[384,256]{1,0:T(8,128)(2,1)S(1)}, bf16[384,256]{1,0:T(8,128)(2,1)S(1)}, u32[]{:S(2)}, u32[]{:S(2)}) %collective-permute-start.13) | collective-permute-done | bytes 196640 | tf_op jit(solution)/shard_map/ppermute | solution.py:55
  36.1 0.8 %last_1.1 = (f32[256,256]{1,0:T(8,128)S(1)}, bf16[256,256]{1,0:T(8,128)(2,1)S(1)}, bf16[256,256]{1,0:T(8,128)(2,1)S(1)}, bf16[256,256]{1,0:T(8,128)(2,1)S(1)}) custom-call(f32[384,256]{1,0:T(8,128)S(1)} %between_1.1.refs_0_, bf16[384,256]{1,0:T(8,128)(2,1)S(1)} %collective-permute-done.13.refs_1_, ...), custom_call_target="tpu_custom_call" | custom-call | flops 6000000000 | tf_op jit(solution)/shard_map/last_1/pallas_call | solution.py:41
  36.9 2.5 %collective-permute-start.14 = (bf16[256,256]{1,0:T(8,128)(2,1)S(1)}, bf16[256,256]{1,0:T(8,128)(2,1)S(1)}, u32[]{:S(2)}, u32[]{:S(2)}) collective-permute-start(bf16[256,256]{1,0:T(8,128)(2,1)S(1)} %get-tuple-element.46), channel_id=1, source_target_pairs={{0,24},{8,16},{16,8},{24,0},{1,25},{9,17},{17,9},{25,1},{2,26},{10... | collective-permute-start | bytes 393224 | tf_op jit(solution)/shard_map/ppermute | solution.py:55
  39.4 0.5 collective-permute-start.15
  39.9 0.5 collective-permute-start.16
  40.4 0.8 %collective-permute-done.11.refs_1_ = bf16[384,256]{1,0:T(8,128)(2,1)S(1)} collective-permute-done((bf16[384,256]{1,0:T(8,128)(2,1)S(1)}, bf16[384,256]{1,0:T(8,128)(2,1)S(1)}, u32[]{:S(2)}, u32[]{:S(2)}) %collective-permute-start.11) | collective-permute-done | bytes 196640 | tf_op jit(solution)/shard_map/ppermute | solution.py:55
  41.2 0.4 level2_3.1.refs_3_.refs_0_
  41.6 3.3 %collective-permute-start.20 = (bf16[384,256]{1,0:T(8,128)(2,1)S(1)}, bf16[384,256]{1,0:T(8,128)(2,1)S(1)}, u32[]{:S(2)}, u32[]{:S(2)}) collective-permute-start(bf16[384,256]{1,0:T(8,128)(2,1)S(1)} %level2_3.1.refs_3_.refs_0_), channel_id=1, source_target_pairs={{0,4},{1,5},{2,6},{3,7},{4,0},{5,1},{6,2},{7,3},{8,12},{9,13},{10,... | collective-permute-start | bytes 589832 | tf_op jit(solution)/shard_map/ppermute | solution.py:55
  44.9 2.8 %collective-permute-done.10.refs_1_ = bf16[384,384]{1,0:T(8,128)(2,1)S(1)} collective-permute-done((bf16[384,384]{1,0:T(8,128)(2,1)S(1)}, bf16[384,384]{1,0:T(8,128)(2,1)S(1)}, u32[]{:S(2)}, u32[]{:S(2)}) %collective-permute-start.10) | collective-permute-done | bytes 294944 | tf_op jit(solution)/shard_map/ppermute | solution.py:55
  47.7 0.5 level3_2.1.refs_0_
  48.3 0.4 between_2.1
  48.7 1.2 %collective-permute-done.17.refs_1_ = bf16[384,384]{1,0:T(8,128)(2,1)S(1)} collective-permute-done((bf16[384,384]{1,0:T(8,128)(2,1)S(1)}, bf16[384,384]{1,0:T(8,128)(2,1)S(1)}, u32[]{:S(2)}, u32[]{:S(2)}) %collective-permute-start.17) | collective-permute-done | bytes 294944 | tf_op jit(solution)/shard_map/ppermute | solution.py:55
  49.8 1.2 %last_2.1 = (f32[256,384]{1,0:T(8,128)S(1)}, bf16[256,384]{1,0:T(8,128)(2,1)S(1)}, f32[256,384]{1,0:T(8,128)S(1)}, bf16[256,384]{1,0:T(8,128)(2,1)S(1)}) custom-call(f32[384,384]{1,0:T(8,128)S(1)} %get-tuple-element.50.refs_0_, bf16[384,384]{1,0:T(8,128)(2,1)S(1)} %collective-permute-done.17.refs_1_, ...), custom_call_target="tpu_custom_call" | custom-call | flops 6000000000 | tf_op jit(solution)/shard_map/last_2/pallas_call | solution.py:41
  51.1 1.6 %collective-permute-start.18 = (bf16[256,384]{1,0:T(8,128)(2,1)S(1)}, bf16[256,384]{1,0:T(8,128)(2,1)S(1)}, u32[]{:S(2)}, u32[]{:S(2)}) collective-permute-start(bf16[256,384]{1,0:T(8,128)(2,1)S(1)} %get-tuple-element.52), channel_id=1, source_target_pairs={{0,8},{8,0},{16,24},{24,16},{1,9},{9,1},{17,25},{25,17},{2,10},{10... | collective-permute-start | bytes 589832 | tf_op jit(solution)/shard_map/ppermute | solution.py:55
  52.7 1.5 %collective-permute-start.19 = (bf16[256,384]{1,0:T(8,128)(2,1)S(1)}, bf16[256,384]{1,0:T(8,128)(2,1)S(1)}, u32[]{:S(2)}, u32[]{:S(2)}) collective-permute-start(bf16[256,384]{1,0:T(8,128)(2,1)S(1)} %get-tuple-element.54), channel_id=1, source_target_pairs={{0,16},{8,24},{16,0},{24,8},{1,17},{9,25},{17,1},{25,9},{2,18},{10... | collective-permute-start | bytes 589832 | tf_op jit(solution)/shard_map/ppermute | solution.py:55
  54.2 0.4 level3_3.1.refs_0_
  54.9 1.2 %collective-permute-done.21.refs_1_ = bf16[384,256]{1,0:T(8,128)(2,1)S(1)} collective-permute-done((bf16[384,256]{1,0:T(8,128)(2,1)S(1)}, bf16[384,256]{1,0:T(8,128)(2,1)S(1)}, u32[]{:S(2)}, u32[]{:S(2)}) %collective-permute-start.21) | collective-permute-done | bytes 196640 | tf_op jit(solution)/shard_map/ppermute | solution.py:55
  56.0 0.8 %last_3.1 = (f32[256,256]{1,0:T(8,128)S(1)}, bf16[256,256]{1,0:T(8,128)(2,1)S(1)}, bf16[256,256]{1,0:T(8,128)(2,1)S(1)}, bf16[256,256]{1,0:T(8,128)(2,1)S(1)}) custom-call(f32[384,256]{1,0:T(8,128)S(1)} %between_3.1.refs_0_, bf16[384,256]{1,0:T(8,128)(2,1)S(1)} %collective-permute-done.21.refs_1_, ...), custom_call_target="tpu_custom_call" | custom-call | tf_op jit(solution)/shard_map/last_3/pallas_call | solution.py:41
  56.9 1.8 %collective-permute-start.24 = (bf16[256,256]{1,0:T(8,128)(2,1)S(1)}, bf16[256,256]{1,0:T(8,128)(2,1)S(1)}, u32[]{:S(2)}, u32[]{:S(2)}) collective-permute-start(bf16[256,256]{1,0:T(8,128)(2,1)S(1)} %get-tuple-element.60), channel_id=1, source_target_pairs={{0,24},{8,16},{16,8},{24,0},{1,25},{9,17},{17,9},{25,1},{2,26},{10... | collective-permute-start | bytes 393224 | tf_op jit(solution)/shard_map/ppermute | solution.py:55
  58.7 0.5 collective-permute-start.25
  59.2 1.2 %collective-permute-start.26 = (bf16[256,256]{1,0:T(8,128)(2,1)S(1)}, bf16[256,256]{1,0:T(8,128)(2,1)S(1)}, u32[]{:S(2)}, u32[]{:S(2)}) collective-permute-start(bf16[256,256]{1,0:T(8,128)(2,1)S(1)} %get-tuple-element.62), channel_id=1, source_target_pairs={{0,8},{8,0},{16,24},{24,16},{1,9},{9,1},{17,25},{25,17},{2,10},{10... | collective-permute-start | bytes 393224 | tf_op jit(solution)/shard_map/ppermute | solution.py:55
  60.5 0.9 %collective-permute-start.22 = (bf16[128,384]{1,0:T(8,128)(2,1)S(1)}, bf16[128,384]{1,0:T(8,128)(2,1)S(1)}, u32[]{:S(2)}, u32[]{:S(2)}) collective-permute-start(bf16[128,384]{1,0:T(8,128)(2,1)S(1)} %get-tuple-element.57), channel_id=1, source_target_pairs={{0,16},{8,24},{16,0},{24,8},{1,17},{9,25},{17,1},{25,9},{2,18},{10... | collective-permute-start | bytes 294920 | tf_op jit(solution)/shard_map/ppermute | solution.py:55
  61.4 1.5 %collective-permute-start.23 = (bf16[128,384]{1,0:T(8,128)(2,1)S(1)}, bf16[128,384]{1,0:T(8,128)(2,1)S(1)}, u32[]{:S(2)}, u32[]{:S(2)}) collective-permute-start(bf16[128,384]{1,0:T(8,128)(2,1)S(1)} %get-tuple-element.59), channel_id=1, source_target_pairs={{0,8},{8,0},{16,24},{24,16},{1,9},{9,1},{17,25},{25,17},{2,10},{10... | collective-permute-start | bytes 294920 | tf_op jit(solution)/shard_map/ppermute | solution.py:55
  62.9 5.4 %collective-permute-done.22.refs_1_ = bf16[128,384]{1,0:T(8,128)(2,1)S(1)} collective-permute-done((bf16[128,384]{1,0:T(8,128)(2,1)S(1)}, bf16[128,384]{1,0:T(8,128)(2,1)S(1)}, u32[]{:S(2)}, u32[]{:S(2)}) %collective-permute-start.22) | collective-permute-done | bytes 98336 | tf_op jit(solution)/shard_map/ppermute | solution.py:55
  68.4 0.9 %end.1 = bf16[2,256,512]{2,1,0:T(8,128)(2,1)} custom-call(bf16[256,128]{1,0:T(8,128)(2,1)S(1)} %sum_0.1.refs_3_.refs_0_, bf16[256,256]{1,0:T(8,128)(2,1)S(1)} %get-tuple-element.49.refs_1_, bf16[256,384]{1,0:T(8,128)(2,1)S(1)} %sum_2.1.refs_2_, f32[256,256]{1,0:T(8,128)S(1)} %get-tuple-element.55.refs_4_.refs_3_, ...), custom_call_target="tpu_custom_call" | custom-call | tf_op jit(solution)/shard_map/end/pallas_call | solution.py:413
  (32 shorter events, 2.7 us)
Async XLA Ops:
  3.7 5.8 %collective-permute-start.2 = (bf16[384,896]{1,0:T(8,128)(2,1)S(1)}, bf16[384,896]{1,0:T(8,128)(2,1)S(1)}, u32[]{:S(2)}, u32[]{:S(2)}) collective-permute-start(bf16[384,896]{1,0:T(8,128)(2,1)S(1)} %get-tuple-element.37.refs_0_), channel_id=1, source_target_pairs={{0,1},{1,0},{2,3},{3,2},{4,5},{5,4},{6,7},{7,6},{8,9},{9,8},{10,11... | collective-permute-start | bytes 2064392 | tf_op jit(solution)/shard_map/ppermute | solution.py:55
  4.2 1.9 %collective-permute-start = (bf16[384,128]{1,0:T(8,128)(2,1)S(1)}, bf16[384,128]{1,0:T(8,128)(2,1)S(1)}, u32[]{:S(2)}, u32[]{:S(2)}) collective-permute-start(bf16[384,128]{1,0:T(8,128)(2,1)S(1)} %get-tuple-element.34.refs_0_), channel_id=1, source_target_pairs={{0,1},{1,0},{2,3},{3,2},{4,5},{5,4},{6,7},{7,6},{8,9},{9,8},{10,11... | collective-permute-start | bytes 294920 | tf_op jit(solution)/shard_map/ppermute | solution.py:55
  6.4 6.3 %collective-permute-start.1 = (bf16[384,128]{1,0:T(8,128)(2,1)S(1)}, bf16[384,128]{1,0:T(8,128)(2,1)S(1)}, u32[]{:S(2)}, u32[]{:S(2)}) collective-permute-start(bf16[384,128]{1,0:T(8,128)(2,1)S(1)} %level1_0.1.refs_3_.refs_0_), channel_id=1, source_target_pairs={{0,2},{1,3},{2,0},{3,1},{4,6},{5,7},{6,4},{7,5},{8,10},{9,11},{10,... | collective-permute-start | bytes 294920 | tf_op jit(solution)/shard_map/ppermute | solution.py:55
  9.8 11.4 %collective-permute-start.4 = (bf16[384,256]{1,0:T(8,128)(2,1)S(1)}, bf16[384,256]{1,0:T(8,128)(2,1)S(1)}, u32[]{:S(2)}, u32[]{:S(2)}) collective-permute-start(bf16[384,256]{1,0:T(8,128)(2,1)S(1)} %level1_1.1.refs_3_.refs_0_), channel_id=1, source_target_pairs={{0,2},{1,3},{2,0},{3,1},{4,6},{5,7},{6,4},{7,5},{8,10},{9,11},{10,... | collective-permute-start | bytes 589832 | tf_op jit(solution)/shard_map/ppermute | solution.py:55
  13.1 8.9 %collective-permute-start.3 = (bf16[384,128]{1,0:T(8,128)(2,1)S(1)}, bf16[384,128]{1,0:T(8,128)(2,1)S(1)}, u32[]{:S(2)}, u32[]{:S(2)}) collective-permute-start(bf16[384,128]{1,0:T(8,128)(2,1)S(1)} %level2_0.1.refs_3_.refs_0_), channel_id=1, source_target_pairs={{0,4},{1,5},{2,6},{3,7},{4,0},{5,1},{6,2},{7,3},{8,12},{9,13},{10,... | collective-permute-start | bytes 294920 | tf_op jit(solution)/shard_map/ppermute | solution.py:55
  16.6 12.1 %collective-permute-start.9 = (bf16[384,384]{1,0:T(8,128)(2,1)S(1)}, bf16[384,384]{1,0:T(8,128)(2,1)S(1)}, u32[]{:S(2)}, u32[]{:S(2)}) collective-permute-start(bf16[384,384]{1,0:T(8,128)(2,1)S(1)} %level1_2.1.refs_3_.refs_0_), channel_id=1, source_target_pairs={{0,2},{1,3},{2,0},{3,1},{4,6},{5,7},{6,4},{7,5},{8,10},{9,11},{10,... | collective-permute-start | bytes 884744 | tf_op jit(solution)/shard_map/ppermute | solution.py:55
  21.6 12.6 %collective-permute-start.12 = (bf16[384,256]{1,0:T(8,128)(2,1)S(1)}, bf16[384,256]{1,0:T(8,128)(2,1)S(1)}, u32[]{:S(2)}, u32[]{:S(2)}) collective-permute-start(bf16[384,256]{1,0:T(8,128)(2,1)S(1)} %level2_1.1.refs_3_.refs_0_), channel_id=1, source_target_pairs={{0,4},{1,5},{2,6},{3,7},{4,0},{5,1},{6,2},{7,3},{8,12},{9,13},{10,... | collective-permute-start | bytes 589832 | tf_op jit(solution)/shard_map/ppermute | solution.py:55
  22.3 1.4 %collective-permute-start.5 = (bf16[384,128]{1,0:T(8,128)(2,1)S(1)}, bf16[384,128]{1,0:T(8,128)(2,1)S(1)}, u32[]{:S(2)}, u32[]{:S(2)}) collective-permute-start(bf16[384,128]{1,0:T(8,128)(2,1)S(1)} %level3_0.1.refs_0_), channel_id=1, source_target_pairs={{0,1},{1,0},{2,3},{3,2},{4,5},{5,4},{6,7},{7,6},{8,9},{9,8},{10,11... | collective-permute-start | bytes 294920 | tf_op jit(solution)/shard_map/ppermute | solution.py:55
  24.3 7.0 %collective-permute-start.6 = (bf16[256,128]{1,0:T(8,128)(2,1)S(1)}, bf16[256,128]{1,0:T(8,128)(2,1)S(1)}, u32[]{:S(2)}, u32[]{:S(2)}) collective-permute-start(bf16[256,128]{1,0:T(8,128)(2,1)S(1)} %get-tuple-element.42), channel_id=1, source_target_pairs={{0,24},{8,16},{16,8},{24,0},{1,25},{9,17},{17,9},{25,1},{2,26},{10... | collective-permute-start | bytes 196616 | tf_op jit(solution)/shard_map/ppermute | solution.py:55
  26.8 4.4 %collective-permute-start.7 = (bf16[256,128]{1,0:T(8,128)(2,1)S(1)}, bf16[256,128]{1,0:T(8,128)(2,1)S(1)}, u32[]{:S(2)}, u32[]{:S(2)}) collective-permute-start(bf16[256,128]{1,0:T(8,128)(2,1)S(1)} %get-tuple-element.43), channel_id=1, source_target_pairs={{0,16},{8,24},{16,0},{24,8},{1,17},{9,25},{17,1},{25,9},{2,18},{10... | collective-permute-start | bytes 196616 | tf_op jit(solution)/shard_map/ppermute | solution.py:55
  27.3 4.3 %collective-permute-start.8 = (bf16[256,128]{1,0:T(8,128)(2,1)S(1)}, bf16[256,128]{1,0:T(8,128)(2,1)S(1)}, u32[]{:S(2)}, u32[]{:S(2)}) collective-permute-start(bf16[256,128]{1,0:T(8,128)(2,1)S(1)} %get-tuple-element.44), channel_id=1, source_target_pairs={{0,8},{8,0},{16,24},{24,16},{1,9},{9,1},{17,25},{25,17},{2,10},{10... | collective-permute-start | bytes 196616 | tf_op jit(solution)/shard_map/ppermute | solution.py:55
  29.2 18.5 %collective-permute-start.10 = (bf16[384,384]{1,0:T(8,128)(2,1)S(1)}, bf16[384,384]{1,0:T(8,128)(2,1)S(1)}, u32[]{:S(2)}, u32[]{:S(2)}) collective-permute-start(bf16[384,384]{1,0:T(8,128)(2,1)S(1)} %level2_2.1.refs_4_.refs_0_), channel_id=1, source_target_pairs={{0,4},{1,5},{2,6},{3,7},{4,0},{5,1},{6,2},{7,3},{8,12},{9,13},{10,... | collective-permute-start | bytes 884744 | tf_op jit(solution)/shard_map/ppermute | solution.py:55
  31.9 9.3 %collective-permute-start.11 = (bf16[384,256]{1,0:T(8,128)(2,1)S(1)}, bf16[384,256]{1,0:T(8,128)(2,1)S(1)}, u32[]{:S(2)}, u32[]{:S(2)}) collective-permute-start(bf16[384,256]{1,0:T(8,128)(2,1)S(1)} %level1_3.1.refs_3_.refs_0_), channel_id=1, source_target_pairs={{0,2},{1,3},{2,0},{3,1},{4,6},{5,7},{6,4},{7,5},{8,10},{9,11},{10,... | collective-permute-start | bytes 589832 | tf_op jit(solution)/shard_map/ppermute | solution.py:55
  34.5 1.5 %collective-permute-start.13 = (bf16[384,256]{1,0:T(8,128)(2,1)S(1)}, bf16[384,256]{1,0:T(8,128)(2,1)S(1)}, u32[]{:S(2)}, u32[]{:S(2)}) collective-permute-start(bf16[384,256]{1,0:T(8,128)(2,1)S(1)} %level3_1.1.refs_0_), channel_id=1, source_target_pairs={{0,1},{1,0},{2,3},{3,2},{4,5},{5,4},{6,7},{7,6},{8,9},{9,8},{10,11... | collective-permute-start | bytes 589832 | tf_op jit(solution)/shard_map/ppermute | solution.py:55
  36.9 11.4 %collective-permute-start.14 = (bf16[256,256]{1,0:T(8,128)(2,1)S(1)}, bf16[256,256]{1,0:T(8,128)(2,1)S(1)}, u32[]{:S(2)}, u32[]{:S(2)}) collective-permute-start(bf16[256,256]{1,0:T(8,128)(2,1)S(1)} %get-tuple-element.46), channel_id=1, source_target_pairs={{0,24},{8,16},{16,8},{24,0},{1,25},{9,17},{17,9},{25,1},{2,26},{10... | collective-permute-start | bytes 393224 | tf_op jit(solution)/shard_map/ppermute | solution.py:55
  39.4 8.9 %collective-permute-start.15 = (bf16[256,256]{1,0:T(8,128)(2,1)S(1)}, bf16[256,256]{1,0:T(8,128)(2,1)S(1)}, u32[]{:S(2)}, u32[]{:S(2)}) collective-permute-start(bf16[256,256]{1,0:T(8,128)(2,1)S(1)} %get-tuple-element.47), channel_id=1, source_target_pairs={{0,16},{8,24},{16,0},{24,8},{1,17},{9,25},{17,1},{25,9},{2,18},{10... | collective-permute-start | bytes 393224 | tf_op jit(solution)/shard_map/ppermute | solution.py:55
  39.9 8.4 %collective-permute-start.16 = (bf16[256,256]{1,0:T(8,128)(2,1)S(1)}, bf16[256,256]{1,0:T(8,128)(2,1)S(1)}, u32[]{:S(2)}, u32[]{:S(2)}) collective-permute-start(bf16[256,256]{1,0:T(8,128)(2,1)S(1)} %get-tuple-element.48), channel_id=1, source_target_pairs={{0,8},{8,0},{16,24},{24,16},{1,9},{9,1},{17,25},{25,17},{2,10},{10... | collective-permute-start | bytes 393224 | tf_op jit(solution)/shard_map/ppermute | solution.py:55
  41.6 12.6 %collective-permute-start.20 = (bf16[384,256]{1,0:T(8,128)(2,1)S(1)}, bf16[384,256]{1,0:T(8,128)(2,1)S(1)}, u32[]{:S(2)}, u32[]{:S(2)}) collective-permute-start(bf16[384,256]{1,0:T(8,128)(2,1)S(1)} %level2_3.1.refs_3_.refs_0_), channel_id=1, source_target_pairs={{0,4},{1,5},{2,6},{3,7},{4,0},{5,1},{6,2},{7,3},{8,12},{9,13},{10,... | collective-permute-start | bytes 589832 | tf_op jit(solution)/shard_map/ppermute | solution.py:55
  48.2 1.6 %collective-permute-start.17 = (bf16[384,384]{1,0:T(8,128)(2,1)S(1)}, bf16[384,384]{1,0:T(8,128)(2,1)S(1)}, u32[]{:S(2)}, u32[]{:S(2)}) collective-permute-start(bf16[384,384]{1,0:T(8,128)(2,1)S(1)} %level3_2.1.refs_0_), channel_id=1, source_target_pairs={{0,1},{1,0},{2,3},{3,2},{4,5},{5,4},{6,7},{7,6},{8,9},{9,8},{10,11... | collective-permute-start | bytes 884744 | tf_op jit(solution)/shard_map/ppermute | solution.py:55
  51.1 9.3 %collective-permute-start.18 = (bf16[256,384]{1,0:T(8,128)(2,1)S(1)}, bf16[256,384]{1,0:T(8,128)(2,1)S(1)}, u32[]{:S(2)}, u32[]{:S(2)}) collective-permute-start(bf16[256,384]{1,0:T(8,128)(2,1)S(1)} %get-tuple-element.52), channel_id=1, source_target_pairs={{0,8},{8,0},{16,24},{24,16},{1,9},{9,1},{17,25},{25,17},{2,10},{10... | collective-permute-start | bytes 589832 | tf_op jit(solution)/shard_map/ppermute | solution.py:55
  52.7 7.8 %collective-permute-start.19 = (bf16[256,384]{1,0:T(8,128)(2,1)S(1)}, bf16[256,384]{1,0:T(8,128)(2,1)S(1)}, u32[]{:S(2)}, u32[]{:S(2)}) collective-permute-start(bf16[256,384]{1,0:T(8,128)(2,1)S(1)} %get-tuple-element.54), channel_id=1, source_target_pairs={{0,16},{8,24},{16,0},{24,8},{1,17},{9,25},{17,1},{25,9},{2,18},{10... | collective-permute-start | bytes 589832 | tf_op jit(solution)/shard_map/ppermute | solution.py:55
  54.5 1.5 %collective-permute-start.21 = (bf16[384,256]{1,0:T(8,128)(2,1)S(1)}, bf16[384,256]{1,0:T(8,128)(2,1)S(1)}, u32[]{:S(2)}, u32[]{:S(2)}) collective-permute-start(bf16[384,256]{1,0:T(8,128)(2,1)S(1)} %level3_3.1.refs_0_), channel_id=1, source_target_pairs={{0,1},{1,0},{2,3},{3,2},{4,5},{5,4},{6,7},{7,6},{8,9},{9,8},{10,11... | collective-permute-start | bytes 589832 | tf_op jit(solution)/shard_map/ppermute | solution.py:55
  56.9 11.5 %collective-permute-start.24 = (bf16[256,256]{1,0:T(8,128)(2,1)S(1)}, bf16[256,256]{1,0:T(8,128)(2,1)S(1)}, u32[]{:S(2)}, u32[]{:S(2)}) collective-permute-start(bf16[256,256]{1,0:T(8,128)(2,1)S(1)} %get-tuple-element.60), channel_id=1, source_target_pairs={{0,24},{8,16},{16,8},{24,0},{1,25},{9,17},{17,9},{25,1},{2,26},{10... | collective-permute-start | bytes 393224 | tf_op jit(solution)/shard_map/ppermute | solution.py:55
  58.7 9.7 %collective-permute-start.25 = (bf16[256,256]{1,0:T(8,128)(2,1)S(1)}, bf16[256,256]{1,0:T(8,128)(2,1)S(1)}, u32[]{:S(2)}, u32[]{:S(2)}) collective-permute-start(bf16[256,256]{1,0:T(8,128)(2,1)S(1)} %get-tuple-element.61), channel_id=1, source_target_pairs={{0,16},{8,24},{16,0},{24,8},{1,17},{9,25},{17,1},{25,9},{2,18},{10... | collective-permute-start | bytes 393224 | tf_op jit(solution)/shard_map/ppermute | solution.py:55
  59.2 9.2 %collective-permute-start.26 = (bf16[256,256]{1,0:T(8,128)(2,1)S(1)}, bf16[256,256]{1,0:T(8,128)(2,1)S(1)}, u32[]{:S(2)}, u32[]{:S(2)}) collective-permute-start(bf16[256,256]{1,0:T(8,128)(2,1)S(1)} %get-tuple-element.62), channel_id=1, source_target_pairs={{0,8},{8,0},{16,24},{24,16},{1,9},{9,1},{17,25},{25,17},{2,10},{10... | collective-permute-start | bytes 393224 | tf_op jit(solution)/shard_map/ppermute | solution.py:55
  60.5 7.8 %collective-permute-start.22 = (bf16[128,384]{1,0:T(8,128)(2,1)S(1)}, bf16[128,384]{1,0:T(8,128)(2,1)S(1)}, u32[]{:S(2)}, u32[]{:S(2)}) collective-permute-start(bf16[128,384]{1,0:T(8,128)(2,1)S(1)} %get-tuple-element.57), channel_id=1, source_target_pairs={{0,16},{8,24},{16,0},{24,8},{1,17},{9,25},{17,1},{25,9},{2,18},{10... | collective-permute-start | bytes 294920 | tf_op jit(solution)/shard_map/ppermute | solution.py:55
  61.4 6.9 %collective-permute-start.23 = (bf16[128,384]{1,0:T(8,128)(2,1)S(1)}, bf16[128,384]{1,0:T(8,128)(2,1)S(1)}, u32[]{:S(2)}, u32[]{:S(2)}) collective-permute-start(bf16[128,384]{1,0:T(8,128)(2,1)S(1)} %get-tuple-element.59), channel_id=1, source_target_pairs={{0,8},{8,0},{16,24},{24,16},{1,9},{9,1},{17,25},{25,17},{2,10},{10... | collective-permute-start | bytes 294920 | tf_op jit(solution)/shard_map/ppermute | solution.py:55

commit v22 on v21

--- a/solution.py
+++ b/solution.py
@@ -32,22 +32,24 @@
     return pltpu.with_memory_space_constraint(value, pltpu.HBM)
 
 
-def call(kernel, name, in_specs, out_shape, scratch, args, after=(), flops=COST, limit=8 * 2**20):
-    count = len(in_specs)
+def call(kernel, name, in_specs, out_shape, scratch, args, after=(), flops=COST, limit=8 * 2**20, through=()):
+    count, outs = len(in_specs), len(out_shape)
 
     def body(*refs):
-        kernel(*refs[:count], *refs[count + len(after) :])
+        held = refs[count + len(after) + len(through) :]
+        kernel(*refs[:count], *held[:outs], *held[outs + len(through) :])
 
     return pl.pallas_call(
         body,
         name=name,
-        in_specs=[*in_specs, *[ANY] * len(after)],
-        out_specs=[VMEM] * len(out_shape),
-        out_shape=out_shape,
+        in_specs=[*in_specs, *[ANY] * (len(after) + len(through))],
+        out_specs=[VMEM] * outs + [ANY] * len(through),
+        out_shape=[*out_shape, *[in_vmem(*v.shape, dtype=v.dtype) for v in through]],
         scratch_shapes=scratch,
+        input_output_aliases={count + len(after) + at: outs + at for at in range(len(through))},
         compiler_params=pltpu.CompilerParams(vmem_limit_bytes=limit),
         cost_estimate=pl.CostEstimate(flops=flops, bytes_accessed=0, transcendentals=0),
-    )(*args, *after)
+    )(*args, *after, *[here(v) for v in through])
 
 
 def partner(value, axis, mask):
@@ -253,9 +255,9 @@
     def cross(level, value):
         return partner(value, "box", 2 ** bits[level])
 
-    near_first, near_rest = cross(1, first), cross(1, rest)
-
-    def step(name, jobs, after=(), flops=COST):
+    near_first = cross(1, first)
+
+    def step(name, jobs, after=(), flops=COST, through=()):
         args = [here(v) for level, j, own, other in jobs for v in (own, other, weights[level])]
         described, sizes = [], []
         for level, j, _, _ in jobs:
@@ -271,6 +273,7 @@
             args,
             after,
             flops,
+            through=through,
         )
 
     def job1(j):
@@ -286,7 +289,8 @@
         coeff3[j] = value
         near3[j] = cross(3, value)
 
-    (value,) = step("level1_0", [job1(0)])
+    value, rest = step("level1_0", [job1(0)], through=[rest])
+    near_rest = cross(1, rest)
     second(0, value)
     (value,) = step("level1_1", [job1(1)], [coeff2[0]])
     second(1, value)

time: 69.5 us -> 71 us (1.022)
  starting transfers between devices: 33.1 us -> 37.7 us
  waiting for transfers between devices: 19.4 us -> 16.4 us
    ppermute x27, starting transfers between devices: 33.1 us -> 37.7 us  [partner(): return lax.ppermute(value, axis, pairs)]
    ppermute x27, waiting for transfers between devices: 19.4 us -> 16.4 us  [partner(): return lax.ppermute(value, axis, pairs)]
  transfers between devices with their start and end apart: 27 -> 27, of which waited for: 11 -> 11; matrix products, arithmetic and copies ran while one was open for 0% -> 0% of each run, Pallas kernels for 17% -> 16%
where the time goes in v22:
time: 71 us; the launch traced here: 70.8 us
  starting transfers between devices  37.7 us (53%)
  Pallas kernels  16.4 us (23%)
  waiting for transfers between devices  16.4 us (23%)
    ppermute x27, starting transfers between devices, partner(): return lax.ppermute(value, axis, pairs)  37.7 us
    ppermute x27, waiting for transfers between devices, partner(): return lax.ppermute(value, axis, pairs)  16.4 us
    pallas_call x25, Pallas kernels, call(): pl.pallas_call(body, name=name, in_specs=[*in_specs, *[ANY] * (len(after)...  15.5 us
  transfers between devices with their start and end apart: 27, of which 11 were waited for; matrix products, arithmetic and copies ran while one was open for 0% of the time, Pallas kernels for 16%

profile of v22, /device:TPU:0, one launch (start us, length us, event | category | flops | bytes accessed | tf_op | source)
XLA Modules:
  0.0 70.8 jit_solution(925564550042111490)
XLA Ops:
  0.0 3.7 %leaf.1 = (bf16[384,128]{1,0:T(8,128)(2,1)S(1)}, bf16[384,896]{1,0:T(8,128)(2,1)S(1)}, bf16[2,384,768]{2,1,0:T(8,128)(2,1)S(1)}, bf16[2,384,768]{2,1,0:T(8,128)(2,1)S(1)}) custom-call(bf16[2,1024,512]{2,1,0:T(8,128)(2,1)} %bitcast.9, bf16[2,384,1024]{2,1,0:T(8,128)(2,1)} %bitcast.10, bf16[5,2,384,768]{3,2,1,0:T(8,128)(2,1)} %bitcast.7, s32[2,5]{1,0:T(2,128)} %bitcast.12), custom_call_target="tpu_custom_call" | custom-call | flops 6000000000 | tf_op jit(solution)/shard_map/leaf/pallas_call | solution.py:42
  3.7 0.5 collective-permute-start
  4.2 0.9 %collective-permute-done.refs_1_ = bf16[384,128]{1,0:T(8,128)(2,1)S(1)} collective-permute-done((bf16[384,128]{1,0:T(8,128)(2,1)S(1)}, bf16[384,128]{1,0:T(8,128)(2,1)S(1)}, u32[]{:S(2)}, u32[]{:S(2)}) %collective-permute-start) | collective-permute-done | bytes 98336 | tf_op jit(solution)/shard_map/ppermute | solution.py:57
  5.5 0.4 collective-permute-start.2
  5.9 2.7 %collective-permute-start.1 = (bf16[384,128]{1,0:T(8,128)(2,1)S(1)}, bf16[384,128]{1,0:T(8,128)(2,1)S(1)}, u32[]{:S(2)}, u32[]{:S(2)}) collective-permute-start(bf16[384,128]{1,0:T(8,128)(2,1)S(1)} %get-tuple-element.39.refs_3_.refs_0_), channel_id=1, source_target_pairs={{0,2},{1,3},{2,0},{3,1},{4,6},{5,7},{6,4},{7,5},{8,10},{9,11},{10,... | collective-permute-start | bytes 294920 | tf_op jit(solution)/shard_map/ppermute | solution.py:57
  8.6 0.4 level1_1.1.refs_3_.refs_0_
  9.0 2.1 %collective-permute-start.4 = (bf16[384,256]{1,0:T(8,128)(2,1)S(1)}, bf16[384,256]{1,0:T(8,128)(2,1)S(1)}, u32[]{:S(2)}, u32[]{:S(2)}) collective-permute-start(bf16[384,256]{1,0:T(8,128)(2,1)S(1)} %level1_1.1.refs_3_.refs_0_), channel_id=1, source_target_pairs={{0,2},{1,3},{2,0},{3,1},{4,6},{5,7},{6,4},{7,5},{8,10},{9,11},{10,... | collective-permute-start | bytes 589832 | tf_op jit(solution)/shard_map/ppermute | solution.py:57
  11.0 0.9 %collective-permute-done.1.refs_1_ = bf16[384,128]{1,0:T(8,128)(2,1)S(1)} collective-permute-done((bf16[384,128]{1,0:T(8,128)(2,1)S(1)}, bf16[384,128]{1,0:T(8,128)(2,1)S(1)}, u32[]{:S(2)}, u32[]{:S(2)}) %collective-permute-start.1) | collective-permute-done | bytes 98336 | tf_op jit(solution)/shard_map/ppermute | solution.py:57
  12.3 2.8 %collective-permute-start.3 = (bf16[384,128]{1,0:T(8,128)(2,1)S(1)}, bf16[384,128]{1,0:T(8,128)(2,1)S(1)}, u32[]{:S(2)}, u32[]{:S(2)}) collective-permute-start(bf16[384,128]{1,0:T(8,128)(2,1)S(1)} %level2_0.1.refs_3_.refs_0_), channel_id=1, source_target_pairs={{0,4},{1,5},{2,6},{3,7},{4,0},{5,1},{6,2},{7,3},{8,12},{9,13},{10,... | collective-permute-start | bytes 294920 | tf_op jit(solution)/shard_map/ppermute | solution.py:57
  15.1 0.5 level1_2.1.refs_3_.refs_0_
  15.6 1.6 %collective-permute-start.9 = (bf16[384,384]{1,0:T(8,128)(2,1)S(1)}, bf16[384,384]{1,0:T(8,128)(2,1)S(1)}, u32[]{:S(2)}, u32[]{:S(2)}) collective-permute-start(bf16[384,384]{1,0:T(8,128)(2,1)S(1)} %level1_2.1.refs_3_.refs_0_), channel_id=1, source_target_pairs={{0,2},{1,3},{2,0},{3,1},{4,6},{5,7},{6,4},{7,5},{8,10},{9,11},{10,... | collective-permute-start | bytes 884744 | tf_op jit(solution)/shard_map/ppermute | solution.py:57
  17.3 2.5 %prefetch.1 = (bf16[2,384,768]{2,1,0:T(8,128)(2,1)S(1)}, bf16[2,384,768]{2,1,0:T(8,128)(2,1)S(1)}, bf16[2,1024,384]{2,1,0:T(8,128)(2,1)S(1)}) custom-call(bf16[5,2,384,768]{3,2,1,0:T(8,128)(2,1)} %bitcast.8, bf16[2,1024,384]{2,1,0:T(8,128)(2,1)} %bitcast.11, s32[2,5]{1,0:T(2,128)} %bitcast.13, bf16[384,384]{1,0:T(8,128)(2,1)S(1)} %level1_2.1.refs_3_.refs_0_), custom_call_target="tpu_custom_call" | custom-call | flops 6000000000 | tf_op jit(solution)/shard_map/prefetch/pallas_call | solution.py:42
  19.8 0.4 level2_1.1.refs_3_.refs_0_
  20.1 0.4 collective-permute-start.12
  21.2 1.0 %collective-permute-done.5.refs_1_ = bf16[384,128]{1,0:T(8,128)(2,1)S(1)} collective-permute-done((bf16[384,128]{1,0:T(8,128)(2,1)S(1)}, bf16[384,128]{1,0:T(8,128)(2,1)S(1)}, u32[]{:S(2)}, u32[]{:S(2)}) %collective-permute-start.5) | collective-permute-done | bytes 98336 | tf_op jit(solution)/shard_map/ppermute | solution.py:57
  22.3 0.6 last_0.1
  22.8 2.5 %collective-permute-start.6 = (bf16[256,128]{1,0:T(8,128)(2,1)S(1)}, bf16[256,128]{1,0:T(8,128)(2,1)S(1)}, u32[]{:S(2)}, u32[]{:S(2)}) collective-permute-start(bf16[256,128]{1,0:T(8,128)(2,1)S(1)} %get-tuple-element.46), channel_id=1, source_target_pairs={{0,24},{8,16},{16,8},{24,0},{1,25},{9,17},{17,9},{25,1},{2,26},{10... | collective-permute-start | bytes 196616 | tf_op jit(solution)/shard_map/ppermute | solution.py:57
  25.4 0.5 collective-permute-start.7
  25.9 0.5 collective-permute-start.8
  26.4 2.5 %collective-permute-done.9.refs_1_ = bf16[384,384]{1,0:T(8,128)(2,1)S(1)} collective-permute-done((bf16[384,384]{1,0:T(8,128)(2,1)S(1)}, bf16[384,384]{1,0:T(8,128)(2,1)S(1)}, u32[]{:S(2)}, u32[]{:S(2)}) %collective-permute-start.9) | collective-permute-done | bytes 294944 | tf_op jit(solution)/shard_map/ppermute | solution.py:57
  28.9 0.5 level2_2.1.refs_4_.refs_0_
  29.4 1.5 %collective-permute-start.10 = (bf16[384,384]{1,0:T(8,128)(2,1)S(1)}, bf16[384,384]{1,0:T(8,128)(2,1)S(1)}, u32[]{:S(2)}, u32[]{:S(2)}) collective-permute-start(bf16[384,384]{1,0:T(8,128)(2,1)S(1)} %level2_2.1.refs_4_.refs_0_), channel_id=1, source_target_pairs={{0,4},{1,5},{2,6},{3,7},{4,0},{5,1},{6,2},{7,3},{8,12},{9,13},{10,... | collective-permute-start | bytes 884744 | tf_op jit(solution)/shard_map/ppermute | solution.py:57
  31.0 0.4 level1_3.1.refs_3_.refs_0_
  31.4 2.5 %collective-permute-start.11 = (bf16[384,256]{1,0:T(8,128)(2,1)S(1)}, bf16[384,256]{1,0:T(8,128)(2,1)S(1)}, u32[]{:S(2)}, u32[]{:S(2)}) collective-permute-start(bf16[384,256]{1,0:T(8,128)(2,1)S(1)} %level1_3.1.refs_3_.refs_0_), channel_id=1, source_target_pairs={{0,2},{1,3},{2,0},{3,1},{4,6},{5,7},{6,4},{7,5},{8,10},{9,11},{10,... | collective-permute-start | bytes 589832 | tf_op jit(solution)/shard_map/ppermute | solution.py:57
  33.9 0.4 level3_1.1.refs_0_
  34.6 1.2 %collective-permute-done.13.refs_1_ = bf16[384,256]{1,0:T(8,128)(2,1)S(1)} collective-permute-done((bf16[384,256]{1,0:T(8,128)(2,1)S(1)}, bf16[384,256]{1,0:T(8,128)(2,1)S(1)}, u32[]{:S(2)}, u32[]{:S(2)}) %collective-permute-start.13) | collective-permute-done | bytes 196640 | tf_op jit(solution)/shard_map/ppermute | solution.py:57
  35.8 0.8 %last_1.1 = (f32[256,256]{1,0:T(8,128)S(1)}, bf16[256,256]{1,0:T(8,128)(2,1)S(1)}, bf16[256,256]{1,0:T(8,128)(2,1)S(1)}, bf16[256,256]{1,0:T(8,128)(2,1)S(1)}) custom-call(f32[384,256]{1,0:T(8,128)S(1)} %between_1.1.refs_0_, bf16[384,256]{1,0:T(8,128)(2,1)S(1)} %collective-permute-done.13.refs_1_, ...), custom_call_target="tpu_custom_call" | custom-call | flops 6000000000 | tf_op jit(solution)/shard_map/last_1/pallas_call | solution.py:42
  36.6 2.5 %collective-permute-start.14 = (bf16[256,256]{1,0:T(8,128)(2,1)S(1)}, bf16[256,256]{1,0:T(8,128)(2,1)S(1)}, u32[]{:S(2)}, u32[]{:S(2)}) collective-permute-start(bf16[256,256]{1,0:T(8,128)(2,1)S(1)} %get-tuple-element.50), channel_id=1, source_target_pairs={{0,24},{8,16},{16,8},{24,0},{1,25},{9,17},{17,9},{25,1},{2,26},{10... | collective-permute-start | bytes 393224 | tf_op jit(solution)/shard_map/ppermute | solution.py:57
  39.1 0.5 collective-permute-start.15
  39.6 0.6 collective-permute-start.16
  40.2 0.8 %collective-permute-done.11.refs_1_ = bf16[384,256]{1,0:T(8,128)(2,1)S(1)} collective-permute-done((bf16[384,256]{1,0:T(8,128)(2,1)S(1)}, bf16[384,256]{1,0:T(8,128)(2,1)S(1)}, u32[]{:S(2)}, u32[]{:S(2)}) %collective-permute-start.11) | collective-permute-done | bytes 196640 | tf_op jit(solution)/shard_map/ppermute | solution.py:57
  41.3 3.3 %collective-permute-start.20 = (bf16[384,256]{1,0:T(8,128)(2,1)S(1)}, bf16[384,256]{1,0:T(8,128)(2,1)S(1)}, u32[]{:S(2)}, u32[]{:S(2)}) collective-permute-start(bf16[384,256]{1,0:T(8,128)(2,1)S(1)} %level2_3.1.refs_3_.refs_0_), channel_id=1, source_target_pairs={{0,4},{1,5},{2,6},{3,7},{4,0},{5,1},{6,2},{7,3},{8,12},{9,13},{10,... | collective-permute-start | bytes 589832 | tf_op jit(solution)/shard_map/ppermute | solution.py:57
  44.6 0.7 collective-permute-done.10.refs_1_
  45.3 0.5 level3_2.1.refs_0_
  46.0 0.4 between_2.1
  46.4 1.1 %collective-permute-done.17.refs_1_ = bf16[384,384]{1,0:T(8,128)(2,1)S(1)} collective-permute-done((bf16[384,384]{1,0:T(8,128)(2,1)S(1)}, bf16[384,384]{1,0:T(8,128)(2,1)S(1)}, u32[]{:S(2)}, u32[]{:S(2)}) %collective-permute-start.17) | collective-permute-done | bytes 294944 | tf_op jit(solution)/shard_map/ppermute | solution.py:57
  47.5 1.2 %last_2.1 = (f32[256,384]{1,0:T(8,128)S(1)}, bf16[256,384]{1,0:T(8,128)(2,1)S(1)}, f32[256,384]{1,0:T(8,128)S(1)}, bf16[256,384]{1,0:T(8,128)(2,1)S(1)}) custom-call(f32[384,384]{1,0:T(8,128)S(1)} %get-tuple-element.54.refs_0_, bf16[384,384]{1,0:T(8,128)(2,1)S(1)} %collective-permute-done.17.refs_1_, ...), custom_call_target="tpu_custom_call" | custom-call | flops 6000000000 | tf_op jit(solution)/shard_map/last_2/pallas_call | solution.py:42
  48.7 6.3 %collective-permute-start.18 = (bf16[256,384]{1,0:T(8,128)(2,1)S(1)}, bf16[256,384]{1,0:T(8,128)(2,1)S(1)}, u32[]{:S(2)}, u32[]{:S(2)}) collective-permute-start(bf16[256,384]{1,0:T(8,128)(2,1)S(1)} %get-tuple-element.56), channel_id=1, source_target_pairs={{0,8},{8,0},{16,24},{24,16},{1,9},{9,1},{17,25},{25,17},{2,10},{10... | collective-permute-start | bytes 589832 | tf_op jit(solution)/shard_map/ppermute | solution.py:57
  55.0 1.5 %collective-permute-start.19 = (bf16[256,384]{1,0:T(8,128)(2,1)S(1)}, bf16[256,384]{1,0:T(8,128)(2,1)S(1)}, u32[]{:S(2)}, u32[]{:S(2)}) collective-permute-start(bf16[256,384]{1,0:T(8,128)(2,1)S(1)} %get-tuple-element.58), channel_id=1, source_target_pairs={{0,16},{8,24},{16,0},{24,8},{1,17},{9,25},{17,1},{25,9},{2,18},{10... | collective-permute-start | bytes 589832 | tf_op jit(solution)/shard_map/ppermute | solution.py:57
  56.5 0.4 level3_3.1.refs_0_
  57.2 1.2 %collective-permute-done.21.refs_1_ = bf16[384,256]{1,0:T(8,128)(2,1)S(1)} collective-permute-done((bf16[384,256]{1,0:T(8,128)(2,1)S(1)}, bf16[384,256]{1,0:T(8,128)(2,1)S(1)}, u32[]{:S(2)}, u32[]{:S(2)}) %collective-permute-start.21) | collective-permute-done | bytes 196640 | tf_op jit(solution)/shard_map/ppermute | solution.py:57
  58.4 0.8 %last_3.1 = (f32[256,256]{1,0:T(8,128)S(1)}, bf16[256,256]{1,0:T(8,128)(2,1)S(1)}, bf16[256,256]{1,0:T(8,128)(2,1)S(1)}, bf16[256,256]{1,0:T(8,128)(2,1)S(1)}) custom-call(f32[384,256]{1,0:T(8,128)S(1)} %between_3.1.refs_0_, bf16[384,256]{1,0:T(8,128)(2,1)S(1)} %collective-permute-done.21.refs_1_, ...), custom_call_target="tpu_custom_call" | custom-call | tf_op jit(solution)/shard_map/last_3/pallas_call | solution.py:42
  59.3 2.0 %collective-permute-start.25 = (bf16[256,256]{1,0:T(8,128)(2,1)S(1)}, bf16[256,256]{1,0:T(8,128)(2,1)S(1)}, u32[]{:S(2)}, u32[]{:S(2)}) collective-permute-start(bf16[256,256]{1,0:T(8,128)(2,1)S(1)} %get-tuple-element.65), channel_id=1, source_target_pairs={{0,16},{8,24},{16,0},{24,8},{1,17},{9,25},{17,1},{25,9},{2,18},{10... | collective-permute-start | bytes 393224 | tf_op jit(solution)/shard_map/ppermute | solution.py:57
  61.3 1.5 %collective-permute-start.26 = (bf16[256,256]{1,0:T(8,128)(2,1)S(1)}, bf16[256,256]{1,0:T(8,128)(2,1)S(1)}, u32[]{:S(2)}, u32[]{:S(2)}) collective-permute-start(bf16[256,256]{1,0:T(8,128)(2,1)S(1)} %get-tuple-element.66), channel_id=1, source_target_pairs={{0,8},{8,0},{16,24},{24,16},{1,9},{9,1},{17,25},{25,17},{2,10},{10... | collective-permute-start | bytes 393224 | tf_op jit(solution)/shard_map/ppermute | solution.py:57
  62.9 0.6 collective-permute-start.22
  63.4 0.5 collective-permute-start.23
  63.9 5.9 %collective-permute-done.22.refs_1_ = bf16[128,384]{1,0:T(8,128)(2,1)S(1)} collective-permute-done((bf16[128,384]{1,0:T(8,128)(2,1)S(1)}, bf16[128,384]{1,0:T(8,128)(2,1)S(1)}, u32[]{:S(2)}, u32[]{:S(2)}) %collective-permute-start.22) | collective-permute-done | bytes 98336 | tf_op jit(solution)/shard_map/ppermute | solution.py:57
  69.9 0.9 %end.1 = bf16[2,256,512]{2,1,0:T(8,128)(2,1)} custom-call(bf16[256,128]{1,0:T(8,128)(2,1)S(1)} %sum_0.1.refs_3_.refs_0_, bf16[256,256]{1,0:T(8,128)(2,1)S(1)} %get-tuple-element.53.refs_1_, bf16[256,384]{1,0:T(8,128)(2,1)S(1)} %sum_2.1.refs_2_, f32[256,256]{1,0:T(8,128)S(1)} %get-tuple-element.59.refs_4_.refs_3_, ...), custom_call_target="tpu_custom_call" | custom-call | tf_op jit(solution)/shard_map/end/pallas_call | solution.py:417
  (32 shorter events, 2.8 us)
Async XLA Ops:
  3.7 1.5 %collective-permute-start = (bf16[384,128]{1,0:T(8,128)(2,1)S(1)}, bf16[384,128]{1,0:T(8,128)(2,1)S(1)}, u32[]{:S(2)}, u32[]{:S(2)}) collective-permute-start(bf16[384,128]{1,0:T(8,128)(2,1)S(1)} %get-tuple-element.36.refs_0_), channel_id=1, source_target_pairs={{0,1},{1,0},{2,3},{3,2},{4,5},{5,4},{6,7},{7,6},{8,9},{9,8},{10,11... | collective-permute-start | bytes 294920 | tf_op jit(solution)/shard_map/ppermute | solution.py:57
  5.5 3.1 %collective-permute-start.2 = (bf16[384,896]{1,0:T(8,128)(2,1)S(1)}, bf16[384,896]{1,0:T(8,128)(2,1)S(1)}, u32[]{:S(2)}, u32[]{:S(2)}) collective-permute-start(bf16[384,896]{1,0:T(8,128)(2,1)S(1)} %get-tuple-element.41.refs_0_), channel_id=1, source_target_pairs={{0,1},{1,0},{2,3},{3,2},{4,5},{5,4},{6,7},{7,6},{8,9},{9,8},{10,11... | collective-permute-start | bytes 2064392 | tf_op jit(solution)/shard_map/ppermute | solution.py:57
  5.9 6.0 %collective-permute-start.1 = (bf16[384,128]{1,0:T(8,128)(2,1)S(1)}, bf16[384,128]{1,0:T(8,128)(2,1)S(1)}, u32[]{:S(2)}, u32[]{:S(2)}) collective-permute-start(bf16[384,128]{1,0:T(8,128)(2,1)S(1)} %get-tuple-element.39.refs_3_.refs_0_), channel_id=1, source_target_pairs={{0,2},{1,3},{2,0},{3,1},{4,6},{5,7},{6,4},{7,5},{8,10},{9,11},{10,... | collective-permute-start | bytes 294920 | tf_op jit(solution)/shard_map/ppermute | solution.py:57
  9.0 10.8 %collective-permute-start.4 = (bf16[384,256]{1,0:T(8,128)(2,1)S(1)}, bf16[384,256]{1,0:T(8,128)(2,1)S(1)}, u32[]{:S(2)}, u32[]{:S(2)}) collective-permute-start(bf16[384,256]{1,0:T(8,128)(2,1)S(1)} %level1_1.1.refs_3_.refs_0_), channel_id=1, source_target_pairs={{0,2},{1,3},{2,0},{3,1},{4,6},{5,7},{6,4},{7,5},{8,10},{9,11},{10,... | collective-permute-start | bytes 589832 | tf_op jit(solution)/shard_map/ppermute | solution.py:57
  12.3 8.3 %collective-permute-start.3 = (bf16[384,128]{1,0:T(8,128)(2,1)S(1)}, bf16[384,128]{1,0:T(8,128)(2,1)S(1)}, u32[]{:S(2)}, u32[]{:S(2)}) collective-permute-start(bf16[384,128]{1,0:T(8,128)(2,1)S(1)} %level2_0.1.refs_3_.refs_0_), channel_id=1, source_target_pairs={{0,4},{1,5},{2,6},{3,7},{4,0},{5,1},{6,2},{7,3},{8,12},{9,13},{10,... | collective-permute-start | bytes 294920 | tf_op jit(solution)/shard_map/ppermute | solution.py:57
  15.6 13.3 %collective-permute-start.9 = (bf16[384,384]{1,0:T(8,128)(2,1)S(1)}, bf16[384,384]{1,0:T(8,128)(2,1)S(1)}, u32[]{:S(2)}, u32[]{:S(2)}) collective-permute-start(bf16[384,384]{1,0:T(8,128)(2,1)S(1)} %level1_2.1.refs_3_.refs_0_), channel_id=1, source_target_pairs={{0,2},{1,3},{2,0},{3,1},{4,6},{5,7},{6,4},{7,5},{8,10},{9,11},{10,... | collective-permute-start | bytes 884744 | tf_op jit(solution)/shard_map/ppermute | solution.py:57
  20.1 13.8 %collective-permute-start.12 = (bf16[384,256]{1,0:T(8,128)(2,1)S(1)}, bf16[384,256]{1,0:T(8,128)(2,1)S(1)}, u32[]{:S(2)}, u32[]{:S(2)}) collective-permute-start(bf16[384,256]{1,0:T(8,128)(2,1)S(1)} %level2_1.1.refs_3_.refs_0_), channel_id=1, source_target_pairs={{0,4},{1,5},{2,6},{3,7},{4,0},{5,1},{6,2},{7,3},{8,12},{9,13},{10,... | collective-permute-start | bytes 589832 | tf_op jit(solution)/shard_map/ppermute | solution.py:57
  20.9 1.4 %collective-permute-start.5 = (bf16[384,128]{1,0:T(8,128)(2,1)S(1)}, bf16[384,128]{1,0:T(8,128)(2,1)S(1)}, u32[]{:S(2)}, u32[]{:S(2)}) collective-permute-start(bf16[384,128]{1,0:T(8,128)(2,1)S(1)} %level3_0.1.refs_0_), channel_id=1, source_target_pairs={{0,1},{1,0},{2,3},{3,2},{4,5},{5,4},{6,7},{7,6},{8,9},{9,8},{10,11... | collective-permute-start | bytes 294920 | tf_op jit(solution)/shard_map/ppermute | solution.py:57
  22.8 8.1 %collective-permute-start.6 = (bf16[256,128]{1,0:T(8,128)(2,1)S(1)}, bf16[256,128]{1,0:T(8,128)(2,1)S(1)}, u32[]{:S(2)}, u32[]{:S(2)}) collective-permute-start(bf16[256,128]{1,0:T(8,128)(2,1)S(1)} %get-tuple-element.46), channel_id=1, source_target_pairs={{0,24},{8,16},{16,8},{24,0},{1,25},{9,17},{17,9},{25,1},{2,26},{10... | collective-permute-start | bytes 196616 | tf_op jit(solution)/shard_map/ppermute | solution.py:57
  25.4 5.6 %collective-permute-start.7 = (bf16[256,128]{1,0:T(8,128)(2,1)S(1)}, bf16[256,128]{1,0:T(8,128)(2,1)S(1)}, u32[]{:S(2)}, u32[]{:S(2)}) collective-permute-start(bf16[256,128]{1,0:T(8,128)(2,1)S(1)} %get-tuple-element.47), channel_id=1, source_target_pairs={{0,16},{8,24},{16,0},{24,8},{1,17},{9,25},{17,1},{25,9},{2,18},{10... | collective-permute-start | bytes 196616 | tf_op jit(solution)/shard_map/ppermute | solution.py:57
  25.9 5.1 %collective-permute-start.8 = (bf16[256,128]{1,0:T(8,128)(2,1)S(1)}, bf16[256,128]{1,0:T(8,128)(2,1)S(1)}, u32[]{:S(2)}, u32[]{:S(2)}) collective-permute-start(bf16[256,128]{1,0:T(8,128)(2,1)S(1)} %get-tuple-element.48), channel_id=1, source_target_pairs={{0,8},{8,0},{16,24},{24,16},{1,9},{9,1},{17,25},{25,17},{2,10},{10... | collective-permute-start | bytes 196616 | tf_op jit(solution)/shard_map/ppermute | solution.py:57
  29.4 15.9 %collective-permute-start.10 = (bf16[384,384]{1,0:T(8,128)(2,1)S(1)}, bf16[384,384]{1,0:T(8,128)(2,1)S(1)}, u32[]{:S(2)}, u32[]{:S(2)}) collective-permute-start(bf16[384,384]{1,0:T(8,128)(2,1)S(1)} %level2_2.1.refs_4_.refs_0_), channel_id=1, source_target_pairs={{0,4},{1,5},{2,6},{3,7},{4,0},{5,1},{6,2},{7,3},{8,12},{9,13},{10,... | collective-permute-start | bytes 884744 | tf_op jit(solution)/shard_map/ppermute | solution.py:57
  31.4 9.6 %collective-permute-start.11 = (bf16[384,256]{1,0:T(8,128)(2,1)S(1)}, bf16[384,256]{1,0:T(8,128)(2,1)S(1)}, u32[]{:S(2)}, u32[]{:S(2)}) collective-permute-start(bf16[384,256]{1,0:T(8,128)(2,1)S(1)} %level1_3.1.refs_3_.refs_0_), channel_id=1, source_target_pairs={{0,2},{1,3},{2,0},{3,1},{4,6},{5,7},{6,4},{7,5},{8,10},{9,11},{10,... | collective-permute-start | bytes 589832 | tf_op jit(solution)/shard_map/ppermute | solution.py:57
  34.3 1.5 %collective-permute-start.13 = (bf16[384,256]{1,0:T(8,128)(2,1)S(1)}, bf16[384,256]{1,0:T(8,128)(2,1)S(1)}, u32[]{:S(2)}, u32[]{:S(2)}) collective-permute-start(bf16[384,256]{1,0:T(8,128)(2,1)S(1)} %level3_1.1.refs_0_), channel_id=1, source_target_pairs={{0,1},{1,0},{2,3},{3,2},{4,5},{5,4},{6,7},{7,6},{8,9},{9,8},{10,11... | collective-permute-start | bytes 589832 | tf_op jit(solution)/shard_map/ppermute | solution.py:57
  36.6 9.3 %collective-permute-start.14 = (bf16[256,256]{1,0:T(8,128)(2,1)S(1)}, bf16[256,256]{1,0:T(8,128)(2,1)S(1)}, u32[]{:S(2)}, u32[]{:S(2)}) collective-permute-start(bf16[256,256]{1,0:T(8,128)(2,1)S(1)} %get-tuple-element.50), channel_id=1, source_target_pairs={{0,24},{8,16},{16,8},{24,0},{1,25},{9,17},{17,9},{25,1},{2,26},{10... | collective-permute-start | bytes 393224 | tf_op jit(solution)/shard_map/ppermute | solution.py:57
  39.1 6.8 %collective-permute-start.15 = (bf16[256,256]{1,0:T(8,128)(2,1)S(1)}, bf16[256,256]{1,0:T(8,128)(2,1)S(1)}, u32[]{:S(2)}, u32[]{:S(2)}) collective-permute-start(bf16[256,256]{1,0:T(8,128)(2,1)S(1)} %get-tuple-element.51), channel_id=1, source_target_pairs={{0,16},{8,24},{16,0},{24,8},{1,17},{9,25},{17,1},{25,9},{2,18},{10... | collective-permute-start | bytes 393224 | tf_op jit(solution)/shard_map/ppermute | solution.py:57
  39.6 6.4 %collective-permute-start.16 = (bf16[256,256]{1,0:T(8,128)(2,1)S(1)}, bf16[256,256]{1,0:T(8,128)(2,1)S(1)}, u32[]{:S(2)}, u32[]{:S(2)}) collective-permute-start(bf16[256,256]{1,0:T(8,128)(2,1)S(1)} %get-tuple-element.52), channel_id=1, source_target_pairs={{0,8},{8,0},{16,24},{24,16},{1,9},{9,1},{17,25},{25,17},{2,10},{10... | collective-permute-start | bytes 393224 | tf_op jit(solution)/shard_map/ppermute | solution.py:57
  41.3 15.2 %collective-permute-start.20 = (bf16[384,256]{1,0:T(8,128)(2,1)S(1)}, bf16[384,256]{1,0:T(8,128)(2,1)S(1)}, u32[]{:S(2)}, u32[]{:S(2)}) collective-permute-start(bf16[384,256]{1,0:T(8,128)(2,1)S(1)} %level2_3.1.refs_3_.refs_0_), channel_id=1, source_target_pairs={{0,4},{1,5},{2,6},{3,7},{4,0},{5,1},{6,2},{7,3},{8,12},{9,13},{10,... | collective-permute-start | bytes 589832 | tf_op jit(solution)/shard_map/ppermute | solution.py:57
  45.8 1.6 %collective-permute-start.17 = (bf16[384,384]{1,0:T(8,128)(2,1)S(1)}, bf16[384,384]{1,0:T(8,128)(2,1)S(1)}, u32[]{:S(2)}, u32[]{:S(2)}) collective-permute-start(bf16[384,384]{1,0:T(8,128)(2,1)S(1)} %level3_2.1.refs_0_), channel_id=1, source_target_pairs={{0,1},{1,0},{2,3},{3,2},{4,5},{5,4},{6,7},{7,6},{8,9},{9,8},{10,11... | collective-permute-start | bytes 884744 | tf_op jit(solution)/shard_map/ppermute | solution.py:57
  48.7 14.1 %collective-permute-start.18 = (bf16[256,384]{1,0:T(8,128)(2,1)S(1)}, bf16[256,384]{1,0:T(8,128)(2,1)S(1)}, u32[]{:S(2)}, u32[]{:S(2)}) collective-permute-start(bf16[256,384]{1,0:T(8,128)(2,1)S(1)} %get-tuple-element.56), channel_id=1, source_target_pairs={{0,8},{8,0},{16,24},{24,16},{1,9},{9,1},{17,25},{25,17},{2,10},{10... | collective-permute-start | bytes 589832 | tf_op jit(solution)/shard_map/ppermute | solution.py:57
  55.0 7.8 %collective-permute-start.19 = (bf16[256,384]{1,0:T(8,128)(2,1)S(1)}, bf16[256,384]{1,0:T(8,128)(2,1)S(1)}, u32[]{:S(2)}, u32[]{:S(2)}) collective-permute-start(bf16[256,384]{1,0:T(8,128)(2,1)S(1)} %get-tuple-element.58), channel_id=1, source_target_pairs={{0,16},{8,24},{16,0},{24,8},{1,17},{9,25},{17,1},{25,9},{2,18},{10... | collective-permute-start | bytes 589832 | tf_op jit(solution)/shard_map/ppermute | solution.py:57
  56.9 1.5 %collective-permute-start.21 = (bf16[384,256]{1,0:T(8,128)(2,1)S(1)}, bf16[384,256]{1,0:T(8,128)(2,1)S(1)}, u32[]{:S(2)}, u32[]{:S(2)}) collective-permute-start(bf16[384,256]{1,0:T(8,128)(2,1)S(1)} %level3_3.1.refs_0_), channel_id=1, source_target_pairs={{0,1},{1,0},{2,3},{3,2},{4,5},{5,4},{6,7},{7,6},{8,9},{9,8},{10,11... | collective-permute-start | bytes 589832 | tf_op jit(solution)/shard_map/ppermute | solution.py:57
  59.2 10.6 %collective-permute-start.24 = (bf16[256,256]{1,0:T(8,128)(2,1)S(1)}, bf16[256,256]{1,0:T(8,128)(2,1)S(1)}, u32[]{:S(2)}, u32[]{:S(2)}) collective-permute-start(bf16[256,256]{1,0:T(8,128)(2,1)S(1)} %get-tuple-element.64), channel_id=1, source_target_pairs={{0,24},{8,16},{16,8},{24,0},{1,25},{9,17},{17,9},{25,1},{2,26},{10... | collective-permute-start | bytes 393224 | tf_op jit(solution)/shard_map/ppermute | solution.py:57
  59.3 10.6 %collective-permute-start.25 = (bf16[256,256]{1,0:T(8,128)(2,1)S(1)}, bf16[256,256]{1,0:T(8,128)(2,1)S(1)}, u32[]{:S(2)}, u32[]{:S(2)}) collective-permute-start(bf16[256,256]{1,0:T(8,128)(2,1)S(1)} %get-tuple-element.65), channel_id=1, source_target_pairs={{0,16},{8,24},{16,0},{24,8},{1,17},{9,25},{17,1},{25,9},{2,18},{10... | collective-permute-start | bytes 393224 | tf_op jit(solution)/shard_map/ppermute | solution.py:57
  61.3 8.6 %collective-permute-start.26 = (bf16[256,256]{1,0:T(8,128)(2,1)S(1)}, bf16[256,256]{1,0:T(8,128)(2,1)S(1)}, u32[]{:S(2)}, u32[]{:S(2)}) collective-permute-start(bf16[256,256]{1,0:T(8,128)(2,1)S(1)} %get-tuple-element.66), channel_id=1, source_target_pairs={{0,8},{8,0},{16,24},{24,16},{1,9},{9,1},{17,25},{25,17},{2,10},{10... | collective-permute-start | bytes 393224 | tf_op jit(solution)/shard_map/ppermute | solution.py:57
  62.9 7.0 %collective-permute-start.22 = (bf16[128,384]{1,0:T(8,128)(2,1)S(1)}, bf16[128,384]{1,0:T(8,128)(2,1)S(1)}, u32[]{:S(2)}, u32[]{:S(2)}) collective-permute-start(bf16[128,384]{1,0:T(8,128)(2,1)S(1)} %get-tuple-element.61), channel_id=1, source_target_pairs={{0,16},{8,24},{16,0},{24,8},{1,17},{9,25},{17,1},{25,9},{2,18},{10... | collective-permute-start | bytes 294920 | tf_op jit(solution)/shard_map/ppermute | solution.py:57
  63.4 6.4 %collective-permute-start.23 = (bf16[128,384]{1,0:T(8,128)(2,1)S(1)}, bf16[128,384]{1,0:T(8,128)(2,1)S(1)}, u32[]{:S(2)}, u32[]{:S(2)}) collective-permute-start(bf16[128,384]{1,0:T(8,128)(2,1)S(1)} %get-tuple-element.63), channel_id=1, source_target_pairs={{0,8},{8,0},{16,24},{24,16},{1,9},{9,1},{17,25},{25,17},{2,10},{10... | collective-permute-start | bytes 294920 | tf_op jit(solution)/shard_map/ppermute | solution.py:57

commit v23 on v22

--- a/solution.py
+++ b/solution.py
@@ -153,6 +153,17 @@
     refs[-1][...] = total.astype(BF16)
 
 
+def half_kernel(bit, parts, own, weights, partial):
+    for s, start, stop in parts:
+        partial[:, start:stop] = half_dot(weights, s, upper_half(bit), own[:, start:stop])
+
+
+def finish_kernel(bit, parts, partial, other, weights, out):
+    for s, start, stop in parts:
+        mixed = partial[:, start:stop] + half_dot(weights, s, 1 - upper_half(bit), other[:, start:stop])
+        out[:, start:stop] = mixed.astype(BF16)
+
+
 def between_kernel(bit, parts, counts, folds, own, weights, *refs):
     refs = list(refs)
     groups = [[refs.pop(0) for _ in range(count)] for count in counts]
@@ -394,7 +405,24 @@
     (value,) = step("level1_3", [job1(3)], [total0])
     second(3, value)
     _, group1, _ = tail(1, [coeff2[3]])
-    (value,) = step("level2_3", [(2, 3, coeff2[3], near2[3])], [group1[0]])
+    (partial,) = call(
+        functools.partial(half_kernel, bits[2], parts[3]),
+        "half_3",
+        [VMEM] * 2,
+        [in_vmem(rank, widths[3], dtype=F32)],
+        [],
+        [here(coeff2[3]), here(weights[2])],
+        [group1[0]],
+    )
+    (value,) = call(
+        functools.partial(finish_kernel, bits[2], parts[3]),
+        "level2_3",
+        [VMEM] * 3,
+        [in_vmem(rank, widths[3])],
+        [],
+        [here(partial), here(near2[3]), here(weights[2])],
+        [group1[1]],
+    )
     third(3, value)
     out2, held2, (total1,) = tail(2, [coeff3[3]], [(1, group1)], halving=True)
     out3, group3, _ = tail(3, [out2[0]])

time: 71 us -> 69.5 us (0.979)
  starting transfers between devices: 37.7 us -> 33.2 us
  waiting for transfers between devices: 16.4 us -> 19.2 us
    ppermute x27, starting transfers between devices: 37.7 us -> 33.2 us  [partner(): return lax.ppermute(value, axis, pairs)]
    ppermute x27, waiting for transfers between devices: 16.4 us -> 19.2 us  [partner(): return lax.ppermute(value, axis, pairs)]
    pallas_call x25 -> x26, Pallas kernels: 15.5 us -> 15.7 us  [call(): pl.pallas_call(body, name=name, in_specs=[*in_specs, *[ANY] * (len(after)...]
  transfers between devices with their start and end apart: 27 -> 27, of which waited for: 11 -> 15; matrix products, arithmetic and copies ran while one was open for 0% -> 0% of each run, Pallas kernels for 16% -> 17%
where the time goes in v23:
time: 69.5 us; the launch traced here: 69.3 us
  starting transfers between devices  33.2 us (48%)
  waiting for transfers between devices  19.2 us (28%)
  Pallas kernels  16.6 us (24%)
    ppermute x27, starting transfers between devices, partner(): return lax.ppermute(value, axis, pairs)  33.2 us
    ppermute x27, waiting for transfers between devices, partner(): return lax.ppermute(value, axis, pairs)  19.2 us
    pallas_call x26, Pallas kernels, call(): pl.pallas_call(body, name=name, in_specs=[*in_specs, *[ANY] * (len(after)...  15.7 us
  transfers between devices with their start and end apart: 27, of which 15 were waited for; matrix products, arithmetic and copies ran while one was open for 0% of the time, Pallas kernels for 17%

profile of v23, /device:TPU:0, one launch (start us, length us, event | category | flops | bytes accessed | tf_op | source)
XLA Modules:
  0.0 69.3 jit_solution(7943632795914607554)
XLA Ops:
  0.0 3.7 %leaf.1 = (bf16[384,128]{1,0:T(8,128)(2,1)S(1)}, bf16[384,896]{1,0:T(8,128)(2,1)S(1)}, bf16[2,384,768]{2,1,0:T(8,128)(2,1)S(1)}, bf16[2,384,768]{2,1,0:T(8,128)(2,1)S(1)}) custom-call(bf16[2,1024,512]{2,1,0:T(8,128)(2,1)} %bitcast.9, bf16[2,384,1024]{2,1,0:T(8,128)(2,1)} %bitcast.10, bf16[5,2,384,768]{3,2,1,0:T(8,128)(2,1)} %bitcast.7, s32[2,5]{1,0:T(2,128)} %bitcast.12), custom_call_target="tpu_custom_call" | custom-call | flops 6000000000 | tf_op jit(solution)/shard_map/leaf/pallas_call | solution.py:42
  3.7 0.5 collective-permute-start
  4.2 0.9 %collective-permute-done.refs_1_ = bf16[384,128]{1,0:T(8,128)(2,1)S(1)} collective-permute-done((bf16[384,128]{1,0:T(8,128)(2,1)S(1)}, bf16[384,128]{1,0:T(8,128)(2,1)S(1)}, u32[]{:S(2)}, u32[]{:S(2)}) %collective-permute-start) | collective-permute-done | bytes 98336 | tf_op jit(solution)/shard_map/ppermute | solution.py:57
  5.5 0.4 collective-permute-start.2
  5.9 2.7 %collective-permute-start.1 = (bf16[384,128]{1,0:T(8,128)(2,1)S(1)}, bf16[384,128]{1,0:T(8,128)(2,1)S(1)}, u32[]{:S(2)}, u32[]{:S(2)}) collective-permute-start(bf16[384,128]{1,0:T(8,128)(2,1)S(1)} %get-tuple-element.39.refs_3_.refs_0_), channel_id=1, source_target_pairs={{0,2},{1,3},{2,0},{3,1},{4,6},{5,7},{6,4},{7,5},{8,10},{9,11},{10,... | collective-permute-start | bytes 294920 | tf_op jit(solution)/shard_map/ppermute | solution.py:57
  8.6 0.4 level1_1.1.refs_3_.refs_0_
  9.0 2.1 %collective-permute-start.4 = (bf16[384,256]{1,0:T(8,128)(2,1)S(1)}, bf16[384,256]{1,0:T(8,128)(2,1)S(1)}, u32[]{:S(2)}, u32[]{:S(2)}) collective-permute-start(bf16[384,256]{1,0:T(8,128)(2,1)S(1)} %level1_1.1.refs_3_.refs_0_), channel_id=1, source_target_pairs={{0,2},{1,3},{2,0},{3,1},{4,6},{5,7},{6,4},{7,5},{8,10},{9,11},{10,... | collective-permute-start | bytes 589832 | tf_op jit(solution)/shard_map/ppermute | solution.py:57
  11.0 0.9 %collective-permute-done.1.refs_1_ = bf16[384,128]{1,0:T(8,128)(2,1)S(1)} collective-permute-done((bf16[384,128]{1,0:T(8,128)(2,1)S(1)}, bf16[384,128]{1,0:T(8,128)(2,1)S(1)}, u32[]{:S(2)}, u32[]{:S(2)}) %collective-permute-start.1) | collective-permute-done | bytes 98336 | tf_op jit(solution)/shard_map/ppermute | solution.py:57
  12.3 2.8 %collective-permute-start.3 = (bf16[384,128]{1,0:T(8,128)(2,1)S(1)}, bf16[384,128]{1,0:T(8,128)(2,1)S(1)}, u32[]{:S(2)}, u32[]{:S(2)}) collective-permute-start(bf16[384,128]{1,0:T(8,128)(2,1)S(1)} %level2_0.1.refs_3_.refs_0_), channel_id=1, source_target_pairs={{0,4},{1,5},{2,6},{3,7},{4,0},{5,1},{6,2},{7,3},{8,12},{9,13},{10,... | collective-permute-start | bytes 294920 | tf_op jit(solution)/shard_map/ppermute | solution.py:57
  15.1 0.5 level1_2.1.refs_3_.refs_0_
  15.6 1.6 %collective-permute-start.9 = (bf16[384,384]{1,0:T(8,128)(2,1)S(1)}, bf16[384,384]{1,0:T(8,128)(2,1)S(1)}, u32[]{:S(2)}, u32[]{:S(2)}) collective-permute-start(bf16[384,384]{1,0:T(8,128)(2,1)S(1)} %level1_2.1.refs_3_.refs_0_), channel_id=1, source_target_pairs={{0,2},{1,3},{2,0},{3,1},{4,6},{5,7},{6,4},{7,5},{8,10},{9,11},{10,... | collective-permute-start | bytes 884744 | tf_op jit(solution)/shard_map/ppermute | solution.py:57
  17.3 2.5 %prefetch.1 = (bf16[2,384,768]{2,1,0:T(8,128)(2,1)S(1)}, bf16[2,384,768]{2,1,0:T(8,128)(2,1)S(1)}, bf16[2,1024,384]{2,1,0:T(8,128)(2,1)S(1)}) custom-call(bf16[5,2,384,768]{3,2,1,0:T(8,128)(2,1)} %bitcast.8, bf16[2,1024,384]{2,1,0:T(8,128)(2,1)} %bitcast.11, s32[2,5]{1,0:T(2,128)} %bitcast.13, bf16[384,384]{1,0:T(8,128)(2,1)S(1)} %level1_2.1.refs_3_.refs_0_), custom_call_target="tpu_custom_call" | custom-call | flops 6000000000 | tf_op jit(solution)/shard_map/prefetch/pallas_call | solution.py:42
  20.1 0.4 collective-permute-start.11
  21.2 1.0 %collective-permute-done.5.refs_1_ = bf16[384,128]{1,0:T(8,128)(2,1)S(1)} collective-permute-done((bf16[384,128]{1,0:T(8,128)(2,1)S(1)}, bf16[384,128]{1,0:T(8,128)(2,1)S(1)}, u32[]{:S(2)}, u32[]{:S(2)}) %collective-permute-start.5) | collective-permute-done | bytes 98336 | tf_op jit(solution)/shard_map/ppermute | solution.py:57
  22.3 0.6 last_0.1
  22.8 2.5 %collective-permute-start.6 = (bf16[256,128]{1,0:T(8,128)(2,1)S(1)}, bf16[256,128]{1,0:T(8,128)(2,1)S(1)}, u32[]{:S(2)}, u32[]{:S(2)}) collective-permute-start(bf16[256,128]{1,0:T(8,128)(2,1)S(1)} %get-tuple-element.46), channel_id=1, source_target_pairs={{0,24},{8,16},{16,8},{24,0},{1,25},{9,17},{17,9},{25,1},{2,26},{10... | collective-permute-start | bytes 196616 | tf_op jit(solution)/shard_map/ppermute | solution.py:57
  25.4 0.5 collective-permute-start.7
  25.9 0.5 collective-permute-start.8
  26.4 2.5 %collective-permute-done.9.refs_1_ = bf16[384,384]{1,0:T(8,128)(2,1)S(1)} collective-permute-done((bf16[384,384]{1,0:T(8,128)(2,1)S(1)}, bf16[384,384]{1,0:T(8,128)(2,1)S(1)}, u32[]{:S(2)}, u32[]{:S(2)}) %collective-permute-start.9) | collective-permute-done | bytes 294944 | tf_op jit(solution)/shard_map/ppermute | solution.py:57
  28.9 0.5 level2_2.1.refs_4_.refs_0_
  29.4 1.5 %collective-permute-start.10 = (bf16[384,384]{1,0:T(8,128)(2,1)S(1)}, bf16[384,384]{1,0:T(8,128)(2,1)S(1)}, u32[]{:S(2)}, u32[]{:S(2)}) collective-permute-start(bf16[384,384]{1,0:T(8,128)(2,1)S(1)} %level2_2.1.refs_4_.refs_0_), channel_id=1, source_target_pairs={{0,4},{1,5},{2,6},{3,7},{4,0},{5,1},{6,2},{7,3},{8,12},{9,13},{10,... | collective-permute-start | bytes 884744 | tf_op jit(solution)/shard_map/ppermute | solution.py:57
  31.0 0.4 level1_3.1.refs_3_.refs_0_
  31.4 2.5 %collective-permute-start.13 = (bf16[384,256]{1,0:T(8,128)(2,1)S(1)}, bf16[384,256]{1,0:T(8,128)(2,1)S(1)}, u32[]{:S(2)}, u32[]{:S(2)}) collective-permute-start(bf16[384,256]{1,0:T(8,128)(2,1)S(1)} %level1_3.1.refs_3_.refs_0_), channel_id=1, source_target_pairs={{0,2},{1,3},{2,0},{3,1},{4,6},{5,7},{6,4},{7,5},{8,10},{9,11},{10,... | collective-permute-start | bytes 589832 | tf_op jit(solution)/shard_map/ppermute | solution.py:57
  34.6 1.2 %collective-permute-done.12.refs_1_ = bf16[384,256]{1,0:T(8,128)(2,1)S(1)} collective-permute-done((bf16[384,256]{1,0:T(8,128)(2,1)S(1)}, bf16[384,256]{1,0:T(8,128)(2,1)S(1)}, u32[]{:S(2)}, u32[]{:S(2)}) %collective-permute-start.12) | collective-permute-done | bytes 196640 | tf_op jit(solution)/shard_map/ppermute | solution.py:57
  35.8 0.8 %last_1.1 = (f32[256,256]{1,0:T(8,128)S(1)}, bf16[256,256]{1,0:T(8,128)(2,1)S(1)}, bf16[256,256]{1,0:T(8,128)(2,1)S(1)}, bf16[256,256]{1,0:T(8,128)(2,1)S(1)}) custom-call(f32[384,256]{1,0:T(8,128)S(1)} %between_1.1.refs_0_, bf16[384,256]{1,0:T(8,128)(2,1)S(1)} %collective-permute-done.12.refs_1_, ...), custom_call_target="tpu_custom_call" | custom-call | flops 6000000000 | tf_op jit(solution)/shard_map/last_1/pallas_call | solution.py:42
  36.6 2.5 %collective-permute-start.14 = (bf16[256,256]{1,0:T(8,128)(2,1)S(1)}, bf16[256,256]{1,0:T(8,128)(2,1)S(1)}, u32[]{:S(2)}, u32[]{:S(2)}) collective-permute-start(bf16[256,256]{1,0:T(8,128)(2,1)S(1)} %get-tuple-element.50), channel_id=1, source_target_pairs={{0,24},{8,16},{16,8},{24,0},{1,25},{9,17},{17,9},{25,1},{2,26},{10... | collective-permute-start | bytes 393224 | tf_op jit(solution)/shard_map/ppermute | solution.py:57
  39.3 0.6 collective-permute-start.15
  39.9 0.6 collective-permute-start.16
  40.5 0.5 collective-permute-done.13.refs_1_
  41.0 2.3 %collective-permute-done.14.refs_3_ = bf16[256,256]{1,0:T(8,128)(2,1)S(1)} collective-permute-done((bf16[256,256]{1,0:T(8,128)(2,1)S(1)}, bf16[256,256]{1,0:T(8,128)(2,1)S(1)}, u32[]{:S(2)}, u32[]{:S(2)}) %collective-permute-start.14) | collective-permute-done | bytes 131104 | tf_op jit(solution)/shard_map/ppermute | solution.py:57
  43.5 1.0 %collective-permute-start.20 = (bf16[384,256]{1,0:T(8,128)(2,1)S(1)}, bf16[384,256]{1,0:T(8,128)(2,1)S(1)}, u32[]{:S(2)}, u32[]{:S(2)}) collective-permute-start(bf16[384,256]{1,0:T(8,128)(2,1)S(1)} %level2_3.1.refs_3_.refs_0_), channel_id=1, source_target_pairs={{0,4},{1,5},{2,6},{3,7},{4,0},{5,1},{6,2},{7,3},{8,12},{9,13},{10,... | collective-permute-start | bytes 589832 | tf_op jit(solution)/shard_map/ppermute | solution.py:57
  44.8 0.5 level3_2.1.refs_0_
  45.4 0.5 collective-permute-done.15.refs_4_
  46.0 0.4 between_2.1
  46.3 0.6 collective-permute-done.17.refs_1_
  47.0 1.2 %last_2.1 = (f32[256,384]{1,0:T(8,128)S(1)}, bf16[256,384]{1,0:T(8,128)(2,1)S(1)}, f32[256,384]{1,0:T(8,128)S(1)}, bf16[256,384]{1,0:T(8,128)(2,1)S(1)}) custom-call(f32[384,384]{1,0:T(8,128)S(1)} %get-tuple-element.54.refs_0_, bf16[384,384]{1,0:T(8,128)(2,1)S(1)} %collective-permute-done.17.refs_1_, ...), custom_call_target="tpu_custom_call" | custom-call | flops 6000000000 | tf_op jit(solution)/shard_map/last_2/pallas_call | solution.py:42
  48.2 1.9 %collective-permute-start.18 = (bf16[256,384]{1,0:T(8,128)(2,1)S(1)}, bf16[256,384]{1,0:T(8,128)(2,1)S(1)}, u32[]{:S(2)}, u32[]{:S(2)}) collective-permute-start(bf16[256,384]{1,0:T(8,128)(2,1)S(1)} %get-tuple-element.56), channel_id=1, source_target_pairs={{0,8},{8,0},{16,24},{24,16},{1,9},{9,1},{17,25},{25,17},{2,10},{10... | collective-permute-start | bytes 589832 | tf_op jit(solution)/shard_map/ppermute | solution.py:57
  50.1 1.5 %collective-permute-start.19 = (bf16[256,384]{1,0:T(8,128)(2,1)S(1)}, bf16[256,384]{1,0:T(8,128)(2,1)S(1)}, u32[]{:S(2)}, u32[]{:S(2)}) collective-permute-start(bf16[256,384]{1,0:T(8,128)(2,1)S(1)} %get-tuple-element.58), channel_id=1, source_target_pairs={{0,16},{8,24},{16,0},{24,8},{1,17},{9,25},{17,1},{25,9},{2,18},{10... | collective-permute-start | bytes 589832 | tf_op jit(solution)/shard_map/ppermute | solution.py:57
  51.6 2.5 %collective-permute-done.20.refs_1_ = bf16[384,256]{1,0:T(8,128)(2,1)S(1)} collective-permute-done((bf16[384,256]{1,0:T(8,128)(2,1)S(1)}, bf16[384,256]{1,0:T(8,128)(2,1)S(1)}, u32[]{:S(2)}, u32[]{:S(2)}) %collective-permute-start.20) | collective-permute-done | bytes 196640 | tf_op jit(solution)/shard_map/ppermute | solution.py:57
  54.8 1.2 %collective-permute-done.21.refs_1_ = bf16[384,256]{1,0:T(8,128)(2,1)S(1)} collective-permute-done((bf16[384,256]{1,0:T(8,128)(2,1)S(1)}, bf16[384,256]{1,0:T(8,128)(2,1)S(1)}, u32[]{:S(2)}, u32[]{:S(2)}) %collective-permute-start.21) | collective-permute-done | bytes 196640 | tf_op jit(solution)/shard_map/ppermute | solution.py:57
  56.0 0.8 %last_3.1 = (f32[256,256]{1,0:T(8,128)S(1)}, bf16[256,256]{1,0:T(8,128)(2,1)S(1)}, bf16[256,256]{1,0:T(8,128)(2,1)S(1)}, bf16[256,256]{1,0:T(8,128)(2,1)S(1)}) custom-call(f32[384,256]{1,0:T(8,128)S(1)} %between_3.1.refs_0_, bf16[384,256]{1,0:T(8,128)(2,1)S(1)} %collective-permute-done.21.refs_1_, ...), custom_call_target="tpu_custom_call" | custom-call | tf_op jit(solution)/shard_map/last_3/pallas_call | solution.py:42
  56.8 2.5 %collective-permute-start.24 = (bf16[256,256]{1,0:T(8,128)(2,1)S(1)}, bf16[256,256]{1,0:T(8,128)(2,1)S(1)}, u32[]{:S(2)}, u32[]{:S(2)}) collective-permute-start(bf16[256,256]{1,0:T(8,128)(2,1)S(1)} %get-tuple-element.64), channel_id=1, source_target_pairs={{0,24},{8,16},{16,8},{24,0},{1,25},{9,17},{17,9},{25,1},{2,26},{10... | collective-permute-start | bytes 393224 | tf_op jit(solution)/shard_map/ppermute | solution.py:57
  59.3 0.5 collective-permute-start.25
  59.8 0.6 collective-permute-start.26
  60.4 1.6 %collective-permute-start.22 = (bf16[128,384]{1,0:T(8,128)(2,1)S(1)}, bf16[128,384]{1,0:T(8,128)(2,1)S(1)}, u32[]{:S(2)}, u32[]{:S(2)}) collective-permute-start(bf16[128,384]{1,0:T(8,128)(2,1)S(1)} %get-tuple-element.61), channel_id=1, source_target_pairs={{0,16},{8,24},{16,0},{24,8},{1,17},{9,25},{17,1},{25,9},{2,18},{10... | collective-permute-start | bytes 294920 | tf_op jit(solution)/shard_map/ppermute | solution.py:57
  62.0 1.5 %collective-permute-start.23 = (bf16[128,384]{1,0:T(8,128)(2,1)S(1)}, bf16[128,384]{1,0:T(8,128)(2,1)S(1)}, u32[]{:S(2)}, u32[]{:S(2)}) collective-permute-start(bf16[128,384]{1,0:T(8,128)(2,1)S(1)} %get-tuple-element.63), channel_id=1, source_target_pairs={{0,8},{8,0},{16,24},{24,16},{1,9},{9,1},{17,25},{25,17},{2,10},{10... | collective-permute-start | bytes 294920 | tf_op jit(solution)/shard_map/ppermute | solution.py:57
  63.5 4.7 %collective-permute-done.22.refs_1_ = bf16[128,384]{1,0:T(8,128)(2,1)S(1)} collective-permute-done((bf16[128,384]{1,0:T(8,128)(2,1)S(1)}, bf16[128,384]{1,0:T(8,128)(2,1)S(1)}, u32[]{:S(2)}, u32[]{:S(2)}) %collective-permute-start.22) | collective-permute-done | bytes 98336 | tf_op jit(solution)/shard_map/ppermute | solution.py:57
  68.4 0.9 %end.1 = bf16[2,256,512]{2,1,0:T(8,128)(2,1)} custom-call(bf16[256,128]{1,0:T(8,128)(2,1)S(1)} %sum_0.1.refs_3_.refs_0_, bf16[256,256]{1,0:T(8,128)(2,1)S(1)} %get-tuple-element.53.refs_1_, bf16[256,384]{1,0:T(8,128)(2,1)S(1)} %sum_2.1.refs_2_, f32[256,256]{1,0:T(8,128)S(1)} %get-tuple-element.59.refs_4_.refs_3_, ...), custom_call_target="tpu_custom_call" | custom-call | tf_op jit(solution)/shard_map/end/pallas_call | solution.py:445
  (33 shorter events, 4.2 us)
Async XLA Ops:
  3.7 1.5 %collective-permute-start = (bf16[384,128]{1,0:T(8,128)(2,1)S(1)}, bf16[384,128]{1,0:T(8,128)(2,1)S(1)}, u32[]{:S(2)}, u32[]{:S(2)}) collective-permute-start(bf16[384,128]{1,0:T(8,128)(2,1)S(1)} %get-tuple-element.36.refs_0_), channel_id=1, source_target_pairs={{0,1},{1,0},{2,3},{3,2},{4,5},{5,4},{6,7},{7,6},{8,9},{9,8},{10,11... | collective-permute-start | bytes 294920 | tf_op jit(solution)/shard_map/ppermute | solution.py:57
  5.5 3.1 %collective-permute-start.2 = (bf16[384,896]{1,0:T(8,128)(2,1)S(1)}, bf16[384,896]{1,0:T(8,128)(2,1)S(1)}, u32[]{:S(2)}, u32[]{:S(2)}) collective-permute-start(bf16[384,896]{1,0:T(8,128)(2,1)S(1)} %get-tuple-element.41.refs_0_), channel_id=1, source_target_pairs={{0,1},{1,0},{2,3},{3,2},{4,5},{5,4},{6,7},{7,6},{8,9},{9,8},{10,11... | collective-permute-start | bytes 2064392 | tf_op jit(solution)/shard_map/ppermute | solution.py:57
  5.9 6.0 %collective-permute-start.1 = (bf16[384,128]{1,0:T(8,128)(2,1)S(1)}, bf16[384,128]{1,0:T(8,128)(2,1)S(1)}, u32[]{:S(2)}, u32[]{:S(2)}) collective-permute-start(bf16[384,128]{1,0:T(8,128)(2,1)S(1)} %get-tuple-element.39.refs_3_.refs_0_), channel_id=1, source_target_pairs={{0,2},{1,3},{2,0},{3,1},{4,6},{5,7},{6,4},{7,5},{8,10},{9,11},{10,... | collective-permute-start | bytes 294920 | tf_op jit(solution)/shard_map/ppermute | solution.py:57
  9.0 10.8 %collective-permute-start.4 = (bf16[384,256]{1,0:T(8,128)(2,1)S(1)}, bf16[384,256]{1,0:T(8,128)(2,1)S(1)}, u32[]{:S(2)}, u32[]{:S(2)}) collective-permute-start(bf16[384,256]{1,0:T(8,128)(2,1)S(1)} %level1_1.1.refs_3_.refs_0_), channel_id=1, source_target_pairs={{0,2},{1,3},{2,0},{3,1},{4,6},{5,7},{6,4},{7,5},{8,10},{9,11},{10,... | collective-permute-start | bytes 589832 | tf_op jit(solution)/shard_map/ppermute | solution.py:57
  12.3 8.3 %collective-permute-start.3 = (bf16[384,128]{1,0:T(8,128)(2,1)S(1)}, bf16[384,128]{1,0:T(8,128)(2,1)S(1)}, u32[]{:S(2)}, u32[]{:S(2)}) collective-permute-start(bf16[384,128]{1,0:T(8,128)(2,1)S(1)} %level2_0.1.refs_3_.refs_0_), channel_id=1, source_target_pairs={{0,4},{1,5},{2,6},{3,7},{4,0},{5,1},{6,2},{7,3},{8,12},{9,13},{10,... | collective-permute-start | bytes 294920 | tf_op jit(solution)/shard_map/ppermute | solution.py:57
  15.6 13.3 %collective-permute-start.9 = (bf16[384,384]{1,0:T(8,128)(2,1)S(1)}, bf16[384,384]{1,0:T(8,128)(2,1)S(1)}, u32[]{:S(2)}, u32[]{:S(2)}) collective-permute-start(bf16[384,384]{1,0:T(8,128)(2,1)S(1)} %level1_2.1.refs_3_.refs_0_), channel_id=1, source_target_pairs={{0,2},{1,3},{2,0},{3,1},{4,6},{5,7},{6,4},{7,5},{8,10},{9,11},{10,... | collective-permute-start | bytes 884744 | tf_op jit(solution)/shard_map/ppermute | solution.py:57
  20.1 13.8 %collective-permute-start.11 = (bf16[384,256]{1,0:T(8,128)(2,1)S(1)}, bf16[384,256]{1,0:T(8,128)(2,1)S(1)}, u32[]{:S(2)}, u32[]{:S(2)}) collective-permute-start(bf16[384,256]{1,0:T(8,128)(2,1)S(1)} %level2_1.1.refs_3_.refs_0_), channel_id=1, source_target_pairs={{0,4},{1,5},{2,6},{3,7},{4,0},{5,1},{6,2},{7,3},{8,12},{9,13},{10,... | collective-permute-start | bytes 589832 | tf_op jit(solution)/shard_map/ppermute | solution.py:57
  20.9 1.4 %collective-permute-start.5 = (bf16[384,128]{1,0:T(8,128)(2,1)S(1)}, bf16[384,128]{1,0:T(8,128)(2,1)S(1)}, u32[]{:S(2)}, u32[]{:S(2)}) collective-permute-start(bf16[384,128]{1,0:T(8,128)(2,1)S(1)} %level3_0.1.refs_0_), channel_id=1, source_target_pairs={{0,1},{1,0},{2,3},{3,2},{4,5},{5,4},{6,7},{7,6},{8,9},{9,8},{10,11... | collective-permute-start | bytes 294920 | tf_op jit(solution)/shard_map/ppermute | solution.py:57
  22.8 8.1 %collective-permute-start.6 = (bf16[256,128]{1,0:T(8,128)(2,1)S(1)}, bf16[256,128]{1,0:T(8,128)(2,1)S(1)}, u32[]{:S(2)}, u32[]{:S(2)}) collective-permute-start(bf16[256,128]{1,0:T(8,128)(2,1)S(1)} %get-tuple-element.46), channel_id=1, source_target_pairs={{0,24},{8,16},{16,8},{24,0},{1,25},{9,17},{17,9},{25,1},{2,26},{10... | collective-permute-start | bytes 196616 | tf_op jit(solution)/shard_map/ppermute | solution.py:57
  25.4 5.6 %collective-permute-start.7 = (bf16[256,128]{1,0:T(8,128)(2,1)S(1)}, bf16[256,128]{1,0:T(8,128)(2,1)S(1)}, u32[]{:S(2)}, u32[]{:S(2)}) collective-permute-start(bf16[256,128]{1,0:T(8,128)(2,1)S(1)} %get-tuple-element.47), channel_id=1, source_target_pairs={{0,16},{8,24},{16,0},{24,8},{1,17},{9,25},{17,1},{25,9},{2,18},{10... | collective-permute-start | bytes 196616 | tf_op jit(solution)/shard_map/ppermute | solution.py:57
  25.9 5.1 %collective-permute-start.8 = (bf16[256,128]{1,0:T(8,128)(2,1)S(1)}, bf16[256,128]{1,0:T(8,128)(2,1)S(1)}, u32[]{:S(2)}, u32[]{:S(2)}) collective-permute-start(bf16[256,128]{1,0:T(8,128)(2,1)S(1)} %get-tuple-element.48), channel_id=1, source_target_pairs={{0,8},{8,0},{16,24},{24,16},{1,9},{9,1},{17,25},{25,17},{2,10},{10... | collective-permute-start | bytes 196616 | tf_op jit(solution)/shard_map/ppermute | solution.py:57
  29.4 15.4 %collective-permute-start.10 = (bf16[384,384]{1,0:T(8,128)(2,1)S(1)}, bf16[384,384]{1,0:T(8,128)(2,1)S(1)}, u32[]{:S(2)}, u32[]{:S(2)}) collective-permute-start(bf16[384,384]{1,0:T(8,128)(2,1)S(1)} %level2_2.1.refs_4_.refs_0_), channel_id=1, source_target_pairs={{0,4},{1,5},{2,6},{3,7},{4,0},{5,1},{6,2},{7,3},{8,12},{9,13},{10,... | collective-permute-start | bytes 884744 | tf_op jit(solution)/shard_map/ppermute | solution.py:57
  31.4 9.6 %collective-permute-start.13 = (bf16[384,256]{1,0:T(8,128)(2,1)S(1)}, bf16[384,256]{1,0:T(8,128)(2,1)S(1)}, u32[]{:S(2)}, u32[]{:S(2)}) collective-permute-start(bf16[384,256]{1,0:T(8,128)(2,1)S(1)} %level1_3.1.refs_3_.refs_0_), channel_id=1, source_target_pairs={{0,2},{1,3},{2,0},{3,1},{4,6},{5,7},{6,4},{7,5},{8,10},{9,11},{10,... | collective-permute-start | bytes 589832 | tf_op jit(solution)/shard_map/ppermute | solution.py:57
  34.3 1.5 %collective-permute-start.12 = (bf16[384,256]{1,0:T(8,128)(2,1)S(1)}, bf16[384,256]{1,0:T(8,128)(2,1)S(1)}, u32[]{:S(2)}, u32[]{:S(2)}) collective-permute-start(bf16[384,256]{1,0:T(8,128)(2,1)S(1)} %level3_1.1.refs_0_), channel_id=1, source_target_pairs={{0,1},{1,0},{2,3},{3,2},{4,5},{5,4},{6,7},{7,6},{8,9},{9,8},{10,11... | collective-permute-start | bytes 589832 | tf_op jit(solution)/shard_map/ppermute | solution.py:57
  36.6 6.6 %collective-permute-start.14 = (bf16[256,256]{1,0:T(8,128)(2,1)S(1)}, bf16[256,256]{1,0:T(8,128)(2,1)S(1)}, u32[]{:S(2)}, u32[]{:S(2)}) collective-permute-start(bf16[256,256]{1,0:T(8,128)(2,1)S(1)} %get-tuple-element.50), channel_id=1, source_target_pairs={{0,24},{8,16},{16,8},{24,0},{1,25},{9,17},{17,9},{25,1},{2,26},{10... | collective-permute-start | bytes 393224 | tf_op jit(solution)/shard_map/ppermute | solution.py:57
  39.3 6.6 %collective-permute-start.15 = (bf16[256,256]{1,0:T(8,128)(2,1)S(1)}, bf16[256,256]{1,0:T(8,128)(2,1)S(1)}, u32[]{:S(2)}, u32[]{:S(2)}) collective-permute-start(bf16[256,256]{1,0:T(8,128)(2,1)S(1)} %get-tuple-element.51), channel_id=1, source_target_pairs={{0,16},{8,24},{16,0},{24,8},{1,17},{9,25},{17,1},{25,9},{2,18},{10... | collective-permute-start | bytes 393224 | tf_op jit(solution)/shard_map/ppermute | solution.py:57
  39.9 6.1 %collective-permute-start.16 = (bf16[256,256]{1,0:T(8,128)(2,1)S(1)}, bf16[256,256]{1,0:T(8,128)(2,1)S(1)}, u32[]{:S(2)}, u32[]{:S(2)}) collective-permute-start(bf16[256,256]{1,0:T(8,128)(2,1)S(1)} %get-tuple-element.52), channel_id=1, source_target_pairs={{0,8},{8,0},{16,24},{24,16},{1,9},{9,1},{17,25},{25,17},{2,10},{10... | collective-permute-start | bytes 393224 | tf_op jit(solution)/shard_map/ppermute | solution.py:57
  43.5 10.6 %collective-permute-start.20 = (bf16[384,256]{1,0:T(8,128)(2,1)S(1)}, bf16[384,256]{1,0:T(8,128)(2,1)S(1)}, u32[]{:S(2)}, u32[]{:S(2)}) collective-permute-start(bf16[384,256]{1,0:T(8,128)(2,1)S(1)} %level2_3.1.refs_3_.refs_0_), channel_id=1, source_target_pairs={{0,4},{1,5},{2,6},{3,7},{4,0},{5,1},{6,2},{7,3},{8,12},{9,13},{10,... | collective-permute-start | bytes 589832 | tf_op jit(solution)/shard_map/ppermute | solution.py:57
  45.3 1.6 %collective-permute-start.17 = (bf16[384,384]{1,0:T(8,128)(2,1)S(1)}, bf16[384,384]{1,0:T(8,128)(2,1)S(1)}, u32[]{:S(2)}, u32[]{:S(2)}) collective-permute-start(bf16[384,384]{1,0:T(8,128)(2,1)S(1)} %level3_2.1.refs_0_), channel_id=1, source_target_pairs={{0,1},{1,0},{2,3},{3,2},{4,5},{5,4},{6,7},{7,6},{8,9},{9,8},{10,11... | collective-permute-start | bytes 884744 | tf_op jit(solution)/shard_map/ppermute | solution.py:57
  48.2 12.2 %collective-permute-start.18 = (bf16[256,384]{1,0:T(8,128)(2,1)S(1)}, bf16[256,384]{1,0:T(8,128)(2,1)S(1)}, u32[]{:S(2)}, u32[]{:S(2)}) collective-permute-start(bf16[256,384]{1,0:T(8,128)(2,1)S(1)} %get-tuple-element.56), channel_id=1, source_target_pairs={{0,8},{8,0},{16,24},{24,16},{1,9},{9,1},{17,25},{25,17},{2,10},{10... | collective-permute-start | bytes 589832 | tf_op jit(solution)/shard_map/ppermute | solution.py:57
  50.1 10.3 %collective-permute-start.19 = (bf16[256,384]{1,0:T(8,128)(2,1)S(1)}, bf16[256,384]{1,0:T(8,128)(2,1)S(1)}, u32[]{:S(2)}, u32[]{:S(2)}) collective-permute-start(bf16[256,384]{1,0:T(8,128)(2,1)S(1)} %get-tuple-element.58), channel_id=1, source_target_pairs={{0,16},{8,24},{16,0},{24,8},{1,17},{9,25},{17,1},{25,9},{2,18},{10... | collective-permute-start | bytes 589832 | tf_op jit(solution)/shard_map/ppermute | solution.py:57
  54.5 1.5 %collective-permute-start.21 = (bf16[384,256]{1,0:T(8,128)(2,1)S(1)}, bf16[384,256]{1,0:T(8,128)(2,1)S(1)}, u32[]{:S(2)}, u32[]{:S(2)}) collective-permute-start(bf16[384,256]{1,0:T(8,128)(2,1)S(1)} %level3_3.1.refs_0_), channel_id=1, source_target_pairs={{0,1},{1,0},{2,3},{3,2},{4,5},{5,4},{6,7},{7,6},{8,9},{9,8},{10,11... | collective-permute-start | bytes 589832 | tf_op jit(solution)/shard_map/ppermute | solution.py:57
  56.8 11.6 %collective-permute-start.24 = (bf16[256,256]{1,0:T(8,128)(2,1)S(1)}, bf16[256,256]{1,0:T(8,128)(2,1)S(1)}, u32[]{:S(2)}, u32[]{:S(2)}) collective-permute-start(bf16[256,256]{1,0:T(8,128)(2,1)S(1)} %get-tuple-element.64), channel_id=1, source_target_pairs={{0,24},{8,16},{16,8},{24,0},{1,25},{9,17},{17,9},{25,1},{2,26},{10... | collective-permute-start | bytes 393224 | tf_op jit(solution)/shard_map/ppermute | solution.py:57
  59.3 9.0 %collective-permute-start.25 = (bf16[256,256]{1,0:T(8,128)(2,1)S(1)}, bf16[256,256]{1,0:T(8,128)(2,1)S(1)}, u32[]{:S(2)}, u32[]{:S(2)}) collective-permute-start(bf16[256,256]{1,0:T(8,128)(2,1)S(1)} %get-tuple-element.65), channel_id=1, source_target_pairs={{0,16},{8,24},{16,0},{24,8},{1,17},{9,25},{17,1},{25,9},{2,18},{10... | collective-permute-start | bytes 393224 | tf_op jit(solution)/shard_map/ppermute | solution.py:57
  59.8 8.6 %collective-permute-start.26 = (bf16[256,256]{1,0:T(8,128)(2,1)S(1)}, bf16[256,256]{1,0:T(8,128)(2,1)S(1)}, u32[]{:S(2)}, u32[]{:S(2)}) collective-permute-start(bf16[256,256]{1,0:T(8,128)(2,1)S(1)} %get-tuple-element.66), channel_id=1, source_target_pairs={{0,8},{8,0},{16,24},{24,16},{1,9},{9,1},{17,25},{25,17},{2,10},{10... | collective-permute-start | bytes 393224 | tf_op jit(solution)/shard_map/ppermute | solution.py:57
  60.4 7.8 %collective-permute-start.22 = (bf16[128,384]{1,0:T(8,128)(2,1)S(1)}, bf16[128,384]{1,0:T(8,128)(2,1)S(1)}, u32[]{:S(2)}, u32[]{:S(2)}) collective-permute-start(bf16[128,384]{1,0:T(8,128)(2,1)S(1)} %get-tuple-element.61), channel_id=1, source_target_pairs={{0,16},{8,24},{16,0},{24,8},{1,17},{9,25},{17,1},{25,9},{2,18},{10... | collective-permute-start | bytes 294920 | tf_op jit(solution)/shard_map/ppermute | solution.py:57
  62.0 6.3 %collective-permute-start.23 = (bf16[128,384]{1,0:T(8,128)(2,1)S(1)}, bf16[128,384]{1,0:T(8,128)(2,1)S(1)}, u32[]{:S(2)}, u32[]{:S(2)}) collective-permute-start(bf16[128,384]{1,0:T(8,128)(2,1)S(1)} %get-tuple-element.63), channel_id=1, source_target_pairs={{0,8},{8,0},{16,24},{24,16},{1,9},{9,1},{17,25},{25,17},{2,10},{10... | collective-permute-start | bytes 294920 | tf_op jit(solution)/shard_map/ppermute | solution.py:57

commit v24 on v23

--- a/solution.py
+++ b/solution.py
@@ -424,20 +424,16 @@
         [group1[1]],
     )
     third(3, value)
-    out2, held2, (total1,) = tail(2, [coeff3[3]], [(1, group1)], halving=True)
-    out3, group3, _ = tail(3, [out2[0]])
-    more = call(
-        fold_kernel, "fold_2", [VMEM] * 4, halves(2, 1), [], [here(v) for v in held2], [out3[0]], 0
-    )
-    held2 = exchange(more, len(masks) - 1)
+    _, group2, (total1,) = tail(2, [coeff3[3]], [(1, group1)])
+    _, group3, _ = tail(3, [group2[0]])
     (total2,) = call(
-        join_kernel,
+        sum_kernel,
         "sum_2",
-        [VMEM] * 4,
+        [VMEM] * n_blk,
         [in_vmem(rows, widths[2])],
         [],
-        [here(v) for v in held2],
-        [out3[0]],
+        [here(v) for v in group2],
+        [group3[0]],
         0,
     )
     groups = [[total0], [total1], [total2], group3]

time: 69.5 us -> 67.5 us (0.971)
  starting transfers between devices: 33.2 us -> 30.3 us
  waiting for transfers between devices: 19.2 us -> 20.2 us
    ppermute x27 -> x26, starting transfers between devices: 33.2 us -> 30.3 us  [partner(): return lax.ppermute(value, axis, pairs)]
    ppermute x27 -> x26, waiting for transfers between devices: 19.2 us -> 20.2 us  [partner(): return lax.ppermute(value, axis, pairs)]
    pallas_call x26 -> x25, Pallas kernels: 15.7 us -> 15.7 us  [call(): pl.pallas_call(body, name=name, in_specs=[*in_specs, *[ANY] * (len(after)...]
  transfers between devices with their start and end apart: 27 -> 26, of which waited for: 15 -> 18; matrix products, arithmetic and copies ran while one was open for 0% -> 0% of each run, Pallas kernels for 17% -> 17%
where the time goes in v24:
time: 67.5 us; the launch traced here: 67.3 us
  starting transfers between devices  30.3 us (45%)
  waiting for transfers between devices  20.2 us (30%)
  Pallas kernels  16.6 us (25%)
    ppermute x26, starting transfers between devices, partner(): return lax.ppermute(value, axis, pairs)  30.3 us
    ppermute x26, waiting for transfers between devices, partner(): return lax.ppermute(value, axis, pairs)  20.2 us
    pallas_call x25, Pallas kernels, call(): pl.pallas_call(body, name=name, in_specs=[*in_specs, *[ANY] * (len(after)...  15.7 us
  transfers between devices with their start and end apart: 26, of which 18 were waited for; matrix products, arithmetic and copies ran while one was open for 0% of the time, Pallas kernels for 17%

profile of v24, /device:TPU:0, one launch (start us, length us, event | category | flops | bytes accessed | tf_op | source)
XLA Modules:
  0.0 67.3 jit_solution(9618695643313006829)
XLA Ops:
  0.0 3.7 %leaf.1 = (bf16[384,128]{1,0:T(8,128)(2,1)S(1)}, bf16[384,896]{1,0:T(8,128)(2,1)S(1)}, bf16[2,384,768]{2,1,0:T(8,128)(2,1)S(1)}, bf16[2,384,768]{2,1,0:T(8,128)(2,1)S(1)}) custom-call(bf16[2,1024,512]{2,1,0:T(8,128)(2,1)} %bitcast.9, bf16[2,384,1024]{2,1,0:T(8,128)(2,1)} %bitcast.10, bf16[5,2,384,768]{3,2,1,0:T(8,128)(2,1)} %bitcast.7, s32[2,5]{1,0:T(2,128)} %bitcast.12), custom_call_target="tpu_custom_call" | custom-call | flops 6000000000 | tf_op jit(solution)/shard_map/leaf/pallas_call | solution.py:42
  3.7 0.5 collective-permute-start
  4.2 0.9 %collective-permute-done.refs_1_ = bf16[384,128]{1,0:T(8,128)(2,1)S(1)} collective-permute-done((bf16[384,128]{1,0:T(8,128)(2,1)S(1)}, bf16[384,128]{1,0:T(8,128)(2,1)S(1)}, u32[]{:S(2)}, u32[]{:S(2)}) %collective-permute-start) | collective-permute-done | bytes 98336 | tf_op jit(solution)/shard_map/ppermute | solution.py:57
  5.5 0.4 collective-permute-start.2
  5.9 2.7 %collective-permute-start.1 = (bf16[384,128]{1,0:T(8,128)(2,1)S(1)}, bf16[384,128]{1,0:T(8,128)(2,1)S(1)}, u32[]{:S(2)}, u32[]{:S(2)}) collective-permute-start(bf16[384,128]{1,0:T(8,128)(2,1)S(1)} %get-tuple-element.35.refs_3_.refs_0_), channel_id=1, source_target_pairs={{0,2},{1,3},{2,0},{3,1},{4,6},{5,7},{6,4},{7,5},{8,10},{9,11},{10,... | collective-permute-start | bytes 294920 | tf_op jit(solution)/shard_map/ppermute | solution.py:57
  8.6 0.4 level1_1.1.refs_3_.refs_0_
  9.0 2.1 %collective-permute-start.4 = (bf16[384,256]{1,0:T(8,128)(2,1)S(1)}, bf16[384,256]{1,0:T(8,128)(2,1)S(1)}, u32[]{:S(2)}, u32[]{:S(2)}) collective-permute-start(bf16[384,256]{1,0:T(8,128)(2,1)S(1)} %level1_1.1.refs_3_.refs_0_), channel_id=1, source_target_pairs={{0,2},{1,3},{2,0},{3,1},{4,6},{5,7},{6,4},{7,5},{8,10},{9,11},{10,... | collective-permute-start | bytes 589832 | tf_op jit(solution)/shard_map/ppermute | solution.py:57
  11.0 0.9 %collective-permute-done.1.refs_1_ = bf16[384,128]{1,0:T(8,128)(2,1)S(1)} collective-permute-done((bf16[384,128]{1,0:T(8,128)(2,1)S(1)}, bf16[384,128]{1,0:T(8,128)(2,1)S(1)}, u32[]{:S(2)}, u32[]{:S(2)}) %collective-permute-start.1) | collective-permute-done | bytes 98336 | tf_op jit(solution)/shard_map/ppermute | solution.py:57
  12.3 2.8 %collective-permute-start.3 = (bf16[384,128]{1,0:T(8,128)(2,1)S(1)}, bf16[384,128]{1,0:T(8,128)(2,1)S(1)}, u32[]{:S(2)}, u32[]{:S(2)}) collective-permute-start(bf16[384,128]{1,0:T(8,128)(2,1)S(1)} %level2_0.1.refs_3_.refs_0_), channel_id=1, source_target_pairs={{0,4},{1,5},{2,6},{3,7},{4,0},{5,1},{6,2},{7,3},{8,12},{9,13},{10,... | collective-permute-start | bytes 294920 | tf_op jit(solution)/shard_map/ppermute | solution.py:57
  15.1 0.5 level1_2.1.refs_3_.refs_0_
  15.6 1.6 %collective-permute-start.9 = (bf16[384,384]{1,0:T(8,128)(2,1)S(1)}, bf16[384,384]{1,0:T(8,128)(2,1)S(1)}, u32[]{:S(2)}, u32[]{:S(2)}) collective-permute-start(bf16[384,384]{1,0:T(8,128)(2,1)S(1)} %level1_2.1.refs_3_.refs_0_), channel_id=1, source_target_pairs={{0,2},{1,3},{2,0},{3,1},{4,6},{5,7},{6,4},{7,5},{8,10},{9,11},{10,... | collective-permute-start | bytes 884744 | tf_op jit(solution)/shard_map/ppermute | solution.py:57
  17.3 2.5 %prefetch.1 = (bf16[2,384,768]{2,1,0:T(8,128)(2,1)S(1)}, bf16[2,384,768]{2,1,0:T(8,128)(2,1)S(1)}, bf16[2,1024,384]{2,1,0:T(8,128)(2,1)S(1)}) custom-call(bf16[5,2,384,768]{3,2,1,0:T(8,128)(2,1)} %bitcast.8, bf16[2,1024,384]{2,1,0:T(8,128)(2,1)} %bitcast.11, s32[2,5]{1,0:T(2,128)} %bitcast.13, bf16[384,384]{1,0:T(8,128)(2,1)S(1)} %level1_2.1.refs_3_.refs_0_), custom_call_target="tpu_custom_call" | custom-call | flops 6000000000 | tf_op jit(solution)/shard_map/prefetch/pallas_call | solution.py:42
  20.1 0.4 collective-permute-start.11
  21.2 1.0 %collective-permute-done.5.refs_1_ = bf16[384,128]{1,0:T(8,128)(2,1)S(1)} collective-permute-done((bf16[384,128]{1,0:T(8,128)(2,1)S(1)}, bf16[384,128]{1,0:T(8,128)(2,1)S(1)}, u32[]{:S(2)}, u32[]{:S(2)}) %collective-permute-start.5) | collective-permute-done | bytes 98336 | tf_op jit(solution)/shard_map/ppermute | solution.py:57
  22.3 0.6 last_0.1
  22.8 2.5 %collective-permute-start.6 = (bf16[256,128]{1,0:T(8,128)(2,1)S(1)}, bf16[256,128]{1,0:T(8,128)(2,1)S(1)}, u32[]{:S(2)}, u32[]{:S(2)}) collective-permute-start(bf16[256,128]{1,0:T(8,128)(2,1)S(1)} %get-tuple-element.42), channel_id=1, source_target_pairs={{0,24},{8,16},{16,8},{24,0},{1,25},{9,17},{17,9},{25,1},{2,26},{10... | collective-permute-start | bytes 196616 | tf_op jit(solution)/shard_map/ppermute | solution.py:57
  25.4 0.5 collective-permute-start.7
  25.9 0.5 collective-permute-start.8
  26.4 2.5 %collective-permute-done.9.refs_1_ = bf16[384,384]{1,0:T(8,128)(2,1)S(1)} collective-permute-done((bf16[384,384]{1,0:T(8,128)(2,1)S(1)}, bf16[384,384]{1,0:T(8,128)(2,1)S(1)}, u32[]{:S(2)}, u32[]{:S(2)}) %collective-permute-start.9) | collective-permute-done | bytes 294944 | tf_op jit(solution)/shard_map/ppermute | solution.py:57
  28.9 0.5 level2_2.1.refs_4_.refs_0_
  29.4 1.5 %collective-permute-start.10 = (bf16[384,384]{1,0:T(8,128)(2,1)S(1)}, bf16[384,384]{1,0:T(8,128)(2,1)S(1)}, u32[]{:S(2)}, u32[]{:S(2)}) collective-permute-start(bf16[384,384]{1,0:T(8,128)(2,1)S(1)} %level2_2.1.refs_4_.refs_0_), channel_id=1, source_target_pairs={{0,4},{1,5},{2,6},{3,7},{4,0},{5,1},{6,2},{7,3},{8,12},{9,13},{10,... | collective-permute-start | bytes 884744 | tf_op jit(solution)/shard_map/ppermute | solution.py:57
  31.0 0.4 level1_3.1.refs_3_.refs_0_
  31.4 2.5 %collective-permute-start.13 = (bf16[384,256]{1,0:T(8,128)(2,1)S(1)}, bf16[384,256]{1,0:T(8,128)(2,1)S(1)}, u32[]{:S(2)}, u32[]{:S(2)}) collective-permute-start(bf16[384,256]{1,0:T(8,128)(2,1)S(1)} %level1_3.1.refs_3_.refs_0_), channel_id=1, source_target_pairs={{0,2},{1,3},{2,0},{3,1},{4,6},{5,7},{6,4},{7,5},{8,10},{9,11},{10,... | collective-permute-start | bytes 589832 | tf_op jit(solution)/shard_map/ppermute | solution.py:57
  34.6 1.2 %collective-permute-done.12.refs_1_ = bf16[384,256]{1,0:T(8,128)(2,1)S(1)} collective-permute-done((bf16[384,256]{1,0:T(8,128)(2,1)S(1)}, bf16[384,256]{1,0:T(8,128)(2,1)S(1)}, u32[]{:S(2)}, u32[]{:S(2)}) %collective-permute-start.12) | collective-permute-done | bytes 196640 | tf_op jit(solution)/shard_map/ppermute | solution.py:57
  35.8 0.8 %last_1.1 = (f32[256,256]{1,0:T(8,128)S(1)}, bf16[256,256]{1,0:T(8,128)(2,1)S(1)}, bf16[256,256]{1,0:T(8,128)(2,1)S(1)}, bf16[256,256]{1,0:T(8,128)(2,1)S(1)}) custom-call(f32[384,256]{1,0:T(8,128)S(1)} %between_1.1.refs_0_, bf16[384,256]{1,0:T(8,128)(2,1)S(1)} %collective-permute-done.12.refs_1_, ...), custom_call_target="tpu_custom_call" | custom-call | flops 6000000000 | tf_op jit(solution)/shard_map/last_1/pallas_call | solution.py:42
  36.6 2.5 %collective-permute-start.14 = (bf16[256,256]{1,0:T(8,128)(2,1)S(1)}, bf16[256,256]{1,0:T(8,128)(2,1)S(1)}, u32[]{:S(2)}, u32[]{:S(2)}) collective-permute-start(bf16[256,256]{1,0:T(8,128)(2,1)S(1)} %get-tuple-element.46), channel_id=1, source_target_pairs={{0,24},{8,16},{16,8},{24,0},{1,25},{9,17},{17,9},{25,1},{2,26},{10... | collective-permute-start | bytes 393224 | tf_op jit(solution)/shard_map/ppermute | solution.py:57
  39.3 0.6 collective-permute-start.15
  39.9 0.6 collective-permute-start.16
  40.5 0.5 collective-permute-done.13.refs_1_
  41.0 2.3 %collective-permute-done.14.refs_3_ = bf16[256,256]{1,0:T(8,128)(2,1)S(1)} collective-permute-done((bf16[256,256]{1,0:T(8,128)(2,1)S(1)}, bf16[256,256]{1,0:T(8,128)(2,1)S(1)}, u32[]{:S(2)}, u32[]{:S(2)}) %collective-permute-start.14) | collective-permute-done | bytes 131104 | tf_op jit(solution)/shard_map/ppermute | solution.py:57
  43.5 1.0 %collective-permute-start.21 = (bf16[384,256]{1,0:T(8,128)(2,1)S(1)}, bf16[384,256]{1,0:T(8,128)(2,1)S(1)}, u32[]{:S(2)}, u32[]{:S(2)}) collective-permute-start(bf16[384,256]{1,0:T(8,128)(2,1)S(1)} %level2_3.1.refs_3_.refs_0_), channel_id=1, source_target_pairs={{0,4},{1,5},{2,6},{3,7},{4,0},{5,1},{6,2},{7,3},{8,12},{9,13},{10,... | collective-permute-start | bytes 589832 | tf_op jit(solution)/shard_map/ppermute | solution.py:57
  44.8 0.5 level3_2.1.refs_0_
  45.4 0.5 collective-permute-done.15.refs_4_
  46.0 0.4 between_2.1
  46.3 0.6 collective-permute-done.17.refs_1_
  47.0 1.2 %last_2.1 = (f32[256,384]{1,0:T(8,128)S(1)}, bf16[256,384]{1,0:T(8,128)(2,1)S(1)}, bf16[256,384]{1,0:T(8,128)(2,1)S(1)}, bf16[256,384]{1,0:T(8,128)(2,1)S(1)}) custom-call(f32[384,384]{1,0:T(8,128)S(1)} %get-tuple-element.50.refs_0_, bf16[384,384]{1,0:T(8,128)(2,1)S(1)} %collective-permute-done.17.refs_1_, ...), custom_call_target="tpu_custom_call" | custom-call | flops 6000000000 | tf_op jit(solution)/shard_map/last_2/pallas_call | solution.py:42
  48.2 2.8 %collective-permute-start.18 = (bf16[256,384]{1,0:T(8,128)(2,1)S(1)}, bf16[256,384]{1,0:T(8,128)(2,1)S(1)}, u32[]{:S(2)}, u32[]{:S(2)}) collective-permute-start(bf16[256,384]{1,0:T(8,128)(2,1)S(1)} %get-tuple-element.52), channel_id=1, source_target_pairs={{0,24},{8,16},{16,8},{24,0},{1,25},{9,17},{17,9},{25,1},{2,26},{10... | collective-permute-start | bytes 589832 | tf_op jit(solution)/shard_map/ppermute | solution.py:57
  51.0 0.5 collective-permute-start.19
  51.8 2.4 %collective-permute-done.21.refs_1_ = bf16[384,256]{1,0:T(8,128)(2,1)S(1)} collective-permute-done((bf16[384,256]{1,0:T(8,128)(2,1)S(1)}, bf16[384,256]{1,0:T(8,128)(2,1)S(1)}, u32[]{:S(2)}, u32[]{:S(2)}) %collective-permute-start.21) | collective-permute-done | bytes 196640 | tf_op jit(solution)/shard_map/ppermute | solution.py:57
  54.8 1.2 %collective-permute-done.22.refs_1_ = bf16[384,256]{1,0:T(8,128)(2,1)S(1)} collective-permute-done((bf16[384,256]{1,0:T(8,128)(2,1)S(1)}, bf16[384,256]{1,0:T(8,128)(2,1)S(1)}, u32[]{:S(2)}, u32[]{:S(2)}) %collective-permute-start.22) | collective-permute-done | bytes 196640 | tf_op jit(solution)/shard_map/ppermute | solution.py:57
  56.0 0.8 %last_3.1 = (f32[256,256]{1,0:T(8,128)S(1)}, bf16[256,256]{1,0:T(8,128)(2,1)S(1)}, bf16[256,256]{1,0:T(8,128)(2,1)S(1)}, bf16[256,256]{1,0:T(8,128)(2,1)S(1)}) custom-call(f32[384,256]{1,0:T(8,128)S(1)} %between_3.1.refs_0_, bf16[384,256]{1,0:T(8,128)(2,1)S(1)} %collective-permute-done.22.refs_1_, ...), custom_call_target="tpu_custom_call" | custom-call | tf_op jit(solution)/shard_map/last_3/pallas_call | solution.py:42
  56.8 2.5 %collective-permute-start.23 = (bf16[256,256]{1,0:T(8,128)(2,1)S(1)}, bf16[256,256]{1,0:T(8,128)(2,1)S(1)}, u32[]{:S(2)}, u32[]{:S(2)}) collective-permute-start(bf16[256,256]{1,0:T(8,128)(2,1)S(1)} %get-tuple-element.56), channel_id=1, source_target_pairs={{0,24},{8,16},{16,8},{24,0},{1,25},{9,17},{17,9},{25,1},{2,26},{10... | collective-permute-start | bytes 393224 | tf_op jit(solution)/shard_map/ppermute | solution.py:57
  59.3 0.5 collective-permute-start.24
  59.8 0.6 collective-permute-start.25
  60.5 0.4 collective-permute-done.20.refs_3_
  61.0 2.6 %collective-permute-done.23.refs_4_ = bf16[256,256]{1,0:T(8,128)(2,1)S(1)} collective-permute-done((bf16[256,256]{1,0:T(8,128)(2,1)S(1)}, bf16[256,256]{1,0:T(8,128)(2,1)S(1)}, u32[]{:S(2)}, u32[]{:S(2)}) %collective-permute-start.23) | collective-permute-done | bytes 131104 | tf_op jit(solution)/shard_map/ppermute | solution.py:57
  63.6 2.5 %collective-permute-done.24.refs_5_ = bf16[256,256]{1,0:T(8,128)(2,1)S(1)} collective-permute-done((bf16[256,256]{1,0:T(8,128)(2,1)S(1)}, bf16[256,256]{1,0:T(8,128)(2,1)S(1)}, u32[]{:S(2)}, u32[]{:S(2)}) %collective-permute-start.24) | collective-permute-done | bytes 131104 | tf_op jit(solution)/shard_map/ppermute | solution.py:57
  66.4 0.9 %end.1 = bf16[2,256,512]{2,1,0:T(8,128)(2,1)} custom-call(bf16[256,128]{1,0:T(8,128)(2,1)S(1)} %sum_0.1.refs_3_.refs_0_, bf16[256,256]{1,0:T(8,128)(2,1)S(1)} %get-tuple-element.49.refs_1_, bf16[256,384]{1,0:T(8,128)(2,1)S(1)} %sum_2.1.refs_2_, f32[256,256]{1,0:T(8,128)S(1)} %get-tuple-element.55.refs_4_.refs_3_, ...), custom_call_target="tpu_custom_call" | custom-call | tf_op jit(solution)/shard_map/end/pallas_call | solution.py:441
  (30 shorter events, 4.7 us)
Async XLA Ops:
  3.7 1.5 %collective-permute-start = (bf16[384,128]{1,0:T(8,128)(2,1)S(1)}, bf16[384,128]{1,0:T(8,128)(2,1)S(1)}, u32[]{:S(2)}, u32[]{:S(2)}) collective-permute-start(bf16[384,128]{1,0:T(8,128)(2,1)S(1)} %get-tuple-element.32.refs_0_), channel_id=1, source_target_pairs={{0,1},{1,0},{2,3},{3,2},{4,5},{5,4},{6,7},{7,6},{8,9},{9,8},{10,11... | collective-permute-start | bytes 294920 | tf_op jit(solution)/shard_map/ppermute | solution.py:57
  5.5 3.1 %collective-permute-start.2 = (bf16[384,896]{1,0:T(8,128)(2,1)S(1)}, bf16[384,896]{1,0:T(8,128)(2,1)S(1)}, u32[]{:S(2)}, u32[]{:S(2)}) collective-permute-start(bf16[384,896]{1,0:T(8,128)(2,1)S(1)} %get-tuple-element.37.refs_0_), channel_id=1, source_target_pairs={{0,1},{1,0},{2,3},{3,2},{4,5},{5,4},{6,7},{7,6},{8,9},{9,8},{10,11... | collective-permute-start | bytes 2064392 | tf_op jit(solution)/shard_map/ppermute | solution.py:57
  5.9 6.0 %collective-permute-start.1 = (bf16[384,128]{1,0:T(8,128)(2,1)S(1)}, bf16[384,128]{1,0:T(8,128)(2,1)S(1)}, u32[]{:S(2)}, u32[]{:S(2)}) collective-permute-start(bf16[384,128]{1,0:T(8,128)(2,1)S(1)} %get-tuple-element.35.refs_3_.refs_0_), channel_id=1, source_target_pairs={{0,2},{1,3},{2,0},{3,1},{4,6},{5,7},{6,4},{7,5},{8,10},{9,11},{10,... | collective-permute-start | bytes 294920 | tf_op jit(solution)/shard_map/ppermute | solution.py:57
  9.0 10.8 %collective-permute-start.4 = (bf16[384,256]{1,0:T(8,128)(2,1)S(1)}, bf16[384,256]{1,0:T(8,128)(2,1)S(1)}, u32[]{:S(2)}, u32[]{:S(2)}) collective-permute-start(bf16[384,256]{1,0:T(8,128)(2,1)S(1)} %level1_1.1.refs_3_.refs_0_), channel_id=1, source_target_pairs={{0,2},{1,3},{2,0},{3,1},{4,6},{5,7},{6,4},{7,5},{8,10},{9,11},{10,... | collective-permute-start | bytes 589832 | tf_op jit(solution)/shard_map/ppermute | solution.py:57
  12.3 8.3 %collective-permute-start.3 = (bf16[384,128]{1,0:T(8,128)(2,1)S(1)}, bf16[384,128]{1,0:T(8,128)(2,1)S(1)}, u32[]{:S(2)}, u32[]{:S(2)}) collective-permute-start(bf16[384,128]{1,0:T(8,128)(2,1)S(1)} %level2_0.1.refs_3_.refs_0_), channel_id=1, source_target_pairs={{0,4},{1,5},{2,6},{3,7},{4,0},{5,1},{6,2},{7,3},{8,12},{9,13},{10,... | collective-permute-start | bytes 294920 | tf_op jit(solution)/shard_map/ppermute | solution.py:57
  15.6 13.3 %collective-permute-start.9 = (bf16[384,384]{1,0:T(8,128)(2,1)S(1)}, bf16[384,384]{1,0:T(8,128)(2,1)S(1)}, u32[]{:S(2)}, u32[]{:S(2)}) collective-permute-start(bf16[384,384]{1,0:T(8,128)(2,1)S(1)} %level1_2.1.refs_3_.refs_0_), channel_id=1, source_target_pairs={{0,2},{1,3},{2,0},{3,1},{4,6},{5,7},{6,4},{7,5},{8,10},{9,11},{10,... | collective-permute-start | bytes 884744 | tf_op jit(solution)/shard_map/ppermute | solution.py:57
  20.1 13.8 %collective-permute-start.11 = (bf16[384,256]{1,0:T(8,128)(2,1)S(1)}, bf16[384,256]{1,0:T(8,128)(2,1)S(1)}, u32[]{:S(2)}, u32[]{:S(2)}) collective-permute-start(bf16[384,256]{1,0:T(8,128)(2,1)S(1)} %level2_1.1.refs_3_.refs_0_), channel_id=1, source_target_pairs={{0,4},{1,5},{2,6},{3,7},{4,0},{5,1},{6,2},{7,3},{8,12},{9,13},{10,... | collective-permute-start | bytes 589832 | tf_op jit(solution)/shard_map/ppermute | solution.py:57
  20.9 1.4 %collective-permute-start.5 = (bf16[384,128]{1,0:T(8,128)(2,1)S(1)}, bf16[384,128]{1,0:T(8,128)(2,1)S(1)}, u32[]{:S(2)}, u32[]{:S(2)}) collective-permute-start(bf16[384,128]{1,0:T(8,128)(2,1)S(1)} %level3_0.1.refs_0_), channel_id=1, source_target_pairs={{0,1},{1,0},{2,3},{3,2},{4,5},{5,4},{6,7},{7,6},{8,9},{9,8},{10,11... | collective-permute-start | bytes 294920 | tf_op jit(solution)/shard_map/ppermute | solution.py:57
  22.8 8.1 %collective-permute-start.6 = (bf16[256,128]{1,0:T(8,128)(2,1)S(1)}, bf16[256,128]{1,0:T(8,128)(2,1)S(1)}, u32[]{:S(2)}, u32[]{:S(2)}) collective-permute-start(bf16[256,128]{1,0:T(8,128)(2,1)S(1)} %get-tuple-element.42), channel_id=1, source_target_pairs={{0,24},{8,16},{16,8},{24,0},{1,25},{9,17},{17,9},{25,1},{2,26},{10... | collective-permute-start | bytes 196616 | tf_op jit(solution)/shard_map/ppermute | solution.py:57
  25.4 5.6 %collective-permute-start.7 = (bf16[256,128]{1,0:T(8,128)(2,1)S(1)}, bf16[256,128]{1,0:T(8,128)(2,1)S(1)}, u32[]{:S(2)}, u32[]{:S(2)}) collective-permute-start(bf16[256,128]{1,0:T(8,128)(2,1)S(1)} %get-tuple-element.43), channel_id=1, source_target_pairs={{0,16},{8,24},{16,0},{24,8},{1,17},{9,25},{17,1},{25,9},{2,18},{10... | collective-permute-start | bytes 196616 | tf_op jit(solution)/shard_map/ppermute | solution.py:57
  25.9 5.0 %collective-permute-start.8 = (bf16[256,128]{1,0:T(8,128)(2,1)S(1)}, bf16[256,128]{1,0:T(8,128)(2,1)S(1)}, u32[]{:S(2)}, u32[]{:S(2)}) collective-permute-start(bf16[256,128]{1,0:T(8,128)(2,1)S(1)} %get-tuple-element.44), channel_id=1, source_target_pairs={{0,8},{8,0},{16,24},{24,16},{1,9},{9,1},{17,25},{25,17},{2,10},{10... | collective-permute-start | bytes 196616 | tf_op jit(solution)/shard_map/ppermute | solution.py:57
  29.4 15.4 %collective-permute-start.10 = (bf16[384,384]{1,0:T(8,128)(2,1)S(1)}, bf16[384,384]{1,0:T(8,128)(2,1)S(1)}, u32[]{:S(2)}, u32[]{:S(2)}) collective-permute-start(bf16[384,384]{1,0:T(8,128)(2,1)S(1)} %level2_2.1.refs_4_.refs_0_), channel_id=1, source_target_pairs={{0,4},{1,5},{2,6},{3,7},{4,0},{5,1},{6,2},{7,3},{8,12},{9,13},{10,... | collective-permute-start | bytes 884744 | tf_op jit(solution)/shard_map/ppermute | solution.py:57
  31.4 9.6 %collective-permute-start.13 = (bf16[384,256]{1,0:T(8,128)(2,1)S(1)}, bf16[384,256]{1,0:T(8,128)(2,1)S(1)}, u32[]{:S(2)}, u32[]{:S(2)}) collective-permute-start(bf16[384,256]{1,0:T(8,128)(2,1)S(1)} %level1_3.1.refs_3_.refs_0_), channel_id=1, source_target_pairs={{0,2},{1,3},{2,0},{3,1},{4,6},{5,7},{6,4},{7,5},{8,10},{9,11},{10,... | collective-permute-start | bytes 589832 | tf_op jit(solution)/shard_map/ppermute | solution.py:57
  34.3 1.5 %collective-permute-start.12 = (bf16[384,256]{1,0:T(8,128)(2,1)S(1)}, bf16[384,256]{1,0:T(8,128)(2,1)S(1)}, u32[]{:S(2)}, u32[]{:S(2)}) collective-permute-start(bf16[384,256]{1,0:T(8,128)(2,1)S(1)} %level3_1.1.refs_0_), channel_id=1, source_target_pairs={{0,1},{1,0},{2,3},{3,2},{4,5},{5,4},{6,7},{7,6},{8,9},{9,8},{10,11... | collective-permute-start | bytes 589832 | tf_op jit(solution)/shard_map/ppermute | solution.py:57
  36.6 6.6 %collective-permute-start.14 = (bf16[256,256]{1,0:T(8,128)(2,1)S(1)}, bf16[256,256]{1,0:T(8,128)(2,1)S(1)}, u32[]{:S(2)}, u32[]{:S(2)}) collective-permute-start(bf16[256,256]{1,0:T(8,128)(2,1)S(1)} %get-tuple-element.46), channel_id=1, source_target_pairs={{0,24},{8,16},{16,8},{24,0},{1,25},{9,17},{17,9},{25,1},{2,26},{10... | collective-permute-start | bytes 393224 | tf_op jit(solution)/shard_map/ppermute | solution.py:57
  39.3 6.6 %collective-permute-start.15 = (bf16[256,256]{1,0:T(8,128)(2,1)S(1)}, bf16[256,256]{1,0:T(8,128)(2,1)S(1)}, u32[]{:S(2)}, u32[]{:S(2)}) collective-permute-start(bf16[256,256]{1,0:T(8,128)(2,1)S(1)} %get-tuple-element.47), channel_id=1, source_target_pairs={{0,16},{8,24},{16,0},{24,8},{1,17},{9,25},{17,1},{25,9},{2,18},{10... | collective-permute-start | bytes 393224 | tf_op jit(solution)/shard_map/ppermute | solution.py:57
  39.9 6.1 %collective-permute-start.16 = (bf16[256,256]{1,0:T(8,128)(2,1)S(1)}, bf16[256,256]{1,0:T(8,128)(2,1)S(1)}, u32[]{:S(2)}, u32[]{:S(2)}) collective-permute-start(bf16[256,256]{1,0:T(8,128)(2,1)S(1)} %get-tuple-element.48), channel_id=1, source_target_pairs={{0,8},{8,0},{16,24},{24,16},{1,9},{9,1},{17,25},{25,17},{2,10},{10... | collective-permute-start | bytes 393224 | tf_op jit(solution)/shard_map/ppermute | solution.py:57
  43.5 10.6 %collective-permute-start.21 = (bf16[384,256]{1,0:T(8,128)(2,1)S(1)}, bf16[384,256]{1,0:T(8,128)(2,1)S(1)}, u32[]{:S(2)}, u32[]{:S(2)}) collective-permute-start(bf16[384,256]{1,0:T(8,128)(2,1)S(1)} %level2_3.1.refs_3_.refs_0_), channel_id=1, source_target_pairs={{0,4},{1,5},{2,6},{3,7},{4,0},{5,1},{6,2},{7,3},{8,12},{9,13},{10,... | collective-permute-start | bytes 589832 | tf_op jit(solution)/shard_map/ppermute | solution.py:57
  45.3 1.6 %collective-permute-start.17 = (bf16[384,384]{1,0:T(8,128)(2,1)S(1)}, bf16[384,384]{1,0:T(8,128)(2,1)S(1)}, u32[]{:S(2)}, u32[]{:S(2)}) collective-permute-start(bf16[384,384]{1,0:T(8,128)(2,1)S(1)} %level3_2.1.refs_0_), channel_id=1, source_target_pairs={{0,1},{1,0},{2,3},{3,2},{4,5},{5,4},{6,7},{7,6},{8,9},{9,8},{10,11... | collective-permute-start | bytes 884744 | tf_op jit(solution)/shard_map/ppermute | solution.py:57
  48.2 11.6 %collective-permute-start.18 = (bf16[256,384]{1,0:T(8,128)(2,1)S(1)}, bf16[256,384]{1,0:T(8,128)(2,1)S(1)}, u32[]{:S(2)}, u32[]{:S(2)}) collective-permute-start(bf16[256,384]{1,0:T(8,128)(2,1)S(1)} %get-tuple-element.52), channel_id=1, source_target_pairs={{0,24},{8,16},{16,8},{24,0},{1,25},{9,17},{17,9},{25,1},{2,26},{10... | collective-permute-start | bytes 589832 | tf_op jit(solution)/shard_map/ppermute | solution.py:57
  51.0 9.4 %collective-permute-start.19 = (bf16[256,384]{1,0:T(8,128)(2,1)S(1)}, bf16[256,384]{1,0:T(8,128)(2,1)S(1)}, u32[]{:S(2)}, u32[]{:S(2)}) collective-permute-start(bf16[256,384]{1,0:T(8,128)(2,1)S(1)} %get-tuple-element.53), channel_id=1, source_target_pairs={{0,16},{8,24},{16,0},{24,8},{1,17},{9,25},{17,1},{25,9},{2,18},{10... | collective-permute-start | bytes 589832 | tf_op jit(solution)/shard_map/ppermute | solution.py:57
  51.6 9.3 %collective-permute-start.20 = (bf16[256,384]{1,0:T(8,128)(2,1)S(1)}, bf16[256,384]{1,0:T(8,128)(2,1)S(1)}, u32[]{:S(2)}, u32[]{:S(2)}) collective-permute-start(bf16[256,384]{1,0:T(8,128)(2,1)S(1)} %get-tuple-element.54), channel_id=1, source_target_pairs={{0,8},{8,0},{16,24},{24,16},{1,9},{9,1},{17,25},{25,17},{2,10},{10... | collective-permute-start | bytes 589832 | tf_op jit(solution)/shard_map/ppermute | solution.py:57
  54.5 1.5 %collective-permute-start.22 = (bf16[384,256]{1,0:T(8,128)(2,1)S(1)}, bf16[384,256]{1,0:T(8,128)(2,1)S(1)}, u32[]{:S(2)}, u32[]{:S(2)}) collective-permute-start(bf16[384,256]{1,0:T(8,128)(2,1)S(1)} %level3_3.1.refs_0_), channel_id=1, source_target_pairs={{0,1},{1,0},{2,3},{3,2},{4,5},{5,4},{6,7},{7,6},{8,9},{9,8},{10,11... | collective-permute-start | bytes 589832 | tf_op jit(solution)/shard_map/ppermute | solution.py:57
  56.8 6.8 %collective-permute-start.23 = (bf16[256,256]{1,0:T(8,128)(2,1)S(1)}, bf16[256,256]{1,0:T(8,128)(2,1)S(1)}, u32[]{:S(2)}, u32[]{:S(2)}) collective-permute-start(bf16[256,256]{1,0:T(8,128)(2,1)S(1)} %get-tuple-element.56), channel_id=1, source_target_pairs={{0,24},{8,16},{16,8},{24,0},{1,25},{9,17},{17,9},{25,1},{2,26},{10... | collective-permute-start | bytes 393224 | tf_op jit(solution)/shard_map/ppermute | solution.py:57
  59.3 6.8 %collective-permute-start.24 = (bf16[256,256]{1,0:T(8,128)(2,1)S(1)}, bf16[256,256]{1,0:T(8,128)(2,1)S(1)}, u32[]{:S(2)}, u32[]{:S(2)}) collective-permute-start(bf16[256,256]{1,0:T(8,128)(2,1)S(1)} %get-tuple-element.57), channel_id=1, source_target_pairs={{0,16},{8,24},{16,0},{24,8},{1,17},{9,25},{17,1},{25,9},{2,18},{10... | collective-permute-start | bytes 393224 | tf_op jit(solution)/shard_map/ppermute | solution.py:57
  59.8 6.6 %collective-permute-start.25 = (bf16[256,256]{1,0:T(8,128)(2,1)S(1)}, bf16[256,256]{1,0:T(8,128)(2,1)S(1)}, u32[]{:S(2)}, u32[]{:S(2)}) collective-permute-start(bf16[256,256]{1,0:T(8,128)(2,1)S(1)} %get-tuple-element.58), channel_id=1, source_target_pairs={{0,8},{8,0},{16,24},{24,16},{1,9},{9,1},{17,25},{25,17},{2,10},{10... | collective-permute-start | bytes 393224 | tf_op jit(solution)/shard_map/ppermute | solution.py:57

commit v25 on v24

--- a/solution.py
+++ b/solution.py
@@ -206,6 +206,24 @@
                 ref[to : to + size, start:stop] = piece[begin : begin + size].astype(ref.dtype)
 
 
+def mixed_kernel(bit, parts, d, partial, other, weights, basis, coeff, ref):
+    rows = ref.shape[0]
+    row = pl.multiple_of((lax.axis_index("blk") ^ d) * rows, rows)
+    for s, start, stop in parts:
+        mixed = partial[:, start:stop] + half_dot(weights, s, 1 - upper_half(bit), other[:, start:stop])
+        coeff[:, start:stop] = mixed.astype(BF16)
+        ref[:, start:stop] = dot(basis[s, pl.ds(row, rows), :], coeff[:, start:stop]).astype(BF16)
+
+
+def pieces_kernel(parts, coeff, basis, *refs):
+    rows = refs[0].shape[0]
+    me = lax.axis_index("blk")
+    for s, start, stop in parts:
+        for d, ref in enumerate(refs):
+            row = pl.multiple_of((me ^ d) * rows, rows)
+            ref[:, start:stop] = dot(basis[s, pl.ds(row, rows), :], coeff[:, start:stop]).astype(ref.dtype)
+
+
 def end_kernel(places, counts, *refs):
     refs = list(refs)
     out = refs[-1]
@@ -373,6 +391,27 @@
             [],
             [here(v) for v in (coeff4, weights[4], *extra)],
         )
+        if j >= 2:
+            coeff5, far = call(
+                functools.partial(mixed_kernel, bits[4], parts[j], n_blk - 1),
+                f"far_{j}",
+                [VMEM] * 4,
+                [in_vmem(rank, widths[j]), in_vmem(rows, widths[j])],
+                [],
+                [here(v) for v in (partial, near4, weights[4], basis_v)],
+                flops=COST if j < len(widths) - 1 else 0,
+            )
+            out = call(
+                functools.partial(pieces_kernel, parts[j]),
+                f"last_{j}",
+                [VMEM] * 2,
+                [in_vmem(rows, widths[j], dtype=BF16 if d else F32) for d in range(n_blk - 1)],
+                [],
+                [here(coeff5), here(basis_v)],
+                flops=10**9 if j == 2 else 2 * 10**8,
+            )
+            out = [*out, far]
+            return out, [out[0]] + [partner(out[d], "blk", d) for d in range(n_blk - 1, 0, -1)], more
         if halving:
             outs = halves(j, n_blk // 2)
         else:

time: 67.5 us -> 67.1 us (level)
  waiting for transfers between devices: 20.2 us -> 19.4 us
    ppermute x26, waiting for transfers between devices: 20.2 us -> 19.4 us  [partner(): return lax.ppermute(value, axis, pairs)]
    pallas_call x25 -> x27, Pallas kernels: 15.7 us -> 16 us  [call(): pl.pallas_call(body, name=name, in_specs=[*in_specs, *[ANY] * (len(after)...]
  transfers between devices with their start and end apart: 26 -> 26, of which waited for: 18 -> 16; matrix products, arithmetic and copies ran while one was open for 0% -> 0% of each run, Pallas kernels for 17% -> 18%
where the time goes in v25:
time: 67.1 us; the launch traced here: 66.9 us
  starting transfers between devices  30.4 us (45%)
  waiting for transfers between devices  19.4 us (29%)
  Pallas kernels  16.9 us (25%)
    ppermute x26, starting transfers between devices, partner(): return lax.ppermute(value, axis, pairs)  30.4 us
    ppermute x26, waiting for transfers between devices, partner(): return lax.ppermute(value, axis, pairs)  19.4 us
    pallas_call x27, Pallas kernels, call(): pl.pallas_call(body, name=name, in_specs=[*in_specs, *[ANY] * (len(after)...  16 us
  transfers between devices with their start and end apart: 26, of which 16 were waited for; matrix products, arithmetic and copies ran while one was open for 0% of the time, Pallas kernels for 18%

profile of v25, /device:TPU:0, one launch (start us, length us, event | category | flops | bytes accessed | tf_op | source)
XLA Modules:
  0.0 66.9 jit_solution(10859733997863160703)
XLA Ops:
  0.0 3.7 %leaf.1 = (bf16[384,128]{1,0:T(8,128)(2,1)S(1)}, bf16[384,896]{1,0:T(8,128)(2,1)S(1)}, bf16[2,384,768]{2,1,0:T(8,128)(2,1)S(1)}, bf16[2,384,768]{2,1,0:T(8,128)(2,1)S(1)}) custom-call(bf16[2,1024,512]{2,1,0:T(8,128)(2,1)} %bitcast.9, bf16[2,384,1024]{2,1,0:T(8,128)(2,1)} %bitcast.10, bf16[5,2,384,768]{3,2,1,0:T(8,128)(2,1)} %bitcast.7, s32[2,5]{1,0:T(2,128)} %bitcast.12), custom_call_target="tpu_custom_call" | custom-call | flops 6000000000 | tf_op jit(solution)/shard_map/leaf/pallas_call | solution.py:42
  3.7 0.5 collective-permute-start
  4.2 0.9 %collective-permute-done.refs_1_ = bf16[384,128]{1,0:T(8,128)(2,1)S(1)} collective-permute-done((bf16[384,128]{1,0:T(8,128)(2,1)S(1)}, bf16[384,128]{1,0:T(8,128)(2,1)S(1)}, u32[]{:S(2)}, u32[]{:S(2)}) %collective-permute-start) | collective-permute-done | bytes 98336 | tf_op jit(solution)/shard_map/ppermute | solution.py:57
  5.5 0.4 collective-permute-start.2
  5.9 2.7 %collective-permute-start.1 = (bf16[384,128]{1,0:T(8,128)(2,1)S(1)}, bf16[384,128]{1,0:T(8,128)(2,1)S(1)}, u32[]{:S(2)}, u32[]{:S(2)}) collective-permute-start(bf16[384,128]{1,0:T(8,128)(2,1)S(1)} %get-tuple-element.37.refs_3_.refs_0_), channel_id=1, source_target_pairs={{0,2},{1,3},{2,0},{3,1},{4,6},{5,7},{6,4},{7,5},{8,10},{9,11},{10,... | collective-permute-start | bytes 294920 | tf_op jit(solution)/shard_map/ppermute | solution.py:57
  9.0 2.1 %collective-permute-start.4 = (bf16[384,256]{1,0:T(8,128)(2,1)S(1)}, bf16[384,256]{1,0:T(8,128)(2,1)S(1)}, u32[]{:S(2)}, u32[]{:S(2)}) collective-permute-start(bf16[384,256]{1,0:T(8,128)(2,1)S(1)} %level1_1.1.refs_3_.refs_0_), channel_id=1, source_target_pairs={{0,2},{1,3},{2,0},{3,1},{4,6},{5,7},{6,4},{7,5},{8,10},{9,11},{10,... | collective-permute-start | bytes 589832 | tf_op jit(solution)/shard_map/ppermute | solution.py:57
  11.0 0.9 %collective-permute-done.1.refs_1_ = bf16[384,128]{1,0:T(8,128)(2,1)S(1)} collective-permute-done((bf16[384,128]{1,0:T(8,128)(2,1)S(1)}, bf16[384,128]{1,0:T(8,128)(2,1)S(1)}, u32[]{:S(2)}, u32[]{:S(2)}) %collective-permute-start.1) | collective-permute-done | bytes 98336 | tf_op jit(solution)/shard_map/ppermute | solution.py:57
  12.3 2.8 %collective-permute-start.3 = (bf16[384,128]{1,0:T(8,128)(2,1)S(1)}, bf16[384,128]{1,0:T(8,128)(2,1)S(1)}, u32[]{:S(2)}, u32[]{:S(2)}) collective-permute-start(bf16[384,128]{1,0:T(8,128)(2,1)S(1)} %level2_0.1.refs_3_.refs_0_), channel_id=1, source_target_pairs={{0,4},{1,5},{2,6},{3,7},{4,0},{5,1},{6,2},{7,3},{8,12},{9,13},{10,... | collective-permute-start | bytes 294920 | tf_op jit(solution)/shard_map/ppermute | solution.py:57
  15.1 0.5 level1_2.1.refs_3_.refs_0_
  15.6 1.6 %collective-permute-start.9 = (bf16[384,384]{1,0:T(8,128)(2,1)S(1)}, bf16[384,384]{1,0:T(8,128)(2,1)S(1)}, u32[]{:S(2)}, u32[]{:S(2)}) collective-permute-start(bf16[384,384]{1,0:T(8,128)(2,1)S(1)} %level1_2.1.refs_3_.refs_0_), channel_id=1, source_target_pairs={{0,2},{1,3},{2,0},{3,1},{4,6},{5,7},{6,4},{7,5},{8,10},{9,11},{10,... | collective-permute-start | bytes 884744 | tf_op jit(solution)/shard_map/ppermute | solution.py:57
  17.3 2.5 %prefetch.1 = (bf16[2,384,768]{2,1,0:T(8,128)(2,1)S(1)}, bf16[2,384,768]{2,1,0:T(8,128)(2,1)S(1)}, bf16[2,1024,384]{2,1,0:T(8,128)(2,1)S(1)}) custom-call(bf16[5,2,384,768]{3,2,1,0:T(8,128)(2,1)} %bitcast.8, bf16[2,1024,384]{2,1,0:T(8,128)(2,1)} %bitcast.11, s32[2,5]{1,0:T(2,128)} %bitcast.13, bf16[384,384]{1,0:T(8,128)(2,1)S(1)} %level1_2.1.refs_3_.refs_0_), custom_call_target="tpu_custom_call" | custom-call | flops 6000000000 | tf_op jit(solution)/shard_map/prefetch/pallas_call | solution.py:42
  20.2 0.4 collective-permute-start.11
  21.2 1.0 %collective-permute-done.5.refs_1_ = bf16[384,128]{1,0:T(8,128)(2,1)S(1)} collective-permute-done((bf16[384,128]{1,0:T(8,128)(2,1)S(1)}, bf16[384,128]{1,0:T(8,128)(2,1)S(1)}, u32[]{:S(2)}, u32[]{:S(2)}) %collective-permute-start.5) | collective-permute-done | bytes 98336 | tf_op jit(solution)/shard_map/ppermute | solution.py:57
  22.3 0.6 last_0.1
  22.8 2.5 %collective-permute-start.6 = (bf16[256,128]{1,0:T(8,128)(2,1)S(1)}, bf16[256,128]{1,0:T(8,128)(2,1)S(1)}, u32[]{:S(2)}, u32[]{:S(2)}) collective-permute-start(bf16[256,128]{1,0:T(8,128)(2,1)S(1)} %get-tuple-element.44), channel_id=1, source_target_pairs={{0,24},{8,16},{16,8},{24,0},{1,25},{9,17},{17,9},{25,1},{2,26},{10... | collective-permute-start | bytes 196616 | tf_op jit(solution)/shard_map/ppermute | solution.py:57
  25.4 0.5 collective-permute-start.7
  25.9 0.5 collective-permute-start.8
  26.4 2.5 %collective-permute-done.9.refs_1_ = bf16[384,384]{1,0:T(8,128)(2,1)S(1)} collective-permute-done((bf16[384,384]{1,0:T(8,128)(2,1)S(1)}, bf16[384,384]{1,0:T(8,128)(2,1)S(1)}, u32[]{:S(2)}, u32[]{:S(2)}) %collective-permute-start.9) | collective-permute-done | bytes 294944 | tf_op jit(solution)/shard_map/ppermute | solution.py:57
  28.9 0.5 level2_2.1.refs_4_.refs_0_
  29.4 1.5 %collective-permute-start.10 = (bf16[384,384]{1,0:T(8,128)(2,1)S(1)}, bf16[384,384]{1,0:T(8,128)(2,1)S(1)}, u32[]{:S(2)}, u32[]{:S(2)}) collective-permute-start(bf16[384,384]{1,0:T(8,128)(2,1)S(1)} %level2_2.1.refs_4_.refs_0_), channel_id=1, source_target_pairs={{0,4},{1,5},{2,6},{3,7},{4,0},{5,1},{6,2},{7,3},{8,12},{9,13},{10,... | collective-permute-start | bytes 884744 | tf_op jit(solution)/shard_map/ppermute | solution.py:57
  31.0 0.4 level1_3.1.refs_3_.refs_0_
  31.4 2.5 %collective-permute-start.13 = (bf16[384,256]{1,0:T(8,128)(2,1)S(1)}, bf16[384,256]{1,0:T(8,128)(2,1)S(1)}, u32[]{:S(2)}, u32[]{:S(2)}) collective-permute-start(bf16[384,256]{1,0:T(8,128)(2,1)S(1)} %level1_3.1.refs_3_.refs_0_), channel_id=1, source_target_pairs={{0,2},{1,3},{2,0},{3,1},{4,6},{5,7},{6,4},{7,5},{8,10},{9,11},{10,... | collective-permute-start | bytes 589832 | tf_op jit(solution)/shard_map/ppermute | solution.py:57
  34.6 1.2 %collective-permute-done.12.refs_1_ = bf16[384,256]{1,0:T(8,128)(2,1)S(1)} collective-permute-done((bf16[384,256]{1,0:T(8,128)(2,1)S(1)}, bf16[384,256]{1,0:T(8,128)(2,1)S(1)}, u32[]{:S(2)}, u32[]{:S(2)}) %collective-permute-start.12) | collective-permute-done | bytes 196640 | tf_op jit(solution)/shard_map/ppermute | solution.py:57
  35.8 0.8 %last_1.1 = (f32[256,256]{1,0:T(8,128)S(1)}, bf16[256,256]{1,0:T(8,128)(2,1)S(1)}, bf16[256,256]{1,0:T(8,128)(2,1)S(1)}, bf16[256,256]{1,0:T(8,128)(2,1)S(1)}) custom-call(f32[384,256]{1,0:T(8,128)S(1)} %between_1.1.refs_0_, bf16[384,256]{1,0:T(8,128)(2,1)S(1)} %collective-permute-done.12.refs_1_, ...), custom_call_target="tpu_custom_call" | custom-call | flops 6000000000 | tf_op jit(solution)/shard_map/last_1/pallas_call | solution.py:42
  36.6 2.5 %collective-permute-start.14 = (bf16[256,256]{1,0:T(8,128)(2,1)S(1)}, bf16[256,256]{1,0:T(8,128)(2,1)S(1)}, u32[]{:S(2)}, u32[]{:S(2)}) collective-permute-start(bf16[256,256]{1,0:T(8,128)(2,1)S(1)} %get-tuple-element.48), channel_id=1, source_target_pairs={{0,24},{8,16},{16,8},{24,0},{1,25},{9,17},{17,9},{25,1},{2,26},{10... | collective-permute-start | bytes 393224 | tf_op jit(solution)/shard_map/ppermute | solution.py:57
  39.3 0.6 collective-permute-start.15
  39.9 0.6 collective-permute-start.16
  40.5 0.5 collective-permute-done.13.refs_1_
  41.0 2.3 %collective-permute-done.14.refs_3_ = bf16[256,256]{1,0:T(8,128)(2,1)S(1)} collective-permute-done((bf16[256,256]{1,0:T(8,128)(2,1)S(1)}, bf16[256,256]{1,0:T(8,128)(2,1)S(1)}, u32[]{:S(2)}, u32[]{:S(2)}) %collective-permute-start.14) | collective-permute-done | bytes 131104 | tf_op jit(solution)/shard_map/ppermute | solution.py:57
  43.5 1.0 %collective-permute-start.21 = (bf16[384,256]{1,0:T(8,128)(2,1)S(1)}, bf16[384,256]{1,0:T(8,128)(2,1)S(1)}, u32[]{:S(2)}, u32[]{:S(2)}) collective-permute-start(bf16[384,256]{1,0:T(8,128)(2,1)S(1)} %level2_3.1.refs_3_.refs_0_), channel_id=1, source_target_pairs={{0,4},{1,5},{2,6},{3,7},{4,0},{5,1},{6,2},{7,3},{8,12},{9,13},{10,... | collective-permute-start | bytes 589832 | tf_op jit(solution)/shard_map/ppermute | solution.py:57
  44.8 0.5 level3_2.1.refs_0_
  45.4 0.5 collective-permute-done.15.refs_4_
  46.0 0.4 between_2.1
  46.3 0.6 collective-permute-done.17.refs_1_
  47.0 0.9 %far_2.1 = (bf16[384,384]{1,0:T(8,128)(2,1)S(1)}, bf16[256,384]{1,0:T(8,128)(2,1)S(1)}) custom-call(f32[384,384]{1,0:T(8,128)S(1)} %get-tuple-element.52.refs_0_, bf16[384,384]{1,0:T(8,128)(2,1)S(1)} %collective-permute-done.17.refs_1_, bf16[2,384,768]{2,1,0:T(8,128)(2,1)S(1)} %get-tuple-element.42.refs_1_.refs_2_, ...), custom_call_target="tpu_custom_call" | custom-call | flops 6000000000 | tf_op jit(solution)/shard_map/far_2/pallas_call | solution.py:42
  47.9 2.8 %collective-permute-start.18 = (bf16[256,384]{1,0:T(8,128)(2,1)S(1)}, bf16[256,384]{1,0:T(8,128)(2,1)S(1)}, u32[]{:S(2)}, u32[]{:S(2)}) collective-permute-start(bf16[256,384]{1,0:T(8,128)(2,1)S(1)} %get-tuple-element.55), channel_id=1, source_target_pairs={{0,24},{8,16},{16,8},{24,0},{1,25},{9,17},{17,9},{25,1},{2,26},{10... | collective-permute-start | bytes 589832 | tf_op jit(solution)/shard_map/ppermute | solution.py:57
  50.7 0.5 last_2.1
  51.2 0.6 collective-permute-start.19
  52.0 2.1 %collective-permute-done.21.refs_1_ = bf16[384,256]{1,0:T(8,128)(2,1)S(1)} collective-permute-done((bf16[384,256]{1,0:T(8,128)(2,1)S(1)}, bf16[384,256]{1,0:T(8,128)(2,1)S(1)}, u32[]{:S(2)}, u32[]{:S(2)}) %collective-permute-start.21) | collective-permute-done | bytes 196640 | tf_op jit(solution)/shard_map/ppermute | solution.py:57
  54.8 1.2 %collective-permute-done.22.refs_1_ = bf16[384,256]{1,0:T(8,128)(2,1)S(1)} collective-permute-done((bf16[384,256]{1,0:T(8,128)(2,1)S(1)}, bf16[384,256]{1,0:T(8,128)(2,1)S(1)}, u32[]{:S(2)}, u32[]{:S(2)}) %collective-permute-start.22) | collective-permute-done | bytes 196640 | tf_op jit(solution)/shard_map/ppermute | solution.py:57
  56.0 0.6 far_3.1
  56.6 2.5 %collective-permute-start.23 = (bf16[256,256]{1,0:T(8,128)(2,1)S(1)}, bf16[256,256]{1,0:T(8,128)(2,1)S(1)}, u32[]{:S(2)}, u32[]{:S(2)}) collective-permute-start(bf16[256,256]{1,0:T(8,128)(2,1)S(1)} %get-tuple-element.60), channel_id=1, source_target_pairs={{0,24},{8,16},{16,8},{24,0},{1,25},{9,17},{17,9},{25,1},{2,26},{10... | collective-permute-start | bytes 393224 | tf_op jit(solution)/shard_map/ppermute | solution.py:57
  59.1 0.4 last_3.1
  59.5 0.5 collective-permute-start.24
  60.0 0.6 collective-permute-start.25
  60.7 2.5 %collective-permute-done.23.refs_4_ = bf16[256,256]{1,0:T(8,128)(2,1)S(1)} collective-permute-done((bf16[256,256]{1,0:T(8,128)(2,1)S(1)}, bf16[256,256]{1,0:T(8,128)(2,1)S(1)}, u32[]{:S(2)}, u32[]{:S(2)}) %collective-permute-start.23) | collective-permute-done | bytes 131104 | tf_op jit(solution)/shard_map/ppermute | solution.py:57
  63.2 2.7 %collective-permute-done.24.refs_5_ = bf16[256,256]{1,0:T(8,128)(2,1)S(1)} collective-permute-done((bf16[256,256]{1,0:T(8,128)(2,1)S(1)}, bf16[256,256]{1,0:T(8,128)(2,1)S(1)}, u32[]{:S(2)}, u32[]{:S(2)}) %collective-permute-start.24) | collective-permute-done | bytes 131104 | tf_op jit(solution)/shard_map/ppermute | solution.py:57
  66.0 0.9 %end.1 = bf16[2,256,512]{2,1,0:T(8,128)(2,1)} custom-call(bf16[256,128]{1,0:T(8,128)(2,1)S(1)} %sum_0.1.refs_3_.refs_0_, bf16[256,256]{1,0:T(8,128)(2,1)S(1)} %get-tuple-element.51.refs_1_, bf16[256,384]{1,0:T(8,128)(2,1)S(1)} %sum_2.1.refs_2_, f32[256,256]{1,0:T(8,128)S(1)} %get-tuple-element.59.refs_4_.refs_3_, ...), custom_call_target="tpu_custom_call" | custom-call | tf_op jit(solution)/shard_map/end/pallas_call | solution.py:480
  (32 shorter events, 4.8 us)
Async XLA Ops:
  3.7 1.5 %collective-permute-start = (bf16[384,128]{1,0:T(8,128)(2,1)S(1)}, bf16[384,128]{1,0:T(8,128)(2,1)S(1)}, u32[]{:S(2)}, u32[]{:S(2)}) collective-permute-start(bf16[384,128]{1,0:T(8,128)(2,1)S(1)} %get-tuple-element.34.refs_0_), channel_id=1, source_target_pairs={{0,1},{1,0},{2,3},{3,2},{4,5},{5,4},{6,7},{7,6},{8,9},{9,8},{10,11... | collective-permute-start | bytes 294920 | tf_op jit(solution)/shard_map/ppermute | solution.py:57
  5.5 3.1 %collective-permute-start.2 = (bf16[384,896]{1,0:T(8,128)(2,1)S(1)}, bf16[384,896]{1,0:T(8,128)(2,1)S(1)}, u32[]{:S(2)}, u32[]{:S(2)}) collective-permute-start(bf16[384,896]{1,0:T(8,128)(2,1)S(1)} %get-tuple-element.39.refs_0_), channel_id=1, source_target_pairs={{0,1},{1,0},{2,3},{3,2},{4,5},{5,4},{6,7},{7,6},{8,9},{9,8},{10,11... | collective-permute-start | bytes 2064392 | tf_op jit(solution)/shard_map/ppermute | solution.py:57
  5.9 6.0 %collective-permute-start.1 = (bf16[384,128]{1,0:T(8,128)(2,1)S(1)}, bf16[384,128]{1,0:T(8,128)(2,1)S(1)}, u32[]{:S(2)}, u32[]{:S(2)}) collective-permute-start(bf16[384,128]{1,0:T(8,128)(2,1)S(1)} %get-tuple-element.37.refs_3_.refs_0_), channel_id=1, source_target_pairs={{0,2},{1,3},{2,0},{3,1},{4,6},{5,7},{6,4},{7,5},{8,10},{9,11},{10,... | collective-permute-start | bytes 294920 | tf_op jit(solution)/shard_map/ppermute | solution.py:57
  9.0 10.8 %collective-permute-start.4 = (bf16[384,256]{1,0:T(8,128)(2,1)S(1)}, bf16[384,256]{1,0:T(8,128)(2,1)S(1)}, u32[]{:S(2)}, u32[]{:S(2)}) collective-permute-start(bf16[384,256]{1,0:T(8,128)(2,1)S(1)} %level1_1.1.refs_3_.refs_0_), channel_id=1, source_target_pairs={{0,2},{1,3},{2,0},{3,1},{4,6},{5,7},{6,4},{7,5},{8,10},{9,11},{10,... | collective-permute-start | bytes 589832 | tf_op jit(solution)/shard_map/ppermute | solution.py:57
  12.3 8.3 %collective-permute-start.3 = (bf16[384,128]{1,0:T(8,128)(2,1)S(1)}, bf16[384,128]{1,0:T(8,128)(2,1)S(1)}, u32[]{:S(2)}, u32[]{:S(2)}) collective-permute-start(bf16[384,128]{1,0:T(8,128)(2,1)S(1)} %level2_0.1.refs_3_.refs_0_), channel_id=1, source_target_pairs={{0,4},{1,5},{2,6},{3,7},{4,0},{5,1},{6,2},{7,3},{8,12},{9,13},{10,... | collective-permute-start | bytes 294920 | tf_op jit(solution)/shard_map/ppermute | solution.py:57
  15.6 13.3 %collective-permute-start.9 = (bf16[384,384]{1,0:T(8,128)(2,1)S(1)}, bf16[384,384]{1,0:T(8,128)(2,1)S(1)}, u32[]{:S(2)}, u32[]{:S(2)}) collective-permute-start(bf16[384,384]{1,0:T(8,128)(2,1)S(1)} %level1_2.1.refs_3_.refs_0_), channel_id=1, source_target_pairs={{0,2},{1,3},{2,0},{3,1},{4,6},{5,7},{6,4},{7,5},{8,10},{9,11},{10,... | collective-permute-start | bytes 884744 | tf_op jit(solution)/shard_map/ppermute | solution.py:57
  20.2 13.7 %collective-permute-start.11 = (bf16[384,256]{1,0:T(8,128)(2,1)S(1)}, bf16[384,256]{1,0:T(8,128)(2,1)S(1)}, u32[]{:S(2)}, u32[]{:S(2)}) collective-permute-start(bf16[384,256]{1,0:T(8,128)(2,1)S(1)} %level2_1.1.refs_3_.refs_0_), channel_id=1, source_target_pairs={{0,4},{1,5},{2,6},{3,7},{4,0},{5,1},{6,2},{7,3},{8,12},{9,13},{10,... | collective-permute-start | bytes 589832 | tf_op jit(solution)/shard_map/ppermute | solution.py:57
  20.9 1.4 %collective-permute-start.5 = (bf16[384,128]{1,0:T(8,128)(2,1)S(1)}, bf16[384,128]{1,0:T(8,128)(2,1)S(1)}, u32[]{:S(2)}, u32[]{:S(2)}) collective-permute-start(bf16[384,128]{1,0:T(8,128)(2,1)S(1)} %level3_0.1.refs_0_), channel_id=1, source_target_pairs={{0,1},{1,0},{2,3},{3,2},{4,5},{5,4},{6,7},{7,6},{8,9},{9,8},{10,11... | collective-permute-start | bytes 294920 | tf_op jit(solution)/shard_map/ppermute | solution.py:57
  22.8 8.1 %collective-permute-start.6 = (bf16[256,128]{1,0:T(8,128)(2,1)S(1)}, bf16[256,128]{1,0:T(8,128)(2,1)S(1)}, u32[]{:S(2)}, u32[]{:S(2)}) collective-permute-start(bf16[256,128]{1,0:T(8,128)(2,1)S(1)} %get-tuple-element.44), channel_id=1, source_target_pairs={{0,24},{8,16},{16,8},{24,0},{1,25},{9,17},{17,9},{25,1},{2,26},{10... | collective-permute-start | bytes 196616 | tf_op jit(solution)/shard_map/ppermute | solution.py:57
  25.4 5.6 %collective-permute-start.7 = (bf16[256,128]{1,0:T(8,128)(2,1)S(1)}, bf16[256,128]{1,0:T(8,128)(2,1)S(1)}, u32[]{:S(2)}, u32[]{:S(2)}) collective-permute-start(bf16[256,128]{1,0:T(8,128)(2,1)S(1)} %get-tuple-element.45), channel_id=1, source_target_pairs={{0,16},{8,24},{16,0},{24,8},{1,17},{9,25},{17,1},{25,9},{2,18},{10... | collective-permute-start | bytes 196616 | tf_op jit(solution)/shard_map/ppermute | solution.py:57
  25.9 5.1 %collective-permute-start.8 = (bf16[256,128]{1,0:T(8,128)(2,1)S(1)}, bf16[256,128]{1,0:T(8,128)(2,1)S(1)}, u32[]{:S(2)}, u32[]{:S(2)}) collective-permute-start(bf16[256,128]{1,0:T(8,128)(2,1)S(1)} %get-tuple-element.46), channel_id=1, source_target_pairs={{0,8},{8,0},{16,24},{24,16},{1,9},{9,1},{17,25},{25,17},{2,10},{10... | collective-permute-start | bytes 196616 | tf_op jit(solution)/shard_map/ppermute | solution.py:57
  29.4 15.4 %collective-permute-start.10 = (bf16[384,384]{1,0:T(8,128)(2,1)S(1)}, bf16[384,384]{1,0:T(8,128)(2,1)S(1)}, u32[]{:S(2)}, u32[]{:S(2)}) collective-permute-start(bf16[384,384]{1,0:T(8,128)(2,1)S(1)} %level2_2.1.refs_4_.refs_0_), channel_id=1, source_target_pairs={{0,4},{1,5},{2,6},{3,7},{4,0},{5,1},{6,2},{7,3},{8,12},{9,13},{10,... | collective-permute-start | bytes 884744 | tf_op jit(solution)/shard_map/ppermute | solution.py:57
  31.4 9.6 %collective-permute-start.13 = (bf16[384,256]{1,0:T(8,128)(2,1)S(1)}, bf16[384,256]{1,0:T(8,128)(2,1)S(1)}, u32[]{:S(2)}, u32[]{:S(2)}) collective-permute-start(bf16[384,256]{1,0:T(8,128)(2,1)S(1)} %level1_3.1.refs_3_.refs_0_), channel_id=1, source_target_pairs={{0,2},{1,3},{2,0},{3,1},{4,6},{5,7},{6,4},{7,5},{8,10},{9,11},{10,... | collective-permute-start | bytes 589832 | tf_op jit(solution)/shard_map/ppermute | solution.py:57
  34.3 1.5 %collective-permute-start.12 = (bf16[384,256]{1,0:T(8,128)(2,1)S(1)}, bf16[384,256]{1,0:T(8,128)(2,1)S(1)}, u32[]{:S(2)}, u32[]{:S(2)}) collective-permute-start(bf16[384,256]{1,0:T(8,128)(2,1)S(1)} %level3_1.1.refs_0_), channel_id=1, source_target_pairs={{0,1},{1,0},{2,3},{3,2},{4,5},{5,4},{6,7},{7,6},{8,9},{9,8},{10,11... | collective-permute-start | bytes 589832 | tf_op jit(solution)/shard_map/ppermute | solution.py:57
  36.6 6.6 %collective-permute-start.14 = (bf16[256,256]{1,0:T(8,128)(2,1)S(1)}, bf16[256,256]{1,0:T(8,128)(2,1)S(1)}, u32[]{:S(2)}, u32[]{:S(2)}) collective-permute-start(bf16[256,256]{1,0:T(8,128)(2,1)S(1)} %get-tuple-element.48), channel_id=1, source_target_pairs={{0,24},{8,16},{16,8},{24,0},{1,25},{9,17},{17,9},{25,1},{2,26},{10... | collective-permute-start | bytes 393224 | tf_op jit(solution)/shard_map/ppermute | solution.py:57
  39.3 6.6 %collective-permute-start.15 = (bf16[256,256]{1,0:T(8,128)(2,1)S(1)}, bf16[256,256]{1,0:T(8,128)(2,1)S(1)}, u32[]{:S(2)}, u32[]{:S(2)}) collective-permute-start(bf16[256,256]{1,0:T(8,128)(2,1)S(1)} %get-tuple-element.49), channel_id=1, source_target_pairs={{0,16},{8,24},{16,0},{24,8},{1,17},{9,25},{17,1},{25,9},{2,18},{10... | collective-permute-start | bytes 393224 | tf_op jit(solution)/shard_map/ppermute | solution.py:57
  39.9 6.1 %collective-permute-start.16 = (bf16[256,256]{1,0:T(8,128)(2,1)S(1)}, bf16[256,256]{1,0:T(8,128)(2,1)S(1)}, u32[]{:S(2)}, u32[]{:S(2)}) collective-permute-start(bf16[256,256]{1,0:T(8,128)(2,1)S(1)} %get-tuple-element.50), channel_id=1, source_target_pairs={{0,8},{8,0},{16,24},{24,16},{1,9},{9,1},{17,25},{25,17},{2,10},{10... | collective-permute-start | bytes 393224 | tf_op jit(solution)/shard_map/ppermute | solution.py:57
  43.5 10.6 %collective-permute-start.21 = (bf16[384,256]{1,0:T(8,128)(2,1)S(1)}, bf16[384,256]{1,0:T(8,128)(2,1)S(1)}, u32[]{:S(2)}, u32[]{:S(2)}) collective-permute-start(bf16[384,256]{1,0:T(8,128)(2,1)S(1)} %level2_3.1.refs_3_.refs_0_), channel_id=1, source_target_pairs={{0,4},{1,5},{2,6},{3,7},{4,0},{5,1},{6,2},{7,3},{8,12},{9,13},{10,... | collective-permute-start | bytes 589832 | tf_op jit(solution)/shard_map/ppermute | solution.py:57
  45.3 1.6 %collective-permute-start.17 = (bf16[384,384]{1,0:T(8,128)(2,1)S(1)}, bf16[384,384]{1,0:T(8,128)(2,1)S(1)}, u32[]{:S(2)}, u32[]{:S(2)}) collective-permute-start(bf16[384,384]{1,0:T(8,128)(2,1)S(1)} %level3_2.1.refs_0_), channel_id=1, source_target_pairs={{0,1},{1,0},{2,3},{3,2},{4,5},{5,4},{6,7},{7,6},{8,9},{9,8},{10,11... | collective-permute-start | bytes 884744 | tf_op jit(solution)/shard_map/ppermute | solution.py:57
  47.9 12.1 %collective-permute-start.18 = (bf16[256,384]{1,0:T(8,128)(2,1)S(1)}, bf16[256,384]{1,0:T(8,128)(2,1)S(1)}, u32[]{:S(2)}, u32[]{:S(2)}) collective-permute-start(bf16[256,384]{1,0:T(8,128)(2,1)S(1)} %get-tuple-element.55), channel_id=1, source_target_pairs={{0,24},{8,16},{16,8},{24,0},{1,25},{9,17},{17,9},{25,1},{2,26},{10... | collective-permute-start | bytes 589832 | tf_op jit(solution)/shard_map/ppermute | solution.py:57
  51.2 9.3 %collective-permute-start.19 = (bf16[256,384]{1,0:T(8,128)(2,1)S(1)}, bf16[256,384]{1,0:T(8,128)(2,1)S(1)}, u32[]{:S(2)}, u32[]{:S(2)}) collective-permute-start(bf16[256,384]{1,0:T(8,128)(2,1)S(1)} %get-tuple-element.56), channel_id=1, source_target_pairs={{0,16},{8,24},{16,0},{24,8},{1,17},{9,25},{17,1},{25,9},{2,18},{10... | collective-permute-start | bytes 589832 | tf_op jit(solution)/shard_map/ppermute | solution.py:57
  51.8 8.8 %collective-permute-start.20 = (bf16[256,384]{1,0:T(8,128)(2,1)S(1)}, bf16[256,384]{1,0:T(8,128)(2,1)S(1)}, u32[]{:S(2)}, u32[]{:S(2)}) collective-permute-start(bf16[256,384]{1,0:T(8,128)(2,1)S(1)} %get-tuple-element.57), channel_id=1, source_target_pairs={{0,8},{8,0},{16,24},{24,16},{1,9},{9,1},{17,25},{25,17},{2,10},{10... | collective-permute-start | bytes 589832 | tf_op jit(solution)/shard_map/ppermute | solution.py:57
  54.5 1.5 %collective-permute-start.22 = (bf16[384,256]{1,0:T(8,128)(2,1)S(1)}, bf16[384,256]{1,0:T(8,128)(2,1)S(1)}, u32[]{:S(2)}, u32[]{:S(2)}) collective-permute-start(bf16[384,256]{1,0:T(8,128)(2,1)S(1)} %level3_3.1.refs_0_), channel_id=1, source_target_pairs={{0,1},{1,0},{2,3},{3,2},{4,5},{5,4},{6,7},{7,6},{8,9},{9,8},{10,11... | collective-permute-start | bytes 589832 | tf_op jit(solution)/shard_map/ppermute | solution.py:57
  56.6 6.6 %collective-permute-start.23 = (bf16[256,256]{1,0:T(8,128)(2,1)S(1)}, bf16[256,256]{1,0:T(8,128)(2,1)S(1)}, u32[]{:S(2)}, u32[]{:S(2)}) collective-permute-start(bf16[256,256]{1,0:T(8,128)(2,1)S(1)} %get-tuple-element.60), channel_id=1, source_target_pairs={{0,24},{8,16},{16,8},{24,0},{1,25},{9,17},{17,9},{25,1},{2,26},{10... | collective-permute-start | bytes 393224 | tf_op jit(solution)/shard_map/ppermute | solution.py:57
  59.5 6.4 %collective-permute-start.24 = (bf16[256,256]{1,0:T(8,128)(2,1)S(1)}, bf16[256,256]{1,0:T(8,128)(2,1)S(1)}, u32[]{:S(2)}, u32[]{:S(2)}) collective-permute-start(bf16[256,256]{1,0:T(8,128)(2,1)S(1)} %get-tuple-element.61), channel_id=1, source_target_pairs={{0,16},{8,24},{16,0},{24,8},{1,17},{9,25},{17,1},{25,9},{2,18},{10... | collective-permute-start | bytes 393224 | tf_op jit(solution)/shard_map/ppermute | solution.py:57
  60.0 6.0 %collective-permute-start.25 = (bf16[256,256]{1,0:T(8,128)(2,1)S(1)}, bf16[256,256]{1,0:T(8,128)(2,1)S(1)}, u32[]{:S(2)}, u32[]{:S(2)}) collective-permute-start(bf16[256,256]{1,0:T(8,128)(2,1)S(1)} %get-tuple-element.62), channel_id=1, source_target_pairs={{0,8},{8,0},{16,24},{24,16},{1,9},{9,1},{17,25},{25,17},{2,10},{10... | collective-permute-start | bytes 393224 | tf_op jit(solution)/shard_map/ppermute | solution.py:57

commit v26 on v25

--- a/solution.py
+++ b/solution.py
@@ -375,7 +375,27 @@
         return held
 
     def tail(j, after, arrived=(), folding=(), halving=False):
-        (coeff4,) = step(f"level3_{j}", [(3, j, coeff3[j], near3[j])], after)
+        if j >= 2:
+            (ahead,) = call(
+                functools.partial(half_kernel, bits[3], parts[j]),
+                f"ahead_{j}",
+                [VMEM] * 2,
+                [in_vmem(rank, widths[j], dtype=F32)],
+                [],
+                [here(coeff3[j]), here(weights[3])],
+                after,
+                0,
+            )
+            (coeff4,) = call(
+                functools.partial(finish_kernel, bits[3], parts[j]),
+                f"level3_{j}",
+                [VMEM] * 3,
+                [in_vmem(rank, widths[j])],
+                [],
+                [here(ahead), here(near3[j]), here(weights[3])],
+            )
+        else:
+            (coeff4,) = step(f"level3_{j}", [(3, j, coeff3[j], near3[j])], after)
         near4 = cross(4, coeff4)
         held = folding[1] if folding else []
         extra = [v for _, group in arrived for v in group] + held

time: 67.1 us -> 67.2 us (level)
    pallas_call x27 -> x29, Pallas kernels: 16 us -> 16.2 us  [call(): pl.pallas_call(body, name=name, in_specs=[*in_specs, *[ANY] * (len(after)...]
  transfers between devices with their start and end apart: 26 -> 26, of which waited for: 16 -> 15; matrix products, arithmetic and copies ran while one was open for 0% -> 0% of each run, Pallas kernels for 18% -> 18%
where the time goes in v26:
time: 67.2 us; the launch traced here: 67.1 us
  starting transfers between devices  30.4 us (45%)
  waiting for transfers between devices  19.2 us (29%)
  Pallas kernels  17.1 us (25%)
    ppermute x26, starting transfers between devices, partner(): return lax.ppermute(value, axis, pairs)  30.4 us
    ppermute x26, waiting for transfers between devices, partner(): return lax.ppermute(value, axis, pairs)  19.2 us
    pallas_call x29, Pallas kernels, call(): pl.pallas_call(body, name=name, in_specs=[*in_specs, *[ANY] * (len(after)...  16.2 us
  transfers between devices with their start and end apart: 26, of which 15 were waited for; matrix products, arithmetic and copies ran while one was open for 0% of the time, Pallas kernels for 18%

profile of v26, /device:TPU:0, one launch (start us, length us, event | category | flops | bytes accessed | tf_op | source)
XLA Modules:
  0.0 67.1 jit_solution(12992655646956512825)
XLA Ops:
  0.0 3.7 %leaf.1 = (bf16[384,128]{1,0:T(8,128)(2,1)S(1)}, bf16[384,896]{1,0:T(8,128)(2,1)S(1)}, bf16[2,384,768]{2,1,0:T(8,128)(2,1)S(1)}, bf16[2,384,768]{2,1,0:T(8,128)(2,1)S(1)}) custom-call(bf16[2,1024,512]{2,1,0:T(8,128)(2,1)} %bitcast.9, bf16[2,384,1024]{2,1,0:T(8,128)(2,1)} %bitcast.10, bf16[5,2,384,768]{3,2,1,0:T(8,128)(2,1)} %bitcast.7, s32[2,5]{1,0:T(2,128)} %bitcast.12), custom_call_target="tpu_custom_call" | custom-call | flops 6000000000 | tf_op jit(solution)/shard_map/leaf/pallas_call | solution.py:42
  3.7 0.5 collective-permute-start
  4.2 0.9 %collective-permute-done.refs_1_ = bf16[384,128]{1,0:T(8,128)(2,1)S(1)} collective-permute-done((bf16[384,128]{1,0:T(8,128)(2,1)S(1)}, bf16[384,128]{1,0:T(8,128)(2,1)S(1)}, u32[]{:S(2)}, u32[]{:S(2)}) %collective-permute-start) | collective-permute-done | bytes 98336 | tf_op jit(solution)/shard_map/ppermute | solution.py:57
  5.5 0.4 collective-permute-start.2
  5.9 2.7 %collective-permute-start.1 = (bf16[384,128]{1,0:T(8,128)(2,1)S(1)}, bf16[384,128]{1,0:T(8,128)(2,1)S(1)}, u32[]{:S(2)}, u32[]{:S(2)}) collective-permute-start(bf16[384,128]{1,0:T(8,128)(2,1)S(1)} %get-tuple-element.37.refs_3_.refs_0_), channel_id=1, source_target_pairs={{0,2},{1,3},{2,0},{3,1},{4,6},{5,7},{6,4},{7,5},{8,10},{9,11},{10,... | collective-permute-start | bytes 294920 | tf_op jit(solution)/shard_map/ppermute | solution.py:57
  8.6 0.4 level1_1.1.refs_3_.refs_0_
  9.0 2.1 %collective-permute-start.4 = (bf16[384,256]{1,0:T(8,128)(2,1)S(1)}, bf16[384,256]{1,0:T(8,128)(2,1)S(1)}, u32[]{:S(2)}, u32[]{:S(2)}) collective-permute-start(bf16[384,256]{1,0:T(8,128)(2,1)S(1)} %level1_1.1.refs_3_.refs_0_), channel_id=1, source_target_pairs={{0,2},{1,3},{2,0},{3,1},{4,6},{5,7},{6,4},{7,5},{8,10},{9,11},{10,... | collective-permute-start | bytes 589832 | tf_op jit(solution)/shard_map/ppermute | solution.py:57
  11.0 0.9 %collective-permute-done.1.refs_1_ = bf16[384,128]{1,0:T(8,128)(2,1)S(1)} collective-permute-done((bf16[384,128]{1,0:T(8,128)(2,1)S(1)}, bf16[384,128]{1,0:T(8,128)(2,1)S(1)}, u32[]{:S(2)}, u32[]{:S(2)}) %collective-permute-start.1) | collective-permute-done | bytes 98336 | tf_op jit(solution)/shard_map/ppermute | solution.py:57
  12.3 2.8 %collective-permute-start.3 = (bf16[384,128]{1,0:T(8,128)(2,1)S(1)}, bf16[384,128]{1,0:T(8,128)(2,1)S(1)}, u32[]{:S(2)}, u32[]{:S(2)}) collective-permute-start(bf16[384,128]{1,0:T(8,128)(2,1)S(1)} %level2_0.1.refs_3_.refs_0_), channel_id=1, source_target_pairs={{0,4},{1,5},{2,6},{3,7},{4,0},{5,1},{6,2},{7,3},{8,12},{9,13},{10,... | collective-permute-start | bytes 294920 | tf_op jit(solution)/shard_map/ppermute | solution.py:57
  15.1 0.5 level1_2.1.refs_3_.refs_0_
  15.6 1.6 %collective-permute-start.9 = (bf16[384,384]{1,0:T(8,128)(2,1)S(1)}, bf16[384,384]{1,0:T(8,128)(2,1)S(1)}, u32[]{:S(2)}, u32[]{:S(2)}) collective-permute-start(bf16[384,384]{1,0:T(8,128)(2,1)S(1)} %level1_2.1.refs_3_.refs_0_), channel_id=1, source_target_pairs={{0,2},{1,3},{2,0},{3,1},{4,6},{5,7},{6,4},{7,5},{8,10},{9,11},{10,... | collective-permute-start | bytes 884744 | tf_op jit(solution)/shard_map/ppermute | solution.py:57
  17.3 2.5 %prefetch.1 = (bf16[2,384,768]{2,1,0:T(8,128)(2,1)S(1)}, bf16[2,384,768]{2,1,0:T(8,128)(2,1)S(1)}, bf16[2,1024,384]{2,1,0:T(8,128)(2,1)S(1)}) custom-call(bf16[5,2,384,768]{3,2,1,0:T(8,128)(2,1)} %bitcast.8, bf16[2,1024,384]{2,1,0:T(8,128)(2,1)} %bitcast.11, s32[2,5]{1,0:T(2,128)} %bitcast.13, bf16[384,384]{1,0:T(8,128)(2,1)S(1)} %level1_2.1.refs_3_.refs_0_), custom_call_target="tpu_custom_call" | custom-call | flops 6000000000 | tf_op jit(solution)/shard_map/prefetch/pallas_call | solution.py:42
  20.1 0.4 collective-permute-start.10
  21.2 1.0 %collective-permute-done.5.refs_1_ = bf16[384,128]{1,0:T(8,128)(2,1)S(1)} collective-permute-done((bf16[384,128]{1,0:T(8,128)(2,1)S(1)}, bf16[384,128]{1,0:T(8,128)(2,1)S(1)}, u32[]{:S(2)}, u32[]{:S(2)}) %collective-permute-start.5) | collective-permute-done | bytes 98336 | tf_op jit(solution)/shard_map/ppermute | solution.py:57
  22.3 0.6 last_0.1
  22.9 2.5 %collective-permute-start.6 = (bf16[256,128]{1,0:T(8,128)(2,1)S(1)}, bf16[256,128]{1,0:T(8,128)(2,1)S(1)}, u32[]{:S(2)}, u32[]{:S(2)}) collective-permute-start(bf16[256,128]{1,0:T(8,128)(2,1)S(1)} %get-tuple-element.44), channel_id=1, source_target_pairs={{0,24},{8,16},{16,8},{24,0},{1,25},{9,17},{17,9},{25,1},{2,26},{10... | collective-permute-start | bytes 196616 | tf_op jit(solution)/shard_map/ppermute | solution.py:57
  25.4 0.5 collective-permute-start.7
  25.9 0.6 collective-permute-start.8
  26.4 2.5 %collective-permute-done.9.refs_1_ = bf16[384,384]{1,0:T(8,128)(2,1)S(1)} collective-permute-done((bf16[384,384]{1,0:T(8,128)(2,1)S(1)}, bf16[384,384]{1,0:T(8,128)(2,1)S(1)}, u32[]{:S(2)}, u32[]{:S(2)}) %collective-permute-start.9) | collective-permute-done | bytes 294944 | tf_op jit(solution)/shard_map/ppermute | solution.py:57
  28.9 0.5 level2_2.1.refs_4_.refs_0_
  29.4 1.5 %collective-permute-start.14 = (bf16[384,384]{1,0:T(8,128)(2,1)S(1)}, bf16[384,384]{1,0:T(8,128)(2,1)S(1)}, u32[]{:S(2)}, u32[]{:S(2)}) collective-permute-start(bf16[384,384]{1,0:T(8,128)(2,1)S(1)} %level2_2.1.refs_4_.refs_0_), channel_id=1, source_target_pairs={{0,4},{1,5},{2,6},{3,7},{4,0},{5,1},{6,2},{7,3},{8,12},{9,13},{10,... | collective-permute-start | bytes 884744 | tf_op jit(solution)/shard_map/ppermute | solution.py:57
  31.0 0.4 level1_3.1.refs_3_.refs_0_
  31.4 2.5 %collective-permute-start.12 = (bf16[384,256]{1,0:T(8,128)(2,1)S(1)}, bf16[384,256]{1,0:T(8,128)(2,1)S(1)}, u32[]{:S(2)}, u32[]{:S(2)}) collective-permute-start(bf16[384,256]{1,0:T(8,128)(2,1)S(1)} %level1_3.1.refs_3_.refs_0_), channel_id=1, source_target_pairs={{0,2},{1,3},{2,0},{3,1},{4,6},{5,7},{6,4},{7,5},{8,10},{9,11},{10,... | collective-permute-start | bytes 589832 | tf_op jit(solution)/shard_map/ppermute | solution.py:57
  34.6 1.2 %collective-permute-done.11.refs_1_ = bf16[384,256]{1,0:T(8,128)(2,1)S(1)} collective-permute-done((bf16[384,256]{1,0:T(8,128)(2,1)S(1)}, bf16[384,256]{1,0:T(8,128)(2,1)S(1)}, u32[]{:S(2)}, u32[]{:S(2)}) %collective-permute-start.11) | collective-permute-done | bytes 196640 | tf_op jit(solution)/shard_map/ppermute | solution.py:57
  35.8 0.8 %last_1.1 = (f32[256,256]{1,0:T(8,128)S(1)}, bf16[256,256]{1,0:T(8,128)(2,1)S(1)}, bf16[256,256]{1,0:T(8,128)(2,1)S(1)}, bf16[256,256]{1,0:T(8,128)(2,1)S(1)}) custom-call(f32[384,256]{1,0:T(8,128)S(1)} %between_1.1.refs_0_, bf16[384,256]{1,0:T(8,128)(2,1)S(1)} %collective-permute-done.11.refs_1_, ...), custom_call_target="tpu_custom_call" | custom-call | flops 6000000000 | tf_op jit(solution)/shard_map/last_1/pallas_call | solution.py:42
  36.6 2.5 %collective-permute-start.13 = (bf16[256,256]{1,0:T(8,128)(2,1)S(1)}, bf16[256,256]{1,0:T(8,128)(2,1)S(1)}, u32[]{:S(2)}, u32[]{:S(2)}) collective-permute-start(bf16[256,256]{1,0:T(8,128)(2,1)S(1)} %get-tuple-element.48), channel_id=1, source_target_pairs={{0,24},{8,16},{16,8},{24,0},{1,25},{9,17},{17,9},{25,1},{2,26},{10... | collective-permute-start | bytes 393224 | tf_op jit(solution)/shard_map/ppermute | solution.py:57
  39.3 0.6 collective-permute-start.15
  39.9 0.6 collective-permute-start.16
  40.5 0.5 collective-permute-done.12.refs_1_
  41.0 2.3 %collective-permute-done.13.refs_3_ = bf16[256,256]{1,0:T(8,128)(2,1)S(1)} collective-permute-done((bf16[256,256]{1,0:T(8,128)(2,1)S(1)}, bf16[256,256]{1,0:T(8,128)(2,1)S(1)}, u32[]{:S(2)}, u32[]{:S(2)}) %collective-permute-start.13) | collective-permute-done | bytes 131104 | tf_op jit(solution)/shard_map/ppermute | solution.py:57
  43.8 1.0 %collective-permute-start.21 = (bf16[384,256]{1,0:T(8,128)(2,1)S(1)}, bf16[384,256]{1,0:T(8,128)(2,1)S(1)}, u32[]{:S(2)}, u32[]{:S(2)}) collective-permute-start(bf16[384,256]{1,0:T(8,128)(2,1)S(1)} %level2_3.1.refs_2_.refs_0_), channel_id=1, source_target_pairs={{0,4},{1,5},{2,6},{3,7},{4,0},{5,1},{6,2},{7,3},{8,12},{9,13},{10,... | collective-permute-start | bytes 589832 | tf_op jit(solution)/shard_map/ppermute | solution.py:57
  45.3 0.7 collective-permute-done.15.refs_4_
  46.0 0.4 between_2.1
  46.3 0.5 collective-permute-done.17.refs_1_
  46.8 0.9 %far_2.1 = (bf16[384,384]{1,0:T(8,128)(2,1)S(1)}, bf16[256,384]{1,0:T(8,128)(2,1)S(1)}) custom-call(f32[384,384]{1,0:T(8,128)S(1)} %get-tuple-element.52.refs_0_, bf16[384,384]{1,0:T(8,128)(2,1)S(1)} %collective-permute-done.17.refs_1_, bf16[2,384,768]{2,1,0:T(8,128)(2,1)S(1)} %get-tuple-element.42.refs_1_.refs_2_, ...), custom_call_target="tpu_custom_call" | custom-call | flops 6000000000 | tf_op jit(solution)/shard_map/far_2/pallas_call | solution.py:42
  47.7 2.8 %collective-permute-start.18 = (bf16[256,384]{1,0:T(8,128)(2,1)S(1)}, bf16[256,384]{1,0:T(8,128)(2,1)S(1)}, u32[]{:S(2)}, u32[]{:S(2)}) collective-permute-start(bf16[256,384]{1,0:T(8,128)(2,1)S(1)} %get-tuple-element.55), channel_id=1, source_target_pairs={{0,24},{8,16},{16,8},{24,0},{1,25},{9,17},{17,9},{25,1},{2,26},{10... | collective-permute-start | bytes 589832 | tf_op jit(solution)/shard_map/ppermute | solution.py:57
  50.5 0.5 last_2.1
  51.0 0.6 collective-permute-start.19
  52.1 2.3 %collective-permute-done.21.refs_1_ = bf16[384,256]{1,0:T(8,128)(2,1)S(1)} collective-permute-done((bf16[384,256]{1,0:T(8,128)(2,1)S(1)}, bf16[384,256]{1,0:T(8,128)(2,1)S(1)}, u32[]{:S(2)}, u32[]{:S(2)}) %collective-permute-start.21) | collective-permute-done | bytes 196640 | tf_op jit(solution)/shard_map/ppermute | solution.py:57
  55.1 1.2 %collective-permute-done.22.refs_1_ = bf16[384,256]{1,0:T(8,128)(2,1)S(1)} collective-permute-done((bf16[384,256]{1,0:T(8,128)(2,1)S(1)}, bf16[384,256]{1,0:T(8,128)(2,1)S(1)}, u32[]{:S(2)}, u32[]{:S(2)}) %collective-permute-start.22) | collective-permute-done | bytes 196640 | tf_op jit(solution)/shard_map/ppermute | solution.py:57
  56.2 0.6 far_3.1
  56.8 2.5 %collective-permute-start.23 = (bf16[256,256]{1,0:T(8,128)(2,1)S(1)}, bf16[256,256]{1,0:T(8,128)(2,1)S(1)}, u32[]{:S(2)}, u32[]{:S(2)}) collective-permute-start(bf16[256,256]{1,0:T(8,128)(2,1)S(1)} %get-tuple-element.60), channel_id=1, source_target_pairs={{0,24},{8,16},{16,8},{24,0},{1,25},{9,17},{17,9},{25,1},{2,26},{10... | collective-permute-start | bytes 393224 | tf_op jit(solution)/shard_map/ppermute | solution.py:57
  59.3 0.4 last_3.1
  59.7 0.5 collective-permute-start.24
  60.2 0.6 collective-permute-start.25
  60.9 2.5 %collective-permute-done.23.refs_4_ = bf16[256,256]{1,0:T(8,128)(2,1)S(1)} collective-permute-done((bf16[256,256]{1,0:T(8,128)(2,1)S(1)}, bf16[256,256]{1,0:T(8,128)(2,1)S(1)}, u32[]{:S(2)}, u32[]{:S(2)}) %collective-permute-start.23) | collective-permute-done | bytes 131104 | tf_op jit(solution)/shard_map/ppermute | solution.py:57
  63.4 2.7 %collective-permute-done.24.refs_5_ = bf16[256,256]{1,0:T(8,128)(2,1)S(1)} collective-permute-done((bf16[256,256]{1,0:T(8,128)(2,1)S(1)}, bf16[256,256]{1,0:T(8,128)(2,1)S(1)}, u32[]{:S(2)}, u32[]{:S(2)}) %collective-permute-start.24) | collective-permute-done | bytes 131104 | tf_op jit(solution)/shard_map/ppermute | solution.py:57
  66.2 0.9 %end.1 = bf16[2,256,512]{2,1,0:T(8,128)(2,1)} custom-call(bf16[256,128]{1,0:T(8,128)(2,1)S(1)} %sum_0.1.refs_3_.refs_0_, bf16[256,256]{1,0:T(8,128)(2,1)S(1)} %get-tuple-element.51.refs_1_, bf16[256,384]{1,0:T(8,128)(2,1)S(1)} %sum_2.1.refs_2_, f32[256,256]{1,0:T(8,128)S(1)} %get-tuple-element.59.refs_4_.refs_3_, ...), custom_call_target="tpu_custom_call" | custom-call | tf_op jit(solution)/shard_map/end/pallas_call | solution.py:500
  (34 shorter events, 5.0 us)
Async XLA Ops:
  3.7 1.5 %collective-permute-start = (bf16[384,128]{1,0:T(8,128)(2,1)S(1)}, bf16[384,128]{1,0:T(8,128)(2,1)S(1)}, u32[]{:S(2)}, u32[]{:S(2)}) collective-permute-start(bf16[384,128]{1,0:T(8,128)(2,1)S(1)} %get-tuple-element.34.refs_0_), channel_id=1, source_target_pairs={{0,1},{1,0},{2,3},{3,2},{4,5},{5,4},{6,7},{7,6},{8,9},{9,8},{10,11... | collective-permute-start | bytes 294920 | tf_op jit(solution)/shard_map/ppermute | solution.py:57
  5.5 3.1 %collective-permute-start.2 = (bf16[384,896]{1,0:T(8,128)(2,1)S(1)}, bf16[384,896]{1,0:T(8,128)(2,1)S(1)}, u32[]{:S(2)}, u32[]{:S(2)}) collective-permute-start(bf16[384,896]{1,0:T(8,128)(2,1)S(1)} %get-tuple-element.39.refs_0_), channel_id=1, source_target_pairs={{0,1},{1,0},{2,3},{3,2},{4,5},{5,4},{6,7},{7,6},{8,9},{9,8},{10,11... | collective-permute-start | bytes 2064392 | tf_op jit(solution)/shard_map/ppermute | solution.py:57
  5.9 6.0 %collective-permute-start.1 = (bf16[384,128]{1,0:T(8,128)(2,1)S(1)}, bf16[384,128]{1,0:T(8,128)(2,1)S(1)}, u32[]{:S(2)}, u32[]{:S(2)}) collective-permute-start(bf16[384,128]{1,0:T(8,128)(2,1)S(1)} %get-tuple-element.37.refs_3_.refs_0_), channel_id=1, source_target_pairs={{0,2},{1,3},{2,0},{3,1},{4,6},{5,7},{6,4},{7,5},{8,10},{9,11},{10,... | collective-permute-start | bytes 294920 | tf_op jit(solution)/shard_map/ppermute | solution.py:57
  9.0 10.8 %collective-permute-start.4 = (bf16[384,256]{1,0:T(8,128)(2,1)S(1)}, bf16[384,256]{1,0:T(8,128)(2,1)S(1)}, u32[]{:S(2)}, u32[]{:S(2)}) collective-permute-start(bf16[384,256]{1,0:T(8,128)(2,1)S(1)} %level1_1.1.refs_3_.refs_0_), channel_id=1, source_target_pairs={{0,2},{1,3},{2,0},{3,1},{4,6},{5,7},{6,4},{7,5},{8,10},{9,11},{10,... | collective-permute-start | bytes 589832 | tf_op jit(solution)/shard_map/ppermute | solution.py:57
  12.3 8.3 %collective-permute-start.3 = (bf16[384,128]{1,0:T(8,128)(2,1)S(1)}, bf16[384,128]{1,0:T(8,128)(2,1)S(1)}, u32[]{:S(2)}, u32[]{:S(2)}) collective-permute-start(bf16[384,128]{1,0:T(8,128)(2,1)S(1)} %level2_0.1.refs_3_.refs_0_), channel_id=1, source_target_pairs={{0,4},{1,5},{2,6},{3,7},{4,0},{5,1},{6,2},{7,3},{8,12},{9,13},{10,... | collective-permute-start | bytes 294920 | tf_op jit(solution)/shard_map/ppermute | solution.py:57
  15.6 13.3 %collective-permute-start.9 = (bf16[384,384]{1,0:T(8,128)(2,1)S(1)}, bf16[384,384]{1,0:T(8,128)(2,1)S(1)}, u32[]{:S(2)}, u32[]{:S(2)}) collective-permute-start(bf16[384,384]{1,0:T(8,128)(2,1)S(1)} %level1_2.1.refs_3_.refs_0_), channel_id=1, source_target_pairs={{0,2},{1,3},{2,0},{3,1},{4,6},{5,7},{6,4},{7,5},{8,10},{9,11},{10,... | collective-permute-start | bytes 884744 | tf_op jit(solution)/shard_map/ppermute | solution.py:57
  20.1 13.8 %collective-permute-start.10 = (bf16[384,256]{1,0:T(8,128)(2,1)S(1)}, bf16[384,256]{1,0:T(8,128)(2,1)S(1)}, u32[]{:S(2)}, u32[]{:S(2)}) collective-permute-start(bf16[384,256]{1,0:T(8,128)(2,1)S(1)} %level2_1.1.refs_3_.refs_0_), channel_id=1, source_target_pairs={{0,4},{1,5},{2,6},{3,7},{4,0},{5,1},{6,2},{7,3},{8,12},{9,13},{10,... | collective-permute-start | bytes 589832 | tf_op jit(solution)/shard_map/ppermute | solution.py:57
  20.9 1.4 %collective-permute-start.5 = (bf16[384,128]{1,0:T(8,128)(2,1)S(1)}, bf16[384,128]{1,0:T(8,128)(2,1)S(1)}, u32[]{:S(2)}, u32[]{:S(2)}) collective-permute-start(bf16[384,128]{1,0:T(8,128)(2,1)S(1)} %level3_0.1.refs_0_), channel_id=1, source_target_pairs={{0,1},{1,0},{2,3},{3,2},{4,5},{5,4},{6,7},{7,6},{8,9},{9,8},{10,11... | collective-permute-start | bytes 294920 | tf_op jit(solution)/shard_map/ppermute | solution.py:57
  22.9 8.1 %collective-permute-start.6 = (bf16[256,128]{1,0:T(8,128)(2,1)S(1)}, bf16[256,128]{1,0:T(8,128)(2,1)S(1)}, u32[]{:S(2)}, u32[]{:S(2)}) collective-permute-start(bf16[256,128]{1,0:T(8,128)(2,1)S(1)} %get-tuple-element.44), channel_id=1, source_target_pairs={{0,24},{8,16},{16,8},{24,0},{1,25},{9,17},{17,9},{25,1},{2,26},{10... | collective-permute-start | bytes 196616 | tf_op jit(solution)/shard_map/ppermute | solution.py:57
  25.4 5.6 %collective-permute-start.7 = (bf16[256,128]{1,0:T(8,128)(2,1)S(1)}, bf16[256,128]{1,0:T(8,128)(2,1)S(1)}, u32[]{:S(2)}, u32[]{:S(2)}) collective-permute-start(bf16[256,128]{1,0:T(8,128)(2,1)S(1)} %get-tuple-element.45), channel_id=1, source_target_pairs={{0,16},{8,24},{16,0},{24,8},{1,17},{9,25},{17,1},{25,9},{2,18},{10... | collective-permute-start | bytes 196616 | tf_op jit(solution)/shard_map/ppermute | solution.py:57
  25.9 5.1 %collective-permute-start.8 = (bf16[256,128]{1,0:T(8,128)(2,1)S(1)}, bf16[256,128]{1,0:T(8,128)(2,1)S(1)}, u32[]{:S(2)}, u32[]{:S(2)}) collective-permute-start(bf16[256,128]{1,0:T(8,128)(2,1)S(1)} %get-tuple-element.46), channel_id=1, source_target_pairs={{0,8},{8,0},{16,24},{24,16},{1,9},{9,1},{17,25},{25,17},{2,10},{10... | collective-permute-start | bytes 196616 | tf_op jit(solution)/shard_map/ppermute | solution.py:57
  29.4 15.4 %collective-permute-start.14 = (bf16[384,384]{1,0:T(8,128)(2,1)S(1)}, bf16[384,384]{1,0:T(8,128)(2,1)S(1)}, u32[]{:S(2)}, u32[]{:S(2)}) collective-permute-start(bf16[384,384]{1,0:T(8,128)(2,1)S(1)} %level2_2.1.refs_4_.refs_0_), channel_id=1, source_target_pairs={{0,4},{1,5},{2,6},{3,7},{4,0},{5,1},{6,2},{7,3},{8,12},{9,13},{10,... | collective-permute-start | bytes 884744 | tf_op jit(solution)/shard_map/ppermute | solution.py:57
  31.4 9.6 %collective-permute-start.12 = (bf16[384,256]{1,0:T(8,128)(2,1)S(1)}, bf16[384,256]{1,0:T(8,128)(2,1)S(1)}, u32[]{:S(2)}, u32[]{:S(2)}) collective-permute-start(bf16[384,256]{1,0:T(8,128)(2,1)S(1)} %level1_3.1.refs_3_.refs_0_), channel_id=1, source_target_pairs={{0,2},{1,3},{2,0},{3,1},{4,6},{5,7},{6,4},{7,5},{8,10},{9,11},{10,... | collective-permute-start | bytes 589832 | tf_op jit(solution)/shard_map/ppermute | solution.py:57
  34.3 1.5 %collective-permute-start.11 = (bf16[384,256]{1,0:T(8,128)(2,1)S(1)}, bf16[384,256]{1,0:T(8,128)(2,1)S(1)}, u32[]{:S(2)}, u32[]{:S(2)}) collective-permute-start(bf16[384,256]{1,0:T(8,128)(2,1)S(1)} %level3_1.1.refs_0_), channel_id=1, source_target_pairs={{0,1},{1,0},{2,3},{3,2},{4,5},{5,4},{6,7},{7,6},{8,9},{9,8},{10,11... | collective-permute-start | bytes 589832 | tf_op jit(solution)/shard_map/ppermute | solution.py:57
  36.6 6.6 %collective-permute-start.13 = (bf16[256,256]{1,0:T(8,128)(2,1)S(1)}, bf16[256,256]{1,0:T(8,128)(2,1)S(1)}, u32[]{:S(2)}, u32[]{:S(2)}) collective-permute-start(bf16[256,256]{1,0:T(8,128)(2,1)S(1)} %get-tuple-element.48), channel_id=1, source_target_pairs={{0,24},{8,16},{16,8},{24,0},{1,25},{9,17},{17,9},{25,1},{2,26},{10... | collective-permute-start | bytes 393224 | tf_op jit(solution)/shard_map/ppermute | solution.py:57
  39.3 6.6 %collective-permute-start.15 = (bf16[256,256]{1,0:T(8,128)(2,1)S(1)}, bf16[256,256]{1,0:T(8,128)(2,1)S(1)}, u32[]{:S(2)}, u32[]{:S(2)}) collective-permute-start(bf16[256,256]{1,0:T(8,128)(2,1)S(1)} %get-tuple-element.49), channel_id=1, source_target_pairs={{0,16},{8,24},{16,0},{24,8},{1,17},{9,25},{17,1},{25,9},{2,18},{10... | collective-permute-start | bytes 393224 | tf_op jit(solution)/shard_map/ppermute | solution.py:57
  39.9 6.1 %collective-permute-start.16 = (bf16[256,256]{1,0:T(8,128)(2,1)S(1)}, bf16[256,256]{1,0:T(8,128)(2,1)S(1)}, u32[]{:S(2)}, u32[]{:S(2)}) collective-permute-start(bf16[256,256]{1,0:T(8,128)(2,1)S(1)} %get-tuple-element.50), channel_id=1, source_target_pairs={{0,8},{8,0},{16,24},{24,16},{1,9},{9,1},{17,25},{25,17},{2,10},{10... | collective-permute-start | bytes 393224 | tf_op jit(solution)/shard_map/ppermute | solution.py:57
  43.8 10.6 %collective-permute-start.21 = (bf16[384,256]{1,0:T(8,128)(2,1)S(1)}, bf16[384,256]{1,0:T(8,128)(2,1)S(1)}, u32[]{:S(2)}, u32[]{:S(2)}) collective-permute-start(bf16[384,256]{1,0:T(8,128)(2,1)S(1)} %level2_3.1.refs_2_.refs_0_), channel_id=1, source_target_pairs={{0,4},{1,5},{2,6},{3,7},{4,0},{5,1},{6,2},{7,3},{8,12},{9,13},{10,... | collective-permute-start | bytes 589832 | tf_op jit(solution)/shard_map/ppermute | solution.py:57
  45.2 1.6 %collective-permute-start.17 = (bf16[384,384]{1,0:T(8,128)(2,1)S(1)}, bf16[384,384]{1,0:T(8,128)(2,1)S(1)}, u32[]{:S(2)}, u32[]{:S(2)}) collective-permute-start(bf16[384,384]{1,0:T(8,128)(2,1)S(1)} %level3_2.1.refs_0_), channel_id=1, source_target_pairs={{0,1},{1,0},{2,3},{3,2},{4,5},{5,4},{6,7},{7,6},{8,9},{9,8},{10,11... | collective-permute-start | bytes 884744 | tf_op jit(solution)/shard_map/ppermute | solution.py:57
  47.7 12.5 %collective-permute-start.18 = (bf16[256,384]{1,0:T(8,128)(2,1)S(1)}, bf16[256,384]{1,0:T(8,128)(2,1)S(1)}, u32[]{:S(2)}, u32[]{:S(2)}) collective-permute-start(bf16[256,384]{1,0:T(8,128)(2,1)S(1)} %get-tuple-element.55), channel_id=1, source_target_pairs={{0,24},{8,16},{16,8},{24,0},{1,25},{9,17},{17,9},{25,1},{2,26},{10... | collective-permute-start | bytes 589832 | tf_op jit(solution)/shard_map/ppermute | solution.py:57
  51.0 9.8 %collective-permute-start.19 = (bf16[256,384]{1,0:T(8,128)(2,1)S(1)}, bf16[256,384]{1,0:T(8,128)(2,1)S(1)}, u32[]{:S(2)}, u32[]{:S(2)}) collective-permute-start(bf16[256,384]{1,0:T(8,128)(2,1)S(1)} %get-tuple-element.56), channel_id=1, source_target_pairs={{0,16},{8,24},{16,0},{24,8},{1,17},{9,25},{17,1},{25,9},{2,18},{10... | collective-permute-start | bytes 589832 | tf_op jit(solution)/shard_map/ppermute | solution.py:57
  51.6 9.2 %collective-permute-start.20 = (bf16[256,384]{1,0:T(8,128)(2,1)S(1)}, bf16[256,384]{1,0:T(8,128)(2,1)S(1)}, u32[]{:S(2)}, u32[]{:S(2)}) collective-permute-start(bf16[256,384]{1,0:T(8,128)(2,1)S(1)} %get-tuple-element.57), channel_id=1, source_target_pairs={{0,8},{8,0},{16,24},{24,16},{1,9},{9,1},{17,25},{25,17},{2,10},{10... | collective-permute-start | bytes 589832 | tf_op jit(solution)/shard_map/ppermute | solution.py:57
  54.7 1.5 %collective-permute-start.22 = (bf16[384,256]{1,0:T(8,128)(2,1)S(1)}, bf16[384,256]{1,0:T(8,128)(2,1)S(1)}, u32[]{:S(2)}, u32[]{:S(2)}) collective-permute-start(bf16[384,256]{1,0:T(8,128)(2,1)S(1)} %level3_3.1.refs_0_), channel_id=1, source_target_pairs={{0,1},{1,0},{2,3},{3,2},{4,5},{5,4},{6,7},{7,6},{8,9},{9,8},{10,11... | collective-permute-start | bytes 589832 | tf_op jit(solution)/shard_map/ppermute | solution.py:57
  56.8 6.6 %collective-permute-start.23 = (bf16[256,256]{1,0:T(8,128)(2,1)S(1)}, bf16[256,256]{1,0:T(8,128)(2,1)S(1)}, u32[]{:S(2)}, u32[]{:S(2)}) collective-permute-start(bf16[256,256]{1,0:T(8,128)(2,1)S(1)} %get-tuple-element.60), channel_id=1, source_target_pairs={{0,24},{8,16},{16,8},{24,0},{1,25},{9,17},{17,9},{25,1},{2,26},{10... | collective-permute-start | bytes 393224 | tf_op jit(solution)/shard_map/ppermute | solution.py:57
  59.7 6.4 %collective-permute-start.24 = (bf16[256,256]{1,0:T(8,128)(2,1)S(1)}, bf16[256,256]{1,0:T(8,128)(2,1)S(1)}, u32[]{:S(2)}, u32[]{:S(2)}) collective-permute-start(bf16[256,256]{1,0:T(8,128)(2,1)S(1)} %get-tuple-element.61), channel_id=1, source_target_pairs={{0,16},{8,24},{16,0},{24,8},{1,17},{9,25},{17,1},{25,9},{2,18},{10... | collective-permute-start | bytes 393224 | tf_op jit(solution)/shard_map/ppermute | solution.py:57
  60.2 5.9 %collective-permute-start.25 = (bf16[256,256]{1,0:T(8,128)(2,1)S(1)}, bf16[256,256]{1,0:T(8,128)(2,1)S(1)}, u32[]{:S(2)}, u32[]{:S(2)}) collective-permute-start(bf16[256,256]{1,0:T(8,128)(2,1)S(1)} %get-tuple-element.62), channel_id=1, source_target_pairs={{0,8},{8,0},{16,24},{24,16},{1,9},{9,1},{17,25},{25,17},{2,10},{10... | collective-permute-start | bytes 393224 | tf_op jit(solution)/shard_map/ppermute | solution.py:57
